TPU v7x, 32 devices: a whole 2x2x4 slice. The times are simulated.
32 devices in a mesh: blk: 8 (over z, core), dx: 2 (over y), dy: 2 (over x).
Axes of the slice: x: 2, y: 2, z: 4, core: 2. Of those that a mesh axis runs over, the one named last changes fastest.
Arguments:
- orbitals: bfloat16 [1024, 8, 16, 128], P('blk', 'dx', 'dy'), may hold values from -6 to 6
- coupling: float32 [8, 16, 128], P('dx', 'dy'), may hold values from 0.3 to 3
- pot_grad: float32 [3, 8, 16, 128], P(None, 'dx', 'dy'), may hold values from -6 to 6
Outputs:
- spin_orbit: float32 [3, 5, 1024, 128], P(None, None, ('blk', 'dx', 'dy'))
All inputs are finite; a program needn't handle non-finite values.
Results may differ from a plain program's by a relative error of at most 0.0029.
Values may be sent and summed in bfloat16 or wider, within the bound.
No kernel may reach another device: no remote copies, remote signals or barrier semaphores. Data moves between devices by JAX's collectives and lax.ppermute only.
A program may use at most 64 MiB of HBM per device.

v0:
```python
import math

import jax
import jax.numpy as jnp
from jax import lax
from jax.sharding import PartitionSpec as P

HALF = 2


def with_halo(cells, sides, width):
    for axis, dim in sides:
        count = lax.axis_size(axis)
        head = lax.slice_in_dim(cells, 0, width, axis=dim)
        tail = lax.slice_in_dim(cells, cells.shape[dim] - width, cells.shape[dim], axis=dim)
        cells = jnp.concatenate(
            [
                lax.ppermute(tail, axis, [(i, (i + 1) % count) for i in range(count)]),
                cells,
                lax.ppermute(head, axis, [((i + 1) % count, i) for i in range(count)]),
            ],
            axis=dim,
        )
    return cells


def from_behind(block, axis, distance):
    devices = range(lax.axis_size(axis))
    route = [((i - distance) % len(devices), i) for i in devices]
    return lax.ppermute(block, axis, route)


def on_device(orbitals, coupling, pot_grad):
    states, width_x, width_y, width_z = orbitals.shape
    cell_count = width_x * width_y * width_z
    weight_scale = 1.0 / math.sqrt(cell_count * lax.axis_size("dx") * lax.axis_size("dy"))
    coeff_field = coupling[None] * pot_grad
    coeff_one, coeff_two, coeff_three = (coeff_field[0], coeff_field[1], coeff_field[2])
    padded = with_halo(orbitals, (("dx", 1), ("dy", 2)), 1)
    grad_x = 0.5 * (
        padded[:, 2:, 1:-1].astype(jnp.float32) - padded[:, :-2, 1:-1].astype(jnp.float32)
    )
    grad_y = 0.5 * (
        padded[:, 1:-1, 2:].astype(jnp.float32) - padded[:, 1:-1, :-2].astype(jnp.float32)
    )
    field_f32 = orbitals.astype(jnp.float32)
    grad_z = 0.5 * (jnp.roll(field_f32, -1, axis=3) - jnp.roll(field_f32, 1, axis=3))
    cross_one = coeff_two * grad_z - coeff_three * grad_y
    cross_two = coeff_three * grad_x - coeff_one * grad_z
    cross_three = coeff_one * grad_y - coeff_two * grad_x
    cross_field = jnp.stack([cross_one, cross_two, cross_three]).astype(jnp.bfloat16)
    cross_field = cross_field.reshape(3, states, cell_count)
    uppers = []
    current = orbitals
    for step_up in range(HALF):
        current = from_behind(current, "blk", -1)
        uppers.append(current)
    lowers = []
    current = orbitals
    for step_down in range(HALF):
        current = from_behind(current, "blk", 1)
        lowers.append(current)
    panels = lowers[::-1] + [orbitals] + uppers

    def make_tile(panel):
        rows_flat = panel.reshape(states, cell_count)
        return (
            jnp.einsum("kjc,ic->kji", cross_field, rows_flat, preferred_element_type=jnp.float32)
            * weight_scale
        )

    stacked = jnp.stack([make_tile(panel) for panel in panels], 1)
    return lax.psum_scatter(stacked, ("dx", "dy"), scatter_dimension=2, tiled=True)


def solution(mesh):
    in_specs = (P("blk", "dx", "dy", None), P("dx", "dy", None), P(None, "dx", "dy", None))
    out_specs = P(None, None, ("blk", "dx", "dy"), None)
    return jax.shard_map(
        on_device, mesh=mesh, in_specs=in_specs, out_specs=out_specs, check_vma=False
    )
```

profile of v0, /device:TPU:0, one launch (start us, length us, event | category | flops | bytes accessed | tf_op | source)
XLA Modules:
  0.0 103.8 jit_solution(12919479020479632633)
XLA Ops:
  6.5 1.7 %copy.4 = bf16[128,4,8,128]{3,0,2,1:T(8,128)(2,1)S(1)} copy(bf16[128,4,8,128]{3,2,1,0:T(8,128)(2,1)} %param.3) | data formatting | bytes 2097152 | tf_op args[0]
  8.3 0.5 collective-permute-start.4
  8.8 4.1 %collective-permute-start.6 = (bf16[128,4,8,128]{3,0,2,1:T(8,128)(2,1)S(1)}, bf16[128,4,8,128]{3,0,2,1:T(8,128)(2,1)S(1)}, u32[]{:S(2)}, u32[]{:S(2)}) collective-permute-start(bf16[128,4,8,128]{3,0,2,1:T(8,128)(2,1)S(1)} %copy.4), channel_id=1, source_target_pairs={{4,0},{8,4},{12,8},{16,12},{20,16},{24,20},{28,24},{0,28},{5,1},{9... | collective-permute-start | bytes 3145736 | tf_op jit(solution)/shard_map/ppermute | solution.py:30
  12.9 2.0 %collective-permute-start = (bf16[128,1,8,128]{3,0,2,1:T(8,128)(2,1)S(1)}, bf16[128,1,8,128]{3,0,2,1:T(8,128)(2,1)S(1)}, u32[]{:S(2)}, u32[]{:S(2)}) collective-permute-start(bf16[128,1,8,128]{3,0,2,1:T(8,128)(2,1)S(1)} %get-tuple-element.16), channel_id=1, source_target_pairs={{0,2},{2,0},{1,3},{3,1},{4,6},{6,4},{5,7},{7,5},{8,10},{10,8},{9,1... | collective-permute-start | bytes 786440 | tf_op jit(solution)/shard_map/ppermute | solution.py:18
  14.9 0.1 collective-permute-start.1
  15.0 0.0 copy-done.2
  15.0 7.2 %collective-permute-done = bf16[128,1,8,128]{3,0,2,1:T(8,128)(2,1)S(1)} collective-permute-done((bf16[128,1,8,128]{3,0,2,1:T(8,128)(2,1)S(1)}, bf16[128,1,8,128]{3,0,2,1:T(8,128)(2,1)S(1)}, u32[]{:S(2)}, u32[]{:S(2)}) %collective-permute-start) | collective-permute-done | bytes 262176 | tf_op jit(solution)/shard_map/ppermute | solution.py:18
  22.3 0.5 copy_convert_fusion
  22.8 2.6 %collective-permute-done.1 = bf16[128,1,8,128]{3,0,2,1:T(8,128)(2,1)S(1)} collective-permute-done((bf16[128,1,8,128]{3,0,2,1:T(8,128)(2,1)S(1)}, bf16[128,1,8,128]{3,0,2,1:T(8,128)(2,1)S(1)}, u32[]{:S(2)}, u32[]{:S(2)}) %collective-permute-start.1) | collective-permute-done | bytes 262176 | tf_op jit(solution)/shard_map/ppermute | solution.py:20
  25.5 1.6 %collective-permute-start.2 = (bf16[128,6,1,128]{3,0,2,1:T(8,128)(2,1)S(1)}, bf16[128,6,1,128]{3,0,2,1:T(8,128)(2,1)S(1)}, u32[]{:S(2)}, u32[]{:S(2)}) collective-permute-start(bf16[128,6,1,128]{3,0,2,1:T(8,128)(2,1)S(1)} %get-tuple-element.13), channel_id=1, source_target_pairs={{1,0},{0,1},{3,2},{2,3},{5,4},{4,5},{7,6},{6,7},{9,8},{8,9},{11,10... | collective-permute-start | bytes 589832 | tf_op jit(solution)/shard_map/ppermute | solution.py:20
  27.0 0.5 collective-permute-start.3
  27.6 0.7 fusion.28
  28.3 5.5 %collective-permute-done.4 = bf16[128,4,8,128]{3,0,2,1:T(8,128)(2,1)S(1)} collective-permute-done((bf16[128,4,8,128]{3,0,2,1:T(8,128)(2,1)S(1)}, bf16[128,4,8,128]{3,0,2,1:T(8,128)(2,1)S(1)}, u32[]{:S(2)}, u32[]{:S(2)}) %collective-permute-start.4) | collective-permute-done | bytes 1048608 | tf_op jit(solution)/shard_map/ppermute | solution.py:30
  33.9 0.0 collective-permute-start.5
  33.9 0.7 fusion.27
  34.6 0.0 collective-permute-done.2
  34.6 0.0 collective-permute-done.3
  34.6 2.4 %fusion.15 = (bf16[1,128,4,8,128]{4,1,3,2,0:T(8,128)(2,1)S(1)}, f32[128,4,8,128]{3,0,2,1:T(8,128)S(1)}, bf16[1,128,4,8,128]{4,1,3,2,0:T(8,128)(2,1)S(1)}) fusion(f32[4,8,128]{2,1,0:T(8,128)S(1)} %get-tuple-element.18, f32[4,8,128]{2,1,0:T(8,128)S(1)} %get-tuple-element.20, bf16[128,6,1,128]{3,0,2,1:T(8,128)(2,1)S(1)} %collective-permute-done.2, ...), kind=kLoop, calls=%fused_computation.27 | loop fusion | flops 11010048 | bytes 11976704 | tf_op jit(solution)/shard_map/stack | solution.py:51
  37.1 0.6 fusion.16
  37.7 0.0 collective-permute-done.6
  37.7 3.6 %collective-permute-start.7 = (bf16[128,4,8,128]{3,0,2,1:T(8,128)(2,1)S(1)}, bf16[128,4,8,128]{3,0,2,1:T(8,128)(2,1)S(1)}, u32[]{:S(2)}, u32[]{:S(2)}) collective-permute-start(bf16[128,4,8,128]{3,0,2,1:T(8,128)(2,1)S(1)} %collective-permute-done.6), channel_id=1, source_target_pairs={{4,0},{8,4},{12,8},{16,12},{20,16},{24,20},{28,24},{0,28},{5,1},{9... | collective-permute-start | bytes 3145736 | tf_op jit(solution)/shard_map/ppermute | solution.py:30
  41.3 12.5 %collective-permute-done.5 = bf16[128,4,8,128]{3,0,2,1:T(8,128)(2,1)S(1)} collective-permute-done((bf16[128,4,8,128]{3,0,2,1:T(8,128)(2,1)S(1)}, bf16[128,4,8,128]{3,0,2,1:T(8,128)(2,1)S(1)}, u32[]{:S(2)}, u32[]{:S(2)}) %collective-permute-start.5) | collective-permute-done | bytes 1048608 | tf_op jit(solution)/shard_map/ppermute | solution.py:30
  53.7 1.0 fusion.14
  54.7 1.0 fusion.11
  55.7 1.0 fusion.8
  56.7 1.0 fusion.5
  57.7 0.0 collective-permute-done.7
  57.7 1.0 fusion.2
  58.7 1.0 copy-done.1
  59.6 0.0 reduce-scatter.2.cloned.1.call-update
  59.6 35.6 %reduce-scatter.2.cloned.1.call-done = f32[3,5,32,128]{3,2,0,1:T(8,128)} async-done(((f32[3,5,128,128]{3,2,0,1:T(8,128)}), f32[3,5,32,128]{3,2,0,1:T(8,128)}) %reduce-scatter.2.cloned.1.call-update) | async-done | bytes 245776 | tf_op jit(solution)/shard_map/reduce_scatter | solution.py:73
  95.3 1.7 %copy.13 = f32[3,5,32,128]{3,2,1,0:T(8,128)} copy(f32[3,5,32,128]{3,2,0,1:T(8,128)} %reduce-scatter.2.cloned.1.call-done) | data formatting | bytes 491520 | tf_op jit(solution)/shard_map/reduce_scatter | solution.py:73
  (13 shorter events, 0.1 us)
Async XLA Ops:
  6.5 15.7 %copy-start = (bf16[128,4,8,128]{3,2,1,0:T(8,128)(2,1)S(1)}, bf16[128,4,8,128]{3,2,1,0:T(8,128)(2,1)}, u32[]{:S(2)}) copy-start(bf16[128,4,8,128]{3,2,1,0:T(8,128)(2,1)} %param.3) | copy-start | bytes 3145732
  6.5 8.5 %copy-start.3 = (f32[4,8,128]{2,1,0:T(8,128)S(1)}, f32[4,8,128]{2,1,0:T(8,128)}, u32[]{:S(2)}) copy-start(f32[4,8,128]{2,1,0:T(8,128)} %param.4) | copy-start | bytes 49156
  6.5 8.5 %copy-start.2 = (f32[3,4,8,128]{3,2,1,0:T(8,128)S(1)}, f32[3,4,8,128]{3,2,1,0:T(8,128)}, u32[]{:S(2)}) copy-start(f32[3,4,8,128]{3,2,1,0:T(8,128)} %param.5) | copy-start | bytes 147460
  6.5 88.7 %reduce-scatter.2.cloned.1.call-start = ((), (), s32[]{:S(2)}) async-start(), calls=%async_computation.1 | async-start | bytes 1228800 | tf_op jit(solution)/shard_map/reduce_scatter | solution.py:73
  8.3 25.6 %collective-permute-start.4 = (bf16[128,4,8,128]{3,0,2,1:T(8,128)(2,1)S(1)}, bf16[128,4,8,128]{3,0,2,1:T(8,128)(2,1)S(1)}, u32[]{:S(2)}, u32[]{:S(2)}) collective-permute-start(bf16[128,4,8,128]{3,0,2,1:T(8,128)(2,1)S(1)} %copy.4), channel_id=1, source_target_pairs={{28,0},{0,4},{4,8},{8,12},{12,16},{16,20},{20,24},{24,28},{29,1},{... | collective-permute-start | bytes 3145736 | tf_op jit(solution)/shard_map/ppermute | solution.py:30
  8.8 28.9 %collective-permute-start.6 = (bf16[128,4,8,128]{3,0,2,1:T(8,128)(2,1)S(1)}, bf16[128,4,8,128]{3,0,2,1:T(8,128)(2,1)S(1)}, u32[]{:S(2)}, u32[]{:S(2)}) collective-permute-start(bf16[128,4,8,128]{3,0,2,1:T(8,128)(2,1)S(1)} %copy.4), channel_id=1, source_target_pairs={{4,0},{8,4},{12,8},{16,12},{20,16},{24,20},{28,24},{0,28},{5,1},{9... | collective-permute-start | bytes 3145736 | tf_op jit(solution)/shard_map/ppermute | solution.py:30
  12.9 9.3 %collective-permute-start = (bf16[128,1,8,128]{3,0,2,1:T(8,128)(2,1)S(1)}, bf16[128,1,8,128]{3,0,2,1:T(8,128)(2,1)S(1)}, u32[]{:S(2)}, u32[]{:S(2)}) collective-permute-start(bf16[128,1,8,128]{3,0,2,1:T(8,128)(2,1)S(1)} %get-tuple-element.16), channel_id=1, source_target_pairs={{0,2},{2,0},{1,3},{3,1},{4,6},{6,4},{5,7},{7,5},{8,10},{10,8},{9,1... | collective-permute-start | bytes 786440 | tf_op jit(solution)/shard_map/ppermute | solution.py:18
  14.9 10.5 %collective-permute-start.1 = (bf16[128,1,8,128]{3,0,2,1:T(8,128)(2,1)S(1)}, bf16[128,1,8,128]{3,0,2,1:T(8,128)(2,1)S(1)}, u32[]{:S(2)}, u32[]{:S(2)}) collective-permute-start(bf16[128,1,8,128]{3,0,2,1:T(8,128)(2,1)S(1)} %get-tuple-element.17), channel_id=1, source_target_pairs={{2,0},{0,2},{3,1},{1,3},{6,4},{4,6},{7,5},{5,7},{10,8},{8,10},{11,... | collective-permute-start | bytes 786440 | tf_op jit(solution)/shard_map/ppermute | solution.py:20
  25.5 9.2 %collective-permute-start.2 = (bf16[128,6,1,128]{3,0,2,1:T(8,128)(2,1)S(1)}, bf16[128,6,1,128]{3,0,2,1:T(8,128)(2,1)S(1)}, u32[]{:S(2)}, u32[]{:S(2)}) collective-permute-start(bf16[128,6,1,128]{3,0,2,1:T(8,128)(2,1)S(1)} %get-tuple-element.13), channel_id=1, source_target_pairs={{1,0},{0,1},{3,2},{2,3},{5,4},{4,5},{7,6},{6,7},{9,8},{8,9},{11,10... | collective-permute-start | bytes 589832 | tf_op jit(solution)/shard_map/ppermute | solution.py:20
  27.0 7.6 %collective-permute-start.3 = (bf16[128,6,1,128]{3,0,2,1:T(8,128)(2,1)S(1)}, bf16[128,6,1,128]{3,0,2,1:T(8,128)(2,1)S(1)}, u32[]{:S(2)}, u32[]{:S(2)}) collective-permute-start(bf16[128,6,1,128]{3,0,2,1:T(8,128)(2,1)S(1)} %get-tuple-element.12), channel_id=1, source_target_pairs={{0,1},{1,0},{2,3},{3,2},{4,5},{5,4},{6,7},{7,6},{8,9},{9,8},{10,11... | collective-permute-start | bytes 589832 | tf_op jit(solution)/shard_map/ppermute | solution.py:18
  33.9 19.9 %collective-permute-start.5 = (bf16[128,4,8,128]{3,0,2,1:T(8,128)(2,1)S(1)}, bf16[128,4,8,128]{3,0,2,1:T(8,128)(2,1)S(1)}, u32[]{:S(2)}, u32[]{:S(2)}) collective-permute-start(bf16[128,4,8,128]{3,0,2,1:T(8,128)(2,1)S(1)} %collective-permute-done.4), channel_id=1, source_target_pairs={{28,0},{0,4},{4,8},{8,12},{12,16},{16,20},{20,24},{24,28},{29,1},{... | collective-permute-start | bytes 3145736 | tf_op jit(solution)/shard_map/ppermute | solution.py:30
  37.7 20.0 %collective-permute-start.7 = (bf16[128,4,8,128]{3,0,2,1:T(8,128)(2,1)S(1)}, bf16[128,4,8,128]{3,0,2,1:T(8,128)(2,1)S(1)}, u32[]{:S(2)}, u32[]{:S(2)}) collective-permute-start(bf16[128,4,8,128]{3,0,2,1:T(8,128)(2,1)S(1)} %collective-permute-done.6), channel_id=1, source_target_pairs={{4,0},{8,4},{12,8},{16,12},{20,16},{24,20},{28,24},{0,28},{5,1},{9... | collective-permute-start | bytes 3145736 | tf_op jit(solution)/shard_map/ppermute | solution.py:30
  58.7 1.0 copy-start.1
Sparse Core Ops, SparseCore 0:
  59.8 35.4 reduce-scatter.1
where the time goes:
time: 104 us
  waiting for transfers between devices  63.5 us (61%)
  between operations  13.6 us (13%)
  starting transfers between devices  12.4 us (12%)
  local copies, waits for them, and re-layouts  5.94 us (6%)
  matrix products  4.88 us (5%)
  other arithmetic  3.52 us (3%)
    reduce_scatter x1, waiting for transfers between devices, on_device(): lax.psum_scatter(stacked, ('dx', 'dy'), scatter_dimension=2, tiled=True)  35.6 us
    ppermute x4, waiting for transfers between devices, from_behind(): return lax.ppermute(block, axis, route)  18 us
    ppermute x4, starting transfers between devices, from_behind(): return lax.ppermute(block, axis, route)  8.2 us
    ppermute x2, waiting for transfers between devices, with_halo(): lax.ppermute(tail, axis, [(i, (i + 1) % count) for i in range(count)])  7.18 us
    dot_general x5, matrix products, make_tile(): jnp.einsum('kjc,ic->kji', cross_field, rows_flat, preferred_element_type=...  4.88 us
    another operation x2, other arithmetic, on_device(): jnp.stack([cross_one, cross_two, cross_three]).astype(jnp.bfloat16)  3 us
    unnamed x10, local copies, waits for them, and re-layouts  2.7 us
    ppermute x2, waiting for transfers between devices, with_halo(): lax.ppermute(head, axis, [((i + 1) % count, i) for i in range(count)])  2.62 us
  transfers between devices with their start and end apart: 9, of which 5 were waited for; matrix products, arithmetic and copies ran while one was open for 9% of the time, Pallas kernels for 0%

commit v1 on v0

v1 whole, which is shorter than its diff:
```python
import math

import jax
import jax.numpy as jnp
from jax import lax
from jax.sharding import PartitionSpec as P

AXES = ("blk", "dx", "dy")


def shift(block, axis, distance):
    count = lax.axis_size(axis)
    return lax.ppermute(block, axis, [((i + distance) % count, i) for i in range(count)])


def edges(cells, axis, dim):
    count = lax.axis_size(axis)
    size = cells.shape[dim]
    head = lax.slice_in_dim(cells, 0, 1, axis=dim)
    tail = lax.slice_in_dim(cells, size - 1, size, axis=dim)
    if count == 2:
        both = shift(jnp.concatenate([tail, head], axis=dim), axis, 1)
        return lax.slice_in_dim(both, 0, 1, axis=dim), lax.slice_in_dim(both, 1, 2, axis=dim)
    return shift(tail, axis, -1), shift(head, axis, 1)


def neighbours(cells, axis, dim):
    before, after = edges(cells, axis, dim)
    size = cells.shape[dim]
    prev = jnp.concatenate([before, lax.slice_in_dim(cells, 0, size - 1, axis=dim)], axis=dim)
    nxt = jnp.concatenate([lax.slice_in_dim(cells, 1, size, axis=dim), after], axis=dim)
    return prev, nxt


def plane_sum(parts):
    nx, ny = lax.axis_size("dx"), lax.axis_size("dy")
    x, y = lax.axis_index("dx"), lax.axis_index("dy")
    total = lax.dynamic_index_in_dim(parts, x * ny + y, 0, keepdims=False)
    for ox in range(nx):
        for oy in range(ny):
            if ox == 0 and oy == 0:
                continue
            dest = ((x + ox) % nx) * ny + (y + oy) % ny
            piece = lax.dynamic_index_in_dim(parts, dest, 0, keepdims=False)
            route = [
                (i * ny + j, ((i + ox) % nx) * ny + (j + oy) % ny) for i in range(nx) for j in range(ny)
            ]
            total = total + lax.ppermute(piece, ("dx", "dy"), route)
    return total


def on_device(orbitals, coupling, pot_grad):
    states, wx, wy, wz = orbitals.shape
    plane = lax.axis_size("dx") * lax.axis_size("dy")
    rows = states // plane
    scale = 1.0 / math.sqrt(wx * wy * wz * plane)
    psi = orbitals.transpose(1, 2, 0, 3)

    ahead_two = shift(psi, "blk", 2)
    core = lax.axis_index("blk") % 2
    count = lax.axis_size("blk")
    ahead_one = lax.ppermute(
        jnp.where(core == 0, ahead_two, psi), "blk", [(i, i ^ 1) for i in range(count)]
    )

    coeff = coupling[None] * pot_grad
    c = [coeff[k][:, :, None, :] for k in range(3)]
    cx = [a for a in neighbours(coeff, "dx", 1)]
    cy = [a for a in neighbours(coeff, "dy", 2)]
    cz = [jnp.roll(coeff, 1, axis=3), jnp.roll(coeff, -1, axis=3)]
    f32 = jnp.float32
    px = [a.astype(f32) for a in neighbours(psi, "dx", 0)]
    py = [a.astype(f32) for a in neighbours(psi, "dy", 1)]
    field = psi.astype(f32)
    pz = [jnp.roll(field, 1, axis=3), jnp.roll(field, -1, axis=3)]
    gx, gy, gz = [0.5 * (p[1] - p[0]) for p in (px, py, pz)]
    u = jnp.stack(
        [c[1] * gz - c[2] * gy, c[2] * gx - c[0] * gz, c[0] * gy - c[1] * gx]
    ).astype(jnp.bfloat16)

    def grad_of(k, cs, ps):
        a, b = [q[k][:, :, None, :] for q in cs]
        return 0.5 * (b * ps[1] - a * ps[0])

    w = jnp.stack(
        [
            grad_of(2, cy, py) - grad_of(1, cz, pz),
            grad_of(0, cz, pz) - grad_of(2, cx, px),
            grad_of(1, cx, px) - grad_of(0, cy, py),
        ]
    ).astype(jnp.bfloat16)

    def dot(spec, a, b):
        return jnp.einsum(spec, a, b, preferred_element_type=f32) * scale

    own = dot("kxyjz,xyiz->kji", u, psi)
    up_two = dot("kxyjz,xyiz->kji", u, ahead_two)
    up_one = dot("kxyjz,xyiz->kji", u, ahead_one)
    down_two = dot("xyjz,kxyiz->kji", ahead_two, w)
    down_one = dot("xyjz,kxyiz->kji", ahead_one, w)

    def by_dest(tiles):
        stacked = jnp.stack(tiles, 1)
        k, t = stacked.shape[:2]
        return stacked.reshape(k, t, plane, rows, states).transpose(2, 0, 1, 3, 4)

    mine = plane_sum(by_dest([own]))
    rest = plane_sum(by_dest([up_one, up_two, down_one, down_two]))
    one = shift(rest[:, 2], "blk", -1)
    two = shift(rest[:, 3], "blk", -2)
    return jnp.stack([two, one, mine[:, 0], rest[:, 0], rest[:, 1]], 1)


def solution(mesh):
    in_specs = (P("blk", "dx", "dy", None), P("dx", "dy", None), P(None, "dx", "dy", None))
    out_specs = P(None, None, ("blk", "dx", "dy"), None)
    return jax.shard_map(
        on_device, mesh=mesh, in_specs=in_specs, out_specs=out_specs, check_vma=False
    )
```

time: 104 us -> 71.9 us (0.69)
  waiting for transfers between devices: 63.5 us -> 9.09 us
  other arithmetic: 3.52 us -> 20.7 us
  between operations: 13.6 us -> 0.51 us
  matrix products: 4.88 us -> 11.8 us
  starting transfers between devices: 12.4 us -> 18.4 us
  local copies, waits for them, and re-layouts: 5.94 us -> 11 us
    reduce_scatter x1 -> x0, waiting for transfers between devices: 35.6 us -> none  [on_device(): lax.psum_scatter(stacked, ('dx', 'dy'), scatter_dimension=2, tiled=True)]
    ppermute x8 -> x14, waiting for transfers between devices: 27.8 us -> 9.09 us  [the longest x6 4.56 us: plane_sum(): total = total + lax.ppermute(piece, ('dx', 'dy'), route)]
    concatenate x1 -> x6, local copies, waits for them, and re-layouts: 0.03 us -> 8.44 us  [the longest x2 5.47 us: on_device(): pz = [jnp.roll(field, 1, axis=3), jnp.roll(field, -1, axis=3)]]
    another operation x2 -> x6, other arithmetic: 3 us -> 11.1 us  [on_device(): jnp.stack([cross_one, cross_two, cross_three]).astype(jnp.bfloat16)]
    dot_general x5, matrix products: 4.88 us -> 11.8 us  [dot(): return jnp.einsum(spec, a, b, preferred_element_type=f32) * scale]
    ppermute x8 -> x14, starting transfers between devices: 12.4 us -> 18.4 us  [the longest x7 9.27 us: shift(): lax.ppermute(block, axis, [((i + distance) % count, i) for i in range(cou...]
    select_n x0 -> x1, other arithmetic: none -> 3.07 us  [on_device(): jnp.where(core == 0, ahead_two, psi)]
    concatenate x0 -> x4, other arithmetic: none -> 2.79 us  [edges(): both = shift(jnp.concatenate([tail, head], axis=dim), axis, 1)]
  transfers between devices with their start and end apart: 9 -> 14, of which waited for: 5 -> 3; matrix products, arithmetic and copies ran while one was open for 9% -> 45% of each run, Pallas kernels for 0% -> 0%
where the time goes in v1:
time: 71.9 us; the launch traced here: 71.6 us
  other arithmetic  20.7 us (29%)
  starting transfers between devices  18.4 us (26%)
  matrix products  11.8 us (16%)
  local copies, waits for them, and re-layouts  11 us (15%)
  waiting for transfers between devices  9.09 us (13%)
    dot_general x5, matrix products, dot(): return jnp.einsum(spec, a, b, preferred_element_type=f32) * scale  11.8 us
    another operation x4, other arithmetic  10.3 us
    ppermute x7, starting transfers between devices, shift(): lax.ppermute(block, axis, [((i + distance) % count, i) for i in range(cou...  9.27 us
    ppermute x6, starting transfers between devices, plane_sum(): total = total + lax.ppermute(piece, ('dx', 'dy'), route)  9.14 us
    concatenate x2, local copies, waits for them, and re-layouts, on_device(): pz = [jnp.roll(field, 1, axis=3), jnp.roll(field, -1, axis=3)]  5.47 us
    ppermute x6, waiting for transfers between devices, plane_sum(): total = total + lax.ppermute(piece, ('dx', 'dy'), route)  4.56 us
    ppermute x7, waiting for transfers between devices, shift(): lax.ppermute(block, axis, [((i + distance) % count, i) for i in range(cou...  4.52 us
    select_n x1, other arithmetic, on_device(): jnp.where(core == 0, ahead_two, psi)  3.07 us
  transfers between devices with their start and end apart: 14, of which 3 were waited for; matrix products, arithmetic and copies ran while one was open for 45% of the time, Pallas kernels for 0%

profile of v1, /device:TPU:0, one launch (start us, length us, event | category | flops | bytes accessed | tf_op | source)
XLA Modules:
  0.0 71.6 jit_solution(480733996023538539)
XLA Ops:
  0.0 1.7 %fusion.46 = (f32[4,8,128,128]{3,2,1,0:T(8,128)S(1)}, bf16[4,8,128,128]{3,2,1,0:T(8,128)(2,1)S(1)}) fusion(bf16[128,4,8,128]{3,2,1,0:T(8,128)(2,1)} %param.3), kind=kLoop, calls=%fused_computation.120 | loop fusion | flops 524288 | bytes 4194304 | tf_op jit(solution)/shard_map/convert_element_type | solution.py:74
  1.7 5.1 %collective-permute-start.2 = (bf16[4,8,128,128]{3,2,1,0:T(8,128)(2,1)S(1)}, bf16[4,8,128,128]{3,2,1,0:T(8,128)(2,1)}, u32[]{:S(2)}, u32[]{:S(2)}) collective-permute-start(bf16[4,8,128,128]{3,2,1,0:T(8,128)(2,1)S(1)} %get-tuple-element.16), channel_id=1, source_target_pairs={{8,0},{12,4},{16,8},{20,12},{24,16},{28,20},{0,24},{4,28},{9,1},{1... | collective-permute-start | bytes 3145736 | tf_op jit(solution)/shard_map/ppermute | solution.py:13
  6.8 0.8 %pad_maximum_fusion.23 = bf16[2,8,128,128]{3,2,1,0:T(8,128)(2,1)} fusion(bf16[1,8,128,128]{3,2,1,0:T(8,128)(2,1)S(1)} %get-tuple-element.24, bf16[1,8,128,128]{3,2,1,0:T(8,128)(2,1)S(1)} %get-tuple-element.23), kind=kLoop, calls=%fused_computation.66 | loop fusion | flops 262144 | bytes 1048576 | tf_op jit(solution)/shard_map/concatenate | solution.py:22
  7.7 1.5 %collective-permute-start.1 = (bf16[2,8,128,128]{3,2,1,0:T(8,128)(2,1)}, bf16[2,8,128,128]{3,2,1,0:T(8,128)(2,1)S(1)}, u32[]{:S(2)}, u32[]{:S(2)}) collective-permute-start(bf16[2,8,128,128]{3,2,1,0:T(8,128)(2,1)} %pad_maximum_fusion.23), channel_id=1, source_target_pairs={{2,0},{0,2},{3,1},{1,3},{6,4},{4,6},{7,5},{5,7},{10,8},{8,10},{11,... | collective-permute-start | bytes 1572872 | tf_op jit(solution)/shard_map/ppermute | solution.py:13
  9.6 0.7 %pad_maximum_fusion.24 = bf16[4,2,128,128]{3,2,0,1:T(8,128)(2,1)} fusion(bf16[4,1,128,128]{3,2,0,1:T(8,128)(2,1)S(1)} %copy.68, bf16[4,1,128,128]{3,2,0,1:T(8,128)(2,1)S(1)} %copy.67), kind=kLoop, calls=%fused_computation.69 | loop fusion | flops 131072 | bytes 524288 | tf_op jit(solution)/shard_map/concatenate | solution.py:22
  10.4 1.5 %collective-permute-start = (bf16[4,2,128,128]{3,2,0,1:T(8,128)(2,1)}, bf16[4,2,128,128]{3,2,0,1:T(8,128)(2,1)}, u32[]{:S(2)}, u32[]{:S(2)}) collective-permute-start(bf16[4,2,128,128]{3,2,0,1:T(8,128)(2,1)} %pad_maximum_fusion.24), channel_id=1, source_target_pairs={{1,0},{0,1},{3,2},{2,3},{5,4},{4,5},{7,6},{6,7},{9,8},{8,9},{11,10... | collective-permute-start | bytes 786440 | tf_op jit(solution)/shard_map/ppermute | solution.py:13
  15.2 1.5 %slice_bitcast_fusion.7 = (bf16[1,3,8,128,128]{4,3,2,1,0:T(8,128)(2,1)}, bf16[1,3,8,128,128]{4,3,2,1,0:T(8,128)(2,1)}) fusion(bf16[4,8,128,128]{3,2,1,0:T(8,128)(2,1)S(1)} %get-tuple-element.16), kind=kLoop, calls=%fused_computation.64 | loop fusion | bytes 3145728 | tf_op jit(solution)/shard_map/concatenate | solution.py:31
  16.7 2.7 %slice_bitcast_fusion.1 = (f32[1,4,8,128,1]{4,3,2,1,0:T(8,128)}, f32[1,4,8,128,1]{4,3,2,1,0:T(8,128)}) fusion(f32[4,8,128,128]{3,2,1,0:T(8,128)S(1)} %get-tuple-element.15), kind=kLoop, calls=%fused_computation.27 | loop fusion | bytes 65536 | tf_op jit(solution)/shard_map/jit(_roll_static)/concatenate | solution.py:75
  19.5 2.7 %slice_bitcast_fusion = (f32[1,4,8,128,127]{4,3,2,1,0:T(8,128)}, f32[1,4,8,128,127]{4,3,2,1,0:T(8,128)}) fusion(f32[4,8,128,128]{3,2,1,0:T(8,128)S(1)} %get-tuple-element.15), kind=kLoop, calls=%fused_computation.26 | loop fusion | bytes 8323072 | tf_op jit(solution)/shard_map/jit(_roll_static)/concatenate | solution.py:75
  23.0 0.7 maximum_bitcast_fusion.2
  23.8 0.8 %fusion.55 = (f32[3,1,8,128]{3,2,1,0:T(8,128)S(1)}, f32[3,1,8,128]{3,2,1,0:T(8,128)S(1)}) fusion(f32[3,2,8,128]{3,2,1,0:T(8,128)} %collective-permute-done.5), kind=kLoop, calls=%fused_computation.129 | loop fusion | bytes 49152 | tf_op jit(solution)/shard_map/slice | solution.py:23
  24.6 0.7 %maximum_bitcast_fusion = (f32[4,8,128]{2,1,0:T(8,128)S(1)}, f32[4,8,128]{2,1,0:T(8,128)S(1)}, f32[4,8,128]{2,1,0:T(8,128)S(1)}, f32[4,8,128]{2,1,0:T(8,128)S(1)}) fusion(f32[3,3,8,128]{3,2,1,0:T(8,128)} %get-tuple-element.58, f32[3,1,8,128]{3,2,1,0:T(8,128)S(1)} %get-tuple-element.66, f32[3,1,8,128]{3,2,1,0:T(8,128)S(1)} %get-tuple-element.65, ...), kind=kLoop, calls=%fused_computation.97 | loop fusion | flops 16384 | bytes 163840 | tf_op jit(solution)/shard_map/mul | solution.py:83
  25.3 1.0 %slice_bitcast_fusion.11 = (bf16[1,4,1,128,128]{4,3,2,1,0:T(8,128)(2,1)S(1)}, bf16[1,4,1,128,128]{4,3,2,1,0:T(8,128)(2,1)S(1)}) fusion(bf16[4,2,128,128]{3,2,0,1:T(8,128)(2,1)} %collective-permute-done), kind=kLoop, calls=%fused_computation.78 | loop fusion | bytes 524288 | tf_op jit(solution)/shard_map/concatenate | solution.py:31
  26.4 5.7 %subtract_convert_fusion.2 = (bf16[1,4,8,128,128]{4,3,2,1,0:T(8,128)(2,1)}, f32[1,4,8,128,128]{4,3,2,1,0:T(8,128)S(1)}, f32[1,4,8,128,128]{4,3,2,1,0:T(8,128)S(1)}, bf16[1,4,8,128,128]{4,3,2,1,0:T(8,128)(2,1)}) fusion(f32[4,8,128]{2,1,0:T(8,128)} %get-tuple-element.47, f32[4,8,128]{2,1,0:T(8,128)} %get-tuple-element.48, ...), kind=kLoop, calls=%fused_computation.34 | loop fusion | flops 11010048 | bytes 14729216 | tf_op jit(solution)/shard_map/convert.3
  32.1 1.1 %fusion.7 = bf16[1,4,8,128,128]{4,3,2,1,0:T(8,128)(2,1)S(1)} fusion(f32[4,8,128]{2,1,0:T(8,128)S(1)} %get-tuple-element.45, f32[4,8,128]{2,1,0:T(8,128)S(1)} %get-tuple-element.69, f32[4,8,128]{2,1,0:T(8,128)S(1)} %get-tuple-element.56, f32[4,8,128]{2,1,0:T(8,128)S(1)} %get-tuple-element.71, bf16[1,3,8,128,128]{4,3,2,1,0:T(8,128)(2,1)S(1)} %copy-done.1, ...), kind=kLoop, calls=%fused_computation.19 | loop fusion | flops 9437184 | bytes 5308416 | tf_op jit(solution)/shard_map/convert.2
  33.3 1.0 %fusion.3 = bf16[1,4,8,128,128]{4,3,2,1,0:T(8,128)(2,1)S(1)} fusion(f32[1,4,8,128,128]{4,3,2,1,0:T(8,128)S(1)} %get-tuple-element.7, f32[1,4,8,128,128]{4,3,2,1,0:T(8,128)S(1)} %get-tuple-element.6, f32[4,8,128]{2,1,0:T(8,128)S(1)} %copy-done.17, f32[4,8,128]{2,1,0:T(8,128)S(1)} %copy-done.18, f32[4,8,128]{2,1,0:T(8,128)S(1)} %get-tuple-element.44, ...), kind=kLoop, calls=%fused_computation.15 | loop fusion | flops 7340032 | bytes 7405568 | tf_op jit(solution)/shard_map/convert
  34.4 2.5 %subtract_convert_fusion.1 = (bf16[1,4,8,128,128]{4,3,2,1,0:T(8,128)(2,1)}, bf16[1,4,8,128,128]{4,3,2,1,0:T(8,128)(2,1)S(1)}) fusion(f32[4,8,128]{2,1,0:T(8,128)S(1)} %copy-done.13, f32[4,8,128]{2,1,0:T(8,128)S(1)} %copy-done.14, f32[1,4,8,128,128]{4,3,2,1,0:T(8,128)S(1)} %get-tuple-element.6, f32[1,4,8,128,128]{4,3,2,1,0:T(8,128)S(1)} %get-tuple-element.7, ...), kind=kLoop, calls=%fused_computation.33 | loop fusion | flops 10485760 | bytes 8486912 | tf_op jit(solution)/shard_map/convert.4
  36.8 3.1 %broadcast_select_fusion = bf16[4,8,128,128]{3,2,1,0:T(8,128)(2,1)} fusion(bf16[4,8,128,128]{3,2,1,0:T(8,128)(2,1)} %collective-permute-done.2, pred[]{:T(512)S(6)} %eq.17, bf16[128,4,8,128]{3,2,1,0:T(8,128)(2,1)S(1)} %copy-done.3), kind=kLoop, calls=%fused_computation.58 | loop fusion | flops 524288 | bytes 3145729 | tf_op jit(solution)/shard_map/jit(_where)/select_n | solution.py:63
  39.9 2.2 %fusion.24 = f32[3,128,128]{1,2,0:T(8,128)S(1)} fusion(bf16[1,4,8,128,128]{4,3,2,1,0:T(8,128)(2,1)S(1)} %fusion.7, bf16[1,4,8,128,128]{4,3,2,1,0:T(8,128)(2,1)S(1)} %get-tuple-element.9, bf16[1,4,8,128,128]{4,3,2,1,0:T(8,128)(2,1)S(1)} %fusion.3, bf16[4,8,128,128]{3,2,1,0:T(8,128)(2,1)} %collective-permute-done.2), kind=kOutput, calls=%fused_computation.48 | convolution fusion | flops 405848064 | bytes 4390912 | tf_op jit(solution)/shard_map/xyjz,kxyiz->kji/dot_general | solution.py:94
  42.3 3.3 %fusion.19 = f32[3,128,128]{2,1,0:T(8,128)S(1)} fusion(bf16[4,8,128,128]{3,2,1,0:T(8,128)(2,1)} %collective-permute-done.2, bf16[1,4,8,128,128]{4,3,2,1,0:T(8,128)(2,1)} %get-tuple-element.10, bf16[1,4,8,128,128]{4,3,2,1,0:T(8,128)(2,1)} %get-tuple-element.8, bf16[1,4,8,128,128]{4,3,2,1,0:T(8,128)(2,1)} %get-tuple-element.5), kind=kOutput, calls=%fused_computation.42 | convolution fusion | flops 405848064 | bytes 4390912 | tf_op jit(solution)/shard_map/kxyjz,xyiz->kji/dot_general | solution.py:94
  45.7 2.2 %fusion.22 = f32[3,128,128]{1,2,0:T(8,128)S(1)} fusion(bf16[1,4,8,128,128]{4,3,2,1,0:T(8,128)(2,1)S(1)} %copy-done.7, bf16[1,4,8,128,128]{4,3,2,1,0:T(8,128)(2,1)S(1)} %copy-done.10, bf16[1,4,8,128,128]{4,3,2,1,0:T(8,128)(2,1)S(1)} %copy-done.5, bf16[4,8,128,128]{3,2,1,0:T(8,128)(2,1)} %collective-permute-done.3), kind=kOutput, calls=%fused_computation.46 | convolution fusion | flops 405848064 | bytes 4390912 | tf_op jit(solution)/shard_map/xyjz,kxyiz->kji/dot_general | solution.py:94
  48.0 3.1 %fusion.20 = f32[3,128,128]{2,1,0:T(8,128)S(1)} fusion(bf16[4,8,128,128]{3,2,1,0:T(8,128)(2,1)} %collective-permute-done.3, bf16[1,4,8,128,128]{4,3,2,1,0:T(8,128)(2,1)} %get-tuple-element.10, bf16[1,4,8,128,128]{4,3,2,1,0:T(8,128)(2,1)} %get-tuple-element.8, bf16[1,4,8,128,128]{4,3,2,1,0:T(8,128)(2,1)} %get-tuple-element.5), kind=kOutput, calls=%fused_computation.44 | convolution fusion | flops 405848064 | bytes 4390912 | tf_op jit(solution)/shard_map/kxyjz,xyiz->kji/dot_general | solution.py:94
  51.3 1.6 %collective-permute-start.6 = (f32[3,4,32,128]{3,2,1,0:T(8,128)S(1)}, f32[3,4,32,128]{3,2,1,0:T(8,128)S(1)}, u32[]{:S(2)}, u32[]{:S(2)}) collective-permute-start(f32[3,4,32,128]{3,2,1,0:T(8,128)S(1)} %bitcast.185), channel_id=1, source_target_pairs={{0,1},{1,0},{2,3},{3,2},{4,5},{5,4},{6,7},{7,6},{8,9},{9,8},{10,11... | collective-permute-start | bytes 589832 | tf_op jit(solution)/shard_map/ppermute | solution.py:48
  52.9 1.6 %collective-permute-start.7 = (f32[3,4,32,128]{3,2,1,0:T(8,128)S(1)}, f32[3,4,32,128]{3,2,1,0:T(8,128)S(1)}, u32[]{:S(2)}, u32[]{:S(2)}) collective-permute-start(f32[3,4,32,128]{3,2,1,0:T(8,128)S(1)} %bitcast.183), channel_id=1, source_target_pairs={{0,2},{1,3},{2,0},{3,1},{4,6},{5,7},{6,4},{7,5},{8,10},{9,11},{10,... | collective-permute-start | bytes 589832 | tf_op jit(solution)/shard_map/ppermute | solution.py:48
  55.1 1.0 %fusion.18 = f32[3,128,128]{2,1,0:T(8,128)S(1)} fusion(bf16[128,4,8,128]{3,2,1,0:T(8,128)(2,1)S(1)} %copy-done.3, bf16[1,4,8,128,128]{4,3,2,1,0:T(8,128)(2,1)S(1)} %copy-done.12, bf16[1,4,8,128,128]{4,3,2,1,0:T(8,128)(2,1)S(1)} %copy-done.8, bf16[1,4,8,128,128]{4,3,2,1,0:T(8,128)(2,1)S(1)} %copy-done.11), kind=kOutput, calls=%fused_computation.40 | convolution fusion | flops 405848064 | bytes 4390912 | tf_op jit(solution)/shard_map/kxyjz,xyiz->kji/dot_general | solution.py:94
  56.1 1.6 %collective-permute-start.11 = (f32[3,1,32,128]{3,2,1,0:T(8,128)S(1)}, f32[3,1,32,128]{3,2,1,0:T(8,128)S(1)}, u32[]{:S(2)}, u32[]{:S(2)}) collective-permute-start(f32[3,1,32,128]{3,2,1,0:T(8,128)S(1)} %get-tuple-element.35), channel_id=1, source_target_pairs={{0,1},{1,0},{2,3},{3,2},{4,5},{5,4},{6,7},{7,6},{8,9},{9,8},{10,11... | collective-permute-start | bytes 147464 | tf_op jit(solution)/shard_map/ppermute | solution.py:48
  57.7 1.5 %collective-permute-start.12 = (f32[3,1,32,128]{3,2,1,0:T(8,128)S(1)}, f32[3,1,32,128]{3,2,1,0:T(8,128)S(1)}, u32[]{:S(2)}, u32[]{:S(2)}) collective-permute-start(f32[3,1,32,128]{3,2,1,0:T(8,128)S(1)} %get-tuple-element.37), channel_id=1, source_target_pairs={{0,2},{1,3},{2,0},{3,1},{4,6},{5,7},{6,4},{7,5},{8,10},{9,11},{10,... | collective-permute-start | bytes 147464 | tf_op jit(solution)/shard_map/ppermute | solution.py:48
  59.2 2.4 %collective-permute-start.13 = (f32[3,1,32,128]{3,2,1,0:T(8,128)S(1)}, f32[3,1,32,128]{3,2,1,0:T(8,128)S(1)}, u32[]{:S(2)}, u32[]{:S(2)}) collective-permute-start(f32[3,1,32,128]{3,2,1,0:T(8,128)S(1)} %get-tuple-element.36), channel_id=1, source_target_pairs={{0,3},{1,2},{2,1},{3,0},{4,7},{5,6},{6,5},{7,4},{8,11},{9,10},{10,... | collective-permute-start | bytes 147464 | tf_op jit(solution)/shard_map/ppermute | solution.py:48
  61.5 3.3 %collective-permute-done.7 = f32[3,4,32,128]{3,2,1,0:T(8,128)S(1)} collective-permute-done((f32[3,4,32,128]{3,2,1,0:T(8,128)S(1)}, f32[3,4,32,128]{3,2,1,0:T(8,128)S(1)}, u32[]{:S(2)}, u32[]{:S(2)}) %collective-permute-start.7) | collective-permute-done | bytes 196640 | tf_op jit(solution)/shard_map/ppermute | solution.py:48
  65.1 1.3 %collective-permute-done.12 = f32[3,1,32,128]{3,2,1,0:T(8,128)S(1)} collective-permute-done((f32[3,1,32,128]{3,2,1,0:T(8,128)S(1)}, f32[3,1,32,128]{3,2,1,0:T(8,128)S(1)}, u32[]{:S(2)}, u32[]{:S(2)}) %collective-permute-start.12) | collective-permute-done | bytes 49184 | tf_op jit(solution)/shard_map/ppermute | solution.py:48
  66.4 4.5 %collective-permute-done.9 = f32[3,32,128]{2,1,0:T(8,128)S(1)} collective-permute-done((f32[3,32,128]{2,1,0:T(8,128)S(1)}, f32[3,32,128]{2,1,0:T(8,128)S(1)}, u32[]{:S(2)}, u32[]{:S(2)}) %collective-permute-start.9) | collective-permute-done | bytes 49184 | tf_op jit(solution)/shard_map/ppermute | solution.py:13
  70.9 0.7 pad_maximum_fusion.25
  (89 shorter events, 6.0 us)
Async XLA Ops:
  1.7 7.6 %copy-start.2 = (bf16[128,4,8,128]{3,2,1,0:T(8,128)(2,1)S(1)}, bf16[128,4,8,128]{3,2,1,0:T(8,128)(2,1)}, u32[]{:S(2)}) copy-start(bf16[128,4,8,128]{3,2,1,0:T(8,128)(2,1)} %param.3) | copy-start | bytes 3145732
  1.7 10.2 %copy-start.19 = (f32[3,4,8,128]{3,2,1,0:T(8,128)S(1)}, f32[3,4,8,128]{3,2,1,0:T(8,128)}, u32[]{:S(2)}) copy-start(f32[3,4,8,128]{3,2,1,0:T(8,128)} %param.5) | copy-start | bytes 147460
  1.7 10.2 %copy-start.20 = (f32[4,8,128]{2,1,0:T(8,128)S(1)}, f32[4,8,128]{2,1,0:T(8,128)}, u32[]{:S(2)}) copy-start(f32[4,8,128]{2,1,0:T(8,128)} %param.4) | copy-start | bytes 49156
  1.7 35.1 %collective-permute-start.2 = (bf16[4,8,128,128]{3,2,1,0:T(8,128)(2,1)S(1)}, bf16[4,8,128,128]{3,2,1,0:T(8,128)(2,1)}, u32[]{:S(2)}, u32[]{:S(2)}) collective-permute-start(bf16[4,8,128,128]{3,2,1,0:T(8,128)(2,1)S(1)} %get-tuple-element.16), channel_id=1, source_target_pairs={{8,0},{12,4},{16,8},{20,12},{24,16},{28,20},{0,24},{4,28},{9,1},{1... | collective-permute-start | bytes 3145736 | tf_op jit(solution)/shard_map/ppermute | solution.py:13
  7.7 18.6 %collective-permute-start.1 = (bf16[2,8,128,128]{3,2,1,0:T(8,128)(2,1)}, bf16[2,8,128,128]{3,2,1,0:T(8,128)(2,1)S(1)}, u32[]{:S(2)}, u32[]{:S(2)}) collective-permute-start(bf16[2,8,128,128]{3,2,1,0:T(8,128)(2,1)} %pad_maximum_fusion.23), channel_id=1, source_target_pairs={{2,0},{0,2},{3,1},{1,3},{6,4},{4,6},{7,5},{5,7},{10,8},{8,10},{11,... | collective-permute-start | bytes 1572872 | tf_op jit(solution)/shard_map/ppermute | solution.py:13
  10.4 15.0 %collective-permute-start = (bf16[4,2,128,128]{3,2,0,1:T(8,128)(2,1)}, bf16[4,2,128,128]{3,2,0,1:T(8,128)(2,1)}, u32[]{:S(2)}, u32[]{:S(2)}) collective-permute-start(bf16[4,2,128,128]{3,2,0,1:T(8,128)(2,1)} %pad_maximum_fusion.24), channel_id=1, source_target_pairs={{1,0},{0,1},{3,2},{2,3},{5,4},{4,5},{7,6},{6,7},{9,8},{8,9},{11,10... | collective-permute-start | bytes 786440 | tf_op jit(solution)/shard_map/ppermute | solution.py:13
  12.5 11.3 %collective-permute-start.5 = (f32[3,2,8,128]{3,2,1,0:T(8,128)}, f32[3,2,8,128]{3,2,1,0:T(8,128)}, u32[]{:S(2)}, u32[]{:S(2)}) collective-permute-start(f32[3,2,8,128]{3,2,1,0:T(8,128)} %pad_maximum_fusion.26), channel_id=1, source_target_pairs={{2,0},{0,2},{3,1},{1,3},{6,4},{4,6},{7,5},{5,7},{10,8},{8,10},{11,... | collective-permute-start | bytes 73736 | tf_op jit(solution)/shard_map/ppermute | solution.py:13
  13.6 10.1 %collective-permute-start.4 = (f32[3,4,2,128]{3,2,1,0:T(2,128)}, f32[3,4,2,128]{3,2,1,0:T(2,128)S(1)}, u32[]{:S(2)}, u32[]{:S(2)}) collective-permute-start(f32[3,4,2,128]{3,2,1,0:T(2,128)} %pad_maximum_fusion.33), channel_id=1, source_target_pairs={{1,0},{0,1},{3,2},{2,3},{5,4},{4,5},{7,6},{6,7},{9,8},{8,9},{11,10... | collective-permute-start | bytes 36872 | tf_op jit(solution)/shard_map/ppermute | solution.py:13
  23.7 2.7 %copy-start = (bf16[1,3,8,128,128]{4,3,2,1,0:T(8,128)(2,1)S(1)}, bf16[1,3,8,128,128]{4,3,2,1,0:T(8,128)(2,1)}, u32[]{:S(2)}) copy-start(bf16[1,3,8,128,128]{4,3,2,1,0:T(8,128)(2,1)} %get-tuple-element.21) | copy-start | bytes 2359300
  23.7 2.7 %copy-start.1 = (bf16[1,3,8,128,128]{4,3,2,1,0:T(8,128)(2,1)S(1)}, bf16[1,3,8,128,128]{4,3,2,1,0:T(8,128)(2,1)}, u32[]{:S(2)}) copy-start(bf16[1,3,8,128,128]{4,3,2,1,0:T(8,128)(2,1)} %get-tuple-element.22) | copy-start | bytes 2359300
  32.1 1.2 %copy-start.17 = (f32[4,8,128]{2,1,0:T(8,128)S(1)}, f32[4,8,128]{2,1,0:T(8,128)}, u32[]{:S(2)}) copy-start(f32[4,8,128]{2,1,0:T(8,128)} %get-tuple-element.40) | copy-start | bytes 49156
  32.1 1.2 %copy-start.18 = (f32[4,8,128]{2,1,0:T(8,128)S(1)}, f32[4,8,128]{2,1,0:T(8,128)}, u32[]{:S(2)}) copy-start(f32[4,8,128]{2,1,0:T(8,128)} %get-tuple-element.74) | copy-start | bytes 49156
  33.2 6.7 %copy-start.6 = (bf16[1,4,8,128,128]{4,3,2,1,0:T(8,128)(2,1)}, bf16[1,4,8,128,128]{4,3,2,1,0:T(8,128)(2,1)S(1)}, u32[]{:S(2)}) copy-start(bf16[1,4,8,128,128]{4,3,2,1,0:T(8,128)(2,1)S(1)} %fusion.7) | copy-start | bytes 3145732
  33.3 1.1 %copy-start.13 = (f32[4,8,128]{2,1,0:T(8,128)S(1)}, f32[4,8,128]{2,1,0:T(8,128)}, u32[]{:S(2)}) copy-start(f32[4,8,128]{2,1,0:T(8,128)} %get-tuple-element.46) | copy-start | bytes 49156
  34.3 5.6 %copy-start.4 = (bf16[1,4,8,128,128]{4,3,2,1,0:T(8,128)(2,1)}, bf16[1,4,8,128,128]{4,3,2,1,0:T(8,128)(2,1)S(1)}, u32[]{:S(2)}) copy-start(bf16[1,4,8,128,128]{4,3,2,1,0:T(8,128)(2,1)S(1)} %fusion.3) | copy-start | bytes 3145732
  34.4 2.5 %copy-start.3 = (bf16[128,4,8,128]{3,2,1,0:T(8,128)(2,1)S(1)}, bf16[128,4,8,128]{3,2,1,0:T(8,128)(2,1)}, u32[]{:S(2)}) copy-start(bf16[128,4,8,128]{3,2,1,0:T(8,128)(2,1)} %param.3) | copy-start | bytes 3145732
  36.8 3.1 %copy-start.9 = (bf16[1,4,8,128,128]{4,3,2,1,0:T(8,128)(2,1)}, bf16[1,4,8,128,128]{4,3,2,1,0:T(8,128)(2,1)S(1)}, u32[]{:S(2)}) copy-start(bf16[1,4,8,128,128]{4,3,2,1,0:T(8,128)(2,1)S(1)} %get-tuple-element.9) | copy-start | bytes 3145732
  39.9 5.7 %collective-permute-start.3 = (bf16[4,8,128,128]{3,2,1,0:T(8,128)(2,1)}, bf16[4,8,128,128]{3,2,1,0:T(8,128)(2,1)}, u32[]{:S(2)}, u32[]{:S(2)}) collective-permute-start(bf16[4,8,128,128]{3,2,1,0:T(8,128)(2,1)} %broadcast_select_fusion), channel_id=1, source_target_pairs={{0,4},{4,0},{8,12},{12,8},{16,20},{20,16},{24,28},{28,24},{1,5},{5... | collective-permute-start | bytes 3145736 | tf_op jit(solution)/shard_map/ppermute | solution.py:62
  42.3 3.3 %copy-start.5 = (bf16[1,4,8,128,128]{4,3,2,1,0:T(8,128)(2,1)S(1)}, bf16[1,4,8,128,128]{4,3,2,1,0:T(8,128)(2,1)}, u32[]{:S(2)}) copy-start(bf16[1,4,8,128,128]{4,3,2,1,0:T(8,128)(2,1)} %copy-done.4) | copy-start | bytes 3145732
  42.3 3.3 %copy-start.7 = (bf16[1,4,8,128,128]{4,3,2,1,0:T(8,128)(2,1)S(1)}, bf16[1,4,8,128,128]{4,3,2,1,0:T(8,128)(2,1)}, u32[]{:S(2)}) copy-start(bf16[1,4,8,128,128]{4,3,2,1,0:T(8,128)(2,1)} %copy-done.6) | copy-start | bytes 3145732
  42.3 3.3 %copy-start.10 = (bf16[1,4,8,128,128]{4,3,2,1,0:T(8,128)(2,1)S(1)}, bf16[1,4,8,128,128]{4,3,2,1,0:T(8,128)(2,1)}, u32[]{:S(2)}) copy-start(bf16[1,4,8,128,128]{4,3,2,1,0:T(8,128)(2,1)} %copy-done.9) | copy-start | bytes 3145732
  51.1 3.9 %copy-start.8 = (bf16[1,4,8,128,128]{4,3,2,1,0:T(8,128)(2,1)S(1)}, bf16[1,4,8,128,128]{4,3,2,1,0:T(8,128)(2,1)}, u32[]{:S(2)}) copy-start(bf16[1,4,8,128,128]{4,3,2,1,0:T(8,128)(2,1)} %get-tuple-element.8) | copy-start | bytes 3145732
  51.1 3.9 %copy-start.11 = (bf16[1,4,8,128,128]{4,3,2,1,0:T(8,128)(2,1)S(1)}, bf16[1,4,8,128,128]{4,3,2,1,0:T(8,128)(2,1)}, u32[]{:S(2)}) copy-start(bf16[1,4,8,128,128]{4,3,2,1,0:T(8,128)(2,1)} %get-tuple-element.5) | copy-start | bytes 3145732
  51.2 3.9 %copy-start.12 = (bf16[1,4,8,128,128]{4,3,2,1,0:T(8,128)(2,1)S(1)}, bf16[1,4,8,128,128]{4,3,2,1,0:T(8,128)(2,1)}, u32[]{:S(2)}) copy-start(bf16[1,4,8,128,128]{4,3,2,1,0:T(8,128)(2,1)} %get-tuple-element.10) | copy-start | bytes 3145732
  51.3 7.8 %collective-permute-start.6 = (f32[3,4,32,128]{3,2,1,0:T(8,128)S(1)}, f32[3,4,32,128]{3,2,1,0:T(8,128)S(1)}, u32[]{:S(2)}, u32[]{:S(2)}) collective-permute-start(f32[3,4,32,128]{3,2,1,0:T(8,128)S(1)} %bitcast.185), channel_id=1, source_target_pairs={{0,1},{1,0},{2,3},{3,2},{4,5},{5,4},{6,7},{7,6},{8,9},{9,8},{10,11... | collective-permute-start | bytes 589832 | tf_op jit(solution)/shard_map/ppermute | solution.py:48
  52.9 11.9 %collective-permute-start.7 = (f32[3,4,32,128]{3,2,1,0:T(8,128)S(1)}, f32[3,4,32,128]{3,2,1,0:T(8,128)S(1)}, u32[]{:S(2)}, u32[]{:S(2)}) collective-permute-start(f32[3,4,32,128]{3,2,1,0:T(8,128)S(1)} %bitcast.183), channel_id=1, source_target_pairs={{0,2},{1,3},{2,0},{3,1},{4,6},{5,7},{6,4},{7,5},{8,10},{9,11},{10,... | collective-permute-start | bytes 589832 | tf_op jit(solution)/shard_map/ppermute | solution.py:48
  54.5 10.3 %collective-permute-start.8 = (f32[3,4,32,128]{3,2,1,0:T(8,128)S(1)}, f32[3,4,32,128]{3,2,1,0:T(8,128)S(1)}, u32[]{:S(2)}, u32[]{:S(2)}) collective-permute-start(f32[3,4,32,128]{3,2,1,0:T(8,128)S(1)} %bitcast.184), channel_id=1, source_target_pairs={{0,3},{1,2},{2,1},{3,0},{4,7},{5,6},{6,5},{7,4},{8,11},{9,10},{10,... | collective-permute-start | bytes 589832 | tf_op jit(solution)/shard_map/ppermute | solution.py:48
  56.1 9.0 %collective-permute-start.11 = (f32[3,1,32,128]{3,2,1,0:T(8,128)S(1)}, f32[3,1,32,128]{3,2,1,0:T(8,128)S(1)}, u32[]{:S(2)}, u32[]{:S(2)}) collective-permute-start(f32[3,1,32,128]{3,2,1,0:T(8,128)S(1)} %get-tuple-element.35), channel_id=1, source_target_pairs={{0,1},{1,0},{2,3},{3,2},{4,5},{5,4},{6,7},{7,6},{8,9},{9,8},{10,11... | collective-permute-start | bytes 147464 | tf_op jit(solution)/shard_map/ppermute | solution.py:48
  57.7 8.7 %collective-permute-start.12 = (f32[3,1,32,128]{3,2,1,0:T(8,128)S(1)}, f32[3,1,32,128]{3,2,1,0:T(8,128)S(1)}, u32[]{:S(2)}, u32[]{:S(2)}) collective-permute-start(f32[3,1,32,128]{3,2,1,0:T(8,128)S(1)} %get-tuple-element.37), channel_id=1, source_target_pairs={{0,2},{1,3},{2,0},{3,1},{4,6},{5,7},{6,4},{7,5},{8,10},{9,11},{10,... | collective-permute-start | bytes 147464 | tf_op jit(solution)/shard_map/ppermute | solution.py:48
  59.2 7.1 %collective-permute-start.13 = (f32[3,1,32,128]{3,2,1,0:T(8,128)S(1)}, f32[3,1,32,128]{3,2,1,0:T(8,128)S(1)}, u32[]{:S(2)}, u32[]{:S(2)}) collective-permute-start(f32[3,1,32,128]{3,2,1,0:T(8,128)S(1)} %get-tuple-element.36), channel_id=1, source_target_pairs={{0,3},{1,2},{2,1},{3,0},{4,7},{5,6},{6,5},{7,4},{8,11},{9,10},{10,... | collective-permute-start | bytes 147464 | tf_op jit(solution)/shard_map/ppermute | solution.py:48
  64.9 6.0 %collective-permute-start.9 = (f32[3,32,128]{2,1,0:T(8,128)S(1)}, f32[3,32,128]{2,1,0:T(8,128)S(1)}, u32[]{:S(2)}, u32[]{:S(2)}) collective-permute-start(f32[3,32,128]{2,1,0:T(8,128)S(1)} %get-tuple-element.33), channel_id=1, source_target_pairs={{24,0},{28,4},{0,8},{4,12},{8,16},{12,20},{16,24},{20,28},{25,1},{... | collective-permute-start | bytes 147464 | tf_op jit(solution)/shard_map/ppermute | solution.py:13
  65.0 5.9 %collective-permute-start.10 = (f32[3,32,128]{2,1,0:T(8,128)S(1)}, f32[3,32,128]{2,1,0:T(8,128)S(1)}, u32[]{:S(2)}, u32[]{:S(2)}) collective-permute-start(f32[3,32,128]{2,1,0:T(8,128)S(1)} %get-tuple-element.34), channel_id=1, source_target_pairs={{28,0},{0,4},{4,8},{8,12},{12,16},{16,20},{20,24},{24,28},{29,1},{... | collective-permute-start | bytes 147464 | tf_op jit(solution)/shard_map/ppermute | solution.py:13
  (3 other events, 3.2 us)

commit v2 on v0

v2 whole, which is shorter than its diff:
```python
import functools
import math

import jax
import jax.numpy as jnp
from jax import lax
from jax.experimental import pallas as pl
from jax.experimental.pallas import tpu as pltpu
from jax.sharding import PartitionSpec as P

F32, BF16 = jnp.float32, jnp.bfloat16
VMEM = pl.BlockSpec(memory_space=pltpu.VMEM)
SMEM = pl.BlockSpec(memory_space=pltpu.SMEM)
LIMIT = 24 * 1024 * 1024
NT = (((1,), (1,)), ((), ()))
CHUNK = 16


def shift(block, axis, distance):
    count = lax.axis_size(axis)
    return lax.ppermute(block, axis, [((i + distance) % count, i) for i in range(count)])


def both_sides(tail_head, coeff, axis):
    if lax.axis_size(axis) == 2:
        other = shift(coeff, axis, 1)
        return shift(tail_head, axis, 1), other, other
    tail, head = jnp.split(tail_head, 2, axis=1)
    pair = jnp.concatenate([shift(tail, axis, -1), shift(head, axis, 1)], axis=1)
    return pair, shift(coeff, axis, -1), shift(coeff, axis, 1)


def call(body, outs, operands, scratch=(), flops=0, scalars=0):
    specs = [SMEM] * scalars + [VMEM] * (len(operands) - scalars)
    moved = sum(math.prod(a.shape) * a.dtype.itemsize for a in [*outs, *operands])
    return pl.pallas_call(
        body,
        out_shape=outs,
        in_specs=specs,
        out_specs=[VMEM] * len(outs),
        scratch_shapes=list(scratch),
        compiler_params=pltpu.CompilerParams(vmem_limit_bytes=LIMIT),
        cost_estimate=pl.CostEstimate(flops=flops, bytes_accessed=moved, transcendentals=0),
    )(*operands)


def destinations(me, nx, ny):
    x, y = me // ny, me % ny
    return [((x + ox) % nx) * ny + (y + oy) % ny for ox in range(nx) for oy in range(ny)]


def edges(psi, coupling, pot_grad, hx, hy, c, *, shape):
    wx, wy, wz = shape
    layer = wy * wz
    hx[:, :layer] = psi[:, (wx - 1) * layer :]
    hx[:, layer:] = psi[:, :layer]
    for x in range(wx):
        for side, y in enumerate((wy - 1, 0)):
            to, at = (side * wx + x) * wz, x * layer + y * wz
            hy[:, to : to + wz] = psi[:, at : at + wz]
    c[...] = coupling[...][None] * pot_grad[...]


def operators(
    me_ref, psi, hx, hy, c, cxb, cxa, cyb, cya, u, w, keep, *rest, shape, plane, scale
):
    wx, wy, wz = shape
    sends, (half, back, ahead, acc) = rest[:-4], rest[-4:]
    states = psi.shape[0]
    rows = states // math.prod(plane)
    layer = wy * wz
    half[...] = 0.5 * c[...]
    for k in range(3):
        for x in range(wx):
            back[k, x] = pltpu.roll(half[k, x], 1, 1)
            ahead[k, x] = pltpu.roll(half[k, x], wz - 1, 1)

    def coeff(k, x, y):
        if x < 0:
            return 0.5 * cxb[k, wx - 1, y : y + 1, :]
        if x >= wx:
            return 0.5 * cxa[k, 0, y : y + 1, :]
        if y < 0:
            return 0.5 * cyb[k, x, wy - 1 : wy, :]
        if y >= wy:
            return 0.5 * cya[k, x, 0:1, :]
        return half[k, x, y : y + 1, :]

    def group(step, _):
        r = pl.ds(pl.multiple_of(step * CHUNK, CHUNK), CHUNK)

        def field(x, y):
            if x < 0:
                ref, at = hx, y * wz
            elif x >= wx:
                ref, at = hx, layer + y * wz
            elif y < 0:
                ref, at = hy, x * wz
            elif y >= wy:
                ref, at = hy, (wx + x) * wz
            else:
                ref, at = psi, x * layer + y * wz
            return ref[r, at : at + wz].astype(F32)

        for x in range(wx):
            for y in range(wy):
                here = field(x, y)
                xb, xa = field(x - 1, y), field(x + 1, y)
                yb, ya = field(x, y - 1), field(x, y + 1)
                zb, za = pltpu.roll(here, 1, 1), pltpu.roll(here, wz - 1, 1)
                gx, gy, gz = xa - xb, ya - yb, za - zb
                c1, c2, c3 = [coeff(k, x, y) for k in range(3)]
                at = x * layer + y * wz
                cols = slice(at, at + wz)

                def put(ref, k, value):
                    place = pl.ds(pl.multiple_of(k * states + step * CHUNK, CHUNK), CHUNK)
                    ref[place, cols] = value.astype(BF16)

                put(u, 0, c2 * gz - c3 * gy)
                put(u, 1, c3 * gx - c1 * gz)
                put(u, 2, c1 * gy - c2 * gx)

                def dx(k):
                    return coeff(k, x + 1, y) * xa - coeff(k, x - 1, y) * xb

                def dy(k):
                    return coeff(k, x, y + 1) * ya - coeff(k, x, y - 1) * yb

                def dz(k):
                    return ahead[k, x, y : y + 1, :] * za - back[k, x, y : y + 1, :] * zb

                put(w, 0, dy(2) - dz(1))
                put(w, 1, dz(0) - dx(2))
                put(w, 2, dx(1) - dy(0))
        return 0

    lax.fori_loop(0, states // CHUNK, group, 0)
    acc[...] = lax.dot_general(u[...], psi[...], NT, preferred_element_type=F32) * scale
    for ref, dest in zip((keep, *sends), destinations(me_ref[0], *plane)):
        for k in range(3):
            place = pl.ds(pl.multiple_of(k * states + dest * rows, rows), rows)
            ref[k] = acc[place, :].astype(ref.dtype)


def tiles(me_ref, u, w, one, two, keep, *rest, plane, scale):
    sends, (up, down) = rest[:-2], rest[-2:]
    states = one.shape[0]
    rows = states // math.prod(plane)
    for t, panel in enumerate((one, two)):
        up[t] = lax.dot_general(u[...], panel[...], NT, preferred_element_type=F32) * scale
        down[t] = lax.dot_general(panel[...], w[...], NT, preferred_element_type=F32) * scale
    for ref, dest in zip((keep, *sends), destinations(me_ref[0], *plane)):
        for t in range(2):
            for k in range(3):
                place = pl.ds(pl.multiple_of(k * states + dest * rows, rows), rows)
                ref[t, k] = up[t, place, :].astype(ref.dtype)
                place = pl.ds(pl.multiple_of(dest * rows, rows), rows)
                cols = slice(k * states, (k + 1) * states)
                ref[2 + t, k] = down[t, place, cols].astype(ref.dtype)


def add_down(keep, *rest):
    parts, (one, two) = rest[:-2], rest[-2:]
    for t, ref in enumerate((one, two)):
        total = keep[2 + t]
        for part in parts:
            total = total + part[2 + t].astype(F32)
        ref[...] = total


def assemble(count, *refs):
    keep, parts = refs[0], refs[1:count]
    mine, own_parts = refs[count], refs[count + 1 : 2 * count]
    one, two, out = refs[2 * count :]
    for k in range(3):
        out[k, 0] = two[k]
        out[k, 1] = one[k]
        total = mine[k]
        for part in own_parts:
            total = total + part[k].astype(F32)
        out[k, 2] = total
        for t in range(2):
            total = keep[t, k]
            for part in parts:
                total = total + part[t, k].astype(F32)
            out[k, 3 + t] = total


def exchange(sends):
    nx, ny = lax.axis_size("dx"), lax.axis_size("dy")
    got = []
    for o, piece in enumerate(sends, 1):
        ox, oy = o // ny, o % ny
        route = [
            (i * ny + j, ((i + ox) % nx) * ny + (j + oy) % ny) for i in range(nx) for j in range(ny)
        ]
        got.append(lax.ppermute(piece, ("dx", "dy"), route))
    return got


def on_device(orbitals, coupling, pot_grad):
    states, wx, wy, wz = orbitals.shape
    plane = (lax.axis_size("dx"), lax.axis_size("dy"))
    places = math.prod(plane)
    rows = states // places
    layer = wy * wz
    cells = wx * layer
    scale = 1.0 / math.sqrt(cells * places)
    me = lax.axis_index(("dx", "dy")).astype(jnp.int32).reshape(1)
    psi = lax.optimization_barrier(orbitals.reshape(states, cells))
    two = shift(psi, "blk", 2)

    hx, hy, coeff = call(
        functools.partial(edges, shape=(wx, wy, wz)),
        [
            jax.ShapeDtypeStruct((states, 2 * layer), BF16),
            jax.ShapeDtypeStruct((states, 2 * wx * wz), BF16),
            jax.ShapeDtypeStruct((3, wx, wy, wz), F32),
        ],
        [psi, coupling, pot_grad],
    )
    hx, cxb, cxa = both_sides(hx, coeff, "dx")
    hy, cyb, cya = both_sides(hy, coeff, "dy")

    field = jax.ShapeDtypeStruct((3 * states, cells), BF16)
    small = (3, rows, states)
    u, w, mine, *own_sends = call(
        functools.partial(operators, shape=(wx, wy, wz), plane=plane, scale=scale),
        [field, field, jax.ShapeDtypeStruct(small, F32)]
        + [jax.ShapeDtypeStruct(small, BF16)] * (places - 1),
        [me, psi, hx, hy, coeff, cxb, cxa, cyb, cya],
        scratch=[pltpu.VMEM((3, wx, wy, wz), F32)] * 3 + [pltpu.VMEM((3 * states, states), F32)],
        flops=2 * 3 * states * states * cells,
        scalars=1,
    )
    own_parts = exchange(own_sends)

    two, u, own_parts = lax.optimization_barrier((two, u, own_parts))
    core = lax.axis_index("blk") % 2
    swap = [(i, i ^ 1) for i in range(lax.axis_size("blk"))]
    one = lax.ppermute(jnp.where(core == 0, two, psi), "blk", swap)
    keep, *sends = call(
        functools.partial(tiles, plane=plane, scale=scale),
        [jax.ShapeDtypeStruct((4, *small), F32)]
        + [jax.ShapeDtypeStruct((4, *small), BF16)] * (places - 1),
        [me, u, w, one, two],
        scratch=[pltpu.VMEM((2, 3 * states, states), F32), pltpu.VMEM((2, states, 3 * states), F32)],
        flops=4 * 2 * 3 * states * states * cells,
        scalars=1,
    )
    parts = exchange(sends)
    down = [jax.ShapeDtypeStruct(small, F32)] * 2
    from_one, from_two = call(add_down, down, [keep, *parts])
    from_one = shift(from_one, "blk", -1)
    from_two = shift(from_two, "blk", -2)
    (out,) = call(
        functools.partial(assemble, places),
        [jax.ShapeDtypeStruct((3, 5, rows, states), F32)],
        [keep, *parts, mine, *own_parts, from_one, from_two],
    )
    return out


def solution(mesh):
    in_specs = (P("blk", "dx", "dy", None), P("dx", "dy", None), P(None, "dx", "dy", None))
    out_specs = P(None, None, ("blk", "dx", "dy"), None)
    return jax.shard_map(
        on_device, mesh=mesh, in_specs=in_specs, out_specs=out_specs, check_vma=False
    )
```

time: 104 us -> 62.7 us (0.60)
  waiting for transfers between devices: 63.5 us -> 27.5 us
  between operations: 13.6 us -> 0.08 us
  Pallas kernels: 0 us -> 9.91 us
  matrix products: 4.88 us -> 0 us
  starting transfers between devices: 12.4 us -> 16.4 us
  other arithmetic: 3.52 us -> 0.11 us
  local copies, waits for them, and re-layouts: 5.94 us -> 8.38 us
    reduce_scatter x1 -> x0, waiting for transfers between devices: 35.6 us -> none  [on_device(): lax.psum_scatter(stacked, ('dx', 'dy'), scatter_dimension=2, tiled=True)]
    pallas_call x0 -> x5, Pallas kernels: none -> 9.91 us  [call(): pl.pallas_call(body, out_shape=outs, in_specs=specs, out_specs=[VMEM] * l...]
    unnamed x10 -> x13, local copies, waits for them, and re-layouts: 2.7 us -> 8.38 us
    dot_general x5 -> x0, matrix products: 4.88 us -> none  [make_tile(): jnp.einsum('kjc,ic->kji', cross_field, rows_flat, preferred_element_type=...]
    ppermute x8 -> x14, starting transfers between devices: 12.4 us -> 16.4 us  [the longest x7 9.27 us: shift(): lax.ppermute(block, axis, [((i + distance) % count, i) for i in range(cou...]
    another operation x2 -> x0, other arithmetic: 3 us -> none  [on_device(): jnp.stack([cross_one, cross_two, cross_three]).astype(jnp.bfloat16)]
    reduce_scatter x1 -> x0, local copies, waits for them, and re-layouts: 1.65 us -> none  [on_device(): lax.psum_scatter(stacked, ('dx', 'dy'), scatter_dimension=2, tiled=True)]
    slice x4 -> x0, local copies, waits for them, and re-layouts: 1.56 us -> none  [the longest x2 1.49 us: on_device(): jnp.roll(field_f32, -1, axis=3) - jnp.roll(field_f32, 1, axis=3)]
  transfers between devices with their start and end apart: 9 -> 14, of which waited for: 5 -> 10; matrix products, arithmetic and copies ran while one was open for 9% -> 0% of each run, Pallas kernels for 0% -> 9%
where the time goes in v2:
time: 62.7 us; the launch traced here: 62.4 us
  waiting for transfers between devices  27.5 us (44%)
  starting transfers between devices  16.4 us (26%)
  Pallas kernels  9.91 us (16%)
  local copies, waits for them, and re-layouts  8.38 us (13%)
    ppermute x7, waiting for transfers between devices, shift(): lax.ppermute(block, axis, [((i + distance) % count, i) for i in range(cou...  16.9 us
    pallas_call x5, Pallas kernels, call(): pl.pallas_call(body, out_shape=outs, in_specs=specs, out_specs=[VMEM] * l...  9.91 us
    ppermute x7, starting transfers between devices, shift(): lax.ppermute(block, axis, [((i + distance) % count, i) for i in range(cou...  9.27 us
    unnamed x13, local copies, waits for them, and re-layouts  8.38 us
    ppermute x6, waiting for transfers between devices, exchange(): got.append(lax.ppermute(piece, ('dx', 'dy'), route))  8.01 us
    ppermute x6, starting transfers between devices, exchange(): got.append(lax.ppermute(piece, ('dx', 'dy'), route))  7.04 us
    ppermute x1, waiting for transfers between devices, on_device(): one = lax.ppermute(jnp.where(core == 0, two, psi), 'blk', swap)  2.65 us
  transfers between devices with their start and end apart: 14, of which 10 were waited for; matrix products, arithmetic and copies ran while one was open for 0% of the time, Pallas kernels for 9%

profile of v2, /device:TPU:0, one launch (start us, length us, event | category | flops | bytes accessed | tf_op | source)
XLA Modules:
  0.0 62.4 jit_solution(10671096157017742823)
XLA Ops:
  0.0 1.7 %copy.6 = bf16[16,8,32,128]{3,1,2,0:T(8,128)(2,1)S(1)} copy(bf16[16,8,32,128]{3,2,1,0:T(8,128)(2,1)} %bitcast.10) | data formatting | bytes 2097152
  1.7 5.1 %collective-permute-start = (bf16[128,4096]{1,0:T(8,128)(2,1)S(1)}, bf16[128,4096]{1,0:T(8,128)(2,1)S(1)}, u32[]{:S(2)}, u32[]{:S(2)}) collective-permute-start(bf16[128,4096]{1,0:T(8,128)(2,1)S(1)} %bitcast.6), channel_id=1, source_target_pairs={{8,0},{12,4},{16,8},{20,12},{24,16},{28,20},{0,24},{4,28},{9,1},{1... | collective-permute-start | bytes 3145736 | tf_op jit(solution)/shard_map/ppermute | solution.py:21
  6.8 0.8 %copy-done.4 = f32[3,4,8,128]{3,2,1,0:T(8,128)S(1)} copy-done((f32[3,4,8,128]{3,2,1,0:T(8,128)S(1)}, f32[3,4,8,128]{3,2,1,0:T(8,128)}, u32[]{:S(2)}) %copy-start.4) | copy-done | bytes 49176
  7.6 0.7 %copy-done.5 = f32[4,8,128]{2,1,0:T(8,128)S(1)} copy-done((f32[4,8,128]{2,1,0:T(8,128)S(1)}, f32[4,8,128]{2,1,0:T(8,128)}, u32[]{:S(2)}) %copy-start.5) | copy-done | bytes 16408
  8.3 0.9 %shard_map.37 = (bf16[128,2048]{1,0:T(8,128)(2,1)}, bf16[128,1024]{1,0:T(8,128)(2,1)S(1)}, f32[3,4,8,128]{3,2,1,0:T(8,128)S(1)}) custom-call(bf16[128,4096]{1,0:T(8,128)(2,1)S(1)} %bitcast.7, f32[4,8,128]{2,1,0:T(8,128)S(1)} %copy-done.5, f32[3,4,8,128]{3,2,1,0:T(8,128)S(1)} %copy-done.4), custom_call_target="tpu_custom_call" | custom-call | bytes 1949696 | tf_op jit(solution)/shard_map/pallas_call | solution.py:36
  9.2 1.5 %collective-permute-start.1 = (bf16[128,2048]{1,0:T(8,128)(2,1)}, bf16[128,2048]{1,0:T(8,128)(2,1)S(1)}, u32[]{:S(2)}, u32[]{:S(2)}) collective-permute-start(bf16[128,2048]{1,0:T(8,128)(2,1)} %get-tuple-element.25), channel_id=1, source_target_pairs={{2,0},{0,2},{3,1},{1,3},{6,4},{4,6},{7,5},{5,7},{10,8},{8,10},{11,... | collective-permute-start | bytes 1572872 | tf_op jit(solution)/shard_map/ppermute | solution.py:21
  10.7 1.5 %collective-permute-start.2 = (bf16[128,1024]{1,0:T(8,128)(2,1)S(1)}, bf16[128,1024]{1,0:T(8,128)(2,1)S(1)}, u32[]{:S(2)}, u32[]{:S(2)}) collective-permute-start(bf16[128,1024]{1,0:T(8,128)(2,1)S(1)} %get-tuple-element.26), channel_id=1, source_target_pairs={{1,0},{0,1},{3,2},{2,3},{5,4},{4,5},{7,6},{6,7},{9,8},{8,9},{11,10... | collective-permute-start | bytes 786440 | tf_op jit(solution)/shard_map/ppermute | solution.py:21
  12.2 0.5 collective-permute-start.4
  12.7 0.5 collective-permute-start.3
  13.2 6.0 %collective-permute-done.4.cyb.cya = f32[3,4,8,128]{3,2,1,0:T(8,128)S(1)} collective-permute-done((f32[3,4,8,128]{3,2,1,0:T(8,128)S(1)}, f32[3,4,8,128]{3,2,1,0:T(8,128)S(1)}, u32[]{:S(2)}, u32[]{:S(2)}) %collective-permute-start.4) | collective-permute-done | bytes 49184 | tf_op jit(solution)/shard_map/ppermute | solution.py:21
  19.2 4.6 %collective-permute-done.3.cxb.cxa = f32[3,4,8,128]{3,2,1,0:T(8,128)S(1)} collective-permute-done((f32[3,4,8,128]{3,2,1,0:T(8,128)S(1)}, f32[3,4,8,128]{3,2,1,0:T(8,128)S(1)}, u32[]{:S(2)}, u32[]{:S(2)}) %collective-permute-start.3) | collective-permute-done | bytes 49184 | tf_op jit(solution)/shard_map/ppermute | solution.py:21
  23.8 4.7 %shard_map.38 = (bf16[384,4096]{1,0:T(8,128)(2,1)S(1)}, bf16[384,4096]{1,0:T(8,128)(2,1)S(1)}, f32[3,32,128]{2,1,0:T(8,128)S(1)}, bf16[3,32,128]{2,1,0:T(8,128)(...) custom-call(s32[1]{0:T(128)} %bitcast.me_ref, bf16[128,4096]{1,0:T(8,128)(2,1)S(1)} %bitcast.8, ...), custom_call_target="tpu_custom_call" | custom-call | flops 402653184 | bytes 8495108 | tf_op jit(solution)/shard_map/pallas_call | solution.py:36
  28.6 1.6 %copy-done = bf16[384,4096]{1,0:T(8,128)(2,1)} copy-done((bf16[384,4096]{1,0:T(8,128)(2,1)}, bf16[384,4096]{1,0:T(8,128)(2,1)S(1)}, u32[]{:S(2)}) %copy-start) | copy-done | bytes 3145752
  30.2 1.7 %copy-done.2 = bf16[384,4096]{1,0:T(8,128)(2,1)} copy-done((bf16[384,4096]{1,0:T(8,128)(2,1)}, bf16[384,4096]{1,0:T(8,128)(2,1)S(1)}, u32[]{:S(2)}) %copy-start.2) | copy-done | bytes 3145752
  31.9 1.5 %collective-permute-start.5 = (bf16[3,32,128]{2,1,0:T(8,128)(2,1)S(1)}, bf16[3,32,128]{2,1,0:T(8,128)(2,1)S(1)}, u32[]{:S(2)}, u32[]{:S(2)}) collective-permute-start(bf16[3,32,128]{2,1,0:T(8,128)(2,1)S(1)} %get-tuple-element.29), channel_id=1, source_target_pairs={{0,1},{1,0},{2,3},{3,2},{4,5},{5,4},{6,7},{7,6},{8,9},{9,8},{10,11... | collective-permute-start | bytes 73736 | tf_op jit(solution)/shard_map/ppermute | solution.py:198
  33.3 1.5 %collective-permute-start.6 = (bf16[3,32,128]{2,1,0:T(8,128)(2,1)S(1)}, bf16[3,32,128]{2,1,0:T(8,128)(2,1)S(1)}, u32[]{:S(2)}, u32[]{:S(2)}) collective-permute-start(bf16[3,32,128]{2,1,0:T(8,128)(2,1)S(1)} %get-tuple-element.30), channel_id=1, source_target_pairs={{0,2},{1,3},{2,0},{3,1},{4,6},{5,7},{6,4},{7,5},{8,10},{9,11},{10,... | collective-permute-start | bytes 73736 | tf_op jit(solution)/shard_map/ppermute | solution.py:198
  34.9 0.5 collective-permute-start.7
  35.3 0.5 collective-permute-done.5.refs_5_
  35.9 1.3 %collective-permute-done.6.refs_6_ = bf16[3,32,128]{2,1,0:T(8,128)(2,1)S(1)} collective-permute-done((bf16[3,32,128]{2,1,0:T(8,128)(2,1)S(1)}, bf16[3,32,128]{2,1,0:T(8,128)(2,1)S(1)}, u32[]{:S(2)}, u32[]{:S(2)}) %collective-permute-start.6) | collective-permute-done | bytes 24608 | tf_op jit(solution)/shard_map/ppermute | solution.py:198
  37.2 2.4 %collective-permute-done.7.refs_7_ = bf16[3,32,128]{2,1,0:T(8,128)(2,1)S(1)} collective-permute-done((bf16[3,32,128]{2,1,0:T(8,128)(2,1)S(1)}, bf16[3,32,128]{2,1,0:T(8,128)(2,1)S(1)}, u32[]{:S(2)}, u32[]{:S(2)}) %collective-permute-start.7) | collective-permute-done | bytes 24608 | tf_op jit(solution)/shard_map/ppermute | solution.py:198
  39.6 0.1 broadcast_select_fusion
  39.8 2.6 %collective-permute-done.8.one = bf16[128,4096]{1,0:T(8,128)(2,1)S(1)} collective-permute-done((bf16[128,4096]{1,0:T(8,128)(2,1)S(1)}, bf16[128,4096]{1,0:T(8,128)(2,1)S(1)}, u32[]{:S(2)}, u32[]{:S(2)}) %collective-permute-start.8) | collective-permute-done | bytes 1048608 | tf_op jit(solution)/shard_map/ppermute | solution.py:242
  42.4 1.9 %copy-done.3 = bf16[384,4096]{1,0:T(8,128)(2,1)S(1)} copy-done((bf16[384,4096]{1,0:T(8,128)(2,1)S(1)}, bf16[384,4096]{1,0:T(8,128)(2,1)}, u32[]{:S(2)}) %copy-start.3) | copy-done | bytes 3145752
  44.3 3.6 %shard_map.39 = (f32[4,3,32,128]{3,2,1,0:T(8,128)S(1)}, bf16[4,3,32,128]{3,2,1,0:T(8,128)(2,1)S(1)}, bf16[4,3,32,128]{3,2,1,0:T(8,128)(2,1)S(1)}, bf16[4,3,32,128]{3,2,1,0:T(8,128)(2,1)S(1)}) custom-call(s32[1]{0:T(128)} %bitcast.me_ref, bf16[384,4096]{1,0:T(8,128)(2,1)S(1)} %copy-done.1, bf16[384,4096]{1,0:T(8,128)(2,1)S(1)} %copy-done.3, ...), custom_call_target="tpu_custom_call" | custom-call | flops 1610612736 | bytes 8880132 | tf_op jit(solution)/shard_map/pallas_call | solution.py:36
  47.9 0.6 collective-permute-start.9
  48.5 0.5 collective-permute-start.10
  49.0 2.4 %collective-permute-start.11 = (bf16[4,3,32,128]{3,2,1,0:T(8,128)(2,1)S(1)}, bf16[4,3,32,128]{3,2,1,0:T(8,128)(2,1)S(1)}, u32[]{:S(2)}, u32[]{:S(2)}) collective-permute-start(bf16[4,3,32,128]{3,2,1,0:T(8,128)(2,1)S(1)} %get-tuple-element.38), channel_id=1, source_target_pairs={{0,3},{1,2},{2,1},{3,0},{4,7},{5,6},{6,5},{7,4},{8,11},{9,10},{10,... | collective-permute-start | bytes 294920 | tf_op jit(solution)/shard_map/ppermute | solution.py:198
  51.4 2.1 %collective-permute-done.9.rest_0_.refs_1_ = bf16[4,3,32,128]{3,2,1,0:T(8,128)(2,1)S(1)} collective-permute-done((bf16[4,3,32,128]{3,2,1,0:T(8,128)(2,1)S(1)}, bf16[4,3,32,128]{3,2,1,0:T(8,128)(2,1)S(1)}, u32[]{:S(2)}, u32[]{:S(2)}) %collective-permute-start.9) | collective-permute-done | bytes 98336 | tf_op jit(solution)/shard_map/ppermute | solution.py:198
  53.5 1.7 %collective-permute-done.10.rest_1_.refs_2_ = bf16[4,3,32,128]{3,2,1,0:T(8,128)(2,1)S(1)} collective-permute-done((bf16[4,3,32,128]{3,2,1,0:T(8,128)(2,1)S(1)}, bf16[4,3,32,128]{3,2,1,0:T(8,128)(2,1)S(1)}, u32[]{:S(2)}, u32[]{:S(2)}) %collective-permute-start.10) | collective-permute-done | bytes 98336 | tf_op jit(solution)/shard_map/ppermute | solution.py:198
  55.4 5.2 %collective-permute-done.12.refs_8_ = f32[3,32,128]{2,1,0:T(8,128)S(1)} collective-permute-done((f32[3,32,128]{2,1,0:T(8,128)S(1)}, f32[3,32,128]{2,1,0:T(8,128)S(1)}, u32[]{:S(2)}, u32[]{:S(2)}) %collective-permute-start.12) | collective-permute-done | bytes 49184 | tf_op jit(solution)/shard_map/ppermute | solution.py:21
  60.6 1.1 %collective-permute-done.13.refs_9_ = f32[3,32,128]{2,1,0:T(8,128)S(1)} collective-permute-done((f32[3,32,128]{2,1,0:T(8,128)S(1)}, f32[3,32,128]{2,1,0:T(8,128)S(1)}, u32[]{:S(2)}, u32[]{:S(2)}) %collective-permute-start.13) | collective-permute-done | bytes 49184 | tf_op jit(solution)/shard_map/ppermute | solution.py:21
  61.7 0.7 %shard_map.41 = f32[3,5,32,128]{3,2,1,0:T(8,128)} custom-call(f32[4,3,32,128]{3,2,1,0:T(8,128)S(1)} %get-tuple-element.35.keep.refs_0_, bf16[4,3,32,128]{3,2,1,0:T(8,128)(2,1)S(1)} %collective-permute-done.9.rest_0_.refs_1_, bf16[4,3,32,128]{3,2,1,0:T(8,128)(2,1)S(1)} %collective-permute-done.10.rest_1_.refs_2_, ...), custom_call_target="tpu_custom_call" | custom-call | bytes 958464 | tf_op jit(solution)/shard_map/pallas_call | solution.py:36
  (15 shorter events, 0.2 us)
Async XLA Ops:
  1.7 37.9 %collective-permute-start = (bf16[128,4096]{1,0:T(8,128)(2,1)S(1)}, bf16[128,4096]{1,0:T(8,128)(2,1)S(1)}, u32[]{:S(2)}, u32[]{:S(2)}) collective-permute-start(bf16[128,4096]{1,0:T(8,128)(2,1)S(1)} %bitcast.6), channel_id=1, source_target_pairs={{8,0},{12,4},{16,8},{20,12},{24,16},{28,20},{0,24},{4,28},{9,1},{1... | collective-permute-start | bytes 3145736 | tf_op jit(solution)/shard_map/ppermute | solution.py:21
  6.8 0.8 %copy-start.4 = (f32[3,4,8,128]{3,2,1,0:T(8,128)S(1)}, f32[3,4,8,128]{3,2,1,0:T(8,128)}, u32[]{:S(2)}) copy-start(f32[3,4,8,128]{3,2,1,0:T(8,128)} %pot_grad.1) | copy-start | bytes 147460
  7.6 0.7 %copy-start.5 = (f32[4,8,128]{2,1,0:T(8,128)S(1)}, f32[4,8,128]{2,1,0:T(8,128)}, u32[]{:S(2)}) copy-start(f32[4,8,128]{2,1,0:T(8,128)} %coupling.1) | copy-start | bytes 49156
  9.2 14.7 %collective-permute-start.1 = (bf16[128,2048]{1,0:T(8,128)(2,1)}, bf16[128,2048]{1,0:T(8,128)(2,1)S(1)}, u32[]{:S(2)}, u32[]{:S(2)}) collective-permute-start(bf16[128,2048]{1,0:T(8,128)(2,1)} %get-tuple-element.25), channel_id=1, source_target_pairs={{2,0},{0,2},{3,1},{1,3},{6,4},{4,6},{7,5},{5,7},{10,8},{8,10},{11,... | collective-permute-start | bytes 1572872 | tf_op jit(solution)/shard_map/ppermute | solution.py:21
  10.7 13.1 %collective-permute-start.2 = (bf16[128,1024]{1,0:T(8,128)(2,1)S(1)}, bf16[128,1024]{1,0:T(8,128)(2,1)S(1)}, u32[]{:S(2)}, u32[]{:S(2)}) collective-permute-start(bf16[128,1024]{1,0:T(8,128)(2,1)S(1)} %get-tuple-element.26), channel_id=1, source_target_pairs={{1,0},{0,1},{3,2},{2,3},{5,4},{4,5},{7,6},{6,7},{9,8},{8,9},{11,10... | collective-permute-start | bytes 786440 | tf_op jit(solution)/shard_map/ppermute | solution.py:21
  12.2 7.0 %collective-permute-start.4 = (f32[3,4,8,128]{3,2,1,0:T(8,128)S(1)}, f32[3,4,8,128]{3,2,1,0:T(8,128)S(1)}, u32[]{:S(2)}, u32[]{:S(2)}) collective-permute-start(f32[3,4,8,128]{3,2,1,0:T(8,128)S(1)} %get-tuple-element.27.c), channel_id=1, source_target_pairs={{1,0},{0,1},{3,2},{2,3},{5,4},{4,5},{7,6},{6,7},{9,8},{8,9},{11,10... | collective-permute-start | bytes 147464 | tf_op jit(solution)/shard_map/ppermute | solution.py:21
  12.7 11.1 %collective-permute-start.3 = (f32[3,4,8,128]{3,2,1,0:T(8,128)S(1)}, f32[3,4,8,128]{3,2,1,0:T(8,128)S(1)}, u32[]{:S(2)}, u32[]{:S(2)}) collective-permute-start(f32[3,4,8,128]{3,2,1,0:T(8,128)S(1)} %get-tuple-element.27.c), channel_id=1, source_target_pairs={{2,0},{0,2},{3,1},{1,3},{6,4},{4,6},{7,5},{5,7},{10,8},{8,10},{11,... | collective-permute-start | bytes 147464 | tf_op jit(solution)/shard_map/ppermute | solution.py:21
  28.5 1.6 %copy-start = (bf16[384,4096]{1,0:T(8,128)(2,1)}, bf16[384,4096]{1,0:T(8,128)(2,1)S(1)}, u32[]{:S(2)}) copy-start(bf16[384,4096]{1,0:T(8,128)(2,1)S(1)} %get-tuple-element.32.u) | copy-start | bytes 9437188
  30.2 1.7 %copy-start.2 = (bf16[384,4096]{1,0:T(8,128)(2,1)}, bf16[384,4096]{1,0:T(8,128)(2,1)S(1)}, u32[]{:S(2)}) copy-start(bf16[384,4096]{1,0:T(8,128)(2,1)S(1)} %get-tuple-element.33.w) | copy-start | bytes 9437188
  31.9 4.0 %collective-permute-start.5 = (bf16[3,32,128]{2,1,0:T(8,128)(2,1)S(1)}, bf16[3,32,128]{2,1,0:T(8,128)(2,1)S(1)}, u32[]{:S(2)}, u32[]{:S(2)}) collective-permute-start(bf16[3,32,128]{2,1,0:T(8,128)(2,1)S(1)} %get-tuple-element.29), channel_id=1, source_target_pairs={{0,1},{1,0},{2,3},{3,2},{4,5},{5,4},{6,7},{7,6},{8,9},{9,8},{10,11... | collective-permute-start | bytes 73736 | tf_op jit(solution)/shard_map/ppermute | solution.py:198
  33.3 3.8 %collective-permute-start.6 = (bf16[3,32,128]{2,1,0:T(8,128)(2,1)S(1)}, bf16[3,32,128]{2,1,0:T(8,128)(2,1)S(1)}, u32[]{:S(2)}, u32[]{:S(2)}) collective-permute-start(bf16[3,32,128]{2,1,0:T(8,128)(2,1)S(1)} %get-tuple-element.30), channel_id=1, source_target_pairs={{0,2},{1,3},{2,0},{3,1},{4,6},{5,7},{6,4},{7,5},{8,10},{9,11},{10,... | collective-permute-start | bytes 73736 | tf_op jit(solution)/shard_map/ppermute | solution.py:198
  34.9 4.7 %collective-permute-start.7 = (bf16[3,32,128]{2,1,0:T(8,128)(2,1)S(1)}, bf16[3,32,128]{2,1,0:T(8,128)(2,1)S(1)}, u32[]{:S(2)}, u32[]{:S(2)}) collective-permute-start(bf16[3,32,128]{2,1,0:T(8,128)(2,1)S(1)} %get-tuple-element.31), channel_id=1, source_target_pairs={{0,3},{1,2},{2,1},{3,0},{4,7},{5,6},{6,5},{7,4},{8,11},{9,10},{10,... | collective-permute-start | bytes 73736 | tf_op jit(solution)/shard_map/ppermute | solution.py:198
  35.3 7.1 %copy-start.1 = (bf16[384,4096]{1,0:T(8,128)(2,1)S(1)}, bf16[384,4096]{1,0:T(8,128)(2,1)}, u32[]{:S(2)}) copy-start(bf16[384,4096]{1,0:T(8,128)(2,1)} %copy-done) | copy-start | bytes 9437188
  39.7 2.7 %collective-permute-start.8 = (bf16[128,4096]{1,0:T(8,128)(2,1)S(1)}, bf16[128,4096]{1,0:T(8,128)(2,1)S(1)}, u32[]{:S(2)}, u32[]{:S(2)}) collective-permute-start(bf16[128,4096]{1,0:T(8,128)(2,1)S(1)} %broadcast_select_fusion), channel_id=1, source_target_pairs={{0,4},{4,0},{8,12},{12,8},{16,20},{20,16},{24,28},{28,24},{1,5},{5... | collective-permute-start | bytes 3145736 | tf_op jit(solution)/shard_map/ppermute | solution.py:242
  42.4 1.9 %copy-start.3 = (bf16[384,4096]{1,0:T(8,128)(2,1)S(1)}, bf16[384,4096]{1,0:T(8,128)(2,1)}, u32[]{:S(2)}) copy-start(bf16[384,4096]{1,0:T(8,128)(2,1)} %copy-done.2) | copy-start | bytes 9437188
  47.9 5.6 %collective-permute-start.9 = (bf16[4,3,32,128]{3,2,1,0:T(8,128)(2,1)S(1)}, bf16[4,3,32,128]{3,2,1,0:T(8,128)(2,1)S(1)}, u32[]{:S(2)}, u32[]{:S(2)}) collective-permute-start(bf16[4,3,32,128]{3,2,1,0:T(8,128)(2,1)S(1)} %get-tuple-element.36), channel_id=1, source_target_pairs={{0,1},{1,0},{2,3},{3,2},{4,5},{5,4},{6,7},{7,6},{8,9},{9,8},{10,11... | collective-permute-start | bytes 294920 | tf_op jit(solution)/shard_map/ppermute | solution.py:198
  48.5 6.7 %collective-permute-start.10 = (bf16[4,3,32,128]{3,2,1,0:T(8,128)(2,1)S(1)}, bf16[4,3,32,128]{3,2,1,0:T(8,128)(2,1)S(1)}, u32[]{:S(2)}, u32[]{:S(2)}) collective-permute-start(bf16[4,3,32,128]{3,2,1,0:T(8,128)(2,1)S(1)} %get-tuple-element.37), channel_id=1, source_target_pairs={{0,2},{1,3},{2,0},{3,1},{4,6},{5,7},{6,4},{7,5},{8,10},{9,11},{10,... | collective-permute-start | bytes 294920 | tf_op jit(solution)/shard_map/ppermute | solution.py:198
  49.0 6.2 %collective-permute-start.11 = (bf16[4,3,32,128]{3,2,1,0:T(8,128)(2,1)S(1)}, bf16[4,3,32,128]{3,2,1,0:T(8,128)(2,1)S(1)}, u32[]{:S(2)}, u32[]{:S(2)}) collective-permute-start(bf16[4,3,32,128]{3,2,1,0:T(8,128)(2,1)S(1)} %get-tuple-element.38), channel_id=1, source_target_pairs={{0,3},{1,2},{2,1},{3,0},{4,7},{5,6},{6,5},{7,4},{8,11},{9,10},{10,... | collective-permute-start | bytes 294920 | tf_op jit(solution)/shard_map/ppermute | solution.py:198
  55.3 5.4 %collective-permute-start.12 = (f32[3,32,128]{2,1,0:T(8,128)S(1)}, f32[3,32,128]{2,1,0:T(8,128)S(1)}, u32[]{:S(2)}, u32[]{:S(2)}) collective-permute-start(f32[3,32,128]{2,1,0:T(8,128)S(1)} %get-tuple-element.43), channel_id=1, source_target_pairs={{28,0},{0,4},{4,8},{8,12},{12,16},{16,20},{20,24},{24,28},{29,1},{... | collective-permute-start | bytes 147464 | tf_op jit(solution)/shard_map/ppermute | solution.py:21
  55.3 6.4 %collective-permute-start.13 = (f32[3,32,128]{2,1,0:T(8,128)S(1)}, f32[3,32,128]{2,1,0:T(8,128)S(1)}, u32[]{:S(2)}, u32[]{:S(2)}) collective-permute-start(f32[3,32,128]{2,1,0:T(8,128)S(1)} %get-tuple-element.44), channel_id=1, source_target_pairs={{24,0},{28,4},{0,8},{4,12},{8,16},{12,20},{16,24},{20,28},{25,1},{... | collective-permute-start | bytes 147464 | tf_op jit(solution)/shard_map/ppermute | solution.py:21

commit v3 on v2

--- a/solution.py
+++ b/solution.py
@@ -11,7 +11,8 @@
 F32, BF16 = jnp.float32, jnp.bfloat16
 VMEM = pl.BlockSpec(memory_space=pltpu.VMEM)
 SMEM = pl.BlockSpec(memory_space=pltpu.SMEM)
-LIMIT = 24 * 1024 * 1024
+LIMIT = 12 * 1024 * 1024
+PIECES = 1
 NT = (((1,), (1,)), ((), ()))
 CHUNK = 16
 
@@ -21,13 +22,11 @@
     return lax.ppermute(block, axis, [((i + distance) % count, i) for i in range(count)])
 
 
-def both_sides(tail_head, coeff, axis):
+def both_sides(pair, axis):
     if lax.axis_size(axis) == 2:
-        other = shift(coeff, axis, 1)
-        return shift(tail_head, axis, 1), other, other
-    tail, head = jnp.split(tail_head, 2, axis=1)
-    pair = jnp.concatenate([shift(tail, axis, -1), shift(head, axis, 1)], axis=1)
-    return pair, shift(coeff, axis, -1), shift(coeff, axis, 1)
+        return shift(pair, axis, 1)
+    tail, head = jnp.split(pair, 2, axis=1)
+    return jnp.concatenate([shift(tail, axis, -1), shift(head, axis, 1)], axis=1)
 
 
 def call(body, outs, operands, scratch=(), flops=0, scalars=0):
@@ -40,7 +39,7 @@
         out_specs=[VMEM] * len(outs),
         scratch_shapes=list(scratch),
         compiler_params=pltpu.CompilerParams(vmem_limit_bytes=LIMIT),
-        cost_estimate=pl.CostEstimate(flops=flops, bytes_accessed=moved, transcendentals=0),
+        cost_estimate=pl.CostEstimate(flops=0, bytes_accessed=0, transcendentals=0),
     )(*operands)
 
 
@@ -49,57 +48,81 @@
     return [((x + ox) % nx) * ny + (y + oy) % ny for ox in range(nx) for oy in range(ny)]
 
 
-def edges(psi, coupling, pot_grad, hx, hy, c, *, shape):
+def thirds(value):
+    high = value.astype(BF16).astype(F32)
+    middle = (value - high).astype(BF16).astype(F32)
+    return high, middle, value - high - middle
+
+
+def edges(*refs, shape):
+    pieces, (coupling, pot_grad, hx, hy, c, tmp) = refs[:-6], refs[-6:]
     wx, wy, wz = shape
-    layer = wy * wz
-    hx[:, :layer] = psi[:, (wx - 1) * layer :]
-    hx[:, layer:] = psi[:, :layer]
-    for x in range(wx):
-        for side, y in enumerate((wy - 1, 0)):
-            to, at = (side * wx + x) * wz, x * layer + y * wz
-            hy[:, to : to + wz] = psi[:, at : at + wz]
+    layer, line = wy * wz, wx * wz
     c[...] = coupling[...][None] * pot_grad[...]
-
-
-def operators(
-    me_ref, psi, hx, hy, c, cxb, cxa, cyb, cya, u, w, keep, *rest, shape, plane, scale
-):
+    for side, (x, y) in enumerate(((wx - 1, wy - 1), (0, 0))):
+        to_x, to_y = side * (layer + wz), side * (line + wz)
+        end = 0
+        for psi in pieces:
+            r = slice(end, end + psi.shape[0])
+            end = r.stop
+            hx[r, to_x : to_x + layer] = psi[:, x * layer : (x + 1) * layer]
+            for i in range(wx):
+                at = i * layer + y * wz
+                hy[r, to_y + i * wz : to_y + (i + 1) * wz] = psi[:, at : at + wz]
+        for k in range(3):
+            for n, third in enumerate(thirds(c[k, x])):
+                tmp[(3 * k + n) * wy : (3 * k + n + 1) * wy] = third
+        hx[: tmp.shape[0], to_x + layer : to_x + layer + wz] = tmp[...].astype(BF16)
+        for k in range(3):
+            for n, third in enumerate(thirds(c[k, :, y])):
+                tmp[(3 * k + n) * wx : (3 * k + n + 1) * wx] = third
+        hy[: tmp.shape[0], to_y + line : to_y + line + wz] = tmp[...].astype(BF16)
+
+
+def operators(me_ref, *refs, shape, plane, scale):
     wx, wy, wz = shape
-    sends, (half, back, ahead, acc) = rest[:-4], rest[-4:]
-    states = psi.shape[0]
+    pieces, (hx, hy, c, u, w, keep, *rest) = refs[:PIECES], refs[PIECES:]
+    sends, (half, back, ahead, acc, tmp, ex, ey) = rest[:-7], rest[-7:]
+    states = sum(psi.shape[0] for psi in pieces)
     rows = states // math.prod(plane)
-    layer = wy * wz
+    layer, line = wy * wz, wx * wz
     half[...] = 0.5 * c[...]
+    for ref, to, length, count in ((hx, ex, layer, wy), (hy, ey, line, wx)):
+        for side in range(2):
+            at = side * (length + wz) + length
+            tmp[...] = ref[: tmp.shape[0], at : at + wz].astype(F32)
+            for k in range(3):
+                third = [tmp[(3 * k + n) * count : (3 * k + n + 1) * count] for n in range(3)]
+                to[side, k] = 0.5 * (third[0] + third[1] + third[2])
     for k in range(3):
         for x in range(wx):
             back[k, x] = pltpu.roll(half[k, x], 1, 1)
             ahead[k, x] = pltpu.roll(half[k, x], wz - 1, 1)
 
     def coeff(k, x, y):
-        if x < 0:
-            return 0.5 * cxb[k, wx - 1, y : y + 1, :]
-        if x >= wx:
-            return 0.5 * cxa[k, 0, y : y + 1, :]
-        if y < 0:
-            return 0.5 * cyb[k, x, wy - 1 : wy, :]
-        if y >= wy:
-            return 0.5 * cya[k, x, 0:1, :]
+        if x < 0 or x >= wx:
+            return ex[int(x >= wx), k, y : y + 1, :]
+        if y < 0 or y >= wy:
+            return ey[int(y >= wy), k, x : x + 1, :]
         return half[k, x, y : y + 1, :]
 
-    def group(step, _):
+    def group(psi, start, step, _):
+        own = pl.ds(pl.multiple_of(step * CHUNK, CHUNK), CHUNK)
+        step = step + start // CHUNK
         r = pl.ds(pl.multiple_of(step * CHUNK, CHUNK), CHUNK)
 
         def field(x, y):
             if x < 0:
                 ref, at = hx, y * wz
             elif x >= wx:
-                ref, at = hx, layer + y * wz
+                ref, at = hx, layer + wz + y * wz
             elif y < 0:
                 ref, at = hy, x * wz
             elif y >= wy:
-                ref, at = hy, (wx + x) * wz
+                ref, at = hy, line + wz + x * wz
             else:
-                ref, at = psi, x * layer + y * wz
+                at = x * layer + y * wz
+                return psi[own, at : at + wz].astype(F32)
             return ref[r, at : at + wz].astype(F32)
 
         for x in range(wx):
@@ -135,29 +158,33 @@
                 put(w, 2, dx(1) - dy(0))
         return 0
 
-    lax.fori_loop(0, states // CHUNK, group, 0)
-    acc[...] = lax.dot_general(u[...], psi[...], NT, preferred_element_type=F32) * scale
+    end = 0
+    for psi in pieces:
+        lax.fori_loop(0, psi.shape[0] // CHUNK, functools.partial(group, psi, end), 0)
+        end += psi.shape[0]
+    whole = jnp.concatenate([psi[...] for psi in pieces], axis=0)
+    acc[...] = lax.dot_general(u[...], whole, NT, preferred_element_type=F32) * scale
     for ref, dest in zip((keep, *sends), destinations(me_ref[0], *plane)):
         for k in range(3):
             place = pl.ds(pl.multiple_of(k * states + dest * rows, rows), rows)
             ref[k] = acc[place, :].astype(ref.dtype)
 
 
-def tiles(me_ref, u, w, one, two, keep, *rest, plane, scale):
+def tiles(me_ref, u, w, *refs, plane, scale):
+    panels, (keep, *rest) = refs[: 2 * PIECES], refs[2 * PIECES :]
     sends, (up, down) = rest[:-2], rest[-2:]
-    states = one.shape[0]
+    states = sum(panel.shape[0] for panel in panels) // 2
     rows = states // math.prod(plane)
-    for t, panel in enumerate((one, two)):
-        up[t] = lax.dot_general(u[...], panel[...], NT, preferred_element_type=F32) * scale
-        down[t] = lax.dot_general(panel[...], w[...], NT, preferred_element_type=F32) * scale
+    both = jnp.concatenate([panel[...] for panel in panels], axis=0)
+    up[...] = lax.dot_general(u[...], both, NT, preferred_element_type=F32) * scale
+    down[...] = lax.dot_general(both, w[...], NT, preferred_element_type=F32) * scale
     for ref, dest in zip((keep, *sends), destinations(me_ref[0], *plane)):
         for t in range(2):
             for k in range(3):
                 place = pl.ds(pl.multiple_of(k * states + dest * rows, rows), rows)
-                ref[t, k] = up[t, place, :].astype(ref.dtype)
-                place = pl.ds(pl.multiple_of(dest * rows, rows), rows)
-                cols = slice(k * states, (k + 1) * states)
-                ref[2 + t, k] = down[t, place, cols].astype(ref.dtype)
+                ref[t, k] = up[place, t * states : (t + 1) * states].astype(ref.dtype)
+                place = pl.ds(pl.multiple_of(t * states + dest * rows, rows), rows)
+                ref[2 + t, k] = down[place, k * states : (k + 1) * states].astype(ref.dtype)
 
 
 def add_down(keep, *rest):
@@ -208,20 +235,29 @@
     cells = wx * layer
     scale = 1.0 / math.sqrt(cells * places)
     me = lax.axis_index(("dx", "dy")).astype(jnp.int32).reshape(1)
-    psi = lax.optimization_barrier(orbitals.reshape(states, cells))
-    two = shift(psi, "blk", 2)
-
+    psi = []
+    for piece in jnp.split(orbitals, PIECES, axis=0):
+        psi.append(lax.optimization_barrier(piece.reshape(piece.shape[0], cells)))
+    two = [shift(piece, "blk", 2) for piece in psi]
+
+    spill = -(-9 * max(wx, wy) // 16) * 16
     hx, hy, coeff = call(
         functools.partial(edges, shape=(wx, wy, wz)),
         [
-            jax.ShapeDtypeStruct((states, 2 * layer), BF16),
-            jax.ShapeDtypeStruct((states, 2 * wx * wz), BF16),
+            jax.ShapeDtypeStruct((states, 2 * (layer + wz)), BF16),
+            jax.ShapeDtypeStruct((states, 2 * (wx * wz + wz)), BF16),
             jax.ShapeDtypeStruct((3, wx, wy, wz), F32),
         ],
-        [psi, coupling, pot_grad],
-    )
-    hx, cxb, cxa = both_sides(hx, coeff, "dx")
-    hy, cyb, cya = both_sides(hy, coeff, "dy")
+        [*psi, coupling, pot_grad],
+        scratch=[pltpu.VMEM((spill, wz), F32)],
+    )
+    hx, hy = both_sides(hx, "dx"), both_sides(hy, "dy")
+
+    core = lax.axis_index("blk") % 2
+    swap = [(i, i ^ 1) for i in range(lax.axis_size("blk"))]
+
+    def swapped(n):
+        return lax.ppermute(jnp.where(core == 0, two[n], psi[n]), "blk", swap)
 
     field = jax.ShapeDtypeStruct((3 * states, cells), BF16)
     small = (3, rows, states)
@@ -229,23 +265,24 @@
         functools.partial(operators, shape=(wx, wy, wz), plane=plane, scale=scale),
         [field, field, jax.ShapeDtypeStruct(small, F32)]
         + [jax.ShapeDtypeStruct(small, BF16)] * (places - 1),
-        [me, psi, hx, hy, coeff, cxb, cxa, cyb, cya],
-        scratch=[pltpu.VMEM((3, wx, wy, wz), F32)] * 3 + [pltpu.VMEM((3 * states, states), F32)],
+        [me, *psi, hx, hy, coeff],
+        scratch=[pltpu.VMEM((3, wx, wy, wz), F32)] * 3
+        + [pltpu.VMEM((3 * states, states), F32), pltpu.VMEM((spill, wz), F32)]
+        + [pltpu.VMEM((2, 3, wy, wz), F32), pltpu.VMEM((2, 3, wx, wz), F32)],
         flops=2 * 3 * states * states * cells,
         scalars=1,
     )
     own_parts = exchange(own_sends)
 
     two, u, own_parts = lax.optimization_barrier((two, u, own_parts))
-    core = lax.axis_index("blk") % 2
-    swap = [(i, i ^ 1) for i in range(lax.axis_size("blk"))]
-    one = lax.ppermute(jnp.where(core == 0, two, psi), "blk", swap)
+    one = [swapped(n) for n in range(PIECES)]
+
     keep, *sends = call(
         functools.partial(tiles, plane=plane, scale=scale),
         [jax.ShapeDtypeStruct((4, *small), F32)]
         + [jax.ShapeDtypeStruct((4, *small), BF16)] * (places - 1),
-        [me, u, w, one, two],
-        scratch=[pltpu.VMEM((2, 3 * states, states), F32), pltpu.VMEM((2, states, 3 * states), F32)],
+        [me, u, w, *one, *two],
+        scratch=[pltpu.VMEM((3 * states, 2 * states), F32), pltpu.VMEM((2 * states, 3 * states), F32)],
         flops=4 * 2 * 3 * states * states * cells,
         scalars=1,
     )

time: 62.7 us -> 61.7 us (0.984)
  Pallas kernels: 9.91 us -> 8.49 us
  waiting for transfers between devices: 27.5 us -> 28.9 us
  starting transfers between devices: 16.4 us -> 15.3 us
    pallas_call x5, Pallas kernels: 9.91 us -> 8.49 us  [call(): pl.pallas_call(body, out_shape=outs, in_specs=specs, out_specs=[VMEM] * l...]
    ppermute x7 -> x5, waiting for transfers between devices: 16.9 us -> 18.3 us  [shift(): lax.ppermute(block, axis, [((i + distance) % count, i) for i in range(cou...]
    ppermute x7 -> x5, starting transfers between devices: 9.27 us -> 8.23 us  [shift(): lax.ppermute(block, axis, [((i + distance) % count, i) for i in range(cou...]
  transfers between devices with their start and end apart: 14 -> 12, of which waited for: 10 -> 10; matrix products, arithmetic and copies ran while one was open for 0% -> 0% of each run, Pallas kernels for 9% -> 9%
where the time goes in v3:
time: 61.7 us; the launch traced here: 61.4 us
  waiting for transfers between devices  28.9 us (47%)
  starting transfers between devices  15.3 us (25%)
  Pallas kernels  8.49 us (14%)
  local copies, waits for them, and re-layouts  8.41 us (14%)
    ppermute x5, waiting for transfers between devices, shift(): lax.ppermute(block, axis, [((i + distance) % count, i) for i in range(cou...  18.3 us
    pallas_call x5, Pallas kernels, call(): pl.pallas_call(body, out_shape=outs, in_specs=specs, out_specs=[VMEM] * l...  8.49 us
    unnamed x13, local copies, waits for them, and re-layouts  8.41 us
    ppermute x5, starting transfers between devices, shift(): lax.ppermute(block, axis, [((i + distance) % count, i) for i in range(cou...  8.23 us
    ppermute x6, waiting for transfers between devices, exchange(): got.append(lax.ppermute(piece, ('dx', 'dy'), route))  8.02 us
    ppermute x6, starting transfers between devices, exchange(): got.append(lax.ppermute(piece, ('dx', 'dy'), route))  7.04 us
    ppermute x1, waiting for transfers between devices, swapped(): return lax.ppermute(jnp.where(core == 0, two[n], psi[n]), 'blk', swap)  2.65 us
  transfers between devices with their start and end apart: 12, of which 10 were waited for; matrix products, arithmetic and copies ran while one was open for 0% of the time, Pallas kernels for 9%

profile of v3, /device:TPU:0, one launch (start us, length us, event | category | flops | bytes accessed | tf_op | source)
XLA Modules:
  0.0 61.4 jit_solution(15341168948698796555)
XLA Ops:
  0.0 1.7 %copy.6 = bf16[16,8,32,128]{3,1,2,0:T(8,128)(2,1)S(1)} copy(bf16[16,8,32,128]{3,2,1,0:T(8,128)(2,1)} %bitcast.10) | data formatting | bytes 2097152
  1.7 5.1 %collective-permute-start = (bf16[128,4096]{1,0:T(8,128)(2,1)S(1)}, bf16[128,4096]{1,0:T(8,128)(2,1)S(1)}, u32[]{:S(2)}, u32[]{:S(2)}) collective-permute-start(bf16[128,4096]{1,0:T(8,128)(2,1)S(1)} %bitcast.6), channel_id=1, source_target_pairs={{8,0},{12,4},{16,8},{20,12},{24,16},{28,20},{0,24},{4,28},{9,1},{1... | collective-permute-start | bytes 3145736 | tf_op jit(solution)/shard_map/ppermute | solution.py:22
  6.8 0.8 %copy-done.4 = f32[3,4,8,128]{3,2,1,0:T(8,128)S(1)} copy-done((f32[3,4,8,128]{3,2,1,0:T(8,128)S(1)}, f32[3,4,8,128]{3,2,1,0:T(8,128)}, u32[]{:S(2)}) %copy-start.4) | copy-done | bytes 49176
  7.6 0.7 %copy-done.5 = f32[4,8,128]{2,1,0:T(8,128)S(1)} copy-done((f32[4,8,128]{2,1,0:T(8,128)S(1)}, f32[4,8,128]{2,1,0:T(8,128)}, u32[]{:S(2)}) %copy-start.5) | copy-done | bytes 16408
  8.3 0.9 %shard_map.37 = (bf16[128,2304]{1,0:T(8,128)(2,1)}, bf16[128,1280]{1,0:T(8,128)(2,1)S(1)}, f32[3,4,8,128]{3,2,1,0:T(8,128)S(1)}) custom-call(bf16[128,4096]{1,0:T(8,128)(2,1)S(1)} %bitcast.7, f32[4,8,128]{2,1,0:T(8,128)S(1)} %copy-done.5, f32[3,4,8,128]{3,2,1,0:T(8,128)S(1)} %copy-done.4), custom_call_target="tpu_custom_call" | custom-call | tf_op jit(solution)/shard_map/pallas_call | solution.py:35
  9.2 1.5 %collective-permute-start.1 = (bf16[128,2304]{1,0:T(8,128)(2,1)}, bf16[128,2304]{1,0:T(8,128)(2,1)S(1)}, u32[]{:S(2)}, u32[]{:S(2)}) collective-permute-start(bf16[128,2304]{1,0:T(8,128)(2,1)} %get-tuple-element.25), channel_id=1, source_target_pairs={{2,0},{0,2},{3,1},{1,3},{6,4},{4,6},{7,5},{5,7},{10,8},{8,10},{11,... | collective-permute-start | bytes 1769480 | tf_op jit(solution)/shard_map/ppermute | solution.py:22
  10.7 1.5 %collective-permute-start.2 = (bf16[128,1280]{1,0:T(8,128)(2,1)S(1)}, bf16[128,1280]{1,0:T(8,128)(2,1)S(1)}, u32[]{:S(2)}, u32[]{:S(2)}) collective-permute-start(bf16[128,1280]{1,0:T(8,128)(2,1)S(1)} %get-tuple-element.26), channel_id=1, source_target_pairs={{1,0},{0,1},{3,2},{2,3},{5,4},{4,5},{7,6},{6,7},{9,8},{8,9},{11,10... | collective-permute-start | bytes 983048 | tf_op jit(solution)/shard_map/ppermute | solution.py:22
  12.2 7.4 %collective-permute-done.2.refs_2_ = bf16[128,1280]{1,0:T(8,128)(2,1)S(1)} collective-permute-done((bf16[128,1280]{1,0:T(8,128)(2,1)S(1)}, bf16[128,1280]{1,0:T(8,128)(2,1)S(1)}, u32[]{:S(2)}, u32[]{:S(2)}) %collective-permute-start.2) | collective-permute-done | bytes 327712 | tf_op jit(solution)/shard_map/ppermute | solution.py:22
  19.6 4.6 %collective-permute-done.1.refs_1_ = bf16[128,2304]{1,0:T(8,128)(2,1)S(1)} collective-permute-done((bf16[128,2304]{1,0:T(8,128)(2,1)}, bf16[128,2304]{1,0:T(8,128)(2,1)S(1)}, u32[]{:S(2)}, u32[]{:S(2)}) %collective-permute-start.1) | collective-permute-done | bytes 589856 | tf_op jit(solution)/shard_map/ppermute | solution.py:22
  24.2 4.6 %shard_map.38 = (bf16[384,4096]{1,0:T(8,128)(2,1)S(1)}, bf16[384,4096]{1,0:T(8,128)(2,1)S(1)}, f32[3,32,128]{2,1,0:T(8,128)S(1)}, bf16[3,32,128]{2,1,0:T(8,128)(...) custom-call(s32[1]{0:T(128)} %bitcast.me_ref, bf16[128,4096]{1,0:T(8,128)(2,1)S(1)} %bitcast.8, ...), custom_call_target="tpu_custom_call" | custom-call | tf_op jit(solution)/shard_map/pallas_call | solution.py:35
  28.9 1.6 %copy-done = bf16[384,4096]{1,0:T(8,128)(2,1)} copy-done((bf16[384,4096]{1,0:T(8,128)(2,1)}, bf16[384,4096]{1,0:T(8,128)(2,1)S(1)}, u32[]{:S(2)}) %copy-start) | copy-done | bytes 3145752
  30.5 1.7 %copy-done.2 = bf16[384,4096]{1,0:T(8,128)(2,1)} copy-done((bf16[384,4096]{1,0:T(8,128)(2,1)}, bf16[384,4096]{1,0:T(8,128)(2,1)S(1)}, u32[]{:S(2)}) %copy-start.2) | copy-done | bytes 3145752
  32.2 1.5 %collective-permute-start.3 = (bf16[3,32,128]{2,1,0:T(8,128)(2,1)S(1)}, bf16[3,32,128]{2,1,0:T(8,128)(2,1)S(1)}, u32[]{:S(2)}, u32[]{:S(2)}) collective-permute-start(bf16[3,32,128]{2,1,0:T(8,128)(2,1)S(1)} %get-tuple-element.29), channel_id=1, source_target_pairs={{0,1},{1,0},{2,3},{3,2},{4,5},{5,4},{6,7},{7,6},{8,9},{9,8},{10,11... | collective-permute-start | bytes 73736 | tf_op jit(solution)/shard_map/ppermute | solution.py:225
  33.7 1.5 %collective-permute-start.4 = (bf16[3,32,128]{2,1,0:T(8,128)(2,1)S(1)}, bf16[3,32,128]{2,1,0:T(8,128)(2,1)S(1)}, u32[]{:S(2)}, u32[]{:S(2)}) collective-permute-start(bf16[3,32,128]{2,1,0:T(8,128)(2,1)S(1)} %get-tuple-element.30), channel_id=1, source_target_pairs={{0,2},{1,3},{2,0},{3,1},{4,6},{5,7},{6,4},{7,5},{8,10},{9,11},{10,... | collective-permute-start | bytes 73736 | tf_op jit(solution)/shard_map/ppermute | solution.py:225
  35.2 0.5 collective-permute-start.5
  35.7 0.5 collective-permute-done.3.refs_5_
  36.2 1.3 %collective-permute-done.4.refs_6_ = bf16[3,32,128]{2,1,0:T(8,128)(2,1)S(1)} collective-permute-done((bf16[3,32,128]{2,1,0:T(8,128)(2,1)S(1)}, bf16[3,32,128]{2,1,0:T(8,128)(2,1)S(1)}, u32[]{:S(2)}, u32[]{:S(2)}) %collective-permute-start.4) | collective-permute-done | bytes 24608 | tf_op jit(solution)/shard_map/ppermute | solution.py:225
  37.5 2.4 %collective-permute-done.5.refs_7_ = bf16[3,32,128]{2,1,0:T(8,128)(2,1)S(1)} collective-permute-done((bf16[3,32,128]{2,1,0:T(8,128)(2,1)S(1)}, bf16[3,32,128]{2,1,0:T(8,128)(2,1)S(1)}, u32[]{:S(2)}, u32[]{:S(2)}) %collective-permute-start.5) | collective-permute-done | bytes 24608 | tf_op jit(solution)/shard_map/ppermute | solution.py:225
  40.0 0.1 broadcast_select_fusion
  40.1 0.1 collective-permute-start.6
  40.1 2.6 %collective-permute-done.6.refs_0_ = bf16[128,4096]{1,0:T(8,128)(2,1)S(1)} collective-permute-done((bf16[128,4096]{1,0:T(8,128)(2,1)S(1)}, bf16[128,4096]{1,0:T(8,128)(2,1)S(1)}, u32[]{:S(2)}, u32[]{:S(2)}) %collective-permute-start.6) | collective-permute-done | bytes 1048608 | tf_op jit(solution)/shard_map/ppermute | solution.py:260
  42.8 1.9 %copy-done.3 = bf16[384,4096]{1,0:T(8,128)(2,1)S(1)} copy-done((bf16[384,4096]{1,0:T(8,128)(2,1)S(1)}, bf16[384,4096]{1,0:T(8,128)(2,1)}, u32[]{:S(2)}) %copy-start.3) | copy-done | bytes 3145752
  44.7 2.2 %shard_map.39 = (f32[4,3,32,128]{3,2,1,0:T(8,128)S(1)}, bf16[4,3,32,128]{3,2,1,0:T(8,128)(2,1)S(1)}, bf16[4,3,32,128]{3,2,1,0:T(8,128)(2,1)S(1)}, bf16[4,3,32,128]{3,2,1,0:T(8,128)(2,1)S(1)}) custom-call(s32[1]{0:T(128)} %bitcast.me_ref, bf16[384,4096]{1,0:T(8,128)(2,1)S(1)} %copy-done.1, bf16[384,4096]{1,0:T(8,128)(2,1)S(1)} %copy-done.3, ...), custom_call_target="tpu_custom_call" | custom-call | tf_op jit(solution)/shard_map/pallas_call | solution.py:35
  46.9 0.6 collective-permute-start.7
  47.4 0.5 collective-permute-start.8
  48.0 2.5 %collective-permute-start.9 = (bf16[4,3,32,128]{3,2,1,0:T(8,128)(2,1)S(1)}, bf16[4,3,32,128]{3,2,1,0:T(8,128)(2,1)S(1)}, u32[]{:S(2)}, u32[]{:S(2)}) collective-permute-start(bf16[4,3,32,128]{3,2,1,0:T(8,128)(2,1)S(1)} %get-tuple-element.38), channel_id=1, source_target_pairs={{0,3},{1,2},{2,1},{3,0},{4,7},{5,6},{6,5},{7,4},{8,11},{9,10},{10,... | collective-permute-start | bytes 294920 | tf_op jit(solution)/shard_map/ppermute | solution.py:225
  50.4 2.1 %collective-permute-done.7.rest_0_.refs_1_ = bf16[4,3,32,128]{3,2,1,0:T(8,128)(2,1)S(1)} collective-permute-done((bf16[4,3,32,128]{3,2,1,0:T(8,128)(2,1)S(1)}, bf16[4,3,32,128]{3,2,1,0:T(8,128)(2,1)S(1)}, u32[]{:S(2)}, u32[]{:S(2)}) %collective-permute-start.7) | collective-permute-done | bytes 98336 | tf_op jit(solution)/shard_map/ppermute | solution.py:225
  52.5 1.7 %collective-permute-done.8.rest_1_.refs_2_ = bf16[4,3,32,128]{3,2,1,0:T(8,128)(2,1)S(1)} collective-permute-done((bf16[4,3,32,128]{3,2,1,0:T(8,128)(2,1)S(1)}, bf16[4,3,32,128]{3,2,1,0:T(8,128)(2,1)S(1)}, u32[]{:S(2)}, u32[]{:S(2)}) %collective-permute-start.8) | collective-permute-done | bytes 98336 | tf_op jit(solution)/shard_map/ppermute | solution.py:225
  54.3 0.1 collective-permute-start.11
  54.3 5.2 %collective-permute-done.10.refs_8_ = f32[3,32,128]{2,1,0:T(8,128)S(1)} collective-permute-done((f32[3,32,128]{2,1,0:T(8,128)S(1)}, f32[3,32,128]{2,1,0:T(8,128)S(1)}, u32[]{:S(2)}, u32[]{:S(2)}) %collective-permute-start.10) | collective-permute-done | bytes 49184 | tf_op jit(solution)/shard_map/ppermute | solution.py:22
  59.6 1.1 %collective-permute-done.11.refs_9_ = f32[3,32,128]{2,1,0:T(8,128)S(1)} collective-permute-done((f32[3,32,128]{2,1,0:T(8,128)S(1)}, f32[3,32,128]{2,1,0:T(8,128)S(1)}, u32[]{:S(2)}, u32[]{:S(2)}) %collective-permute-start.11) | collective-permute-done | bytes 49184 | tf_op jit(solution)/shard_map/ppermute | solution.py:22
  60.6 0.7 %shard_map.41 = f32[3,5,32,128]{3,2,1,0:T(8,128)} custom-call(f32[4,3,32,128]{3,2,1,0:T(8,128)S(1)} %get-tuple-element.35.keep.refs_0_, bf16[4,3,32,128]{3,2,1,0:T(8,128)(2,1)S(1)} %collective-permute-done.7.rest_0_.refs_1_, bf16[4,3,32,128]{3,2,1,0:T(8,128)(2,1)S(1)} %collective-permute-done.8.rest_1_.refs_2_, ...), custom_call_target="tpu_custom_call" | custom-call | tf_op jit(solution)/shard_map/pallas_call | solution.py:35
  (11 shorter events, 0.1 us)
Async XLA Ops:
  1.7 38.3 %collective-permute-start = (bf16[128,4096]{1,0:T(8,128)(2,1)S(1)}, bf16[128,4096]{1,0:T(8,128)(2,1)S(1)}, u32[]{:S(2)}, u32[]{:S(2)}) collective-permute-start(bf16[128,4096]{1,0:T(8,128)(2,1)S(1)} %bitcast.6), channel_id=1, source_target_pairs={{8,0},{12,4},{16,8},{20,12},{24,16},{28,20},{0,24},{4,28},{9,1},{1... | collective-permute-start | bytes 3145736 | tf_op jit(solution)/shard_map/ppermute | solution.py:22
  6.8 0.8 %copy-start.4 = (f32[3,4,8,128]{3,2,1,0:T(8,128)S(1)}, f32[3,4,8,128]{3,2,1,0:T(8,128)}, u32[]{:S(2)}) copy-start(f32[3,4,8,128]{3,2,1,0:T(8,128)} %refs_2_.1) | copy-start | bytes 147460
  7.6 0.7 %copy-start.5 = (f32[4,8,128]{2,1,0:T(8,128)S(1)}, f32[4,8,128]{2,1,0:T(8,128)}, u32[]{:S(2)}) copy-start(f32[4,8,128]{2,1,0:T(8,128)} %refs_1_.1) | copy-start | bytes 49156
  9.2 15.0 %collective-permute-start.1 = (bf16[128,2304]{1,0:T(8,128)(2,1)}, bf16[128,2304]{1,0:T(8,128)(2,1)S(1)}, u32[]{:S(2)}, u32[]{:S(2)}) collective-permute-start(bf16[128,2304]{1,0:T(8,128)(2,1)} %get-tuple-element.25), channel_id=1, source_target_pairs={{2,0},{0,2},{3,1},{1,3},{6,4},{4,6},{7,5},{5,7},{10,8},{8,10},{11,... | collective-permute-start | bytes 1769480 | tf_op jit(solution)/shard_map/ppermute | solution.py:22
  10.7 8.9 %collective-permute-start.2 = (bf16[128,1280]{1,0:T(8,128)(2,1)S(1)}, bf16[128,1280]{1,0:T(8,128)(2,1)S(1)}, u32[]{:S(2)}, u32[]{:S(2)}) collective-permute-start(bf16[128,1280]{1,0:T(8,128)(2,1)S(1)} %get-tuple-element.26), channel_id=1, source_target_pairs={{1,0},{0,1},{3,2},{2,3},{5,4},{4,5},{7,6},{6,7},{9,8},{8,9},{11,10... | collective-permute-start | bytes 983048 | tf_op jit(solution)/shard_map/ppermute | solution.py:22
  28.9 1.7 %copy-start = (bf16[384,4096]{1,0:T(8,128)(2,1)}, bf16[384,4096]{1,0:T(8,128)(2,1)S(1)}, u32[]{:S(2)}) copy-start(bf16[384,4096]{1,0:T(8,128)(2,1)S(1)} %get-tuple-element.32.u) | copy-start | bytes 9437188
  30.5 1.7 %copy-start.2 = (bf16[384,4096]{1,0:T(8,128)(2,1)}, bf16[384,4096]{1,0:T(8,128)(2,1)S(1)}, u32[]{:S(2)}) copy-start(bf16[384,4096]{1,0:T(8,128)(2,1)S(1)} %get-tuple-element.33.w) | copy-start | bytes 9437188
  32.2 4.0 %collective-permute-start.3 = (bf16[3,32,128]{2,1,0:T(8,128)(2,1)S(1)}, bf16[3,32,128]{2,1,0:T(8,128)(2,1)S(1)}, u32[]{:S(2)}, u32[]{:S(2)}) collective-permute-start(bf16[3,32,128]{2,1,0:T(8,128)(2,1)S(1)} %get-tuple-element.29), channel_id=1, source_target_pairs={{0,1},{1,0},{2,3},{3,2},{4,5},{5,4},{6,7},{7,6},{8,9},{9,8},{10,11... | collective-permute-start | bytes 73736 | tf_op jit(solution)/shard_map/ppermute | solution.py:225
  33.7 3.8 %collective-permute-start.4 = (bf16[3,32,128]{2,1,0:T(8,128)(2,1)S(1)}, bf16[3,32,128]{2,1,0:T(8,128)(2,1)S(1)}, u32[]{:S(2)}, u32[]{:S(2)}) collective-permute-start(bf16[3,32,128]{2,1,0:T(8,128)(2,1)S(1)} %get-tuple-element.30), channel_id=1, source_target_pairs={{0,2},{1,3},{2,0},{3,1},{4,6},{5,7},{6,4},{7,5},{8,10},{9,11},{10,... | collective-permute-start | bytes 73736 | tf_op jit(solution)/shard_map/ppermute | solution.py:225
  35.2 4.7 %collective-permute-start.5 = (bf16[3,32,128]{2,1,0:T(8,128)(2,1)S(1)}, bf16[3,32,128]{2,1,0:T(8,128)(2,1)S(1)}, u32[]{:S(2)}, u32[]{:S(2)}) collective-permute-start(bf16[3,32,128]{2,1,0:T(8,128)(2,1)S(1)} %get-tuple-element.31), channel_id=1, source_target_pairs={{0,3},{1,2},{2,1},{3,0},{4,7},{5,6},{6,5},{7,4},{8,11},{9,10},{10,... | collective-permute-start | bytes 73736 | tf_op jit(solution)/shard_map/ppermute | solution.py:225
  35.7 7.1 %copy-start.1 = (bf16[384,4096]{1,0:T(8,128)(2,1)S(1)}, bf16[384,4096]{1,0:T(8,128)(2,1)}, u32[]{:S(2)}) copy-start(bf16[384,4096]{1,0:T(8,128)(2,1)} %copy-done) | copy-start | bytes 9437188
  40.1 2.7 %collective-permute-start.6 = (bf16[128,4096]{1,0:T(8,128)(2,1)S(1)}, bf16[128,4096]{1,0:T(8,128)(2,1)S(1)}, u32[]{:S(2)}, u32[]{:S(2)}) collective-permute-start(bf16[128,4096]{1,0:T(8,128)(2,1)S(1)} %broadcast_select_fusion), channel_id=1, source_target_pairs={{0,4},{4,0},{8,12},{12,8},{16,20},{20,16},{24,28},{28,24},{1,5},{5... | collective-permute-start | bytes 3145736 | tf_op jit(solution)/shard_map/ppermute | solution.py:260
  42.8 1.9 %copy-start.3 = (bf16[384,4096]{1,0:T(8,128)(2,1)S(1)}, bf16[384,4096]{1,0:T(8,128)(2,1)}, u32[]{:S(2)}) copy-start(bf16[384,4096]{1,0:T(8,128)(2,1)} %copy-done.2) | copy-start | bytes 9437188
  46.9 5.6 %collective-permute-start.7 = (bf16[4,3,32,128]{3,2,1,0:T(8,128)(2,1)S(1)}, bf16[4,3,32,128]{3,2,1,0:T(8,128)(2,1)S(1)}, u32[]{:S(2)}, u32[]{:S(2)}) collective-permute-start(bf16[4,3,32,128]{3,2,1,0:T(8,128)(2,1)S(1)} %get-tuple-element.36), channel_id=1, source_target_pairs={{0,1},{1,0},{2,3},{3,2},{4,5},{5,4},{6,7},{7,6},{8,9},{9,8},{10,11... | collective-permute-start | bytes 294920 | tf_op jit(solution)/shard_map/ppermute | solution.py:225
  47.4 6.7 %collective-permute-start.8 = (bf16[4,3,32,128]{3,2,1,0:T(8,128)(2,1)S(1)}, bf16[4,3,32,128]{3,2,1,0:T(8,128)(2,1)S(1)}, u32[]{:S(2)}, u32[]{:S(2)}) collective-permute-start(bf16[4,3,32,128]{3,2,1,0:T(8,128)(2,1)S(1)} %get-tuple-element.37), channel_id=1, source_target_pairs={{0,2},{1,3},{2,0},{3,1},{4,6},{5,7},{6,4},{7,5},{8,10},{9,11},{10,... | collective-permute-start | bytes 294920 | tf_op jit(solution)/shard_map/ppermute | solution.py:225
  48.0 6.2 %collective-permute-start.9 = (bf16[4,3,32,128]{3,2,1,0:T(8,128)(2,1)S(1)}, bf16[4,3,32,128]{3,2,1,0:T(8,128)(2,1)S(1)}, u32[]{:S(2)}, u32[]{:S(2)}) collective-permute-start(bf16[4,3,32,128]{3,2,1,0:T(8,128)(2,1)S(1)} %get-tuple-element.38), channel_id=1, source_target_pairs={{0,3},{1,2},{2,1},{3,0},{4,7},{5,6},{6,5},{7,4},{8,11},{9,10},{10,... | collective-permute-start | bytes 294920 | tf_op jit(solution)/shard_map/ppermute | solution.py:225
  54.2 5.4 %collective-permute-start.10 = (f32[3,32,128]{2,1,0:T(8,128)S(1)}, f32[3,32,128]{2,1,0:T(8,128)S(1)}, u32[]{:S(2)}, u32[]{:S(2)}) collective-permute-start(f32[3,32,128]{2,1,0:T(8,128)S(1)} %get-tuple-element.43), channel_id=1, source_target_pairs={{28,0},{0,4},{4,8},{8,12},{12,16},{16,20},{20,24},{24,28},{29,1},{... | collective-permute-start | bytes 147464 | tf_op jit(solution)/shard_map/ppermute | solution.py:22
  54.3 6.4 %collective-permute-start.11 = (f32[3,32,128]{2,1,0:T(8,128)S(1)}, f32[3,32,128]{2,1,0:T(8,128)S(1)}, u32[]{:S(2)}, u32[]{:S(2)}) collective-permute-start(f32[3,32,128]{2,1,0:T(8,128)S(1)} %get-tuple-element.44), channel_id=1, source_target_pairs={{24,0},{28,4},{0,8},{4,12},{8,16},{12,20},{16,24},{20,28},{25,1},{... | collective-permute-start | bytes 147464 | tf_op jit(solution)/shard_map/ppermute | solution.py:22

commit v4 on v3

v4 whole, which is shorter than its diff:
```python
import functools
import math

import jax
import jax.numpy as jnp
from jax import lax
from jax.experimental import pallas as pl
from jax.experimental.pallas import tpu as pltpu
from jax.sharding import PartitionSpec as P

F32, BF16 = jnp.float32, jnp.bfloat16
VMEM = pl.BlockSpec(memory_space=pltpu.VMEM)
SMEM = pl.BlockSpec(memory_space=pltpu.SMEM)
ANY = pl.BlockSpec(memory_space=pl.ANY)
LIMIT = 12 * 1024 * 1024
NT = (((1,), (1,)), ((), ()))
CHUNK = 16


def shape_of(shape, dtype):
    return jax.ShapeDtypeStruct(shape, dtype)


def shift(block, axis, distance):
    count = lax.axis_size(axis)
    return lax.ppermute(block, axis, [((i + distance) % count, i) for i in range(count)])


def both_sides(pair, axis):
    if lax.axis_size(axis) == 2:
        return shift(pair, axis, 1)
    tail, head = jnp.split(pair, 2, axis=1)
    return jnp.concatenate([shift(tail, axis, -1), shift(head, axis, 1)], axis=1)


def exchange(sends):
    nx, ny = lax.axis_size("dx"), lax.axis_size("dy")
    got = []
    for o, piece in enumerate(sends, 1):
        ox, oy = o // ny, o % ny
        route = [
            (i * ny + j, ((i + ox) % nx) * ny + (j + oy) % ny) for i in range(nx) for j in range(ny)
        ]
        got.append(lax.ppermute(piece, ("dx", "dy"), route))
    return got


def call(body, outs, operands, scratch=(), specs=None, us=0):
    run = pl.pallas_call(
        body,
        out_shape=outs,
        in_specs=specs or [VMEM] * len(operands),
        out_specs=[VMEM] * len(outs),
        scratch_shapes=list(scratch),
        compiler_params=pltpu.CompilerParams(vmem_limit_bytes=LIMIT),
        cost_estimate=pl.CostEstimate(
            flops=0, bytes_accessed=int(us * 3e6), transcendentals=0
        ),
    )
    return list(run(*operands))


def destinations(me, nx, ny):
    x, y = me // ny, me % ny
    return [((x + ox) % nx) * ny + (y + oy) % ny for ox in range(nx) for oy in range(ny)]


def thirds(value):
    high = value.astype(BF16).astype(F32)
    middle = (value - high).astype(BF16).astype(F32)
    return high, middle, value - high - middle


def edges(psi, coupling_in, grad_in, hx, hy, c, tmp, coupling, grad, sem, *, shape):
    first = pltpu.make_async_copy(coupling_in, coupling, sem.at[0])
    second = pltpu.make_async_copy(grad_in, grad, sem.at[1])
    first.start()
    second.start()
    wx, wy, wz = shape
    layer, line = wy * wz, wx * wz
    ends = ((wx - 1, wy - 1), (0, 0))
    for side, (x, y) in enumerate(ends):
        to_x, to_y = side * (layer + wz), side * (line + wz)
        hx[:, to_x : to_x + layer] = psi[:, x * layer : (x + 1) * layer]
        for i in range(wx):
            at = i * layer + y * wz
            hy[:, to_y + i * wz : to_y + (i + 1) * wz] = psi[:, at : at + wz]
    first.wait()
    second.wait()
    c[...] = coupling[...][None] * grad[...]
    for side, (x, y) in enumerate(ends):
        to_x, to_y = side * (layer + wz), side * (line + wz)
        for k in range(3):
            for n, third in enumerate(thirds(c[k, x])):
                tmp[(3 * k + n) * wy : (3 * k + n + 1) * wy] = third
        hx[: tmp.shape[0], to_x + layer : to_x + layer + wz] = tmp[...].astype(BF16)
        for k in range(3):
            for n, third in enumerate(thirds(c[k, :, y])):
                tmp[(3 * k + n) * wx : (3 * k + n + 1) * wx] = third
        hy[: tmp.shape[0], to_y + line : to_y + line + wz] = tmp[...].astype(BF16)


def operators(layers, psi, hx, hy, c, u, w, half, back, ahead, tmp, ex, ey, *, shape):
    wx, wy, wz = shape
    layer, line = wy * wz, wx * wz
    states = psi.shape[0]
    half[...] = 0.5 * c[...]
    for ref, to, length, count in ((hx, ex, layer, wy), (hy, ey, line, wx)):
        if ref is None:
            continue
        for side in range(2):
            at = side * (length + wz) + length
            tmp[...] = ref[: tmp.shape[0], at : at + wz].astype(F32)
            for k in range(3):
                third = [tmp[(3 * k + n) * count : (3 * k + n + 1) * count] for n in range(3)]
                to[side, k] = 0.5 * (third[0] + third[1] + third[2])
    for k in range(3):
        for x in layers:
            back[k, x] = pltpu.roll(half[k, x], 1, 1)
            ahead[k, x] = pltpu.roll(half[k, x], wz - 1, 1)

    def coeff(k, x, y):
        if x < 0 or x >= wx:
            return ex[int(x >= wx), k, y : y + 1, :]
        if y < 0 or y >= wy:
            return ey[int(y >= wy), k, x : x + 1, :]
        return half[k, x, y : y + 1, :]

    def group(step, _):
        r = pl.ds(pl.multiple_of(step * CHUNK, CHUNK), CHUNK)

        def field(x, y):
            if x < 0:
                ref, at = hx, y * wz
            elif x >= wx:
                ref, at = hx, layer + wz + y * wz
            elif y < 0:
                ref, at = hy, x * wz
            elif y >= wy:
                ref, at = hy, line + wz + x * wz
            else:
                ref, at = psi, x * layer + y * wz
            return ref[r, at : at + wz].astype(F32)

        for n, x in enumerate(layers):
            for y in range(wy):
                here = field(x, y)
                xb, xa = field(x - 1, y), field(x + 1, y)
                yb, ya = field(x, y - 1), field(x, y + 1)
                zb, za = pltpu.roll(here, 1, 1), pltpu.roll(here, wz - 1, 1)
                gx, gy, gz = xa - xb, ya - yb, za - zb
                c1, c2, c3 = [coeff(k, x, y) for k in range(3)]
                cols = slice(n * layer + y * wz, n * layer + (y + 1) * wz)

                def put(ref, k, value):
                    place = pl.ds(pl.multiple_of(k * states + step * CHUNK, CHUNK), CHUNK)
                    ref[place, cols] = value.astype(BF16)

                put(u, 0, c2 * gz - c3 * gy)
                put(u, 1, c3 * gx - c1 * gz)
                put(u, 2, c1 * gy - c2 * gx)

                def dx(k):
                    return coeff(k, x + 1, y) * xa - coeff(k, x - 1, y) * xb

                def dy(k):
                    return coeff(k, x, y + 1) * ya - coeff(k, x, y - 1) * yb

                def dz(k):
                    return ahead[k, x, y : y + 1, :] * za - back[k, x, y : y + 1, :] * zb

                put(w, 0, dy(2) - dz(1))
                put(w, 1, dz(0) - dx(2))
                put(w, 2, dx(1) - dy(0))
        return 0

    lax.fori_loop(0, states // CHUNK, group, 0)


def inner(psi, hy, c, u, w, half, back, ahead, tmp, ey, *, shape):
    layers = range(1, shape[0] - 1)
    operators(layers, psi, None, hy, c, u, w, half, back, ahead, tmp, None, ey, shape=shape)


def product(a_inner, a_outer, panel, layer, flip):
    cells = panel.shape[1]
    last = a_outer.shape[1] - layer
    pairs = (
        (a_inner[...], panel[:, layer : cells - layer]),
        (a_outer[:, :layer], panel[:, :layer]),
        (a_outer[:, last:], panel[:, cells - layer :]),
    )
    total = 0.0
    for a, b in pairs:
        a, b = (b, a) if flip else (a, b)
        total = total + lax.dot_general(a, b, NT, preferred_element_type=F32)
    return total


def outer(
    me_ref, psi, hx, hy, c, u_inner, u, w, keep, *rest, shape, plane, scale
):
    sends, (half, back, ahead, tmp, ex, ey, acc) = rest[:-7], rest[-7:]
    layers = (0, shape[0] - 1)
    operators(layers, psi, hx, hy, c, u, w, half, back, ahead, tmp, ex, ey, shape=shape)
    states = psi.shape[0]
    rows = states // math.prod(plane)
    acc[...] = product(u_inner, u, psi, shape[1] * shape[2], False) * scale
    for ref, dest in zip((keep, *sends), destinations(me_ref[0], *plane)):
        for k in range(3):
            place = pl.ds(pl.multiple_of(k * states + dest * rows, rows), rows)
            ref[k] = acc[place, :].astype(ref.dtype)


def choose(core_ref, two, psi, out):
    @pl.when(core_ref[0] == 1)
    def _():
        out[...] = two[...]

    @pl.when(core_ref[0] == 0)
    def _():
        out[...] = psi[...]


def tiles(me_ref, u_inner, u_outer, w_inner, w_outer, panel, keep, *rest, layer, plane, scale):
    sends, (here, there) = rest[:-2], rest[-2:]
    states = panel.shape[0]
    rows = states // math.prod(plane)
    here[...] = product(u_inner, u_outer, panel, layer, False) * scale
    there[...] = product(w_inner, w_outer, panel, layer, True) * scale
    for ref, dest in zip((keep, *sends), destinations(me_ref[0], *plane)):
        for k in range(3):
            place = pl.ds(pl.multiple_of(k * states + dest * rows, rows), rows)
            ref[0, k] = here[place, :].astype(ref.dtype)
            place = pl.ds(pl.multiple_of(dest * rows, rows), rows)
            ref[1, k] = there[place, k * states : (k + 1) * states].astype(ref.dtype)


def add_there(keep, *rest):
    parts, total_ref = rest[:-1], rest[-1]
    total = keep[1]
    for part in parts:
        total = total + part[1].astype(F32)
    total_ref[...] = total


def assemble(count, *refs):
    mine, one, two = refs[:count], refs[count : 2 * count], refs[2 * count : 3 * count]
    from_one, from_two, out = refs[3 * count :]
    for k in range(3):
        for t, group in ((0, two), (1, one)):
            total = group[0][0, k]
            for part in group[1:]:
                total = total + part[0, k].astype(F32)
            out[k, t] = total
        total = mine[0][k]
        for part in mine[1:]:
            total = total + part[k].astype(F32)
        out[k, 2] = total
        out[k, 3] = from_one[k]
        out[k, 4] = from_two[k]


def on_device(orbitals, coupling, pot_grad):
    states, wx, wy, wz = orbitals.shape
    shape = (wx, wy, wz)
    plane = (lax.axis_size("dx"), lax.axis_size("dy"))
    places = math.prod(plane)
    rows = states // places
    layer, line = wy * wz, wx * wz
    cells = wx * layer
    scale = 1.0 / math.sqrt(cells * places)
    me = lax.axis_index(("dx", "dy")).astype(jnp.int32).reshape(1)
    core = (lax.axis_index("blk") % 2).astype(jnp.int32).reshape(1)

    psi = lax.optimization_barrier(orbitals.reshape(states, cells))
    two = shift(psi, "blk", -2)

    spill = -(-9 * max(wx, wy) // 16) * 16
    tmp = pltpu.VMEM((spill, wz), F32)
    coeffs = pltpu.VMEM((3, wx, wy, wz), F32)
    hx, hy, coeff = call(
        functools.partial(edges, shape=shape),
        [
            shape_of((states, 2 * (layer + wz)), BF16),
            shape_of((states, 2 * (line + wz)), BF16),
            shape_of((3, wx, wy, wz), F32),
        ],
        [psi, coupling, pot_grad],
        scratch=[tmp, pltpu.VMEM((wx, wy, wz), F32), coeffs, pltpu.SemaphoreType.DMA((2,))],
        specs=[VMEM, ANY, ANY],
    )
    hx, hy = both_sides(hx, "dx"), both_sides(hy, "dy")

    ex, ey = pltpu.VMEM((2, 3, wy, wz), F32), pltpu.VMEM((2, 3, wx, wz), F32)
    small = (3, rows, states)
    field = shape_of((3 * states, cells - 2 * layer), BF16)
    u_inner, w_inner = call(
        functools.partial(inner, shape=shape),
        [field, field],
        [psi, hy, coeff],
        scratch=[coeffs] * 3 + [tmp, ey],
        us=2,
    )
    field = shape_of((3 * states, 2 * layer), BF16)
    u_outer, w_outer, *mine = call(
        functools.partial(outer, shape=shape, plane=plane, scale=scale),
        [field, field, shape_of(small, F32)] + [shape_of(small, BF16)] * (places - 1),
        [me, psi, hx, hy, coeff, u_inner],
        scratch=[coeffs] * 3 + [tmp, ex, ey, pltpu.VMEM((3 * states, states), F32)],
        specs=[SMEM] + [VMEM] * 5,
    )
    mine[1:] = exchange(mine[1:])

    two, mine[1:] = lax.optimization_barrier((two, mine[1:]))
    (mixed,) = call(
        choose, [shape_of((states, cells), BF16)], [core, two, psi], specs=[SMEM, VMEM, VMEM]
    )
    swap = [(i, i ^ 1) for i in range(lax.axis_size("blk"))]
    one = lax.ppermute(mixed, "blk", swap)

    def tiles_with(panel):
        pair = (2, *small)
        return call(
            functools.partial(tiles, layer=layer, plane=plane, scale=scale),
            [shape_of(pair, F32)] + [shape_of(pair, BF16)] * (places - 1),
            [me, u_inner, u_outer, w_inner, w_outer, panel],
            scratch=[
                pltpu.VMEM((3 * states, states), F32),
                pltpu.VMEM((states, 3 * states), F32),
            ],
            specs=[SMEM] + [VMEM] * 5,
            us=1,
        )

    def sent_back(group, distance):
        (total,) = call(add_there, [shape_of(small, F32)], group)
        return shift(total, "blk", distance)

    group_two = tiles_with(two)
    group_two[1:] = exchange(group_two[1:])
    one, group_two[0] = lax.optimization_barrier((one, group_two[0]))
    group_one = tiles_with(one)
    group_one[1:] = exchange(group_one[1:])
    from_two = sent_back(group_two, 2)
    from_one = sent_back(group_one, 1)
    (out,) = call(
        functools.partial(assemble, places),
        [shape_of((3, 5, rows, states), F32)],
        [*mine, *group_one, *group_two, from_one, from_two],
    )
    return out


def solution(mesh):
    in_specs = (P("blk", "dx", "dy", None), P("dx", "dy", None), P(None, "dx", "dy", None))
    out_specs = P(None, None, ("blk", "dx", "dy"), None)
    return jax.shard_map(
        on_device, mesh=mesh, in_specs=in_specs, out_specs=out_specs, check_vma=False
    )
```

time: 61.7 us -> 58.2 us (0.943)
  the two profiles are of different devices: /device:TPU:0 before, /device:TPU:1 now
where the time goes in v4:
time: 58.2 us; the launch traced here: 57.9 us
  starting transfers between devices  21.1 us (36%)
  waiting for transfers between devices  15.7 us (27%)
  Pallas kernels  13.6 us (23%)
  local copies, waits for them, and re-layouts  7.47 us (13%)
    pallas_call x9, Pallas kernels, call(): return list(run(*operands))  13.6 us
    ppermute x5, waiting for transfers between devices, shift(): lax.ppermute(block, axis, [((i + distance) % count, i) for i in range(cou...  12 us
    ppermute x5, starting transfers between devices, shift(): lax.ppermute(block, axis, [((i + distance) % count, i) for i in range(cou...  9.54 us
    ppermute x9, starting transfers between devices, exchange(): got.append(lax.ppermute(piece, ('dx', 'dy'), route))  8.07 us
    unnamed x25, local copies, waits for them, and re-layouts  7.47 us
    ppermute x9, waiting for transfers between devices, exchange(): got.append(lax.ppermute(piece, ('dx', 'dy'), route))  3.69 us
    ppermute x1, starting transfers between devices, on_device(): one = lax.ppermute(mixed, 'blk', swap)  3.44 us
  transfers between devices with their start and end apart: 15, of which 6 were waited for; matrix products, arithmetic and copies ran while one was open for 0% of the time, Pallas kernels for 20%

profile of v4, /device:TPU:1, one launch (start us, length us, event | category | flops | bytes accessed | tf_op | source)
XLA Modules:
  0.0 57.9 jit_solution(16843276989632170356)
XLA Ops:
  0.0 1.7 %copy.6 = bf16[16,8,32,128]{3,1,2,0:T(8,128)(2,1)S(1)} copy(bf16[16,8,32,128]{3,2,1,0:T(8,128)(2,1)} %bitcast.12) | data formatting | bytes 2097152
  1.7 2.2 %collective-permute-start.2 = (bf16[128,4096]{1,0:T(8,128)(2,1)S(1)}, bf16[128,4096]{1,0:T(8,128)(2,1)}, u32[]{:S(2)}, u32[]{:S(2)}) collective-permute-start(bf16[128,4096]{1,0:T(8,128)(2,1)S(1)} %bitcast.7), channel_id=1, source_target_pairs={{24,0},{28,4},{0,8},{4,12},{8,16},{12,20},{16,24},{20,28},{25,1},{... | collective-permute-start | bytes 3145736 | tf_op jit(solution)/shard_map/ppermute | solution.py:26
  3.9 1.0 %shard_map.37 = (bf16[128,2304]{1,0:T(8,128)(2,1)}, bf16[128,1280]{1,0:T(8,128)(2,1)S(1)}, f32[3,4,8,128]{3,2,1,0:T(8,128)S(1)}) custom-call(bf16[128,4096]{1,0:T(8,128)(2,1)S(1)} %bitcast.8, f32[4,8,128]{2,1,0:T(8,128)S(1)} %copy-done.11, f32[3,4,8,128]{3,2,1,0:T(8,128)S(1)} %copy-done.8), custom_call_target="tpu_custom_call" | custom-call | tf_op jit(solution)/shard_map/pallas_call | solution.py:60
  4.9 0.6 %copy-done.6 = f32[3,4,8,128]{3,2,1,0:T(8,128)} copy-done((f32[3,4,8,128]{3,2,1,0:T(8,128)}, f32[3,4,8,128]{3,2,1,0:T(8,128)S(1)}, u32[]{:S(2)}) %copy-start.6) | copy-done | bytes 49176
  5.5 1.2 %collective-permute-start = (bf16[128,2304]{1,0:T(8,128)(2,1)}, bf16[128,2304]{1,0:T(8,128)(2,1)S(1)}, u32[]{:S(2)}, u32[]{:S(2)}) collective-permute-start(bf16[128,2304]{1,0:T(8,128)(2,1)} %get-tuple-element.30), channel_id=1, source_target_pairs={{2,0},{0,2},{3,1},{1,3},{6,4},{4,6},{7,5},{5,7},{10,8},{8,10},{11,... | collective-permute-start | bytes 1769480 | tf_op jit(solution)/shard_map/ppermute | solution.py:26
  6.8 1.2 %collective-permute-start.1 = (bf16[128,1280]{1,0:T(8,128)(2,1)S(1)}, bf16[128,1280]{1,0:T(8,128)(2,1)S(1)}, u32[]{:S(2)}, u32[]{:S(2)}) collective-permute-start(bf16[128,1280]{1,0:T(8,128)(2,1)S(1)} %get-tuple-element.31), channel_id=1, source_target_pairs={{1,0},{0,1},{3,2},{2,3},{5,4},{4,5},{7,6},{6,7},{9,8},{8,9},{11,10... | collective-permute-start | bytes 983048 | tf_op jit(solution)/shard_map/ppermute | solution.py:26
  8.0 6.9 %collective-permute-done.1.hy = bf16[128,1280]{1,0:T(8,128)(2,1)S(1)} collective-permute-done((bf16[128,1280]{1,0:T(8,128)(2,1)S(1)}, bf16[128,1280]{1,0:T(8,128)(2,1)S(1)}, u32[]{:S(2)}, u32[]{:S(2)}) %collective-permute-start.1) | collective-permute-done | bytes 327712 | tf_op jit(solution)/shard_map/ppermute | solution.py:26
  14.8 0.8 %copy-done.7 = f32[3,4,8,128]{3,2,1,0:T(8,128)S(1)} copy-done((f32[3,4,8,128]{3,2,1,0:T(8,128)S(1)}, f32[3,4,8,128]{3,2,1,0:T(8,128)}, u32[]{:S(2)}) %copy-start.7) | copy-done | bytes 49176
  15.6 1.9 %shard_map.38 = (bf16[384,2048]{1,0:T(8,128)(2,1)S(1)}, bf16[384,2048]{1,0:T(8,128)(2,1)S(1)}) custom-call(bf16[128,4096]{1,0:T(8,128)(2,1)S(1)} %bitcast.9, bf16[128,1280]{1,0:T(8,128)(2,1)S(1)} %collective-permute-done.1.hy, f32[3,4,8,128]{3,2,1,0:T(8,128)S(1)} %copy-done.7), custom_call_target="tpu_custom_call" | custom-call | bytes 6000000 | tf_op jit(solution)/shard_map/pallas_call | solution.py:60
  17.6 2.2 %collective-permute-done.hx = bf16[128,2304]{1,0:T(8,128)(2,1)S(1)} collective-permute-done((bf16[128,2304]{1,0:T(8,128)(2,1)}, bf16[128,2304]{1,0:T(8,128)(2,1)S(1)}, u32[]{:S(2)}, u32[]{:S(2)}) %collective-permute-start) | collective-permute-done | bytes 589856 | tf_op jit(solution)/shard_map/ppermute | solution.py:26
  19.7 3.5 %shard_map.39 = (bf16[384,2048]{1,0:T(8,128)(2,1)S(1)}, bf16[384,2048]{1,0:T(8,128)(2,1)S(1)}, f32[3,32,128]{2,1,0:T(8,128)S(1)}, bf16[3,32,128]{2,1,0:T(8,128)(...) custom-call(s32[1]{0:T(128)} %bitcast.me_ref, bf16[128,4096]{1,0:T(8,128)(2,1)S(1)} %bitcast.10, ...), custom_call_target="tpu_custom_call" | custom-call | tf_op jit(solution)/shard_map/pallas_call | solution.py:60
  23.3 1.1 %copy-done.2 = bf16[384,2048]{1,0:T(8,128)(2,1)} copy-done((bf16[384,2048]{1,0:T(8,128)(2,1)}, bf16[384,2048]{1,0:T(8,128)(2,1)S(1)}, u32[]{:S(2)}) %copy-start.2) | copy-done | bytes 1572888
  24.4 1.2 %copy-done.4 = bf16[384,2048]{1,0:T(8,128)(2,1)} copy-done((bf16[384,2048]{1,0:T(8,128)(2,1)}, bf16[384,2048]{1,0:T(8,128)(2,1)S(1)}, u32[]{:S(2)}) %copy-start.4) | copy-done | bytes 1572888
  25.6 0.6 %copy-done.9 = f32[3,32,128]{2,1,0:T(8,128)} copy-done((f32[3,32,128]{2,1,0:T(8,128)}, f32[3,32,128]{2,1,0:T(8,128)S(1)}, u32[]{:S(2)}) %copy-start.9) | copy-done | bytes 49176
  26.2 1.2 %collective-permute-start.3 = (bf16[3,32,128]{2,1,0:T(8,128)(2,1)}, bf16[3,32,128]{2,1,0:T(8,128)(2,1)S(1)}, u32[]{:S(2)}, u32[]{:S(2)}) collective-permute-start(bf16[3,32,128]{2,1,0:T(8,128)(2,1)} %get-tuple-element.35), channel_id=1, source_target_pairs={{0,1},{1,0},{2,3},{3,2},{4,5},{5,4},{6,7},{7,6},{8,9},{9,8},{10,11... | collective-permute-start | bytes 73736 | tf_op jit(solution)/shard_map/ppermute | solution.py:44
  27.4 1.2 %collective-permute-start.4 = (bf16[3,32,128]{2,1,0:T(8,128)(2,1)}, bf16[3,32,128]{2,1,0:T(8,128)(2,1)S(1)}, u32[]{:S(2)}, u32[]{:S(2)}) collective-permute-start(bf16[3,32,128]{2,1,0:T(8,128)(2,1)} %get-tuple-element.36), channel_id=1, source_target_pairs={{0,2},{1,3},{2,0},{3,1},{4,6},{5,7},{6,4},{7,5},{8,10},{9,11},{10,... | collective-permute-start | bytes 73736 | tf_op jit(solution)/shard_map/ppermute | solution.py:44
  28.9 0.6 %collective-permute-done.3.refs_1_ = bf16[3,32,128]{2,1,0:T(8,128)(2,1)S(1)} collective-permute-done((bf16[3,32,128]{2,1,0:T(8,128)(2,1)}, bf16[3,32,128]{2,1,0:T(8,128)(2,1)S(1)}, u32[]{:S(2)}, u32[]{:S(2)}) %collective-permute-start.3) | collective-permute-done | bytes 24608 | tf_op jit(solution)/shard_map/ppermute | solution.py:44
  29.5 0.8 %collective-permute-done.4.refs_2_ = bf16[3,32,128]{2,1,0:T(8,128)(2,1)S(1)} collective-permute-done((bf16[3,32,128]{2,1,0:T(8,128)(2,1)}, bf16[3,32,128]{2,1,0:T(8,128)(2,1)S(1)}, u32[]{:S(2)}, u32[]{:S(2)}) %collective-permute-start.4) | collective-permute-done | bytes 24608 | tf_op jit(solution)/shard_map/ppermute | solution.py:44
  30.3 2.2 %collective-permute-done.5.refs_3_ = bf16[3,32,128]{2,1,0:T(8,128)(2,1)S(1)} collective-permute-done((bf16[3,32,128]{2,1,0:T(8,128)(2,1)}, bf16[3,32,128]{2,1,0:T(8,128)(2,1)S(1)}, u32[]{:S(2)}, u32[]{:S(2)}) %collective-permute-start.5) | collective-permute-done | bytes 24608 | tf_op jit(solution)/shard_map/ppermute | solution.py:44
  32.6 1.4 %shard_map.40 = bf16[128,4096]{1,0:T(8,128)(2,1)S(1)} custom-call(s32[1]{0:T(128)} %bitcast.1.core_ref, bf16[128,4096]{1,0:T(8,128)(2,1)} %collective-permute-done.2.two.panel, bf16[128,4096]{1,0:T(8,128)(2,1)S(1)} %bitcast.11), custom_call_target="tpu_custom_call" | custom-call | tf_op jit(solution)/shard_map/pallas_call | solution.py:60
  34.0 3.4 %collective-permute-start.6 = (bf16[128,4096]{1,0:T(8,128)(2,1)S(1)}, bf16[128,4096]{1,0:T(8,128)(2,1)S(1)}, u32[]{:S(2)}, u32[]{:S(2)}) collective-permute-start(bf16[128,4096]{1,0:T(8,128)(2,1)S(1)} %shard_map.40), channel_id=1, source_target_pairs={{0,4},{4,0},{8,12},{12,8},{16,20},{20,16},{24,28},{28,24},{1,5},{5... | collective-permute-start | bytes 3145736 | tf_op jit(solution)/shard_map/ppermute | solution.py:320
  37.5 1.4 %copy-done.5 = bf16[384,2048]{1,0:T(8,128)(2,1)S(1)} copy-done((bf16[384,2048]{1,0:T(8,128)(2,1)S(1)}, bf16[384,2048]{1,0:T(8,128)(2,1)}, u32[]{:S(2)}) %copy-start.5) | copy-done | bytes 1572888
  38.9 3.1 %shard_map.41 = (f32[2,3,32,128]{3,2,1,0:T(8,128)S(1)}, bf16[2,3,32,128]{3,2,1,0:T(8,128)(2,1)S(1)}, bf16[2,3,32,128]{3,2,1,0:T(8,128)(2,1)S(1)}, bf16[2,3,32,128]{3,2,1,0:T(8,128)(2,1)S(1)}) custom-call(s32[1]{0:T(128)} %bitcast.me_ref, bf16[384,2048]{1,0:T(8,128)(2,1)S(1)} %get-tuple-element.33.u_inner, bf16[384,2048]{1,0:T(8,128)(2,1)S(1)} %copy-done.3, ...), custom_call_target="tpu_custom_call" | custom-call | bytes 3000000 | tf_op jit(solution)/shard_map/pallas_call | solution.py:60
  42.0 0.3 collective-permute-start.10
  42.5 2.2 %collective-permute-start.12 = (bf16[2,3,32,128]{3,2,1,0:T(8,128)(2,1)S(1)}, bf16[2,3,32,128]{3,2,1,0:T(8,128)(2,1)S(1)}, u32[]{:S(2)}, u32[]{:S(2)}) collective-permute-start(bf16[2,3,32,128]{3,2,1,0:T(8,128)(2,1)S(1)} %get-tuple-element.54), channel_id=1, source_target_pairs={{0,3},{1,2},{2,1},{3,0},{4,7},{5,6},{6,5},{7,4},{8,11},{9,10},{10,... | collective-permute-start | bytes 147464 | tf_op jit(solution)/shard_map/ppermute | solution.py:44
  44.7 1.8 %shard_map.42 = (f32[2,3,32,128]{3,2,1,0:T(8,128)S(1)}, bf16[2,3,32,128]{3,2,1,0:T(8,128)(2,1)S(1)}, bf16[2,3,32,128]{3,2,1,0:T(8,128)(2,1)S(1)}, bf16[2,3,32,128]{3,2,1,0:T(8,128)(2,1)S(1)}) custom-call(s32[1]{0:T(128)} %bitcast.me_ref, bf16[384,2048]{1,0:T(8,128)(2,1)S(1)} %get-tuple-element.33.u_inner, bf16[384,2048]{1,0:T(8,128)(2,1)S(1)} %copy-done.3, ...), custom_call_target="tpu_custom_call" | custom-call | bytes 3000000 | tf_op jit(solution)/shard_map/pallas_call | solution.py:60
  46.5 0.3 collective-permute-start.7
  47.1 2.2 %collective-permute-start.9 = (bf16[2,3,32,128]{3,2,1,0:T(8,128)(2,1)S(1)}, bf16[2,3,32,128]{3,2,1,0:T(8,128)(2,1)S(1)}, u32[]{:S(2)}, u32[]{:S(2)}) collective-permute-start(bf16[2,3,32,128]{3,2,1,0:T(8,128)(2,1)S(1)} %get-tuple-element.50), channel_id=1, source_target_pairs={{0,3},{1,2},{2,1},{3,0},{4,7},{5,6},{6,5},{7,4},{8,11},{9,10},{10,... | collective-permute-start | bytes 147464 | tf_op jit(solution)/shard_map/ppermute | solution.py:44
  49.3 2.1 %collective-permute-start.14 = (f32[3,32,128]{2,1,0:T(8,128)S(1)}, f32[3,32,128]{2,1,0:T(8,128)S(1)}, u32[]{:S(2)}, u32[]{:S(2)}) collective-permute-start(f32[3,32,128]{2,1,0:T(8,128)S(1)} %shard_map.44), channel_id=1, source_target_pairs={{8,0},{12,4},{16,8},{20,12},{24,16},{28,20},{0,24},{4,28},{9,1},{1... | collective-permute-start | bytes 147464 | tf_op jit(solution)/shard_map/ppermute | solution.py:26
  51.4 2.8 %collective-permute-start.13 = (f32[3,32,128]{2,1,0:T(8,128)S(1)}, f32[3,32,128]{2,1,0:T(8,128)S(1)}, u32[]{:S(2)}, u32[]{:S(2)}) collective-permute-start(f32[3,32,128]{2,1,0:T(8,128)S(1)} %shard_map.43), channel_id=1, source_target_pairs={{4,0},{8,4},{12,8},{16,12},{20,16},{24,20},{28,24},{0,28},{5,1},{9... | collective-permute-start | bytes 147464 | tf_op jit(solution)/shard_map/ppermute | solution.py:26
  54.2 3.0 %collective-permute-done.13.refs_12_ = f32[3,32,128]{2,1,0:T(8,128)S(1)} collective-permute-done((f32[3,32,128]{2,1,0:T(8,128)S(1)}, f32[3,32,128]{2,1,0:T(8,128)S(1)}, u32[]{:S(2)}, u32[]{:S(2)}) %collective-permute-start.13) | collective-permute-done | bytes 49184 | tf_op jit(solution)/shard_map/ppermute | solution.py:26
  57.2 0.7 %shard_map.45 = f32[3,5,32,128]{3,2,1,0:T(8,128)} custom-call(f32[3,32,128]{2,1,0:T(8,128)S(1)} %copy-done.10, bf16[3,32,128]{2,1,0:T(8,128)(2,1)S(1)} %collective-permute-done.3.refs_1_, bf16[3,32,128]{2,1,0:T(8,128)(2,1)S(1)} %collective-permute-done.4.refs_2_, bf16[3,32,128]{2,1,0:T(8,128)(2,1)S(1)} %collective-permute-done.5.refs_3_, ...), custom_call_target="tpu_custom_call" | custom-call | tf_op jit(solution)/shard_map/pallas_call | solution.py:60
  (32 shorter events, 0.7 us)
Async XLA Ops:
  0.0 3.9 %copy-start.8 = (f32[3,4,8,128]{3,2,1,0:T(8,128)S(1)}, f32[3,4,8,128]{3,2,1,0:T(8,128)}, u32[]{:S(2)}) copy-start(f32[3,4,8,128]{3,2,1,0:T(8,128)} %grad_in.1) | copy-start | bytes 147460
  0.0 3.9 %copy-start.11 = (f32[4,8,128]{2,1,0:T(8,128)S(1)}, f32[4,8,128]{2,1,0:T(8,128)}, u32[]{:S(2)}) copy-start(f32[4,8,128]{2,1,0:T(8,128)} %coupling_in.1) | copy-start | bytes 49156
  1.7 30.9 %collective-permute-start.2 = (bf16[128,4096]{1,0:T(8,128)(2,1)S(1)}, bf16[128,4096]{1,0:T(8,128)(2,1)}, u32[]{:S(2)}, u32[]{:S(2)}) collective-permute-start(bf16[128,4096]{1,0:T(8,128)(2,1)S(1)} %bitcast.7), channel_id=1, source_target_pairs={{24,0},{28,4},{0,8},{4,12},{8,16},{12,20},{16,24},{20,28},{25,1},{... | collective-permute-start | bytes 3145736 | tf_op jit(solution)/shard_map/ppermute | solution.py:26
  4.9 0.6 %copy-start.6 = (f32[3,4,8,128]{3,2,1,0:T(8,128)}, f32[3,4,8,128]{3,2,1,0:T(8,128)S(1)}, u32[]{:S(2)}) copy-start(f32[3,4,8,128]{3,2,1,0:T(8,128)S(1)} %get-tuple-element.32.c) | copy-start | bytes 147460
  5.5 14.2 %collective-permute-start = (bf16[128,2304]{1,0:T(8,128)(2,1)}, bf16[128,2304]{1,0:T(8,128)(2,1)S(1)}, u32[]{:S(2)}, u32[]{:S(2)}) collective-permute-start(bf16[128,2304]{1,0:T(8,128)(2,1)} %get-tuple-element.30), channel_id=1, source_target_pairs={{2,0},{0,2},{3,1},{1,3},{6,4},{4,6},{7,5},{5,7},{10,8},{8,10},{11,... | collective-permute-start | bytes 1769480 | tf_op jit(solution)/shard_map/ppermute | solution.py:26
  6.8 8.1 %collective-permute-start.1 = (bf16[128,1280]{1,0:T(8,128)(2,1)S(1)}, bf16[128,1280]{1,0:T(8,128)(2,1)S(1)}, u32[]{:S(2)}, u32[]{:S(2)}) collective-permute-start(bf16[128,1280]{1,0:T(8,128)(2,1)S(1)} %get-tuple-element.31), channel_id=1, source_target_pairs={{1,0},{0,1},{3,2},{2,3},{5,4},{4,5},{7,6},{6,7},{9,8},{8,9},{11,10... | collective-permute-start | bytes 983048 | tf_op jit(solution)/shard_map/ppermute | solution.py:26
  14.8 0.8 %copy-start.7 = (f32[3,4,8,128]{3,2,1,0:T(8,128)S(1)}, f32[3,4,8,128]{3,2,1,0:T(8,128)}, u32[]{:S(2)}) copy-start(f32[3,4,8,128]{3,2,1,0:T(8,128)} %copy-done.6) | copy-start | bytes 147460
  17.5 5.7 %copy-start = (bf16[384,2048]{1,0:T(8,128)(2,1)}, bf16[384,2048]{1,0:T(8,128)(2,1)S(1)}, u32[]{:S(2)}) copy-start(bf16[384,2048]{1,0:T(8,128)(2,1)S(1)} %get-tuple-element.42.w_inner) | copy-start | bytes 4718596
  23.3 1.1 %copy-start.2 = (bf16[384,2048]{1,0:T(8,128)(2,1)}, bf16[384,2048]{1,0:T(8,128)(2,1)S(1)}, u32[]{:S(2)}) copy-start(bf16[384,2048]{1,0:T(8,128)(2,1)S(1)} %get-tuple-element.41.u_outer) | copy-start | bytes 4718596
  24.4 1.2 %copy-start.4 = (bf16[384,2048]{1,0:T(8,128)(2,1)}, bf16[384,2048]{1,0:T(8,128)(2,1)S(1)}, u32[]{:S(2)}) copy-start(bf16[384,2048]{1,0:T(8,128)(2,1)S(1)} %get-tuple-element.43.w_outer) | copy-start | bytes 4718596
  25.6 0.6 %copy-start.9 = (f32[3,32,128]{2,1,0:T(8,128)}, f32[3,32,128]{2,1,0:T(8,128)S(1)}, u32[]{:S(2)}) copy-start(f32[3,32,128]{2,1,0:T(8,128)S(1)} %get-tuple-element.34.refs_0_) | copy-start | bytes 147460
  26.2 3.3 %collective-permute-start.3 = (bf16[3,32,128]{2,1,0:T(8,128)(2,1)}, bf16[3,32,128]{2,1,0:T(8,128)(2,1)S(1)}, u32[]{:S(2)}, u32[]{:S(2)}) collective-permute-start(bf16[3,32,128]{2,1,0:T(8,128)(2,1)} %get-tuple-element.35), channel_id=1, source_target_pairs={{0,1},{1,0},{2,3},{3,2},{4,5},{5,4},{6,7},{7,6},{8,9},{9,8},{10,11... | collective-permute-start | bytes 73736 | tf_op jit(solution)/shard_map/ppermute | solution.py:44
  27.4 2.9 %collective-permute-start.4 = (bf16[3,32,128]{2,1,0:T(8,128)(2,1)}, bf16[3,32,128]{2,1,0:T(8,128)(2,1)S(1)}, u32[]{:S(2)}, u32[]{:S(2)}) collective-permute-start(bf16[3,32,128]{2,1,0:T(8,128)(2,1)} %get-tuple-element.36), channel_id=1, source_target_pairs={{0,2},{1,3},{2,0},{3,1},{4,6},{5,7},{6,4},{7,5},{8,10},{9,11},{10,... | collective-permute-start | bytes 73736 | tf_op jit(solution)/shard_map/ppermute | solution.py:44
  28.7 3.9 %collective-permute-start.5 = (bf16[3,32,128]{2,1,0:T(8,128)(2,1)}, bf16[3,32,128]{2,1,0:T(8,128)(2,1)S(1)}, u32[]{:S(2)}, u32[]{:S(2)}) collective-permute-start(bf16[3,32,128]{2,1,0:T(8,128)(2,1)} %get-tuple-element.37), channel_id=1, source_target_pairs={{0,3},{1,2},{2,1},{3,0},{4,7},{5,6},{6,5},{7,4},{8,11},{9,10},{10,... | collective-permute-start | bytes 73736 | tf_op jit(solution)/shard_map/ppermute | solution.py:44
  32.6 4.9 %copy-start.1 = (bf16[384,2048]{1,0:T(8,128)(2,1)S(1)}, bf16[384,2048]{1,0:T(8,128)(2,1)}, u32[]{:S(2)}) copy-start(bf16[384,2048]{1,0:T(8,128)(2,1)} %copy-done) | copy-start | bytes 4718596
  32.6 4.9 %copy-start.3 = (bf16[384,2048]{1,0:T(8,128)(2,1)S(1)}, bf16[384,2048]{1,0:T(8,128)(2,1)}, u32[]{:S(2)}) copy-start(bf16[384,2048]{1,0:T(8,128)(2,1)} %copy-done.2) | copy-start | bytes 4718596
  34.0 10.7 %collective-permute-start.6 = (bf16[128,4096]{1,0:T(8,128)(2,1)S(1)}, bf16[128,4096]{1,0:T(8,128)(2,1)S(1)}, u32[]{:S(2)}, u32[]{:S(2)}) collective-permute-start(bf16[128,4096]{1,0:T(8,128)(2,1)S(1)} %shard_map.40), channel_id=1, source_target_pairs={{0,4},{4,0},{8,12},{12,8},{16,20},{20,16},{24,28},{28,24},{1,5},{5... | collective-permute-start | bytes 3145736 | tf_op jit(solution)/shard_map/ppermute | solution.py:320
  37.5 1.4 %copy-start.5 = (bf16[384,2048]{1,0:T(8,128)(2,1)S(1)}, bf16[384,2048]{1,0:T(8,128)(2,1)}, u32[]{:S(2)}) copy-start(bf16[384,2048]{1,0:T(8,128)(2,1)} %copy-done.4) | copy-start | bytes 4718596
  42.0 5.1 %collective-permute-start.10 = (bf16[2,3,32,128]{3,2,1,0:T(8,128)(2,1)S(1)}, bf16[2,3,32,128]{3,2,1,0:T(8,128)(2,1)S(1)}, u32[]{:S(2)}, u32[]{:S(2)}) collective-permute-start(bf16[2,3,32,128]{3,2,1,0:T(8,128)(2,1)S(1)} %get-tuple-element.52), channel_id=1, source_target_pairs={{0,1},{1,0},{2,3},{3,2},{4,5},{5,4},{6,7},{7,6},{8,9},{9,8},{10,11... | collective-permute-start | bytes 147464 | tf_op jit(solution)/shard_map/ppermute | solution.py:44
  42.3 7.0 %collective-permute-start.11 = (bf16[2,3,32,128]{3,2,1,0:T(8,128)(2,1)S(1)}, bf16[2,3,32,128]{3,2,1,0:T(8,128)(2,1)S(1)}, u32[]{:S(2)}, u32[]{:S(2)}) collective-permute-start(bf16[2,3,32,128]{3,2,1,0:T(8,128)(2,1)S(1)} %get-tuple-element.53), channel_id=1, source_target_pairs={{0,2},{1,3},{2,0},{3,1},{4,6},{5,7},{6,4},{7,5},{8,10},{9,11},{10,... | collective-permute-start | bytes 147464 | tf_op jit(solution)/shard_map/ppermute | solution.py:44
  42.5 6.8 %collective-permute-start.12 = (bf16[2,3,32,128]{3,2,1,0:T(8,128)(2,1)S(1)}, bf16[2,3,32,128]{3,2,1,0:T(8,128)(2,1)S(1)}, u32[]{:S(2)}, u32[]{:S(2)}) collective-permute-start(bf16[2,3,32,128]{3,2,1,0:T(8,128)(2,1)S(1)} %get-tuple-element.54), channel_id=1, source_target_pairs={{0,3},{1,2},{2,1},{3,0},{4,7},{5,6},{6,5},{7,4},{8,11},{9,10},{10,... | collective-permute-start | bytes 147464 | tf_op jit(solution)/shard_map/ppermute | solution.py:44
  44.7 12.5 %copy-start.10 = (f32[3,32,128]{2,1,0:T(8,128)S(1)}, f32[3,32,128]{2,1,0:T(8,128)}, u32[]{:S(2)}) copy-start(f32[3,32,128]{2,1,0:T(8,128)} %copy-done.9) | copy-start | bytes 147460
  46.5 4.9 %collective-permute-start.7 = (bf16[2,3,32,128]{3,2,1,0:T(8,128)(2,1)S(1)}, bf16[2,3,32,128]{3,2,1,0:T(8,128)(2,1)S(1)}, u32[]{:S(2)}, u32[]{:S(2)}) collective-permute-start(bf16[2,3,32,128]{3,2,1,0:T(8,128)(2,1)S(1)} %get-tuple-element.48), channel_id=1, source_target_pairs={{0,1},{1,0},{2,3},{3,2},{4,5},{5,4},{6,7},{7,6},{8,9},{9,8},{10,11... | collective-permute-start | bytes 147464 | tf_op jit(solution)/shard_map/ppermute | solution.py:44
  46.9 4.5 %collective-permute-start.8 = (bf16[2,3,32,128]{3,2,1,0:T(8,128)(2,1)S(1)}, bf16[2,3,32,128]{3,2,1,0:T(8,128)(2,1)S(1)}, u32[]{:S(2)}, u32[]{:S(2)}) collective-permute-start(bf16[2,3,32,128]{3,2,1,0:T(8,128)(2,1)S(1)} %get-tuple-element.49), channel_id=1, source_target_pairs={{0,2},{1,3},{2,0},{3,1},{4,6},{5,7},{6,4},{7,5},{8,10},{9,11},{10,... | collective-permute-start | bytes 147464 | tf_op jit(solution)/shard_map/ppermute | solution.py:44
  47.1 4.3 %collective-permute-start.9 = (bf16[2,3,32,128]{3,2,1,0:T(8,128)(2,1)S(1)}, bf16[2,3,32,128]{3,2,1,0:T(8,128)(2,1)S(1)}, u32[]{:S(2)}, u32[]{:S(2)}) collective-permute-start(bf16[2,3,32,128]{3,2,1,0:T(8,128)(2,1)S(1)} %get-tuple-element.50), channel_id=1, source_target_pairs={{0,3},{1,2},{2,1},{3,0},{4,7},{5,6},{6,5},{7,4},{8,11},{9,10},{10,... | collective-permute-start | bytes 147464 | tf_op jit(solution)/shard_map/ppermute | solution.py:44
  49.3 4.9 %collective-permute-start.14 = (f32[3,32,128]{2,1,0:T(8,128)S(1)}, f32[3,32,128]{2,1,0:T(8,128)S(1)}, u32[]{:S(2)}, u32[]{:S(2)}) collective-permute-start(f32[3,32,128]{2,1,0:T(8,128)S(1)} %shard_map.44), channel_id=1, source_target_pairs={{8,0},{12,4},{16,8},{20,12},{24,16},{28,20},{0,24},{4,28},{9,1},{1... | collective-permute-start | bytes 147464 | tf_op jit(solution)/shard_map/ppermute | solution.py:26
  51.4 5.7 %collective-permute-start.13 = (f32[3,32,128]{2,1,0:T(8,128)S(1)}, f32[3,32,128]{2,1,0:T(8,128)S(1)}, u32[]{:S(2)}, u32[]{:S(2)}) collective-permute-start(f32[3,32,128]{2,1,0:T(8,128)S(1)} %shard_map.43), channel_id=1, source_target_pairs={{4,0},{8,4},{12,8},{16,12},{20,16},{24,20},{28,24},{0,28},{5,1},{9... | collective-permute-start | bytes 147464 | tf_op jit(solution)/shard_map/ppermute | solution.py:26

commit v5 on v4

v5 whole, which is shorter than its diff:
```python
import functools
import math

import jax
import jax.numpy as jnp
from jax import lax
from jax.experimental import pallas as pl
from jax.experimental.pallas import tpu as pltpu
from jax.sharding import PartitionSpec as P

F32, BF16 = jnp.float32, jnp.bfloat16
VMEM = pl.BlockSpec(memory_space=pltpu.VMEM)
ANY = pl.BlockSpec(memory_space=pl.ANY)
LIMIT = 12 * 1024 * 1024
NT = (((1,), (1,)), ((), ()))
CHUNK = 16


def shape_of(shape, dtype):
    return jax.ShapeDtypeStruct(shape, dtype)


def shift(block, axis, distance):
    count = lax.axis_size(axis)
    return lax.ppermute(block, axis, [((i + distance) % count, i) for i in range(count)])


def both_sides(pair, axis):
    if lax.axis_size(axis) == 2:
        return shift(pair, axis, 1)
    tail, head = jnp.split(pair, 2, axis=1)
    return jnp.concatenate([shift(tail, axis, -1), shift(head, axis, 1)], axis=1)


def exchange(sends):
    nx, ny = lax.axis_size("dx"), lax.axis_size("dy")
    got = []
    for o, piece in enumerate(sends, 1):
        ox, oy = o // ny, o % ny
        route = [
            (i * ny + j, ((i + ox) % nx) * ny + (j + oy) % ny) for i in range(nx) for j in range(ny)
        ]
        got.append(lax.ppermute(piece, ("dx", "dy"), route))
    return got


def call(body, outs, operands, scratch=(), specs=None, out_specs=None, us=0):
    run = pl.pallas_call(
        body,
        out_shape=outs,
        in_specs=specs or [VMEM] * len(operands),
        out_specs=out_specs or [VMEM] * len(outs),
        scratch_shapes=list(scratch),
        compiler_params=pltpu.CompilerParams(vmem_limit_bytes=LIMIT),
        cost_estimate=pl.CostEstimate(
            flops=0, bytes_accessed=int(us * 3e6), transcendentals=0
        ),
    )
    return list(run(*operands))


def destinations(nx, ny):
    x, y = lax.axis_index("dx"), lax.axis_index("dy")
    return [
        lax.rem(x + ox, nx) * ny + lax.rem(y + oy, ny) for ox in range(nx) for oy in range(ny)
    ]


def thirds(value):
    high = value.astype(BF16).astype(F32)
    middle = (value - high).astype(BF16).astype(F32)
    return high, middle, value - high - middle


def edges(psi, coupling, grad, hx, hy, tmp, *, shape):
    wx, wy, wz = shape
    layer, line = wy * wz, wx * wz
    for side, (x, y) in enumerate(((wx - 1, wy - 1), (0, 0))):
        to_x, to_y = side * (layer + wz), side * (line + wz)
        hx[:, to_x : to_x + layer] = psi[:, x * layer : (x + 1) * layer]
        for i in range(wx):
            at = i * layer + y * wz
            hy[:, to_y + i * wz : to_y + (i + 1) * wz] = psi[:, at : at + wz]
        for k in range(3):
            for n, third in enumerate(thirds(coupling[x] * grad[k, x])):
                tmp[(3 * k + n) * wy : (3 * k + n + 1) * wy] = third
        hx[: tmp.shape[0], to_x + layer : to_x + layer + wz] = tmp[...].astype(BF16)
        for k in range(3):
            for n, third in enumerate(thirds(coupling[:, y] * grad[k, :, y])):
                tmp[(3 * k + n) * wx : (3 * k + n + 1) * wx] = third
        hy[: tmp.shape[0], to_y + line : to_y + line + wz] = tmp[...].astype(BF16)


def operators(layers, psi, hx, hy, coupling, grad, u, w, half, back, ahead, tmp, ex, ey, *, shape):
    wx, wy, wz = shape
    layer, line = wy * wz, wx * wz
    states = psi.shape[0]
    half[...] = 0.5 * (coupling[...][None] * grad[...])
    for ref, to, length, count in ((hx, ex, layer, wy), (hy, ey, line, wx)):
        if ref is None:
            continue
        for side in range(2):
            at = side * (length + wz) + length
            tmp[...] = ref[: tmp.shape[0], at : at + wz].astype(F32)
            for k in range(3):
                third = [tmp[(3 * k + n) * count : (3 * k + n + 1) * count] for n in range(3)]
                to[side, k] = 0.5 * (third[0] + third[1] + third[2])
    for k in range(3):
        for x in layers:
            back[k, x] = pltpu.roll(half[k, x], 1, 1)
            ahead[k, x] = pltpu.roll(half[k, x], wz - 1, 1)

    def coeff(k, x, y):
        if x < 0 or x >= wx:
            return ex[int(x >= wx), k, y : y + 1, :]
        if y < 0 or y >= wy:
            return ey[int(y >= wy), k, x : x + 1, :]
        return half[k, x, y : y + 1, :]

    def group(step, _):
        r = pl.ds(pl.multiple_of(step * CHUNK, CHUNK), CHUNK)

        def field(x, y):
            if x < 0:
                ref, at = hx, y * wz
            elif x >= wx:
                ref, at = hx, layer + wz + y * wz
            elif y < 0:
                ref, at = hy, x * wz
            elif y >= wy:
                ref, at = hy, line + wz + x * wz
            else:
                ref, at = psi, x * layer + y * wz
            return ref[r, at : at + wz].astype(F32)

        for n, x in enumerate(layers):
            for y in range(wy):
                here = field(x, y)
                xb, xa = field(x - 1, y), field(x + 1, y)
                yb, ya = field(x, y - 1), field(x, y + 1)
                zb, za = pltpu.roll(here, 1, 1), pltpu.roll(here, wz - 1, 1)
                gx, gy, gz = xa - xb, ya - yb, za - zb
                c1, c2, c3 = [coeff(k, x, y) for k in range(3)]
                cols = slice(n * layer + y * wz, n * layer + (y + 1) * wz)

                def put(ref, k, value):
                    place = pl.ds(pl.multiple_of(k * states + step * CHUNK, CHUNK), CHUNK)
                    ref[place, cols] = value.astype(BF16)

                put(u, 0, c2 * gz - c3 * gy)
                put(u, 1, c3 * gx - c1 * gz)
                put(u, 2, c1 * gy - c2 * gx)

                def dx(k):
                    return coeff(k, x + 1, y) * xa - coeff(k, x - 1, y) * xb

                def dy(k):
                    return coeff(k, x, y + 1) * ya - coeff(k, x, y - 1) * yb

                def dz(k):
                    return ahead[k, x, y : y + 1, :] * za - back[k, x, y : y + 1, :] * zb

                put(w, 0, dy(2) - dz(1))
                put(w, 1, dz(0) - dx(2))
                put(w, 2, dx(1) - dy(0))
        return 0

    lax.fori_loop(0, states // CHUNK, group, 0)


def inner(psi, hy, coupling, grad, u, w, half, back, ahead, tmp, ey, *, shape):
    layers = range(1, shape[0] - 1)
    operators(
        layers, psi, None, hy, coupling, grad, u, w, half, back, ahead, tmp, None, ey, shape=shape
    )


def outer(psi, hx, hy, coupling, grad, u_inner, w_inner, u, w, *scratch, shape):
    operators((0, shape[0] - 1), psi, hx, hy, coupling, grad, u, w, *scratch, shape=shape)


def product(a_inner, a_outer, panel, layer, flip):
    cells = panel.shape[1]
    last = a_outer.shape[1] - layer
    pairs = (
        (a_inner[...], panel[:, layer : cells - layer]),
        (a_outer[:, :layer], panel[:, :layer]),
        (a_outer[:, last:], panel[:, cells - layer :]),
    )
    total = 0.0
    for a, b in pairs:
        a, b = (b, a) if flip else (a, b)
        total = total + lax.dot_general(a, b, NT, preferred_element_type=F32)
    return total


def own_tiles(u_inner, u_outer, w_inner, w_outer, psi, here, *, layer, scale):
    here[...] = product(u_inner, u_outer, psi, layer, False) * scale


def choose(two, psi, out, sem):
    core = lax.rem(lax.axis_index("blk"), 2)

    @pl.when(core == 1)
    def _():
        copy = pltpu.make_async_copy(two, out, sem)
        copy.start()
        copy.wait()

    @pl.when(core != 1)
    def _():
        copy = pltpu.make_async_copy(psi, out, sem)
        copy.start()
        copy.wait()


def tiles(u_inner, u_outer, w_inner, w_outer, panel, here, there, *, layer, scale):
    here[...] = product(u_inner, u_outer, panel, layer, False) * scale
    there[...] = product(w_inner, w_outer, panel, layer, True) * scale


def tiles_and_pieces(
    u_inner, u_outer, w_inner, w_outer, panel, own, here_two, there_two, *rest,
    layer, plane, scale
):
    outs, (here, there) = rest[:-2], rest[-2:]
    tiles(u_inner, u_outer, w_inner, w_outer, panel, here, there, layer=layer, scale=scale)
    states = panel.shape[0]
    rows = states // math.prod(plane)
    for ref, dest in zip(outs, destinations(*plane)):
        for k in range(3):
            place = pl.ds(pl.multiple_of(k * states + dest * rows, rows), rows)
            for t, tile in enumerate((here_two, here, own)):
                ref[t, k] = tile[place, :].astype(ref.dtype)
            place = pl.ds(pl.multiple_of(dest * rows, rows), rows)
            for t, tile in ((3, there), (4, there_two)):
                ref[t, k] = tile[place, k * states : (k + 1) * states].astype(ref.dtype)


def add(keep, *rest):
    parts, (one, two) = rest[:-2], rest[-2:]
    for t, ref in ((3, one), (4, two)):
        total = keep[t]
        for part in parts:
            total = total + part[t].astype(F32)
        ref[...] = total


def assemble(keep, *rest):
    parts, (from_one, from_two, out) = rest[:-3], rest[-3:]
    for k in range(3):
        for t in range(3):
            total = keep[t, k]
            for part in parts:
                total = total + part[t, k].astype(F32)
            out[k, t] = total
        out[k, 3] = from_one[k]
        out[k, 4] = from_two[k]


def on_device(orbitals, coupling, pot_grad):
    states, wx, wy, wz = orbitals.shape
    shape = (wx, wy, wz)
    plane = (lax.axis_size("dx"), lax.axis_size("dy"))
    places = math.prod(plane)
    rows = states // places
    layer, line = wy * wz, wx * wz
    cells = wx * layer
    scale = 1.0 / math.sqrt(cells * places)

    psi = lax.optimization_barrier(orbitals.reshape(states, cells))
    two = shift(psi, "blk", -2)

    spill = -(-9 * max(wx, wy) // 16) * 16
    tmp = pltpu.VMEM((spill, wz), F32)
    hx, hy = call(
        functools.partial(edges, shape=shape),
        [
            shape_of((states, 2 * (layer + wz)), BF16),
            shape_of((states, 2 * (line + wz)), BF16),
        ],
        [psi, coupling, pot_grad],
        scratch=[tmp],
    )
    hx, hy = both_sides(hx, "dx"), both_sides(hy, "dy")

    coeffs = pltpu.VMEM((3, wx, wy, wz), F32)
    ex, ey = pltpu.VMEM((2, 3, wy, wz), F32), pltpu.VMEM((2, 3, wx, wz), F32)
    field = shape_of((3 * states, cells - 2 * layer), BF16)
    u_inner, w_inner = call(
        functools.partial(inner, shape=shape),
        [field, field],
        [psi, hy, coupling, pot_grad],
        scratch=[coeffs] * 3 + [tmp, ey],
        us=2,
    )
    field = shape_of((3 * states, 2 * layer), BF16)
    u_outer, w_outer = call(
        functools.partial(outer, shape=shape),
        [field, field],
        [psi, hx, hy, coupling, pot_grad, u_inner, w_inner],
        scratch=[coeffs] * 3 + [tmp, ex, ey],
    )
    operands = [u_inner, u_outer, w_inner, w_outer]
    tall, wide = shape_of((3 * states, states), F32), shape_of((states, 3 * states), F32)
    (own,) = call(
        functools.partial(own_tiles, layer=layer, scale=scale), [tall], [*operands, psi]
    )

    two, own = lax.optimization_barrier((two, own))
    (mixed,) = call(
        choose,
        [shape_of((states, cells), BF16)],
        [two, psi],
        scratch=[pltpu.SemaphoreType.DMA],
        specs=[ANY, ANY],
        out_specs=[ANY],
    )
    swap = [(i, i ^ 1) for i in range(lax.axis_size("blk"))]
    one = lax.ppermute(mixed, "blk", swap)
    far = call(
        functools.partial(tiles, layer=layer, scale=scale),
        [tall, wide],
        [*operands, two],
        us=1,
    )
    one, far = lax.optimization_barrier((one, far))
    pieces = (5, 3, rows, states)
    keep, *sends = call(
        functools.partial(tiles_and_pieces, layer=layer, plane=plane, scale=scale),
        [shape_of(pieces, F32)] + [shape_of(pieces, BF16)] * (places - 1),
        [*operands, one, own, *far],
        scratch=[pltpu.VMEM(tall.shape, F32), pltpu.VMEM(wide.shape, F32)],
        us=1,
    )
    parts = exchange(sends)
    from_one, from_two = call(add, [shape_of(pieces[1:], F32)] * 2, [keep, *parts])
    from_one, from_two = shift(from_one, "blk", 1), shift(from_two, "blk", 2)
    (out,) = call(
        assemble,
        [shape_of((3, 5, rows, states), F32)],
        [keep, *parts, from_one, from_two],
    )
    return out


def solution(mesh):
    in_specs = (P("blk", "dx", "dy", None), P("dx", "dy", None), P(None, "dx", "dy", None))
    out_specs = P(None, None, ("blk", "dx", "dy"), None)
    return jax.shard_map(
        on_device, mesh=mesh, in_specs=in_specs, out_specs=out_specs, check_vma=False
    )
```

time: 58.2 us -> 49 us (0.84)
  the two profiles are of different devices: /device:TPU:1 before, /device:TPU:0 now
where the time goes in v5:
time: 49 us; the launch traced here: 48.9 us
  waiting for transfers between devices  26 us (53%)
  starting transfers between devices  11.6 us (24%)
  Pallas kernels  9.46 us (19%)
  local copies, waits for them, and re-layouts  1.69 us (3%)
    ppermute x5, waiting for transfers between devices, shift(): lax.ppermute(block, axis, [((i + distance) % count, i) for i in range(cou...  19.5 us
    pallas_call x9, Pallas kernels, call(): return list(run(*operands))  9.46 us
    ppermute x5, starting transfers between devices, shift(): lax.ppermute(block, axis, [((i + distance) % count, i) for i in range(cou...  8.01 us
    ppermute x3, waiting for transfers between devices, exchange(): got.append(lax.ppermute(piece, ('dx', 'dy'), route))  5.72 us
    ppermute x3, starting transfers between devices, exchange(): got.append(lax.ppermute(piece, ('dx', 'dy'), route))  3.55 us
    unnamed x5, local copies, waits for them, and re-layouts  1.69 us
  transfers between devices with their start and end apart: 9, of which 7 were waited for; matrix products, arithmetic and copies ran while one was open for 0% of the time, Pallas kernels for 14%

profile of v5, /device:TPU:0, one launch (start us, length us, event | category | flops | bytes accessed | tf_op | source)
XLA Modules:
  0.0 48.9 jit_solution(6761865845183225531)
XLA Ops:
  0.0 0.0 copy-start
  0.0 0.0 copy-start.1
  0.0 1.7 %copy.6 = bf16[16,8,32,128]{3,1,2,0:T(8,128)(2,1)S(1)} copy(bf16[16,8,32,128]{3,2,1,0:T(8,128)(2,1)} %bitcast.11) | data formatting | bytes 2097152
  1.7 3.1 %collective-permute-start.2 = (bf16[128,4096]{1,0:T(8,128)(2,1)S(1)}, bf16[128,4096]{1,0:T(8,128)(2,1)S(1)}, u32[]{:S(2)}, u32[]{:S(2)}) collective-permute-start(bf16[128,4096]{1,0:T(8,128)(2,1)S(1)} %bitcast.5), channel_id=1, source_target_pairs={{24,0},{28,4},{0,8},{4,12},{8,16},{12,20},{16,24},{20,28},{25,1},{... | collective-permute-start | bytes 3145736 | tf_op jit(solution)/shard_map/ppermute | solution.py:25
  4.8 0.0 copy-done
  4.8 0.0 copy-done.1
  4.8 0.1 shard_map.37
  4.9 1.6 %collective-permute-start.1 = (bf16[128,2304]{1,0:T(8,128)(2,1)S(1)}, bf16[128,2304]{1,0:T(8,128)(2,1)S(1)}, u32[]{:S(2)}, u32[]{:S(2)}) collective-permute-start(bf16[128,2304]{1,0:T(8,128)(2,1)S(1)} %get-tuple-element.26), channel_id=1, source_target_pairs={{2,0},{0,2},{3,1},{1,3},{6,4},{4,6},{7,5},{5,7},{10,8},{8,10},{11,... | collective-permute-start | bytes 1769480 | tf_op jit(solution)/shard_map/ppermute | solution.py:25
  6.5 1.5 %collective-permute-start = (bf16[128,1280]{1,0:T(8,128)(2,1)S(1)}, bf16[128,1280]{1,0:T(8,128)(2,1)S(1)}, u32[]{:S(2)}, u32[]{:S(2)}) collective-permute-start(bf16[128,1280]{1,0:T(8,128)(2,1)S(1)} %get-tuple-element.24), channel_id=1, source_target_pairs={{1,0},{0,1},{3,2},{2,3},{5,4},{4,5},{7,6},{6,7},{9,8},{8,9},{11,10... | collective-permute-start | bytes 983048 | tf_op jit(solution)/shard_map/ppermute | solution.py:25
  8.0 7.4 %collective-permute-done.hy = bf16[128,1280]{1,0:T(8,128)(2,1)S(1)} collective-permute-done((bf16[128,1280]{1,0:T(8,128)(2,1)S(1)}, bf16[128,1280]{1,0:T(8,128)(2,1)S(1)}, u32[]{:S(2)}, u32[]{:S(2)}) %collective-permute-start) | collective-permute-done | bytes 327712 | tf_op jit(solution)/shard_map/ppermute | solution.py:25
  15.4 1.9 %shard_map.38 = (bf16[384,2048]{1,0:T(8,128)(2,1)S(1)}, bf16[384,2048]{1,0:T(8,128)(2,1)S(1)}) custom-call(bf16[128,4096]{1,0:T(8,128)(2,1)S(1)} %bitcast.7, bf16[128,1280]{1,0:T(8,128)(2,1)S(1)} %collective-permute-done.hy, f32[4,8,128]{2,1,0:T(8,128)S(1)} %copy-done.1, f32[3,4,8,128]{3,2,1,0:T(8,128)S(1)} %copy-done), custom_call_target="tpu_custom_call" | custom-call | bytes 6000000 | tf_op jit(solution)/shard_map/pallas_call | solution.py:59
  17.3 2.5 %collective-permute-done.1.hx = bf16[128,2304]{1,0:T(8,128)(2,1)S(1)} collective-permute-done((bf16[128,2304]{1,0:T(8,128)(2,1)S(1)}, bf16[128,2304]{1,0:T(8,128)(2,1)S(1)}, u32[]{:S(2)}, u32[]{:S(2)}) %collective-permute-start.1) | collective-permute-done | bytes 589856 | tf_op jit(solution)/shard_map/ppermute | solution.py:25
  19.8 1.9 %shard_map.39 = (bf16[384,2048]{1,0:T(8,128)(2,1)S(1)}, bf16[384,2048]{1,0:T(8,128)(2,1)S(1)}) custom-call(bf16[128,4096]{1,0:T(8,128)(2,1)S(1)} %bitcast.8, bf16[128,2304]{1,0:T(8,128)(2,1)S(1)} %collective-permute-done.1.hx, bf16[128,1280]{1,0:T(8,128)(2,1)S(1)} %collective-permute-done.hy, f32[4,8,128]{2,1,0:T(8,128)S(1)} %copy-done.1, ...), custom_call_target="tpu_custom_call" | custom-call | tf_op jit(solution)/shard_map/pallas_call | solution.py:59
  21.7 1.0 %shard_map.40.own = f32[384,128]{1,0:T(8,128)S(1)} custom-call(bf16[384,2048]{1,0:T(8,128)(2,1)S(1)} %get-tuple-element.25.u_inner, bf16[384,2048]{1,0:T(8,128)(2,1)S(1)} %get-tuple-element.28.u_outer, bf16[384,2048]{1,0:T(8,128)(2,1)S(1)} %get-tuple-element.27.w_inner, bf16[384,2048]{1,0:T(8,128)(2,1)S(1)} %get-tuple-element.29.w_outer, ...), custom_call_target="tpu_custom_call" | custom-call | tf_op jit(solution)/shard_map/pallas_call | solution.py:59
  22.7 7.3 %collective-permute-done.2.two.panel = bf16[128,4096]{1,0:T(8,128)(2,1)S(1)} collective-permute-done((bf16[128,4096]{1,0:T(8,128)(2,1)S(1)}, bf16[128,4096]{1,0:T(8,128)(2,1)S(1)}, u32[]{:S(2)}, u32[]{:S(2)}) %collective-permute-start.2) | collective-permute-done | bytes 1048608 | tf_op jit(solution)/shard_map/ppermute | solution.py:25
  29.9 0.1 shard_map.41
  30.0 0.1 collective-permute-start.3
  30.1 1.8 %shard_map.42 = (f32[384,128]{1,0:T(8,128)S(1)}, f32[128,384]{1,0:T(8,128)S(1)}) custom-call(bf16[384,2048]{1,0:T(8,128)(2,1)S(1)} %get-tuple-element.25.u_inner, bf16[384,2048]{1,0:T(8,128)(2,1)S(1)} %get-tuple-element.28.u_outer, bf16[384,2048]{1,0:T(8,128)(2,1)S(1)} %get-tuple-element.27.w_inner, bf16[384,2048]{1,0:T(8,128)(2,1)S(1)} %get-tuple-element.29.w_outer, ...), custom_call_target="tpu_custom_call" | custom-call | bytes 3000000 | tf_op jit(solution)/shard_map/pallas_call | solution.py:59
  31.9 0.8 %collective-permute-done.3.panel = bf16[128,4096]{1,0:T(8,128)(2,1)S(1)} collective-permute-done((bf16[128,4096]{1,0:T(8,128)(2,1)S(1)}, bf16[128,4096]{1,0:T(8,128)(2,1)S(1)}, u32[]{:S(2)}, u32[]{:S(2)}) %collective-permute-start.3) | collective-permute-done | bytes 1048608 | tf_op jit(solution)/shard_map/ppermute | solution.py:320
  32.8 1.8 %shard_map.43 = (f32[5,3,32,128]{3,2,1,0:T(8,128)S(1)}, bf16[5,3,32,128]{3,2,1,0:T(8,128)(2,1)S(1)}, bf16[5,3,32,128]{3,2,1,0:T(8,128)(2,1)S(1)}, bf16[5,3,32,128]{3,2,1,0:T(8,128)(2,1)S(1)}) custom-call(bf16[384,2048]{1,0:T(8,128)(2,1)S(1)} %get-tuple-element.25.u_inner, bf16[384,2048]{1,0:T(8,128)(2,1)S(1)} %get-tuple-element.28.u_outer, ...), custom_call_target="tpu_custom_call" | custom-call | bytes 3000000 | tf_op jit(solution)/shard_map/pallas_call | solution.py:59
  34.6 1.6 %collective-permute-start.4 = (bf16[5,3,32,128]{3,2,1,0:T(8,128)(2,1)S(1)}, bf16[5,3,32,128]{3,2,1,0:T(8,128)(2,1)S(1)}, u32[]{:S(2)}, u32[]{:S(2)}) collective-permute-start(bf16[5,3,32,128]{3,2,1,0:T(8,128)(2,1)S(1)} %get-tuple-element.38), channel_id=1, source_target_pairs={{0,1},{1,0},{2,3},{3,2},{4,5},{5,4},{6,7},{7,6},{8,9},{9,8},{10,11... | collective-permute-start | bytes 368648 | tf_op jit(solution)/shard_map/ppermute | solution.py:43
  36.2 1.5 %collective-permute-start.5 = (bf16[5,3,32,128]{3,2,1,0:T(8,128)(2,1)S(1)}, bf16[5,3,32,128]{3,2,1,0:T(8,128)(2,1)S(1)}, u32[]{:S(2)}, u32[]{:S(2)}) collective-permute-start(bf16[5,3,32,128]{3,2,1,0:T(8,128)(2,1)S(1)} %get-tuple-element.39), channel_id=1, source_target_pairs={{0,2},{1,3},{2,0},{3,1},{4,6},{5,7},{6,4},{7,5},{8,10},{9,11},{10,... | collective-permute-start | bytes 368648 | tf_op jit(solution)/shard_map/ppermute | solution.py:43
  37.7 0.5 collective-permute-start.6
  38.2 2.0 %collective-permute-done.4.rest_0_ = bf16[5,3,32,128]{3,2,1,0:T(8,128)(2,1)S(1)} collective-permute-done((bf16[5,3,32,128]{3,2,1,0:T(8,128)(2,1)S(1)}, bf16[5,3,32,128]{3,2,1,0:T(8,128)(2,1)S(1)}, u32[]{:S(2)}, u32[]{:S(2)}) %collective-permute-start.4) | collective-permute-done | bytes 122912 | tf_op jit(solution)/shard_map/ppermute | solution.py:43
  40.2 3.7 %collective-permute-done.5.rest_1_ = bf16[5,3,32,128]{3,2,1,0:T(8,128)(2,1)S(1)} collective-permute-done((bf16[5,3,32,128]{3,2,1,0:T(8,128)(2,1)S(1)}, bf16[5,3,32,128]{3,2,1,0:T(8,128)(2,1)S(1)}, u32[]{:S(2)}, u32[]{:S(2)}) %collective-permute-start.5) | collective-permute-done | bytes 122912 | tf_op jit(solution)/shard_map/ppermute | solution.py:43
  43.9 0.0 collective-permute-done.6.rest_2_
  43.9 0.1 collective-permute-start.7
  44.0 1.7 %collective-permute-start.8 = (f32[3,32,128]{2,1,0:T(8,128)S(1)}, f32[3,32,128]{2,1,0:T(8,128)S(1)}, u32[]{:S(2)}, u32[]{:S(2)}) collective-permute-start(f32[3,32,128]{2,1,0:T(8,128)S(1)} %get-tuple-element.42), channel_id=1, source_target_pairs={{8,0},{12,4},{16,8},{20,12},{24,16},{28,20},{0,24},{4,28},{9,1},{1... | collective-permute-start | bytes 147464 | tf_op jit(solution)/shard_map/ppermute | solution.py:25
  45.8 0.0 collective-permute-done.7.rest_3_
  45.8 2.3 %collective-permute-done.8.rest_4_ = f32[3,32,128]{2,1,0:T(8,128)S(1)} collective-permute-done((f32[3,32,128]{2,1,0:T(8,128)S(1)}, f32[3,32,128]{2,1,0:T(8,128)S(1)}, u32[]{:S(2)}, u32[]{:S(2)}) %collective-permute-start.8) | collective-permute-done | bytes 49184 | tf_op jit(solution)/shard_map/ppermute | solution.py:25
  48.1 0.7 %shard_map.45 = f32[3,5,32,128]{3,2,1,0:T(8,128)} custom-call(f32[5,3,32,128]{3,2,1,0:T(8,128)S(1)} %get-tuple-element.37.keep, bf16[5,3,32,128]{3,2,1,0:T(8,128)(2,1)S(1)} %collective-permute-done.4.rest_0_, bf16[5,3,32,128]{3,2,1,0:T(8,128)(2,1)S(1)} %collective-permute-done.5.rest_1_, bf16[5,3,32,128]{3,2,1,0:T(8,128)(2,1)S(1)} %collective-permute-done.6.rest_2_, ...), custom_call_target="tpu_custom_call" | custom-call | tf_op jit(solution)/shard_map/pallas_call | solution.py:59
  (1 shorter events, 0.0 us)
Async XLA Ops:
  0.0 4.8 %copy-start = (f32[3,4,8,128]{3,2,1,0:T(8,128)S(1)}, f32[3,4,8,128]{3,2,1,0:T(8,128)}, u32[]{:S(2)}) copy-start(f32[3,4,8,128]{3,2,1,0:T(8,128)} %grad.5) | copy-start | bytes 147460
  0.0 4.8 %copy-start.1 = (f32[4,8,128]{2,1,0:T(8,128)S(1)}, f32[4,8,128]{2,1,0:T(8,128)}, u32[]{:S(2)}) copy-start(f32[4,8,128]{2,1,0:T(8,128)} %coupling.5) | copy-start | bytes 49156
  1.7 28.3 %collective-permute-start.2 = (bf16[128,4096]{1,0:T(8,128)(2,1)S(1)}, bf16[128,4096]{1,0:T(8,128)(2,1)S(1)}, u32[]{:S(2)}, u32[]{:S(2)}) collective-permute-start(bf16[128,4096]{1,0:T(8,128)(2,1)S(1)} %bitcast.5), channel_id=1, source_target_pairs={{24,0},{28,4},{0,8},{4,12},{8,16},{12,20},{16,24},{20,28},{25,1},{... | collective-permute-start | bytes 3145736 | tf_op jit(solution)/shard_map/ppermute | solution.py:25
  4.9 14.9 %collective-permute-start.1 = (bf16[128,2304]{1,0:T(8,128)(2,1)S(1)}, bf16[128,2304]{1,0:T(8,128)(2,1)S(1)}, u32[]{:S(2)}, u32[]{:S(2)}) collective-permute-start(bf16[128,2304]{1,0:T(8,128)(2,1)S(1)} %get-tuple-element.26), channel_id=1, source_target_pairs={{2,0},{0,2},{3,1},{1,3},{6,4},{4,6},{7,5},{5,7},{10,8},{8,10},{11,... | collective-permute-start | bytes 1769480 | tf_op jit(solution)/shard_map/ppermute | solution.py:25
  6.5 8.9 %collective-permute-start = (bf16[128,1280]{1,0:T(8,128)(2,1)S(1)}, bf16[128,1280]{1,0:T(8,128)(2,1)S(1)}, u32[]{:S(2)}, u32[]{:S(2)}) collective-permute-start(bf16[128,1280]{1,0:T(8,128)(2,1)S(1)} %get-tuple-element.24), channel_id=1, source_target_pairs={{1,0},{0,1},{3,2},{2,3},{5,4},{4,5},{7,6},{6,7},{9,8},{8,9},{11,10... | collective-permute-start | bytes 983048 | tf_op jit(solution)/shard_map/ppermute | solution.py:25
  30.0 2.7 %collective-permute-start.3 = (bf16[128,4096]{1,0:T(8,128)(2,1)S(1)}, bf16[128,4096]{1,0:T(8,128)(2,1)S(1)}, u32[]{:S(2)}, u32[]{:S(2)}) collective-permute-start(bf16[128,4096]{1,0:T(8,128)(2,1)S(1)} %shard_map.41), channel_id=1, source_target_pairs={{0,4},{4,0},{8,12},{12,8},{16,20},{20,16},{24,28},{28,24},{1,5},{5... | collective-permute-start | bytes 3145736 | tf_op jit(solution)/shard_map/ppermute | solution.py:320
  34.6 5.6 %collective-permute-start.4 = (bf16[5,3,32,128]{3,2,1,0:T(8,128)(2,1)S(1)}, bf16[5,3,32,128]{3,2,1,0:T(8,128)(2,1)S(1)}, u32[]{:S(2)}, u32[]{:S(2)}) collective-permute-start(bf16[5,3,32,128]{3,2,1,0:T(8,128)(2,1)S(1)} %get-tuple-element.38), channel_id=1, source_target_pairs={{0,1},{1,0},{2,3},{3,2},{4,5},{5,4},{6,7},{7,6},{8,9},{9,8},{10,11... | collective-permute-start | bytes 368648 | tf_op jit(solution)/shard_map/ppermute | solution.py:43
  36.2 7.7 %collective-permute-start.5 = (bf16[5,3,32,128]{3,2,1,0:T(8,128)(2,1)S(1)}, bf16[5,3,32,128]{3,2,1,0:T(8,128)(2,1)S(1)}, u32[]{:S(2)}, u32[]{:S(2)}) collective-permute-start(bf16[5,3,32,128]{3,2,1,0:T(8,128)(2,1)S(1)} %get-tuple-element.39), channel_id=1, source_target_pairs={{0,2},{1,3},{2,0},{3,1},{4,6},{5,7},{6,4},{7,5},{8,10},{9,11},{10,... | collective-permute-start | bytes 368648 | tf_op jit(solution)/shard_map/ppermute | solution.py:43
  37.7 6.2 %collective-permute-start.6 = (bf16[5,3,32,128]{3,2,1,0:T(8,128)(2,1)S(1)}, bf16[5,3,32,128]{3,2,1,0:T(8,128)(2,1)S(1)}, u32[]{:S(2)}, u32[]{:S(2)}) collective-permute-start(bf16[5,3,32,128]{3,2,1,0:T(8,128)(2,1)S(1)} %get-tuple-element.40), channel_id=1, source_target_pairs={{0,3},{1,2},{2,1},{3,0},{4,7},{5,6},{6,5},{7,4},{8,11},{9,10},{10,... | collective-permute-start | bytes 368648 | tf_op jit(solution)/shard_map/ppermute | solution.py:43
  43.9 1.9 %collective-permute-start.7 = (f32[3,32,128]{2,1,0:T(8,128)S(1)}, f32[3,32,128]{2,1,0:T(8,128)S(1)}, u32[]{:S(2)}, u32[]{:S(2)}) collective-permute-start(f32[3,32,128]{2,1,0:T(8,128)S(1)} %get-tuple-element.41), channel_id=1, source_target_pairs={{4,0},{8,4},{12,8},{16,12},{20,16},{24,20},{28,24},{0,28},{5,1},{9... | collective-permute-start | bytes 147464 | tf_op jit(solution)/shard_map/ppermute | solution.py:25
  44.0 4.1 %collective-permute-start.8 = (f32[3,32,128]{2,1,0:T(8,128)S(1)}, f32[3,32,128]{2,1,0:T(8,128)S(1)}, u32[]{:S(2)}, u32[]{:S(2)}) collective-permute-start(f32[3,32,128]{2,1,0:T(8,128)S(1)} %get-tuple-element.42), channel_id=1, source_target_pairs={{8,0},{12,4},{16,8},{20,12},{24,16},{28,20},{0,24},{4,28},{9,1},{1... | collective-permute-start | bytes 147464 | tf_op jit(solution)/shard_map/ppermute | solution.py:25

commit v6 on v5

--- a/solution.py
+++ b/solution.py
@@ -30,18 +30,6 @@
         return shift(pair, axis, 1)
     tail, head = jnp.split(pair, 2, axis=1)
     return jnp.concatenate([shift(tail, axis, -1), shift(head, axis, 1)], axis=1)
-
-
-def exchange(sends):
-    nx, ny = lax.axis_size("dx"), lax.axis_size("dy")
-    got = []
-    for o, piece in enumerate(sends, 1):
-        ox, oy = o // ny, o % ny
-        route = [
-            (i * ny + j, ((i + ox) % nx) * ny + (j + oy) % ny) for i in range(nx) for j in range(ny)
-        ]
-        got.append(lax.ppermute(piece, ("dx", "dy"), route))
-    return got
 
 
 def call(body, outs, operands, scratch=(), specs=None, out_specs=None, us=0):
@@ -57,13 +45,6 @@
         ),
     )
     return list(run(*operands))
-
-
-def destinations(nx, ny):
-    x, y = lax.axis_index("dx"), lax.axis_index("dy")
-    return [
-        lax.rem(x + ox, nx) * ny + lax.rem(y + oy, ny) for ox in range(nx) for oy in range(ny)
-    ]
 
 
 def thirds(value):
@@ -223,11 +204,13 @@
     u_inner, u_outer, w_inner, w_outer, panel, own, here_two, there_two, *rest,
     layer, plane, scale
 ):
-    outs, (here, there) = rest[:-2], rest[-2:]
+    keep, sends, here, there = rest
     tiles(u_inner, u_outer, w_inner, w_outer, panel, here, there, layer=layer, scale=scale)
     states = panel.shape[0]
-    rows = states // math.prod(plane)
-    for ref, dest in zip(outs, destinations(*plane)):
+    places = math.prod(plane)
+    rows = states // places
+    me = lax.axis_index("dx") * plane[1] + lax.axis_index("dy")
+    for ref, dest in [(keep, me)] + [(sends.at[d], d) for d in range(places)]:
         for k in range(3):
             place = pl.ds(pl.multiple_of(k * states + dest * rows, rows), rows)
             for t, tile in enumerate((here_two, here, own)):
@@ -237,23 +220,24 @@
                 ref[t, k] = tile[place, k * states : (k + 1) * states].astype(ref.dtype)
 
 
-def add(keep, *rest):
-    parts, (one, two) = rest[:-2], rest[-2:]
-    for t, ref in ((3, one), (4, two)):
-        total = keep[t]
-        for part in parts:
-            total = total + part[t].astype(F32)
-        ref[...] = total
-
-
-def assemble(keep, *rest):
-    parts, (from_one, from_two, out) = rest[:-3], rest[-3:]
+def total_of(keep, parts, t, k):
+    me = lax.axis_index("dx") * lax.axis_size("dy") + lax.axis_index("dy")
+    total = keep[t, k]
+    for d in range(parts.shape[0]):
+        total = total + jnp.where(d == me, 0.0, parts[d, t, k].astype(F32))
+    return total
+
+
+def add(keep, parts, one, two):
+    for k in range(3):
+        one[k] = total_of(keep, parts, 3, k)
+        two[k] = total_of(keep, parts, 4, k)
+
+
+def assemble(keep, parts, from_one, from_two, out):
     for k in range(3):
         for t in range(3):
-            total = keep[t, k]
-            for part in parts:
-                total = total + part[t, k].astype(F32)
-            out[k, t] = total
+            out[k, t] = total_of(keep, parts, t, k)
         out[k, 3] = from_one[k]
         out[k, 4] = from_two[k]
 
@@ -326,20 +310,20 @@
     )
     one, far = lax.optimization_barrier((one, far))
     pieces = (5, 3, rows, states)
-    keep, *sends = call(
+    keep, sends = call(
         functools.partial(tiles_and_pieces, layer=layer, plane=plane, scale=scale),
-        [shape_of(pieces, F32)] + [shape_of(pieces, BF16)] * (places - 1),
+        [shape_of(pieces, F32), shape_of((places, *pieces), BF16)],
         [*operands, one, own, *far],
         scratch=[pltpu.VMEM(tall.shape, F32), pltpu.VMEM(wide.shape, F32)],
         us=1,
     )
-    parts = exchange(sends)
-    from_one, from_two = call(add, [shape_of(pieces[1:], F32)] * 2, [keep, *parts])
+    parts = lax.all_to_all(sends, ("dx", "dy"), 0, 0)
+    from_one, from_two = call(add, [shape_of(pieces[1:], F32)] * 2, [keep, parts])
     from_one, from_two = shift(from_one, "blk", 1), shift(from_two, "blk", 2)
     (out,) = call(
         assemble,
         [shape_of((3, 5, rows, states), F32)],
-        [keep, *parts, from_one, from_two],
+        [keep, parts, from_one, from_two],
     )
     return out
 

time: 49 us -> 51.9 us (1.059)
  blocking collectives: 0 us -> 12.1 us
  waiting for transfers between devices: 26 us -> 20.3 us
  starting transfers between devices: 11.6 us -> 8.07 us
    all_to_all x0 -> x1, blocking collectives: none -> 12.1 us  [on_device(): parts = lax.all_to_all(sends, ('dx', 'dy'), 0, 0)]
    ppermute x3 -> x0, waiting for transfers between devices: 5.72 us -> none  [exchange(): got.append(lax.ppermute(piece, ('dx', 'dy'), route))]
    ppermute x3 -> x0, starting transfers between devices: 3.55 us -> none  [exchange(): got.append(lax.ppermute(piece, ('dx', 'dy'), route))]
  transfers between devices with their start and end apart: 9 -> 6, of which waited for: 7 -> 5; matrix products, arithmetic and copies ran while one was open for 0% -> 0% of each run, Pallas kernels for 14% -> 13%
where the time goes in v6:
time: 51.9 us; the launch traced here: 51.7 us
  waiting for transfers between devices  20.3 us (39%)
  blocking collectives  12.1 us (23%)
  Pallas kernels  9.5 us (18%)
  starting transfers between devices  8.07 us (16%)
  local copies, waits for them, and re-layouts  1.69 us (3%)
    ppermute x5, waiting for transfers between devices, shift(): lax.ppermute(block, axis, [((i + distance) % count, i) for i in range(cou...  19.5 us
    all_to_all x1, blocking collectives, on_device(): parts = lax.all_to_all(sends, ('dx', 'dy'), 0, 0)  12.1 us
    pallas_call x9, Pallas kernels, call(): return list(run(*operands))  9.5 us
    ppermute x5, starting transfers between devices, shift(): lax.ppermute(block, axis, [((i + distance) % count, i) for i in range(cou...  8 us
    unnamed x5, local copies, waits for them, and re-layouts  1.69 us
  transfers between devices with their start and end apart: 6, of which 5 were waited for; matrix products, arithmetic and copies ran while one was open for 0% of the time, Pallas kernels for 13%

profile of v6, /device:TPU:0, one launch (start us, length us, event | category | flops | bytes accessed | tf_op | source)
XLA Modules:
  0.0 51.7 jit_solution(1559878201614978602)
XLA Ops:
  0.0 0.0 copy-start
  0.0 0.0 copy-start.1
  0.0 1.7 %copy.6 = bf16[16,8,32,128]{3,1,2,0:T(8,128)(2,1)S(1)} copy(bf16[16,8,32,128]{3,2,1,0:T(8,128)(2,1)} %bitcast.11) | data formatting | bytes 2097152
  1.7 3.1 %collective-permute-start.2 = (bf16[128,4096]{1,0:T(8,128)(2,1)S(1)}, bf16[128,4096]{1,0:T(8,128)(2,1)S(1)}, u32[]{:S(2)}, u32[]{:S(2)}) collective-permute-start(bf16[128,4096]{1,0:T(8,128)(2,1)S(1)} %bitcast.5), channel_id=1, source_target_pairs={{24,0},{28,4},{0,8},{4,12},{8,16},{12,20},{16,24},{20,28},{25,1},{... | collective-permute-start | bytes 3145736 | tf_op jit(solution)/shard_map/ppermute | solution.py:25
  4.8 0.0 copy-done
  4.8 0.0 copy-done.1
  4.8 0.1 shard_map.37
  4.9 1.6 %collective-permute-start.1 = (bf16[128,2304]{1,0:T(8,128)(2,1)S(1)}, bf16[128,2304]{1,0:T(8,128)(2,1)S(1)}, u32[]{:S(2)}, u32[]{:S(2)}) collective-permute-start(bf16[128,2304]{1,0:T(8,128)(2,1)S(1)} %get-tuple-element.24), channel_id=1, source_target_pairs={{2,0},{0,2},{3,1},{1,3},{6,4},{4,6},{7,5},{5,7},{10,8},{8,10},{11,... | collective-permute-start | bytes 1769480 | tf_op jit(solution)/shard_map/ppermute | solution.py:25
  6.5 1.5 %collective-permute-start = (bf16[128,1280]{1,0:T(8,128)(2,1)S(1)}, bf16[128,1280]{1,0:T(8,128)(2,1)S(1)}, u32[]{:S(2)}, u32[]{:S(2)}) collective-permute-start(bf16[128,1280]{1,0:T(8,128)(2,1)S(1)} %get-tuple-element.22), channel_id=1, source_target_pairs={{1,0},{0,1},{3,2},{2,3},{5,4},{4,5},{7,6},{6,7},{9,8},{8,9},{11,10... | collective-permute-start | bytes 983048 | tf_op jit(solution)/shard_map/ppermute | solution.py:25
  8.0 7.4 %collective-permute-done.hy = bf16[128,1280]{1,0:T(8,128)(2,1)S(1)} collective-permute-done((bf16[128,1280]{1,0:T(8,128)(2,1)S(1)}, bf16[128,1280]{1,0:T(8,128)(2,1)S(1)}, u32[]{:S(2)}, u32[]{:S(2)}) %collective-permute-start) | collective-permute-done | bytes 327712 | tf_op jit(solution)/shard_map/ppermute | solution.py:25
  15.4 1.9 %shard_map.38 = (bf16[384,2048]{1,0:T(8,128)(2,1)S(1)}, bf16[384,2048]{1,0:T(8,128)(2,1)S(1)}) custom-call(bf16[128,4096]{1,0:T(8,128)(2,1)S(1)} %bitcast.7, bf16[128,1280]{1,0:T(8,128)(2,1)S(1)} %collective-permute-done.hy, f32[4,8,128]{2,1,0:T(8,128)S(1)} %copy-done.1, f32[3,4,8,128]{3,2,1,0:T(8,128)S(1)} %copy-done), custom_call_target="tpu_custom_call" | custom-call | bytes 6000000 | tf_op jit(solution)/shard_map/pallas_call | solution.py:47
  17.3 2.5 %collective-permute-done.1.hx = bf16[128,2304]{1,0:T(8,128)(2,1)S(1)} collective-permute-done((bf16[128,2304]{1,0:T(8,128)(2,1)S(1)}, bf16[128,2304]{1,0:T(8,128)(2,1)S(1)}, u32[]{:S(2)}, u32[]{:S(2)}) %collective-permute-start.1) | collective-permute-done | bytes 589856 | tf_op jit(solution)/shard_map/ppermute | solution.py:25
  19.8 1.9 %shard_map.39 = (bf16[384,2048]{1,0:T(8,128)(2,1)S(1)}, bf16[384,2048]{1,0:T(8,128)(2,1)S(1)}) custom-call(bf16[128,4096]{1,0:T(8,128)(2,1)S(1)} %bitcast.8, bf16[128,2304]{1,0:T(8,128)(2,1)S(1)} %collective-permute-done.1.hx, bf16[128,1280]{1,0:T(8,128)(2,1)S(1)} %collective-permute-done.hy, f32[4,8,128]{2,1,0:T(8,128)S(1)} %copy-done.1, ...), custom_call_target="tpu_custom_call" | custom-call | tf_op jit(solution)/shard_map/pallas_call | solution.py:47
  21.7 1.0 %shard_map.40.own = f32[384,128]{1,0:T(8,128)S(1)} custom-call(bf16[384,2048]{1,0:T(8,128)(2,1)S(1)} %get-tuple-element.23.u_inner, bf16[384,2048]{1,0:T(8,128)(2,1)S(1)} %get-tuple-element.26.u_outer, bf16[384,2048]{1,0:T(8,128)(2,1)S(1)} %get-tuple-element.25.w_inner, bf16[384,2048]{1,0:T(8,128)(2,1)S(1)} %get-tuple-element.27.w_outer, ...), custom_call_target="tpu_custom_call" | custom-call | tf_op jit(solution)/shard_map/pallas_call | solution.py:47
  22.7 7.3 %collective-permute-done.2.two.panel = bf16[128,4096]{1,0:T(8,128)(2,1)S(1)} collective-permute-done((bf16[128,4096]{1,0:T(8,128)(2,1)S(1)}, bf16[128,4096]{1,0:T(8,128)(2,1)S(1)}, u32[]{:S(2)}, u32[]{:S(2)}) %collective-permute-start.2) | collective-permute-done | bytes 1048608 | tf_op jit(solution)/shard_map/ppermute | solution.py:25
  29.9 0.1 shard_map.41
  30.0 0.1 collective-permute-start.3
  30.1 1.8 %shard_map.42 = (f32[384,128]{1,0:T(8,128)S(1)}, f32[128,384]{1,0:T(8,128)S(1)}) custom-call(bf16[384,2048]{1,0:T(8,128)(2,1)S(1)} %get-tuple-element.23.u_inner, bf16[384,2048]{1,0:T(8,128)(2,1)S(1)} %get-tuple-element.26.u_outer, bf16[384,2048]{1,0:T(8,128)(2,1)S(1)} %get-tuple-element.25.w_inner, bf16[384,2048]{1,0:T(8,128)(2,1)S(1)} %get-tuple-element.27.w_outer, ...), custom_call_target="tpu_custom_call" | custom-call | bytes 3000000 | tf_op jit(solution)/shard_map/pallas_call | solution.py:47
  31.9 0.8 %collective-permute-done.3.panel = bf16[128,4096]{1,0:T(8,128)(2,1)S(1)} collective-permute-done((bf16[128,4096]{1,0:T(8,128)(2,1)S(1)}, bf16[128,4096]{1,0:T(8,128)(2,1)S(1)}, u32[]{:S(2)}, u32[]{:S(2)}) %collective-permute-start.3) | collective-permute-done | bytes 1048608 | tf_op jit(solution)/shard_map/ppermute | solution.py:304
  32.8 1.8 %shard_map.43 = (f32[5,3,32,128]{3,2,1,0:T(8,128)S(1)}, bf16[4,5,3,32,128]{4,3,2,1,0:T(8,128)(2,1)S(1)}) custom-call(bf16[384,2048]{1,0:T(8,128)(2,1)S(1)} %get-tuple-element.23.u_inner, bf16[384,2048]{1,0:T(8,128)(2,1)S(1)} %get-tuple-element.26.u_outer, bf16[384,2048]{1,0:T(8,128)(2,1)S(1)} %get-tuple-element.25.w_inner, ...), custom_call_target="tpu_custom_call" | custom-call | bytes 3000000 | tf_op jit(solution)/shard_map/pallas_call | solution.py:47
  34.6 12.1 %all_to_all.5.parts = bf16[4,5,3,32,128]{4,3,2,1,0:T(8,128)(2,1)S(1)} all-to-all(bf16[4,5,3,32,128]{4,3,2,1,0:T(8,128)(2,1)S(1)} %get-tuple-element.36), channel_id=1, replica_groups=mesh['blk'=8,'dx'=2,'dy'=2] {'dx','dy'}, dimensions={0} | all-to-all | bytes 983040 | tf_op jit(solution)/shard_map/all_to_all | solution.py:320
  46.7 0.1 shard_map.44
  46.7 0.1 collective-permute-start.4
  46.8 1.8 %collective-permute-start.5 = (f32[3,32,128]{2,1,0:T(8,128)S(1)}, f32[3,32,128]{2,1,0:T(8,128)S(1)}, u32[]{:S(2)}, u32[]{:S(2)}) collective-permute-start(f32[3,32,128]{2,1,0:T(8,128)S(1)} %get-tuple-element.38), channel_id=1, source_target_pairs={{8,0},{12,4},{16,8},{20,12},{24,16},{28,20},{0,24},{4,28},{9,1},{1... | collective-permute-start | bytes 147464 | tf_op jit(solution)/shard_map/ppermute | solution.py:25
  48.6 0.0 collective-permute-done.4.from_one
  48.6 2.3 %collective-permute-done.5.from_two = f32[3,32,128]{2,1,0:T(8,128)S(1)} collective-permute-done((f32[3,32,128]{2,1,0:T(8,128)S(1)}, f32[3,32,128]{2,1,0:T(8,128)S(1)}, u32[]{:S(2)}, u32[]{:S(2)}) %collective-permute-start.5) | collective-permute-done | bytes 49184 | tf_op jit(solution)/shard_map/ppermute | solution.py:25
  50.9 0.8 %shard_map.45 = f32[3,5,32,128]{3,2,1,0:T(8,128)} custom-call(f32[5,3,32,128]{3,2,1,0:T(8,128)S(1)} %get-tuple-element.35.keep, bf16[4,5,3,32,128]{4,3,2,1,0:T(8,128)(2,1)S(1)} %all_to_all.5.parts, f32[3,32,128]{2,1,0:T(8,128)S(1)} %collective-permute-done.4.from_one, f32[3,32,128]{2,1,0:T(8,128)S(1)} %collective-permute-done.5.from_two), custom_call_target="tpu_custom_call" | custom-call | tf_op jit(solution)/shard_map/pallas_call | solution.py:47
Async XLA Ops:
  0.0 4.8 %copy-start = (f32[3,4,8,128]{3,2,1,0:T(8,128)S(1)}, f32[3,4,8,128]{3,2,1,0:T(8,128)}, u32[]{:S(2)}) copy-start(f32[3,4,8,128]{3,2,1,0:T(8,128)} %grad.5) | copy-start | bytes 147460
  0.0 4.8 %copy-start.1 = (f32[4,8,128]{2,1,0:T(8,128)S(1)}, f32[4,8,128]{2,1,0:T(8,128)}, u32[]{:S(2)}) copy-start(f32[4,8,128]{2,1,0:T(8,128)} %coupling.5) | copy-start | bytes 49156
  1.7 28.3 %collective-permute-start.2 = (bf16[128,4096]{1,0:T(8,128)(2,1)S(1)}, bf16[128,4096]{1,0:T(8,128)(2,1)S(1)}, u32[]{:S(2)}, u32[]{:S(2)}) collective-permute-start(bf16[128,4096]{1,0:T(8,128)(2,1)S(1)} %bitcast.5), channel_id=1, source_target_pairs={{24,0},{28,4},{0,8},{4,12},{8,16},{12,20},{16,24},{20,28},{25,1},{... | collective-permute-start | bytes 3145736 | tf_op jit(solution)/shard_map/ppermute | solution.py:25
  4.9 14.9 %collective-permute-start.1 = (bf16[128,2304]{1,0:T(8,128)(2,1)S(1)}, bf16[128,2304]{1,0:T(8,128)(2,1)S(1)}, u32[]{:S(2)}, u32[]{:S(2)}) collective-permute-start(bf16[128,2304]{1,0:T(8,128)(2,1)S(1)} %get-tuple-element.24), channel_id=1, source_target_pairs={{2,0},{0,2},{3,1},{1,3},{6,4},{4,6},{7,5},{5,7},{10,8},{8,10},{11,... | collective-permute-start | bytes 1769480 | tf_op jit(solution)/shard_map/ppermute | solution.py:25
  6.5 8.9 %collective-permute-start = (bf16[128,1280]{1,0:T(8,128)(2,1)S(1)}, bf16[128,1280]{1,0:T(8,128)(2,1)S(1)}, u32[]{:S(2)}, u32[]{:S(2)}) collective-permute-start(bf16[128,1280]{1,0:T(8,128)(2,1)S(1)} %get-tuple-element.22), channel_id=1, source_target_pairs={{1,0},{0,1},{3,2},{2,3},{5,4},{4,5},{7,6},{6,7},{9,8},{8,9},{11,10... | collective-permute-start | bytes 983048 | tf_op jit(solution)/shard_map/ppermute | solution.py:25
  30.0 2.7 %collective-permute-start.3 = (bf16[128,4096]{1,0:T(8,128)(2,1)S(1)}, bf16[128,4096]{1,0:T(8,128)(2,1)S(1)}, u32[]{:S(2)}, u32[]{:S(2)}) collective-permute-start(bf16[128,4096]{1,0:T(8,128)(2,1)S(1)} %shard_map.41), channel_id=1, source_target_pairs={{0,4},{4,0},{8,12},{12,8},{16,20},{20,16},{24,28},{28,24},{1,5},{5... | collective-permute-start | bytes 3145736 | tf_op jit(solution)/shard_map/ppermute | solution.py:304
  46.7 1.9 %collective-permute-start.4 = (f32[3,32,128]{2,1,0:T(8,128)S(1)}, f32[3,32,128]{2,1,0:T(8,128)S(1)}, u32[]{:S(2)}, u32[]{:S(2)}) collective-permute-start(f32[3,32,128]{2,1,0:T(8,128)S(1)} %get-tuple-element.37), channel_id=1, source_target_pairs={{4,0},{8,4},{12,8},{16,12},{20,16},{24,20},{28,24},{0,28},{5,1},{9... | collective-permute-start | bytes 147464 | tf_op jit(solution)/shard_map/ppermute | solution.py:25
  46.8 4.1 %collective-permute-start.5 = (f32[3,32,128]{2,1,0:T(8,128)S(1)}, f32[3,32,128]{2,1,0:T(8,128)S(1)}, u32[]{:S(2)}, u32[]{:S(2)}) collective-permute-start(f32[3,32,128]{2,1,0:T(8,128)S(1)} %get-tuple-element.38), channel_id=1, source_target_pairs={{8,0},{12,4},{16,8},{20,12},{24,16},{28,20},{0,24},{4,28},{9,1},{1... | collective-permute-start | bytes 147464 | tf_op jit(solution)/shard_map/ppermute | solution.py:25

commit v7 on v5

v7 whole, which is shorter than its diff:
```python
import functools
import math

import jax
import jax.numpy as jnp
from jax import lax
from jax.experimental import pallas as pl
from jax.experimental.pallas import tpu as pltpu
from jax.sharding import PartitionSpec as P

F32, BF16 = jnp.float32, jnp.bfloat16
VMEM = pl.BlockSpec(memory_space=pltpu.VMEM)
ANY = pl.BlockSpec(memory_space=pl.ANY)
LIMIT = 12 * 1024 * 1024
NT = (((1,), (1,)), ((), ()))
CHUNK = 16
PIECES = 2


def shape_of(shape, dtype):
    return jax.ShapeDtypeStruct(shape, dtype)


def shift(block, axis, distance):
    count = lax.axis_size(axis)
    return lax.ppermute(block, axis, [((i + distance) % count, i) for i in range(count)])


def both_sides(pair, axis):
    if lax.axis_size(axis) == 2:
        return shift(pair, axis, 1)
    tail, head = jnp.split(pair, 2, axis=1)
    return jnp.concatenate([shift(tail, axis, -1), shift(head, axis, 1)], axis=1)


def exchange(sends):
    nx, ny = lax.axis_size("dx"), lax.axis_size("dy")
    got = []
    for o, piece in enumerate(sends, 1):
        ox, oy = o // ny, o % ny
        route = [
            (i * ny + j, ((i + ox) % nx) * ny + (j + oy) % ny) for i in range(nx) for j in range(ny)
        ]
        got.append(lax.ppermute(piece, ("dx", "dy"), route))
    return got


def call(body, outs, operands, scratch=(), specs=None, out_specs=None, us=0):
    run = pl.pallas_call(
        body,
        out_shape=outs,
        in_specs=specs or [VMEM] * len(operands),
        out_specs=out_specs or [VMEM] * len(outs),
        scratch_shapes=list(scratch),
        compiler_params=pltpu.CompilerParams(vmem_limit_bytes=LIMIT),
        cost_estimate=pl.CostEstimate(
            flops=0, bytes_accessed=int(us * 3e6), transcendentals=0
        ),
    )
    return list(run(*operands))


def destinations(nx, ny):
    x, y = lax.axis_index("dx"), lax.axis_index("dy")
    return [
        lax.rem(x + ox, nx) * ny + lax.rem(y + oy, ny) for ox in range(nx) for oy in range(ny)
    ]


def thirds(value):
    high = value.astype(BF16).astype(F32)
    middle = (value - high).astype(BF16).astype(F32)
    return high, middle, value - high - middle


def edges(*refs, shape):
    pieces, (coupling, grad, tail, head, hy, tmp) = refs[:-6], refs[-6:]
    wx, wy, wz = shape
    layer, line = wy * wz, wx * wz
    for side, (x, y, hx) in enumerate(((wx - 1, wy - 1, tail), (0, 0, head))):
        to_y = side * (line + wz)
        end = 0
        for psi in pieces:
            r = slice(end, end + psi.shape[0])
            end = r.stop
            hx[r, :layer] = psi[:, x * layer : (x + 1) * layer]
            for i in range(wx):
                at = i * layer + y * wz
                hy[r, to_y + i * wz : to_y + (i + 1) * wz] = psi[:, at : at + wz]
        for k in range(3):
            for n, third in enumerate(thirds(coupling[x] * grad[k, x])):
                tmp[(3 * k + n) * wy : (3 * k + n + 1) * wy] = third
        hx[: tmp.shape[0], layer:] = tmp[...].astype(BF16)
        for k in range(3):
            for n, third in enumerate(thirds(coupling[:, y] * grad[k, :, y])):
                tmp[(3 * k + n) * wx : (3 * k + n + 1) * wx] = third
        hy[: tmp.shape[0], to_y + line : to_y + line + wz] = tmp[...].astype(BF16)


def operators(*refs, layers, shape):
    pieces, refs = refs[:PIECES], refs[PIECES:]
    outer = len(refs) == 12
    hx = refs[0] if outer else None
    hy, coupling, grad, u, w, half, back, ahead, tmp, ex, ey = refs[-11:]
    wx, wy, wz = shape
    layer, line = wy * wz, wx * wz
    states = sum(psi.shape[0] for psi in pieces)
    half[...] = 0.5 * (coupling[...][None] * grad[...])

    def unpack(ref, at, to, count):
        tmp[...] = ref[: tmp.shape[0], at : at + wz].astype(F32)
        for k in range(3):
            third = [tmp[(3 * k + n) * count : (3 * k + n + 1) * count] for n in range(3)]
            to[k] = 0.5 * (third[0] + third[1] + third[2])

    if outer:
        unpack(hx, layer, ex, wy)
    for side in range(2):
        unpack(hy, side * (line + wz) + line, ey.at[side], wx)
    for k in range(3):
        for x in layers:
            back[k, x] = pltpu.roll(half[k, x], 1, 1)
            ahead[k, x] = pltpu.roll(half[k, x], wz - 1, 1)

    def coeff(k, x, y):
        if x < 0 or x >= wx:
            return ex[k, y : y + 1, :]
        if y < 0 or y >= wy:
            return ey[int(y >= wy), k, x : x + 1, :]
        return half[k, x, y : y + 1, :]

    def group(psi, start, step, _):
        own = pl.ds(pl.multiple_of(step * CHUNK, CHUNK), CHUNK)
        first = start + step * CHUNK
        r = pl.ds(pl.multiple_of(first, CHUNK), CHUNK)

        def field(x, y):
            if x < 0 or x >= wx:
                return hx[r, y * wz : (y + 1) * wz].astype(F32)
            if y < 0 or y >= wy:
                at = int(y >= wy) * (line + wz) + x * wz
                return hy[r, at : at + wz].astype(F32)
            at = x * layer + y * wz
            return psi[own, at : at + wz].astype(F32)

        for n, x in enumerate(layers):
            for y in range(wy):
                here = field(x, y)
                xb, xa = field(x - 1, y), field(x + 1, y)
                yb, ya = field(x, y - 1), field(x, y + 1)
                zb, za = pltpu.roll(here, 1, 1), pltpu.roll(here, wz - 1, 1)
                gx, gy, gz = xa - xb, ya - yb, za - zb
                c1, c2, c3 = [coeff(k, x, y) for k in range(3)]
                cols = slice(n * layer + y * wz, n * layer + (y + 1) * wz)

                def put(ref, k, value):
                    place = pl.ds(pl.multiple_of(k * states + first, CHUNK), CHUNK)
                    ref[place, cols] = value.astype(BF16)

                put(u, 0, c2 * gz - c3 * gy)
                put(u, 1, c3 * gx - c1 * gz)
                put(u, 2, c1 * gy - c2 * gx)

                def dx(k):
                    return coeff(k, x + 1, y) * xa - coeff(k, x - 1, y) * xb

                def dy(k):
                    return coeff(k, x, y + 1) * ya - coeff(k, x, y - 1) * yb

                def dz(k):
                    return ahead[k, x, y : y + 1, :] * za - back[k, x, y : y + 1, :] * zb

                put(w, 0, dy(2) - dz(1))
                put(w, 1, dz(0) - dx(2))
                put(w, 2, dx(1) - dy(0))
        return 0

    end = 0
    for psi in pieces:
        lax.fori_loop(0, psi.shape[0] // CHUNK, functools.partial(group, psi, end), 0)
        end += psi.shape[0]


def product(fields, panel, layer, flip=False):
    inner, left, right = fields
    cells = inner.shape[1] + 2 * layer
    total = 0.0
    for a, start, stop in (
        (inner, layer, cells - layer), (left, 0, layer), (right, cells - layer, cells)
    ):
        a, b = a[...], panel(slice(start, stop))
        a, b = (b, a) if flip else (a, b)
        total = total + lax.dot_general(a, b, NT, preferred_element_type=F32)
    return total


def stacked(*pieces):
    def rows(cols):
        values = []
        for piece in pieces:
            if isinstance(piece, int):
                piece = jnp.zeros((piece, cols.stop - cols.start), BF16)
            else:
                piece = piece[:, cols]
            if piece.shape[0]:
                values.append(piece)
        return jnp.concatenate(values, axis=0)

    return rows


def own_tiles(*refs, layer, scale):
    fields, pieces, here = refs[:3], refs[3:-1], refs[-1]
    here[...] = product(fields, stacked(*pieces), layer) * scale


def choose(two, psi, out, sem):
    core = lax.rem(lax.axis_index("blk"), 2)

    @pl.when(core == 1)
    def _():
        copy = pltpu.make_async_copy(two, out, sem)
        copy.start()
        copy.wait()

    @pl.when(core != 1)
    def _():
        copy = pltpu.make_async_copy(psi, out, sem)
        copy.start()
        copy.wait()


def tiles(*refs, before, layer, scale):
    u, w, (two, one, here, there) = refs[:3], refs[3:6], refs[6:]
    states = here.shape[0] // 3
    after = states - before - two.shape[0]
    both = stacked(before, two, after, before, one, after)
    here[...] = product(u, both, layer) * scale
    both = product(w, stacked(two, one), layer, True) * scale
    there[0] = both[: two.shape[0]]
    there[1] = both[two.shape[0] :]


def tiles_and_pieces(*refs, before, layer, plane, scale):
    (own, here_first, there_first), rest = refs[8:11], refs[11:]
    outs, (here, there) = rest[:-2], rest[-2:]
    tiles(*refs[:8], here, there.at[:, before:], before=before, layer=layer, scale=scale)
    here[...] += here_first[...]
    there[:, :before] = there_first[...]
    states = here.shape[0] // 3
    rows = states // math.prod(plane)
    for ref, dest in zip(outs, destinations(*plane)):
        for k in range(3):
            place = pl.ds(pl.multiple_of(k * states + dest * rows, rows), rows)
            ref[0, k] = here[place, :states].astype(ref.dtype)
            ref[1, k] = here[place, states:].astype(ref.dtype)
            ref[2, k] = own[place, :].astype(ref.dtype)
            place = pl.ds(pl.multiple_of(dest * rows, rows), rows)
            cols = slice(k * states, (k + 1) * states)
            ref[3, k] = there[1, place, cols].astype(ref.dtype)
            ref[4, k] = there[0, place, cols].astype(ref.dtype)


def add(keep, *rest):
    parts, (one, two) = rest[:-2], rest[-2:]
    for t, ref in ((3, one), (4, two)):
        total = keep[t]
        for part in parts:
            total = total + part[t].astype(F32)
        ref[...] = total


def assemble(keep, *rest):
    parts, (from_one, from_two, out) = rest[:-3], rest[-3:]
    for k in range(3):
        for t in range(3):
            total = keep[t, k]
            for part in parts:
                total = total + part[t, k].astype(F32)
            out[k, t] = total
        out[k, 3] = from_one[k]
        out[k, 4] = from_two[k]


def on_device(orbitals, coupling, pot_grad):
    states, wx, wy, wz = orbitals.shape
    shape = (wx, wy, wz)
    plane = (lax.axis_size("dx"), lax.axis_size("dy"))
    places = math.prod(plane)
    rows = states // places
    layer, line = wy * wz, wx * wz
    cells = wx * layer
    scale = 1.0 / math.sqrt(cells * places)

    before = states * 3 // 8 // CHUNK * CHUNK
    psi = []
    for piece in jnp.split(orbitals, [before], axis=0):
        psi.append(lax.optimization_barrier(piece.reshape(piece.shape[0], cells)))
    two = [shift(piece, "blk", -2) for piece in psi]

    tmp = pltpu.VMEM((-(-9 * max(wx, wy) // 16) * 16, wz), F32)
    tail, head, hy = call(
        functools.partial(edges, shape=shape),
        [shape_of((states, layer + wz), BF16)] * 2 + [shape_of((states, 2 * (line + wz)), BF16)],
        [*psi, coupling, pot_grad],
        scratch=[tmp],
    )
    from_left, from_right = shift(tail, "dx", -1), shift(head, "dx", 1)
    hy = both_sides(hy, "dy")

    coeffs = pltpu.VMEM((3, wx, wy, wz), F32)
    ends = [pltpu.VMEM((3, wy, wz), F32), pltpu.VMEM((2, 3, wx, wz), F32)]
    u, w = [], []
    for layers, hx in (
        (range(1, wx - 1), []), ((0,), [from_left]), ((wx - 1,), [from_right])
    ):
        field = shape_of((3 * states, len(layers) * layer), BF16)
        results = call(
            functools.partial(operators, layers=layers, shape=shape),
            [field, field],
            [*psi, *hx, hy, coupling, pot_grad],
            scratch=[coeffs] * 3 + [tmp, *ends],
        )
        u.append(results[0])
        w.append(results[1])
    tall = shape_of((3 * states, states), F32)
    (own,) = call(
        functools.partial(own_tiles, layer=layer, scale=scale), [tall], [*u, *psi]
    )

    swap = [(i, i ^ 1) for i in range(lax.axis_size("blk"))]

    def swapped(n):
        (mixed,) = call(
            choose,
            [shape_of(psi[n].shape, BF16)],
            [two[n], psi[n]],
            scratch=[pltpu.SemaphoreType.DMA],
            specs=[ANY, ANY],
            out_specs=[ANY],
        )
        return lax.ppermute(mixed, "blk", swap)

    both_here = (3 * states, 2 * states)
    two[0], u = lax.optimization_barrier((two[0], u))
    one = [swapped(0)]
    one[0], own = lax.optimization_barrier((one[0], own))
    first = call(
        functools.partial(tiles, before=0, layer=layer, scale=scale),
        [shape_of(both_here, F32), shape_of((2, before, 3 * states), F32)],
        [*u, *w, two[0], one[0]],
    )
    two[1], first[0] = lax.optimization_barrier((two[1], first[0]))
    one.append(swapped(1))
    pieces = (5, 3, rows, states)
    keep, *sends = call(
        functools.partial(tiles_and_pieces, before=before, layer=layer, plane=plane, scale=scale),
        [shape_of(pieces, F32)] + [shape_of(pieces, BF16)] * (places - 1),
        [*u, *w, two[1], one[1], own, *first],
        scratch=[pltpu.VMEM(both_here, F32), pltpu.VMEM((2, states, 3 * states), F32)],
    )
    parts = exchange(sends)
    from_one, from_two = call(add, [shape_of(pieces[1:], F32)] * 2, [keep, *parts])
    from_one, from_two = shift(from_one, "blk", 1), shift(from_two, "blk", 2)
    (out,) = call(
        assemble,
        [shape_of((3, 5, rows, states), F32)],
        [keep, *parts, from_one, from_two],
    )
    return out


def solution(mesh):
    in_specs = (P("blk", "dx", "dy", None), P("dx", "dy", None), P(None, "dx", "dy", None))
    out_specs = P(None, None, ("blk", "dx", "dy"), None)
    return jax.shard_map(
        on_device, mesh=mesh, in_specs=in_specs, out_specs=out_specs, check_vma=False
    )
```

time: 49 us -> 48.3 us (0.986)
  waiting for transfers between devices: 26 us -> 22.4 us
  starting transfers between devices: 11.6 us -> 13.8 us
  Pallas kernels: 9.46 us -> 10.3 us
    ppermute x5 -> x7, waiting for transfers between devices: 19.5 us -> 13.9 us  [shift(): lax.ppermute(block, axis, [((i + distance) % count, i) for i in range(cou...]
    ppermute x5 -> x7, starting transfers between devices: 8.01 us -> 10.1 us  [shift(): lax.ppermute(block, axis, [((i + distance) % count, i) for i in range(cou...]
    ppermute x1 -> x2, waiting for transfers between devices: 0.81 us -> 2.8 us  [swapped(): return lax.ppermute(mixed, 'blk', swap)]
    unnamed x5 -> x6, local copies, waits for them, and re-layouts: 1.69 us -> 0.43 us
    split x0 -> x3, local copies, waits for them, and re-layouts: none -> 1.09 us  [on_device(): jnp.split(orbitals, [before], axis=0)]
    pallas_call x9 -> x11, Pallas kernels: 9.46 us -> 10.3 us  [call(): return list(run(*operands))]
  transfers between devices with their start and end apart: 9 -> 12, of which waited for: 7 -> 9; matrix products, arithmetic and copies ran while one was open for 0% -> 1% of each run, Pallas kernels for 14% -> 15%
where the time goes in v7:
time: 48.3 us; the launch traced here: 48.1 us
  waiting for transfers between devices  22.4 us (46%)
  starting transfers between devices  13.8 us (29%)
  Pallas kernels  10.3 us (21%)
  local copies, waits for them, and re-layouts  1.52 us (3%)
    ppermute x7, waiting for transfers between devices, shift(): lax.ppermute(block, axis, [((i + distance) % count, i) for i in range(cou...  13.9 us
    pallas_call x11, Pallas kernels, call(): return list(run(*operands))  10.3 us
    ppermute x7, starting transfers between devices, shift(): lax.ppermute(block, axis, [((i + distance) % count, i) for i in range(cou...  10.1 us
    ppermute x3, waiting for transfers between devices, exchange(): got.append(lax.ppermute(piece, ('dx', 'dy'), route))  5.72 us
    ppermute x3, starting transfers between devices, exchange(): got.append(lax.ppermute(piece, ('dx', 'dy'), route))  3.55 us
    ppermute x2, waiting for transfers between devices, swapped(): return lax.ppermute(mixed, 'blk', swap)  2.8 us
    split x3, local copies, waits for them, and re-layouts, on_device(): jnp.split(orbitals, [before], axis=0)  1.09 us
  transfers between devices with their start and end apart: 12, of which 9 were waited for; matrix products, arithmetic and copies ran while one was open for 1% of the time, Pallas kernels for 15%

profile of v7, /device:TPU:0, one launch (start us, length us, event | category | flops | bytes accessed | tf_op | source)
XLA Modules:
  0.0 48.1 jit_solution(4351727613342970788)
XLA Ops:
  0.0 1.1 %split.6 = bf16[48,4,8,128]{3,2,1,0:T(8,128)(2,1)S(1)} slice(bf16[128,4,8,128]{3,2,1,0:T(8,128)(2,1)} %param.3), slice={[0:48], [0:4], [0:8], [0:128]} | slice | bytes 786432 | tf_op jit(solution)/shard_map/split | solution.py:297
  1.1 0.2 copy.9
  1.3 3.1 %collective-permute-start = (bf16[48,4096]{1,0:T(8,128)(2,1)S(1)}, bf16[48,4096]{1,0:T(8,128)(2,1)S(1)}, u32[]{:S(2)}, u32[]{:S(2)}) collective-permute-start(bf16[48,4096]{1,0:T(8,128)(2,1)S(1)} %bitcast.17), channel_id=1, source_target_pairs={{24,0},{28,4},{0,8},{4,12},{8,16},{12,20},{16,24},{20,28},{25,1},{... | collective-permute-start | bytes 1179656 | tf_op jit(solution)/shard_map/ppermute | solution.py:26
  4.4 0.3 copy.8
  4.6 0.1 shard_map.37
  4.8 1.6 %collective-permute-start.1 = (bf16[128,1280]{1,0:T(8,128)(2,1)S(1)}, bf16[128,1280]{1,0:T(8,128)(2,1)S(1)}, u32[]{:S(2)}, u32[]{:S(2)}) collective-permute-start(bf16[128,1280]{1,0:T(8,128)(2,1)S(1)} %get-tuple-element.30), channel_id=1, source_target_pairs={{1,0},{0,1},{3,2},{2,3},{5,4},{4,5},{7,6},{6,7},{9,8},{8,9},{11,10... | collective-permute-start | bytes 983048 | tf_op jit(solution)/shard_map/ppermute | solution.py:26
  6.3 1.5 %collective-permute-start.3 = (bf16[128,1152]{1,0:T(8,128)(2,1)S(1)}, bf16[128,1152]{1,0:T(8,128)(2,1)S(1)}, u32[]{:S(2)}, u32[]{:S(2)}) collective-permute-start(bf16[128,1152]{1,0:T(8,128)(2,1)S(1)} %get-tuple-element.34), channel_id=1, source_target_pairs={{2,0},{0,2},{3,1},{1,3},{6,4},{4,6},{7,5},{5,7},{10,8},{8,10},{11,... | collective-permute-start | bytes 884744 | tf_op jit(solution)/shard_map/ppermute | solution.py:26
  7.9 0.5 %collective-permute-start.2 = (bf16[128,1152]{1,0:T(8,128)(2,1)S(1)}, bf16[128,1152]{1,0:T(8,128)(2,1)S(1)}, u32[]{:S(2)}, u32[]{:S(2)}) collective-permute-start(bf16[128,1152]{1,0:T(8,128)(2,1)S(1)} %get-tuple-element.32), channel_id=1, source_target_pairs={{2,0},{0,2},{3,1},{1,3},{6,4},{4,6},{7,5},{5,7},{10,8},{8,10},{11,... | collective-permute-start | bytes 884744 | tf_op jit(solution)/shard_map/ppermute | solution.py:26
  8.4 1.6 %collective-permute-start.4 = (bf16[80,4096]{1,0:T(8,128)(2,1)S(1)}, bf16[80,4096]{1,0:T(8,128)(2,1)S(1)}, u32[]{:S(2)}, u32[]{:S(2)}) collective-permute-start(bf16[80,4096]{1,0:T(8,128)(2,1)S(1)} %bitcast.11), channel_id=1, source_target_pairs={{24,0},{28,4},{0,8},{4,12},{8,16},{12,20},{16,24},{20,28},{25,1},{... | collective-permute-start | bytes 1966088 | tf_op jit(solution)/shard_map/ppermute | solution.py:26
  9.9 4.1 %collective-permute-done.1.refs_2_.refs_3_ = bf16[128,1280]{1,0:T(8,128)(2,1)S(1)} collective-permute-done((bf16[128,1280]{1,0:T(8,128)(2,1)S(1)}, bf16[128,1280]{1,0:T(8,128)(2,1)S(1)}, u32[]{:S(2)}, u32[]{:S(2)}) %collective-permute-start.1) | collective-permute-done | bytes 327712 | tf_op jit(solution)/shard_map/ppermute | solution.py:26
  14.0 1.9 %shard_map.38 = (bf16[384,2048]{1,0:T(8,128)(2,1)S(1)}, bf16[384,2048]{1,0:T(8,128)(2,1)S(1)}) custom-call(bf16[48,4096]{1,0:T(8,128)(2,1)S(1)} %bitcast.19, bf16[80,4096]{1,0:T(8,128)(2,1)S(1)} %bitcast.12, bf16[128,1280]{1,0:T(8,128)(2,1)S(1)} %collective-permute-done.1.refs_2_.refs_3_, f32[4,8,128]{2,1,0:T(8,128)S(1)} %copy-done.1, ...), custom_call_target="tpu_custom_call" | custom-call | tf_op jit(solution)/shard_map/pallas_call | solution.py:60
  15.9 0.4 collective-permute-done.3.refs_2_
  16.3 1.2 %shard_map.40 = (bf16[384,1024]{1,0:T(8,128)(2,1)S(1)}, bf16[384,1024]{1,0:T(8,128)(2,1)S(1)}) custom-call(bf16[48,4096]{1,0:T(8,128)(2,1)S(1)} %bitcast.20, bf16[80,4096]{1,0:T(8,128)(2,1)S(1)} %bitcast.13, bf16[128,1152]{1,0:T(8,128)(2,1)S(1)} %collective-permute-done.3.refs_2_, bf16[128,1280]{1,0:T(8,128)(2,1)S(1)} %collective-permute-done.1.refs_2_.refs_3_, ...), custom_call_target="tpu_custom_call" | custom-call | tf_op jit(solution)/shard_map/pallas_call | solution.py:60
  17.5 3.4 %collective-permute-done.2.refs_2_ = bf16[128,1152]{1,0:T(8,128)(2,1)S(1)} collective-permute-done((bf16[128,1152]{1,0:T(8,128)(2,1)S(1)}, bf16[128,1152]{1,0:T(8,128)(2,1)S(1)}, u32[]{:S(2)}, u32[]{:S(2)}) %collective-permute-start.2) | collective-permute-done | bytes 294944 | tf_op jit(solution)/shard_map/ppermute | solution.py:26
  20.8 1.1 %shard_map.39 = (bf16[384,1024]{1,0:T(8,128)(2,1)S(1)}, bf16[384,1024]{1,0:T(8,128)(2,1)S(1)}) custom-call(bf16[48,4096]{1,0:T(8,128)(2,1)S(1)} %bitcast.21, bf16[80,4096]{1,0:T(8,128)(2,1)S(1)} %bitcast.14, bf16[128,1152]{1,0:T(8,128)(2,1)S(1)} %collective-permute-done.2.refs_2_, bf16[128,1280]{1,0:T(8,128)(2,1)S(1)} %collective-permute-done.1.refs_2_.refs_3_, ...), custom_call_target="tpu_custom_call" | custom-call | tf_op jit(solution)/shard_map/pallas_call | solution.py:60
  21.9 0.2 shard_map.41
  22.3 1.0 %shard_map.42.refs_8_ = f32[384,128]{1,0:T(8,128)S(1)} custom-call(bf16[384,2048]{1,0:T(8,128)(2,1)S(1)} %get-tuple-element.36.refs_0_, bf16[384,1024]{1,0:T(8,128)(2,1)S(1)} %get-tuple-element.37.refs_1_, bf16[384,1024]{1,0:T(8,128)(2,1)S(1)} %get-tuple-element.38.refs_2_, bf16[48,4096]{1,0:T(8,128)(2,1)S(1)} %bitcast.23, bf16[80,4096]{1,0:T(8,128)(2,1)S(1)} %bitcast.15), custom_call_target="tpu_custom_call" | custom-call | tf_op jit(solution)/shard_map/pallas_call | solution.py:60
  23.2 0.7 %collective-permute-done.5.refs_7_ = bf16[48,4096]{1,0:T(8,128)(2,1)S(1)} collective-permute-done((bf16[48,4096]{1,0:T(8,128)(2,1)S(1)}, bf16[48,4096]{1,0:T(8,128)(2,1)S(1)}, u32[]{:S(2)}, u32[]{:S(2)}) %collective-permute-start.5) | collective-permute-done | bytes 393248 | tf_op jit(solution)/shard_map/ppermute | solution.py:342
  24.0 1.8 %shard_map.43 = (f32[384,256]{1,0:T(8,128)S(1)}, f32[2,48,384]{2,1,0:T(8,128)S(1)}) custom-call(bf16[384,2048]{1,0:T(8,128)(2,1)S(1)} %get-tuple-element.36.refs_0_, bf16[384,1024]{1,0:T(8,128)(2,1)S(1)} %get-tuple-element.37.refs_1_, bf16[384,1024]{1,0:T(8,128)(2,1)S(1)} %get-tuple-element.38.refs_2_, bf16[384,2048]{1,0:T(8,128)(2,1)S(1)} %get-tuple-element.39.refs_3_, ...), custom_call_target="tpu_custom_call" | custom-call | tf_op jit(solution)/shard_map/pallas_call | solution.py:60
  25.8 3.7 %collective-permute-done.4.two.refs_6_ = bf16[80,4096]{1,0:T(8,128)(2,1)S(1)} collective-permute-done((bf16[80,4096]{1,0:T(8,128)(2,1)S(1)}, bf16[80,4096]{1,0:T(8,128)(2,1)S(1)}, u32[]{:S(2)}, u32[]{:S(2)}) %collective-permute-start.4) | collective-permute-done | bytes 655392 | tf_op jit(solution)/shard_map/ppermute | solution.py:26
  29.5 0.2 shard_map.44
  29.8 2.1 %collective-permute-done.6.refs_7_ = bf16[80,4096]{1,0:T(8,128)(2,1)S(1)} collective-permute-done((bf16[80,4096]{1,0:T(8,128)(2,1)S(1)}, bf16[80,4096]{1,0:T(8,128)(2,1)S(1)}, u32[]{:S(2)}, u32[]{:S(2)}) %collective-permute-start.6) | collective-permute-done | bytes 655392 | tf_op jit(solution)/shard_map/ppermute | solution.py:342
  31.9 2.0 %shard_map.45 = (f32[5,3,32,128]{3,2,1,0:T(8,128)S(1)}, bf16[5,3,32,128]{3,2,1,0:T(8,128)(2,1)S(1)}, bf16[5,3,32,128]{3,2,1,0:T(8,128)(2,1)S(1)}, bf16[5,3,32,128]{3,2,1,0:T(8,128)(2,1)S(1)}) custom-call(bf16[384,2048]{1,0:T(8,128)(2,1)S(1)} %get-tuple-element.36.refs_0_, bf16[384,1024]{1,0:T(8,128)(2,1)S(1)} %get-tuple-element.37.refs_1_, ...), custom_call_target="tpu_custom_call" | custom-call | tf_op jit(solution)/shard_map/pallas_call | solution.py:60
  33.9 1.6 %collective-permute-start.7 = (bf16[5,3,32,128]{3,2,1,0:T(8,128)(2,1)S(1)}, bf16[5,3,32,128]{3,2,1,0:T(8,128)(2,1)S(1)}, u32[]{:S(2)}, u32[]{:S(2)}) collective-permute-start(bf16[5,3,32,128]{3,2,1,0:T(8,128)(2,1)S(1)} %get-tuple-element.50), channel_id=1, source_target_pairs={{0,1},{1,0},{2,3},{3,2},{4,5},{5,4},{6,7},{7,6},{8,9},{9,8},{10,11... | collective-permute-start | bytes 368648 | tf_op jit(solution)/shard_map/ppermute | solution.py:44
  35.4 1.5 %collective-permute-start.8 = (bf16[5,3,32,128]{3,2,1,0:T(8,128)(2,1)S(1)}, bf16[5,3,32,128]{3,2,1,0:T(8,128)(2,1)S(1)}, u32[]{:S(2)}, u32[]{:S(2)}) collective-permute-start(bf16[5,3,32,128]{3,2,1,0:T(8,128)(2,1)S(1)} %get-tuple-element.51), channel_id=1, source_target_pairs={{0,2},{1,3},{2,0},{3,1},{4,6},{5,7},{6,4},{7,5},{8,10},{9,11},{10,... | collective-permute-start | bytes 368648 | tf_op jit(solution)/shard_map/ppermute | solution.py:44
  37.0 0.5 collective-permute-start.9
  37.4 2.0 %collective-permute-done.7.rest_0_ = bf16[5,3,32,128]{3,2,1,0:T(8,128)(2,1)S(1)} collective-permute-done((bf16[5,3,32,128]{3,2,1,0:T(8,128)(2,1)S(1)}, bf16[5,3,32,128]{3,2,1,0:T(8,128)(2,1)S(1)}, u32[]{:S(2)}, u32[]{:S(2)}) %collective-permute-start.7) | collective-permute-done | bytes 122912 | tf_op jit(solution)/shard_map/ppermute | solution.py:44
  39.5 3.7 %collective-permute-done.8.rest_1_ = bf16[5,3,32,128]{3,2,1,0:T(8,128)(2,1)S(1)} collective-permute-done((bf16[5,3,32,128]{3,2,1,0:T(8,128)(2,1)S(1)}, bf16[5,3,32,128]{3,2,1,0:T(8,128)(2,1)S(1)}, u32[]{:S(2)}, u32[]{:S(2)}) %collective-permute-start.8) | collective-permute-done | bytes 122912 | tf_op jit(solution)/shard_map/ppermute | solution.py:44
  43.2 0.1 collective-permute-start.10
  43.3 1.7 %collective-permute-start.11 = (f32[3,32,128]{2,1,0:T(8,128)S(1)}, f32[3,32,128]{2,1,0:T(8,128)S(1)}, u32[]{:S(2)}, u32[]{:S(2)}) collective-permute-start(f32[3,32,128]{2,1,0:T(8,128)S(1)} %get-tuple-element.54), channel_id=1, source_target_pairs={{8,0},{12,4},{16,8},{20,12},{24,16},{28,20},{0,24},{4,28},{9,1},{1... | collective-permute-start | bytes 147464 | tf_op jit(solution)/shard_map/ppermute | solution.py:26
  45.1 2.3 %collective-permute-done.11.rest_4_ = f32[3,32,128]{2,1,0:T(8,128)S(1)} collective-permute-done((f32[3,32,128]{2,1,0:T(8,128)S(1)}, f32[3,32,128]{2,1,0:T(8,128)S(1)}, u32[]{:S(2)}, u32[]{:S(2)}) %collective-permute-start.11) | collective-permute-done | bytes 49184 | tf_op jit(solution)/shard_map/ppermute | solution.py:26
  47.4 0.7 %shard_map.47 = f32[3,5,32,128]{3,2,1,0:T(8,128)} custom-call(f32[5,3,32,128]{3,2,1,0:T(8,128)S(1)} %get-tuple-element.49.keep, bf16[5,3,32,128]{3,2,1,0:T(8,128)(2,1)S(1)} %collective-permute-done.7.rest_0_, bf16[5,3,32,128]{3,2,1,0:T(8,128)(2,1)S(1)} %collective-permute-done.8.rest_1_, bf16[5,3,32,128]{3,2,1,0:T(8,128)(2,1)S(1)} %collective-permute-done.9.rest_2_, ...), custom_call_target="tpu_custom_call" | custom-call | tf_op jit(solution)/shard_map/pallas_call | solution.py:60
  (12 shorter events, 0.2 us)
Async XLA Ops:
  0.0 4.4 %slice-start = ((bf16[128,4,8,128]{3,2,1,0:T(8,128)(2,1)}), bf16[80,4,8,128]{3,2,1,0:T(8,128)(2,1)S(1)}, s32[]{:S(2)}) async-start(bf16[128,4,8,128]{3,2,1,0:T(8,128)(2,1)} %param.3), calls=%async_computation | async-start | bytes 1310720 | tf_op jit(solution)/shard_map/split | solution.py:297
  1.1 3.5 %copy-start = (f32[3,4,8,128]{3,2,1,0:T(8,128)S(1)}, f32[3,4,8,128]{3,2,1,0:T(8,128)}, u32[]{:S(2)}) copy-start(f32[3,4,8,128]{3,2,1,0:T(8,128)} %refs_5_.3) | copy-start | bytes 147460
  1.1 3.5 %copy-start.1 = (f32[4,8,128]{2,1,0:T(8,128)S(1)}, f32[4,8,128]{2,1,0:T(8,128)}, u32[]{:S(2)}) copy-start(f32[4,8,128]{2,1,0:T(8,128)} %refs_4_.5) | copy-start | bytes 49156
  1.3 20.7 %collective-permute-start = (bf16[48,4096]{1,0:T(8,128)(2,1)S(1)}, bf16[48,4096]{1,0:T(8,128)(2,1)S(1)}, u32[]{:S(2)}, u32[]{:S(2)}) collective-permute-start(bf16[48,4096]{1,0:T(8,128)(2,1)S(1)} %bitcast.17), channel_id=1, source_target_pairs={{24,0},{28,4},{0,8},{4,12},{8,16},{12,20},{16,24},{20,28},{25,1},{... | collective-permute-start | bytes 1179656 | tf_op jit(solution)/shard_map/ppermute | solution.py:26
  4.8 9.2 %collective-permute-start.1 = (bf16[128,1280]{1,0:T(8,128)(2,1)S(1)}, bf16[128,1280]{1,0:T(8,128)(2,1)S(1)}, u32[]{:S(2)}, u32[]{:S(2)}) collective-permute-start(bf16[128,1280]{1,0:T(8,128)(2,1)S(1)} %get-tuple-element.30), channel_id=1, source_target_pairs={{1,0},{0,1},{3,2},{2,3},{5,4},{4,5},{7,6},{6,7},{9,8},{8,9},{11,10... | collective-permute-start | bytes 983048 | tf_op jit(solution)/shard_map/ppermute | solution.py:26
  6.3 9.9 %collective-permute-start.3 = (bf16[128,1152]{1,0:T(8,128)(2,1)S(1)}, bf16[128,1152]{1,0:T(8,128)(2,1)S(1)}, u32[]{:S(2)}, u32[]{:S(2)}) collective-permute-start(bf16[128,1152]{1,0:T(8,128)(2,1)S(1)} %get-tuple-element.34), channel_id=1, source_target_pairs={{2,0},{0,2},{3,1},{1,3},{6,4},{4,6},{7,5},{5,7},{10,8},{8,10},{11,... | collective-permute-start | bytes 884744 | tf_op jit(solution)/shard_map/ppermute | solution.py:26
  7.9 13.0 %collective-permute-start.2 = (bf16[128,1152]{1,0:T(8,128)(2,1)S(1)}, bf16[128,1152]{1,0:T(8,128)(2,1)S(1)}, u32[]{:S(2)}, u32[]{:S(2)}) collective-permute-start(bf16[128,1152]{1,0:T(8,128)(2,1)S(1)} %get-tuple-element.32), channel_id=1, source_target_pairs={{2,0},{0,2},{3,1},{1,3},{6,4},{4,6},{7,5},{5,7},{10,8},{8,10},{11,... | collective-permute-start | bytes 884744 | tf_op jit(solution)/shard_map/ppermute | solution.py:26
  8.4 21.2 %collective-permute-start.4 = (bf16[80,4096]{1,0:T(8,128)(2,1)S(1)}, bf16[80,4096]{1,0:T(8,128)(2,1)S(1)}, u32[]{:S(2)}, u32[]{:S(2)}) collective-permute-start(bf16[80,4096]{1,0:T(8,128)(2,1)S(1)} %bitcast.11), channel_id=1, source_target_pairs={{24,0},{28,4},{0,8},{4,12},{8,16},{12,20},{16,24},{20,28},{25,1},{... | collective-permute-start | bytes 1966088 | tf_op jit(solution)/shard_map/ppermute | solution.py:26
  22.2 1.8 %collective-permute-start.5 = (bf16[48,4096]{1,0:T(8,128)(2,1)S(1)}, bf16[48,4096]{1,0:T(8,128)(2,1)S(1)}, u32[]{:S(2)}, u32[]{:S(2)}) collective-permute-start(bf16[48,4096]{1,0:T(8,128)(2,1)S(1)} %shard_map.41), channel_id=1, source_target_pairs={{0,4},{4,0},{8,12},{12,8},{16,20},{20,16},{24,28},{28,24},{1,5},{5... | collective-permute-start | bytes 1179656 | tf_op jit(solution)/shard_map/ppermute | solution.py:342
  29.8 2.2 %collective-permute-start.6 = (bf16[80,4096]{1,0:T(8,128)(2,1)S(1)}, bf16[80,4096]{1,0:T(8,128)(2,1)S(1)}, u32[]{:S(2)}, u32[]{:S(2)}) collective-permute-start(bf16[80,4096]{1,0:T(8,128)(2,1)S(1)} %shard_map.44), channel_id=1, source_target_pairs={{0,4},{4,0},{8,12},{12,8},{16,20},{20,16},{24,28},{28,24},{1,5},{5... | collective-permute-start | bytes 1966088 | tf_op jit(solution)/shard_map/ppermute | solution.py:342
  33.9 5.6 %collective-permute-start.7 = (bf16[5,3,32,128]{3,2,1,0:T(8,128)(2,1)S(1)}, bf16[5,3,32,128]{3,2,1,0:T(8,128)(2,1)S(1)}, u32[]{:S(2)}, u32[]{:S(2)}) collective-permute-start(bf16[5,3,32,128]{3,2,1,0:T(8,128)(2,1)S(1)} %get-tuple-element.50), channel_id=1, source_target_pairs={{0,1},{1,0},{2,3},{3,2},{4,5},{5,4},{6,7},{7,6},{8,9},{9,8},{10,11... | collective-permute-start | bytes 368648 | tf_op jit(solution)/shard_map/ppermute | solution.py:44
  35.4 7.7 %collective-permute-start.8 = (bf16[5,3,32,128]{3,2,1,0:T(8,128)(2,1)S(1)}, bf16[5,3,32,128]{3,2,1,0:T(8,128)(2,1)S(1)}, u32[]{:S(2)}, u32[]{:S(2)}) collective-permute-start(bf16[5,3,32,128]{3,2,1,0:T(8,128)(2,1)S(1)} %get-tuple-element.51), channel_id=1, source_target_pairs={{0,2},{1,3},{2,0},{3,1},{4,6},{5,7},{6,4},{7,5},{8,10},{9,11},{10,... | collective-permute-start | bytes 368648 | tf_op jit(solution)/shard_map/ppermute | solution.py:44
  37.0 6.2 %collective-permute-start.9 = (bf16[5,3,32,128]{3,2,1,0:T(8,128)(2,1)S(1)}, bf16[5,3,32,128]{3,2,1,0:T(8,128)(2,1)S(1)}, u32[]{:S(2)}, u32[]{:S(2)}) collective-permute-start(bf16[5,3,32,128]{3,2,1,0:T(8,128)(2,1)S(1)} %get-tuple-element.52), channel_id=1, source_target_pairs={{0,3},{1,2},{2,1},{3,0},{4,7},{5,6},{6,5},{7,4},{8,11},{9,10},{10,... | collective-permute-start | bytes 368648 | tf_op jit(solution)/shard_map/ppermute | solution.py:44
  43.2 1.9 %collective-permute-start.10 = (f32[3,32,128]{2,1,0:T(8,128)S(1)}, f32[3,32,128]{2,1,0:T(8,128)S(1)}, u32[]{:S(2)}, u32[]{:S(2)}) collective-permute-start(f32[3,32,128]{2,1,0:T(8,128)S(1)} %get-tuple-element.53), channel_id=1, source_target_pairs={{4,0},{8,4},{12,8},{16,12},{20,16},{24,20},{28,24},{0,28},{5,1},{9... | collective-permute-start | bytes 147464 | tf_op jit(solution)/shard_map/ppermute | solution.py:26
  43.3 4.1 %collective-permute-start.11 = (f32[3,32,128]{2,1,0:T(8,128)S(1)}, f32[3,32,128]{2,1,0:T(8,128)S(1)}, u32[]{:S(2)}, u32[]{:S(2)}) collective-permute-start(f32[3,32,128]{2,1,0:T(8,128)S(1)} %get-tuple-element.54), channel_id=1, source_target_pairs={{8,0},{12,4},{16,8},{20,12},{24,16},{28,20},{0,24},{4,28},{9,1},{1... | collective-permute-start | bytes 147464 | tf_op jit(solution)/shard_map/ppermute | solution.py:26

commit v8 on v7

--- a/solution.py
+++ b/solution.py
@@ -231,55 +231,70 @@
 
 
 def tiles(*refs, before, layer, scale):
-    u, w, (two, one, here, there) = refs[:3], refs[3:6], refs[6:]
+    u, w, (panel, here, there) = refs[:3], refs[3:6], refs[6:]
     states = here.shape[0] // 3
-    after = states - before - two.shape[0]
+    after = states - before - panel.shape[0]
+    here[...] = product(u, stacked(before, panel, after), layer) * scale
+    there[...] = product(w, stacked(panel), layer, True) * scale
+
+
+def both_tiles(*refs, before, layer, scale):
+    fields, (two, one), outs = refs[:6], refs[6:8], refs[8:]
+    here_two, there_two, here_one, there_one = outs
+    states = here_two.shape[0] // 3
+    height = two.shape[0]
+    after = states - before - height
     both = stacked(before, two, after, before, one, after)
-    here[...] = product(u, both, layer) * scale
-    both = product(w, stacked(two, one), layer, True) * scale
-    there[0] = both[: two.shape[0]]
-    there[1] = both[two.shape[0] :]
-
-
-def tiles_and_pieces(*refs, before, layer, plane, scale):
-    (own, here_first, there_first), rest = refs[8:11], refs[11:]
+    here = product(fields[:3], both, layer) * scale
+    here_two[...], here_one[...] = here[:, :states], here[:, states:]
+    there = product(fields[3:], stacked(two, one), layer, True) * scale
+    there_two[...], there_one[...] = there[:height], there[height:]
+
+
+def tiles_and_pieces(*refs, before, layer, plane, scale, with_own):
+    here_first, there_first, *rest = refs[7:]
+    own = [rest.pop(0)] if with_own else []
     outs, (here, there) = rest[:-2], rest[-2:]
-    tiles(*refs[:8], here, there.at[:, before:], before=before, layer=layer, scale=scale)
+    tiles(*refs[:7], here, there.at[before:], before=before, layer=layer, scale=scale)
     here[...] += here_first[...]
-    there[:, :before] = there_first[...]
+    there[:before] = there_first[...]
     states = here.shape[0] // 3
     rows = states // math.prod(plane)
     for ref, dest in zip(outs, destinations(*plane)):
         for k in range(3):
             place = pl.ds(pl.multiple_of(k * states + dest * rows, rows), rows)
-            ref[0, k] = here[place, :states].astype(ref.dtype)
-            ref[1, k] = here[place, states:].astype(ref.dtype)
-            ref[2, k] = own[place, :].astype(ref.dtype)
+            for t, tile in enumerate((here, *own)):
+                ref[t, k] = tile[place, :].astype(ref.dtype)
             place = pl.ds(pl.multiple_of(dest * rows, rows), rows)
             cols = slice(k * states, (k + 1) * states)
-            ref[3, k] = there[1, place, cols].astype(ref.dtype)
-            ref[4, k] = there[0, place, cols].astype(ref.dtype)
+            ref[len(own) + 1, k] = there[place, cols].astype(ref.dtype)
 
 
 def add(keep, *rest):
-    parts, (one, two) = rest[:-2], rest[-2:]
-    for t, ref in ((3, one), (4, two)):
-        total = keep[t]
-        for part in parts:
-            total = total + part[t].astype(F32)
-        ref[...] = total
-
-
-def assemble(keep, *rest):
-    parts, (from_one, from_two, out) = rest[:-3], rest[-3:]
+    parts, out = rest[:-1], rest[-1]
+    total = keep[keep.shape[0] - 1]
+    for part in parts:
+        total = total + part[keep.shape[0] - 1].astype(F32)
+    out[...] = total
+
+
+def assemble(*refs):
+    from_one, from_two, out = refs[-3:]
+    size = (len(refs) - 3) // 2
     for k in range(3):
-        for t in range(3):
-            total = keep[t, k]
-            for part in parts:
-                total = total + part[t, k].astype(F32)
+        for t, group, n in ((0, refs[:size], 0), (1, refs[size:-3], 0), (2, refs[:size], 1)):
+            total = group[0][n, k]
+            for part in group[1:]:
+                total = total + part[n, k].astype(F32)
             out[k, t] = total
         out[k, 3] = from_one[k]
         out[k, 4] = from_two[k]
+
+
+def fetch(whole, piece, sem):
+    copy = pltpu.make_async_copy(whole.at[pl.ds(0, piece.shape[0])], piece, sem)
+    copy.start()
+    copy.wait()
 
 
 def on_device(orbitals, coupling, pot_grad):
@@ -293,8 +308,15 @@
     scale = 1.0 / math.sqrt(cells * places)
 
     before = states * 3 // 8 // CHUNK * CHUNK
+    (first,) = call(
+        fetch,
+        [shape_of((before, wx, wy, wz), BF16)],
+        [orbitals],
+        scratch=[pltpu.SemaphoreType.DMA],
+        specs=[pl.BlockSpec(memory_space=pltpu.HBM)],
+    )
     psi = []
-    for piece in jnp.split(orbitals, [before], axis=0):
+    for piece in (first, orbitals[before:]):
         psi.append(lax.optimization_barrier(piece.reshape(piece.shape[0], cells)))
     two = [shift(piece, "blk", -2) for piece in psi]
 
@@ -341,31 +363,49 @@
         )
         return lax.ppermute(mixed, "blk", swap)
 
-    both_here = (3 * states, 2 * states)
+    wide = shape_of((before, 3 * states), F32)
     two[0], u = lax.optimization_barrier((two[0], u))
     one = [swapped(0)]
     one[0], own = lax.optimization_barrier((one[0], own))
     first = call(
-        functools.partial(tiles, before=0, layer=layer, scale=scale),
-        [shape_of(both_here, F32), shape_of((2, before, 3 * states), F32)],
+        functools.partial(both_tiles, before=0, layer=layer, scale=scale),
+        [tall, wide, tall, wide],
         [*u, *w, two[0], one[0]],
     )
     two[1], first[0] = lax.optimization_barrier((two[1], first[0]))
     one.append(swapped(1))
-    pieces = (5, 3, rows, states)
-    keep, *sends = call(
-        functools.partial(tiles_and_pieces, before=before, layer=layer, plane=plane, scale=scale),
-        [shape_of(pieces, F32)] + [shape_of(pieces, BF16)] * (places - 1),
-        [*u, *w, two[1], one[1], own, *first],
-        scratch=[pltpu.VMEM(both_here, F32), pltpu.VMEM((2, states, 3 * states), F32)],
-    )
-    parts = exchange(sends)
-    from_one, from_two = call(add, [shape_of(pieces[1:], F32)] * 2, [keep, *parts])
-    from_one, from_two = shift(from_one, "blk", 1), shift(from_two, "blk", 2)
+
+    def summed(panel, earlier, with_own):
+        pieces = (2 + with_own, 3, rows, states)
+        keep, *sends = call(
+            functools.partial(
+                tiles_and_pieces,
+                before=before,
+                layer=layer,
+                plane=plane,
+                scale=scale,
+                with_own=with_own,
+            ),
+            [shape_of(pieces, F32)] + [shape_of(pieces, BF16)] * (places - 1),
+            [*u, *w, panel, *earlier] + [own] * with_own,
+            scratch=[pltpu.VMEM(tall.shape, F32), pltpu.VMEM((states, 3 * states), F32)],
+            us=1,
+        )
+        return [keep, *exchange(sends)]
+
+    def sent_back(group, distance):
+        (total,) = call(add, [shape_of((3, rows, states), F32)], group)
+        return shift(total, "blk", distance)
+
+    group_two = summed(two[1], first[:2], True)
+    one[1], group_two[0] = lax.optimization_barrier((one[1], group_two[0]))
+    group_one = summed(one[1], first[2:], False)
+    from_two = sent_back(group_two, 2)
+    from_one = sent_back(group_one, 1)
     (out,) = call(
         assemble,
         [shape_of((3, 5, rows, states), F32)],
-        [keep, *parts, from_one, from_two],
+        [*group_two, *group_one, from_one, from_two],
     )
     return out
 

time: 48.3 us -> 48.3 us (level)
  waiting for transfers between devices: 22.4 us -> 16.7 us
  starting transfers between devices: 13.8 us -> 17.3 us
  Pallas kernels: 10.3 us -> 12.4 us
    ppermute x3 -> x6, starting transfers between devices: 3.55 us -> 7.11 us  [exchange(): got.append(lax.ppermute(piece, ('dx', 'dy'), route))]
    ppermute x3 -> x6, waiting for transfers between devices: 5.72 us -> 2.7 us  [exchange(): got.append(lax.ppermute(piece, ('dx', 'dy'), route))]
    pallas_call x11 -> x14, Pallas kernels: 10.3 us -> 12.4 us  [call(): return list(run(*operands))]
    ppermute x2, waiting for transfers between devices: 2.8 us -> 0.73 us  [swapped(): return lax.ppermute(mixed, 'blk', swap)]
    unnamed x6 -> x8, local copies, waits for them, and re-layouts: 0.43 us -> 1.66 us
    split x3 -> x0, local copies, waits for them, and re-layouts: 1.09 us -> none  [on_device(): jnp.split(orbitals, [before], axis=0)]
    ppermute x7, waiting for transfers between devices: 13.9 us -> 13.2 us  [shift(): lax.ppermute(block, axis, [((i + distance) % count, i) for i in range(cou...]
  transfers between devices with their start and end apart: 12 -> 15, of which waited for: 9 -> 8; matrix products, arithmetic and copies ran while one was open for 1% -> 1% of each run, Pallas kernels for 15% -> 23%
where the time goes in v8:
time: 48.3 us; the launch traced here: 48.2 us
  starting transfers between devices  17.3 us (36%)
  waiting for transfers between devices  16.7 us (35%)
  Pallas kernels  12.4 us (26%)
  local copies, waits for them, and re-layouts  1.66 us (3%)
    ppermute x7, waiting for transfers between devices, shift(): lax.ppermute(block, axis, [((i + distance) % count, i) for i in range(cou...  13.2 us
    pallas_call x14, Pallas kernels, call(): return list(run(*operands))  12.4 us
    ppermute x7, starting transfers between devices, shift(): lax.ppermute(block, axis, [((i + distance) % count, i) for i in range(cou...  10.1 us
    ppermute x6, starting transfers between devices, exchange(): got.append(lax.ppermute(piece, ('dx', 'dy'), route))  7.11 us
    ppermute x6, waiting for transfers between devices, exchange(): got.append(lax.ppermute(piece, ('dx', 'dy'), route))  2.7 us
    unnamed x8, local copies, waits for them, and re-layouts  1.66 us
  transfers between devices with their start and end apart: 15, of which 8 were waited for; matrix products, arithmetic and copies ran while one was open for 1% of the time, Pallas kernels for 23%

profile of v8, /device:TPU:0, one launch (start us, length us, event | category | flops | bytes accessed | tf_op | source)
XLA Modules:
  0.0 48.2 jit_solution(10512965168116949014)
XLA Ops:
  0.0 1.2 %copy-done = bf16[128,4,8,128]{3,2,1,0:T(8,128)(2,1)S(1)} copy-done((bf16[128,4,8,128]{3,2,1,0:T(8,128)(2,1)S(1)}, bf16[128,4,8,128]{3,2,1,0:T(8,128)(2,1)}, u32[]{:S(2)}) %copy-start) | copy-done | bytes 1048600
  1.6 3.1 %collective-permute-start.1 = (bf16[48,4096]{1,0:T(8,128)(2,1)S(1)}, bf16[48,4096]{1,0:T(8,128)(2,1)S(1)}, u32[]{:S(2)}, u32[]{:S(2)}) collective-permute-start(bf16[48,4096]{1,0:T(8,128)(2,1)S(1)} %bitcast.17), channel_id=1, source_target_pairs={{24,0},{28,4},{0,8},{4,12},{8,16},{12,20},{16,24},{20,28},{25,1},{... | collective-permute-start | bytes 1179656 | tf_op jit(solution)/shard_map/ppermute | solution.py:26
  4.7 0.3 copy.8
  5.1 1.6 %collective-permute-start.2 = (bf16[128,1280]{1,0:T(8,128)(2,1)S(1)}, bf16[128,1280]{1,0:T(8,128)(2,1)S(1)}, u32[]{:S(2)}, u32[]{:S(2)}) collective-permute-start(bf16[128,1280]{1,0:T(8,128)(2,1)S(1)} %get-tuple-element.36), channel_id=1, source_target_pairs={{1,0},{0,1},{3,2},{2,3},{5,4},{4,5},{7,6},{6,7},{9,8},{8,9},{11,10... | collective-permute-start | bytes 983048 | tf_op jit(solution)/shard_map/ppermute | solution.py:26
  6.7 1.5 %collective-permute-start.4 = (bf16[128,1152]{1,0:T(8,128)(2,1)S(1)}, bf16[128,1152]{1,0:T(8,128)(2,1)S(1)}, u32[]{:S(2)}, u32[]{:S(2)}) collective-permute-start(bf16[128,1152]{1,0:T(8,128)(2,1)S(1)} %get-tuple-element.40), channel_id=1, source_target_pairs={{2,0},{0,2},{3,1},{1,3},{6,4},{4,6},{7,5},{5,7},{10,8},{8,10},{11,... | collective-permute-start | bytes 884744 | tf_op jit(solution)/shard_map/ppermute | solution.py:26
  8.2 0.5 %collective-permute-start.3 = (bf16[128,1152]{1,0:T(8,128)(2,1)S(1)}, bf16[128,1152]{1,0:T(8,128)(2,1)S(1)}, u32[]{:S(2)}, u32[]{:S(2)}) collective-permute-start(bf16[128,1152]{1,0:T(8,128)(2,1)S(1)} %get-tuple-element.38), channel_id=1, source_target_pairs={{2,0},{0,2},{3,1},{1,3},{6,4},{4,6},{7,5},{5,7},{10,8},{8,10},{11,... | collective-permute-start | bytes 884744 | tf_op jit(solution)/shard_map/ppermute | solution.py:26
  8.7 1.6 %collective-permute-start = (bf16[80,4096]{1,0:T(8,128)(2,1)S(1)}, bf16[80,4096]{1,0:T(8,128)(2,1)S(1)}, u32[]{:S(2)}, u32[]{:S(2)}) collective-permute-start(bf16[80,4096]{1,0:T(8,128)(2,1)S(1)} %bitcast.11), channel_id=1, source_target_pairs={{24,0},{28,4},{0,8},{4,12},{8,16},{12,20},{16,24},{20,28},{25,1},{... | collective-permute-start | bytes 1966088 | tf_op jit(solution)/shard_map/ppermute | solution.py:26
  10.3 4.1 %collective-permute-done.2.refs_2_.refs_3_ = bf16[128,1280]{1,0:T(8,128)(2,1)S(1)} collective-permute-done((bf16[128,1280]{1,0:T(8,128)(2,1)S(1)}, bf16[128,1280]{1,0:T(8,128)(2,1)S(1)}, u32[]{:S(2)}, u32[]{:S(2)}) %collective-permute-start.2) | collective-permute-done | bytes 327712 | tf_op jit(solution)/shard_map/ppermute | solution.py:26
  14.3 1.9 %shard_map.39 = (bf16[384,2048]{1,0:T(8,128)(2,1)S(1)}, bf16[384,2048]{1,0:T(8,128)(2,1)S(1)}) custom-call(bf16[48,4096]{1,0:T(8,128)(2,1)S(1)} %bitcast.19, bf16[80,4096]{1,0:T(8,128)(2,1)S(1)} %bitcast.12, bf16[128,1280]{1,0:T(8,128)(2,1)S(1)} %collective-permute-done.2.refs_2_.refs_3_, f32[4,8,128]{2,1,0:T(8,128)S(1)} %copy-done.2, ...), custom_call_target="tpu_custom_call" | custom-call | tf_op jit(solution)/shard_map/pallas_call | solution.py:60
  16.3 0.4 collective-permute-done.4.refs_2_
  16.6 1.2 %shard_map.41 = (bf16[384,1024]{1,0:T(8,128)(2,1)S(1)}, bf16[384,1024]{1,0:T(8,128)(2,1)S(1)}) custom-call(bf16[48,4096]{1,0:T(8,128)(2,1)S(1)} %bitcast.20, bf16[80,4096]{1,0:T(8,128)(2,1)S(1)} %bitcast.13, bf16[128,1152]{1,0:T(8,128)(2,1)S(1)} %collective-permute-done.4.refs_2_, bf16[128,1280]{1,0:T(8,128)(2,1)S(1)} %collective-permute-done.2.refs_2_.refs_3_, ...), custom_call_target="tpu_custom_call" | custom-call | tf_op jit(solution)/shard_map/pallas_call | solution.py:60
  17.8 3.4 %collective-permute-done.3.refs_2_ = bf16[128,1152]{1,0:T(8,128)(2,1)S(1)} collective-permute-done((bf16[128,1152]{1,0:T(8,128)(2,1)S(1)}, bf16[128,1152]{1,0:T(8,128)(2,1)S(1)}, u32[]{:S(2)}, u32[]{:S(2)}) %collective-permute-start.3) | collective-permute-done | bytes 294944 | tf_op jit(solution)/shard_map/ppermute | solution.py:26
  21.2 1.2 %shard_map.40 = (bf16[384,1024]{1,0:T(8,128)(2,1)S(1)}, bf16[384,1024]{1,0:T(8,128)(2,1)S(1)}) custom-call(bf16[48,4096]{1,0:T(8,128)(2,1)S(1)} %bitcast.21, bf16[80,4096]{1,0:T(8,128)(2,1)S(1)} %bitcast.14, bf16[128,1152]{1,0:T(8,128)(2,1)S(1)} %collective-permute-done.3.refs_2_, bf16[128,1280]{1,0:T(8,128)(2,1)S(1)} %collective-permute-done.2.refs_2_.refs_3_, ...), custom_call_target="tpu_custom_call" | custom-call | tf_op jit(solution)/shard_map/pallas_call | solution.py:60
  22.4 0.2 shard_map.42
  22.7 1.0 %shard_map.43.refs_9_ = f32[384,128]{1,0:T(8,128)S(1)} custom-call(bf16[384,2048]{1,0:T(8,128)(2,1)S(1)} %get-tuple-element.42.refs_0_, bf16[384,1024]{1,0:T(8,128)(2,1)S(1)} %get-tuple-element.43.refs_1_, bf16[384,1024]{1,0:T(8,128)(2,1)S(1)} %get-tuple-element.44.refs_2_, bf16[48,4096]{1,0:T(8,128)(2,1)S(1)} %bitcast.23, bf16[80,4096]{1,0:T(8,128)(2,1)S(1)} %bitcast.15), custom_call_target="tpu_custom_call" | custom-call | tf_op jit(solution)/shard_map/pallas_call | solution.py:60
  23.6 0.7 %collective-permute-done.5.refs_7_ = bf16[48,4096]{1,0:T(8,128)(2,1)S(1)} collective-permute-done((bf16[48,4096]{1,0:T(8,128)(2,1)S(1)}, bf16[48,4096]{1,0:T(8,128)(2,1)S(1)}, u32[]{:S(2)}, u32[]{:S(2)}) %collective-permute-start.5) | collective-permute-done | bytes 393248 | tf_op jit(solution)/shard_map/ppermute | solution.py:364
  24.4 1.8 %shard_map.44 = (f32[384,128]{1,0:T(8,128)S(1)}, f32[48,384]{1,0:T(8,128)S(1)}, f32[384,128]{1,0:T(8,128)S(1)}, f32[48,384]{1,0:T(8,128)S(1)}) custom-call(bf16[384,2048]{1,0:T(8,128)(2,1)S(1)} %get-tuple-element.42.refs_0_, bf16[384,1024]{1,0:T(8,128)(2,1)S(1)} %get-tuple-element.43.refs_1_, bf16[384,1024]{1,0:T(8,128)(2,1)S(1)} %get-tuple-element.44.refs_2_, ...), custom_call_target="tpu_custom_call" | custom-call | tf_op jit(solution)/shard_map/pallas_call | solution.py:60
  26.2 3.7 %collective-permute-done.two.refs_6_ = bf16[80,4096]{1,0:T(8,128)(2,1)S(1)} collective-permute-done((bf16[80,4096]{1,0:T(8,128)(2,1)S(1)}, bf16[80,4096]{1,0:T(8,128)(2,1)S(1)}, u32[]{:S(2)}, u32[]{:S(2)}) %collective-permute-start) | collective-permute-done | bytes 655392 | tf_op jit(solution)/shard_map/ppermute | solution.py:26
  29.9 0.2 shard_map.45
  30.2 1.9 %shard_map.46 = (f32[3,3,32,128]{3,2,1,0:T(8,128)S(1)}, bf16[3,3,32,128]{3,2,1,0:T(8,128)(2,1)S(1)}, bf16[3,3,32,128]{3,2,1,0:T(8,128)(2,1)S(1)}, bf16[3,3,32,128]{3,2,1,0:T(8,128)(2,1)S(1)}) custom-call(bf16[384,2048]{1,0:T(8,128)(2,1)S(1)} %get-tuple-element.42.refs_0_, bf16[384,1024]{1,0:T(8,128)(2,1)S(1)} %get-tuple-element.43.refs_1_, ...), custom_call_target="tpu_custom_call" | custom-call | bytes 3000000 | tf_op jit(solution)/shard_map/pallas_call | solution.py:60
  32.1 1.6 %collective-permute-start.7 = (bf16[3,3,32,128]{3,2,1,0:T(8,128)(2,1)S(1)}, bf16[3,3,32,128]{3,2,1,0:T(8,128)(2,1)S(1)}, u32[]{:S(2)}, u32[]{:S(2)}) collective-permute-start(bf16[3,3,32,128]{3,2,1,0:T(8,128)(2,1)S(1)} %get-tuple-element.57), channel_id=1, source_target_pairs={{0,1},{1,0},{2,3},{3,2},{4,5},{5,4},{6,7},{7,6},{8,9},{9,8},{10,11... | collective-permute-start | bytes 221192 | tf_op jit(solution)/shard_map/ppermute | solution.py:44
  33.6 1.5 %collective-permute-start.8 = (bf16[3,3,32,128]{3,2,1,0:T(8,128)(2,1)S(1)}, bf16[3,3,32,128]{3,2,1,0:T(8,128)(2,1)S(1)}, u32[]{:S(2)}, u32[]{:S(2)}) collective-permute-start(bf16[3,3,32,128]{3,2,1,0:T(8,128)(2,1)S(1)} %get-tuple-element.58), channel_id=1, source_target_pairs={{0,2},{1,3},{2,0},{3,1},{4,6},{5,7},{6,4},{7,5},{8,10},{9,11},{10,... | collective-permute-start | bytes 221192 | tf_op jit(solution)/shard_map/ppermute | solution.py:44
  35.1 0.5 %collective-permute-start.9 = (bf16[3,3,32,128]{3,2,1,0:T(8,128)(2,1)S(1)}, bf16[3,3,32,128]{3,2,1,0:T(8,128)(2,1)S(1)}, u32[]{:S(2)}, u32[]{:S(2)}) collective-permute-start(bf16[3,3,32,128]{3,2,1,0:T(8,128)(2,1)S(1)} %get-tuple-element.59), channel_id=1, source_target_pairs={{0,3},{1,2},{2,1},{3,0},{4,7},{5,6},{6,5},{7,4},{8,11},{9,10},{10,... | collective-permute-start | bytes 221192 | tf_op jit(solution)/shard_map/ppermute | solution.py:44
  35.6 1.9 %shard_map.47 = (f32[2,3,32,128]{3,2,1,0:T(8,128)S(1)}, bf16[2,3,32,128]{3,2,1,0:T(8,128)(2,1)S(1)}, bf16[2,3,32,128]{3,2,1,0:T(8,128)(2,1)S(1)}, bf16[2,3,32,128]{3,2,1,0:T(8,128)(2,1)S(1)}) custom-call(bf16[384,2048]{1,0:T(8,128)(2,1)S(1)} %get-tuple-element.42.refs_0_, bf16[384,1024]{1,0:T(8,128)(2,1)S(1)} %get-tuple-element.43.refs_1_, ...), custom_call_target="tpu_custom_call" | custom-call | bytes 3000000 | tf_op jit(solution)/shard_map/pallas_call | solution.py:60
  37.5 1.6 %collective-permute-start.10 = (bf16[2,3,32,128]{3,2,1,0:T(8,128)(2,1)S(1)}, bf16[2,3,32,128]{3,2,1,0:T(8,128)(2,1)S(1)}, u32[]{:S(2)}, u32[]{:S(2)}) collective-permute-start(bf16[2,3,32,128]{3,2,1,0:T(8,128)(2,1)S(1)} %get-tuple-element.64), channel_id=1, source_target_pairs={{0,1},{1,0},{2,3},{3,2},{4,5},{5,4},{6,7},{7,6},{8,9},{9,8},{10,11... | collective-permute-start | bytes 147464 | tf_op jit(solution)/shard_map/ppermute | solution.py:44
  39.1 1.5 %collective-permute-start.11 = (bf16[2,3,32,128]{3,2,1,0:T(8,128)(2,1)S(1)}, bf16[2,3,32,128]{3,2,1,0:T(8,128)(2,1)S(1)}, u32[]{:S(2)}, u32[]{:S(2)}) collective-permute-start(bf16[2,3,32,128]{3,2,1,0:T(8,128)(2,1)S(1)} %get-tuple-element.65), channel_id=1, source_target_pairs={{0,2},{1,3},{2,0},{3,1},{4,6},{5,7},{6,4},{7,5},{8,10},{9,11},{10,... | collective-permute-start | bytes 147464 | tf_op jit(solution)/shard_map/ppermute | solution.py:44
  40.6 0.5 collective-permute-start.12
  41.1 1.8 %collective-permute-start.14 = (f32[3,32,128]{2,1,0:T(8,128)S(1)}, f32[3,32,128]{2,1,0:T(8,128)S(1)}, u32[]{:S(2)}, u32[]{:S(2)}) collective-permute-start(f32[3,32,128]{2,1,0:T(8,128)S(1)} %shard_map.49), channel_id=1, source_target_pairs={{8,0},{12,4},{16,8},{20,12},{24,16},{28,20},{0,24},{4,28},{9,1},{1... | collective-permute-start | bytes 147464 | tf_op jit(solution)/shard_map/ppermute | solution.py:26
  42.9 0.3 collective-permute-done.11.rest_1_.refs_6_
  43.2 2.4 %collective-permute-done.12.rest_2_.refs_7_ = bf16[2,3,32,128]{3,2,1,0:T(8,128)(2,1)S(1)} collective-permute-done((bf16[2,3,32,128]{3,2,1,0:T(8,128)(2,1)S(1)}, bf16[2,3,32,128]{3,2,1,0:T(8,128)(2,1)S(1)}, u32[]{:S(2)}, u32[]{:S(2)}) %collective-permute-start.12) | collective-permute-done | bytes 49184 | tf_op jit(solution)/shard_map/ppermute | solution.py:44
  45.7 1.7 %collective-permute-done.13.refs_8_ = f32[3,32,128]{2,1,0:T(8,128)S(1)} collective-permute-done((f32[3,32,128]{2,1,0:T(8,128)S(1)}, f32[3,32,128]{2,1,0:T(8,128)S(1)}, u32[]{:S(2)}, u32[]{:S(2)}) %collective-permute-start.13) | collective-permute-done | bytes 49184 | tf_op jit(solution)/shard_map/ppermute | solution.py:26
  47.4 0.7 %shard_map.50 = f32[3,5,32,128]{3,2,1,0:T(8,128)} custom-call(f32[3,3,32,128]{3,2,1,0:T(8,128)S(1)} %get-tuple-element.56.keep.refs_0_, bf16[3,3,32,128]{3,2,1,0:T(8,128)(2,1)S(1)} %collective-permute-done.7.rest_0_.refs_1_, bf16[3,3,32,128]{3,2,1,0:T(8,128)(2,1)S(1)} %collective-permute-done.8.rest_1_.refs_2_, ...), custom_call_target="tpu_custom_call" | custom-call | tf_op jit(solution)/shard_map/pallas_call | solution.py:60
  (22 shorter events, 0.7 us)
Async XLA Ops:
  0.0 1.2 %copy-start = (bf16[128,4,8,128]{3,2,1,0:T(8,128)(2,1)S(1)}, bf16[128,4,8,128]{3,2,1,0:T(8,128)(2,1)}, u32[]{:S(2)}) copy-start(bf16[128,4,8,128]{3,2,1,0:T(8,128)(2,1)} %whole.1) | copy-start | bytes 3145732
  1.2 3.5 %slice-start = ((bf16[128,4,8,128]{3,2,1,0:T(8,128)(2,1)}), bf16[80,4,8,128]{3,2,1,0:T(8,128)(2,1)S(1)}, s32[]{:S(2)}) async-start(bf16[128,4,8,128]{3,2,1,0:T(8,128)(2,1)} %whole.1), calls=%async_computation | async-start | bytes 1310720 | tf_op jit(solution)/shard_map/slice | solution.py:319
  1.4 3.5 %copy-start.1 = (f32[3,4,8,128]{3,2,1,0:T(8,128)S(1)}, f32[3,4,8,128]{3,2,1,0:T(8,128)}, u32[]{:S(2)}) copy-start(f32[3,4,8,128]{3,2,1,0:T(8,128)} %refs_5_.3) | copy-start | bytes 147460
  1.4 3.5 %copy-start.2 = (f32[4,8,128]{2,1,0:T(8,128)S(1)}, f32[4,8,128]{2,1,0:T(8,128)}, u32[]{:S(2)}) copy-start(f32[4,8,128]{2,1,0:T(8,128)} %refs_4_.5) | copy-start | bytes 49156
  1.6 20.7 %collective-permute-start.1 = (bf16[48,4096]{1,0:T(8,128)(2,1)S(1)}, bf16[48,4096]{1,0:T(8,128)(2,1)S(1)}, u32[]{:S(2)}, u32[]{:S(2)}) collective-permute-start(bf16[48,4096]{1,0:T(8,128)(2,1)S(1)} %bitcast.17), channel_id=1, source_target_pairs={{24,0},{28,4},{0,8},{4,12},{8,16},{12,20},{16,24},{20,28},{25,1},{... | collective-permute-start | bytes 1179656 | tf_op jit(solution)/shard_map/ppermute | solution.py:26
  5.1 9.2 %collective-permute-start.2 = (bf16[128,1280]{1,0:T(8,128)(2,1)S(1)}, bf16[128,1280]{1,0:T(8,128)(2,1)S(1)}, u32[]{:S(2)}, u32[]{:S(2)}) collective-permute-start(bf16[128,1280]{1,0:T(8,128)(2,1)S(1)} %get-tuple-element.36), channel_id=1, source_target_pairs={{1,0},{0,1},{3,2},{2,3},{5,4},{4,5},{7,6},{6,7},{9,8},{8,9},{11,10... | collective-permute-start | bytes 983048 | tf_op jit(solution)/shard_map/ppermute | solution.py:26
  6.7 9.9 %collective-permute-start.4 = (bf16[128,1152]{1,0:T(8,128)(2,1)S(1)}, bf16[128,1152]{1,0:T(8,128)(2,1)S(1)}, u32[]{:S(2)}, u32[]{:S(2)}) collective-permute-start(bf16[128,1152]{1,0:T(8,128)(2,1)S(1)} %get-tuple-element.40), channel_id=1, source_target_pairs={{2,0},{0,2},{3,1},{1,3},{6,4},{4,6},{7,5},{5,7},{10,8},{8,10},{11,... | collective-permute-start | bytes 884744 | tf_op jit(solution)/shard_map/ppermute | solution.py:26
  8.2 13.0 %collective-permute-start.3 = (bf16[128,1152]{1,0:T(8,128)(2,1)S(1)}, bf16[128,1152]{1,0:T(8,128)(2,1)S(1)}, u32[]{:S(2)}, u32[]{:S(2)}) collective-permute-start(bf16[128,1152]{1,0:T(8,128)(2,1)S(1)} %get-tuple-element.38), channel_id=1, source_target_pairs={{2,0},{0,2},{3,1},{1,3},{6,4},{4,6},{7,5},{5,7},{10,8},{8,10},{11,... | collective-permute-start | bytes 884744 | tf_op jit(solution)/shard_map/ppermute | solution.py:26
  8.7 21.2 %collective-permute-start = (bf16[80,4096]{1,0:T(8,128)(2,1)S(1)}, bf16[80,4096]{1,0:T(8,128)(2,1)S(1)}, u32[]{:S(2)}, u32[]{:S(2)}) collective-permute-start(bf16[80,4096]{1,0:T(8,128)(2,1)S(1)} %bitcast.11), channel_id=1, source_target_pairs={{24,0},{28,4},{0,8},{4,12},{8,16},{12,20},{16,24},{20,28},{25,1},{... | collective-permute-start | bytes 1966088 | tf_op jit(solution)/shard_map/ppermute | solution.py:26
  22.6 1.8 %collective-permute-start.5 = (bf16[48,4096]{1,0:T(8,128)(2,1)S(1)}, bf16[48,4096]{1,0:T(8,128)(2,1)S(1)}, u32[]{:S(2)}, u32[]{:S(2)}) collective-permute-start(bf16[48,4096]{1,0:T(8,128)(2,1)S(1)} %shard_map.42), channel_id=1, source_target_pairs={{0,4},{4,0},{8,12},{12,8},{16,20},{20,16},{24,28},{28,24},{1,5},{5... | collective-permute-start | bytes 1179656 | tf_op jit(solution)/shard_map/ppermute | solution.py:364
  30.1 5.5 %collective-permute-start.6 = (bf16[80,4096]{1,0:T(8,128)(2,1)S(1)}, bf16[80,4096]{1,0:T(8,128)(2,1)S(1)}, u32[]{:S(2)}, u32[]{:S(2)}) collective-permute-start(bf16[80,4096]{1,0:T(8,128)(2,1)S(1)} %shard_map.45), channel_id=1, source_target_pairs={{0,4},{4,0},{8,12},{12,8},{16,20},{20,16},{24,28},{28,24},{1,5},{5... | collective-permute-start | bytes 1966088 | tf_op jit(solution)/shard_map/ppermute | solution.py:364
  32.1 8.5 %collective-permute-start.7 = (bf16[3,3,32,128]{3,2,1,0:T(8,128)(2,1)S(1)}, bf16[3,3,32,128]{3,2,1,0:T(8,128)(2,1)S(1)}, u32[]{:S(2)}, u32[]{:S(2)}) collective-permute-start(bf16[3,3,32,128]{3,2,1,0:T(8,128)(2,1)S(1)} %get-tuple-element.57), channel_id=1, source_target_pairs={{0,1},{1,0},{2,3},{3,2},{4,5},{5,4},{6,7},{7,6},{8,9},{9,8},{10,11... | collective-permute-start | bytes 221192 | tf_op jit(solution)/shard_map/ppermute | solution.py:44
  33.6 7.5 %collective-permute-start.8 = (bf16[3,3,32,128]{3,2,1,0:T(8,128)(2,1)S(1)}, bf16[3,3,32,128]{3,2,1,0:T(8,128)(2,1)S(1)}, u32[]{:S(2)}, u32[]{:S(2)}) collective-permute-start(bf16[3,3,32,128]{3,2,1,0:T(8,128)(2,1)S(1)} %get-tuple-element.58), channel_id=1, source_target_pairs={{0,2},{1,3},{2,0},{3,1},{4,6},{5,7},{6,4},{7,5},{8,10},{9,11},{10,... | collective-permute-start | bytes 221192 | tf_op jit(solution)/shard_map/ppermute | solution.py:44
  35.1 6.0 %collective-permute-start.9 = (bf16[3,3,32,128]{3,2,1,0:T(8,128)(2,1)S(1)}, bf16[3,3,32,128]{3,2,1,0:T(8,128)(2,1)S(1)}, u32[]{:S(2)}, u32[]{:S(2)}) collective-permute-start(bf16[3,3,32,128]{3,2,1,0:T(8,128)(2,1)S(1)} %get-tuple-element.59), channel_id=1, source_target_pairs={{0,3},{1,2},{2,1},{3,0},{4,7},{5,6},{6,5},{7,4},{8,11},{9,10},{10,... | collective-permute-start | bytes 221192 | tf_op jit(solution)/shard_map/ppermute | solution.py:44
  37.5 5.4 %collective-permute-start.10 = (bf16[2,3,32,128]{3,2,1,0:T(8,128)(2,1)S(1)}, bf16[2,3,32,128]{3,2,1,0:T(8,128)(2,1)S(1)}, u32[]{:S(2)}, u32[]{:S(2)}) collective-permute-start(bf16[2,3,32,128]{3,2,1,0:T(8,128)(2,1)S(1)} %get-tuple-element.64), channel_id=1, source_target_pairs={{0,1},{1,0},{2,3},{3,2},{4,5},{5,4},{6,7},{7,6},{8,9},{9,8},{10,11... | collective-permute-start | bytes 147464 | tf_op jit(solution)/shard_map/ppermute | solution.py:44
  39.1 4.1 %collective-permute-start.11 = (bf16[2,3,32,128]{3,2,1,0:T(8,128)(2,1)S(1)}, bf16[2,3,32,128]{3,2,1,0:T(8,128)(2,1)S(1)}, u32[]{:S(2)}, u32[]{:S(2)}) collective-permute-start(bf16[2,3,32,128]{3,2,1,0:T(8,128)(2,1)S(1)} %get-tuple-element.65), channel_id=1, source_target_pairs={{0,2},{1,3},{2,0},{3,1},{4,6},{5,7},{6,4},{7,5},{8,10},{9,11},{10,... | collective-permute-start | bytes 147464 | tf_op jit(solution)/shard_map/ppermute | solution.py:44
  40.6 5.0 %collective-permute-start.12 = (bf16[2,3,32,128]{3,2,1,0:T(8,128)(2,1)S(1)}, bf16[2,3,32,128]{3,2,1,0:T(8,128)(2,1)S(1)}, u32[]{:S(2)}, u32[]{:S(2)}) collective-permute-start(bf16[2,3,32,128]{3,2,1,0:T(8,128)(2,1)S(1)} %get-tuple-element.66), channel_id=1, source_target_pairs={{0,3},{1,2},{2,1},{3,0},{4,7},{5,6},{6,5},{7,4},{8,11},{9,10},{10,... | collective-permute-start | bytes 147464 | tf_op jit(solution)/shard_map/ppermute | solution.py:44
  41.1 4.6 %collective-permute-start.14 = (f32[3,32,128]{2,1,0:T(8,128)S(1)}, f32[3,32,128]{2,1,0:T(8,128)S(1)}, u32[]{:S(2)}, u32[]{:S(2)}) collective-permute-start(f32[3,32,128]{2,1,0:T(8,128)S(1)} %shard_map.49), channel_id=1, source_target_pairs={{8,0},{12,4},{16,8},{20,12},{24,16},{28,20},{0,24},{4,28},{9,1},{1... | collective-permute-start | bytes 147464 | tf_op jit(solution)/shard_map/ppermute | solution.py:26
  45.6 1.8 %collective-permute-start.13 = (f32[3,32,128]{2,1,0:T(8,128)S(1)}, f32[3,32,128]{2,1,0:T(8,128)S(1)}, u32[]{:S(2)}, u32[]{:S(2)}) collective-permute-start(f32[3,32,128]{2,1,0:T(8,128)S(1)} %shard_map.48), channel_id=1, source_target_pairs={{4,0},{8,4},{12,8},{16,12},{20,16},{24,20},{28,24},{0,28},{5,1},{9... | collective-permute-start | bytes 147464 | tf_op jit(solution)/shard_map/ppermute | solution.py:26

commit v9 on v5

v9 whole, which is shorter than its diff:
```python
import functools
import math

import jax
import jax.numpy as jnp
from jax import lax
from jax.experimental import pallas as pl
from jax.experimental.pallas import tpu as pltpu
from jax.sharding import PartitionSpec as P

F32, BF16 = jnp.float32, jnp.bfloat16
VMEM = pl.BlockSpec(memory_space=pltpu.VMEM)
ANY = pl.BlockSpec(memory_space=pl.ANY)
LIMIT = 12 * 1024 * 1024
NT = (((1,), (1,)), ((), ()))
CHUNK = 16


def shape_of(shape, dtype):
    return jax.ShapeDtypeStruct(shape, dtype)


def shift(block, axis, distance):
    count = lax.axis_size(axis)
    return lax.ppermute(block, axis, [((i + distance) % count, i) for i in range(count)])


def both_sides(pair, axis):
    if lax.axis_size(axis) == 2:
        return shift(pair, axis, 1)
    tail, head = jnp.split(pair, 2, axis=1)
    return jnp.concatenate([shift(tail, axis, -1), shift(head, axis, 1)], axis=1)


def exchange(sends):
    nx, ny = lax.axis_size("dx"), lax.axis_size("dy")
    got = []
    for o, piece in enumerate(sends, 1):
        ox, oy = o // ny, o % ny
        route = [
            (i * ny + j, ((i + ox) % nx) * ny + (j + oy) % ny) for i in range(nx) for j in range(ny)
        ]
        got.append(lax.ppermute(piece, ("dx", "dy"), route))
    return got


def call(body, outs, operands, scratch=(), specs=None, out_specs=None, us=0):
    run = pl.pallas_call(
        body,
        out_shape=outs,
        in_specs=specs or [VMEM] * len(operands),
        out_specs=out_specs or [VMEM] * len(outs),
        scratch_shapes=list(scratch),
        compiler_params=pltpu.CompilerParams(vmem_limit_bytes=LIMIT),
        cost_estimate=pl.CostEstimate(
            flops=0, bytes_accessed=int(us * 3e6), transcendentals=0
        ),
    )
    return list(run(*operands))


def destinations(nx, ny):
    x, y = lax.axis_index("dx"), lax.axis_index("dy")
    return [
        lax.rem(x + ox, nx) * ny + lax.rem(y + oy, ny) for ox in range(nx) for oy in range(ny)
    ]


def thirds(value):
    high = value.astype(BF16).astype(F32)
    middle = (value - high).astype(BF16).astype(F32)
    return high, middle, value - high - middle


def edges(psi, coupling, grad, tail, head, hy, tmp, *, shape):
    wx, wy, wz = shape
    layer, line = wy * wz, wx * wz
    for side, (x, y, hx) in enumerate(((wx - 1, wy - 1, tail), (0, 0, head))):
        to_y = side * (line + wz)
        hx[:, :layer] = psi[:, x * layer : (x + 1) * layer]
        for i in range(wx):
            at = i * layer + y * wz
            hy[:, to_y + i * wz : to_y + (i + 1) * wz] = psi[:, at : at + wz]
        for k in range(3):
            for n, third in enumerate(thirds(coupling[x] * grad[k, x])):
                tmp[(3 * k + n) * wy : (3 * k + n + 1) * wy] = third
        hx[: tmp.shape[0], layer:] = tmp[...].astype(BF16)
        for k in range(3):
            for n, third in enumerate(thirds(coupling[:, y] * grad[k, :, y])):
                tmp[(3 * k + n) * wx : (3 * k + n + 1) * wx] = third
        hy[: tmp.shape[0], to_y + line : to_y + line + wz] = tmp[...].astype(BF16)


def operators(*refs, layers, shape):
    psi, *refs = refs
    outer = len(refs) == 13
    hx = refs[:2]
    hy, coupling, grad, u, w, half, back, ahead, tmp, ex, ey = refs[-11:]
    wx, wy, wz = shape
    layer, line = wy * wz, wx * wz
    states = psi.shape[0]
    half[...] = 0.5 * (coupling[...][None] * grad[...])

    def unpack(ref, at, to, count):
        tmp[...] = ref[: tmp.shape[0], at : at + wz].astype(F32)
        for k in range(3):
            third = [tmp[(3 * k + n) * count : (3 * k + n + 1) * count] for n in range(3)]
            to[k] = 0.5 * (third[0] + third[1] + third[2])

    for side in range(2):
        if outer:
            unpack(hx[side], layer, ex.at[side], wy)
        unpack(hy, side * (line + wz) + line, ey.at[side], wx)
    for k in range(3):
        for x in layers:
            back[k, x] = pltpu.roll(half[k, x], 1, 1)
            ahead[k, x] = pltpu.roll(half[k, x], wz - 1, 1)

    def coeff(k, x, y):
        if x < 0 or x >= wx:
            return ex[int(x >= wx), k, y : y + 1, :]
        if y < 0 or y >= wy:
            return ey[int(y >= wy), k, x : x + 1, :]
        return half[k, x, y : y + 1, :]

    def group(step, _):
        r = pl.ds(pl.multiple_of(step * CHUNK, CHUNK), CHUNK)

        def field(x, y):
            if x < 0 or x >= wx:
                return hx[int(x >= wx)][r, y * wz : (y + 1) * wz].astype(F32)
            if y < 0 or y >= wy:
                at = int(y >= wy) * (line + wz) + x * wz
                return hy[r, at : at + wz].astype(F32)
            at = x * layer + y * wz
            return psi[r, at : at + wz].astype(F32)

        for n, x in enumerate(layers):
            for y in range(wy):
                here = field(x, y)
                xb, xa = field(x - 1, y), field(x + 1, y)
                yb, ya = field(x, y - 1), field(x, y + 1)
                zb, za = pltpu.roll(here, 1, 1), pltpu.roll(here, wz - 1, 1)
                gx, gy, gz = xa - xb, ya - yb, za - zb
                c1, c2, c3 = [coeff(k, x, y) for k in range(3)]
                cols = slice(n * layer + y * wz, n * layer + (y + 1) * wz)

                def put(ref, k, value):
                    place = pl.ds(pl.multiple_of(k * states + step * CHUNK, CHUNK), CHUNK)
                    ref[place, cols] = value.astype(BF16)

                put(u, 0, c2 * gz - c3 * gy)
                put(u, 1, c3 * gx - c1 * gz)
                put(u, 2, c1 * gy - c2 * gx)

                def dx(k):
                    return coeff(k, x + 1, y) * xa - coeff(k, x - 1, y) * xb

                def dy(k):
                    return coeff(k, x, y + 1) * ya - coeff(k, x, y - 1) * yb

                def dz(k):
                    return ahead[k, x, y : y + 1, :] * za - back[k, x, y : y + 1, :] * zb

                put(w, 0, dy(2) - dz(1))
                put(w, 1, dz(0) - dx(2))
                put(w, 2, dx(1) - dy(0))
        return 0

    lax.fori_loop(0, states // CHUNK, group, 0)


def product(fields, panel, layer, flip=False):
    inner, outer = fields
    cells = inner.shape[1] + outer.shape[1]
    total = 0.0
    for a, start, stop in (
        (inner[...], layer, cells - layer),
        (outer[:, :layer], 0, layer),
        (outer[:, layer:], cells - layer, cells),
    ):
        b = panel(slice(start, stop))
        a, b = (b, a) if flip else (a, b)
        total = total + lax.dot_general(a, b, NT, preferred_element_type=F32)
    return total


def stacked(*panels):
    return lambda cols: jnp.concatenate([panel[:, cols] for panel in panels], axis=0)


def own_tiles(*refs, layer, scale):
    u, (psi, own) = refs[:2], refs[2:]
    own[...] = product(u, stacked(psi), layer) * scale


def duplicate(source, target, sem):
    copy = pltpu.make_async_copy(source, target, sem)
    copy.start()
    copy.wait()


def cut(outs, slots, plane, states):
    rows = states // math.prod(plane)
    for ref, dest in zip(outs, destinations(*plane)):
        for n, slot in enumerate(slots):
            for k in range(3):
                ref[n, k] = slot(k, dest * rows, rows).astype(ref.dtype)


def tall_rows(tile):
    states = tile.shape[0] // 3

    def rows_of(k, start, rows):
        return tile[pl.ds(pl.multiple_of(k * states + start, rows), rows), :]

    return rows_of


def wide_rows(tile):
    states = tile.shape[0]

    def rows_of(k, start, rows):
        cols = slice(k * states, (k + 1) * states)
        return tile[pl.ds(pl.multiple_of(start, rows), rows), cols]

    return rows_of


def either(first, second):
    core = lax.rem(lax.axis_index("blk"), 2)
    return lambda *place: jnp.where(core == 0, first(*place), second(*place))


def there_tiles(*refs, layer, plane, scale):
    w, w_mate, (two, psi, own), refs = refs[:2], refs[2:4], refs[4:7], refs[7:]
    mate, outs, (there, there_mate) = refs[0], refs[1:-2], refs[-2:]
    states = two.shape[0]
    there[...] = product(w, stacked(two), layer, True) * scale
    both = product(w_mate, stacked(two, psi), layer, True) * scale
    there_mate[...], mate[...] = both[:states], both[states:]
    slots = (wide_rows(there), either(tall_rows(own), wide_rows(there_mate)))
    cut(outs, slots, plane, states)


def here_tiles(*refs, layer, plane, scale):
    u, (two, one, own, mate), refs = refs[:2], refs[2:6], refs[6:]
    outs, (here_two, here_one) = refs[:-2], refs[-2:]
    states = two.shape[0]
    both = product(u, stacked(two, one), layer) * scale
    here_two[...], here_one[...] = both[:, :states], both[:, states:]
    slots = (
        tall_rows(here_two), wide_rows(mate), either(tall_rows(here_one), tall_rows(own))
    )
    cut(outs, slots, plane, states)


def total_of(group, n, k):
    total = group[0][n, k]
    for part in group[1:]:
        total = total + part[n, k].astype(F32)
    return total


def add(*refs):
    group, out = refs[:-1], refs[-1]
    for n in range(out.shape[0]):
        for k in range(3):
            out[n, k] = total_of(group, n, k)


def assemble(*refs):
    group, (there, back, out) = refs[:-3], refs[-3:]
    core = lax.rem(lax.axis_index("blk"), 2)
    for k in range(3):
        mate, third = total_of(group, 1, k), total_of(group, 2, k)
        out[k, 0] = total_of(group, 0, k)
        out[k, 1] = jnp.where(core == 0, third, mate)
        out[k, 2] = jnp.where(core == 0, there[1, k], third)
        out[k, 3] = jnp.where(core == 0, mate, back[1, k])
        out[k, 4] = back[0, k]


def on_device(orbitals, coupling, pot_grad):
    states, wx, wy, wz = orbitals.shape
    shape = (wx, wy, wz)
    plane = (lax.axis_size("dx"), lax.axis_size("dy"))
    places = math.prod(plane)
    rows = states // places
    layer, line = wy * wz, wx * wz
    cells = wx * layer
    scale = 1.0 / math.sqrt(cells * places)

    swap = [(i, i ^ 1) for i in range(lax.axis_size("blk"))]
    psi = lax.optimization_barrier(orbitals.reshape(states, cells))
    two = shift(psi, "blk", -2)

    tmp = pltpu.VMEM((-(-9 * max(wx, wy) // 16) * 16, wz), F32)
    tail, head, hy = call(
        functools.partial(edges, shape=shape),
        [shape_of((states, layer + wz), BF16)] * 2 + [shape_of((states, 2 * (line + wz)), BF16)],
        [psi, coupling, pot_grad],
        scratch=[tmp],
    )
    hx = [shift(tail, "dx", -1), shift(head, "dx", 1)]
    hy = both_sides(hy, "dy")

    coeffs = pltpu.VMEM((3, wx, wy, wz), F32)
    ends = [pltpu.VMEM((2, 3, wy, wz), F32), pltpu.VMEM((2, 3, wx, wz), F32)]
    u, w, w_mate = [], [], []
    for layers, sides in ((range(1, wx - 1), []), ((0, wx - 1), hx)):
        if sides:
            sides, u[0] = lax.optimization_barrier((sides, u[0]))
        field = shape_of((3 * states, len(layers) * layer), BF16)
        results = call(
            functools.partial(operators, layers=layers, shape=shape),
            [field, field],
            [psi, *sides, hy, coupling, pot_grad],
            scratch=[coeffs] * 3 + [tmp, *ends],
        )
        u.append(results[0])
        w.append(results[1])
        w_mate.append(lax.ppermute(w[-1], "blk", swap))
    tall, wide = shape_of((3 * states, states), F32), shape_of((states, 3 * states), F32)
    (own,) = call(
        functools.partial(own_tiles, layer=layer, scale=scale), [tall], [*u, psi]
    )

    def cut_shapes(slots):
        shape = (slots, 3, rows, states)
        return [shape_of(shape, F32)] + [shape_of(shape, BF16)] * (places - 1)

    given = dict(layer=layer, plane=plane, scale=scale)
    two, own = lax.optimization_barrier((two, own))
    one = lax.ppermute(two, "blk", swap)
    (two,) = call(
        duplicate,
        [shape_of((states, cells), BF16)],
        [two],
        scratch=[pltpu.SemaphoreType.DMA],
        specs=[ANY],
        out_specs=[ANY],
        us=60,
    )
    mate, kept_there, *sends = call(
        functools.partial(there_tiles, **given),
        [wide, *cut_shapes(2)],
        [*w, *w_mate, two, psi, own],
        scratch=[pltpu.VMEM(wide.shape, F32)] * 2,
        us=1,
    )
    first = exchange(sends)
    one, mate = lax.optimization_barrier((one, mate))
    kept, *sends = call(
        functools.partial(here_tiles, **given),
        cut_shapes(3),
        [*u, two, one, own, mate],
        scratch=[pltpu.VMEM(tall.shape, F32)] * 2,
        us=1,
    )
    second = exchange(sends)
    first, kept = lax.optimization_barrier((first, kept))
    (there,) = call(add, [shape_of((2, 3, rows, states), F32)], [kept_there, *first])
    back = shift(there, "blk", 2)
    (out,) = call(
        assemble, [shape_of((3, 5, rows, states), F32)], [kept, *second, there, back]
    )
    return out


def solution(mesh):
    in_specs = (P("blk", "dx", "dy", None), P("dx", "dy", None), P(None, "dx", "dy", None))
    out_specs = P(None, None, ("blk", "dx", "dy"), None)
    return jax.shard_map(
        on_device, mesh=mesh, in_specs=in_specs, out_specs=out_specs, check_vma=False
    )
```

time: 49 us -> 49.3 us (level)
  starting transfers between devices: 11.6 us -> 16.1 us
  waiting for transfers between devices: 26 us -> 22.3 us
  Pallas kernels: 9.46 us -> 8.96 us
    ppermute x3 -> x6, starting transfers between devices: 3.55 us -> 7.04 us  [exchange(): got.append(lax.ppermute(piece, ('dx', 'dy'), route))]
    ppermute x5, waiting for transfers between devices: 19.5 us -> 16.1 us  [shift(): lax.ppermute(block, axis, [((i + distance) % count, i) for i in range(cou...]
    ppermute x1 -> x3, waiting for transfers between devices: 0.81 us -> 0.01 us  [the longest x2 0.01 us: on_device(): w_mate.append(lax.ppermute(w[-1], 'blk', swap))]
    ppermute x3 -> x6, waiting for transfers between devices: 5.72 us -> 6.26 us  [exchange(): got.append(lax.ppermute(piece, ('dx', 'dy'), route))]
    ppermute x1 -> x3, starting transfers between devices: 0.07 us -> 0.58 us  [the longest x2 0.57 us: on_device(): w_mate.append(lax.ppermute(w[-1], 'blk', swap))]
    pallas_call x9, Pallas kernels: 9.46 us -> 8.96 us  [call(): return list(run(*operands))]
  transfers between devices with their start and end apart: 9 -> 14, of which waited for: 7 -> 9; matrix products, arithmetic and copies ran while one was open for 0% -> 0% of each run, Pallas kernels for 14% -> 17%
where the time goes in v9:
time: 49.3 us; the launch traced here: 49.1 us
  waiting for transfers between devices  22.3 us (45%)
  starting transfers between devices  16.1 us (33%)
  Pallas kernels  8.96 us (18%)
  local copies, waits for them, and re-layouts  1.69 us (3%)
    ppermute x5, waiting for transfers between devices, shift(): lax.ppermute(block, axis, [((i + distance) % count, i) for i in range(cou...  16.1 us
    pallas_call x9, Pallas kernels, call(): return list(run(*operands))  8.96 us
    ppermute x5, starting transfers between devices, shift(): lax.ppermute(block, axis, [((i + distance) % count, i) for i in range(cou...  8.45 us
    ppermute x6, starting transfers between devices, exchange(): got.append(lax.ppermute(piece, ('dx', 'dy'), route))  7.04 us
    ppermute x6, waiting for transfers between devices, exchange(): got.append(lax.ppermute(piece, ('dx', 'dy'), route))  6.26 us
    unnamed x5, local copies, waits for them, and re-layouts  1.69 us
  transfers between devices with their start and end apart: 14, of which 9 were waited for; matrix products, arithmetic and copies ran while one was open for 0% of the time, Pallas kernels for 17%

profile of v9, /device:TPU:0, one launch (start us, length us, event | category | flops | bytes accessed | tf_op | source)
XLA Modules:
  0.0 49.1 jit_solution(13134734679074387587)
XLA Ops:
  0.0 1.7 %copy.6 = bf16[16,8,32,128]{3,1,2,0:T(8,128)(2,1)S(1)} copy(bf16[16,8,32,128]{3,2,1,0:T(8,128)(2,1)} %bitcast.11) | data formatting | bytes 2097152
  1.7 3.1 %collective-permute-start.5 = (bf16[128,4096]{1,0:T(8,128)(2,1)S(1)}, bf16[128,4096]{1,0:T(8,128)(2,1)S(1)}, u32[]{:S(2)}, u32[]{:S(2)}) collective-permute-start(bf16[128,4096]{1,0:T(8,128)(2,1)S(1)} %bitcast.5), channel_id=1, source_target_pairs={{24,0},{28,4},{0,8},{4,12},{8,16},{12,20},{16,24},{20,28},{25,1},{... | collective-permute-start | bytes 3145736 | tf_op jit(solution)/shard_map/ppermute | solution.py:25
  4.8 0.1 shard_map.37
  4.9 1.6 %collective-permute-start = (bf16[128,1280]{1,0:T(8,128)(2,1)S(1)}, bf16[128,1280]{1,0:T(8,128)(2,1)S(1)}, u32[]{:S(2)}, u32[]{:S(2)}) collective-permute-start(bf16[128,1280]{1,0:T(8,128)(2,1)S(1)} %get-tuple-element.32), channel_id=1, source_target_pairs={{1,0},{0,1},{3,2},{2,3},{5,4},{4,5},{7,6},{6,7},{9,8},{8,9},{11,10... | collective-permute-start | bytes 983048 | tf_op jit(solution)/shard_map/ppermute | solution.py:25
  6.5 1.5 %collective-permute-start.1 = (bf16[128,1152]{1,0:T(8,128)(2,1)S(1)}, bf16[128,1152]{1,0:T(8,128)(2,1)S(1)}, u32[]{:S(2)}, u32[]{:S(2)}) collective-permute-start(bf16[128,1152]{1,0:T(8,128)(2,1)S(1)} %get-tuple-element.34), channel_id=1, source_target_pairs={{2,0},{0,2},{3,1},{1,3},{6,4},{4,6},{7,5},{5,7},{10,8},{8,10},{11,... | collective-permute-start | bytes 884744 | tf_op jit(solution)/shard_map/ppermute | solution.py:25
  8.0 0.5 %collective-permute-start.2 = (bf16[128,1152]{1,0:T(8,128)(2,1)S(1)}, bf16[128,1152]{1,0:T(8,128)(2,1)S(1)}, u32[]{:S(2)}, u32[]{:S(2)}) collective-permute-start(bf16[128,1152]{1,0:T(8,128)(2,1)S(1)} %get-tuple-element.35), channel_id=1, source_target_pairs={{2,0},{0,2},{3,1},{1,3},{6,4},{4,6},{7,5},{5,7},{10,8},{8,10},{11,... | collective-permute-start | bytes 884744 | tf_op jit(solution)/shard_map/ppermute | solution.py:25
  8.5 5.7 %collective-permute-done.refs_1_.refs_3_ = bf16[128,1280]{1,0:T(8,128)(2,1)S(1)} collective-permute-done((bf16[128,1280]{1,0:T(8,128)(2,1)S(1)}, bf16[128,1280]{1,0:T(8,128)(2,1)S(1)}, u32[]{:S(2)}, u32[]{:S(2)}) %collective-permute-start) | collective-permute-done | bytes 327712 | tf_op jit(solution)/shard_map/ppermute | solution.py:25
  14.1 1.9 %shard_map.38 = (bf16[384,2048]{1,0:T(8,128)(2,1)S(1)}, bf16[384,2048]{1,0:T(8,128)(2,1)S(1)}) custom-call(bf16[128,4096]{1,0:T(8,128)(2,1)S(1)} %bitcast.7, bf16[128,1280]{1,0:T(8,128)(2,1)S(1)} %collective-permute-done.refs_1_.refs_3_, f32[4,8,128]{2,1,0:T(8,128)S(1)} %copy-done.1, f32[3,4,8,128]{3,2,1,0:T(8,128)S(1)} %copy-done), custom_call_target="tpu_custom_call" | custom-call | tf_op jit(solution)/shard_map/pallas_call | solution.py:59
  16.0 0.4 collective-permute-done.1.refs_1_
  16.4 4.6 %collective-permute-done.2.refs_2_ = bf16[128,1152]{1,0:T(8,128)(2,1)S(1)} collective-permute-done((bf16[128,1152]{1,0:T(8,128)(2,1)S(1)}, bf16[128,1152]{1,0:T(8,128)(2,1)S(1)}, u32[]{:S(2)}, u32[]{:S(2)}) %collective-permute-start.2) | collective-permute-done | bytes 294944 | tf_op jit(solution)/shard_map/ppermute | solution.py:25
  21.0 0.0 collective-permute-start.3
  21.0 1.9 %shard_map.39 = (bf16[384,2048]{1,0:T(8,128)(2,1)S(1)}, bf16[384,2048]{1,0:T(8,128)(2,1)S(1)}) custom-call(bf16[128,4096]{1,0:T(8,128)(2,1)S(1)} %bitcast.8, bf16[128,1152]{1,0:T(8,128)(2,1)S(1)} %collective-permute-done.1.refs_1_, bf16[128,1152]{1,0:T(8,128)(2,1)S(1)} %collective-permute-done.2.refs_2_, ...), custom_call_target="tpu_custom_call" | custom-call | tf_op jit(solution)/shard_map/pallas_call | solution.py:59
  22.9 0.6 %collective-permute-start.4 = (bf16[384,2048]{1,0:T(8,128)(2,1)S(1)}, bf16[384,2048]{1,0:T(8,128)(2,1)S(1)}, u32[]{:S(2)}, u32[]{:S(2)}) collective-permute-start(bf16[384,2048]{1,0:T(8,128)(2,1)S(1)} %get-tuple-element.39.refs_1_), channel_id=1, source_target_pairs={{0,4},{4,0},{8,12},{12,8},{16,20},{20,16},{24,28},{28,24},{1,5},{5... | collective-permute-start | bytes 4718600 | tf_op jit(solution)/shard_map/ppermute | solution.py:323
  23.5 1.0 %shard_map.40.refs_6_.refs_4_ = f32[384,128]{1,0:T(8,128)S(1)} custom-call(bf16[384,2048]{1,0:T(8,128)(2,1)S(1)} %get-tuple-element.40.refs_0_, bf16[384,2048]{1,0:T(8,128)(2,1)S(1)} %get-tuple-element.41.refs_1_, bf16[128,4096]{1,0:T(8,128)(2,1)S(1)} %bitcast.9), custom_call_target="tpu_custom_call" | custom-call | tf_op jit(solution)/shard_map/pallas_call | solution.py:59
  24.5 5.5 %collective-permute-done.5.source = bf16[128,4096]{1,0:T(8,128)(2,1)S(1)} collective-permute-done((bf16[128,4096]{1,0:T(8,128)(2,1)S(1)}, bf16[128,4096]{1,0:T(8,128)(2,1)S(1)}, u32[]{:S(2)}, u32[]{:S(2)}) %collective-permute-start.5) | collective-permute-done | bytes 1048608 | tf_op jit(solution)/shard_map/ppermute | solution.py:25
  29.9 0.0 collective-permute-start.9
  29.9 0.1 shard_map.41.refs_4_.refs_2_
  30.1 2.1 %shard_map.42 = (f32[128,384]{1,0:T(8,128)S(1)}, f32[2,3,32,128]{3,2,1,0:T(8,128)S(1)}, bf16[2,3,32,128]{3,2,1,0:T(8,128)(2,1)S(1)}, bf16[2,3,32,128]{3,2,1,0:T(8,128)(2,1)S(1)}, bf16[2,3,32,128]{3,2,1,0:T(8,128)(2,1)S(1)}) custom-call(bf16[384,2048]{1,0:T(8,128)(2,1)S(1)} %get-tuple-element.33.refs_0_, bf16[384,2048]{1,0:T(8,128)(2,1)S(1)} %get-tuple-element.39.refs_1_, ...), custom_call_target="tpu_custom_call" | custom-call | bytes 3000000 | tf_op jit(solution)/shard_map/pallas_call | solution.py:59
  32.2 1.6 %collective-permute-start.6 = (bf16[2,3,32,128]{3,2,1,0:T(8,128)(2,1)S(1)}, bf16[2,3,32,128]{3,2,1,0:T(8,128)(2,1)S(1)}, u32[]{:S(2)}, u32[]{:S(2)}) collective-permute-start(bf16[2,3,32,128]{3,2,1,0:T(8,128)(2,1)S(1)} %get-tuple-element.44), channel_id=1, source_target_pairs={{0,1},{1,0},{2,3},{3,2},{4,5},{5,4},{6,7},{7,6},{8,9},{9,8},{10,11... | collective-permute-start | bytes 147464 | tf_op jit(solution)/shard_map/ppermute | solution.py:43
  33.8 1.5 %collective-permute-start.7 = (bf16[2,3,32,128]{3,2,1,0:T(8,128)(2,1)S(1)}, bf16[2,3,32,128]{3,2,1,0:T(8,128)(2,1)S(1)}, u32[]{:S(2)}, u32[]{:S(2)}) collective-permute-start(bf16[2,3,32,128]{3,2,1,0:T(8,128)(2,1)S(1)} %get-tuple-element.45), channel_id=1, source_target_pairs={{0,2},{1,3},{2,0},{3,1},{4,6},{5,7},{6,4},{7,5},{8,10},{9,11},{10,... | collective-permute-start | bytes 147464 | tf_op jit(solution)/shard_map/ppermute | solution.py:43
  35.3 0.5 collective-permute-start.8
  35.8 1.0 %shard_map.43 = (f32[3,3,32,128]{3,2,1,0:T(8,128)S(1)}, bf16[3,3,32,128]{3,2,1,0:T(8,128)(2,1)S(1)}, bf16[3,3,32,128]{3,2,1,0:T(8,128)(2,1)S(1)}, bf16[3,3,32,128]{3,2,1,0:T(8,128)(2,1)S(1)}) custom-call(bf16[384,2048]{1,0:T(8,128)(2,1)S(1)} %get-tuple-element.40.refs_0_, bf16[384,2048]{1,0:T(8,128)(2,1)S(1)} %get-tuple-element.41.refs_1_, ...), custom_call_target="tpu_custom_call" | custom-call | bytes 3000000 | tf_op jit(solution)/shard_map/pallas_call | solution.py:59
  36.8 1.0 %collective-permute-done.7.refs_2_ = bf16[2,3,32,128]{3,2,1,0:T(8,128)(2,1)S(1)} collective-permute-done((bf16[2,3,32,128]{3,2,1,0:T(8,128)(2,1)S(1)}, bf16[2,3,32,128]{3,2,1,0:T(8,128)(2,1)S(1)}, u32[]{:S(2)}, u32[]{:S(2)}) %collective-permute-start.7) | collective-permute-done | bytes 49184 | tf_op jit(solution)/shard_map/ppermute | solution.py:43
  37.8 2.4 %collective-permute-done.8.refs_3_ = bf16[2,3,32,128]{3,2,1,0:T(8,128)(2,1)S(1)} collective-permute-done((bf16[2,3,32,128]{3,2,1,0:T(8,128)(2,1)S(1)}, bf16[2,3,32,128]{3,2,1,0:T(8,128)(2,1)S(1)}, u32[]{:S(2)}, u32[]{:S(2)}) %collective-permute-start.8) | collective-permute-done | bytes 49184 | tf_op jit(solution)/shard_map/ppermute | solution.py:43
  40.3 1.8 %collective-permute-start.13 = (f32[2,3,32,128]{3,2,1,0:T(8,128)S(1)}, f32[2,3,32,128]{3,2,1,0:T(8,128)S(1)}, u32[]{:S(2)}, u32[]{:S(2)}) collective-permute-start(f32[2,3,32,128]{3,2,1,0:T(8,128)S(1)} %shard_map.44.refs_4_), channel_id=1, source_target_pairs={{8,0},{12,4},{16,8},{20,12},{24,16},{28,20},{0,24},{4,28},{9,1},{1... | collective-permute-start | bytes 294920 | tf_op jit(solution)/shard_map/ppermute | solution.py:25
  42.1 0.5 %collective-permute-start.10 = (bf16[3,3,32,128]{3,2,1,0:T(8,128)(2,1)S(1)}, bf16[3,3,32,128]{3,2,1,0:T(8,128)(2,1)S(1)}, u32[]{:S(2)}, u32[]{:S(2)}) collective-permute-start(bf16[3,3,32,128]{3,2,1,0:T(8,128)(2,1)S(1)} %get-tuple-element.52), channel_id=1, source_target_pairs={{0,1},{1,0},{2,3},{3,2},{4,5},{5,4},{6,7},{7,6},{8,9},{9,8},{10,11... | collective-permute-start | bytes 221192 | tf_op jit(solution)/shard_map/ppermute | solution.py:43
  42.6 0.5 %collective-permute-start.11 = (bf16[3,3,32,128]{3,2,1,0:T(8,128)(2,1)S(1)}, bf16[3,3,32,128]{3,2,1,0:T(8,128)(2,1)S(1)}, u32[]{:S(2)}, u32[]{:S(2)}) collective-permute-start(bf16[3,3,32,128]{3,2,1,0:T(8,128)(2,1)S(1)} %get-tuple-element.53), channel_id=1, source_target_pairs={{0,2},{1,3},{2,0},{3,1},{4,6},{5,7},{6,4},{7,5},{8,10},{9,11},{10,... | collective-permute-start | bytes 221192 | tf_op jit(solution)/shard_map/ppermute | solution.py:43
  43.1 2.4 %collective-permute-start.12 = (bf16[3,3,32,128]{3,2,1,0:T(8,128)(2,1)S(1)}, bf16[3,3,32,128]{3,2,1,0:T(8,128)(2,1)S(1)}, u32[]{:S(2)}, u32[]{:S(2)}) collective-permute-start(bf16[3,3,32,128]{3,2,1,0:T(8,128)(2,1)S(1)} %get-tuple-element.54), channel_id=1, source_target_pairs={{0,3},{1,2},{2,1},{3,0},{4,7},{5,6},{6,5},{7,4},{8,11},{9,10},{10,... | collective-permute-start | bytes 221192 | tf_op jit(solution)/shard_map/ppermute | solution.py:43
  45.6 0.9 %collective-permute-done.10.refs_1_ = bf16[3,3,32,128]{3,2,1,0:T(8,128)(2,1)S(1)} collective-permute-done((bf16[3,3,32,128]{3,2,1,0:T(8,128)(2,1)S(1)}, bf16[3,3,32,128]{3,2,1,0:T(8,128)(2,1)S(1)}, u32[]{:S(2)}, u32[]{:S(2)}) %collective-permute-start.10) | collective-permute-done | bytes 73760 | tf_op jit(solution)/shard_map/ppermute | solution.py:43
  46.4 0.5 %collective-permute-done.11.refs_2_ = bf16[3,3,32,128]{3,2,1,0:T(8,128)(2,1)S(1)} collective-permute-done((bf16[3,3,32,128]{3,2,1,0:T(8,128)(2,1)S(1)}, bf16[3,3,32,128]{3,2,1,0:T(8,128)(2,1)S(1)}, u32[]{:S(2)}, u32[]{:S(2)}) %collective-permute-start.11) | collective-permute-done | bytes 73760 | tf_op jit(solution)/shard_map/ppermute | solution.py:43
  47.0 1.4 %collective-permute-done.12.refs_3_ = bf16[3,3,32,128]{3,2,1,0:T(8,128)(2,1)S(1)} collective-permute-done((bf16[3,3,32,128]{3,2,1,0:T(8,128)(2,1)S(1)}, bf16[3,3,32,128]{3,2,1,0:T(8,128)(2,1)S(1)}, u32[]{:S(2)}, u32[]{:S(2)}) %collective-permute-start.12) | collective-permute-done | bytes 73760 | tf_op jit(solution)/shard_map/ppermute | solution.py:43
  48.4 0.7 %shard_map.45 = f32[3,5,32,128]{3,2,1,0:T(8,128)} custom-call(f32[3,3,32,128]{3,2,1,0:T(8,128)S(1)} %get-tuple-element.51.refs_0_, bf16[3,3,32,128]{3,2,1,0:T(8,128)(2,1)S(1)} %collective-permute-done.10.refs_1_, bf16[3,3,32,128]{3,2,1,0:T(8,128)(2,1)S(1)} %collective-permute-done.11.refs_2_, bf16[3,3,32,128]{3,2,1,0:T(8,128)(2,1)S(1)} %collective-permute-done.12.refs_3_, ...), custom_call_target="tpu_custom_call" | custom-call | tf_op jit(solution)/shard_map/pallas_call | solution.py:59
  (10 shorter events, 0.0 us)
Async XLA Ops:
  0.0 4.8 %copy-start = (f32[3,4,8,128]{3,2,1,0:T(8,128)S(1)}, f32[3,4,8,128]{3,2,1,0:T(8,128)}, u32[]{:S(2)}) copy-start(f32[3,4,8,128]{3,2,1,0:T(8,128)} %refs_5_.1) | copy-start | bytes 147460
  0.0 4.8 %copy-start.1 = (f32[4,8,128]{2,1,0:T(8,128)S(1)}, f32[4,8,128]{2,1,0:T(8,128)}, u32[]{:S(2)}) copy-start(f32[4,8,128]{2,1,0:T(8,128)} %refs_4_.1) | copy-start | bytes 49156
  1.7 28.3 %collective-permute-start.5 = (bf16[128,4096]{1,0:T(8,128)(2,1)S(1)}, bf16[128,4096]{1,0:T(8,128)(2,1)S(1)}, u32[]{:S(2)}, u32[]{:S(2)}) collective-permute-start(bf16[128,4096]{1,0:T(8,128)(2,1)S(1)} %bitcast.5), channel_id=1, source_target_pairs={{24,0},{28,4},{0,8},{4,12},{8,16},{12,20},{16,24},{20,28},{25,1},{... | collective-permute-start | bytes 3145736 | tf_op jit(solution)/shard_map/ppermute | solution.py:25
  4.9 9.2 %collective-permute-start = (bf16[128,1280]{1,0:T(8,128)(2,1)S(1)}, bf16[128,1280]{1,0:T(8,128)(2,1)S(1)}, u32[]{:S(2)}, u32[]{:S(2)}) collective-permute-start(bf16[128,1280]{1,0:T(8,128)(2,1)S(1)} %get-tuple-element.32), channel_id=1, source_target_pairs={{1,0},{0,1},{3,2},{2,3},{5,4},{4,5},{7,6},{6,7},{9,8},{8,9},{11,10... | collective-permute-start | bytes 983048 | tf_op jit(solution)/shard_map/ppermute | solution.py:25
  6.5 9.9 %collective-permute-start.1 = (bf16[128,1152]{1,0:T(8,128)(2,1)S(1)}, bf16[128,1152]{1,0:T(8,128)(2,1)S(1)}, u32[]{:S(2)}, u32[]{:S(2)}) collective-permute-start(bf16[128,1152]{1,0:T(8,128)(2,1)S(1)} %get-tuple-element.34), channel_id=1, source_target_pairs={{2,0},{0,2},{3,1},{1,3},{6,4},{4,6},{7,5},{5,7},{10,8},{8,10},{11,... | collective-permute-start | bytes 884744 | tf_op jit(solution)/shard_map/ppermute | solution.py:25
  8.0 13.0 %collective-permute-start.2 = (bf16[128,1152]{1,0:T(8,128)(2,1)S(1)}, bf16[128,1152]{1,0:T(8,128)(2,1)S(1)}, u32[]{:S(2)}, u32[]{:S(2)}) collective-permute-start(bf16[128,1152]{1,0:T(8,128)(2,1)S(1)} %get-tuple-element.35), channel_id=1, source_target_pairs={{2,0},{0,2},{3,1},{1,3},{6,4},{4,6},{7,5},{5,7},{10,8},{8,10},{11,... | collective-permute-start | bytes 884744 | tf_op jit(solution)/shard_map/ppermute | solution.py:25
  21.0 9.1 %collective-permute-start.3 = (bf16[384,2048]{1,0:T(8,128)(2,1)S(1)}, bf16[384,2048]{1,0:T(8,128)(2,1)S(1)}, u32[]{:S(2)}, u32[]{:S(2)}) collective-permute-start(bf16[384,2048]{1,0:T(8,128)(2,1)S(1)} %get-tuple-element.33.refs_0_), channel_id=1, source_target_pairs={{0,4},{4,0},{8,12},{12,8},{16,20},{20,16},{24,28},{28,24},{1,5},{5... | collective-permute-start | bytes 4718600 | tf_op jit(solution)/shard_map/ppermute | solution.py:323
  22.9 7.1 %collective-permute-start.4 = (bf16[384,2048]{1,0:T(8,128)(2,1)S(1)}, bf16[384,2048]{1,0:T(8,128)(2,1)S(1)}, u32[]{:S(2)}, u32[]{:S(2)}) collective-permute-start(bf16[384,2048]{1,0:T(8,128)(2,1)S(1)} %get-tuple-element.39.refs_1_), channel_id=1, source_target_pairs={{0,4},{4,0},{8,12},{12,8},{16,20},{20,16},{24,28},{28,24},{1,5},{5... | collective-permute-start | bytes 4718600 | tf_op jit(solution)/shard_map/ppermute | solution.py:323
  29.9 5.8 %collective-permute-start.9 = (bf16[128,4096]{1,0:T(8,128)(2,1)S(1)}, bf16[128,4096]{1,0:T(8,128)(2,1)S(1)}, u32[]{:S(2)}, u32[]{:S(2)}) collective-permute-start(bf16[128,4096]{1,0:T(8,128)(2,1)S(1)} %collective-permute-done.5.source), channel_id=1, source_target_pairs={{0,4},{4,0},{8,12},{12,8},{16,20},{20,16},{24,28},{28,24},{1,5},{5... | collective-permute-start | bytes 3145736 | tf_op jit(solution)/shard_map/ppermute | solution.py:335
  32.2 4.6 %collective-permute-start.6 = (bf16[2,3,32,128]{3,2,1,0:T(8,128)(2,1)S(1)}, bf16[2,3,32,128]{3,2,1,0:T(8,128)(2,1)S(1)}, u32[]{:S(2)}, u32[]{:S(2)}) collective-permute-start(bf16[2,3,32,128]{3,2,1,0:T(8,128)(2,1)S(1)} %get-tuple-element.44), channel_id=1, source_target_pairs={{0,1},{1,0},{2,3},{3,2},{4,5},{5,4},{6,7},{7,6},{8,9},{9,8},{10,11... | collective-permute-start | bytes 147464 | tf_op jit(solution)/shard_map/ppermute | solution.py:43
  33.8 4.1 %collective-permute-start.7 = (bf16[2,3,32,128]{3,2,1,0:T(8,128)(2,1)S(1)}, bf16[2,3,32,128]{3,2,1,0:T(8,128)(2,1)S(1)}, u32[]{:S(2)}, u32[]{:S(2)}) collective-permute-start(bf16[2,3,32,128]{3,2,1,0:T(8,128)(2,1)S(1)} %get-tuple-element.45), channel_id=1, source_target_pairs={{0,2},{1,3},{2,0},{3,1},{4,6},{5,7},{6,4},{7,5},{8,10},{9,11},{10,... | collective-permute-start | bytes 147464 | tf_op jit(solution)/shard_map/ppermute | solution.py:43
  35.3 5.0 %collective-permute-start.8 = (bf16[2,3,32,128]{3,2,1,0:T(8,128)(2,1)S(1)}, bf16[2,3,32,128]{3,2,1,0:T(8,128)(2,1)S(1)}, u32[]{:S(2)}, u32[]{:S(2)}) collective-permute-start(bf16[2,3,32,128]{3,2,1,0:T(8,128)(2,1)S(1)} %get-tuple-element.46), channel_id=1, source_target_pairs={{0,3},{1,2},{2,1},{3,0},{4,7},{5,6},{6,5},{7,4},{8,11},{9,10},{10,... | collective-permute-start | bytes 147464 | tf_op jit(solution)/shard_map/ppermute | solution.py:43
  40.3 8.1 %collective-permute-start.13 = (f32[2,3,32,128]{3,2,1,0:T(8,128)S(1)}, f32[2,3,32,128]{3,2,1,0:T(8,128)S(1)}, u32[]{:S(2)}, u32[]{:S(2)}) collective-permute-start(f32[2,3,32,128]{3,2,1,0:T(8,128)S(1)} %shard_map.44.refs_4_), channel_id=1, source_target_pairs={{8,0},{12,4},{16,8},{20,12},{24,16},{28,20},{0,24},{4,28},{9,1},{1... | collective-permute-start | bytes 294920 | tf_op jit(solution)/shard_map/ppermute | solution.py:25
  42.1 4.4 %collective-permute-start.10 = (bf16[3,3,32,128]{3,2,1,0:T(8,128)(2,1)S(1)}, bf16[3,3,32,128]{3,2,1,0:T(8,128)(2,1)S(1)}, u32[]{:S(2)}, u32[]{:S(2)}) collective-permute-start(bf16[3,3,32,128]{3,2,1,0:T(8,128)(2,1)S(1)} %get-tuple-element.52), channel_id=1, source_target_pairs={{0,1},{1,0},{2,3},{3,2},{4,5},{5,4},{6,7},{7,6},{8,9},{9,8},{10,11... | collective-permute-start | bytes 221192 | tf_op jit(solution)/shard_map/ppermute | solution.py:43
  42.6 4.4 %collective-permute-start.11 = (bf16[3,3,32,128]{3,2,1,0:T(8,128)(2,1)S(1)}, bf16[3,3,32,128]{3,2,1,0:T(8,128)(2,1)S(1)}, u32[]{:S(2)}, u32[]{:S(2)}) collective-permute-start(bf16[3,3,32,128]{3,2,1,0:T(8,128)(2,1)S(1)} %get-tuple-element.53), channel_id=1, source_target_pairs={{0,2},{1,3},{2,0},{3,1},{4,6},{5,7},{6,4},{7,5},{8,10},{9,11},{10,... | collective-permute-start | bytes 221192 | tf_op jit(solution)/shard_map/ppermute | solution.py:43
  43.1 5.3 %collective-permute-start.12 = (bf16[3,3,32,128]{3,2,1,0:T(8,128)(2,1)S(1)}, bf16[3,3,32,128]{3,2,1,0:T(8,128)(2,1)S(1)}, u32[]{:S(2)}, u32[]{:S(2)}) collective-permute-start(bf16[3,3,32,128]{3,2,1,0:T(8,128)(2,1)S(1)} %get-tuple-element.54), channel_id=1, source_target_pairs={{0,3},{1,2},{2,1},{3,0},{4,7},{5,6},{6,5},{7,4},{8,11},{9,10},{10,... | collective-permute-start | bytes 221192 | tf_op jit(solution)/shard_map/ppermute | solution.py:43

commit v10 on v9

--- a/solution.py
+++ b/solution.py
@@ -10,7 +10,6 @@
 
 F32, BF16 = jnp.float32, jnp.bfloat16
 VMEM = pl.BlockSpec(memory_space=pltpu.VMEM)
-ANY = pl.BlockSpec(memory_space=pl.ANY)
 LIMIT = 12 * 1024 * 1024
 NT = (((1,), (1,)), ((), ()))
 CHUNK = 16
@@ -194,12 +193,6 @@
     own[...] = product(u, stacked(psi), layer) * scale
 
 
-def duplicate(source, target, sem):
-    copy = pltpu.make_async_copy(source, target, sem)
-    copy.start()
-    copy.wait()
-
-
 def cut(outs, slots, plane, states):
     rows = states // math.prod(plane)
     for ref, dest in zip(outs, destinations(*plane)):
@@ -263,22 +256,22 @@
 
 
 def add(*refs):
-    group, out = refs[:-1], refs[-1]
-    for n in range(out.shape[0]):
+    group, outs = refs[:-2], refs[-2:]
+    for n, out in enumerate(outs):
         for k in range(3):
-            out[n, k] = total_of(group, n, k)
+            out[k] = total_of(group, n, k)
 
 
 def assemble(*refs):
-    group, (there, back, out) = refs[:-3], refs[-3:]
+    group, (ours, back_two, back_one, out) = refs[:-4], refs[-4:]
     core = lax.rem(lax.axis_index("blk"), 2)
     for k in range(3):
         mate, third = total_of(group, 1, k), total_of(group, 2, k)
         out[k, 0] = total_of(group, 0, k)
         out[k, 1] = jnp.where(core == 0, third, mate)
-        out[k, 2] = jnp.where(core == 0, there[1, k], third)
-        out[k, 3] = jnp.where(core == 0, mate, back[1, k])
-        out[k, 4] = back[0, k]
+        out[k, 2] = jnp.where(core == 0, ours[k], third)
+        out[k, 3] = jnp.where(core == 0, mate, back_one[k])
+        out[k, 4] = back_two[k]
 
 
 def on_device(orbitals, coupling, pot_grad):
@@ -333,15 +326,6 @@
     given = dict(layer=layer, plane=plane, scale=scale)
     two, own = lax.optimization_barrier((two, own))
     one = lax.ppermute(two, "blk", swap)
-    (two,) = call(
-        duplicate,
-        [shape_of((states, cells), BF16)],
-        [two],
-        scratch=[pltpu.SemaphoreType.DMA],
-        specs=[ANY],
-        out_specs=[ANY],
-        us=60,
-    )
     mate, kept_there, *sends = call(
         functools.partial(there_tiles, **given),
         [wide, *cut_shapes(2)],
@@ -360,10 +344,16 @@
     )
     second = exchange(sends)
     first, kept = lax.optimization_barrier((first, kept))
-    (there,) = call(add, [shape_of((2, 3, rows, states), F32)], [kept_there, *first])
-    back = shift(there, "blk", 2)
+    small = shape_of((3, rows, states), F32)
+    there, ours = call(add, [small, small], [kept_there, *first])
+    count = lax.axis_size("blk")
+    back_two = shift(there, "blk", 2)
+    odd = [((i + 2) % count, i) for i in range(1, count, 2)]
+    back_one = lax.ppermute(ours, "blk", odd)
     (out,) = call(
-        assemble, [shape_of((3, 5, rows, states), F32)], [kept, *second, there, back]
+        assemble,
+        [shape_of((3, 5, rows, states), F32)],
+        [kept, *second, ours, back_two, back_one],
     )
     return out
 

time: 49.3 us -> 45.9 us (0.931)
  waiting for transfers between devices: 22.3 us -> 18.4 us
  starting transfers between devices: 16.1 us -> 16.8 us
    ppermute x6, waiting for transfers between devices: 6.26 us -> 0.6 us  [exchange(): got.append(lax.ppermute(piece, ('dx', 'dy'), route))]
    ppermute x5, waiting for transfers between devices: 16.1 us -> 17.7 us  [shift(): lax.ppermute(block, axis, [((i + distance) % count, i) for i in range(cou...]
    ppermute x0 -> x1, starting transfers between devices: none -> 0.65 us  [on_device(): back_one = lax.ppermute(ours, 'blk', odd)]
    pallas_call x9 -> x8, Pallas kernels: 8.96 us -> 8.86 us  [call(): return list(run(*operands))]
  transfers between devices with their start and end apart: 14 -> 15, of which waited for: 9 -> 7; matrix products, arithmetic and copies ran while one was open for 0% -> 0% of each run, Pallas kernels for 17% -> 18%
where the time goes in v10:
time: 45.9 us; the launch traced here: 45.8 us
  waiting for transfers between devices  18.4 us (40%)
  starting transfers between devices  16.8 us (37%)
  Pallas kernels  8.86 us (19%)
  local copies, waits for them, and re-layouts  1.69 us (4%)
    ppermute x5, waiting for transfers between devices, shift(): lax.ppermute(block, axis, [((i + distance) % count, i) for i in range(cou...  17.7 us
    pallas_call x8, Pallas kernels, call(): return list(run(*operands))  8.86 us
    ppermute x5, starting transfers between devices, shift(): lax.ppermute(block, axis, [((i + distance) % count, i) for i in range(cou...  8.46 us
    ppermute x6, starting transfers between devices, exchange(): got.append(lax.ppermute(piece, ('dx', 'dy'), route))  7.11 us
    unnamed x5, local copies, waits for them, and re-layouts  1.69 us
  transfers between devices with their start and end apart: 15, of which 7 were waited for; matrix products, arithmetic and copies ran while one was open for 0% of the time, Pallas kernels for 18%

profile of v10, /device:TPU:0, one launch (start us, length us, event | category | flops | bytes accessed | tf_op | source)
XLA Modules:
  0.0 45.8 jit_solution(2490624883492008695)
XLA Ops:
  0.0 1.7 %copy.6 = bf16[16,8,32,128]{3,1,2,0:T(8,128)(2,1)S(1)} copy(bf16[16,8,32,128]{3,2,1,0:T(8,128)(2,1)} %bitcast.11) | data formatting | bytes 2097152
  1.7 3.1 %collective-permute-start.5 = (bf16[128,4096]{1,0:T(8,128)(2,1)S(1)}, bf16[128,4096]{1,0:T(8,128)(2,1)S(1)}, u32[]{:S(2)}, u32[]{:S(2)}) collective-permute-start(bf16[128,4096]{1,0:T(8,128)(2,1)S(1)} %bitcast.5), channel_id=1, source_target_pairs={{24,0},{28,4},{0,8},{4,12},{8,16},{12,20},{16,24},{20,28},{25,1},{... | collective-permute-start | bytes 3145736 | tf_op jit(solution)/shard_map/ppermute | solution.py:24
  4.8 0.1 shard_map.37
  4.9 1.6 %collective-permute-start = (bf16[128,1280]{1,0:T(8,128)(2,1)S(1)}, bf16[128,1280]{1,0:T(8,128)(2,1)S(1)}, u32[]{:S(2)}, u32[]{:S(2)}) collective-permute-start(bf16[128,1280]{1,0:T(8,128)(2,1)S(1)} %get-tuple-element.34), channel_id=1, source_target_pairs={{1,0},{0,1},{3,2},{2,3},{5,4},{4,5},{7,6},{6,7},{9,8},{8,9},{11,10... | collective-permute-start | bytes 983048 | tf_op jit(solution)/shard_map/ppermute | solution.py:24
  6.5 1.5 %collective-permute-start.1 = (bf16[128,1152]{1,0:T(8,128)(2,1)S(1)}, bf16[128,1152]{1,0:T(8,128)(2,1)S(1)}, u32[]{:S(2)}, u32[]{:S(2)}) collective-permute-start(bf16[128,1152]{1,0:T(8,128)(2,1)S(1)} %get-tuple-element.36), channel_id=1, source_target_pairs={{2,0},{0,2},{3,1},{1,3},{6,4},{4,6},{7,5},{5,7},{10,8},{8,10},{11,... | collective-permute-start | bytes 884744 | tf_op jit(solution)/shard_map/ppermute | solution.py:24
  8.0 0.5 %collective-permute-start.2 = (bf16[128,1152]{1,0:T(8,128)(2,1)S(1)}, bf16[128,1152]{1,0:T(8,128)(2,1)S(1)}, u32[]{:S(2)}, u32[]{:S(2)}) collective-permute-start(bf16[128,1152]{1,0:T(8,128)(2,1)S(1)} %get-tuple-element.37), channel_id=1, source_target_pairs={{2,0},{0,2},{3,1},{1,3},{6,4},{4,6},{7,5},{5,7},{10,8},{8,10},{11,... | collective-permute-start | bytes 884744 | tf_op jit(solution)/shard_map/ppermute | solution.py:24
  8.5 5.7 %collective-permute-done.refs_1_.refs_3_ = bf16[128,1280]{1,0:T(8,128)(2,1)S(1)} collective-permute-done((bf16[128,1280]{1,0:T(8,128)(2,1)S(1)}, bf16[128,1280]{1,0:T(8,128)(2,1)S(1)}, u32[]{:S(2)}, u32[]{:S(2)}) %collective-permute-start) | collective-permute-done | bytes 327712 | tf_op jit(solution)/shard_map/ppermute | solution.py:24
  14.1 1.9 %shard_map.38 = (bf16[384,2048]{1,0:T(8,128)(2,1)S(1)}, bf16[384,2048]{1,0:T(8,128)(2,1)S(1)}) custom-call(bf16[128,4096]{1,0:T(8,128)(2,1)S(1)} %bitcast.7, bf16[128,1280]{1,0:T(8,128)(2,1)S(1)} %collective-permute-done.refs_1_.refs_3_, f32[4,8,128]{2,1,0:T(8,128)S(1)} %copy-done.1, f32[3,4,8,128]{3,2,1,0:T(8,128)S(1)} %copy-done), custom_call_target="tpu_custom_call" | custom-call | tf_op jit(solution)/shard_map/pallas_call | solution.py:58
  16.1 0.4 collective-permute-done.1.refs_1_
  16.4 4.6 %collective-permute-done.2.refs_2_ = bf16[128,1152]{1,0:T(8,128)(2,1)S(1)} collective-permute-done((bf16[128,1152]{1,0:T(8,128)(2,1)S(1)}, bf16[128,1152]{1,0:T(8,128)(2,1)S(1)}, u32[]{:S(2)}, u32[]{:S(2)}) %collective-permute-start.2) | collective-permute-done | bytes 294944 | tf_op jit(solution)/shard_map/ppermute | solution.py:24
  21.0 1.9 %shard_map.39 = (bf16[384,2048]{1,0:T(8,128)(2,1)S(1)}, bf16[384,2048]{1,0:T(8,128)(2,1)S(1)}) custom-call(bf16[128,4096]{1,0:T(8,128)(2,1)S(1)} %bitcast.8, bf16[128,1152]{1,0:T(8,128)(2,1)S(1)} %collective-permute-done.1.refs_1_, bf16[128,1152]{1,0:T(8,128)(2,1)S(1)} %collective-permute-done.2.refs_2_, ...), custom_call_target="tpu_custom_call" | custom-call | tf_op jit(solution)/shard_map/pallas_call | solution.py:58
  22.9 0.6 %collective-permute-start.4 = (bf16[384,2048]{1,0:T(8,128)(2,1)S(1)}, bf16[384,2048]{1,0:T(8,128)(2,1)S(1)}, u32[]{:S(2)}, u32[]{:S(2)}) collective-permute-start(bf16[384,2048]{1,0:T(8,128)(2,1)S(1)} %get-tuple-element.41.refs_1_), channel_id=1, source_target_pairs={{0,4},{4,0},{8,12},{12,8},{16,20},{20,16},{24,28},{28,24},{1,5},{5... | collective-permute-start | bytes 4718600 | tf_op jit(solution)/shard_map/ppermute | solution.py:316
  23.5 1.0 %shard_map.40.refs_6_.refs_4_ = f32[384,128]{1,0:T(8,128)S(1)} custom-call(bf16[384,2048]{1,0:T(8,128)(2,1)S(1)} %get-tuple-element.42.refs_0_, bf16[384,2048]{1,0:T(8,128)(2,1)S(1)} %get-tuple-element.43.refs_1_, bf16[128,4096]{1,0:T(8,128)(2,1)S(1)} %bitcast.9), custom_call_target="tpu_custom_call" | custom-call | tf_op jit(solution)/shard_map/pallas_call | solution.py:58
  24.5 5.5 %collective-permute-done.5.refs_4_.refs_2_ = bf16[128,4096]{1,0:T(8,128)(2,1)S(1)} collective-permute-done((bf16[128,4096]{1,0:T(8,128)(2,1)S(1)}, bf16[128,4096]{1,0:T(8,128)(2,1)S(1)}, u32[]{:S(2)}, u32[]{:S(2)}) %collective-permute-start.5) | collective-permute-done | bytes 1048608 | tf_op jit(solution)/shard_map/ppermute | solution.py:24
  30.0 2.1 %shard_map.41 = (f32[128,384]{1,0:T(8,128)S(1)}, f32[2,3,32,128]{3,2,1,0:T(8,128)S(1)}, bf16[2,3,32,128]{3,2,1,0:T(8,128)(2,1)S(1)}, bf16[2,3,32,128]{3,2,1,0:T(8,128)(2,1)S(1)}, bf16[2,3,32,128]{3,2,1,0:T(8,128)(2,1)S(1)}) custom-call(bf16[384,2048]{1,0:T(8,128)(2,1)S(1)} %get-tuple-element.35.refs_0_, bf16[384,2048]{1,0:T(8,128)(2,1)S(1)} %get-tuple-element.41.refs_1_, ...), custom_call_target="tpu_custom_call" | custom-call | bytes 3000000 | tf_op jit(solution)/shard_map/pallas_call | solution.py:58
  32.1 1.6 %collective-permute-start.6 = (bf16[2,3,32,128]{3,2,1,0:T(8,128)(2,1)S(1)}, bf16[2,3,32,128]{3,2,1,0:T(8,128)(2,1)S(1)}, u32[]{:S(2)}, u32[]{:S(2)}) collective-permute-start(bf16[2,3,32,128]{3,2,1,0:T(8,128)(2,1)S(1)} %get-tuple-element.46), channel_id=1, source_target_pairs={{0,1},{1,0},{2,3},{3,2},{4,5},{5,4},{6,7},{7,6},{8,9},{9,8},{10,11... | collective-permute-start | bytes 147464 | tf_op jit(solution)/shard_map/ppermute | solution.py:42
  33.7 1.5 %collective-permute-start.7 = (bf16[2,3,32,128]{3,2,1,0:T(8,128)(2,1)S(1)}, bf16[2,3,32,128]{3,2,1,0:T(8,128)(2,1)S(1)}, u32[]{:S(2)}, u32[]{:S(2)}) collective-permute-start(bf16[2,3,32,128]{3,2,1,0:T(8,128)(2,1)S(1)} %get-tuple-element.47), channel_id=1, source_target_pairs={{0,2},{1,3},{2,0},{3,1},{4,6},{5,7},{6,4},{7,5},{8,10},{9,11},{10,... | collective-permute-start | bytes 147464 | tf_op jit(solution)/shard_map/ppermute | solution.py:42
  35.2 0.5 %collective-permute-start.8 = (bf16[2,3,32,128]{3,2,1,0:T(8,128)(2,1)S(1)}, bf16[2,3,32,128]{3,2,1,0:T(8,128)(2,1)S(1)}, u32[]{:S(2)}, u32[]{:S(2)}) collective-permute-start(bf16[2,3,32,128]{3,2,1,0:T(8,128)(2,1)S(1)} %get-tuple-element.48), channel_id=1, source_target_pairs={{0,3},{1,2},{2,1},{3,0},{4,7},{5,6},{6,5},{7,4},{8,11},{9,10},{10,... | collective-permute-start | bytes 147464 | tf_op jit(solution)/shard_map/ppermute | solution.py:42
  35.7 1.0 %shard_map.42 = (f32[3,3,32,128]{3,2,1,0:T(8,128)S(1)}, bf16[3,3,32,128]{3,2,1,0:T(8,128)(2,1)S(1)}, bf16[3,3,32,128]{3,2,1,0:T(8,128)(2,1)S(1)}, bf16[3,3,32,128]{3,2,1,0:T(8,128)(2,1)S(1)}) custom-call(bf16[384,2048]{1,0:T(8,128)(2,1)S(1)} %get-tuple-element.42.refs_0_, bf16[384,2048]{1,0:T(8,128)(2,1)S(1)} %get-tuple-element.43.refs_1_, ...), custom_call_target="tpu_custom_call" | custom-call | bytes 3000000 | tf_op jit(solution)/shard_map/pallas_call | solution.py:58
  36.7 1.6 %collective-permute-start.10 = (bf16[3,3,32,128]{3,2,1,0:T(8,128)(2,1)S(1)}, bf16[3,3,32,128]{3,2,1,0:T(8,128)(2,1)S(1)}, u32[]{:S(2)}, u32[]{:S(2)}) collective-permute-start(bf16[3,3,32,128]{3,2,1,0:T(8,128)(2,1)S(1)} %get-tuple-element.54), channel_id=1, source_target_pairs={{0,1},{1,0},{2,3},{3,2},{4,5},{5,4},{6,7},{7,6},{8,9},{9,8},{10,11... | collective-permute-start | bytes 221192 | tf_op jit(solution)/shard_map/ppermute | solution.py:42
  38.3 1.5 %collective-permute-start.11 = (bf16[3,3,32,128]{3,2,1,0:T(8,128)(2,1)S(1)}, bf16[3,3,32,128]{3,2,1,0:T(8,128)(2,1)S(1)}, u32[]{:S(2)}, u32[]{:S(2)}) collective-permute-start(bf16[3,3,32,128]{3,2,1,0:T(8,128)(2,1)S(1)} %get-tuple-element.55), channel_id=1, source_target_pairs={{0,2},{1,3},{2,0},{3,1},{4,6},{5,7},{6,4},{7,5},{8,10},{9,11},{10,... | collective-permute-start | bytes 221192 | tf_op jit(solution)/shard_map/ppermute | solution.py:42
  39.8 0.0 collective-permute-done.6.refs_1_
  39.8 0.5 %collective-permute-start.12 = (bf16[3,3,32,128]{3,2,1,0:T(8,128)(2,1)S(1)}, bf16[3,3,32,128]{3,2,1,0:T(8,128)(2,1)S(1)}, u32[]{:S(2)}, u32[]{:S(2)}) collective-permute-start(bf16[3,3,32,128]{3,2,1,0:T(8,128)(2,1)S(1)} %get-tuple-element.56), channel_id=1, source_target_pairs={{0,3},{1,2},{2,1},{3,0},{4,7},{5,6},{6,5},{7,4},{8,11},{9,10},{10,... | collective-permute-start | bytes 221192 | tf_op jit(solution)/shard_map/ppermute | solution.py:42
  40.3 0.0 collective-permute-done.7.refs_2_
  40.3 0.1 collective-permute-done.8.refs_3_
  40.4 1.8 %collective-permute-start.13 = (f32[3,32,128]{2,1,0:T(8,128)S(1)}, f32[3,32,128]{2,1,0:T(8,128)S(1)}, u32[]{:S(2)}, u32[]{:S(2)}) collective-permute-start(f32[3,32,128]{2,1,0:T(8,128)S(1)} %get-tuple-element.62), channel_id=1, source_target_pairs={{8,0},{12,4},{16,8},{20,12},{24,16},{28,20},{0,24},{4,28},{9,1},{1... | collective-permute-start | bytes 147464 | tf_op jit(solution)/shard_map/ppermute | solution.py:24
  42.2 0.7 %collective-permute-start.14 = (f32[3,32,128]{2,1,0:T(8,128)S(1)}, f32[3,32,128]{2,1,0:T(8,128)S(1)}, u32[]{:S(2)}, u32[]{:S(2)}) collective-permute-start(f32[3,32,128]{2,1,0:T(8,128)S(1)} %get-tuple-element.61.refs_4_), channel_id=1, source_target_pairs={{12,4},{20,12},{28,20},{4,28},{13,5},{21,13},{29,21},{5,29},{14,6}... | collective-permute-start | bytes 147464 | tf_op jit(solution)/shard_map/ppermute | solution.py:352
  42.8 1.7 %collective-permute-done.13.refs_5_ = f32[3,32,128]{2,1,0:T(8,128)S(1)} collective-permute-done((f32[3,32,128]{2,1,0:T(8,128)S(1)}, f32[3,32,128]{2,1,0:T(8,128)S(1)}, u32[]{:S(2)}, u32[]{:S(2)}) %collective-permute-start.13) | collective-permute-done | bytes 49184 | tf_op jit(solution)/shard_map/ppermute | solution.py:24
  44.5 0.0 collective-permute-done.14.refs_6_
  44.5 0.0 collective-permute-done.10.refs_1_
  44.5 0.5 %collective-permute-done.12.refs_3_ = bf16[3,3,32,128]{3,2,1,0:T(8,128)(2,1)S(1)} collective-permute-done((bf16[3,3,32,128]{3,2,1,0:T(8,128)(2,1)S(1)}, bf16[3,3,32,128]{3,2,1,0:T(8,128)(2,1)S(1)}, u32[]{:S(2)}, u32[]{:S(2)}) %collective-permute-start.12) | collective-permute-done | bytes 73760 | tf_op jit(solution)/shard_map/ppermute | solution.py:42
  45.0 0.7 %shard_map.44 = f32[3,5,32,128]{3,2,1,0:T(8,128)} custom-call(f32[3,3,32,128]{3,2,1,0:T(8,128)S(1)} %get-tuple-element.53.refs_0_, bf16[3,3,32,128]{3,2,1,0:T(8,128)(2,1)S(1)} %collective-permute-done.10.refs_1_, bf16[3,3,32,128]{3,2,1,0:T(8,128)(2,1)S(1)} %collective-permute-done.11.refs_2_, bf16[3,3,32,128]{3,2,1,0:T(8,128)(2,1)S(1)} %collective-permute-done.12.refs_3_, ...), custom_call_target="tpu_custom_call" | custom-call | tf_op jit(solution)/shard_map/pallas_call | solution.py:58
  (11 shorter events, 0.0 us)
Async XLA Ops:
  0.0 4.8 %copy-start.1 = (f32[4,8,128]{2,1,0:T(8,128)S(1)}, f32[4,8,128]{2,1,0:T(8,128)}, u32[]{:S(2)}) copy-start(f32[4,8,128]{2,1,0:T(8,128)} %refs_4_.1) | copy-start | bytes 49156
  0.0 4.8 %copy-start = (f32[3,4,8,128]{3,2,1,0:T(8,128)S(1)}, f32[3,4,8,128]{3,2,1,0:T(8,128)}, u32[]{:S(2)}) copy-start(f32[3,4,8,128]{3,2,1,0:T(8,128)} %refs_5_.1) | copy-start | bytes 147460
  1.7 28.3 %collective-permute-start.5 = (bf16[128,4096]{1,0:T(8,128)(2,1)S(1)}, bf16[128,4096]{1,0:T(8,128)(2,1)S(1)}, u32[]{:S(2)}, u32[]{:S(2)}) collective-permute-start(bf16[128,4096]{1,0:T(8,128)(2,1)S(1)} %bitcast.5), channel_id=1, source_target_pairs={{24,0},{28,4},{0,8},{4,12},{8,16},{12,20},{16,24},{20,28},{25,1},{... | collective-permute-start | bytes 3145736 | tf_op jit(solution)/shard_map/ppermute | solution.py:24
  4.9 9.2 %collective-permute-start = (bf16[128,1280]{1,0:T(8,128)(2,1)S(1)}, bf16[128,1280]{1,0:T(8,128)(2,1)S(1)}, u32[]{:S(2)}, u32[]{:S(2)}) collective-permute-start(bf16[128,1280]{1,0:T(8,128)(2,1)S(1)} %get-tuple-element.34), channel_id=1, source_target_pairs={{1,0},{0,1},{3,2},{2,3},{5,4},{4,5},{7,6},{6,7},{9,8},{8,9},{11,10... | collective-permute-start | bytes 983048 | tf_op jit(solution)/shard_map/ppermute | solution.py:24
  6.5 9.9 %collective-permute-start.1 = (bf16[128,1152]{1,0:T(8,128)(2,1)S(1)}, bf16[128,1152]{1,0:T(8,128)(2,1)S(1)}, u32[]{:S(2)}, u32[]{:S(2)}) collective-permute-start(bf16[128,1152]{1,0:T(8,128)(2,1)S(1)} %get-tuple-element.36), channel_id=1, source_target_pairs={{2,0},{0,2},{3,1},{1,3},{6,4},{4,6},{7,5},{5,7},{10,8},{8,10},{11,... | collective-permute-start | bytes 884744 | tf_op jit(solution)/shard_map/ppermute | solution.py:24
  8.0 13.0 %collective-permute-start.2 = (bf16[128,1152]{1,0:T(8,128)(2,1)S(1)}, bf16[128,1152]{1,0:T(8,128)(2,1)S(1)}, u32[]{:S(2)}, u32[]{:S(2)}) collective-permute-start(bf16[128,1152]{1,0:T(8,128)(2,1)S(1)} %get-tuple-element.37), channel_id=1, source_target_pairs={{2,0},{0,2},{3,1},{1,3},{6,4},{4,6},{7,5},{5,7},{10,8},{8,10},{11,... | collective-permute-start | bytes 884744 | tf_op jit(solution)/shard_map/ppermute | solution.py:24
  21.0 9.0 %collective-permute-start.3 = (bf16[384,2048]{1,0:T(8,128)(2,1)S(1)}, bf16[384,2048]{1,0:T(8,128)(2,1)S(1)}, u32[]{:S(2)}, u32[]{:S(2)}) collective-permute-start(bf16[384,2048]{1,0:T(8,128)(2,1)S(1)} %get-tuple-element.35.refs_0_), channel_id=1, source_target_pairs={{0,4},{4,0},{8,12},{12,8},{16,20},{20,16},{24,28},{28,24},{1,5},{5... | collective-permute-start | bytes 4718600 | tf_op jit(solution)/shard_map/ppermute | solution.py:316
  22.9 7.0 %collective-permute-start.4 = (bf16[384,2048]{1,0:T(8,128)(2,1)S(1)}, bf16[384,2048]{1,0:T(8,128)(2,1)S(1)}, u32[]{:S(2)}, u32[]{:S(2)}) collective-permute-start(bf16[384,2048]{1,0:T(8,128)(2,1)S(1)} %get-tuple-element.41.refs_1_), channel_id=1, source_target_pairs={{0,4},{4,0},{8,12},{12,8},{16,20},{20,16},{24,28},{28,24},{1,5},{5... | collective-permute-start | bytes 4718600 | tf_op jit(solution)/shard_map/ppermute | solution.py:316
  30.0 5.7 %collective-permute-start.9 = (bf16[128,4096]{1,0:T(8,128)(2,1)S(1)}, bf16[128,4096]{1,0:T(8,128)(2,1)S(1)}, u32[]{:S(2)}, u32[]{:S(2)}) collective-permute-start(bf16[128,4096]{1,0:T(8,128)(2,1)S(1)} %collective-permute-done.5.refs_4_.refs_2_), channel_id=1, source_target_pairs={{0,4},{4,0},{8,12},{12,8},{16,20},{20,16},{24,28},{28,24},{1,5},{5... | collective-permute-start | bytes 3145736 | tf_op jit(solution)/shard_map/ppermute | solution.py:328
  32.1 7.7 %collective-permute-start.6 = (bf16[2,3,32,128]{3,2,1,0:T(8,128)(2,1)S(1)}, bf16[2,3,32,128]{3,2,1,0:T(8,128)(2,1)S(1)}, u32[]{:S(2)}, u32[]{:S(2)}) collective-permute-start(bf16[2,3,32,128]{3,2,1,0:T(8,128)(2,1)S(1)} %get-tuple-element.46), channel_id=1, source_target_pairs={{0,1},{1,0},{2,3},{3,2},{4,5},{5,4},{6,7},{7,6},{8,9},{9,8},{10,11... | collective-permute-start | bytes 147464 | tf_op jit(solution)/shard_map/ppermute | solution.py:42
  33.7 6.6 %collective-permute-start.7 = (bf16[2,3,32,128]{3,2,1,0:T(8,128)(2,1)S(1)}, bf16[2,3,32,128]{3,2,1,0:T(8,128)(2,1)S(1)}, u32[]{:S(2)}, u32[]{:S(2)}) collective-permute-start(bf16[2,3,32,128]{3,2,1,0:T(8,128)(2,1)S(1)} %get-tuple-element.47), channel_id=1, source_target_pairs={{0,2},{1,3},{2,0},{3,1},{4,6},{5,7},{6,4},{7,5},{8,10},{9,11},{10,... | collective-permute-start | bytes 147464 | tf_op jit(solution)/shard_map/ppermute | solution.py:42
  35.2 5.2 %collective-permute-start.8 = (bf16[2,3,32,128]{3,2,1,0:T(8,128)(2,1)S(1)}, bf16[2,3,32,128]{3,2,1,0:T(8,128)(2,1)S(1)}, u32[]{:S(2)}, u32[]{:S(2)}) collective-permute-start(bf16[2,3,32,128]{3,2,1,0:T(8,128)(2,1)S(1)} %get-tuple-element.48), channel_id=1, source_target_pairs={{0,3},{1,2},{2,1},{3,0},{4,7},{5,6},{6,5},{7,4},{8,11},{9,10},{10,... | collective-permute-start | bytes 147464 | tf_op jit(solution)/shard_map/ppermute | solution.py:42
  36.7 7.8 %collective-permute-start.10 = (bf16[3,3,32,128]{3,2,1,0:T(8,128)(2,1)S(1)}, bf16[3,3,32,128]{3,2,1,0:T(8,128)(2,1)S(1)}, u32[]{:S(2)}, u32[]{:S(2)}) collective-permute-start(bf16[3,3,32,128]{3,2,1,0:T(8,128)(2,1)S(1)} %get-tuple-element.54), channel_id=1, source_target_pairs={{0,1},{1,0},{2,3},{3,2},{4,5},{5,4},{6,7},{7,6},{8,9},{9,8},{10,11... | collective-permute-start | bytes 221192 | tf_op jit(solution)/shard_map/ppermute | solution.py:42
  38.3 6.3 %collective-permute-start.11 = (bf16[3,3,32,128]{3,2,1,0:T(8,128)(2,1)S(1)}, bf16[3,3,32,128]{3,2,1,0:T(8,128)(2,1)S(1)}, u32[]{:S(2)}, u32[]{:S(2)}) collective-permute-start(bf16[3,3,32,128]{3,2,1,0:T(8,128)(2,1)S(1)} %get-tuple-element.55), channel_id=1, source_target_pairs={{0,2},{1,3},{2,0},{3,1},{4,6},{5,7},{6,4},{7,5},{8,10},{9,11},{10,... | collective-permute-start | bytes 221192 | tf_op jit(solution)/shard_map/ppermute | solution.py:42
  39.8 5.3 %collective-permute-start.12 = (bf16[3,3,32,128]{3,2,1,0:T(8,128)(2,1)S(1)}, bf16[3,3,32,128]{3,2,1,0:T(8,128)(2,1)S(1)}, u32[]{:S(2)}, u32[]{:S(2)}) collective-permute-start(bf16[3,3,32,128]{3,2,1,0:T(8,128)(2,1)S(1)} %get-tuple-element.56), channel_id=1, source_target_pairs={{0,3},{1,2},{2,1},{3,0},{4,7},{5,6},{6,5},{7,4},{8,11},{9,10},{10,... | collective-permute-start | bytes 221192 | tf_op jit(solution)/shard_map/ppermute | solution.py:42
  40.4 4.1 %collective-permute-start.13 = (f32[3,32,128]{2,1,0:T(8,128)S(1)}, f32[3,32,128]{2,1,0:T(8,128)S(1)}, u32[]{:S(2)}, u32[]{:S(2)}) collective-permute-start(f32[3,32,128]{2,1,0:T(8,128)S(1)} %get-tuple-element.62), channel_id=1, source_target_pairs={{8,0},{12,4},{16,8},{20,12},{24,16},{28,20},{0,24},{4,28},{9,1},{1... | collective-permute-start | bytes 147464 | tf_op jit(solution)/shard_map/ppermute | solution.py:24
  42.2 2.3 %collective-permute-start.14 = (f32[3,32,128]{2,1,0:T(8,128)S(1)}, f32[3,32,128]{2,1,0:T(8,128)S(1)}, u32[]{:S(2)}, u32[]{:S(2)}) collective-permute-start(f32[3,32,128]{2,1,0:T(8,128)S(1)} %get-tuple-element.61.refs_4_), channel_id=1, source_target_pairs={{12,4},{20,12},{28,20},{4,28},{13,5},{21,13},{29,21},{5,29},{14,6}... | collective-permute-start | bytes 147464 | tf_op jit(solution)/shard_map/ppermute | solution.py:352

commit v11 on v10

--- a/solution.py
+++ b/solution.py
@@ -10,9 +10,12 @@
 
 F32, BF16 = jnp.float32, jnp.bfloat16
 VMEM = pl.BlockSpec(memory_space=pltpu.VMEM)
+ANY = pl.BlockSpec(memory_space=pl.ANY)
 LIMIT = 12 * 1024 * 1024
 NT = (((1,), (1,)), ((), ()))
 CHUNK = 16
+FETCHES = 8
+MOST = 53248 * 1024
 
 
 def shape_of(shape, dtype):
@@ -43,14 +46,14 @@
     return got
 
 
-def call(body, outs, operands, scratch=(), specs=None, out_specs=None, us=0):
+def call(body, outs, operands, scratch=(), specs=None, out_specs=None, us=0, limit=LIMIT):
     run = pl.pallas_call(
         body,
         out_shape=outs,
         in_specs=specs or [VMEM] * len(operands),
         out_specs=out_specs or [VMEM] * len(outs),
         scratch_shapes=list(scratch),
-        compiler_params=pltpu.CompilerParams(vmem_limit_bytes=LIMIT),
+        compiler_params=pltpu.CompilerParams(vmem_limit_bytes=limit),
         cost_estimate=pl.CostEstimate(
             flops=0, bytes_accessed=int(us * 3e6), transcendentals=0
         ),
@@ -69,6 +72,17 @@
     high = value.astype(BF16).astype(F32)
     middle = (value - high).astype(BF16).astype(F32)
     return high, middle, value - high - middle
+
+
+def fetch(source, target, sems):
+    size = source.shape[0] // FETCHES
+    copies = []
+    for n in range(FETCHES):
+        part = pl.ds(n * size, size)
+        copies.append(pltpu.make_async_copy(source.at[part], target.at[part], sems.at[n]))
+        copies[n].start()
+    for copy in copies:
+        copy.wait()
 
 
 def edges(psi, coupling, grad, tail, head, hy, tmp, *, shape):
@@ -285,7 +299,15 @@
     scale = 1.0 / math.sqrt(cells * places)
 
     swap = [(i, i ^ 1) for i in range(lax.axis_size("blk"))]
-    psi = lax.optimization_barrier(orbitals.reshape(states, cells))
+    (raw,) = call(
+        fetch,
+        [shape_of(orbitals.shape, BF16)],
+        [orbitals],
+        scratch=[pltpu.SemaphoreType.DMA((FETCHES,))],
+        specs=[ANY],
+        limit=MOST,
+    )
+    psi = lax.optimization_barrier(raw.reshape(states, cells))
     two = shift(psi, "blk", -2)
 
     tmp = pltpu.VMEM((-(-9 * max(wx, wy) // 16) * 16, wz), F32)

time: 45.9 us -> 46.1 us (level)
  Pallas kernels: 8.86 us -> 10.2 us
  local copies, waits for them, and re-layouts: 1.69 us -> 0.46 us
    pallas_call x8 -> x9, Pallas kernels: 8.86 us -> 10.2 us  [call(): return list(run(*operands))]
    unnamed x5, local copies, waits for them, and re-layouts: 1.69 us -> 0.46 us
where the time goes in v11:
time: 46.1 us; the launch traced here: 45.9 us
  waiting for transfers between devices  18.4 us (40%)
  starting transfers between devices  16.8 us (36%)
  Pallas kernels  10.2 us (22%)
    ppermute x5, waiting for transfers between devices, shift(): lax.ppermute(block, axis, [((i + distance) % count, i) for i in range(cou...  17.8 us
    pallas_call x9, Pallas kernels, call(): return list(run(*operands))  10.2 us
    ppermute x5, starting transfers between devices, shift(): lax.ppermute(block, axis, [((i + distance) % count, i) for i in range(cou...  8.45 us
    ppermute x6, starting transfers between devices, exchange(): got.append(lax.ppermute(piece, ('dx', 'dy'), route))  7.11 us
  transfers between devices with their start and end apart: 15, of which 7 were waited for; matrix products, arithmetic and copies ran while one was open for 0% of the time, Pallas kernels for 18%

profile of v11, /device:TPU:0, one launch (start us, length us, event | category | flops | bytes accessed | tf_op | source)
XLA Modules:
  0.0 45.9 jit_solution(7294086854146681024)
XLA Ops:
  0.0 1.3 %shard_map.37 = bf16[128,4,8,128]{3,2,1,0:T(8,128)(2,1)S(1)} custom-call(bf16[128,4,8,128]{3,2,1,0:T(8,128)(2,1)} %source.1), custom_call_target="tpu_custom_call" | custom-call | tf_op jit(solution)/shard_map/pallas_call | solution.py:61
  1.4 0.0 copy-start
  1.4 0.0 copy-start.1
  1.4 0.5 copy.6
  1.8 3.1 %collective-permute-start.5 = (bf16[128,4096]{1,0:T(8,128)(2,1)S(1)}, bf16[128,4096]{1,0:T(8,128)(2,1)S(1)}, u32[]{:S(2)}, u32[]{:S(2)}) collective-permute-start(bf16[128,4096]{1,0:T(8,128)(2,1)S(1)} %bitcast.5), channel_id=1, source_target_pairs={{24,0},{28,4},{0,8},{4,12},{8,16},{12,20},{16,24},{20,28},{25,1},{... | collective-permute-start | bytes 3145736 | tf_op jit(solution)/shard_map/ppermute | solution.py:27
  4.9 0.1 shard_map.38
  5.1 1.6 %collective-permute-start = (bf16[128,1280]{1,0:T(8,128)(2,1)S(1)}, bf16[128,1280]{1,0:T(8,128)(2,1)S(1)}, u32[]{:S(2)}, u32[]{:S(2)}) collective-permute-start(bf16[128,1280]{1,0:T(8,128)(2,1)S(1)} %get-tuple-element.34), channel_id=1, source_target_pairs={{1,0},{0,1},{3,2},{2,3},{5,4},{4,5},{7,6},{6,7},{9,8},{8,9},{11,10... | collective-permute-start | bytes 983048 | tf_op jit(solution)/shard_map/ppermute | solution.py:27
  6.6 1.5 %collective-permute-start.1 = (bf16[128,1152]{1,0:T(8,128)(2,1)S(1)}, bf16[128,1152]{1,0:T(8,128)(2,1)S(1)}, u32[]{:S(2)}, u32[]{:S(2)}) collective-permute-start(bf16[128,1152]{1,0:T(8,128)(2,1)S(1)} %get-tuple-element.36), channel_id=1, source_target_pairs={{2,0},{0,2},{3,1},{1,3},{6,4},{4,6},{7,5},{5,7},{10,8},{8,10},{11,... | collective-permute-start | bytes 884744 | tf_op jit(solution)/shard_map/ppermute | solution.py:27
  8.1 0.5 %collective-permute-start.2 = (bf16[128,1152]{1,0:T(8,128)(2,1)S(1)}, bf16[128,1152]{1,0:T(8,128)(2,1)S(1)}, u32[]{:S(2)}, u32[]{:S(2)}) collective-permute-start(bf16[128,1152]{1,0:T(8,128)(2,1)S(1)} %get-tuple-element.37), channel_id=1, source_target_pairs={{2,0},{0,2},{3,1},{1,3},{6,4},{4,6},{7,5},{5,7},{10,8},{8,10},{11,... | collective-permute-start | bytes 884744 | tf_op jit(solution)/shard_map/ppermute | solution.py:27
  8.6 5.7 %collective-permute-done.refs_1_.refs_3_ = bf16[128,1280]{1,0:T(8,128)(2,1)S(1)} collective-permute-done((bf16[128,1280]{1,0:T(8,128)(2,1)S(1)}, bf16[128,1280]{1,0:T(8,128)(2,1)S(1)}, u32[]{:S(2)}, u32[]{:S(2)}) %collective-permute-start) | collective-permute-done | bytes 327712 | tf_op jit(solution)/shard_map/ppermute | solution.py:27
  14.3 1.9 %shard_map.39 = (bf16[384,2048]{1,0:T(8,128)(2,1)S(1)}, bf16[384,2048]{1,0:T(8,128)(2,1)S(1)}) custom-call(bf16[128,4096]{1,0:T(8,128)(2,1)S(1)} %bitcast.7, bf16[128,1280]{1,0:T(8,128)(2,1)S(1)} %collective-permute-done.refs_1_.refs_3_, f32[4,8,128]{2,1,0:T(8,128)S(1)} %copy-done.1, f32[3,4,8,128]{3,2,1,0:T(8,128)S(1)} %copy-done), custom_call_target="tpu_custom_call" | custom-call | tf_op jit(solution)/shard_map/pallas_call | solution.py:61
  16.2 0.4 collective-permute-done.1.refs_1_
  16.6 4.6 %collective-permute-done.2.refs_2_ = bf16[128,1152]{1,0:T(8,128)(2,1)S(1)} collective-permute-done((bf16[128,1152]{1,0:T(8,128)(2,1)S(1)}, bf16[128,1152]{1,0:T(8,128)(2,1)S(1)}, u32[]{:S(2)}, u32[]{:S(2)}) %collective-permute-start.2) | collective-permute-done | bytes 294944 | tf_op jit(solution)/shard_map/ppermute | solution.py:27
  21.1 0.0 collective-permute-start.3
  21.1 1.9 %shard_map.40 = (bf16[384,2048]{1,0:T(8,128)(2,1)S(1)}, bf16[384,2048]{1,0:T(8,128)(2,1)S(1)}) custom-call(bf16[128,4096]{1,0:T(8,128)(2,1)S(1)} %bitcast.8, bf16[128,1152]{1,0:T(8,128)(2,1)S(1)} %collective-permute-done.1.refs_1_, bf16[128,1152]{1,0:T(8,128)(2,1)S(1)} %collective-permute-done.2.refs_2_, ...), custom_call_target="tpu_custom_call" | custom-call | tf_op jit(solution)/shard_map/pallas_call | solution.py:61
  23.1 0.6 %collective-permute-start.4 = (bf16[384,2048]{1,0:T(8,128)(2,1)S(1)}, bf16[384,2048]{1,0:T(8,128)(2,1)S(1)}, u32[]{:S(2)}, u32[]{:S(2)}) collective-permute-start(bf16[384,2048]{1,0:T(8,128)(2,1)S(1)} %get-tuple-element.41.refs_1_), channel_id=1, source_target_pairs={{0,4},{4,0},{8,12},{12,8},{16,20},{20,16},{24,28},{28,24},{1,5},{5... | collective-permute-start | bytes 4718600 | tf_op jit(solution)/shard_map/ppermute | solution.py:338
  23.6 1.0 %shard_map.41.refs_6_.refs_4_ = f32[384,128]{1,0:T(8,128)S(1)} custom-call(bf16[384,2048]{1,0:T(8,128)(2,1)S(1)} %get-tuple-element.42.refs_0_, bf16[384,2048]{1,0:T(8,128)(2,1)S(1)} %get-tuple-element.43.refs_1_, bf16[128,4096]{1,0:T(8,128)(2,1)S(1)} %bitcast.9), custom_call_target="tpu_custom_call" | custom-call | tf_op jit(solution)/shard_map/pallas_call | solution.py:61
  24.6 5.5 %collective-permute-done.5.refs_4_.refs_2_ = bf16[128,4096]{1,0:T(8,128)(2,1)S(1)} collective-permute-done((bf16[128,4096]{1,0:T(8,128)(2,1)S(1)}, bf16[128,4096]{1,0:T(8,128)(2,1)S(1)}, u32[]{:S(2)}, u32[]{:S(2)}) %collective-permute-start.5) | collective-permute-done | bytes 1048608 | tf_op jit(solution)/shard_map/ppermute | solution.py:27
  30.1 2.1 %shard_map.42 = (f32[128,384]{1,0:T(8,128)S(1)}, f32[2,3,32,128]{3,2,1,0:T(8,128)S(1)}, bf16[2,3,32,128]{3,2,1,0:T(8,128)(2,1)S(1)}, bf16[2,3,32,128]{3,2,1,0:T(8,128)(2,1)S(1)}, bf16[2,3,32,128]{3,2,1,0:T(8,128)(2,1)S(1)}) custom-call(bf16[384,2048]{1,0:T(8,128)(2,1)S(1)} %get-tuple-element.35.refs_0_, bf16[384,2048]{1,0:T(8,128)(2,1)S(1)} %get-tuple-element.41.refs_1_, ...), custom_call_target="tpu_custom_call" | custom-call | bytes 3000000 | tf_op jit(solution)/shard_map/pallas_call | solution.py:61
  32.3 1.6 %collective-permute-start.6 = (bf16[2,3,32,128]{3,2,1,0:T(8,128)(2,1)S(1)}, bf16[2,3,32,128]{3,2,1,0:T(8,128)(2,1)S(1)}, u32[]{:S(2)}, u32[]{:S(2)}) collective-permute-start(bf16[2,3,32,128]{3,2,1,0:T(8,128)(2,1)S(1)} %get-tuple-element.46), channel_id=1, source_target_pairs={{0,1},{1,0},{2,3},{3,2},{4,5},{5,4},{6,7},{7,6},{8,9},{9,8},{10,11... | collective-permute-start | bytes 147464 | tf_op jit(solution)/shard_map/ppermute | solution.py:45
  33.8 1.5 %collective-permute-start.7 = (bf16[2,3,32,128]{3,2,1,0:T(8,128)(2,1)S(1)}, bf16[2,3,32,128]{3,2,1,0:T(8,128)(2,1)S(1)}, u32[]{:S(2)}, u32[]{:S(2)}) collective-permute-start(bf16[2,3,32,128]{3,2,1,0:T(8,128)(2,1)S(1)} %get-tuple-element.47), channel_id=1, source_target_pairs={{0,2},{1,3},{2,0},{3,1},{4,6},{5,7},{6,4},{7,5},{8,10},{9,11},{10,... | collective-permute-start | bytes 147464 | tf_op jit(solution)/shard_map/ppermute | solution.py:45
  35.3 0.5 %collective-permute-start.8 = (bf16[2,3,32,128]{3,2,1,0:T(8,128)(2,1)S(1)}, bf16[2,3,32,128]{3,2,1,0:T(8,128)(2,1)S(1)}, u32[]{:S(2)}, u32[]{:S(2)}) collective-permute-start(bf16[2,3,32,128]{3,2,1,0:T(8,128)(2,1)S(1)} %get-tuple-element.48), channel_id=1, source_target_pairs={{0,3},{1,2},{2,1},{3,0},{4,7},{5,6},{6,5},{7,4},{8,11},{9,10},{10,... | collective-permute-start | bytes 147464 | tf_op jit(solution)/shard_map/ppermute | solution.py:45
  35.8 1.0 %shard_map.43 = (f32[3,3,32,128]{3,2,1,0:T(8,128)S(1)}, bf16[3,3,32,128]{3,2,1,0:T(8,128)(2,1)S(1)}, bf16[3,3,32,128]{3,2,1,0:T(8,128)(2,1)S(1)}, bf16[3,3,32,128]{3,2,1,0:T(8,128)(2,1)S(1)}) custom-call(bf16[384,2048]{1,0:T(8,128)(2,1)S(1)} %get-tuple-element.42.refs_0_, bf16[384,2048]{1,0:T(8,128)(2,1)S(1)} %get-tuple-element.43.refs_1_, ...), custom_call_target="tpu_custom_call" | custom-call | bytes 3000000 | tf_op jit(solution)/shard_map/pallas_call | solution.py:61
  36.8 1.6 %collective-permute-start.10 = (bf16[3,3,32,128]{3,2,1,0:T(8,128)(2,1)S(1)}, bf16[3,3,32,128]{3,2,1,0:T(8,128)(2,1)S(1)}, u32[]{:S(2)}, u32[]{:S(2)}) collective-permute-start(bf16[3,3,32,128]{3,2,1,0:T(8,128)(2,1)S(1)} %get-tuple-element.54), channel_id=1, source_target_pairs={{0,1},{1,0},{2,3},{3,2},{4,5},{5,4},{6,7},{7,6},{8,9},{9,8},{10,11... | collective-permute-start | bytes 221192 | tf_op jit(solution)/shard_map/ppermute | solution.py:45
  38.4 1.5 %collective-permute-start.11 = (bf16[3,3,32,128]{3,2,1,0:T(8,128)(2,1)S(1)}, bf16[3,3,32,128]{3,2,1,0:T(8,128)(2,1)S(1)}, u32[]{:S(2)}, u32[]{:S(2)}) collective-permute-start(bf16[3,3,32,128]{3,2,1,0:T(8,128)(2,1)S(1)} %get-tuple-element.55), channel_id=1, source_target_pairs={{0,2},{1,3},{2,0},{3,1},{4,6},{5,7},{6,4},{7,5},{8,10},{9,11},{10,... | collective-permute-start | bytes 221192 | tf_op jit(solution)/shard_map/ppermute | solution.py:45
  39.9 0.5 %collective-permute-start.12 = (bf16[3,3,32,128]{3,2,1,0:T(8,128)(2,1)S(1)}, bf16[3,3,32,128]{3,2,1,0:T(8,128)(2,1)S(1)}, u32[]{:S(2)}, u32[]{:S(2)}) collective-permute-start(bf16[3,3,32,128]{3,2,1,0:T(8,128)(2,1)S(1)} %get-tuple-element.56), channel_id=1, source_target_pairs={{0,3},{1,2},{2,1},{3,0},{4,7},{5,6},{6,5},{7,4},{8,11},{9,10},{10,... | collective-permute-start | bytes 221192 | tf_op jit(solution)/shard_map/ppermute | solution.py:45
  40.4 0.1 collective-permute-done.8.refs_3_
  40.5 1.8 %collective-permute-start.13 = (f32[3,32,128]{2,1,0:T(8,128)S(1)}, f32[3,32,128]{2,1,0:T(8,128)S(1)}, u32[]{:S(2)}, u32[]{:S(2)}) collective-permute-start(f32[3,32,128]{2,1,0:T(8,128)S(1)} %get-tuple-element.62), channel_id=1, source_target_pairs={{8,0},{12,4},{16,8},{20,12},{24,16},{28,20},{0,24},{4,28},{9,1},{1... | collective-permute-start | bytes 147464 | tf_op jit(solution)/shard_map/ppermute | solution.py:27
  42.3 0.7 %collective-permute-start.14 = (f32[3,32,128]{2,1,0:T(8,128)S(1)}, f32[3,32,128]{2,1,0:T(8,128)S(1)}, u32[]{:S(2)}, u32[]{:S(2)}) collective-permute-start(f32[3,32,128]{2,1,0:T(8,128)S(1)} %get-tuple-element.61.refs_4_), channel_id=1, source_target_pairs={{12,4},{20,12},{28,20},{4,28},{13,5},{21,13},{29,21},{5,29},{14,6}... | collective-permute-start | bytes 147464 | tf_op jit(solution)/shard_map/ppermute | solution.py:374
  43.0 1.7 %collective-permute-done.13.refs_5_ = f32[3,32,128]{2,1,0:T(8,128)S(1)} collective-permute-done((f32[3,32,128]{2,1,0:T(8,128)S(1)}, f32[3,32,128]{2,1,0:T(8,128)S(1)}, u32[]{:S(2)}, u32[]{:S(2)}) %collective-permute-start.13) | collective-permute-done | bytes 49184 | tf_op jit(solution)/shard_map/ppermute | solution.py:27
  44.7 0.5 %collective-permute-done.12.refs_3_ = bf16[3,3,32,128]{3,2,1,0:T(8,128)(2,1)S(1)} collective-permute-done((bf16[3,3,32,128]{3,2,1,0:T(8,128)(2,1)S(1)}, bf16[3,3,32,128]{3,2,1,0:T(8,128)(2,1)S(1)}, u32[]{:S(2)}, u32[]{:S(2)}) %collective-permute-start.12) | collective-permute-done | bytes 73760 | tf_op jit(solution)/shard_map/ppermute | solution.py:45
  45.2 0.7 %shard_map.45 = f32[3,5,32,128]{3,2,1,0:T(8,128)} custom-call(f32[3,3,32,128]{3,2,1,0:T(8,128)S(1)} %get-tuple-element.53.refs_0_, bf16[3,3,32,128]{3,2,1,0:T(8,128)(2,1)S(1)} %collective-permute-done.10.refs_1_, bf16[3,3,32,128]{3,2,1,0:T(8,128)(2,1)S(1)} %collective-permute-done.11.refs_2_, bf16[3,3,32,128]{3,2,1,0:T(8,128)(2,1)S(1)} %collective-permute-done.12.refs_3_, ...), custom_call_target="tpu_custom_call" | custom-call | tf_op jit(solution)/shard_map/pallas_call | solution.py:61
  (12 shorter events, 0.1 us)
Async XLA Ops:
  1.4 3.6 %copy-start = (f32[3,4,8,128]{3,2,1,0:T(8,128)S(1)}, f32[3,4,8,128]{3,2,1,0:T(8,128)}, u32[]{:S(2)}) copy-start(f32[3,4,8,128]{3,2,1,0:T(8,128)} %refs_5_.1) | copy-start | bytes 147460
  1.4 3.5 %copy-start.1 = (f32[4,8,128]{2,1,0:T(8,128)S(1)}, f32[4,8,128]{2,1,0:T(8,128)}, u32[]{:S(2)}) copy-start(f32[4,8,128]{2,1,0:T(8,128)} %refs_4_.1) | copy-start | bytes 49156
  1.8 28.3 %collective-permute-start.5 = (bf16[128,4096]{1,0:T(8,128)(2,1)S(1)}, bf16[128,4096]{1,0:T(8,128)(2,1)S(1)}, u32[]{:S(2)}, u32[]{:S(2)}) collective-permute-start(bf16[128,4096]{1,0:T(8,128)(2,1)S(1)} %bitcast.5), channel_id=1, source_target_pairs={{24,0},{28,4},{0,8},{4,12},{8,16},{12,20},{16,24},{20,28},{25,1},{... | collective-permute-start | bytes 3145736 | tf_op jit(solution)/shard_map/ppermute | solution.py:27
  5.1 9.2 %collective-permute-start = (bf16[128,1280]{1,0:T(8,128)(2,1)S(1)}, bf16[128,1280]{1,0:T(8,128)(2,1)S(1)}, u32[]{:S(2)}, u32[]{:S(2)}) collective-permute-start(bf16[128,1280]{1,0:T(8,128)(2,1)S(1)} %get-tuple-element.34), channel_id=1, source_target_pairs={{1,0},{0,1},{3,2},{2,3},{5,4},{4,5},{7,6},{6,7},{9,8},{8,9},{11,10... | collective-permute-start | bytes 983048 | tf_op jit(solution)/shard_map/ppermute | solution.py:27
  6.6 9.9 %collective-permute-start.1 = (bf16[128,1152]{1,0:T(8,128)(2,1)S(1)}, bf16[128,1152]{1,0:T(8,128)(2,1)S(1)}, u32[]{:S(2)}, u32[]{:S(2)}) collective-permute-start(bf16[128,1152]{1,0:T(8,128)(2,1)S(1)} %get-tuple-element.36), channel_id=1, source_target_pairs={{2,0},{0,2},{3,1},{1,3},{6,4},{4,6},{7,5},{5,7},{10,8},{8,10},{11,... | collective-permute-start | bytes 884744 | tf_op jit(solution)/shard_map/ppermute | solution.py:27
  8.1 13.0 %collective-permute-start.2 = (bf16[128,1152]{1,0:T(8,128)(2,1)S(1)}, bf16[128,1152]{1,0:T(8,128)(2,1)S(1)}, u32[]{:S(2)}, u32[]{:S(2)}) collective-permute-start(bf16[128,1152]{1,0:T(8,128)(2,1)S(1)} %get-tuple-element.37), channel_id=1, source_target_pairs={{2,0},{0,2},{3,1},{1,3},{6,4},{4,6},{7,5},{5,7},{10,8},{8,10},{11,... | collective-permute-start | bytes 884744 | tf_op jit(solution)/shard_map/ppermute | solution.py:27
  21.1 9.0 %collective-permute-start.3 = (bf16[384,2048]{1,0:T(8,128)(2,1)S(1)}, bf16[384,2048]{1,0:T(8,128)(2,1)S(1)}, u32[]{:S(2)}, u32[]{:S(2)}) collective-permute-start(bf16[384,2048]{1,0:T(8,128)(2,1)S(1)} %get-tuple-element.35.refs_0_), channel_id=1, source_target_pairs={{0,4},{4,0},{8,12},{12,8},{16,20},{20,16},{24,28},{28,24},{1,5},{5... | collective-permute-start | bytes 4718600 | tf_op jit(solution)/shard_map/ppermute | solution.py:338
  23.1 7.0 %collective-permute-start.4 = (bf16[384,2048]{1,0:T(8,128)(2,1)S(1)}, bf16[384,2048]{1,0:T(8,128)(2,1)S(1)}, u32[]{:S(2)}, u32[]{:S(2)}) collective-permute-start(bf16[384,2048]{1,0:T(8,128)(2,1)S(1)} %get-tuple-element.41.refs_1_), channel_id=1, source_target_pairs={{0,4},{4,0},{8,12},{12,8},{16,20},{20,16},{24,28},{28,24},{1,5},{5... | collective-permute-start | bytes 4718600 | tf_op jit(solution)/shard_map/ppermute | solution.py:338
  30.1 5.7 %collective-permute-start.9 = (bf16[128,4096]{1,0:T(8,128)(2,1)S(1)}, bf16[128,4096]{1,0:T(8,128)(2,1)S(1)}, u32[]{:S(2)}, u32[]{:S(2)}) collective-permute-start(bf16[128,4096]{1,0:T(8,128)(2,1)S(1)} %collective-permute-done.5.refs_4_.refs_2_), channel_id=1, source_target_pairs={{0,4},{4,0},{8,12},{12,8},{16,20},{20,16},{24,28},{28,24},{1,5},{5... | collective-permute-start | bytes 3145736 | tf_op jit(solution)/shard_map/ppermute | solution.py:350
  32.3 7.7 %collective-permute-start.6 = (bf16[2,3,32,128]{3,2,1,0:T(8,128)(2,1)S(1)}, bf16[2,3,32,128]{3,2,1,0:T(8,128)(2,1)S(1)}, u32[]{:S(2)}, u32[]{:S(2)}) collective-permute-start(bf16[2,3,32,128]{3,2,1,0:T(8,128)(2,1)S(1)} %get-tuple-element.46), channel_id=1, source_target_pairs={{0,1},{1,0},{2,3},{3,2},{4,5},{5,4},{6,7},{7,6},{8,9},{9,8},{10,11... | collective-permute-start | bytes 147464 | tf_op jit(solution)/shard_map/ppermute | solution.py:45
  33.8 6.6 %collective-permute-start.7 = (bf16[2,3,32,128]{3,2,1,0:T(8,128)(2,1)S(1)}, bf16[2,3,32,128]{3,2,1,0:T(8,128)(2,1)S(1)}, u32[]{:S(2)}, u32[]{:S(2)}) collective-permute-start(bf16[2,3,32,128]{3,2,1,0:T(8,128)(2,1)S(1)} %get-tuple-element.47), channel_id=1, source_target_pairs={{0,2},{1,3},{2,0},{3,1},{4,6},{5,7},{6,4},{7,5},{8,10},{9,11},{10,... | collective-permute-start | bytes 147464 | tf_op jit(solution)/shard_map/ppermute | solution.py:45
  35.3 5.2 %collective-permute-start.8 = (bf16[2,3,32,128]{3,2,1,0:T(8,128)(2,1)S(1)}, bf16[2,3,32,128]{3,2,1,0:T(8,128)(2,1)S(1)}, u32[]{:S(2)}, u32[]{:S(2)}) collective-permute-start(bf16[2,3,32,128]{3,2,1,0:T(8,128)(2,1)S(1)} %get-tuple-element.48), channel_id=1, source_target_pairs={{0,3},{1,2},{2,1},{3,0},{4,7},{5,6},{6,5},{7,4},{8,11},{9,10},{10,... | collective-permute-start | bytes 147464 | tf_op jit(solution)/shard_map/ppermute | solution.py:45
  36.8 7.8 %collective-permute-start.10 = (bf16[3,3,32,128]{3,2,1,0:T(8,128)(2,1)S(1)}, bf16[3,3,32,128]{3,2,1,0:T(8,128)(2,1)S(1)}, u32[]{:S(2)}, u32[]{:S(2)}) collective-permute-start(bf16[3,3,32,128]{3,2,1,0:T(8,128)(2,1)S(1)} %get-tuple-element.54), channel_id=1, source_target_pairs={{0,1},{1,0},{2,3},{3,2},{4,5},{5,4},{6,7},{7,6},{8,9},{9,8},{10,11... | collective-permute-start | bytes 221192 | tf_op jit(solution)/shard_map/ppermute | solution.py:45
  38.4 6.3 %collective-permute-start.11 = (bf16[3,3,32,128]{3,2,1,0:T(8,128)(2,1)S(1)}, bf16[3,3,32,128]{3,2,1,0:T(8,128)(2,1)S(1)}, u32[]{:S(2)}, u32[]{:S(2)}) collective-permute-start(bf16[3,3,32,128]{3,2,1,0:T(8,128)(2,1)S(1)} %get-tuple-element.55), channel_id=1, source_target_pairs={{0,2},{1,3},{2,0},{3,1},{4,6},{5,7},{6,4},{7,5},{8,10},{9,11},{10,... | collective-permute-start | bytes 221192 | tf_op jit(solution)/shard_map/ppermute | solution.py:45
  39.9 5.3 %collective-permute-start.12 = (bf16[3,3,32,128]{3,2,1,0:T(8,128)(2,1)S(1)}, bf16[3,3,32,128]{3,2,1,0:T(8,128)(2,1)S(1)}, u32[]{:S(2)}, u32[]{:S(2)}) collective-permute-start(bf16[3,3,32,128]{3,2,1,0:T(8,128)(2,1)S(1)} %get-tuple-element.56), channel_id=1, source_target_pairs={{0,3},{1,2},{2,1},{3,0},{4,7},{5,6},{6,5},{7,4},{8,11},{9,10},{10,... | collective-permute-start | bytes 221192 | tf_op jit(solution)/shard_map/ppermute | solution.py:45
  40.5 4.1 %collective-permute-start.13 = (f32[3,32,128]{2,1,0:T(8,128)S(1)}, f32[3,32,128]{2,1,0:T(8,128)S(1)}, u32[]{:S(2)}, u32[]{:S(2)}) collective-permute-start(f32[3,32,128]{2,1,0:T(8,128)S(1)} %get-tuple-element.62), channel_id=1, source_target_pairs={{8,0},{12,4},{16,8},{20,12},{24,16},{28,20},{0,24},{4,28},{9,1},{1... | collective-permute-start | bytes 147464 | tf_op jit(solution)/shard_map/ppermute | solution.py:27
  42.3 2.4 %collective-permute-start.14 = (f32[3,32,128]{2,1,0:T(8,128)S(1)}, f32[3,32,128]{2,1,0:T(8,128)S(1)}, u32[]{:S(2)}, u32[]{:S(2)}) collective-permute-start(f32[3,32,128]{2,1,0:T(8,128)S(1)} %get-tuple-element.61.refs_4_), channel_id=1, source_target_pairs={{12,4},{20,12},{28,20},{4,28},{13,5},{21,13},{29,21},{5,29},{14,6}... | collective-permute-start | bytes 147464 | tf_op jit(solution)/shard_map/ppermute | solution.py:374

commit v12 on v10

--- a/solution.py
+++ b/solution.py
@@ -285,8 +285,8 @@
     scale = 1.0 / math.sqrt(cells * places)
 
     swap = [(i, i ^ 1) for i in range(lax.axis_size("blk"))]
+    two = shift(orbitals, "blk", -2)
     psi = lax.optimization_barrier(orbitals.reshape(states, cells))
-    two = shift(psi, "blk", -2)
 
     tmp = pltpu.VMEM((-(-9 * max(wx, wy) // 16) * 16, wz), F32)
     tail, head, hy = call(
@@ -325,6 +325,7 @@
 
     given = dict(layer=layer, plane=plane, scale=scale)
     two, own = lax.optimization_barrier((two, own))
+    two = lax.optimization_barrier(two.reshape(states, cells))
     one = lax.ppermute(two, "blk", swap)
     mate, kept_there, *sends = call(
         functools.partial(there_tiles, **given),

time: 45.9 us -> 44.9 us (0.978)
  waiting for transfers between devices: 18.4 us -> 16.8 us
  local copies, waits for them, and re-layouts: 1.69 us -> 2.16 us
    ppermute x5, waiting for transfers between devices: 17.7 us -> 16.2 us  [shift(): lax.ppermute(block, axis, [((i + distance) % count, i) for i in range(cou...]
    unnamed x5 -> x6, local copies, waits for them, and re-layouts: 1.69 us -> 2.16 us
  transfers between devices with their start and end apart: 15 -> 15, of which waited for: 7 -> 7; matrix products, arithmetic and copies ran while one was open for 0% -> 5% of each run, Pallas kernels for 18% -> 18%
where the time goes in v12:
time: 44.9 us; the launch traced here: 44.8 us
  starting transfers between devices  16.8 us (37%)
  waiting for transfers between devices  16.8 us (37%)
  Pallas kernels  8.87 us (20%)
  local copies, waits for them, and re-layouts  2.16 us (5%)
    ppermute x5, waiting for transfers between devices, shift(): lax.ppermute(block, axis, [((i + distance) % count, i) for i in range(cou...  16.2 us
    pallas_call x8, Pallas kernels, call(): return list(run(*operands))  8.87 us
    ppermute x5, starting transfers between devices, shift(): lax.ppermute(block, axis, [((i + distance) % count, i) for i in range(cou...  8.4 us
    ppermute x6, starting transfers between devices, exchange(): got.append(lax.ppermute(piece, ('dx', 'dy'), route))  7.11 us
    unnamed x6, local copies, waits for them, and re-layouts  2.16 us
  transfers between devices with their start and end apart: 15, of which 7 were waited for; matrix products, arithmetic and copies ran while one was open for 5% of the time, Pallas kernels for 18%

profile of v12, /device:TPU:0, one launch (start us, length us, event | category | flops | bytes accessed | tf_op | source)
XLA Modules:
  0.0 44.8 jit_solution(15224945182567697236)
XLA Ops:
  0.0 3.0 %collective-permute-start.5 = (bf16[128,4,8,128]{3,2,1,0:T(8,128)(2,1)}, bf16[128,4,8,128]{3,2,1,0:T(8,128)(2,1)S(1)}, u32[]{:S(2)}, u32[]{:S(2)}) collective-permute-start(bf16[128,4,8,128]{3,2,1,0:T(8,128)(2,1)} %param.3), channel_id=1, source_target_pairs={{24,0},{28,4},{0,8},{4,12},{8,16},{12,20},{16,24},{20,28},{25,1},{... | collective-permute-start | bytes 3145736 | tf_op jit(solution)/shard_map/ppermute | solution.py:24
  3.0 1.7 %copy.9 = bf16[16,8,32,128]{3,1,2,0:T(8,128)(2,1)S(1)} copy(bf16[16,8,32,128]{3,2,1,0:T(8,128)(2,1)} %bitcast.18) | data formatting | bytes 2097152
  4.8 0.1 shard_map.37
  4.9 1.6 %collective-permute-start = (bf16[128,1280]{1,0:T(8,128)(2,1)S(1)}, bf16[128,1280]{1,0:T(8,128)(2,1)S(1)}, u32[]{:S(2)}, u32[]{:S(2)}) collective-permute-start(bf16[128,1280]{1,0:T(8,128)(2,1)S(1)} %get-tuple-element.34), channel_id=1, source_target_pairs={{1,0},{0,1},{3,2},{2,3},{5,4},{4,5},{7,6},{6,7},{9,8},{8,9},{11,10... | collective-permute-start | bytes 983048 | tf_op jit(solution)/shard_map/ppermute | solution.py:24
  6.4 1.5 %collective-permute-start.1 = (bf16[128,1152]{1,0:T(8,128)(2,1)S(1)}, bf16[128,1152]{1,0:T(8,128)(2,1)S(1)}, u32[]{:S(2)}, u32[]{:S(2)}) collective-permute-start(bf16[128,1152]{1,0:T(8,128)(2,1)S(1)} %get-tuple-element.36), channel_id=1, source_target_pairs={{2,0},{0,2},{3,1},{1,3},{6,4},{4,6},{7,5},{5,7},{10,8},{8,10},{11,... | collective-permute-start | bytes 884744 | tf_op jit(solution)/shard_map/ppermute | solution.py:24
  8.0 0.5 %collective-permute-start.2 = (bf16[128,1152]{1,0:T(8,128)(2,1)S(1)}, bf16[128,1152]{1,0:T(8,128)(2,1)S(1)}, u32[]{:S(2)}, u32[]{:S(2)}) collective-permute-start(bf16[128,1152]{1,0:T(8,128)(2,1)S(1)} %get-tuple-element.37), channel_id=1, source_target_pairs={{2,0},{0,2},{3,1},{1,3},{6,4},{4,6},{7,5},{5,7},{10,8},{8,10},{11,... | collective-permute-start | bytes 884744 | tf_op jit(solution)/shard_map/ppermute | solution.py:24
  8.5 5.7 %collective-permute-done.refs_1_.refs_3_ = bf16[128,1280]{1,0:T(8,128)(2,1)S(1)} collective-permute-done((bf16[128,1280]{1,0:T(8,128)(2,1)S(1)}, bf16[128,1280]{1,0:T(8,128)(2,1)S(1)}, u32[]{:S(2)}, u32[]{:S(2)}) %collective-permute-start) | collective-permute-done | bytes 327712 | tf_op jit(solution)/shard_map/ppermute | solution.py:24
  14.1 1.9 %shard_map.38 = (bf16[384,2048]{1,0:T(8,128)(2,1)S(1)}, bf16[384,2048]{1,0:T(8,128)(2,1)S(1)}) custom-call(bf16[128,4096]{1,0:T(8,128)(2,1)S(1)} %bitcast.11, bf16[128,1280]{1,0:T(8,128)(2,1)S(1)} %collective-permute-done.refs_1_.refs_3_, f32[4,8,128]{2,1,0:T(8,128)S(1)} %copy-done.1, f32[3,4,8,128]{3,2,1,0:T(8,128)S(1)} %copy-done), custom_call_target="tpu_custom_call" | custom-call | tf_op jit(solution)/shard_map/pallas_call | solution.py:58
  16.0 0.4 collective-permute-done.1.refs_1_
  16.4 4.6 %collective-permute-done.2.refs_2_ = bf16[128,1152]{1,0:T(8,128)(2,1)S(1)} collective-permute-done((bf16[128,1152]{1,0:T(8,128)(2,1)S(1)}, bf16[128,1152]{1,0:T(8,128)(2,1)S(1)}, u32[]{:S(2)}, u32[]{:S(2)}) %collective-permute-start.2) | collective-permute-done | bytes 294944 | tf_op jit(solution)/shard_map/ppermute | solution.py:24
  21.0 0.0 collective-permute-start.3
  21.0 1.9 %shard_map.39 = (bf16[384,2048]{1,0:T(8,128)(2,1)S(1)}, bf16[384,2048]{1,0:T(8,128)(2,1)S(1)}) custom-call(bf16[128,4096]{1,0:T(8,128)(2,1)S(1)} %bitcast.12, bf16[128,1152]{1,0:T(8,128)(2,1)S(1)} %collective-permute-done.1.refs_1_, bf16[128,1152]{1,0:T(8,128)(2,1)S(1)} %collective-permute-done.2.refs_2_, ...), custom_call_target="tpu_custom_call" | custom-call | tf_op jit(solution)/shard_map/pallas_call | solution.py:58
  22.9 0.6 %collective-permute-start.4 = (bf16[384,2048]{1,0:T(8,128)(2,1)S(1)}, bf16[384,2048]{1,0:T(8,128)(2,1)S(1)}, u32[]{:S(2)}, u32[]{:S(2)}) collective-permute-start(bf16[384,2048]{1,0:T(8,128)(2,1)S(1)} %get-tuple-element.41.refs_1_), channel_id=1, source_target_pairs={{0,4},{4,0},{8,12},{12,8},{16,20},{20,16},{24,28},{28,24},{1,5},{5... | collective-permute-start | bytes 4718600 | tf_op jit(solution)/shard_map/ppermute | solution.py:316
  23.5 1.0 %shard_map.40.refs_6_.refs_4_ = f32[384,128]{1,0:T(8,128)S(1)} custom-call(bf16[384,2048]{1,0:T(8,128)(2,1)S(1)} %get-tuple-element.42.refs_0_, bf16[384,2048]{1,0:T(8,128)(2,1)S(1)} %get-tuple-element.43.refs_1_, bf16[128,4096]{1,0:T(8,128)(2,1)S(1)} %bitcast.13), custom_call_target="tpu_custom_call" | custom-call | tf_op jit(solution)/shard_map/pallas_call | solution.py:58
  24.4 4.0 %collective-permute-done.5 = bf16[128,4,8,128]{3,2,1,0:T(8,128)(2,1)S(1)} collective-permute-done((bf16[128,4,8,128]{3,2,1,0:T(8,128)(2,1)}, bf16[128,4,8,128]{3,2,1,0:T(8,128)(2,1)S(1)}, u32[]{:S(2)}, u32[]{:S(2)}) %collective-permute-start.5) | collective-permute-done | bytes 1048608 | tf_op jit(solution)/shard_map/ppermute | solution.py:24
  28.4 0.5 %copy.8 = bf16[16,8,32,128]{3,1,2,0:T(8,128)(2,1)S(1)} copy(bf16[16,8,32,128]{3,2,1,0:T(8,128)(2,1)S(1)} %bitcast.19) | data formatting | bytes 2097152
  28.9 0.1 collective-permute-start.9
  29.0 0.0 collective-permute-done.3.refs_2_
  29.0 2.1 %shard_map.41 = (f32[128,384]{1,0:T(8,128)S(1)}, f32[2,3,32,128]{3,2,1,0:T(8,128)S(1)}, bf16[2,3,32,128]{3,2,1,0:T(8,128)(2,1)S(1)}, bf16[2,3,32,128]{3,2,1,0:T(8,128)(2,1)S(1)}, bf16[2,3,32,128]{3,2,1,0:T(8,128)(2,1)S(1)}) custom-call(bf16[384,2048]{1,0:T(8,128)(2,1)S(1)} %get-tuple-element.35.refs_0_, bf16[384,2048]{1,0:T(8,128)(2,1)S(1)} %get-tuple-element.41.refs_1_, ...), custom_call_target="tpu_custom_call" | custom-call | bytes 3000000 | tf_op jit(solution)/shard_map/pallas_call | solution.py:58
  31.1 1.6 %collective-permute-start.6 = (bf16[2,3,32,128]{3,2,1,0:T(8,128)(2,1)S(1)}, bf16[2,3,32,128]{3,2,1,0:T(8,128)(2,1)S(1)}, u32[]{:S(2)}, u32[]{:S(2)}) collective-permute-start(bf16[2,3,32,128]{3,2,1,0:T(8,128)(2,1)S(1)} %get-tuple-element.46), channel_id=1, source_target_pairs={{0,1},{1,0},{2,3},{3,2},{4,5},{5,4},{6,7},{7,6},{8,9},{9,8},{10,11... | collective-permute-start | bytes 147464 | tf_op jit(solution)/shard_map/ppermute | solution.py:42
  32.7 1.5 %collective-permute-start.7 = (bf16[2,3,32,128]{3,2,1,0:T(8,128)(2,1)S(1)}, bf16[2,3,32,128]{3,2,1,0:T(8,128)(2,1)S(1)}, u32[]{:S(2)}, u32[]{:S(2)}) collective-permute-start(bf16[2,3,32,128]{3,2,1,0:T(8,128)(2,1)S(1)} %get-tuple-element.47), channel_id=1, source_target_pairs={{0,2},{1,3},{2,0},{3,1},{4,6},{5,7},{6,4},{7,5},{8,10},{9,11},{10,... | collective-permute-start | bytes 147464 | tf_op jit(solution)/shard_map/ppermute | solution.py:42
  34.2 0.5 %collective-permute-start.8 = (bf16[2,3,32,128]{3,2,1,0:T(8,128)(2,1)S(1)}, bf16[2,3,32,128]{3,2,1,0:T(8,128)(2,1)S(1)}, u32[]{:S(2)}, u32[]{:S(2)}) collective-permute-start(bf16[2,3,32,128]{3,2,1,0:T(8,128)(2,1)S(1)} %get-tuple-element.48), channel_id=1, source_target_pairs={{0,3},{1,2},{2,1},{3,0},{4,7},{5,6},{6,5},{7,4},{8,11},{9,10},{10,... | collective-permute-start | bytes 147464 | tf_op jit(solution)/shard_map/ppermute | solution.py:42
  34.7 1.0 %shard_map.42 = (f32[3,3,32,128]{3,2,1,0:T(8,128)S(1)}, bf16[3,3,32,128]{3,2,1,0:T(8,128)(2,1)S(1)}, bf16[3,3,32,128]{3,2,1,0:T(8,128)(2,1)S(1)}, bf16[3,3,32,128]{3,2,1,0:T(8,128)(2,1)S(1)}) custom-call(bf16[384,2048]{1,0:T(8,128)(2,1)S(1)} %get-tuple-element.42.refs_0_, bf16[384,2048]{1,0:T(8,128)(2,1)S(1)} %get-tuple-element.43.refs_1_, ...), custom_call_target="tpu_custom_call" | custom-call | bytes 3000000 | tf_op jit(solution)/shard_map/pallas_call | solution.py:58
  35.7 1.6 %collective-permute-start.10 = (bf16[3,3,32,128]{3,2,1,0:T(8,128)(2,1)S(1)}, bf16[3,3,32,128]{3,2,1,0:T(8,128)(2,1)S(1)}, u32[]{:S(2)}, u32[]{:S(2)}) collective-permute-start(bf16[3,3,32,128]{3,2,1,0:T(8,128)(2,1)S(1)} %get-tuple-element.54), channel_id=1, source_target_pairs={{0,1},{1,0},{2,3},{3,2},{4,5},{5,4},{6,7},{7,6},{8,9},{9,8},{10,11... | collective-permute-start | bytes 221192 | tf_op jit(solution)/shard_map/ppermute | solution.py:42
  37.3 1.5 %collective-permute-start.11 = (bf16[3,3,32,128]{3,2,1,0:T(8,128)(2,1)S(1)}, bf16[3,3,32,128]{3,2,1,0:T(8,128)(2,1)S(1)}, u32[]{:S(2)}, u32[]{:S(2)}) collective-permute-start(bf16[3,3,32,128]{3,2,1,0:T(8,128)(2,1)S(1)} %get-tuple-element.55), channel_id=1, source_target_pairs={{0,2},{1,3},{2,0},{3,1},{4,6},{5,7},{6,4},{7,5},{8,10},{9,11},{10,... | collective-permute-start | bytes 221192 | tf_op jit(solution)/shard_map/ppermute | solution.py:42
  38.8 0.5 %collective-permute-start.12 = (bf16[3,3,32,128]{3,2,1,0:T(8,128)(2,1)S(1)}, bf16[3,3,32,128]{3,2,1,0:T(8,128)(2,1)S(1)}, u32[]{:S(2)}, u32[]{:S(2)}) collective-permute-start(bf16[3,3,32,128]{3,2,1,0:T(8,128)(2,1)S(1)} %get-tuple-element.56), channel_id=1, source_target_pairs={{0,3},{1,2},{2,1},{3,0},{4,7},{5,6},{6,5},{7,4},{8,11},{9,10},{10,... | collective-permute-start | bytes 221192 | tf_op jit(solution)/shard_map/ppermute | solution.py:42
  39.3 0.1 collective-permute-done.8.refs_3_
  39.4 1.8 %collective-permute-start.13 = (f32[3,32,128]{2,1,0:T(8,128)S(1)}, f32[3,32,128]{2,1,0:T(8,128)S(1)}, u32[]{:S(2)}, u32[]{:S(2)}) collective-permute-start(f32[3,32,128]{2,1,0:T(8,128)S(1)} %get-tuple-element.62), channel_id=1, source_target_pairs={{8,0},{12,4},{16,8},{20,12},{24,16},{28,20},{0,24},{4,28},{9,1},{1... | collective-permute-start | bytes 147464 | tf_op jit(solution)/shard_map/ppermute | solution.py:24
  41.2 0.7 %collective-permute-start.14 = (f32[3,32,128]{2,1,0:T(8,128)S(1)}, f32[3,32,128]{2,1,0:T(8,128)S(1)}, u32[]{:S(2)}, u32[]{:S(2)}) collective-permute-start(f32[3,32,128]{2,1,0:T(8,128)S(1)} %get-tuple-element.61.refs_4_), channel_id=1, source_target_pairs={{12,4},{20,12},{28,20},{4,28},{13,5},{21,13},{29,21},{5,29},{14,6}... | collective-permute-start | bytes 147464 | tf_op jit(solution)/shard_map/ppermute | solution.py:353
  41.9 1.7 %collective-permute-done.13.refs_5_ = f32[3,32,128]{2,1,0:T(8,128)S(1)} collective-permute-done((f32[3,32,128]{2,1,0:T(8,128)S(1)}, f32[3,32,128]{2,1,0:T(8,128)S(1)}, u32[]{:S(2)}, u32[]{:S(2)}) %collective-permute-start.13) | collective-permute-done | bytes 49184 | tf_op jit(solution)/shard_map/ppermute | solution.py:24
  43.6 0.5 %collective-permute-done.12.refs_3_ = bf16[3,3,32,128]{3,2,1,0:T(8,128)(2,1)S(1)} collective-permute-done((bf16[3,3,32,128]{3,2,1,0:T(8,128)(2,1)S(1)}, bf16[3,3,32,128]{3,2,1,0:T(8,128)(2,1)S(1)}, u32[]{:S(2)}, u32[]{:S(2)}) %collective-permute-start.12) | collective-permute-done | bytes 73760 | tf_op jit(solution)/shard_map/ppermute | solution.py:42
  44.0 0.7 %shard_map.44 = f32[3,5,32,128]{3,2,1,0:T(8,128)} custom-call(f32[3,3,32,128]{3,2,1,0:T(8,128)S(1)} %get-tuple-element.53.refs_0_, bf16[3,3,32,128]{3,2,1,0:T(8,128)(2,1)S(1)} %collective-permute-done.10.refs_1_, bf16[3,3,32,128]{3,2,1,0:T(8,128)(2,1)S(1)} %collective-permute-done.11.refs_2_, bf16[3,3,32,128]{3,2,1,0:T(8,128)(2,1)S(1)} %collective-permute-done.12.refs_3_, ...), custom_call_target="tpu_custom_call" | custom-call | tf_op jit(solution)/shard_map/pallas_call | solution.py:58
  (12 shorter events, 0.0 us)
Async XLA Ops:
  0.0 4.7 %copy-start.1 = (f32[4,8,128]{2,1,0:T(8,128)S(1)}, f32[4,8,128]{2,1,0:T(8,128)}, u32[]{:S(2)}) copy-start(f32[4,8,128]{2,1,0:T(8,128)} %refs_4_.1) | copy-start | bytes 49156
  0.0 4.7 %copy-start = (f32[3,4,8,128]{3,2,1,0:T(8,128)S(1)}, f32[3,4,8,128]{3,2,1,0:T(8,128)}, u32[]{:S(2)}) copy-start(f32[3,4,8,128]{3,2,1,0:T(8,128)} %refs_5_.1) | copy-start | bytes 147460
  0.0 28.4 %collective-permute-start.5 = (bf16[128,4,8,128]{3,2,1,0:T(8,128)(2,1)}, bf16[128,4,8,128]{3,2,1,0:T(8,128)(2,1)S(1)}, u32[]{:S(2)}, u32[]{:S(2)}) collective-permute-start(bf16[128,4,8,128]{3,2,1,0:T(8,128)(2,1)} %param.3), channel_id=1, source_target_pairs={{24,0},{28,4},{0,8},{4,12},{8,16},{12,20},{16,24},{20,28},{25,1},{... | collective-permute-start | bytes 3145736 | tf_op jit(solution)/shard_map/ppermute | solution.py:24
  4.9 9.2 %collective-permute-start = (bf16[128,1280]{1,0:T(8,128)(2,1)S(1)}, bf16[128,1280]{1,0:T(8,128)(2,1)S(1)}, u32[]{:S(2)}, u32[]{:S(2)}) collective-permute-start(bf16[128,1280]{1,0:T(8,128)(2,1)S(1)} %get-tuple-element.34), channel_id=1, source_target_pairs={{1,0},{0,1},{3,2},{2,3},{5,4},{4,5},{7,6},{6,7},{9,8},{8,9},{11,10... | collective-permute-start | bytes 983048 | tf_op jit(solution)/shard_map/ppermute | solution.py:24
  6.4 9.9 %collective-permute-start.1 = (bf16[128,1152]{1,0:T(8,128)(2,1)S(1)}, bf16[128,1152]{1,0:T(8,128)(2,1)S(1)}, u32[]{:S(2)}, u32[]{:S(2)}) collective-permute-start(bf16[128,1152]{1,0:T(8,128)(2,1)S(1)} %get-tuple-element.36), channel_id=1, source_target_pairs={{2,0},{0,2},{3,1},{1,3},{6,4},{4,6},{7,5},{5,7},{10,8},{8,10},{11,... | collective-permute-start | bytes 884744 | tf_op jit(solution)/shard_map/ppermute | solution.py:24
  8.0 13.0 %collective-permute-start.2 = (bf16[128,1152]{1,0:T(8,128)(2,1)S(1)}, bf16[128,1152]{1,0:T(8,128)(2,1)S(1)}, u32[]{:S(2)}, u32[]{:S(2)}) collective-permute-start(bf16[128,1152]{1,0:T(8,128)(2,1)S(1)} %get-tuple-element.37), channel_id=1, source_target_pairs={{2,0},{0,2},{3,1},{1,3},{6,4},{4,6},{7,5},{5,7},{10,8},{8,10},{11,... | collective-permute-start | bytes 884744 | tf_op jit(solution)/shard_map/ppermute | solution.py:24
  21.0 8.0 %collective-permute-start.3 = (bf16[384,2048]{1,0:T(8,128)(2,1)S(1)}, bf16[384,2048]{1,0:T(8,128)(2,1)S(1)}, u32[]{:S(2)}, u32[]{:S(2)}) collective-permute-start(bf16[384,2048]{1,0:T(8,128)(2,1)S(1)} %get-tuple-element.35.refs_0_), channel_id=1, source_target_pairs={{0,4},{4,0},{8,12},{12,8},{16,20},{20,16},{24,28},{28,24},{1,5},{5... | collective-permute-start | bytes 4718600 | tf_op jit(solution)/shard_map/ppermute | solution.py:316
  22.9 6.1 %collective-permute-start.4 = (bf16[384,2048]{1,0:T(8,128)(2,1)S(1)}, bf16[384,2048]{1,0:T(8,128)(2,1)S(1)}, u32[]{:S(2)}, u32[]{:S(2)}) collective-permute-start(bf16[384,2048]{1,0:T(8,128)(2,1)S(1)} %get-tuple-element.41.refs_1_), channel_id=1, source_target_pairs={{0,4},{4,0},{8,12},{12,8},{16,20},{20,16},{24,28},{28,24},{1,5},{5... | collective-permute-start | bytes 4718600 | tf_op jit(solution)/shard_map/ppermute | solution.py:316
  28.9 5.8 %collective-permute-start.9 = (bf16[128,4096]{1,0:T(8,128)(2,1)S(1)}, bf16[128,4096]{1,0:T(8,128)(2,1)S(1)}, u32[]{:S(2)}, u32[]{:S(2)}) collective-permute-start(bf16[128,4096]{1,0:T(8,128)(2,1)S(1)} %bitcast.15), channel_id=1, source_target_pairs={{0,4},{4,0},{8,12},{12,8},{16,20},{20,16},{24,28},{28,24},{1,5},{5... | collective-permute-start | bytes 3145736 | tf_op jit(solution)/shard_map/ppermute | solution.py:329
  31.1 7.7 %collective-permute-start.6 = (bf16[2,3,32,128]{3,2,1,0:T(8,128)(2,1)S(1)}, bf16[2,3,32,128]{3,2,1,0:T(8,128)(2,1)S(1)}, u32[]{:S(2)}, u32[]{:S(2)}) collective-permute-start(bf16[2,3,32,128]{3,2,1,0:T(8,128)(2,1)S(1)} %get-tuple-element.46), channel_id=1, source_target_pairs={{0,1},{1,0},{2,3},{3,2},{4,5},{5,4},{6,7},{7,6},{8,9},{9,8},{10,11... | collective-permute-start | bytes 147464 | tf_op jit(solution)/shard_map/ppermute | solution.py:42
  32.7 6.6 %collective-permute-start.7 = (bf16[2,3,32,128]{3,2,1,0:T(8,128)(2,1)S(1)}, bf16[2,3,32,128]{3,2,1,0:T(8,128)(2,1)S(1)}, u32[]{:S(2)}, u32[]{:S(2)}) collective-permute-start(bf16[2,3,32,128]{3,2,1,0:T(8,128)(2,1)S(1)} %get-tuple-element.47), channel_id=1, source_target_pairs={{0,2},{1,3},{2,0},{3,1},{4,6},{5,7},{6,4},{7,5},{8,10},{9,11},{10,... | collective-permute-start | bytes 147464 | tf_op jit(solution)/shard_map/ppermute | solution.py:42
  34.2 5.2 %collective-permute-start.8 = (bf16[2,3,32,128]{3,2,1,0:T(8,128)(2,1)S(1)}, bf16[2,3,32,128]{3,2,1,0:T(8,128)(2,1)S(1)}, u32[]{:S(2)}, u32[]{:S(2)}) collective-permute-start(bf16[2,3,32,128]{3,2,1,0:T(8,128)(2,1)S(1)} %get-tuple-element.48), channel_id=1, source_target_pairs={{0,3},{1,2},{2,1},{3,0},{4,7},{5,6},{6,5},{7,4},{8,11},{9,10},{10,... | collective-permute-start | bytes 147464 | tf_op jit(solution)/shard_map/ppermute | solution.py:42
  35.7 7.9 %collective-permute-start.10 = (bf16[3,3,32,128]{3,2,1,0:T(8,128)(2,1)S(1)}, bf16[3,3,32,128]{3,2,1,0:T(8,128)(2,1)S(1)}, u32[]{:S(2)}, u32[]{:S(2)}) collective-permute-start(bf16[3,3,32,128]{3,2,1,0:T(8,128)(2,1)S(1)} %get-tuple-element.54), channel_id=1, source_target_pairs={{0,1},{1,0},{2,3},{3,2},{4,5},{5,4},{6,7},{7,6},{8,9},{9,8},{10,11... | collective-permute-start | bytes 221192 | tf_op jit(solution)/shard_map/ppermute | solution.py:42
  37.3 6.3 %collective-permute-start.11 = (bf16[3,3,32,128]{3,2,1,0:T(8,128)(2,1)S(1)}, bf16[3,3,32,128]{3,2,1,0:T(8,128)(2,1)S(1)}, u32[]{:S(2)}, u32[]{:S(2)}) collective-permute-start(bf16[3,3,32,128]{3,2,1,0:T(8,128)(2,1)S(1)} %get-tuple-element.55), channel_id=1, source_target_pairs={{0,2},{1,3},{2,0},{3,1},{4,6},{5,7},{6,4},{7,5},{8,10},{9,11},{10,... | collective-permute-start | bytes 221192 | tf_op jit(solution)/shard_map/ppermute | solution.py:42
  38.8 5.3 %collective-permute-start.12 = (bf16[3,3,32,128]{3,2,1,0:T(8,128)(2,1)S(1)}, bf16[3,3,32,128]{3,2,1,0:T(8,128)(2,1)S(1)}, u32[]{:S(2)}, u32[]{:S(2)}) collective-permute-start(bf16[3,3,32,128]{3,2,1,0:T(8,128)(2,1)S(1)} %get-tuple-element.56), channel_id=1, source_target_pairs={{0,3},{1,2},{2,1},{3,0},{4,7},{5,6},{6,5},{7,4},{8,11},{9,10},{10,... | collective-permute-start | bytes 221192 | tf_op jit(solution)/shard_map/ppermute | solution.py:42
  39.4 4.1 %collective-permute-start.13 = (f32[3,32,128]{2,1,0:T(8,128)S(1)}, f32[3,32,128]{2,1,0:T(8,128)S(1)}, u32[]{:S(2)}, u32[]{:S(2)}) collective-permute-start(f32[3,32,128]{2,1,0:T(8,128)S(1)} %get-tuple-element.62), channel_id=1, source_target_pairs={{8,0},{12,4},{16,8},{20,12},{24,16},{28,20},{0,24},{4,28},{9,1},{1... | collective-permute-start | bytes 147464 | tf_op jit(solution)/shard_map/ppermute | solution.py:24
  41.2 2.3 %collective-permute-start.14 = (f32[3,32,128]{2,1,0:T(8,128)S(1)}, f32[3,32,128]{2,1,0:T(8,128)S(1)}, u32[]{:S(2)}, u32[]{:S(2)}) collective-permute-start(f32[3,32,128]{2,1,0:T(8,128)S(1)} %get-tuple-element.61.refs_4_), channel_id=1, source_target_pairs={{12,4},{20,12},{28,20},{4,28},{13,5},{21,13},{29,21},{5,29},{14,6}... | collective-permute-start | bytes 147464 | tf_op jit(solution)/shard_map/ppermute | solution.py:353

commit v13 on v12

--- a/solution.py
+++ b/solution.py
@@ -347,10 +347,7 @@
     first, kept = lax.optimization_barrier((first, kept))
     small = shape_of((3, rows, states), F32)
     there, ours = call(add, [small, small], [kept_there, *first])
-    count = lax.axis_size("blk")
-    back_two = shift(there, "blk", 2)
-    odd = [((i + 2) % count, i) for i in range(1, count, 2)]
-    back_one = lax.ppermute(ours, "blk", odd)
+    back_two, back_one = shift(there, "blk", 2), shift(ours, "blk", 2)
     (out,) = call(
         assemble,
         [shape_of((3, 5, rows, states), F32)],

time: 44.9 us -> 46.2 us (1.029)
  waiting for transfers between devices: 16.8 us -> 18.3 us
    ppermute x5 -> x6, waiting for transfers between devices: 16.2 us -> 18.2 us  [shift(): lax.ppermute(block, axis, [((i + distance) % count, i) for i in range(cou...]
    ppermute x1 -> x0, starting transfers between devices: 0.65 us -> none  [on_device(): back_one = lax.ppermute(ours, 'blk', odd)]
    ppermute x6, waiting for transfers between devices: 0.6 us -> 0.13 us  [exchange(): got.append(lax.ppermute(piece, ('dx', 'dy'), route))]
    ppermute x5 -> x6, starting transfers between devices: 8.4 us -> 8.85 us  [shift(): lax.ppermute(block, axis, [((i + distance) % count, i) for i in range(cou...]
where the time goes in v13:
time: 46.2 us; the launch traced here: 46.1 us
  waiting for transfers between devices  18.3 us (40%)
  starting transfers between devices  16.6 us (36%)
  Pallas kernels  8.87 us (19%)
  local copies, waits for them, and re-layouts  2.16 us (5%)
    ppermute x6, waiting for transfers between devices, shift(): lax.ppermute(block, axis, [((i + distance) % count, i) for i in range(cou...  18.2 us
    pallas_call x8, Pallas kernels, call(): return list(run(*operands))  8.87 us
    ppermute x6, starting transfers between devices, shift(): lax.ppermute(block, axis, [((i + distance) % count, i) for i in range(cou...  8.85 us
    ppermute x6, starting transfers between devices, exchange(): got.append(lax.ppermute(piece, ('dx', 'dy'), route))  7.11 us
    unnamed x6, local copies, waits for them, and re-layouts  2.16 us
  transfers between devices with their start and end apart: 15, of which 7 were waited for; matrix products, arithmetic and copies ran while one was open for 5% of the time, Pallas kernels for 18%

profile of v13, /device:TPU:0, one launch (start us, length us, event | category | flops | bytes accessed | tf_op | source)
XLA Modules:
  0.0 46.1 jit_solution(6970132205447508993)
XLA Ops:
  0.0 3.0 %collective-permute-start.5 = (bf16[128,4,8,128]{3,2,1,0:T(8,128)(2,1)}, bf16[128,4,8,128]{3,2,1,0:T(8,128)(2,1)S(1)}, u32[]{:S(2)}, u32[]{:S(2)}) collective-permute-start(bf16[128,4,8,128]{3,2,1,0:T(8,128)(2,1)} %param.3), channel_id=1, source_target_pairs={{24,0},{28,4},{0,8},{4,12},{8,16},{12,20},{16,24},{20,28},{25,1},{... | collective-permute-start | bytes 3145736 | tf_op jit(solution)/shard_map/ppermute | solution.py:24
  3.0 1.7 %copy.9 = bf16[16,8,32,128]{3,1,2,0:T(8,128)(2,1)S(1)} copy(bf16[16,8,32,128]{3,2,1,0:T(8,128)(2,1)} %bitcast.18) | data formatting | bytes 2097152
  4.8 0.1 shard_map.37
  4.9 1.6 %collective-permute-start = (bf16[128,1280]{1,0:T(8,128)(2,1)S(1)}, bf16[128,1280]{1,0:T(8,128)(2,1)S(1)}, u32[]{:S(2)}, u32[]{:S(2)}) collective-permute-start(bf16[128,1280]{1,0:T(8,128)(2,1)S(1)} %get-tuple-element.34), channel_id=1, source_target_pairs={{1,0},{0,1},{3,2},{2,3},{5,4},{4,5},{7,6},{6,7},{9,8},{8,9},{11,10... | collective-permute-start | bytes 983048 | tf_op jit(solution)/shard_map/ppermute | solution.py:24
  6.4 1.5 %collective-permute-start.1 = (bf16[128,1152]{1,0:T(8,128)(2,1)S(1)}, bf16[128,1152]{1,0:T(8,128)(2,1)S(1)}, u32[]{:S(2)}, u32[]{:S(2)}) collective-permute-start(bf16[128,1152]{1,0:T(8,128)(2,1)S(1)} %get-tuple-element.36), channel_id=1, source_target_pairs={{2,0},{0,2},{3,1},{1,3},{6,4},{4,6},{7,5},{5,7},{10,8},{8,10},{11,... | collective-permute-start | bytes 884744 | tf_op jit(solution)/shard_map/ppermute | solution.py:24
  8.0 0.5 %collective-permute-start.2 = (bf16[128,1152]{1,0:T(8,128)(2,1)S(1)}, bf16[128,1152]{1,0:T(8,128)(2,1)S(1)}, u32[]{:S(2)}, u32[]{:S(2)}) collective-permute-start(bf16[128,1152]{1,0:T(8,128)(2,1)S(1)} %get-tuple-element.37), channel_id=1, source_target_pairs={{2,0},{0,2},{3,1},{1,3},{6,4},{4,6},{7,5},{5,7},{10,8},{8,10},{11,... | collective-permute-start | bytes 884744 | tf_op jit(solution)/shard_map/ppermute | solution.py:24
  8.5 5.7 %collective-permute-done.refs_1_.refs_3_ = bf16[128,1280]{1,0:T(8,128)(2,1)S(1)} collective-permute-done((bf16[128,1280]{1,0:T(8,128)(2,1)S(1)}, bf16[128,1280]{1,0:T(8,128)(2,1)S(1)}, u32[]{:S(2)}, u32[]{:S(2)}) %collective-permute-start) | collective-permute-done | bytes 327712 | tf_op jit(solution)/shard_map/ppermute | solution.py:24
  14.1 1.9 %shard_map.38 = (bf16[384,2048]{1,0:T(8,128)(2,1)S(1)}, bf16[384,2048]{1,0:T(8,128)(2,1)S(1)}) custom-call(bf16[128,4096]{1,0:T(8,128)(2,1)S(1)} %bitcast.11, bf16[128,1280]{1,0:T(8,128)(2,1)S(1)} %collective-permute-done.refs_1_.refs_3_, f32[4,8,128]{2,1,0:T(8,128)S(1)} %copy-done.1, f32[3,4,8,128]{3,2,1,0:T(8,128)S(1)} %copy-done), custom_call_target="tpu_custom_call" | custom-call | tf_op jit(solution)/shard_map/pallas_call | solution.py:58
  16.0 0.4 collective-permute-done.1.refs_1_
  16.4 4.6 %collective-permute-done.2.refs_2_ = bf16[128,1152]{1,0:T(8,128)(2,1)S(1)} collective-permute-done((bf16[128,1152]{1,0:T(8,128)(2,1)S(1)}, bf16[128,1152]{1,0:T(8,128)(2,1)S(1)}, u32[]{:S(2)}, u32[]{:S(2)}) %collective-permute-start.2) | collective-permute-done | bytes 294944 | tf_op jit(solution)/shard_map/ppermute | solution.py:24
  21.0 0.0 collective-permute-start.3
  21.0 1.9 %shard_map.39 = (bf16[384,2048]{1,0:T(8,128)(2,1)S(1)}, bf16[384,2048]{1,0:T(8,128)(2,1)S(1)}) custom-call(bf16[128,4096]{1,0:T(8,128)(2,1)S(1)} %bitcast.12, bf16[128,1152]{1,0:T(8,128)(2,1)S(1)} %collective-permute-done.1.refs_1_, bf16[128,1152]{1,0:T(8,128)(2,1)S(1)} %collective-permute-done.2.refs_2_, ...), custom_call_target="tpu_custom_call" | custom-call | tf_op jit(solution)/shard_map/pallas_call | solution.py:58
  22.9 0.6 %collective-permute-start.4 = (bf16[384,2048]{1,0:T(8,128)(2,1)S(1)}, bf16[384,2048]{1,0:T(8,128)(2,1)S(1)}, u32[]{:S(2)}, u32[]{:S(2)}) collective-permute-start(bf16[384,2048]{1,0:T(8,128)(2,1)S(1)} %get-tuple-element.41.refs_1_), channel_id=1, source_target_pairs={{0,4},{4,0},{8,12},{12,8},{16,20},{20,16},{24,28},{28,24},{1,5},{5... | collective-permute-start | bytes 4718600 | tf_op jit(solution)/shard_map/ppermute | solution.py:316
  23.5 1.0 %shard_map.40.refs_6_.refs_4_ = f32[384,128]{1,0:T(8,128)S(1)} custom-call(bf16[384,2048]{1,0:T(8,128)(2,1)S(1)} %get-tuple-element.42.refs_0_, bf16[384,2048]{1,0:T(8,128)(2,1)S(1)} %get-tuple-element.43.refs_1_, bf16[128,4096]{1,0:T(8,128)(2,1)S(1)} %bitcast.13), custom_call_target="tpu_custom_call" | custom-call | tf_op jit(solution)/shard_map/pallas_call | solution.py:58
  24.4 4.0 %collective-permute-done.5 = bf16[128,4,8,128]{3,2,1,0:T(8,128)(2,1)S(1)} collective-permute-done((bf16[128,4,8,128]{3,2,1,0:T(8,128)(2,1)}, bf16[128,4,8,128]{3,2,1,0:T(8,128)(2,1)S(1)}, u32[]{:S(2)}, u32[]{:S(2)}) %collective-permute-start.5) | collective-permute-done | bytes 1048608 | tf_op jit(solution)/shard_map/ppermute | solution.py:24
  28.4 0.5 copy.8
  28.9 0.1 collective-permute-start.9
  29.0 0.0 collective-permute-done.3.refs_2_
  29.0 2.1 %shard_map.41 = (f32[128,384]{1,0:T(8,128)S(1)}, f32[2,3,32,128]{3,2,1,0:T(8,128)S(1)}, bf16[2,3,32,128]{3,2,1,0:T(8,128)(2,1)S(1)}, bf16[2,3,32,128]{3,2,1,0:T(8,128)(2,1)S(1)}, bf16[2,3,32,128]{3,2,1,0:T(8,128)(2,1)S(1)}) custom-call(bf16[384,2048]{1,0:T(8,128)(2,1)S(1)} %get-tuple-element.35.refs_0_, bf16[384,2048]{1,0:T(8,128)(2,1)S(1)} %get-tuple-element.41.refs_1_, ...), custom_call_target="tpu_custom_call" | custom-call | bytes 3000000 | tf_op jit(solution)/shard_map/pallas_call | solution.py:58
  31.1 1.6 %collective-permute-start.6 = (bf16[2,3,32,128]{3,2,1,0:T(8,128)(2,1)S(1)}, bf16[2,3,32,128]{3,2,1,0:T(8,128)(2,1)S(1)}, u32[]{:S(2)}, u32[]{:S(2)}) collective-permute-start(bf16[2,3,32,128]{3,2,1,0:T(8,128)(2,1)S(1)} %get-tuple-element.46), channel_id=1, source_target_pairs={{0,1},{1,0},{2,3},{3,2},{4,5},{5,4},{6,7},{7,6},{8,9},{9,8},{10,11... | collective-permute-start | bytes 147464 | tf_op jit(solution)/shard_map/ppermute | solution.py:42
  32.7 1.5 %collective-permute-start.7 = (bf16[2,3,32,128]{3,2,1,0:T(8,128)(2,1)S(1)}, bf16[2,3,32,128]{3,2,1,0:T(8,128)(2,1)S(1)}, u32[]{:S(2)}, u32[]{:S(2)}) collective-permute-start(bf16[2,3,32,128]{3,2,1,0:T(8,128)(2,1)S(1)} %get-tuple-element.47), channel_id=1, source_target_pairs={{0,2},{1,3},{2,0},{3,1},{4,6},{5,7},{6,4},{7,5},{8,10},{9,11},{10,... | collective-permute-start | bytes 147464 | tf_op jit(solution)/shard_map/ppermute | solution.py:42
  34.2 0.5 %collective-permute-start.8 = (bf16[2,3,32,128]{3,2,1,0:T(8,128)(2,1)S(1)}, bf16[2,3,32,128]{3,2,1,0:T(8,128)(2,1)S(1)}, u32[]{:S(2)}, u32[]{:S(2)}) collective-permute-start(bf16[2,3,32,128]{3,2,1,0:T(8,128)(2,1)S(1)} %get-tuple-element.48), channel_id=1, source_target_pairs={{0,3},{1,2},{2,1},{3,0},{4,7},{5,6},{6,5},{7,4},{8,11},{9,10},{10,... | collective-permute-start | bytes 147464 | tf_op jit(solution)/shard_map/ppermute | solution.py:42
  34.7 1.0 %shard_map.42 = (f32[3,3,32,128]{3,2,1,0:T(8,128)S(1)}, bf16[3,3,32,128]{3,2,1,0:T(8,128)(2,1)S(1)}, bf16[3,3,32,128]{3,2,1,0:T(8,128)(2,1)S(1)}, bf16[3,3,32,128]{3,2,1,0:T(8,128)(2,1)S(1)}) custom-call(bf16[384,2048]{1,0:T(8,128)(2,1)S(1)} %get-tuple-element.42.refs_0_, bf16[384,2048]{1,0:T(8,128)(2,1)S(1)} %get-tuple-element.43.refs_1_, ...), custom_call_target="tpu_custom_call" | custom-call | bytes 3000000 | tf_op jit(solution)/shard_map/pallas_call | solution.py:58
  35.7 1.6 %collective-permute-start.10 = (bf16[3,3,32,128]{3,2,1,0:T(8,128)(2,1)S(1)}, bf16[3,3,32,128]{3,2,1,0:T(8,128)(2,1)S(1)}, u32[]{:S(2)}, u32[]{:S(2)}) collective-permute-start(bf16[3,3,32,128]{3,2,1,0:T(8,128)(2,1)S(1)} %get-tuple-element.54), channel_id=1, source_target_pairs={{0,1},{1,0},{2,3},{3,2},{4,5},{5,4},{6,7},{7,6},{8,9},{9,8},{10,11... | collective-permute-start | bytes 221192 | tf_op jit(solution)/shard_map/ppermute | solution.py:42
  37.3 1.5 %collective-permute-start.11 = (bf16[3,3,32,128]{3,2,1,0:T(8,128)(2,1)S(1)}, bf16[3,3,32,128]{3,2,1,0:T(8,128)(2,1)S(1)}, u32[]{:S(2)}, u32[]{:S(2)}) collective-permute-start(bf16[3,3,32,128]{3,2,1,0:T(8,128)(2,1)S(1)} %get-tuple-element.55), channel_id=1, source_target_pairs={{0,2},{1,3},{2,0},{3,1},{4,6},{5,7},{6,4},{7,5},{8,10},{9,11},{10,... | collective-permute-start | bytes 221192 | tf_op jit(solution)/shard_map/ppermute | solution.py:42
  38.8 0.5 %collective-permute-start.12 = (bf16[3,3,32,128]{3,2,1,0:T(8,128)(2,1)S(1)}, bf16[3,3,32,128]{3,2,1,0:T(8,128)(2,1)S(1)}, u32[]{:S(2)}, u32[]{:S(2)}) collective-permute-start(bf16[3,3,32,128]{3,2,1,0:T(8,128)(2,1)S(1)} %get-tuple-element.56), channel_id=1, source_target_pairs={{0,3},{1,2},{2,1},{3,0},{4,7},{5,6},{6,5},{7,4},{8,11},{9,10},{10,... | collective-permute-start | bytes 221192 | tf_op jit(solution)/shard_map/ppermute | solution.py:42
  39.3 0.1 collective-permute-done.8.refs_3_
  39.4 1.8 %collective-permute-start.13 = (f32[3,32,128]{2,1,0:T(8,128)S(1)}, f32[3,32,128]{2,1,0:T(8,128)S(1)}, u32[]{:S(2)}, u32[]{:S(2)}) collective-permute-start(f32[3,32,128]{2,1,0:T(8,128)S(1)} %get-tuple-element.62), channel_id=1, source_target_pairs={{8,0},{12,4},{16,8},{20,12},{24,16},{28,20},{0,24},{4,28},{9,1},{1... | collective-permute-start | bytes 147464 | tf_op jit(solution)/shard_map/ppermute | solution.py:24
  41.2 0.4 collective-permute-start.14
  41.7 1.9 %collective-permute-done.13.refs_5_ = f32[3,32,128]{2,1,0:T(8,128)S(1)} collective-permute-done((f32[3,32,128]{2,1,0:T(8,128)S(1)}, f32[3,32,128]{2,1,0:T(8,128)S(1)}, u32[]{:S(2)}, u32[]{:S(2)}) %collective-permute-start.13) | collective-permute-done | bytes 49184 | tf_op jit(solution)/shard_map/ppermute | solution.py:24
  43.6 1.7 %collective-permute-done.14.refs_6_ = f32[3,32,128]{2,1,0:T(8,128)S(1)} collective-permute-done((f32[3,32,128]{2,1,0:T(8,128)S(1)}, f32[3,32,128]{2,1,0:T(8,128)S(1)}, u32[]{:S(2)}, u32[]{:S(2)}) %collective-permute-start.14) | collective-permute-done | bytes 49184 | tf_op jit(solution)/shard_map/ppermute | solution.py:24
  45.3 0.7 %shard_map.44 = f32[3,5,32,128]{3,2,1,0:T(8,128)} custom-call(f32[3,3,32,128]{3,2,1,0:T(8,128)S(1)} %get-tuple-element.53.refs_0_, bf16[3,3,32,128]{3,2,1,0:T(8,128)(2,1)S(1)} %collective-permute-done.10.refs_1_, bf16[3,3,32,128]{3,2,1,0:T(8,128)(2,1)S(1)} %collective-permute-done.11.refs_2_, bf16[3,3,32,128]{3,2,1,0:T(8,128)(2,1)S(1)} %collective-permute-done.12.refs_3_, ...), custom_call_target="tpu_custom_call" | custom-call | tf_op jit(solution)/shard_map/pallas_call | solution.py:58
  (12 shorter events, 0.0 us)
Async XLA Ops:
  0.0 4.7 %copy-start.1 = (f32[4,8,128]{2,1,0:T(8,128)S(1)}, f32[4,8,128]{2,1,0:T(8,128)}, u32[]{:S(2)}) copy-start(f32[4,8,128]{2,1,0:T(8,128)} %refs_4_.1) | copy-start | bytes 49156
  0.0 4.7 %copy-start = (f32[3,4,8,128]{3,2,1,0:T(8,128)S(1)}, f32[3,4,8,128]{3,2,1,0:T(8,128)}, u32[]{:S(2)}) copy-start(f32[3,4,8,128]{3,2,1,0:T(8,128)} %refs_5_.1) | copy-start | bytes 147460
  0.0 28.4 %collective-permute-start.5 = (bf16[128,4,8,128]{3,2,1,0:T(8,128)(2,1)}, bf16[128,4,8,128]{3,2,1,0:T(8,128)(2,1)S(1)}, u32[]{:S(2)}, u32[]{:S(2)}) collective-permute-start(bf16[128,4,8,128]{3,2,1,0:T(8,128)(2,1)} %param.3), channel_id=1, source_target_pairs={{24,0},{28,4},{0,8},{4,12},{8,16},{12,20},{16,24},{20,28},{25,1},{... | collective-permute-start | bytes 3145736 | tf_op jit(solution)/shard_map/ppermute | solution.py:24
  4.9 9.2 %collective-permute-start = (bf16[128,1280]{1,0:T(8,128)(2,1)S(1)}, bf16[128,1280]{1,0:T(8,128)(2,1)S(1)}, u32[]{:S(2)}, u32[]{:S(2)}) collective-permute-start(bf16[128,1280]{1,0:T(8,128)(2,1)S(1)} %get-tuple-element.34), channel_id=1, source_target_pairs={{1,0},{0,1},{3,2},{2,3},{5,4},{4,5},{7,6},{6,7},{9,8},{8,9},{11,10... | collective-permute-start | bytes 983048 | tf_op jit(solution)/shard_map/ppermute | solution.py:24
  6.4 9.9 %collective-permute-start.1 = (bf16[128,1152]{1,0:T(8,128)(2,1)S(1)}, bf16[128,1152]{1,0:T(8,128)(2,1)S(1)}, u32[]{:S(2)}, u32[]{:S(2)}) collective-permute-start(bf16[128,1152]{1,0:T(8,128)(2,1)S(1)} %get-tuple-element.36), channel_id=1, source_target_pairs={{2,0},{0,2},{3,1},{1,3},{6,4},{4,6},{7,5},{5,7},{10,8},{8,10},{11,... | collective-permute-start | bytes 884744 | tf_op jit(solution)/shard_map/ppermute | solution.py:24
  8.0 13.0 %collective-permute-start.2 = (bf16[128,1152]{1,0:T(8,128)(2,1)S(1)}, bf16[128,1152]{1,0:T(8,128)(2,1)S(1)}, u32[]{:S(2)}, u32[]{:S(2)}) collective-permute-start(bf16[128,1152]{1,0:T(8,128)(2,1)S(1)} %get-tuple-element.37), channel_id=1, source_target_pairs={{2,0},{0,2},{3,1},{1,3},{6,4},{4,6},{7,5},{5,7},{10,8},{8,10},{11,... | collective-permute-start | bytes 884744 | tf_op jit(solution)/shard_map/ppermute | solution.py:24
  21.0 8.0 %collective-permute-start.3 = (bf16[384,2048]{1,0:T(8,128)(2,1)S(1)}, bf16[384,2048]{1,0:T(8,128)(2,1)S(1)}, u32[]{:S(2)}, u32[]{:S(2)}) collective-permute-start(bf16[384,2048]{1,0:T(8,128)(2,1)S(1)} %get-tuple-element.35.refs_0_), channel_id=1, source_target_pairs={{0,4},{4,0},{8,12},{12,8},{16,20},{20,16},{24,28},{28,24},{1,5},{5... | collective-permute-start | bytes 4718600 | tf_op jit(solution)/shard_map/ppermute | solution.py:316
  22.9 6.1 %collective-permute-start.4 = (bf16[384,2048]{1,0:T(8,128)(2,1)S(1)}, bf16[384,2048]{1,0:T(8,128)(2,1)S(1)}, u32[]{:S(2)}, u32[]{:S(2)}) collective-permute-start(bf16[384,2048]{1,0:T(8,128)(2,1)S(1)} %get-tuple-element.41.refs_1_), channel_id=1, source_target_pairs={{0,4},{4,0},{8,12},{12,8},{16,20},{20,16},{24,28},{28,24},{1,5},{5... | collective-permute-start | bytes 4718600 | tf_op jit(solution)/shard_map/ppermute | solution.py:316
  28.9 5.8 %collective-permute-start.9 = (bf16[128,4096]{1,0:T(8,128)(2,1)S(1)}, bf16[128,4096]{1,0:T(8,128)(2,1)S(1)}, u32[]{:S(2)}, u32[]{:S(2)}) collective-permute-start(bf16[128,4096]{1,0:T(8,128)(2,1)S(1)} %bitcast.15), channel_id=1, source_target_pairs={{0,4},{4,0},{8,12},{12,8},{16,20},{20,16},{24,28},{28,24},{1,5},{5... | collective-permute-start | bytes 3145736 | tf_op jit(solution)/shard_map/ppermute | solution.py:329
  31.1 7.7 %collective-permute-start.6 = (bf16[2,3,32,128]{3,2,1,0:T(8,128)(2,1)S(1)}, bf16[2,3,32,128]{3,2,1,0:T(8,128)(2,1)S(1)}, u32[]{:S(2)}, u32[]{:S(2)}) collective-permute-start(bf16[2,3,32,128]{3,2,1,0:T(8,128)(2,1)S(1)} %get-tuple-element.46), channel_id=1, source_target_pairs={{0,1},{1,0},{2,3},{3,2},{4,5},{5,4},{6,7},{7,6},{8,9},{9,8},{10,11... | collective-permute-start | bytes 147464 | tf_op jit(solution)/shard_map/ppermute | solution.py:42
  32.7 6.6 %collective-permute-start.7 = (bf16[2,3,32,128]{3,2,1,0:T(8,128)(2,1)S(1)}, bf16[2,3,32,128]{3,2,1,0:T(8,128)(2,1)S(1)}, u32[]{:S(2)}, u32[]{:S(2)}) collective-permute-start(bf16[2,3,32,128]{3,2,1,0:T(8,128)(2,1)S(1)} %get-tuple-element.47), channel_id=1, source_target_pairs={{0,2},{1,3},{2,0},{3,1},{4,6},{5,7},{6,4},{7,5},{8,10},{9,11},{10,... | collective-permute-start | bytes 147464 | tf_op jit(solution)/shard_map/ppermute | solution.py:42
  34.2 5.2 %collective-permute-start.8 = (bf16[2,3,32,128]{3,2,1,0:T(8,128)(2,1)S(1)}, bf16[2,3,32,128]{3,2,1,0:T(8,128)(2,1)S(1)}, u32[]{:S(2)}, u32[]{:S(2)}) collective-permute-start(bf16[2,3,32,128]{3,2,1,0:T(8,128)(2,1)S(1)} %get-tuple-element.48), channel_id=1, source_target_pairs={{0,3},{1,2},{2,1},{3,0},{4,7},{5,6},{6,5},{7,4},{8,11},{9,10},{10,... | collective-permute-start | bytes 147464 | tf_op jit(solution)/shard_map/ppermute | solution.py:42
  35.7 9.6 %collective-permute-start.10 = (bf16[3,3,32,128]{3,2,1,0:T(8,128)(2,1)S(1)}, bf16[3,3,32,128]{3,2,1,0:T(8,128)(2,1)S(1)}, u32[]{:S(2)}, u32[]{:S(2)}) collective-permute-start(bf16[3,3,32,128]{3,2,1,0:T(8,128)(2,1)S(1)} %get-tuple-element.54), channel_id=1, source_target_pairs={{0,1},{1,0},{2,3},{3,2},{4,5},{5,4},{6,7},{7,6},{8,9},{9,8},{10,11... | collective-permute-start | bytes 221192 | tf_op jit(solution)/shard_map/ppermute | solution.py:42
  37.3 8.0 %collective-permute-start.11 = (bf16[3,3,32,128]{3,2,1,0:T(8,128)(2,1)S(1)}, bf16[3,3,32,128]{3,2,1,0:T(8,128)(2,1)S(1)}, u32[]{:S(2)}, u32[]{:S(2)}) collective-permute-start(bf16[3,3,32,128]{3,2,1,0:T(8,128)(2,1)S(1)} %get-tuple-element.55), channel_id=1, source_target_pairs={{0,2},{1,3},{2,0},{3,1},{4,6},{5,7},{6,4},{7,5},{8,10},{9,11},{10,... | collective-permute-start | bytes 221192 | tf_op jit(solution)/shard_map/ppermute | solution.py:42
  38.8 6.5 %collective-permute-start.12 = (bf16[3,3,32,128]{3,2,1,0:T(8,128)(2,1)S(1)}, bf16[3,3,32,128]{3,2,1,0:T(8,128)(2,1)S(1)}, u32[]{:S(2)}, u32[]{:S(2)}) collective-permute-start(bf16[3,3,32,128]{3,2,1,0:T(8,128)(2,1)S(1)} %get-tuple-element.56), channel_id=1, source_target_pairs={{0,3},{1,2},{2,1},{3,0},{4,7},{5,6},{6,5},{7,4},{8,11},{9,10},{10,... | collective-permute-start | bytes 221192 | tf_op jit(solution)/shard_map/ppermute | solution.py:42
  39.4 4.1 %collective-permute-start.13 = (f32[3,32,128]{2,1,0:T(8,128)S(1)}, f32[3,32,128]{2,1,0:T(8,128)S(1)}, u32[]{:S(2)}, u32[]{:S(2)}) collective-permute-start(f32[3,32,128]{2,1,0:T(8,128)S(1)} %get-tuple-element.62), channel_id=1, source_target_pairs={{8,0},{12,4},{16,8},{20,12},{24,16},{28,20},{0,24},{4,28},{9,1},{1... | collective-permute-start | bytes 147464 | tf_op jit(solution)/shard_map/ppermute | solution.py:24
  41.2 4.1 %collective-permute-start.14 = (f32[3,32,128]{2,1,0:T(8,128)S(1)}, f32[3,32,128]{2,1,0:T(8,128)S(1)}, u32[]{:S(2)}, u32[]{:S(2)}) collective-permute-start(f32[3,32,128]{2,1,0:T(8,128)S(1)} %get-tuple-element.61.refs_4_), channel_id=1, source_target_pairs={{8,0},{12,4},{16,8},{20,12},{24,16},{28,20},{0,24},{4,28},{9,1},{1... | collective-permute-start | bytes 147464 | tf_op jit(solution)/shard_map/ppermute | solution.py:24

commit v14 on v13

--- a/solution.py
+++ b/solution.py
@@ -29,6 +29,13 @@
         return shift(pair, axis, 1)
     tail, head = jnp.split(pair, 2, axis=1)
     return jnp.concatenate([shift(tail, axis, -1), shift(head, axis, 1)], axis=1)
+
+
+def both_sides_in_two(first, second, axis):
+    if lax.axis_size(axis) == 2:
+        return [shift(first, axis, 1), shift(second, axis, 1)]
+    pair = both_sides(jnp.concatenate([first, second], axis=1), axis)
+    return jnp.split(pair, [first.shape[1]], axis=1)
 
 
 def exchange(sends):
@@ -71,19 +78,28 @@
     return high, middle, value - high - middle
 
 
-def edges(psi, coupling, grad, tail, head, hy, tmp, *, shape):
+def parted(parts, at):
+    first = parts[0].shape[1]
+    return (parts[0], at) if at < first else (parts[1], at - first)
+
+
+def edges(psi, coupling, grad, first, second, hy, tmp, *, shape):
     wx, wy, wz = shape
     layer, line = wy * wz, wx * wz
-    for side, (x, y, hx) in enumerate(((wx - 1, wy - 1, tail), (0, 0, head))):
-        to_y = side * (line + wz)
-        hx[:, :layer] = psi[:, x * layer : (x + 1) * layer]
+    for side, (x, y) in enumerate(((wx - 1, wy - 1), (0, 0))):
+        to_x, to_y = side * (layer + wz), side * (line + wz)
+        for i in range(wy):
+            ref, to = parted((first, second), to_x + i * wz)
+            at = x * layer + i * wz
+            ref[:, to : to + wz] = psi[:, at : at + wz]
         for i in range(wx):
             at = i * layer + y * wz
             hy[:, to_y + i * wz : to_y + (i + 1) * wz] = psi[:, at : at + wz]
         for k in range(3):
             for n, third in enumerate(thirds(coupling[x] * grad[k, x])):
                 tmp[(3 * k + n) * wy : (3 * k + n + 1) * wy] = third
-        hx[: tmp.shape[0], layer:] = tmp[...].astype(BF16)
+        ref, to = parted((first, second), to_x + layer)
+        ref[: tmp.shape[0], to : to + wz] = tmp[...].astype(BF16)
         for k in range(3):
             for n, third in enumerate(thirds(coupling[:, y] * grad[k, :, y])):
                 tmp[(3 * k + n) * wx : (3 * k + n + 1) * wx] = third
@@ -108,7 +124,7 @@
 
     for side in range(2):
         if outer:
-            unpack(hx[side], layer, ex.at[side], wy)
+            unpack(*parted(hx, side * (layer + wz) + layer), ex.at[side], wy)
         unpack(hy, side * (line + wz) + line, ey.at[side], wx)
     for k in range(3):
         for x in layers:
@@ -127,7 +143,8 @@
 
         def field(x, y):
             if x < 0 or x >= wx:
-                return hx[int(x >= wx)][r, y * wz : (y + 1) * wz].astype(F32)
+                ref, at = parted(hx, int(x >= wx) * (layer + wz) + y * wz)
+                return ref[r, at : at + wz].astype(F32)
             if y < 0 or y >= wy:
                 at = int(y >= wy) * (line + wz) + x * wz
                 return hy[r, at : at + wz].astype(F32)
@@ -188,11 +205,6 @@
     return lambda cols: jnp.concatenate([panel[:, cols] for panel in panels], axis=0)
 
 
-def own_tiles(*refs, layer, scale):
-    u, (psi, own) = refs[:2], refs[2:]
-    own[...] = product(u, stacked(psi), layer) * scale
-
-
 def cut(outs, slots, plane, states):
     rows = states // math.prod(plane)
     for ref, dest in zip(outs, destinations(*plane)):
@@ -225,27 +237,28 @@
     return lambda *place: jnp.where(core == 0, first(*place), second(*place))
 
 
-def there_tiles(*refs, layer, plane, scale):
-    w, w_mate, (two, psi, own), refs = refs[:2], refs[2:4], refs[4:7], refs[7:]
-    mate, outs, (there, there_mate) = refs[0], refs[1:-2], refs[-2:]
-    states = two.shape[0]
+def near_tiles(*refs, layer, plane, scale):
+    u, panels, outs, (here, here_mate) = refs[:2], refs[2:5], refs[5:-2], refs[-2:]
+    states = panels[0].shape[0]
+    both = product(u, stacked(*panels), layer) * scale
+    here[...], here_mate[...] = both[:, :states], both[:, states:]
+    cut(outs, (tall_rows(here), tall_rows(here_mate)), plane, states)
+
+
+def there_tiles(*refs, layer, scale):
+    w, w_mate, (two, there, there_mate) = refs[:2], refs[2:4], refs[4:]
     there[...] = product(w, stacked(two), layer, True) * scale
-    both = product(w_mate, stacked(two, psi), layer, True) * scale
-    there_mate[...], mate[...] = both[:states], both[states:]
-    slots = (wide_rows(there), either(tall_rows(own), wide_rows(there_mate)))
-    cut(outs, slots, plane, states)
+    there_mate[...] = product(w_mate, stacked(two), layer, True) * scale
 
 
 def here_tiles(*refs, layer, plane, scale):
-    u, (two, one, own, mate), refs = refs[:2], refs[2:6], refs[6:]
+    u, (two, one, there, there_mate), refs = refs[:2], refs[2:6], refs[6:]
     outs, (here_two, here_one) = refs[:-2], refs[-2:]
     states = two.shape[0]
     both = product(u, stacked(two, one), layer) * scale
     here_two[...], here_one[...] = both[:, :states], both[:, states:]
-    slots = (
-        tall_rows(here_two), wide_rows(mate), either(tall_rows(here_one), tall_rows(own))
-    )
-    cut(outs, slots, plane, states)
+    third = either(tall_rows(here_one), wide_rows(there_mate))
+    cut(outs, (tall_rows(here_two), wide_rows(there), third), plane, states)
 
 
 def total_of(group, n, k):
@@ -256,22 +269,25 @@
 
 
 def add(*refs):
-    group, outs = refs[:-2], refs[-2:]
-    for n, out in enumerate(outs):
-        for k in range(3):
-            out[k] = total_of(group, n, k)
+    group, back = refs[:-1], refs[-1]
+    for k in range(3):
+        total = total_of(group, 1, k)
+        back[0, k] = total.astype(BF16)
+        back[1, k] = (total - back[0, k].astype(F32)).astype(BF16)
+        back[2, k] = total_of(group, 2, k).astype(BF16)
 
 
 def assemble(*refs):
-    group, (ours, back_two, back_one, out) = refs[:-4], refs[-4:]
+    size = (len(refs) - 2) // 2
+    early, late, (back, out) = refs[:size], refs[size:-2], refs[-2:]
     core = lax.rem(lax.axis_index("blk"), 2)
     for k in range(3):
-        mate, third = total_of(group, 1, k), total_of(group, 2, k)
-        out[k, 0] = total_of(group, 0, k)
-        out[k, 1] = jnp.where(core == 0, third, mate)
-        out[k, 2] = jnp.where(core == 0, ours[k], third)
-        out[k, 3] = jnp.where(core == 0, mate, back_one[k])
-        out[k, 4] = back_two[k]
+        mate = total_of(early, 1, k)
+        out[k, 0] = total_of(late, 0, k)
+        out[k, 1] = jnp.where(core == 0, total_of(late, 2, k), mate)
+        out[k, 2] = total_of(early, 0, k)
+        out[k, 3] = jnp.where(core == 0, mate, back[2, k].astype(F32))
+        out[k, 4] = back[0, k].astype(F32) + back[1, k].astype(F32)
 
 
 def on_device(orbitals, coupling, pot_grad):
@@ -287,15 +303,17 @@
     swap = [(i, i ^ 1) for i in range(lax.axis_size("blk"))]
     two = shift(orbitals, "blk", -2)
     psi = lax.optimization_barrier(orbitals.reshape(states, cells))
+    mate = [lax.ppermute(half, "blk", swap) for half in jnp.split(psi, 2, axis=0)]
 
     tmp = pltpu.VMEM((-(-9 * max(wx, wy) // 16) * 16, wz), F32)
-    tail, head, hy = call(
+    widths = (layer + wz + layer // 4, layer + wz - layer // 4, 2 * (line + wz))
+    *hx, hy = call(
         functools.partial(edges, shape=shape),
-        [shape_of((states, layer + wz), BF16)] * 2 + [shape_of((states, 2 * (line + wz)), BF16)],
+        [shape_of((states, width), BF16) for width in widths],
         [psi, coupling, pot_grad],
         scratch=[tmp],
     )
-    hx = [shift(tail, "dx", -1), shift(head, "dx", 1)]
+    hx = both_sides_in_two(*hx, "dx")
     hy = both_sides(hy, "dy")
 
     coeffs = pltpu.VMEM((3, wx, wy, wz), F32)
@@ -315,44 +333,30 @@
         w.append(results[1])
         w_mate.append(lax.ppermute(w[-1], "blk", swap))
     tall, wide = shape_of((3 * states, states), F32), shape_of((states, 3 * states), F32)
-    (own,) = call(
-        functools.partial(own_tiles, layer=layer, scale=scale), [tall], [*u, psi]
-    )
-
-    def cut_shapes(slots):
+    given = dict(layer=layer, scale=scale)
+
+    def summed(body, slots, operands):
         shape = (slots, 3, rows, states)
-        return [shape_of(shape, F32)] + [shape_of(shape, BF16)] * (places - 1)
-
-    given = dict(layer=layer, plane=plane, scale=scale)
-    two, own = lax.optimization_barrier((two, own))
+        kept, *sends = call(
+            functools.partial(body, plane=plane, **given),
+            [shape_of(shape, F32)] + [shape_of(shape, BF16)] * (places - 1),
+            operands,
+            scratch=[pltpu.VMEM(tall.shape, F32)] * 2,
+        )
+        return [kept, *exchange(sends)]
+
+    early = summed(near_tiles, 2, [*u, psi, *mate])
+    two, early = lax.optimization_barrier((two, early))
     two = lax.optimization_barrier(two.reshape(states, cells))
     one = lax.ppermute(two, "blk", swap)
-    mate, kept_there, *sends = call(
-        functools.partial(there_tiles, **given),
-        [wide, *cut_shapes(2)],
-        [*w, *w_mate, two, psi, own],
-        scratch=[pltpu.VMEM(wide.shape, F32)] * 2,
-        us=1,
+    there = call(
+        functools.partial(there_tiles, **given), [wide, wide], [*w, *w_mate, two]
     )
-    first = exchange(sends)
-    one, mate = lax.optimization_barrier((one, mate))
-    kept, *sends = call(
-        functools.partial(here_tiles, **given),
-        cut_shapes(3),
-        [*u, two, one, own, mate],
-        scratch=[pltpu.VMEM(tall.shape, F32)] * 2,
-        us=1,
-    )
-    second = exchange(sends)
-    first, kept = lax.optimization_barrier((first, kept))
-    small = shape_of((3, rows, states), F32)
-    there, ours = call(add, [small, small], [kept_there, *first])
-    back_two, back_one = shift(there, "blk", 2), shift(ours, "blk", 2)
-    (out,) = call(
-        assemble,
-        [shape_of((3, 5, rows, states), F32)],
-        [kept, *second, ours, back_two, back_one],
-    )
+    one, there = lax.optimization_barrier((one, there))
+    late = summed(here_tiles, 3, [*u, two, one, *there])
+    (back,) = call(add, [shape_of((3, 3, rows, states), BF16)], late)
+    back = shift(back, "blk", 2)
+    (out,) = call(assemble, [shape_of((3, 5, rows, states), F32)], [*early, *late, back])
     return out
 
 

time: 46.2 us -> 50.6 us (1.095)
  waiting for transfers between devices: 18.3 us -> 22.5 us
    ppermute x6, waiting for transfers between devices: 0.13 us -> 9.35 us  [exchange(): got.append(lax.ppermute(piece, ('dx', 'dy'), route))]
    ppermute x6 -> x5, waiting for transfers between devices: 18.2 us -> 12.4 us  [shift(): lax.ppermute(block, axis, [((i + distance) % count, i) for i in range(cou...]
    ppermute x1, waiting for transfers between devices: 0.01 us -> 0.66 us  [on_device(): one = lax.ppermute(two, 'blk', swap)]
    ppermute x6 -> x5, starting transfers between devices: 8.85 us -> 8.97 us  [shift(): lax.ppermute(block, axis, [((i + distance) % count, i) for i in range(cou...]
  transfers between devices with their start and end apart: 15 -> 16, of which waited for: 7 -> 9; matrix products, arithmetic and copies ran while one was open for 5% -> 4% of each run, Pallas kernels for 18% -> 14%
where the time goes in v14:
time: 50.6 us; the launch traced here: 50.5 us
  waiting for transfers between devices  22.5 us (44%)
  starting transfers between devices  16.9 us (33%)
  Pallas kernels  8.77 us (17%)
  local copies, waits for them, and re-layouts  2.25 us (4%)
    ppermute x5, waiting for transfers between devices, shift(): lax.ppermute(block, axis, [((i + distance) % count, i) for i in range(cou...  12.4 us
    ppermute x6, waiting for transfers between devices, exchange(): got.append(lax.ppermute(piece, ('dx', 'dy'), route))  9.35 us
    ppermute x5, starting transfers between devices, shift(): lax.ppermute(block, axis, [((i + distance) % count, i) for i in range(cou...  8.97 us
    pallas_call x8, Pallas kernels, call(): return list(run(*operands))  8.77 us
    ppermute x6, starting transfers between devices, exchange(): got.append(lax.ppermute(piece, ('dx', 'dy'), route))  7.17 us
    unnamed x6, local copies, waits for them, and re-layouts  2.16 us
  transfers between devices with their start and end apart: 16, of which 9 were waited for; matrix products, arithmetic and copies ran while one was open for 4% of the time, Pallas kernels for 14%

profile of v14, /device:TPU:0, one launch (start us, length us, event | category | flops | bytes accessed | tf_op | source)
XLA Modules:
  0.0 50.5 jit_solution(677597396296114342)
XLA Ops:
  0.0 3.0 %collective-permute-start = (bf16[128,4,8,128]{3,2,1,0:T(8,128)(2,1)}, bf16[128,4,8,128]{3,2,1,0:T(8,128)(2,1)S(1)}, u32[]{:S(2)}, u32[]{:S(2)}) collective-permute-start(bf16[128,4,8,128]{3,2,1,0:T(8,128)(2,1)} %param.3), channel_id=1, source_target_pairs={{24,0},{28,4},{0,8},{4,12},{8,16},{12,20},{16,24},{20,28},{25,1},{... | collective-permute-start | bytes 3145736 | tf_op jit(solution)/shard_map/ppermute | solution.py:24
  3.0 1.7 %copy.9 = bf16[16,8,32,128]{3,1,2,0:T(8,128)(2,1)S(1)} copy(bf16[16,8,32,128]{3,2,1,0:T(8,128)(2,1)} %bitcast.18) | data formatting | bytes 2097152
  4.8 0.1 shard_map.37
  4.9 1.6 %collective-permute-start.3 = (bf16[128,1280]{1,0:T(8,128)(2,1)S(1)}, bf16[128,1280]{1,0:T(8,128)(2,1)S(1)}, u32[]{:S(2)}, u32[]{:S(2)}) collective-permute-start(bf16[128,1280]{1,0:T(8,128)(2,1)S(1)} %get-tuple-element.35), channel_id=1, source_target_pairs={{1,0},{0,1},{3,2},{2,3},{5,4},{4,5},{7,6},{6,7},{9,8},{8,9},{11,10... | collective-permute-start | bytes 983048 | tf_op jit(solution)/shard_map/ppermute | solution.py:24
  6.4 1.5 %collective-permute-start.1 = (bf16[128,1408]{1,0:T(8,128)(2,1)S(1)}, bf16[128,1408]{1,0:T(8,128)(2,1)S(1)}, u32[]{:S(2)}, u32[]{:S(2)}) collective-permute-start(bf16[128,1408]{1,0:T(8,128)(2,1)S(1)} %get-tuple-element.33), channel_id=1, source_target_pairs={{2,0},{0,2},{3,1},{1,3},{6,4},{4,6},{7,5},{5,7},{10,8},{8,10},{11,... | collective-permute-start | bytes 1081352 | tf_op jit(solution)/shard_map/ppermute | solution.py:24
  8.0 0.5 %collective-permute-start.2 = (bf16[128,896]{1,0:T(8,128)(2,1)S(1)}, bf16[128,896]{1,0:T(8,128)(2,1)S(1)}, u32[]{:S(2)}, u32[]{:S(2)}) collective-permute-start(bf16[128,896]{1,0:T(8,128)(2,1)S(1)} %get-tuple-element.34), channel_id=1, source_target_pairs={{2,0},{0,2},{3,1},{1,3},{6,4},{4,6},{7,5},{5,7},{10,8},{8,10},{11,... | collective-permute-start | bytes 688136 | tf_op jit(solution)/shard_map/ppermute | solution.py:24
  8.5 0.1 fusion
  8.6 0.1 collective-permute-start.4
  8.7 5.5 %collective-permute-done.3.refs_1_.refs_3_ = bf16[128,1280]{1,0:T(8,128)(2,1)S(1)} collective-permute-done((bf16[128,1280]{1,0:T(8,128)(2,1)S(1)}, bf16[128,1280]{1,0:T(8,128)(2,1)S(1)}, u32[]{:S(2)}, u32[]{:S(2)}) %collective-permute-start.3) | collective-permute-done | bytes 327712 | tf_op jit(solution)/shard_map/ppermute | solution.py:24
  14.1 1.9 %shard_map.38 = (bf16[384,2048]{1,0:T(8,128)(2,1)S(1)}, bf16[384,2048]{1,0:T(8,128)(2,1)S(1)}) custom-call(bf16[128,4096]{1,0:T(8,128)(2,1)S(1)} %bitcast.12, bf16[128,1280]{1,0:T(8,128)(2,1)S(1)} %collective-permute-done.3.refs_1_.refs_3_, f32[4,8,128]{2,1,0:T(8,128)S(1)} %copy-done.1, f32[3,4,8,128]{3,2,1,0:T(8,128)S(1)} %copy-done), custom_call_target="tpu_custom_call" | custom-call | tf_op jit(solution)/shard_map/pallas_call | solution.py:65
  16.0 4.9 %collective-permute-done.2.refs_2_ = bf16[128,896]{1,0:T(8,128)(2,1)S(1)} collective-permute-done((bf16[128,896]{1,0:T(8,128)(2,1)S(1)}, bf16[128,896]{1,0:T(8,128)(2,1)S(1)}, u32[]{:S(2)}, u32[]{:S(2)}) %collective-permute-start.2) | collective-permute-done | bytes 229408 | tf_op jit(solution)/shard_map/ppermute | solution.py:24
  21.0 1.9 %shard_map.39 = (bf16[384,2048]{1,0:T(8,128)(2,1)S(1)}, bf16[384,2048]{1,0:T(8,128)(2,1)S(1)}) custom-call(bf16[128,4096]{1,0:T(8,128)(2,1)S(1)} %bitcast.13, bf16[128,1408]{1,0:T(8,128)(2,1)S(1)} %collective-permute-done.1.refs_1_, bf16[128,896]{1,0:T(8,128)(2,1)S(1)} %collective-permute-done.2.refs_2_, ...), custom_call_target="tpu_custom_call" | custom-call | tf_op jit(solution)/shard_map/pallas_call | solution.py:65
  22.9 0.6 %collective-permute-start.11 = (bf16[384,2048]{1,0:T(8,128)(2,1)S(1)}, bf16[384,2048]{1,0:T(8,128)(2,1)S(1)}, u32[]{:S(2)}, u32[]{:S(2)}) collective-permute-start(bf16[384,2048]{1,0:T(8,128)(2,1)S(1)} %get-tuple-element.51.refs_1_), channel_id=1, source_target_pairs={{0,4},{4,0},{8,12},{12,8},{16,20},{20,16},{24,28},{28,24},{1,5},{5... | collective-permute-start | bytes 4718600 | tf_op jit(solution)/shard_map/ppermute | solution.py:334
  23.5 1.0 %shard_map.40 = (f32[2,3,32,128]{3,2,1,0:T(8,128)S(1)}, bf16[2,3,32,128]{3,2,1,0:T(8,128)(2,1)S(1)}, bf16[2,3,32,128]{3,2,1,0:T(8,128)(2,1)S(1)}, bf16[2,3,32,128]{3,2,1,0:T(8,128)(2,1)S(1)}) custom-call(bf16[384,2048]{1,0:T(8,128)(2,1)S(1)} %get-tuple-element.37.refs_0_, bf16[384,2048]{1,0:T(8,128)(2,1)S(1)} %get-tuple-element.40.refs_1_, ...), custom_call_target="tpu_custom_call" | custom-call | tf_op jit(solution)/shard_map/pallas_call | solution.py:65
  24.5 0.6 %collective-permute-start.6 = (bf16[2,3,32,128]{3,2,1,0:T(8,128)(2,1)S(1)}, bf16[2,3,32,128]{3,2,1,0:T(8,128)(2,1)S(1)}, u32[]{:S(2)}, u32[]{:S(2)}) collective-permute-start(bf16[2,3,32,128]{3,2,1,0:T(8,128)(2,1)S(1)} %get-tuple-element.42), channel_id=1, source_target_pairs={{0,1},{1,0},{2,3},{3,2},{4,5},{5,4},{6,7},{7,6},{8,9},{9,8},{10,11... | collective-permute-start | bytes 147464 | tf_op jit(solution)/shard_map/ppermute | solution.py:49
  25.1 1.5 %collective-permute-start.7 = (bf16[2,3,32,128]{3,2,1,0:T(8,128)(2,1)S(1)}, bf16[2,3,32,128]{3,2,1,0:T(8,128)(2,1)S(1)}, u32[]{:S(2)}, u32[]{:S(2)}) collective-permute-start(bf16[2,3,32,128]{3,2,1,0:T(8,128)(2,1)S(1)} %get-tuple-element.43), channel_id=1, source_target_pairs={{0,2},{1,3},{2,0},{3,1},{4,6},{5,7},{6,4},{7,5},{8,10},{9,11},{10,... | collective-permute-start | bytes 147464 | tf_op jit(solution)/shard_map/ppermute | solution.py:49
  26.6 2.0 %collective-permute-done.6.refs_1_ = bf16[2,3,32,128]{3,2,1,0:T(8,128)(2,1)S(1)} collective-permute-done((bf16[2,3,32,128]{3,2,1,0:T(8,128)(2,1)S(1)}, bf16[2,3,32,128]{3,2,1,0:T(8,128)(2,1)S(1)}, u32[]{:S(2)}, u32[]{:S(2)}) %collective-permute-start.6) | collective-permute-done | bytes 49184 | tf_op jit(solution)/shard_map/ppermute | solution.py:49
  28.7 1.5 %collective-permute-start.8 = (bf16[2,3,32,128]{3,2,1,0:T(8,128)(2,1)S(1)}, bf16[2,3,32,128]{3,2,1,0:T(8,128)(2,1)S(1)}, u32[]{:S(2)}, u32[]{:S(2)}) collective-permute-start(bf16[2,3,32,128]{3,2,1,0:T(8,128)(2,1)S(1)} %get-tuple-element.44), channel_id=1, source_target_pairs={{0,3},{1,2},{2,1},{3,0},{4,7},{5,6},{6,5},{7,4},{8,11},{9,10},{10,... | collective-permute-start | bytes 147464 | tf_op jit(solution)/shard_map/ppermute | solution.py:49
  30.2 3.5 %collective-permute-done.8.refs_3_ = bf16[2,3,32,128]{3,2,1,0:T(8,128)(2,1)S(1)} collective-permute-done((bf16[2,3,32,128]{3,2,1,0:T(8,128)(2,1)S(1)}, bf16[2,3,32,128]{3,2,1,0:T(8,128)(2,1)S(1)}, u32[]{:S(2)}, u32[]{:S(2)}) %collective-permute-start.8) | collective-permute-done | bytes 49184 | tf_op jit(solution)/shard_map/ppermute | solution.py:49
  33.7 0.5 copy.8
  34.2 2.0 %shard_map.41 = (f32[128,384]{1,0:T(8,128)S(1)}, f32[128,384]{1,0:T(8,128)S(1)}) custom-call(bf16[384,2048]{1,0:T(8,128)(2,1)S(1)} %get-tuple-element.50.refs_0_, bf16[384,2048]{1,0:T(8,128)(2,1)S(1)} %get-tuple-element.51.refs_1_, bf16[384,2048]{1,0:T(8,128)(2,1)S(1)} %collective-permute-done.10.refs_2_, ...), custom_call_target="tpu_custom_call" | custom-call | tf_op jit(solution)/shard_map/pallas_call | solution.py:65
  36.2 0.7 %collective-permute-done.9.refs_3_ = bf16[128,4096]{1,0:T(8,128)(2,1)S(1)} collective-permute-done((bf16[128,4096]{1,0:T(8,128)(2,1)S(1)}, bf16[128,4096]{1,0:T(8,128)(2,1)S(1)}, u32[]{:S(2)}, u32[]{:S(2)}) %collective-permute-start.9) | collective-permute-done | bytes 1048608 | tf_op jit(solution)/shard_map/ppermute | solution.py:351
  36.9 1.0 %shard_map.42 = (f32[3,3,32,128]{3,2,1,0:T(8,128)S(1)}, bf16[3,3,32,128]{3,2,1,0:T(8,128)(2,1)S(1)}, bf16[3,3,32,128]{3,2,1,0:T(8,128)(2,1)S(1)}, bf16[3,3,32,128]{3,2,1,0:T(8,128)(2,1)S(1)}) custom-call(bf16[384,2048]{1,0:T(8,128)(2,1)S(1)} %get-tuple-element.37.refs_0_, bf16[384,2048]{1,0:T(8,128)(2,1)S(1)} %get-tuple-element.40.refs_1_, ...), custom_call_target="tpu_custom_call" | custom-call | tf_op jit(solution)/shard_map/pallas_call | solution.py:65
  37.9 0.6 %collective-permute-start.12 = (bf16[3,3,32,128]{3,2,1,0:T(8,128)(2,1)S(1)}, bf16[3,3,32,128]{3,2,1,0:T(8,128)(2,1)S(1)}, u32[]{:S(2)}, u32[]{:S(2)}) collective-permute-start(bf16[3,3,32,128]{3,2,1,0:T(8,128)(2,1)S(1)} %get-tuple-element.58), channel_id=1, source_target_pairs={{0,1},{1,0},{2,3},{3,2},{4,5},{5,4},{6,7},{7,6},{8,9},{9,8},{10,11... | collective-permute-start | bytes 221192 | tf_op jit(solution)/shard_map/ppermute | solution.py:49
  38.5 1.5 %collective-permute-start.13 = (bf16[3,3,32,128]{3,2,1,0:T(8,128)(2,1)S(1)}, bf16[3,3,32,128]{3,2,1,0:T(8,128)(2,1)S(1)}, u32[]{:S(2)}, u32[]{:S(2)}) collective-permute-start(bf16[3,3,32,128]{3,2,1,0:T(8,128)(2,1)S(1)} %get-tuple-element.59), channel_id=1, source_target_pairs={{0,2},{1,3},{2,0},{3,1},{4,6},{5,7},{6,4},{7,5},{8,10},{9,11},{10,... | collective-permute-start | bytes 221192 | tf_op jit(solution)/shard_map/ppermute | solution.py:49
  40.0 1.4 %collective-permute-start.14 = (bf16[3,3,32,128]{3,2,1,0:T(8,128)(2,1)S(1)}, bf16[3,3,32,128]{3,2,1,0:T(8,128)(2,1)S(1)}, u32[]{:S(2)}, u32[]{:S(2)}) collective-permute-start(bf16[3,3,32,128]{3,2,1,0:T(8,128)(2,1)S(1)} %get-tuple-element.60), channel_id=1, source_target_pairs={{0,3},{1,2},{2,1},{3,0},{4,7},{5,6},{6,5},{7,4},{8,11},{9,10},{10,... | collective-permute-start | bytes 221192 | tf_op jit(solution)/shard_map/ppermute | solution.py:49
  41.4 1.1 %collective-permute-done.12.refs_1_.refs_5_ = bf16[3,3,32,128]{3,2,1,0:T(8,128)(2,1)S(1)} collective-permute-done((bf16[3,3,32,128]{3,2,1,0:T(8,128)(2,1)S(1)}, bf16[3,3,32,128]{3,2,1,0:T(8,128)(2,1)S(1)}, u32[]{:S(2)}, u32[]{:S(2)}) %collective-permute-start.12) | collective-permute-done | bytes 73760 | tf_op jit(solution)/shard_map/ppermute | solution.py:49
  42.5 0.3 collective-permute-done.13.refs_2_.refs_6_
  42.8 2.4 %collective-permute-done.14.refs_3_.refs_7_ = bf16[3,3,32,128]{3,2,1,0:T(8,128)(2,1)S(1)} collective-permute-done((bf16[3,3,32,128]{3,2,1,0:T(8,128)(2,1)S(1)}, bf16[3,3,32,128]{3,2,1,0:T(8,128)(2,1)S(1)}, u32[]{:S(2)}, u32[]{:S(2)}) %collective-permute-start.14) | collective-permute-done | bytes 73760 | tf_op jit(solution)/shard_map/ppermute | solution.py:49
  45.3 2.4 %collective-permute-start.15 = (bf16[3,3,32,128]{3,2,1,0:T(8,128)(2,1)S(1)}, bf16[3,3,32,128]{3,2,1,0:T(8,128)(2,1)S(1)}, u32[]{:S(2)}, u32[]{:S(2)}) collective-permute-start(bf16[3,3,32,128]{3,2,1,0:T(8,128)(2,1)S(1)} %shard_map.43), channel_id=1, source_target_pairs={{8,0},{12,4},{16,8},{20,12},{24,16},{28,20},{0,24},{4,28},{9,1},{1... | collective-permute-start | bytes 221192 | tf_op jit(solution)/shard_map/ppermute | solution.py:24
  47.7 2.0 %collective-permute-done.15.refs_8_ = bf16[3,3,32,128]{3,2,1,0:T(8,128)(2,1)S(1)} collective-permute-done((bf16[3,3,32,128]{3,2,1,0:T(8,128)(2,1)S(1)}, bf16[3,3,32,128]{3,2,1,0:T(8,128)(2,1)S(1)}, u32[]{:S(2)}, u32[]{:S(2)}) %collective-permute-start.15) | collective-permute-done | bytes 73760 | tf_op jit(solution)/shard_map/ppermute | solution.py:24
  49.7 0.8 %shard_map.44 = f32[3,5,32,128]{3,2,1,0:T(8,128)} custom-call(f32[2,3,32,128]{3,2,1,0:T(8,128)S(1)} %get-tuple-element.45.refs_0_, bf16[2,3,32,128]{3,2,1,0:T(8,128)(2,1)S(1)} %collective-permute-done.6.refs_1_, bf16[2,3,32,128]{3,2,1,0:T(8,128)(2,1)S(1)} %collective-permute-done.7.refs_2_, bf16[2,3,32,128]{3,2,1,0:T(8,128)(2,1)S(1)} %collective-permute-done.8.refs_3_, ...), custom_call_target="tpu_custom_call" | custom-call | tf_op jit(solution)/shard_map/pallas_call | solution.py:65
  (15 shorter events, 0.1 us)
Async XLA Ops:
  0.0 4.7 %copy-start.1 = (f32[4,8,128]{2,1,0:T(8,128)S(1)}, f32[4,8,128]{2,1,0:T(8,128)}, u32[]{:S(2)}) copy-start(f32[4,8,128]{2,1,0:T(8,128)} %refs_4_.1) | copy-start | bytes 49156
  0.0 4.7 %copy-start = (f32[3,4,8,128]{3,2,1,0:T(8,128)S(1)}, f32[3,4,8,128]{3,2,1,0:T(8,128)}, u32[]{:S(2)}) copy-start(f32[3,4,8,128]{3,2,1,0:T(8,128)} %refs_5_.1) | copy-start | bytes 147460
  0.0 33.7 %collective-permute-start = (bf16[128,4,8,128]{3,2,1,0:T(8,128)(2,1)}, bf16[128,4,8,128]{3,2,1,0:T(8,128)(2,1)S(1)}, u32[]{:S(2)}, u32[]{:S(2)}) collective-permute-start(bf16[128,4,8,128]{3,2,1,0:T(8,128)(2,1)} %param.3), channel_id=1, source_target_pairs={{24,0},{28,4},{0,8},{4,12},{8,16},{12,20},{16,24},{20,28},{25,1},{... | collective-permute-start | bytes 3145736 | tf_op jit(solution)/shard_map/ppermute | solution.py:24
  4.9 9.2 %collective-permute-start.3 = (bf16[128,1280]{1,0:T(8,128)(2,1)S(1)}, bf16[128,1280]{1,0:T(8,128)(2,1)S(1)}, u32[]{:S(2)}, u32[]{:S(2)}) collective-permute-start(bf16[128,1280]{1,0:T(8,128)(2,1)S(1)} %get-tuple-element.35), channel_id=1, source_target_pairs={{1,0},{0,1},{3,2},{2,3},{5,4},{4,5},{7,6},{6,7},{9,8},{8,9},{11,10... | collective-permute-start | bytes 983048 | tf_op jit(solution)/shard_map/ppermute | solution.py:24
  6.4 14.5 %collective-permute-start.1 = (bf16[128,1408]{1,0:T(8,128)(2,1)S(1)}, bf16[128,1408]{1,0:T(8,128)(2,1)S(1)}, u32[]{:S(2)}, u32[]{:S(2)}) collective-permute-start(bf16[128,1408]{1,0:T(8,128)(2,1)S(1)} %get-tuple-element.33), channel_id=1, source_target_pairs={{2,0},{0,2},{3,1},{1,3},{6,4},{4,6},{7,5},{5,7},{10,8},{8,10},{11,... | collective-permute-start | bytes 1081352 | tf_op jit(solution)/shard_map/ppermute | solution.py:24
  8.0 13.0 %collective-permute-start.2 = (bf16[128,896]{1,0:T(8,128)(2,1)S(1)}, bf16[128,896]{1,0:T(8,128)(2,1)S(1)}, u32[]{:S(2)}, u32[]{:S(2)}) collective-permute-start(bf16[128,896]{1,0:T(8,128)(2,1)S(1)} %get-tuple-element.34), channel_id=1, source_target_pairs={{2,0},{0,2},{3,1},{1,3},{6,4},{4,6},{7,5},{5,7},{10,8},{8,10},{11,... | collective-permute-start | bytes 688136 | tf_op jit(solution)/shard_map/ppermute | solution.py:24
  8.6 14.9 %collective-permute-start.4 = (bf16[64,4096]{1,0:T(8,128)(2,1)S(1)}, bf16[64,4096]{1,0:T(8,128)(2,1)S(1)}, u32[]{:S(2)}, u32[]{:S(2)}) collective-permute-start(bf16[64,4096]{1,0:T(8,128)(2,1)S(1)} %get-tuple-element.62), channel_id=1, source_target_pairs={{0,4},{4,0},{8,12},{12,8},{16,20},{20,16},{24,28},{28,24},{1,5},{5... | collective-permute-start | bytes 1572872 | tf_op jit(solution)/shard_map/ppermute | solution.py:306
  14.1 9.4 %collective-permute-start.5 = (bf16[64,4096]{1,0:T(8,128)(2,1)S(1)}, bf16[64,4096]{1,0:T(8,128)(2,1)S(1)}, u32[]{:S(2)}, u32[]{:S(2)}) collective-permute-start(bf16[64,4096]{1,0:T(8,128)(2,1)S(1)} %get-tuple-element.61), channel_id=1, source_target_pairs={{0,4},{4,0},{8,12},{12,8},{16,20},{20,16},{24,28},{28,24},{1,5},{5... | collective-permute-start | bytes 1572872 | tf_op jit(solution)/shard_map/ppermute | solution.py:306
  21.0 13.2 %collective-permute-start.10 = (bf16[384,2048]{1,0:T(8,128)(2,1)S(1)}, bf16[384,2048]{1,0:T(8,128)(2,1)S(1)}, u32[]{:S(2)}, u32[]{:S(2)}) collective-permute-start(bf16[384,2048]{1,0:T(8,128)(2,1)S(1)} %get-tuple-element.50.refs_0_), channel_id=1, source_target_pairs={{0,4},{4,0},{8,12},{12,8},{16,20},{20,16},{24,28},{28,24},{1,5},{5... | collective-permute-start | bytes 4718600 | tf_op jit(solution)/shard_map/ppermute | solution.py:334
  22.9 11.3 %collective-permute-start.11 = (bf16[384,2048]{1,0:T(8,128)(2,1)S(1)}, bf16[384,2048]{1,0:T(8,128)(2,1)S(1)}, u32[]{:S(2)}, u32[]{:S(2)}) collective-permute-start(bf16[384,2048]{1,0:T(8,128)(2,1)S(1)} %get-tuple-element.51.refs_1_), channel_id=1, source_target_pairs={{0,4},{4,0},{8,12},{12,8},{16,20},{20,16},{24,28},{28,24},{1,5},{5... | collective-permute-start | bytes 4718600 | tf_op jit(solution)/shard_map/ppermute | solution.py:334
  24.5 4.2 %collective-permute-start.6 = (bf16[2,3,32,128]{3,2,1,0:T(8,128)(2,1)S(1)}, bf16[2,3,32,128]{3,2,1,0:T(8,128)(2,1)S(1)}, u32[]{:S(2)}, u32[]{:S(2)}) collective-permute-start(bf16[2,3,32,128]{3,2,1,0:T(8,128)(2,1)S(1)} %get-tuple-element.42), channel_id=1, source_target_pairs={{0,1},{1,0},{2,3},{3,2},{4,5},{5,4},{6,7},{7,6},{8,9},{9,8},{10,11... | collective-permute-start | bytes 147464 | tf_op jit(solution)/shard_map/ppermute | solution.py:49
  25.1 5.1 %collective-permute-start.7 = (bf16[2,3,32,128]{3,2,1,0:T(8,128)(2,1)S(1)}, bf16[2,3,32,128]{3,2,1,0:T(8,128)(2,1)S(1)}, u32[]{:S(2)}, u32[]{:S(2)}) collective-permute-start(bf16[2,3,32,128]{3,2,1,0:T(8,128)(2,1)S(1)} %get-tuple-element.43), channel_id=1, source_target_pairs={{0,2},{1,3},{2,0},{3,1},{4,6},{5,7},{6,4},{7,5},{8,10},{9,11},{10,... | collective-permute-start | bytes 147464 | tf_op jit(solution)/shard_map/ppermute | solution.py:49
  28.7 5.0 %collective-permute-start.8 = (bf16[2,3,32,128]{3,2,1,0:T(8,128)(2,1)S(1)}, bf16[2,3,32,128]{3,2,1,0:T(8,128)(2,1)S(1)}, u32[]{:S(2)}, u32[]{:S(2)}) collective-permute-start(bf16[2,3,32,128]{3,2,1,0:T(8,128)(2,1)S(1)} %get-tuple-element.44), channel_id=1, source_target_pairs={{0,3},{1,2},{2,1},{3,0},{4,7},{5,6},{6,5},{7,4},{8,11},{9,10},{10,... | collective-permute-start | bytes 147464 | tf_op jit(solution)/shard_map/ppermute | solution.py:49
  34.1 2.7 %collective-permute-start.9 = (bf16[128,4096]{1,0:T(8,128)(2,1)S(1)}, bf16[128,4096]{1,0:T(8,128)(2,1)S(1)}, u32[]{:S(2)}, u32[]{:S(2)}) collective-permute-start(bf16[128,4096]{1,0:T(8,128)(2,1)S(1)} %bitcast.15), channel_id=1, source_target_pairs={{0,4},{4,0},{8,12},{12,8},{16,20},{20,16},{24,28},{28,24},{1,5},{5... | collective-permute-start | bytes 3145736 | tf_op jit(solution)/shard_map/ppermute | solution.py:351
  37.9 4.7 %collective-permute-start.12 = (bf16[3,3,32,128]{3,2,1,0:T(8,128)(2,1)S(1)}, bf16[3,3,32,128]{3,2,1,0:T(8,128)(2,1)S(1)}, u32[]{:S(2)}, u32[]{:S(2)}) collective-permute-start(bf16[3,3,32,128]{3,2,1,0:T(8,128)(2,1)S(1)} %get-tuple-element.58), channel_id=1, source_target_pairs={{0,1},{1,0},{2,3},{3,2},{4,5},{5,4},{6,7},{7,6},{8,9},{9,8},{10,11... | collective-permute-start | bytes 221192 | tf_op jit(solution)/shard_map/ppermute | solution.py:49
  38.5 4.4 %collective-permute-start.13 = (bf16[3,3,32,128]{3,2,1,0:T(8,128)(2,1)S(1)}, bf16[3,3,32,128]{3,2,1,0:T(8,128)(2,1)S(1)}, u32[]{:S(2)}, u32[]{:S(2)}) collective-permute-start(bf16[3,3,32,128]{3,2,1,0:T(8,128)(2,1)S(1)} %get-tuple-element.59), channel_id=1, source_target_pairs={{0,2},{1,3},{2,0},{3,1},{4,6},{5,7},{6,4},{7,5},{8,10},{9,11},{10,... | collective-permute-start | bytes 221192 | tf_op jit(solution)/shard_map/ppermute | solution.py:49
  40.0 5.3 %collective-permute-start.14 = (bf16[3,3,32,128]{3,2,1,0:T(8,128)(2,1)S(1)}, bf16[3,3,32,128]{3,2,1,0:T(8,128)(2,1)S(1)}, u32[]{:S(2)}, u32[]{:S(2)}) collective-permute-start(bf16[3,3,32,128]{3,2,1,0:T(8,128)(2,1)S(1)} %get-tuple-element.60), channel_id=1, source_target_pairs={{0,3},{1,2},{2,1},{3,0},{4,7},{5,6},{6,5},{7,4},{8,11},{9,10},{10,... | collective-permute-start | bytes 221192 | tf_op jit(solution)/shard_map/ppermute | solution.py:49
  45.3 4.4 %collective-permute-start.15 = (bf16[3,3,32,128]{3,2,1,0:T(8,128)(2,1)S(1)}, bf16[3,3,32,128]{3,2,1,0:T(8,128)(2,1)S(1)}, u32[]{:S(2)}, u32[]{:S(2)}) collective-permute-start(bf16[3,3,32,128]{3,2,1,0:T(8,128)(2,1)S(1)} %shard_map.43), channel_id=1, source_target_pairs={{8,0},{12,4},{16,8},{20,12},{24,16},{28,20},{0,24},{4,28},{9,1},{1... | collective-permute-start | bytes 221192 | tf_op jit(solution)/shard_map/ppermute | solution.py:24

commit v15 on v13

--- a/solution.py
+++ b/solution.py
@@ -256,22 +256,23 @@
 
 
 def add(*refs):
-    group, outs = refs[:-2], refs[-2:]
-    for n, out in enumerate(outs):
-        for k in range(3):
-            out[k] = total_of(group, n, k)
+    group, (ours, back) = refs[:-2], refs[-2:]
+    for k in range(3):
+        total = total_of(group, 1, k)
+        ours[k], back[1, k] = total, total.astype(BF16)
+        back[0, k] = total_of(group, 0, k).astype(BF16)
 
 
 def assemble(*refs):
-    group, (ours, back_two, back_one, out) = refs[:-4], refs[-4:]
+    group, (ours, back, out) = refs[:-3], refs[-3:]
     core = lax.rem(lax.axis_index("blk"), 2)
     for k in range(3):
         mate, third = total_of(group, 1, k), total_of(group, 2, k)
         out[k, 0] = total_of(group, 0, k)
         out[k, 1] = jnp.where(core == 0, third, mate)
         out[k, 2] = jnp.where(core == 0, ours[k], third)
-        out[k, 3] = jnp.where(core == 0, mate, back_one[k])
-        out[k, 4] = back_two[k]
+        out[k, 3] = jnp.where(core == 0, mate, back[1, k].astype(F32))
+        out[k, 4] = back[0, k].astype(F32)
 
 
 def on_device(orbitals, coupling, pot_grad):
@@ -345,13 +346,13 @@
     )
     second = exchange(sends)
     first, kept = lax.optimization_barrier((first, kept))
-    small = shape_of((3, rows, states), F32)
-    there, ours = call(add, [small, small], [kept_there, *first])
-    back_two, back_one = shift(there, "blk", 2), shift(ours, "blk", 2)
+    small = (3, rows, states)
+    ours, back = call(
+        add, [shape_of(small, F32), shape_of((2, *small), BF16)], [kept_there, *first]
+    )
+    back = shift(back, "blk", 2)
     (out,) = call(
-        assemble,
-        [shape_of((3, 5, rows, states), F32)],
-        [kept, *second, ours, back_two, back_one],
+        assemble, [shape_of((3, 5, rows, states), F32)], [kept, *second, ours, back]
     )
     return out
 

time: 46.2 us -> 44.9 us (0.972)
  waiting for transfers between devices: 18.3 us -> 17.5 us
    ppermute x6 -> x5, waiting for transfers between devices: 18.2 us -> 16.9 us  [shift(): lax.ppermute(block, axis, [((i + distance) % count, i) for i in range(cou...]
    ppermute x6, waiting for transfers between devices: 0.13 us -> 0.61 us  [exchange(): got.append(lax.ppermute(piece, ('dx', 'dy'), route))]
    ppermute x6 -> x5, starting transfers between devices: 8.85 us -> 8.4 us  [shift(): lax.ppermute(block, axis, [((i + distance) % count, i) for i in range(cou...]
  transfers between devices with their start and end apart: 15 -> 14, of which waited for: 7 -> 7; matrix products, arithmetic and copies ran while one was open for 5% -> 5% of each run, Pallas kernels for 18% -> 18%
where the time goes in v15:
time: 44.9 us; the launch traced here: 44.8 us
  waiting for transfers between devices  17.5 us (39%)
  starting transfers between devices  16.2 us (36%)
  Pallas kernels  8.87 us (20%)
  local copies, waits for them, and re-layouts  2.16 us (5%)
    ppermute x5, waiting for transfers between devices, shift(): lax.ppermute(block, axis, [((i + distance) % count, i) for i in range(cou...  16.9 us
    pallas_call x8, Pallas kernels, call(): return list(run(*operands))  8.87 us
    ppermute x5, starting transfers between devices, shift(): lax.ppermute(block, axis, [((i + distance) % count, i) for i in range(cou...  8.4 us
    ppermute x6, starting transfers between devices, exchange(): got.append(lax.ppermute(piece, ('dx', 'dy'), route))  7.11 us
    unnamed x6, local copies, waits for them, and re-layouts  2.16 us
  transfers between devices with their start and end apart: 14, of which 7 were waited for; matrix products, arithmetic and copies ran while one was open for 5% of the time, Pallas kernels for 18%

profile of v15, /device:TPU:0, one launch (start us, length us, event | category | flops | bytes accessed | tf_op | source)
XLA Modules:
  0.0 44.8 jit_solution(850534977707800371)
XLA Ops:
  0.0 3.0 %collective-permute-start.5 = (bf16[128,4,8,128]{3,2,1,0:T(8,128)(2,1)}, bf16[128,4,8,128]{3,2,1,0:T(8,128)(2,1)S(1)}, u32[]{:S(2)}, u32[]{:S(2)}) collective-permute-start(bf16[128,4,8,128]{3,2,1,0:T(8,128)(2,1)} %param.3), channel_id=1, source_target_pairs={{24,0},{28,4},{0,8},{4,12},{8,16},{12,20},{16,24},{20,28},{25,1},{... | collective-permute-start | bytes 3145736 | tf_op jit(solution)/shard_map/ppermute | solution.py:24
  3.0 1.7 %copy.9 = bf16[16,8,32,128]{3,1,2,0:T(8,128)(2,1)S(1)} copy(bf16[16,8,32,128]{3,2,1,0:T(8,128)(2,1)} %bitcast.18) | data formatting | bytes 2097152
  4.8 0.1 shard_map.37
  4.9 1.6 %collective-permute-start = (bf16[128,1280]{1,0:T(8,128)(2,1)S(1)}, bf16[128,1280]{1,0:T(8,128)(2,1)S(1)}, u32[]{:S(2)}, u32[]{:S(2)}) collective-permute-start(bf16[128,1280]{1,0:T(8,128)(2,1)S(1)} %get-tuple-element.34), channel_id=1, source_target_pairs={{1,0},{0,1},{3,2},{2,3},{5,4},{4,5},{7,6},{6,7},{9,8},{8,9},{11,10... | collective-permute-start | bytes 983048 | tf_op jit(solution)/shard_map/ppermute | solution.py:24
  6.4 1.5 %collective-permute-start.1 = (bf16[128,1152]{1,0:T(8,128)(2,1)S(1)}, bf16[128,1152]{1,0:T(8,128)(2,1)S(1)}, u32[]{:S(2)}, u32[]{:S(2)}) collective-permute-start(bf16[128,1152]{1,0:T(8,128)(2,1)S(1)} %get-tuple-element.36), channel_id=1, source_target_pairs={{2,0},{0,2},{3,1},{1,3},{6,4},{4,6},{7,5},{5,7},{10,8},{8,10},{11,... | collective-permute-start | bytes 884744 | tf_op jit(solution)/shard_map/ppermute | solution.py:24
  8.0 0.5 %collective-permute-start.2 = (bf16[128,1152]{1,0:T(8,128)(2,1)S(1)}, bf16[128,1152]{1,0:T(8,128)(2,1)S(1)}, u32[]{:S(2)}, u32[]{:S(2)}) collective-permute-start(bf16[128,1152]{1,0:T(8,128)(2,1)S(1)} %get-tuple-element.37), channel_id=1, source_target_pairs={{2,0},{0,2},{3,1},{1,3},{6,4},{4,6},{7,5},{5,7},{10,8},{8,10},{11,... | collective-permute-start | bytes 884744 | tf_op jit(solution)/shard_map/ppermute | solution.py:24
  8.5 5.7 %collective-permute-done.refs_1_.refs_3_ = bf16[128,1280]{1,0:T(8,128)(2,1)S(1)} collective-permute-done((bf16[128,1280]{1,0:T(8,128)(2,1)S(1)}, bf16[128,1280]{1,0:T(8,128)(2,1)S(1)}, u32[]{:S(2)}, u32[]{:S(2)}) %collective-permute-start) | collective-permute-done | bytes 327712 | tf_op jit(solution)/shard_map/ppermute | solution.py:24
  14.1 1.9 %shard_map.38 = (bf16[384,2048]{1,0:T(8,128)(2,1)S(1)}, bf16[384,2048]{1,0:T(8,128)(2,1)S(1)}) custom-call(bf16[128,4096]{1,0:T(8,128)(2,1)S(1)} %bitcast.11, bf16[128,1280]{1,0:T(8,128)(2,1)S(1)} %collective-permute-done.refs_1_.refs_3_, f32[4,8,128]{2,1,0:T(8,128)S(1)} %copy-done.1, f32[3,4,8,128]{3,2,1,0:T(8,128)S(1)} %copy-done), custom_call_target="tpu_custom_call" | custom-call | tf_op jit(solution)/shard_map/pallas_call | solution.py:58
  16.0 0.4 collective-permute-done.1.refs_1_
  16.4 4.6 %collective-permute-done.2.refs_2_ = bf16[128,1152]{1,0:T(8,128)(2,1)S(1)} collective-permute-done((bf16[128,1152]{1,0:T(8,128)(2,1)S(1)}, bf16[128,1152]{1,0:T(8,128)(2,1)S(1)}, u32[]{:S(2)}, u32[]{:S(2)}) %collective-permute-start.2) | collective-permute-done | bytes 294944 | tf_op jit(solution)/shard_map/ppermute | solution.py:24
  21.0 1.9 %shard_map.39 = (bf16[384,2048]{1,0:T(8,128)(2,1)S(1)}, bf16[384,2048]{1,0:T(8,128)(2,1)S(1)}) custom-call(bf16[128,4096]{1,0:T(8,128)(2,1)S(1)} %bitcast.12, bf16[128,1152]{1,0:T(8,128)(2,1)S(1)} %collective-permute-done.1.refs_1_, bf16[128,1152]{1,0:T(8,128)(2,1)S(1)} %collective-permute-done.2.refs_2_, ...), custom_call_target="tpu_custom_call" | custom-call | tf_op jit(solution)/shard_map/pallas_call | solution.py:58
  22.9 0.6 %collective-permute-start.4 = (bf16[384,2048]{1,0:T(8,128)(2,1)S(1)}, bf16[384,2048]{1,0:T(8,128)(2,1)S(1)}, u32[]{:S(2)}, u32[]{:S(2)}) collective-permute-start(bf16[384,2048]{1,0:T(8,128)(2,1)S(1)} %get-tuple-element.41.refs_1_), channel_id=1, source_target_pairs={{0,4},{4,0},{8,12},{12,8},{16,20},{20,16},{24,28},{28,24},{1,5},{5... | collective-permute-start | bytes 4718600 | tf_op jit(solution)/shard_map/ppermute | solution.py:317
  23.5 1.0 %shard_map.40.refs_6_.refs_4_ = f32[384,128]{1,0:T(8,128)S(1)} custom-call(bf16[384,2048]{1,0:T(8,128)(2,1)S(1)} %get-tuple-element.42.refs_0_, bf16[384,2048]{1,0:T(8,128)(2,1)S(1)} %get-tuple-element.43.refs_1_, bf16[128,4096]{1,0:T(8,128)(2,1)S(1)} %bitcast.13), custom_call_target="tpu_custom_call" | custom-call | tf_op jit(solution)/shard_map/pallas_call | solution.py:58
  24.4 4.0 %collective-permute-done.5 = bf16[128,4,8,128]{3,2,1,0:T(8,128)(2,1)S(1)} collective-permute-done((bf16[128,4,8,128]{3,2,1,0:T(8,128)(2,1)}, bf16[128,4,8,128]{3,2,1,0:T(8,128)(2,1)S(1)}, u32[]{:S(2)}, u32[]{:S(2)}) %collective-permute-start.5) | collective-permute-done | bytes 1048608 | tf_op jit(solution)/shard_map/ppermute | solution.py:24
  28.4 0.5 %copy.8 = bf16[16,8,32,128]{3,1,2,0:T(8,128)(2,1)S(1)} copy(bf16[16,8,32,128]{3,2,1,0:T(8,128)(2,1)S(1)} %bitcast.19) | data formatting | bytes 2097152
  28.9 0.1 collective-permute-start.9
  29.0 0.0 collective-permute-done.3.refs_2_
  29.0 0.0 collective-permute-done.4.refs_3_
  29.0 2.1 %shard_map.41 = (f32[128,384]{1,0:T(8,128)S(1)}, f32[2,3,32,128]{3,2,1,0:T(8,128)S(1)}, bf16[2,3,32,128]{3,2,1,0:T(8,128)(2,1)S(1)}, bf16[2,3,32,128]{3,2,1,0:T(8,128)(2,1)S(1)}, bf16[2,3,32,128]{3,2,1,0:T(8,128)(2,1)S(1)}) custom-call(bf16[384,2048]{1,0:T(8,128)(2,1)S(1)} %get-tuple-element.35.refs_0_, bf16[384,2048]{1,0:T(8,128)(2,1)S(1)} %get-tuple-element.41.refs_1_, ...), custom_call_target="tpu_custom_call" | custom-call | bytes 3000000 | tf_op jit(solution)/shard_map/pallas_call | solution.py:58
  31.1 1.6 %collective-permute-start.6 = (bf16[2,3,32,128]{3,2,1,0:T(8,128)(2,1)S(1)}, bf16[2,3,32,128]{3,2,1,0:T(8,128)(2,1)S(1)}, u32[]{:S(2)}, u32[]{:S(2)}) collective-permute-start(bf16[2,3,32,128]{3,2,1,0:T(8,128)(2,1)S(1)} %get-tuple-element.46), channel_id=1, source_target_pairs={{0,1},{1,0},{2,3},{3,2},{4,5},{5,4},{6,7},{7,6},{8,9},{9,8},{10,11... | collective-permute-start | bytes 147464 | tf_op jit(solution)/shard_map/ppermute | solution.py:42
  32.7 1.5 %collective-permute-start.7 = (bf16[2,3,32,128]{3,2,1,0:T(8,128)(2,1)S(1)}, bf16[2,3,32,128]{3,2,1,0:T(8,128)(2,1)S(1)}, u32[]{:S(2)}, u32[]{:S(2)}) collective-permute-start(bf16[2,3,32,128]{3,2,1,0:T(8,128)(2,1)S(1)} %get-tuple-element.47), channel_id=1, source_target_pairs={{0,2},{1,3},{2,0},{3,1},{4,6},{5,7},{6,4},{7,5},{8,10},{9,11},{10,... | collective-permute-start | bytes 147464 | tf_op jit(solution)/shard_map/ppermute | solution.py:42
  34.2 0.5 %collective-permute-start.8 = (bf16[2,3,32,128]{3,2,1,0:T(8,128)(2,1)S(1)}, bf16[2,3,32,128]{3,2,1,0:T(8,128)(2,1)S(1)}, u32[]{:S(2)}, u32[]{:S(2)}) collective-permute-start(bf16[2,3,32,128]{3,2,1,0:T(8,128)(2,1)S(1)} %get-tuple-element.48), channel_id=1, source_target_pairs={{0,3},{1,2},{2,1},{3,0},{4,7},{5,6},{6,5},{7,4},{8,11},{9,10},{10,... | collective-permute-start | bytes 147464 | tf_op jit(solution)/shard_map/ppermute | solution.py:42
  34.7 0.0 collective-permute-done.9.refs_3_
  34.7 1.0 %shard_map.42 = (f32[3,3,32,128]{3,2,1,0:T(8,128)S(1)}, bf16[3,3,32,128]{3,2,1,0:T(8,128)(2,1)S(1)}, bf16[3,3,32,128]{3,2,1,0:T(8,128)(2,1)S(1)}, bf16[3,3,32,128]{3,2,1,0:T(8,128)(2,1)S(1)}) custom-call(bf16[384,2048]{1,0:T(8,128)(2,1)S(1)} %get-tuple-element.42.refs_0_, bf16[384,2048]{1,0:T(8,128)(2,1)S(1)} %get-tuple-element.43.refs_1_, ...), custom_call_target="tpu_custom_call" | custom-call | bytes 3000000 | tf_op jit(solution)/shard_map/pallas_call | solution.py:58
  35.7 1.6 %collective-permute-start.10 = (bf16[3,3,32,128]{3,2,1,0:T(8,128)(2,1)S(1)}, bf16[3,3,32,128]{3,2,1,0:T(8,128)(2,1)S(1)}, u32[]{:S(2)}, u32[]{:S(2)}) collective-permute-start(bf16[3,3,32,128]{3,2,1,0:T(8,128)(2,1)S(1)} %get-tuple-element.54), channel_id=1, source_target_pairs={{0,1},{1,0},{2,3},{3,2},{4,5},{5,4},{6,7},{7,6},{8,9},{9,8},{10,11... | collective-permute-start | bytes 221192 | tf_op jit(solution)/shard_map/ppermute | solution.py:42
  37.3 1.5 %collective-permute-start.11 = (bf16[3,3,32,128]{3,2,1,0:T(8,128)(2,1)S(1)}, bf16[3,3,32,128]{3,2,1,0:T(8,128)(2,1)S(1)}, u32[]{:S(2)}, u32[]{:S(2)}) collective-permute-start(bf16[3,3,32,128]{3,2,1,0:T(8,128)(2,1)S(1)} %get-tuple-element.55), channel_id=1, source_target_pairs={{0,2},{1,3},{2,0},{3,1},{4,6},{5,7},{6,4},{7,5},{8,10},{9,11},{10,... | collective-permute-start | bytes 221192 | tf_op jit(solution)/shard_map/ppermute | solution.py:42
  38.8 0.5 %collective-permute-start.12 = (bf16[3,3,32,128]{3,2,1,0:T(8,128)(2,1)S(1)}, bf16[3,3,32,128]{3,2,1,0:T(8,128)(2,1)S(1)}, u32[]{:S(2)}, u32[]{:S(2)}) collective-permute-start(bf16[3,3,32,128]{3,2,1,0:T(8,128)(2,1)S(1)} %get-tuple-element.56), channel_id=1, source_target_pairs={{0,3},{1,2},{2,1},{3,0},{4,7},{5,6},{6,5},{7,4},{8,11},{9,10},{10,... | collective-permute-start | bytes 221192 | tf_op jit(solution)/shard_map/ppermute | solution.py:42
  39.3 0.1 collective-permute-done.8.refs_3_
  39.4 1.8 %collective-permute-start.13 = (bf16[2,3,32,128]{3,2,1,0:T(8,128)(2,1)S(1)}, bf16[2,3,32,128]{3,2,1,0:T(8,128)(2,1)S(1)}, u32[]{:S(2)}, u32[]{:S(2)}) collective-permute-start(bf16[2,3,32,128]{3,2,1,0:T(8,128)(2,1)S(1)} %get-tuple-element.62), channel_id=1, source_target_pairs={{8,0},{12,4},{16,8},{20,12},{24,16},{28,20},{0,24},{4,28},{9,1},{1... | collective-permute-start | bytes 147464 | tf_op jit(solution)/shard_map/ppermute | solution.py:24
  41.2 2.3 %collective-permute-done.13.refs_5_ = bf16[2,3,32,128]{3,2,1,0:T(8,128)(2,1)S(1)} collective-permute-done((bf16[2,3,32,128]{3,2,1,0:T(8,128)(2,1)S(1)}, bf16[2,3,32,128]{3,2,1,0:T(8,128)(2,1)S(1)}, u32[]{:S(2)}, u32[]{:S(2)}) %collective-permute-start.13) | collective-permute-done | bytes 49184 | tf_op jit(solution)/shard_map/ppermute | solution.py:24
  43.6 0.5 %collective-permute-done.12.refs_3_ = bf16[3,3,32,128]{3,2,1,0:T(8,128)(2,1)S(1)} collective-permute-done((bf16[3,3,32,128]{3,2,1,0:T(8,128)(2,1)S(1)}, bf16[3,3,32,128]{3,2,1,0:T(8,128)(2,1)S(1)}, u32[]{:S(2)}, u32[]{:S(2)}) %collective-permute-start.12) | collective-permute-done | bytes 73760 | tf_op jit(solution)/shard_map/ppermute | solution.py:42
  44.0 0.7 %shard_map.44 = f32[3,5,32,128]{3,2,1,0:T(8,128)} custom-call(f32[3,3,32,128]{3,2,1,0:T(8,128)S(1)} %get-tuple-element.53.refs_0_, bf16[3,3,32,128]{3,2,1,0:T(8,128)(2,1)S(1)} %collective-permute-done.10.refs_1_, bf16[3,3,32,128]{3,2,1,0:T(8,128)(2,1)S(1)} %collective-permute-done.11.refs_2_, bf16[3,3,32,128]{3,2,1,0:T(8,128)(2,1)S(1)} %collective-permute-done.12.refs_3_, ...), custom_call_target="tpu_custom_call" | custom-call | tf_op jit(solution)/shard_map/pallas_call | solution.py:58
  (10 shorter events, 0.0 us)
Async XLA Ops:
  0.0 4.7 %copy-start.1 = (f32[4,8,128]{2,1,0:T(8,128)S(1)}, f32[4,8,128]{2,1,0:T(8,128)}, u32[]{:S(2)}) copy-start(f32[4,8,128]{2,1,0:T(8,128)} %refs_4_.1) | copy-start | bytes 49156
  0.0 4.7 %copy-start = (f32[3,4,8,128]{3,2,1,0:T(8,128)S(1)}, f32[3,4,8,128]{3,2,1,0:T(8,128)}, u32[]{:S(2)}) copy-start(f32[3,4,8,128]{3,2,1,0:T(8,128)} %refs_5_.1) | copy-start | bytes 147460
  0.0 28.4 %collective-permute-start.5 = (bf16[128,4,8,128]{3,2,1,0:T(8,128)(2,1)}, bf16[128,4,8,128]{3,2,1,0:T(8,128)(2,1)S(1)}, u32[]{:S(2)}, u32[]{:S(2)}) collective-permute-start(bf16[128,4,8,128]{3,2,1,0:T(8,128)(2,1)} %param.3), channel_id=1, source_target_pairs={{24,0},{28,4},{0,8},{4,12},{8,16},{12,20},{16,24},{20,28},{25,1},{... | collective-permute-start | bytes 3145736 | tf_op jit(solution)/shard_map/ppermute | solution.py:24
  4.9 9.2 %collective-permute-start = (bf16[128,1280]{1,0:T(8,128)(2,1)S(1)}, bf16[128,1280]{1,0:T(8,128)(2,1)S(1)}, u32[]{:S(2)}, u32[]{:S(2)}) collective-permute-start(bf16[128,1280]{1,0:T(8,128)(2,1)S(1)} %get-tuple-element.34), channel_id=1, source_target_pairs={{1,0},{0,1},{3,2},{2,3},{5,4},{4,5},{7,6},{6,7},{9,8},{8,9},{11,10... | collective-permute-start | bytes 983048 | tf_op jit(solution)/shard_map/ppermute | solution.py:24
  6.4 9.9 %collective-permute-start.1 = (bf16[128,1152]{1,0:T(8,128)(2,1)S(1)}, bf16[128,1152]{1,0:T(8,128)(2,1)S(1)}, u32[]{:S(2)}, u32[]{:S(2)}) collective-permute-start(bf16[128,1152]{1,0:T(8,128)(2,1)S(1)} %get-tuple-element.36), channel_id=1, source_target_pairs={{2,0},{0,2},{3,1},{1,3},{6,4},{4,6},{7,5},{5,7},{10,8},{8,10},{11,... | collective-permute-start | bytes 884744 | tf_op jit(solution)/shard_map/ppermute | solution.py:24
  8.0 13.0 %collective-permute-start.2 = (bf16[128,1152]{1,0:T(8,128)(2,1)S(1)}, bf16[128,1152]{1,0:T(8,128)(2,1)S(1)}, u32[]{:S(2)}, u32[]{:S(2)}) collective-permute-start(bf16[128,1152]{1,0:T(8,128)(2,1)S(1)} %get-tuple-element.37), channel_id=1, source_target_pairs={{2,0},{0,2},{3,1},{1,3},{6,4},{4,6},{7,5},{5,7},{10,8},{8,10},{11,... | collective-permute-start | bytes 884744 | tf_op jit(solution)/shard_map/ppermute | solution.py:24
  21.0 8.0 %collective-permute-start.3 = (bf16[384,2048]{1,0:T(8,128)(2,1)S(1)}, bf16[384,2048]{1,0:T(8,128)(2,1)S(1)}, u32[]{:S(2)}, u32[]{:S(2)}) collective-permute-start(bf16[384,2048]{1,0:T(8,128)(2,1)S(1)} %get-tuple-element.35.refs_0_), channel_id=1, source_target_pairs={{0,4},{4,0},{8,12},{12,8},{16,20},{20,16},{24,28},{28,24},{1,5},{5... | collective-permute-start | bytes 4718600 | tf_op jit(solution)/shard_map/ppermute | solution.py:317
  22.9 6.1 %collective-permute-start.4 = (bf16[384,2048]{1,0:T(8,128)(2,1)S(1)}, bf16[384,2048]{1,0:T(8,128)(2,1)S(1)}, u32[]{:S(2)}, u32[]{:S(2)}) collective-permute-start(bf16[384,2048]{1,0:T(8,128)(2,1)S(1)} %get-tuple-element.41.refs_1_), channel_id=1, source_target_pairs={{0,4},{4,0},{8,12},{12,8},{16,20},{20,16},{24,28},{28,24},{1,5},{5... | collective-permute-start | bytes 4718600 | tf_op jit(solution)/shard_map/ppermute | solution.py:317
  28.9 5.8 %collective-permute-start.9 = (bf16[128,4096]{1,0:T(8,128)(2,1)S(1)}, bf16[128,4096]{1,0:T(8,128)(2,1)S(1)}, u32[]{:S(2)}, u32[]{:S(2)}) collective-permute-start(bf16[128,4096]{1,0:T(8,128)(2,1)S(1)} %bitcast.15), channel_id=1, source_target_pairs={{0,4},{4,0},{8,12},{12,8},{16,20},{20,16},{24,28},{28,24},{1,5},{5... | collective-permute-start | bytes 3145736 | tf_op jit(solution)/shard_map/ppermute | solution.py:330
  31.1 7.7 %collective-permute-start.6 = (bf16[2,3,32,128]{3,2,1,0:T(8,128)(2,1)S(1)}, bf16[2,3,32,128]{3,2,1,0:T(8,128)(2,1)S(1)}, u32[]{:S(2)}, u32[]{:S(2)}) collective-permute-start(bf16[2,3,32,128]{3,2,1,0:T(8,128)(2,1)S(1)} %get-tuple-element.46), channel_id=1, source_target_pairs={{0,1},{1,0},{2,3},{3,2},{4,5},{5,4},{6,7},{7,6},{8,9},{9,8},{10,11... | collective-permute-start | bytes 147464 | tf_op jit(solution)/shard_map/ppermute | solution.py:42
  32.7 6.6 %collective-permute-start.7 = (bf16[2,3,32,128]{3,2,1,0:T(8,128)(2,1)S(1)}, bf16[2,3,32,128]{3,2,1,0:T(8,128)(2,1)S(1)}, u32[]{:S(2)}, u32[]{:S(2)}) collective-permute-start(bf16[2,3,32,128]{3,2,1,0:T(8,128)(2,1)S(1)} %get-tuple-element.47), channel_id=1, source_target_pairs={{0,2},{1,3},{2,0},{3,1},{4,6},{5,7},{6,4},{7,5},{8,10},{9,11},{10,... | collective-permute-start | bytes 147464 | tf_op jit(solution)/shard_map/ppermute | solution.py:42
  34.2 5.2 %collective-permute-start.8 = (bf16[2,3,32,128]{3,2,1,0:T(8,128)(2,1)S(1)}, bf16[2,3,32,128]{3,2,1,0:T(8,128)(2,1)S(1)}, u32[]{:S(2)}, u32[]{:S(2)}) collective-permute-start(bf16[2,3,32,128]{3,2,1,0:T(8,128)(2,1)S(1)} %get-tuple-element.48), channel_id=1, source_target_pairs={{0,3},{1,2},{2,1},{3,0},{4,7},{5,6},{6,5},{7,4},{8,11},{9,10},{10,... | collective-permute-start | bytes 147464 | tf_op jit(solution)/shard_map/ppermute | solution.py:42
  35.7 7.9 %collective-permute-start.10 = (bf16[3,3,32,128]{3,2,1,0:T(8,128)(2,1)S(1)}, bf16[3,3,32,128]{3,2,1,0:T(8,128)(2,1)S(1)}, u32[]{:S(2)}, u32[]{:S(2)}) collective-permute-start(bf16[3,3,32,128]{3,2,1,0:T(8,128)(2,1)S(1)} %get-tuple-element.54), channel_id=1, source_target_pairs={{0,1},{1,0},{2,3},{3,2},{4,5},{5,4},{6,7},{7,6},{8,9},{9,8},{10,11... | collective-permute-start | bytes 221192 | tf_op jit(solution)/shard_map/ppermute | solution.py:42
  37.3 6.3 %collective-permute-start.11 = (bf16[3,3,32,128]{3,2,1,0:T(8,128)(2,1)S(1)}, bf16[3,3,32,128]{3,2,1,0:T(8,128)(2,1)S(1)}, u32[]{:S(2)}, u32[]{:S(2)}) collective-permute-start(bf16[3,3,32,128]{3,2,1,0:T(8,128)(2,1)S(1)} %get-tuple-element.55), channel_id=1, source_target_pairs={{0,2},{1,3},{2,0},{3,1},{4,6},{5,7},{6,4},{7,5},{8,10},{9,11},{10,... | collective-permute-start | bytes 221192 | tf_op jit(solution)/shard_map/ppermute | solution.py:42
  38.8 5.3 %collective-permute-start.12 = (bf16[3,3,32,128]{3,2,1,0:T(8,128)(2,1)S(1)}, bf16[3,3,32,128]{3,2,1,0:T(8,128)(2,1)S(1)}, u32[]{:S(2)}, u32[]{:S(2)}) collective-permute-start(bf16[3,3,32,128]{3,2,1,0:T(8,128)(2,1)S(1)} %get-tuple-element.56), channel_id=1, source_target_pairs={{0,3},{1,2},{2,1},{3,0},{4,7},{5,6},{6,5},{7,4},{8,11},{9,10},{10,... | collective-permute-start | bytes 221192 | tf_op jit(solution)/shard_map/ppermute | solution.py:42
  39.4 4.1 %collective-permute-start.13 = (bf16[2,3,32,128]{3,2,1,0:T(8,128)(2,1)S(1)}, bf16[2,3,32,128]{3,2,1,0:T(8,128)(2,1)S(1)}, u32[]{:S(2)}, u32[]{:S(2)}) collective-permute-start(bf16[2,3,32,128]{3,2,1,0:T(8,128)(2,1)S(1)} %get-tuple-element.62), channel_id=1, source_target_pairs={{8,0},{12,4},{16,8},{20,12},{24,16},{28,20},{0,24},{4,28},{9,1},{1... | collective-permute-start | bytes 147464 | tf_op jit(solution)/shard_map/ppermute | solution.py:24

commit v16 on v12

--- a/solution.py
+++ b/solution.py
@@ -34,7 +34,7 @@
 def exchange(sends):
     nx, ny = lax.axis_size("dx"), lax.axis_size("dy")
     got = []
-    for o, piece in enumerate(sends, 1):
+    for o, piece in reversed(list(enumerate(sends, 1))):
         ox, oy = o // ny, o % ny
         route = [
             (i * ny + j, ((i + ox) % nx) * ny + (j + oy) % ny) for i in range(nx) for j in range(ny)

time: 44.9 us -> 44.9 us (level); the launches traced: 44.8 us -> 44.2 us
  waiting for transfers between devices: 16.8 us -> 16.3 us
    ppermute x6, waiting for transfers between devices: 0.6 us -> 0.02 us  [exchange(): got.append(lax.ppermute(piece, ('dx', 'dy'), route))]
  transfers between devices with their start and end apart: 15 -> 15, of which waited for: 7 -> 5; matrix products, arithmetic and copies ran while one was open for 5% -> 5% of each run, Pallas kernels for 18% -> 18%
where the time goes in v16:
time: 44.9 us; the launch traced here: 44.2 us
  starting transfers between devices  16.8 us (37%)
  waiting for transfers between devices  16.3 us (36%)
  Pallas kernels  8.88 us (20%)
  local copies, waits for them, and re-layouts  2.16 us (5%)
    ppermute x5, waiting for transfers between devices, shift(): lax.ppermute(block, axis, [((i + distance) % count, i) for i in range(cou...  16.2 us
    pallas_call x8, Pallas kernels, call(): return list(run(*operands))  8.88 us
    ppermute x5, starting transfers between devices, shift(): lax.ppermute(block, axis, [((i + distance) % count, i) for i in range(cou...  8.4 us
    ppermute x6, starting transfers between devices, exchange(): got.append(lax.ppermute(piece, ('dx', 'dy'), route))  7.11 us
    unnamed x6, local copies, waits for them, and re-layouts  2.16 us
  transfers between devices with their start and end apart: 15, of which 5 were waited for; matrix products, arithmetic and copies ran while one was open for 5% of the time, Pallas kernels for 18%

profile of v16, /device:TPU:0, one launch (start us, length us, event | category | flops | bytes accessed | tf_op | source)
XLA Modules:
  0.0 44.2 jit_solution(7557730527928187666)
XLA Ops:
  0.0 3.0 %collective-permute-start.5 = (bf16[128,4,8,128]{3,2,1,0:T(8,128)(2,1)}, bf16[128,4,8,128]{3,2,1,0:T(8,128)(2,1)S(1)}, u32[]{:S(2)}, u32[]{:S(2)}) collective-permute-start(bf16[128,4,8,128]{3,2,1,0:T(8,128)(2,1)} %param.3), channel_id=1, source_target_pairs={{24,0},{28,4},{0,8},{4,12},{8,16},{12,20},{16,24},{20,28},{25,1},{... | collective-permute-start | bytes 3145736 | tf_op jit(solution)/shard_map/ppermute | solution.py:24
  3.0 1.7 %copy.9 = bf16[16,8,32,128]{3,1,2,0:T(8,128)(2,1)S(1)} copy(bf16[16,8,32,128]{3,2,1,0:T(8,128)(2,1)} %bitcast.18) | data formatting | bytes 2097152
  4.8 0.1 shard_map.37
  4.9 1.6 %collective-permute-start = (bf16[128,1280]{1,0:T(8,128)(2,1)S(1)}, bf16[128,1280]{1,0:T(8,128)(2,1)S(1)}, u32[]{:S(2)}, u32[]{:S(2)}) collective-permute-start(bf16[128,1280]{1,0:T(8,128)(2,1)S(1)} %get-tuple-element.34), channel_id=1, source_target_pairs={{1,0},{0,1},{3,2},{2,3},{5,4},{4,5},{7,6},{6,7},{9,8},{8,9},{11,10... | collective-permute-start | bytes 983048 | tf_op jit(solution)/shard_map/ppermute | solution.py:24
  6.4 1.5 %collective-permute-start.1 = (bf16[128,1152]{1,0:T(8,128)(2,1)S(1)}, bf16[128,1152]{1,0:T(8,128)(2,1)S(1)}, u32[]{:S(2)}, u32[]{:S(2)}) collective-permute-start(bf16[128,1152]{1,0:T(8,128)(2,1)S(1)} %get-tuple-element.36), channel_id=1, source_target_pairs={{2,0},{0,2},{3,1},{1,3},{6,4},{4,6},{7,5},{5,7},{10,8},{8,10},{11,... | collective-permute-start | bytes 884744 | tf_op jit(solution)/shard_map/ppermute | solution.py:24
  8.0 0.5 %collective-permute-start.2 = (bf16[128,1152]{1,0:T(8,128)(2,1)S(1)}, bf16[128,1152]{1,0:T(8,128)(2,1)S(1)}, u32[]{:S(2)}, u32[]{:S(2)}) collective-permute-start(bf16[128,1152]{1,0:T(8,128)(2,1)S(1)} %get-tuple-element.37), channel_id=1, source_target_pairs={{2,0},{0,2},{3,1},{1,3},{6,4},{4,6},{7,5},{5,7},{10,8},{8,10},{11,... | collective-permute-start | bytes 884744 | tf_op jit(solution)/shard_map/ppermute | solution.py:24
  8.5 5.7 %collective-permute-done.refs_1_.refs_3_ = bf16[128,1280]{1,0:T(8,128)(2,1)S(1)} collective-permute-done((bf16[128,1280]{1,0:T(8,128)(2,1)S(1)}, bf16[128,1280]{1,0:T(8,128)(2,1)S(1)}, u32[]{:S(2)}, u32[]{:S(2)}) %collective-permute-start) | collective-permute-done | bytes 327712 | tf_op jit(solution)/shard_map/ppermute | solution.py:24
  14.1 1.9 %shard_map.38 = (bf16[384,2048]{1,0:T(8,128)(2,1)S(1)}, bf16[384,2048]{1,0:T(8,128)(2,1)S(1)}) custom-call(bf16[128,4096]{1,0:T(8,128)(2,1)S(1)} %bitcast.11, bf16[128,1280]{1,0:T(8,128)(2,1)S(1)} %collective-permute-done.refs_1_.refs_3_, f32[4,8,128]{2,1,0:T(8,128)S(1)} %copy-done.1, f32[3,4,8,128]{3,2,1,0:T(8,128)S(1)} %copy-done), custom_call_target="tpu_custom_call" | custom-call | tf_op jit(solution)/shard_map/pallas_call | solution.py:58
  16.0 0.4 collective-permute-done.1.refs_1_
  16.4 4.6 %collective-permute-done.2.refs_2_ = bf16[128,1152]{1,0:T(8,128)(2,1)S(1)} collective-permute-done((bf16[128,1152]{1,0:T(8,128)(2,1)S(1)}, bf16[128,1152]{1,0:T(8,128)(2,1)S(1)}, u32[]{:S(2)}, u32[]{:S(2)}) %collective-permute-start.2) | collective-permute-done | bytes 294944 | tf_op jit(solution)/shard_map/ppermute | solution.py:24
  21.0 1.9 %shard_map.39 = (bf16[384,2048]{1,0:T(8,128)(2,1)S(1)}, bf16[384,2048]{1,0:T(8,128)(2,1)S(1)}) custom-call(bf16[128,4096]{1,0:T(8,128)(2,1)S(1)} %bitcast.12, bf16[128,1152]{1,0:T(8,128)(2,1)S(1)} %collective-permute-done.1.refs_1_, bf16[128,1152]{1,0:T(8,128)(2,1)S(1)} %collective-permute-done.2.refs_2_, ...), custom_call_target="tpu_custom_call" | custom-call | tf_op jit(solution)/shard_map/pallas_call | solution.py:58
  22.9 0.6 %collective-permute-start.4 = (bf16[384,2048]{1,0:T(8,128)(2,1)S(1)}, bf16[384,2048]{1,0:T(8,128)(2,1)S(1)}, u32[]{:S(2)}, u32[]{:S(2)}) collective-permute-start(bf16[384,2048]{1,0:T(8,128)(2,1)S(1)} %get-tuple-element.41.refs_1_), channel_id=1, source_target_pairs={{0,4},{4,0},{8,12},{12,8},{16,20},{20,16},{24,28},{28,24},{1,5},{5... | collective-permute-start | bytes 4718600 | tf_op jit(solution)/shard_map/ppermute | solution.py:316
  23.5 1.0 %shard_map.40.refs_6_.refs_4_ = f32[384,128]{1,0:T(8,128)S(1)} custom-call(bf16[384,2048]{1,0:T(8,128)(2,1)S(1)} %get-tuple-element.42.refs_0_, bf16[384,2048]{1,0:T(8,128)(2,1)S(1)} %get-tuple-element.43.refs_1_, bf16[128,4096]{1,0:T(8,128)(2,1)S(1)} %bitcast.13), custom_call_target="tpu_custom_call" | custom-call | tf_op jit(solution)/shard_map/pallas_call | solution.py:58
  24.4 4.0 %collective-permute-done.5 = bf16[128,4,8,128]{3,2,1,0:T(8,128)(2,1)S(1)} collective-permute-done((bf16[128,4,8,128]{3,2,1,0:T(8,128)(2,1)}, bf16[128,4,8,128]{3,2,1,0:T(8,128)(2,1)S(1)}, u32[]{:S(2)}, u32[]{:S(2)}) %collective-permute-start.5) | collective-permute-done | bytes 1048608 | tf_op jit(solution)/shard_map/ppermute | solution.py:24
  28.4 0.5 %copy.8 = bf16[16,8,32,128]{3,1,2,0:T(8,128)(2,1)S(1)} copy(bf16[16,8,32,128]{3,2,1,0:T(8,128)(2,1)S(1)} %bitcast.19) | data formatting | bytes 2097152
  28.9 0.1 collective-permute-start.9
  29.0 0.0 collective-permute-done.3.refs_2_
  29.0 0.0 collective-permute-done.4.refs_3_
  29.0 2.1 %shard_map.41 = (f32[128,384]{1,0:T(8,128)S(1)}, f32[2,3,32,128]{3,2,1,0:T(8,128)S(1)}, bf16[2,3,32,128]{3,2,1,0:T(8,128)(2,1)S(1)}, bf16[2,3,32,128]{3,2,1,0:T(8,128)(2,1)S(1)}, bf16[2,3,32,128]{3,2,1,0:T(8,128)(2,1)S(1)}) custom-call(bf16[384,2048]{1,0:T(8,128)(2,1)S(1)} %get-tuple-element.35.refs_0_, bf16[384,2048]{1,0:T(8,128)(2,1)S(1)} %get-tuple-element.41.refs_1_, ...), custom_call_target="tpu_custom_call" | custom-call | bytes 3000000 | tf_op jit(solution)/shard_map/pallas_call | solution.py:58
  31.1 2.5 %collective-permute-start.6 = (bf16[2,3,32,128]{3,2,1,0:T(8,128)(2,1)S(1)}, bf16[2,3,32,128]{3,2,1,0:T(8,128)(2,1)S(1)}, u32[]{:S(2)}, u32[]{:S(2)}) collective-permute-start(bf16[2,3,32,128]{3,2,1,0:T(8,128)(2,1)S(1)} %get-tuple-element.46), channel_id=1, source_target_pairs={{0,3},{1,2},{2,1},{3,0},{4,7},{5,6},{6,5},{7,4},{8,11},{9,10},{10,... | collective-permute-start | bytes 147464 | tf_op jit(solution)/shard_map/ppermute | solution.py:42
  33.6 0.5 %collective-permute-start.7 = (bf16[2,3,32,128]{3,2,1,0:T(8,128)(2,1)S(1)}, bf16[2,3,32,128]{3,2,1,0:T(8,128)(2,1)S(1)}, u32[]{:S(2)}, u32[]{:S(2)}) collective-permute-start(bf16[2,3,32,128]{3,2,1,0:T(8,128)(2,1)S(1)} %get-tuple-element.47), channel_id=1, source_target_pairs={{0,2},{1,3},{2,0},{3,1},{4,6},{5,7},{6,4},{7,5},{8,10},{9,11},{10,... | collective-permute-start | bytes 147464 | tf_op jit(solution)/shard_map/ppermute | solution.py:42
  34.1 0.5 %collective-permute-start.8 = (bf16[2,3,32,128]{3,2,1,0:T(8,128)(2,1)S(1)}, bf16[2,3,32,128]{3,2,1,0:T(8,128)(2,1)S(1)}, u32[]{:S(2)}, u32[]{:S(2)}) collective-permute-start(bf16[2,3,32,128]{3,2,1,0:T(8,128)(2,1)S(1)} %get-tuple-element.48), channel_id=1, source_target_pairs={{0,1},{1,0},{2,3},{3,2},{4,5},{5,4},{6,7},{7,6},{8,9},{9,8},{10,11... | collective-permute-start | bytes 147464 | tf_op jit(solution)/shard_map/ppermute | solution.py:42
  34.7 1.0 %shard_map.42 = (f32[3,3,32,128]{3,2,1,0:T(8,128)S(1)}, bf16[3,3,32,128]{3,2,1,0:T(8,128)(2,1)S(1)}, bf16[3,3,32,128]{3,2,1,0:T(8,128)(2,1)S(1)}, bf16[3,3,32,128]{3,2,1,0:T(8,128)(2,1)S(1)}) custom-call(bf16[384,2048]{1,0:T(8,128)(2,1)S(1)} %get-tuple-element.42.refs_0_, bf16[384,2048]{1,0:T(8,128)(2,1)S(1)} %get-tuple-element.43.refs_1_, ...), custom_call_target="tpu_custom_call" | custom-call | bytes 3000000 | tf_op jit(solution)/shard_map/pallas_call | solution.py:58
  35.7 2.5 %collective-permute-start.10 = (bf16[3,3,32,128]{3,2,1,0:T(8,128)(2,1)S(1)}, bf16[3,3,32,128]{3,2,1,0:T(8,128)(2,1)S(1)}, u32[]{:S(2)}, u32[]{:S(2)}) collective-permute-start(bf16[3,3,32,128]{3,2,1,0:T(8,128)(2,1)S(1)} %get-tuple-element.54), channel_id=1, source_target_pairs={{0,3},{1,2},{2,1},{3,0},{4,7},{5,6},{6,5},{7,4},{8,11},{9,10},{10,... | collective-permute-start | bytes 221192 | tf_op jit(solution)/shard_map/ppermute | solution.py:42
  38.2 0.5 %collective-permute-start.11 = (bf16[3,3,32,128]{3,2,1,0:T(8,128)(2,1)S(1)}, bf16[3,3,32,128]{3,2,1,0:T(8,128)(2,1)S(1)}, u32[]{:S(2)}, u32[]{:S(2)}) collective-permute-start(bf16[3,3,32,128]{3,2,1,0:T(8,128)(2,1)S(1)} %get-tuple-element.55), channel_id=1, source_target_pairs={{0,2},{1,3},{2,0},{3,1},{4,6},{5,7},{6,4},{7,5},{8,10},{9,11},{10,... | collective-permute-start | bytes 221192 | tf_op jit(solution)/shard_map/ppermute | solution.py:42
  38.7 0.5 %collective-permute-start.12 = (bf16[3,3,32,128]{3,2,1,0:T(8,128)(2,1)S(1)}, bf16[3,3,32,128]{3,2,1,0:T(8,128)(2,1)S(1)}, u32[]{:S(2)}, u32[]{:S(2)}) collective-permute-start(bf16[3,3,32,128]{3,2,1,0:T(8,128)(2,1)S(1)} %get-tuple-element.56), channel_id=1, source_target_pairs={{0,1},{1,0},{2,3},{3,2},{4,5},{5,4},{6,7},{7,6},{8,9},{9,8},{10,11... | collective-permute-start | bytes 221192 | tf_op jit(solution)/shard_map/ppermute | solution.py:42
  39.3 0.0 collective-permute-done.7.refs_2_
  39.3 0.0 collective-permute-done.8.refs_3_
  39.3 1.8 %collective-permute-start.13 = (f32[3,32,128]{2,1,0:T(8,128)S(1)}, f32[3,32,128]{2,1,0:T(8,128)S(1)}, u32[]{:S(2)}, u32[]{:S(2)}) collective-permute-start(f32[3,32,128]{2,1,0:T(8,128)S(1)} %get-tuple-element.62), channel_id=1, source_target_pairs={{8,0},{12,4},{16,8},{20,12},{24,16},{28,20},{0,24},{4,28},{9,1},{1... | collective-permute-start | bytes 147464 | tf_op jit(solution)/shard_map/ppermute | solution.py:24
  41.1 0.7 %collective-permute-start.14 = (f32[3,32,128]{2,1,0:T(8,128)S(1)}, f32[3,32,128]{2,1,0:T(8,128)S(1)}, u32[]{:S(2)}, u32[]{:S(2)}) collective-permute-start(f32[3,32,128]{2,1,0:T(8,128)S(1)} %get-tuple-element.61.refs_4_), channel_id=1, source_target_pairs={{12,4},{20,12},{28,20},{4,28},{13,5},{21,13},{29,21},{5,29},{14,6}... | collective-permute-start | bytes 147464 | tf_op jit(solution)/shard_map/ppermute | solution.py:353
  41.8 1.7 %collective-permute-done.13.refs_5_ = f32[3,32,128]{2,1,0:T(8,128)S(1)} collective-permute-done((f32[3,32,128]{2,1,0:T(8,128)S(1)}, f32[3,32,128]{2,1,0:T(8,128)S(1)}, u32[]{:S(2)}, u32[]{:S(2)}) %collective-permute-start.13) | collective-permute-done | bytes 49184 | tf_op jit(solution)/shard_map/ppermute | solution.py:24
  43.5 0.7 %shard_map.44 = f32[3,5,32,128]{3,2,1,0:T(8,128)} custom-call(f32[3,3,32,128]{3,2,1,0:T(8,128)S(1)} %get-tuple-element.53.refs_0_, bf16[3,3,32,128]{3,2,1,0:T(8,128)(2,1)S(1)} %collective-permute-done.10.refs_1_, bf16[3,3,32,128]{3,2,1,0:T(8,128)(2,1)S(1)} %collective-permute-done.11.refs_2_, bf16[3,3,32,128]{3,2,1,0:T(8,128)(2,1)S(1)} %collective-permute-done.12.refs_3_, ...), custom_call_target="tpu_custom_call" | custom-call | tf_op jit(solution)/shard_map/pallas_call | solution.py:58
  (12 shorter events, 0.0 us)
Async XLA Ops:
  0.0 4.7 %copy-start.1 = (f32[4,8,128]{2,1,0:T(8,128)S(1)}, f32[4,8,128]{2,1,0:T(8,128)}, u32[]{:S(2)}) copy-start(f32[4,8,128]{2,1,0:T(8,128)} %refs_4_.1) | copy-start | bytes 49156
  0.0 4.7 %copy-start = (f32[3,4,8,128]{3,2,1,0:T(8,128)S(1)}, f32[3,4,8,128]{3,2,1,0:T(8,128)}, u32[]{:S(2)}) copy-start(f32[3,4,8,128]{3,2,1,0:T(8,128)} %refs_5_.1) | copy-start | bytes 147460
  0.0 28.4 %collective-permute-start.5 = (bf16[128,4,8,128]{3,2,1,0:T(8,128)(2,1)}, bf16[128,4,8,128]{3,2,1,0:T(8,128)(2,1)S(1)}, u32[]{:S(2)}, u32[]{:S(2)}) collective-permute-start(bf16[128,4,8,128]{3,2,1,0:T(8,128)(2,1)} %param.3), channel_id=1, source_target_pairs={{24,0},{28,4},{0,8},{4,12},{8,16},{12,20},{16,24},{20,28},{25,1},{... | collective-permute-start | bytes 3145736 | tf_op jit(solution)/shard_map/ppermute | solution.py:24
  4.9 9.2 %collective-permute-start = (bf16[128,1280]{1,0:T(8,128)(2,1)S(1)}, bf16[128,1280]{1,0:T(8,128)(2,1)S(1)}, u32[]{:S(2)}, u32[]{:S(2)}) collective-permute-start(bf16[128,1280]{1,0:T(8,128)(2,1)S(1)} %get-tuple-element.34), channel_id=1, source_target_pairs={{1,0},{0,1},{3,2},{2,3},{5,4},{4,5},{7,6},{6,7},{9,8},{8,9},{11,10... | collective-permute-start | bytes 983048 | tf_op jit(solution)/shard_map/ppermute | solution.py:24
  6.4 9.9 %collective-permute-start.1 = (bf16[128,1152]{1,0:T(8,128)(2,1)S(1)}, bf16[128,1152]{1,0:T(8,128)(2,1)S(1)}, u32[]{:S(2)}, u32[]{:S(2)}) collective-permute-start(bf16[128,1152]{1,0:T(8,128)(2,1)S(1)} %get-tuple-element.36), channel_id=1, source_target_pairs={{2,0},{0,2},{3,1},{1,3},{6,4},{4,6},{7,5},{5,7},{10,8},{8,10},{11,... | collective-permute-start | bytes 884744 | tf_op jit(solution)/shard_map/ppermute | solution.py:24
  8.0 13.0 %collective-permute-start.2 = (bf16[128,1152]{1,0:T(8,128)(2,1)S(1)}, bf16[128,1152]{1,0:T(8,128)(2,1)S(1)}, u32[]{:S(2)}, u32[]{:S(2)}) collective-permute-start(bf16[128,1152]{1,0:T(8,128)(2,1)S(1)} %get-tuple-element.37), channel_id=1, source_target_pairs={{2,0},{0,2},{3,1},{1,3},{6,4},{4,6},{7,5},{5,7},{10,8},{8,10},{11,... | collective-permute-start | bytes 884744 | tf_op jit(solution)/shard_map/ppermute | solution.py:24
  21.0 8.0 %collective-permute-start.3 = (bf16[384,2048]{1,0:T(8,128)(2,1)S(1)}, bf16[384,2048]{1,0:T(8,128)(2,1)S(1)}, u32[]{:S(2)}, u32[]{:S(2)}) collective-permute-start(bf16[384,2048]{1,0:T(8,128)(2,1)S(1)} %get-tuple-element.35.refs_0_), channel_id=1, source_target_pairs={{0,4},{4,0},{8,12},{12,8},{16,20},{20,16},{24,28},{28,24},{1,5},{5... | collective-permute-start | bytes 4718600 | tf_op jit(solution)/shard_map/ppermute | solution.py:316
  22.9 6.1 %collective-permute-start.4 = (bf16[384,2048]{1,0:T(8,128)(2,1)S(1)}, bf16[384,2048]{1,0:T(8,128)(2,1)S(1)}, u32[]{:S(2)}, u32[]{:S(2)}) collective-permute-start(bf16[384,2048]{1,0:T(8,128)(2,1)S(1)} %get-tuple-element.41.refs_1_), channel_id=1, source_target_pairs={{0,4},{4,0},{8,12},{12,8},{16,20},{20,16},{24,28},{28,24},{1,5},{5... | collective-permute-start | bytes 4718600 | tf_op jit(solution)/shard_map/ppermute | solution.py:316
  28.9 5.8 %collective-permute-start.9 = (bf16[128,4096]{1,0:T(8,128)(2,1)S(1)}, bf16[128,4096]{1,0:T(8,128)(2,1)S(1)}, u32[]{:S(2)}, u32[]{:S(2)}) collective-permute-start(bf16[128,4096]{1,0:T(8,128)(2,1)S(1)} %bitcast.15), channel_id=1, source_target_pairs={{0,4},{4,0},{8,12},{12,8},{16,20},{20,16},{24,28},{28,24},{1,5},{5... | collective-permute-start | bytes 3145736 | tf_op jit(solution)/shard_map/ppermute | solution.py:329
  31.1 7.6 %collective-permute-start.6 = (bf16[2,3,32,128]{3,2,1,0:T(8,128)(2,1)S(1)}, bf16[2,3,32,128]{3,2,1,0:T(8,128)(2,1)S(1)}, u32[]{:S(2)}, u32[]{:S(2)}) collective-permute-start(bf16[2,3,32,128]{3,2,1,0:T(8,128)(2,1)S(1)} %get-tuple-element.46), channel_id=1, source_target_pairs={{0,3},{1,2},{2,1},{3,0},{4,7},{5,6},{6,5},{7,4},{8,11},{9,10},{10,... | collective-permute-start | bytes 147464 | tf_op jit(solution)/shard_map/ppermute | solution.py:42
  33.6 5.7 %collective-permute-start.7 = (bf16[2,3,32,128]{3,2,1,0:T(8,128)(2,1)S(1)}, bf16[2,3,32,128]{3,2,1,0:T(8,128)(2,1)S(1)}, u32[]{:S(2)}, u32[]{:S(2)}) collective-permute-start(bf16[2,3,32,128]{3,2,1,0:T(8,128)(2,1)S(1)} %get-tuple-element.47), channel_id=1, source_target_pairs={{0,2},{1,3},{2,0},{3,1},{4,6},{5,7},{6,4},{7,5},{8,10},{9,11},{10,... | collective-permute-start | bytes 147464 | tf_op jit(solution)/shard_map/ppermute | solution.py:42
  34.1 5.1 %collective-permute-start.8 = (bf16[2,3,32,128]{3,2,1,0:T(8,128)(2,1)S(1)}, bf16[2,3,32,128]{3,2,1,0:T(8,128)(2,1)S(1)}, u32[]{:S(2)}, u32[]{:S(2)}) collective-permute-start(bf16[2,3,32,128]{3,2,1,0:T(8,128)(2,1)S(1)} %get-tuple-element.48), channel_id=1, source_target_pairs={{0,1},{1,0},{2,3},{3,2},{4,5},{5,4},{6,7},{7,6},{8,9},{9,8},{10,11... | collective-permute-start | bytes 147464 | tf_op jit(solution)/shard_map/ppermute | solution.py:42
  35.7 7.7 %collective-permute-start.10 = (bf16[3,3,32,128]{3,2,1,0:T(8,128)(2,1)S(1)}, bf16[3,3,32,128]{3,2,1,0:T(8,128)(2,1)S(1)}, u32[]{:S(2)}, u32[]{:S(2)}) collective-permute-start(bf16[3,3,32,128]{3,2,1,0:T(8,128)(2,1)S(1)} %get-tuple-element.54), channel_id=1, source_target_pairs={{0,3},{1,2},{2,1},{3,0},{4,7},{5,6},{6,5},{7,4},{8,11},{9,10},{10,... | collective-permute-start | bytes 221192 | tf_op jit(solution)/shard_map/ppermute | solution.py:42
  38.2 5.2 %collective-permute-start.11 = (bf16[3,3,32,128]{3,2,1,0:T(8,128)(2,1)S(1)}, bf16[3,3,32,128]{3,2,1,0:T(8,128)(2,1)S(1)}, u32[]{:S(2)}, u32[]{:S(2)}) collective-permute-start(bf16[3,3,32,128]{3,2,1,0:T(8,128)(2,1)S(1)} %get-tuple-element.55), channel_id=1, source_target_pairs={{0,2},{1,3},{2,0},{3,1},{4,6},{5,7},{6,4},{7,5},{8,10},{9,11},{10,... | collective-permute-start | bytes 221192 | tf_op jit(solution)/shard_map/ppermute | solution.py:42
  38.7 4.7 %collective-permute-start.12 = (bf16[3,3,32,128]{3,2,1,0:T(8,128)(2,1)S(1)}, bf16[3,3,32,128]{3,2,1,0:T(8,128)(2,1)S(1)}, u32[]{:S(2)}, u32[]{:S(2)}) collective-permute-start(bf16[3,3,32,128]{3,2,1,0:T(8,128)(2,1)S(1)} %get-tuple-element.56), channel_id=1, source_target_pairs={{0,1},{1,0},{2,3},{3,2},{4,5},{5,4},{6,7},{7,6},{8,9},{9,8},{10,11... | collective-permute-start | bytes 221192 | tf_op jit(solution)/shard_map/ppermute | solution.py:42
  39.3 4.1 %collective-permute-start.13 = (f32[3,32,128]{2,1,0:T(8,128)S(1)}, f32[3,32,128]{2,1,0:T(8,128)S(1)}, u32[]{:S(2)}, u32[]{:S(2)}) collective-permute-start(f32[3,32,128]{2,1,0:T(8,128)S(1)} %get-tuple-element.62), channel_id=1, source_target_pairs={{8,0},{12,4},{16,8},{20,12},{24,16},{28,20},{0,24},{4,28},{9,1},{1... | collective-permute-start | bytes 147464 | tf_op jit(solution)/shard_map/ppermute | solution.py:24
  41.1 2.3 %collective-permute-start.14 = (f32[3,32,128]{2,1,0:T(8,128)S(1)}, f32[3,32,128]{2,1,0:T(8,128)S(1)}, u32[]{:S(2)}, u32[]{:S(2)}) collective-permute-start(f32[3,32,128]{2,1,0:T(8,128)S(1)} %get-tuple-element.61.refs_4_), channel_id=1, source_target_pairs={{12,4},{20,12},{28,20},{4,28},{13,5},{21,13},{29,21},{5,29},{14,6}... | collective-permute-start | bytes 147464 | tf_op jit(solution)/shard_map/ppermute | solution.py:353

commit v17 on v15

--- a/solution.py
+++ b/solution.py
@@ -34,7 +34,7 @@
 def exchange(sends):
     nx, ny = lax.axis_size("dx"), lax.axis_size("dy")
     got = []
-    for o, piece in enumerate(sends, 1):
+    for o, piece in reversed(list(enumerate(sends, 1))):
         ox, oy = o // ny, o % ny
         route = [
             (i * ny + j, ((i + ox) % nx) * ny + (j + oy) % ny) for i in range(nx) for j in range(ny)
@@ -220,20 +220,14 @@
     return rows_of
 
 
-def either(first, second):
-    core = lax.rem(lax.axis_index("blk"), 2)
-    return lambda *place: jnp.where(core == 0, first(*place), second(*place))
-
-
 def there_tiles(*refs, layer, plane, scale):
-    w, w_mate, (two, psi, own), refs = refs[:2], refs[2:4], refs[4:7], refs[7:]
+    w, w_mate, (two, psi), refs = refs[:2], refs[2:4], refs[4:6], refs[6:]
     mate, outs, (there, there_mate) = refs[0], refs[1:-2], refs[-2:]
     states = two.shape[0]
     there[...] = product(w, stacked(two), layer, True) * scale
     both = product(w_mate, stacked(two, psi), layer, True) * scale
     there_mate[...], mate[...] = both[:states], both[states:]
-    slots = (wide_rows(there), either(tall_rows(own), wide_rows(there_mate)))
-    cut(outs, slots, plane, states)
+    cut(outs, (wide_rows(there), wide_rows(there_mate)), plane, states)
 
 
 def here_tiles(*refs, layer, plane, scale):
@@ -242,9 +236,7 @@
     states = two.shape[0]
     both = product(u, stacked(two, one), layer) * scale
     here_two[...], here_one[...] = both[:, :states], both[:, states:]
-    slots = (
-        tall_rows(here_two), wide_rows(mate), either(tall_rows(here_one), tall_rows(own))
-    )
+    slots = (tall_rows(here_two), tall_rows(here_one), tall_rows(own), wide_rows(mate))
     cut(outs, slots, plane, states)
 
 
@@ -256,23 +248,24 @@
 
 
 def add(*refs):
-    group, (ours, back) = refs[:-2], refs[-2:]
+    group, back = refs[:-1], refs[-1]
     for k in range(3):
-        total = total_of(group, 1, k)
-        ours[k], back[1, k] = total, total.astype(BF16)
-        back[0, k] = total_of(group, 0, k).astype(BF16)
+        total = total_of(group, 0, k)
+        back[0, k] = total.astype(BF16)
+        back[1, k] = (total - back[0, k].astype(F32)).astype(BF16)
+        back[2, k] = total_of(group, 1, k).astype(BF16)
 
 
 def assemble(*refs):
-    group, (ours, back, out) = refs[:-3], refs[-3:]
+    group, (back, out) = refs[:-2], refs[-2:]
     core = lax.rem(lax.axis_index("blk"), 2)
     for k in range(3):
-        mate, third = total_of(group, 1, k), total_of(group, 2, k)
+        mate = total_of(group, 3, k)
         out[k, 0] = total_of(group, 0, k)
-        out[k, 1] = jnp.where(core == 0, third, mate)
-        out[k, 2] = jnp.where(core == 0, ours[k], third)
-        out[k, 3] = jnp.where(core == 0, mate, back[1, k].astype(F32))
-        out[k, 4] = back[0, k].astype(F32)
+        out[k, 1] = jnp.where(core == 0, total_of(group, 1, k), mate)
+        out[k, 2] = total_of(group, 2, k)
+        out[k, 3] = jnp.where(core == 0, mate, back[2, k].astype(F32))
+        out[k, 4] = back[0, k].astype(F32) + back[1, k].astype(F32)
 
 
 def on_device(orbitals, coupling, pot_grad):
@@ -331,7 +324,7 @@
     mate, kept_there, *sends = call(
         functools.partial(there_tiles, **given),
         [wide, *cut_shapes(2)],
-        [*w, *w_mate, two, psi, own],
+        [*w, *w_mate, two, psi],
         scratch=[pltpu.VMEM(wide.shape, F32)] * 2,
         us=1,
     )
@@ -339,20 +332,17 @@
     one, mate = lax.optimization_barrier((one, mate))
     kept, *sends = call(
         functools.partial(here_tiles, **given),
-        cut_shapes(3),
+        cut_shapes(4),
         [*u, two, one, own, mate],
         scratch=[pltpu.VMEM(tall.shape, F32)] * 2,
         us=1,
     )
     second = exchange(sends)
     first, kept = lax.optimization_barrier((first, kept))
-    small = (3, rows, states)
-    ours, back = call(
-        add, [shape_of(small, F32), shape_of((2, *small), BF16)], [kept_there, *first]
-    )
+    (back,) = call(add, [shape_of((3, 3, rows, states), BF16)], [kept_there, *first])
     back = shift(back, "blk", 2)
     (out,) = call(
-        assemble, [shape_of((3, 5, rows, states), F32)], [kept, *second, ours, back]
+        assemble, [shape_of((3, 5, rows, states), F32)], [kept, *second, back]
     )
     return out
 

time: 44.9 us -> 44.6 us (level)
    ppermute x6, waiting for transfers between devices: 0.61 us -> 0.02 us  [exchange(): got.append(lax.ppermute(piece, ('dx', 'dy'), route))]
  transfers between devices with their start and end apart: 14 -> 14, of which waited for: 7 -> 5; matrix products, arithmetic and copies ran while one was open for 5% -> 5% of each run, Pallas kernels for 18% -> 18%
where the time goes in v17:
time: 44.6 us; the launch traced here: 44.5 us
  waiting for transfers between devices  17.2 us (39%)
  starting transfers between devices  16.2 us (36%)
  Pallas kernels  8.89 us (20%)
  local copies, waits for them, and re-layouts  2.16 us (5%)
    ppermute x5, waiting for transfers between devices, shift(): lax.ppermute(block, axis, [((i + distance) % count, i) for i in range(cou...  17.2 us
    pallas_call x8, Pallas kernels, call(): return list(run(*operands))  8.89 us
    ppermute x5, starting transfers between devices, shift(): lax.ppermute(block, axis, [((i + distance) % count, i) for i in range(cou...  8.4 us
    ppermute x6, starting transfers between devices, exchange(): got.append(lax.ppermute(piece, ('dx', 'dy'), route))  7.11 us
    unnamed x6, local copies, waits for them, and re-layouts  2.16 us
  transfers between devices with their start and end apart: 14, of which 5 were waited for; matrix products, arithmetic and copies ran while one was open for 5% of the time, Pallas kernels for 18%

profile of v17, /device:TPU:0, one launch (start us, length us, event | category | flops | bytes accessed | tf_op | source)
XLA Modules:
  0.0 44.5 jit_solution(5661393941120223217)
XLA Ops:
  0.0 3.0 %collective-permute-start.5 = (bf16[128,4,8,128]{3,2,1,0:T(8,128)(2,1)}, bf16[128,4,8,128]{3,2,1,0:T(8,128)(2,1)S(1)}, u32[]{:S(2)}, u32[]{:S(2)}) collective-permute-start(bf16[128,4,8,128]{3,2,1,0:T(8,128)(2,1)} %param.3), channel_id=1, source_target_pairs={{24,0},{28,4},{0,8},{4,12},{8,16},{12,20},{16,24},{20,28},{25,1},{... | collective-permute-start | bytes 3145736 | tf_op jit(solution)/shard_map/ppermute | solution.py:24
  3.0 1.7 %copy.9 = bf16[16,8,32,128]{3,1,2,0:T(8,128)(2,1)S(1)} copy(bf16[16,8,32,128]{3,2,1,0:T(8,128)(2,1)} %bitcast.18) | data formatting | bytes 2097152
  4.8 0.1 shard_map.37
  4.9 1.6 %collective-permute-start = (bf16[128,1280]{1,0:T(8,128)(2,1)S(1)}, bf16[128,1280]{1,0:T(8,128)(2,1)S(1)}, u32[]{:S(2)}, u32[]{:S(2)}) collective-permute-start(bf16[128,1280]{1,0:T(8,128)(2,1)S(1)} %get-tuple-element.32), channel_id=1, source_target_pairs={{1,0},{0,1},{3,2},{2,3},{5,4},{4,5},{7,6},{6,7},{9,8},{8,9},{11,10... | collective-permute-start | bytes 983048 | tf_op jit(solution)/shard_map/ppermute | solution.py:24
  6.4 1.5 %collective-permute-start.1 = (bf16[128,1152]{1,0:T(8,128)(2,1)S(1)}, bf16[128,1152]{1,0:T(8,128)(2,1)S(1)}, u32[]{:S(2)}, u32[]{:S(2)}) collective-permute-start(bf16[128,1152]{1,0:T(8,128)(2,1)S(1)} %get-tuple-element.34), channel_id=1, source_target_pairs={{2,0},{0,2},{3,1},{1,3},{6,4},{4,6},{7,5},{5,7},{10,8},{8,10},{11,... | collective-permute-start | bytes 884744 | tf_op jit(solution)/shard_map/ppermute | solution.py:24
  8.0 0.5 %collective-permute-start.2 = (bf16[128,1152]{1,0:T(8,128)(2,1)S(1)}, bf16[128,1152]{1,0:T(8,128)(2,1)S(1)}, u32[]{:S(2)}, u32[]{:S(2)}) collective-permute-start(bf16[128,1152]{1,0:T(8,128)(2,1)S(1)} %get-tuple-element.35), channel_id=1, source_target_pairs={{2,0},{0,2},{3,1},{1,3},{6,4},{4,6},{7,5},{5,7},{10,8},{8,10},{11,... | collective-permute-start | bytes 884744 | tf_op jit(solution)/shard_map/ppermute | solution.py:24
  8.5 5.7 %collective-permute-done.refs_1_.refs_3_ = bf16[128,1280]{1,0:T(8,128)(2,1)S(1)} collective-permute-done((bf16[128,1280]{1,0:T(8,128)(2,1)S(1)}, bf16[128,1280]{1,0:T(8,128)(2,1)S(1)}, u32[]{:S(2)}, u32[]{:S(2)}) %collective-permute-start) | collective-permute-done | bytes 327712 | tf_op jit(solution)/shard_map/ppermute | solution.py:24
  14.1 1.9 %shard_map.38 = (bf16[384,2048]{1,0:T(8,128)(2,1)S(1)}, bf16[384,2048]{1,0:T(8,128)(2,1)S(1)}) custom-call(bf16[128,4096]{1,0:T(8,128)(2,1)S(1)} %bitcast.11, bf16[128,1280]{1,0:T(8,128)(2,1)S(1)} %collective-permute-done.refs_1_.refs_3_, f32[4,8,128]{2,1,0:T(8,128)S(1)} %copy-done.1, f32[3,4,8,128]{3,2,1,0:T(8,128)S(1)} %copy-done), custom_call_target="tpu_custom_call" | custom-call | tf_op jit(solution)/shard_map/pallas_call | solution.py:58
  16.0 0.4 collective-permute-done.1.refs_1_
  16.4 4.6 %collective-permute-done.2.refs_2_ = bf16[128,1152]{1,0:T(8,128)(2,1)S(1)} collective-permute-done((bf16[128,1152]{1,0:T(8,128)(2,1)S(1)}, bf16[128,1152]{1,0:T(8,128)(2,1)S(1)}, u32[]{:S(2)}, u32[]{:S(2)}) %collective-permute-start.2) | collective-permute-done | bytes 294944 | tf_op jit(solution)/shard_map/ppermute | solution.py:24
  21.0 1.9 %shard_map.39 = (bf16[384,2048]{1,0:T(8,128)(2,1)S(1)}, bf16[384,2048]{1,0:T(8,128)(2,1)S(1)}) custom-call(bf16[128,4096]{1,0:T(8,128)(2,1)S(1)} %bitcast.12, bf16[128,1152]{1,0:T(8,128)(2,1)S(1)} %collective-permute-done.1.refs_1_, bf16[128,1152]{1,0:T(8,128)(2,1)S(1)} %collective-permute-done.2.refs_2_, ...), custom_call_target="tpu_custom_call" | custom-call | tf_op jit(solution)/shard_map/pallas_call | solution.py:58
  22.9 0.6 %collective-permute-start.4 = (bf16[384,2048]{1,0:T(8,128)(2,1)S(1)}, bf16[384,2048]{1,0:T(8,128)(2,1)S(1)}, u32[]{:S(2)}, u32[]{:S(2)}) collective-permute-start(bf16[384,2048]{1,0:T(8,128)(2,1)S(1)} %get-tuple-element.39.refs_1_), channel_id=1, source_target_pairs={{0,4},{4,0},{8,12},{12,8},{16,20},{20,16},{24,28},{28,24},{1,5},{5... | collective-permute-start | bytes 4718600 | tf_op jit(solution)/shard_map/ppermute | solution.py:310
  23.5 1.0 %shard_map.40.refs_4_ = f32[384,128]{1,0:T(8,128)S(1)} custom-call(bf16[384,2048]{1,0:T(8,128)(2,1)S(1)} %get-tuple-element.40.refs_0_, bf16[384,2048]{1,0:T(8,128)(2,1)S(1)} %get-tuple-element.41.refs_1_, bf16[128,4096]{1,0:T(8,128)(2,1)S(1)} %bitcast.13), custom_call_target="tpu_custom_call" | custom-call | tf_op jit(solution)/shard_map/pallas_call | solution.py:58
  24.4 4.0 %collective-permute-done.5 = bf16[128,4,8,128]{3,2,1,0:T(8,128)(2,1)S(1)} collective-permute-done((bf16[128,4,8,128]{3,2,1,0:T(8,128)(2,1)}, bf16[128,4,8,128]{3,2,1,0:T(8,128)(2,1)S(1)}, u32[]{:S(2)}, u32[]{:S(2)}) %collective-permute-start.5) | collective-permute-done | bytes 1048608 | tf_op jit(solution)/shard_map/ppermute | solution.py:24
  28.4 0.5 %copy.8 = bf16[16,8,32,128]{3,1,2,0:T(8,128)(2,1)S(1)} copy(bf16[16,8,32,128]{3,2,1,0:T(8,128)(2,1)S(1)} %bitcast.19) | data formatting | bytes 2097152
  28.9 0.1 collective-permute-start.9
  29.0 0.0 collective-permute-done.3.refs_2_
  29.0 0.0 collective-permute-done.4.refs_3_
  29.0 2.1 %shard_map.41 = (f32[128,384]{1,0:T(8,128)S(1)}, f32[2,3,32,128]{3,2,1,0:T(8,128)S(1)}, bf16[2,3,32,128]{3,2,1,0:T(8,128)(2,1)S(1)}, bf16[2,3,32,128]{3,2,1,0:T(8,128)(2,1)S(1)}, bf16[2,3,32,128]{3,2,1,0:T(8,128)(2,1)S(1)}) custom-call(bf16[384,2048]{1,0:T(8,128)(2,1)S(1)} %get-tuple-element.33.refs_0_, bf16[384,2048]{1,0:T(8,128)(2,1)S(1)} %get-tuple-element.39.refs_1_, ...), custom_call_target="tpu_custom_call" | custom-call | bytes 3000000 | tf_op jit(solution)/shard_map/pallas_call | solution.py:58
  31.1 2.5 %collective-permute-start.6 = (bf16[2,3,32,128]{3,2,1,0:T(8,128)(2,1)S(1)}, bf16[2,3,32,128]{3,2,1,0:T(8,128)(2,1)S(1)}, u32[]{:S(2)}, u32[]{:S(2)}) collective-permute-start(bf16[2,3,32,128]{3,2,1,0:T(8,128)(2,1)S(1)} %get-tuple-element.43), channel_id=1, source_target_pairs={{0,3},{1,2},{2,1},{3,0},{4,7},{5,6},{6,5},{7,4},{8,11},{9,10},{10,... | collective-permute-start | bytes 147464 | tf_op jit(solution)/shard_map/ppermute | solution.py:42
  33.6 0.5 %collective-permute-start.7 = (bf16[2,3,32,128]{3,2,1,0:T(8,128)(2,1)S(1)}, bf16[2,3,32,128]{3,2,1,0:T(8,128)(2,1)S(1)}, u32[]{:S(2)}, u32[]{:S(2)}) collective-permute-start(bf16[2,3,32,128]{3,2,1,0:T(8,128)(2,1)S(1)} %get-tuple-element.44), channel_id=1, source_target_pairs={{0,2},{1,3},{2,0},{3,1},{4,6},{5,7},{6,4},{7,5},{8,10},{9,11},{10,... | collective-permute-start | bytes 147464 | tf_op jit(solution)/shard_map/ppermute | solution.py:42
  34.1 0.5 %collective-permute-start.8 = (bf16[2,3,32,128]{3,2,1,0:T(8,128)(2,1)S(1)}, bf16[2,3,32,128]{3,2,1,0:T(8,128)(2,1)S(1)}, u32[]{:S(2)}, u32[]{:S(2)}) collective-permute-start(bf16[2,3,32,128]{3,2,1,0:T(8,128)(2,1)S(1)} %get-tuple-element.45), channel_id=1, source_target_pairs={{0,1},{1,0},{2,3},{3,2},{4,5},{5,4},{6,7},{7,6},{8,9},{9,8},{10,11... | collective-permute-start | bytes 147464 | tf_op jit(solution)/shard_map/ppermute | solution.py:42
  34.7 1.0 %shard_map.42 = (f32[4,3,32,128]{3,2,1,0:T(8,128)S(1)}, bf16[4,3,32,128]{3,2,1,0:T(8,128)(2,1)S(1)}, bf16[4,3,32,128]{3,2,1,0:T(8,128)(2,1)S(1)}, bf16[4,3,32,128]{3,2,1,0:T(8,128)(2,1)S(1)}) custom-call(bf16[384,2048]{1,0:T(8,128)(2,1)S(1)} %get-tuple-element.40.refs_0_, bf16[384,2048]{1,0:T(8,128)(2,1)S(1)} %get-tuple-element.41.refs_1_, ...), custom_call_target="tpu_custom_call" | custom-call | bytes 3000000 | tf_op jit(solution)/shard_map/pallas_call | solution.py:58
  35.7 2.5 %collective-permute-start.10 = (bf16[4,3,32,128]{3,2,1,0:T(8,128)(2,1)S(1)}, bf16[4,3,32,128]{3,2,1,0:T(8,128)(2,1)S(1)}, u32[]{:S(2)}, u32[]{:S(2)}) collective-permute-start(bf16[4,3,32,128]{3,2,1,0:T(8,128)(2,1)S(1)} %get-tuple-element.52), channel_id=1, source_target_pairs={{0,3},{1,2},{2,1},{3,0},{4,7},{5,6},{6,5},{7,4},{8,11},{9,10},{10,... | collective-permute-start | bytes 294920 | tf_op jit(solution)/shard_map/ppermute | solution.py:42
  38.2 0.5 %collective-permute-start.11 = (bf16[4,3,32,128]{3,2,1,0:T(8,128)(2,1)S(1)}, bf16[4,3,32,128]{3,2,1,0:T(8,128)(2,1)S(1)}, u32[]{:S(2)}, u32[]{:S(2)}) collective-permute-start(bf16[4,3,32,128]{3,2,1,0:T(8,128)(2,1)S(1)} %get-tuple-element.53), channel_id=1, source_target_pairs={{0,2},{1,3},{2,0},{3,1},{4,6},{5,7},{6,4},{7,5},{8,10},{9,11},{10,... | collective-permute-start | bytes 294920 | tf_op jit(solution)/shard_map/ppermute | solution.py:42
  38.7 0.0 collective-permute-done.6.refs_1_
  38.7 0.5 %collective-permute-start.12 = (bf16[4,3,32,128]{3,2,1,0:T(8,128)(2,1)S(1)}, bf16[4,3,32,128]{3,2,1,0:T(8,128)(2,1)S(1)}, u32[]{:S(2)}, u32[]{:S(2)}) collective-permute-start(bf16[4,3,32,128]{3,2,1,0:T(8,128)(2,1)S(1)} %get-tuple-element.54), channel_id=1, source_target_pairs={{0,1},{1,0},{2,3},{3,2},{4,5},{5,4},{6,7},{7,6},{8,9},{9,8},{10,11... | collective-permute-start | bytes 294920 | tf_op jit(solution)/shard_map/ppermute | solution.py:42
  39.3 0.0 collective-permute-done.7.refs_2_
  39.3 1.8 %collective-permute-start.13 = (bf16[3,3,32,128]{3,2,1,0:T(8,128)(2,1)S(1)}, bf16[3,3,32,128]{3,2,1,0:T(8,128)(2,1)S(1)}, u32[]{:S(2)}, u32[]{:S(2)}) collective-permute-start(bf16[3,3,32,128]{3,2,1,0:T(8,128)(2,1)S(1)} %shard_map.43), channel_id=1, source_target_pairs={{8,0},{12,4},{16,8},{20,12},{24,16},{28,20},{0,24},{4,28},{9,1},{1... | collective-permute-start | bytes 221192 | tf_op jit(solution)/shard_map/ppermute | solution.py:24
  41.1 2.6 %collective-permute-done.13.refs_4_ = bf16[3,3,32,128]{3,2,1,0:T(8,128)(2,1)S(1)} collective-permute-done((bf16[3,3,32,128]{3,2,1,0:T(8,128)(2,1)S(1)}, bf16[3,3,32,128]{3,2,1,0:T(8,128)(2,1)S(1)}, u32[]{:S(2)}, u32[]{:S(2)}) %collective-permute-start.13) | collective-permute-done | bytes 73760 | tf_op jit(solution)/shard_map/ppermute | solution.py:24
  43.7 0.0 collective-permute-done.10.refs_1_
  43.7 0.8 %shard_map.44 = f32[3,5,32,128]{3,2,1,0:T(8,128)} custom-call(f32[4,3,32,128]{3,2,1,0:T(8,128)S(1)} %get-tuple-element.51.refs_0_, bf16[4,3,32,128]{3,2,1,0:T(8,128)(2,1)S(1)} %collective-permute-done.10.refs_1_, bf16[4,3,32,128]{3,2,1,0:T(8,128)(2,1)S(1)} %collective-permute-done.11.refs_2_, bf16[4,3,32,128]{3,2,1,0:T(8,128)(2,1)S(1)} %collective-permute-done.12.refs_3_, ...), custom_call_target="tpu_custom_call" | custom-call | tf_op jit(solution)/shard_map/pallas_call | solution.py:58
  (10 shorter events, 0.1 us)
Async XLA Ops:
  0.0 4.7 %copy-start.1 = (f32[4,8,128]{2,1,0:T(8,128)S(1)}, f32[4,8,128]{2,1,0:T(8,128)}, u32[]{:S(2)}) copy-start(f32[4,8,128]{2,1,0:T(8,128)} %refs_4_.1) | copy-start | bytes 49156
  0.0 4.7 %copy-start = (f32[3,4,8,128]{3,2,1,0:T(8,128)S(1)}, f32[3,4,8,128]{3,2,1,0:T(8,128)}, u32[]{:S(2)}) copy-start(f32[3,4,8,128]{3,2,1,0:T(8,128)} %refs_5_.1) | copy-start | bytes 147460
  0.0 28.4 %collective-permute-start.5 = (bf16[128,4,8,128]{3,2,1,0:T(8,128)(2,1)}, bf16[128,4,8,128]{3,2,1,0:T(8,128)(2,1)S(1)}, u32[]{:S(2)}, u32[]{:S(2)}) collective-permute-start(bf16[128,4,8,128]{3,2,1,0:T(8,128)(2,1)} %param.3), channel_id=1, source_target_pairs={{24,0},{28,4},{0,8},{4,12},{8,16},{12,20},{16,24},{20,28},{25,1},{... | collective-permute-start | bytes 3145736 | tf_op jit(solution)/shard_map/ppermute | solution.py:24
  4.9 9.2 %collective-permute-start = (bf16[128,1280]{1,0:T(8,128)(2,1)S(1)}, bf16[128,1280]{1,0:T(8,128)(2,1)S(1)}, u32[]{:S(2)}, u32[]{:S(2)}) collective-permute-start(bf16[128,1280]{1,0:T(8,128)(2,1)S(1)} %get-tuple-element.32), channel_id=1, source_target_pairs={{1,0},{0,1},{3,2},{2,3},{5,4},{4,5},{7,6},{6,7},{9,8},{8,9},{11,10... | collective-permute-start | bytes 983048 | tf_op jit(solution)/shard_map/ppermute | solution.py:24
  6.4 9.9 %collective-permute-start.1 = (bf16[128,1152]{1,0:T(8,128)(2,1)S(1)}, bf16[128,1152]{1,0:T(8,128)(2,1)S(1)}, u32[]{:S(2)}, u32[]{:S(2)}) collective-permute-start(bf16[128,1152]{1,0:T(8,128)(2,1)S(1)} %get-tuple-element.34), channel_id=1, source_target_pairs={{2,0},{0,2},{3,1},{1,3},{6,4},{4,6},{7,5},{5,7},{10,8},{8,10},{11,... | collective-permute-start | bytes 884744 | tf_op jit(solution)/shard_map/ppermute | solution.py:24
  8.0 13.0 %collective-permute-start.2 = (bf16[128,1152]{1,0:T(8,128)(2,1)S(1)}, bf16[128,1152]{1,0:T(8,128)(2,1)S(1)}, u32[]{:S(2)}, u32[]{:S(2)}) collective-permute-start(bf16[128,1152]{1,0:T(8,128)(2,1)S(1)} %get-tuple-element.35), channel_id=1, source_target_pairs={{2,0},{0,2},{3,1},{1,3},{6,4},{4,6},{7,5},{5,7},{10,8},{8,10},{11,... | collective-permute-start | bytes 884744 | tf_op jit(solution)/shard_map/ppermute | solution.py:24
  21.0 8.0 %collective-permute-start.3 = (bf16[384,2048]{1,0:T(8,128)(2,1)S(1)}, bf16[384,2048]{1,0:T(8,128)(2,1)S(1)}, u32[]{:S(2)}, u32[]{:S(2)}) collective-permute-start(bf16[384,2048]{1,0:T(8,128)(2,1)S(1)} %get-tuple-element.33.refs_0_), channel_id=1, source_target_pairs={{0,4},{4,0},{8,12},{12,8},{16,20},{20,16},{24,28},{28,24},{1,5},{5... | collective-permute-start | bytes 4718600 | tf_op jit(solution)/shard_map/ppermute | solution.py:310
  22.9 6.1 %collective-permute-start.4 = (bf16[384,2048]{1,0:T(8,128)(2,1)S(1)}, bf16[384,2048]{1,0:T(8,128)(2,1)S(1)}, u32[]{:S(2)}, u32[]{:S(2)}) collective-permute-start(bf16[384,2048]{1,0:T(8,128)(2,1)S(1)} %get-tuple-element.39.refs_1_), channel_id=1, source_target_pairs={{0,4},{4,0},{8,12},{12,8},{16,20},{20,16},{24,28},{28,24},{1,5},{5... | collective-permute-start | bytes 4718600 | tf_op jit(solution)/shard_map/ppermute | solution.py:310
  28.9 5.8 %collective-permute-start.9 = (bf16[128,4096]{1,0:T(8,128)(2,1)S(1)}, bf16[128,4096]{1,0:T(8,128)(2,1)S(1)}, u32[]{:S(2)}, u32[]{:S(2)}) collective-permute-start(bf16[128,4096]{1,0:T(8,128)(2,1)S(1)} %bitcast.15), channel_id=1, source_target_pairs={{0,4},{4,0},{8,12},{12,8},{16,20},{20,16},{24,28},{28,24},{1,5},{5... | collective-permute-start | bytes 3145736 | tf_op jit(solution)/shard_map/ppermute | solution.py:323
  31.1 7.6 %collective-permute-start.6 = (bf16[2,3,32,128]{3,2,1,0:T(8,128)(2,1)S(1)}, bf16[2,3,32,128]{3,2,1,0:T(8,128)(2,1)S(1)}, u32[]{:S(2)}, u32[]{:S(2)}) collective-permute-start(bf16[2,3,32,128]{3,2,1,0:T(8,128)(2,1)S(1)} %get-tuple-element.43), channel_id=1, source_target_pairs={{0,3},{1,2},{2,1},{3,0},{4,7},{5,6},{6,5},{7,4},{8,11},{9,10},{10,... | collective-permute-start | bytes 147464 | tf_op jit(solution)/shard_map/ppermute | solution.py:42
  33.6 5.6 %collective-permute-start.7 = (bf16[2,3,32,128]{3,2,1,0:T(8,128)(2,1)S(1)}, bf16[2,3,32,128]{3,2,1,0:T(8,128)(2,1)S(1)}, u32[]{:S(2)}, u32[]{:S(2)}) collective-permute-start(bf16[2,3,32,128]{3,2,1,0:T(8,128)(2,1)S(1)} %get-tuple-element.44), channel_id=1, source_target_pairs={{0,2},{1,3},{2,0},{3,1},{4,6},{5,7},{6,4},{7,5},{8,10},{9,11},{10,... | collective-permute-start | bytes 147464 | tf_op jit(solution)/shard_map/ppermute | solution.py:42
  34.1 5.1 %collective-permute-start.8 = (bf16[2,3,32,128]{3,2,1,0:T(8,128)(2,1)S(1)}, bf16[2,3,32,128]{3,2,1,0:T(8,128)(2,1)S(1)}, u32[]{:S(2)}, u32[]{:S(2)}) collective-permute-start(bf16[2,3,32,128]{3,2,1,0:T(8,128)(2,1)S(1)} %get-tuple-element.45), channel_id=1, source_target_pairs={{0,1},{1,0},{2,3},{3,2},{4,5},{5,4},{6,7},{7,6},{8,9},{9,8},{10,11... | collective-permute-start | bytes 147464 | tf_op jit(solution)/shard_map/ppermute | solution.py:42
  35.7 8.0 %collective-permute-start.10 = (bf16[4,3,32,128]{3,2,1,0:T(8,128)(2,1)S(1)}, bf16[4,3,32,128]{3,2,1,0:T(8,128)(2,1)S(1)}, u32[]{:S(2)}, u32[]{:S(2)}) collective-permute-start(bf16[4,3,32,128]{3,2,1,0:T(8,128)(2,1)S(1)} %get-tuple-element.52), channel_id=1, source_target_pairs={{0,3},{1,2},{2,1},{3,0},{4,7},{5,6},{6,5},{7,4},{8,11},{9,10},{10,... | collective-permute-start | bytes 294920 | tf_op jit(solution)/shard_map/ppermute | solution.py:42
  38.2 5.5 %collective-permute-start.11 = (bf16[4,3,32,128]{3,2,1,0:T(8,128)(2,1)S(1)}, bf16[4,3,32,128]{3,2,1,0:T(8,128)(2,1)S(1)}, u32[]{:S(2)}, u32[]{:S(2)}) collective-permute-start(bf16[4,3,32,128]{3,2,1,0:T(8,128)(2,1)S(1)} %get-tuple-element.53), channel_id=1, source_target_pairs={{0,2},{1,3},{2,0},{3,1},{4,6},{5,7},{6,4},{7,5},{8,10},{9,11},{10,... | collective-permute-start | bytes 294920 | tf_op jit(solution)/shard_map/ppermute | solution.py:42
  38.7 5.0 %collective-permute-start.12 = (bf16[4,3,32,128]{3,2,1,0:T(8,128)(2,1)S(1)}, bf16[4,3,32,128]{3,2,1,0:T(8,128)(2,1)S(1)}, u32[]{:S(2)}, u32[]{:S(2)}) collective-permute-start(bf16[4,3,32,128]{3,2,1,0:T(8,128)(2,1)S(1)} %get-tuple-element.54), channel_id=1, source_target_pairs={{0,1},{1,0},{2,3},{3,2},{4,5},{5,4},{6,7},{7,6},{8,9},{9,8},{10,11... | collective-permute-start | bytes 294920 | tf_op jit(solution)/shard_map/ppermute | solution.py:42
  39.3 4.4 %collective-permute-start.13 = (bf16[3,3,32,128]{3,2,1,0:T(8,128)(2,1)S(1)}, bf16[3,3,32,128]{3,2,1,0:T(8,128)(2,1)S(1)}, u32[]{:S(2)}, u32[]{:S(2)}) collective-permute-start(bf16[3,3,32,128]{3,2,1,0:T(8,128)(2,1)S(1)} %shard_map.43), channel_id=1, source_target_pairs={{8,0},{12,4},{16,8},{20,12},{24,16},{28,20},{0,24},{4,28},{9,1},{1... | collective-permute-start | bytes 221192 | tf_op jit(solution)/shard_map/ppermute | solution.py:24

commit v18 on v15

--- a/solution.py
+++ b/solution.py
@@ -34,7 +34,7 @@
 def exchange(sends):
     nx, ny = lax.axis_size("dx"), lax.axis_size("dy")
     got = []
-    for o, piece in enumerate(sends, 1):
+    for o, piece in reversed(list(enumerate(sends, 1))):
         ox, oy = o // ny, o % ny
         route = [
             (i * ny + j, ((i + ox) % nx) * ny + (j + oy) % ny) for i in range(nx) for j in range(ny)
@@ -257,10 +257,12 @@
 
 def add(*refs):
     group, (ours, back) = refs[:-2], refs[-2:]
+    core = lax.rem(lax.axis_index("blk"), 2)
     for k in range(3):
-        total = total_of(group, 1, k)
-        ours[k], back[1, k] = total, total.astype(BF16)
-        back[0, k] = total_of(group, 0, k).astype(BF16)
+        total, other = total_of(group, 0, k), total_of(group, 1, k)
+        high = total.astype(BF16)
+        ours[k], back[0, k] = other, high
+        back[1, k] = jnp.where(core == 0, total - high.astype(F32), other).astype(BF16)
 
 
 def assemble(*refs):
@@ -268,11 +270,12 @@
     core = lax.rem(lax.axis_index("blk"), 2)
     for k in range(3):
         mate, third = total_of(group, 1, k), total_of(group, 2, k)
+        first, second = back[0, k].astype(F32), back[1, k].astype(F32)
         out[k, 0] = total_of(group, 0, k)
         out[k, 1] = jnp.where(core == 0, third, mate)
         out[k, 2] = jnp.where(core == 0, ours[k], third)
-        out[k, 3] = jnp.where(core == 0, mate, back[1, k].astype(F32))
-        out[k, 4] = back[0, k].astype(F32)
+        out[k, 3] = jnp.where(core == 0, mate, second)
+        out[k, 4] = jnp.where(core == 0, first + second, first)
 
 
 def on_device(orbitals, coupling, pot_grad):

time: 44.9 us -> 44.4 us (0.989)
  waiting for transfers between devices: 17.5 us -> 16.9 us
    ppermute x6, waiting for transfers between devices: 0.61 us -> 0.02 us  [exchange(): got.append(lax.ppermute(piece, ('dx', 'dy'), route))]
  transfers between devices with their start and end apart: 14 -> 14, of which waited for: 7 -> 5; matrix products, arithmetic and copies ran while one was open for 5% -> 5% of each run, Pallas kernels for 18% -> 18%
where the time goes in v18:
time: 44.4 us; the launch traced here: 44.2 us
  waiting for transfers between devices  16.9 us (38%)
  starting transfers between devices  16.2 us (36%)
  Pallas kernels  8.89 us (20%)
  local copies, waits for them, and re-layouts  2.16 us (5%)
    ppermute x5, waiting for transfers between devices, shift(): lax.ppermute(block, axis, [((i + distance) % count, i) for i in range(cou...  16.9 us
    pallas_call x8, Pallas kernels, call(): return list(run(*operands))  8.89 us
    ppermute x5, starting transfers between devices, shift(): lax.ppermute(block, axis, [((i + distance) % count, i) for i in range(cou...  8.4 us
    ppermute x6, starting transfers between devices, exchange(): got.append(lax.ppermute(piece, ('dx', 'dy'), route))  7.11 us
    unnamed x6, local copies, waits for them, and re-layouts  2.16 us
  transfers between devices with their start and end apart: 14, of which 5 were waited for; matrix products, arithmetic and copies ran while one was open for 5% of the time, Pallas kernels for 18%

profile of v18, /device:TPU:0, one launch (start us, length us, event | category | flops | bytes accessed | tf_op | source)
XLA Modules:
  0.0 44.2 jit_solution(3550732471294584205)
XLA Ops:
  0.0 3.0 %collective-permute-start.5 = (bf16[128,4,8,128]{3,2,1,0:T(8,128)(2,1)}, bf16[128,4,8,128]{3,2,1,0:T(8,128)(2,1)S(1)}, u32[]{:S(2)}, u32[]{:S(2)}) collective-permute-start(bf16[128,4,8,128]{3,2,1,0:T(8,128)(2,1)} %param.3), channel_id=1, source_target_pairs={{24,0},{28,4},{0,8},{4,12},{8,16},{12,20},{16,24},{20,28},{25,1},{... | collective-permute-start | bytes 3145736 | tf_op jit(solution)/shard_map/ppermute | solution.py:24
  3.0 1.7 %copy.9 = bf16[16,8,32,128]{3,1,2,0:T(8,128)(2,1)S(1)} copy(bf16[16,8,32,128]{3,2,1,0:T(8,128)(2,1)} %bitcast.18) | data formatting | bytes 2097152
  4.8 0.1 shard_map.37
  4.9 1.6 %collective-permute-start = (bf16[128,1280]{1,0:T(8,128)(2,1)S(1)}, bf16[128,1280]{1,0:T(8,128)(2,1)S(1)}, u32[]{:S(2)}, u32[]{:S(2)}) collective-permute-start(bf16[128,1280]{1,0:T(8,128)(2,1)S(1)} %get-tuple-element.34), channel_id=1, source_target_pairs={{1,0},{0,1},{3,2},{2,3},{5,4},{4,5},{7,6},{6,7},{9,8},{8,9},{11,10... | collective-permute-start | bytes 983048 | tf_op jit(solution)/shard_map/ppermute | solution.py:24
  6.4 1.5 %collective-permute-start.1 = (bf16[128,1152]{1,0:T(8,128)(2,1)S(1)}, bf16[128,1152]{1,0:T(8,128)(2,1)S(1)}, u32[]{:S(2)}, u32[]{:S(2)}) collective-permute-start(bf16[128,1152]{1,0:T(8,128)(2,1)S(1)} %get-tuple-element.36), channel_id=1, source_target_pairs={{2,0},{0,2},{3,1},{1,3},{6,4},{4,6},{7,5},{5,7},{10,8},{8,10},{11,... | collective-permute-start | bytes 884744 | tf_op jit(solution)/shard_map/ppermute | solution.py:24
  8.0 0.5 %collective-permute-start.2 = (bf16[128,1152]{1,0:T(8,128)(2,1)S(1)}, bf16[128,1152]{1,0:T(8,128)(2,1)S(1)}, u32[]{:S(2)}, u32[]{:S(2)}) collective-permute-start(bf16[128,1152]{1,0:T(8,128)(2,1)S(1)} %get-tuple-element.37), channel_id=1, source_target_pairs={{2,0},{0,2},{3,1},{1,3},{6,4},{4,6},{7,5},{5,7},{10,8},{8,10},{11,... | collective-permute-start | bytes 884744 | tf_op jit(solution)/shard_map/ppermute | solution.py:24
  8.5 5.7 %collective-permute-done.refs_1_.refs_3_ = bf16[128,1280]{1,0:T(8,128)(2,1)S(1)} collective-permute-done((bf16[128,1280]{1,0:T(8,128)(2,1)S(1)}, bf16[128,1280]{1,0:T(8,128)(2,1)S(1)}, u32[]{:S(2)}, u32[]{:S(2)}) %collective-permute-start) | collective-permute-done | bytes 327712 | tf_op jit(solution)/shard_map/ppermute | solution.py:24
  14.1 1.9 %shard_map.38 = (bf16[384,2048]{1,0:T(8,128)(2,1)S(1)}, bf16[384,2048]{1,0:T(8,128)(2,1)S(1)}) custom-call(bf16[128,4096]{1,0:T(8,128)(2,1)S(1)} %bitcast.11, bf16[128,1280]{1,0:T(8,128)(2,1)S(1)} %collective-permute-done.refs_1_.refs_3_, f32[4,8,128]{2,1,0:T(8,128)S(1)} %copy-done.1, f32[3,4,8,128]{3,2,1,0:T(8,128)S(1)} %copy-done), custom_call_target="tpu_custom_call" | custom-call | tf_op jit(solution)/shard_map/pallas_call | solution.py:58
  16.0 0.4 collective-permute-done.1.refs_1_
  16.4 4.6 %collective-permute-done.2.refs_2_ = bf16[128,1152]{1,0:T(8,128)(2,1)S(1)} collective-permute-done((bf16[128,1152]{1,0:T(8,128)(2,1)S(1)}, bf16[128,1152]{1,0:T(8,128)(2,1)S(1)}, u32[]{:S(2)}, u32[]{:S(2)}) %collective-permute-start.2) | collective-permute-done | bytes 294944 | tf_op jit(solution)/shard_map/ppermute | solution.py:24
  21.0 0.0 collective-permute-start.3
  21.0 1.9 %shard_map.39 = (bf16[384,2048]{1,0:T(8,128)(2,1)S(1)}, bf16[384,2048]{1,0:T(8,128)(2,1)S(1)}) custom-call(bf16[128,4096]{1,0:T(8,128)(2,1)S(1)} %bitcast.12, bf16[128,1152]{1,0:T(8,128)(2,1)S(1)} %collective-permute-done.1.refs_1_, bf16[128,1152]{1,0:T(8,128)(2,1)S(1)} %collective-permute-done.2.refs_2_, ...), custom_call_target="tpu_custom_call" | custom-call | tf_op jit(solution)/shard_map/pallas_call | solution.py:58
  22.9 0.6 %collective-permute-start.4 = (bf16[384,2048]{1,0:T(8,128)(2,1)S(1)}, bf16[384,2048]{1,0:T(8,128)(2,1)S(1)}, u32[]{:S(2)}, u32[]{:S(2)}) collective-permute-start(bf16[384,2048]{1,0:T(8,128)(2,1)S(1)} %get-tuple-element.41.refs_1_), channel_id=1, source_target_pairs={{0,4},{4,0},{8,12},{12,8},{16,20},{20,16},{24,28},{28,24},{1,5},{5... | collective-permute-start | bytes 4718600 | tf_op jit(solution)/shard_map/ppermute | solution.py:320
  23.5 1.0 %shard_map.40.refs_6_.refs_4_ = f32[384,128]{1,0:T(8,128)S(1)} custom-call(bf16[384,2048]{1,0:T(8,128)(2,1)S(1)} %get-tuple-element.42.refs_0_, bf16[384,2048]{1,0:T(8,128)(2,1)S(1)} %get-tuple-element.43.refs_1_, bf16[128,4096]{1,0:T(8,128)(2,1)S(1)} %bitcast.13), custom_call_target="tpu_custom_call" | custom-call | tf_op jit(solution)/shard_map/pallas_call | solution.py:58
  24.4 4.0 %collective-permute-done.5 = bf16[128,4,8,128]{3,2,1,0:T(8,128)(2,1)S(1)} collective-permute-done((bf16[128,4,8,128]{3,2,1,0:T(8,128)(2,1)}, bf16[128,4,8,128]{3,2,1,0:T(8,128)(2,1)S(1)}, u32[]{:S(2)}, u32[]{:S(2)}) %collective-permute-start.5) | collective-permute-done | bytes 1048608 | tf_op jit(solution)/shard_map/ppermute | solution.py:24
  28.4 0.5 %copy.8 = bf16[16,8,32,128]{3,1,2,0:T(8,128)(2,1)S(1)} copy(bf16[16,8,32,128]{3,2,1,0:T(8,128)(2,1)S(1)} %bitcast.19) | data formatting | bytes 2097152
  28.9 0.1 collective-permute-start.9
  29.0 0.0 collective-permute-done.3.refs_2_
  29.0 2.1 %shard_map.41 = (f32[128,384]{1,0:T(8,128)S(1)}, f32[2,3,32,128]{3,2,1,0:T(8,128)S(1)}, bf16[2,3,32,128]{3,2,1,0:T(8,128)(2,1)S(1)}, bf16[2,3,32,128]{3,2,1,0:T(8,128)(2,1)S(1)}, bf16[2,3,32,128]{3,2,1,0:T(8,128)(2,1)S(1)}) custom-call(bf16[384,2048]{1,0:T(8,128)(2,1)S(1)} %get-tuple-element.35.refs_0_, bf16[384,2048]{1,0:T(8,128)(2,1)S(1)} %get-tuple-element.41.refs_1_, ...), custom_call_target="tpu_custom_call" | custom-call | bytes 3000000 | tf_op jit(solution)/shard_map/pallas_call | solution.py:58
  31.1 2.5 %collective-permute-start.6 = (bf16[2,3,32,128]{3,2,1,0:T(8,128)(2,1)S(1)}, bf16[2,3,32,128]{3,2,1,0:T(8,128)(2,1)S(1)}, u32[]{:S(2)}, u32[]{:S(2)}) collective-permute-start(bf16[2,3,32,128]{3,2,1,0:T(8,128)(2,1)S(1)} %get-tuple-element.46), channel_id=1, source_target_pairs={{0,3},{1,2},{2,1},{3,0},{4,7},{5,6},{6,5},{7,4},{8,11},{9,10},{10,... | collective-permute-start | bytes 147464 | tf_op jit(solution)/shard_map/ppermute | solution.py:42
  33.6 0.5 %collective-permute-start.7 = (bf16[2,3,32,128]{3,2,1,0:T(8,128)(2,1)S(1)}, bf16[2,3,32,128]{3,2,1,0:T(8,128)(2,1)S(1)}, u32[]{:S(2)}, u32[]{:S(2)}) collective-permute-start(bf16[2,3,32,128]{3,2,1,0:T(8,128)(2,1)S(1)} %get-tuple-element.47), channel_id=1, source_target_pairs={{0,2},{1,3},{2,0},{3,1},{4,6},{5,7},{6,4},{7,5},{8,10},{9,11},{10,... | collective-permute-start | bytes 147464 | tf_op jit(solution)/shard_map/ppermute | solution.py:42
  34.1 0.5 %collective-permute-start.8 = (bf16[2,3,32,128]{3,2,1,0:T(8,128)(2,1)S(1)}, bf16[2,3,32,128]{3,2,1,0:T(8,128)(2,1)S(1)}, u32[]{:S(2)}, u32[]{:S(2)}) collective-permute-start(bf16[2,3,32,128]{3,2,1,0:T(8,128)(2,1)S(1)} %get-tuple-element.48), channel_id=1, source_target_pairs={{0,1},{1,0},{2,3},{3,2},{4,5},{5,4},{6,7},{7,6},{8,9},{9,8},{10,11... | collective-permute-start | bytes 147464 | tf_op jit(solution)/shard_map/ppermute | solution.py:42
  34.7 0.0 collective-permute-done.9.refs_3_
  34.7 1.0 %shard_map.42 = (f32[3,3,32,128]{3,2,1,0:T(8,128)S(1)}, bf16[3,3,32,128]{3,2,1,0:T(8,128)(2,1)S(1)}, bf16[3,3,32,128]{3,2,1,0:T(8,128)(2,1)S(1)}, bf16[3,3,32,128]{3,2,1,0:T(8,128)(2,1)S(1)}) custom-call(bf16[384,2048]{1,0:T(8,128)(2,1)S(1)} %get-tuple-element.42.refs_0_, bf16[384,2048]{1,0:T(8,128)(2,1)S(1)} %get-tuple-element.43.refs_1_, ...), custom_call_target="tpu_custom_call" | custom-call | bytes 3000000 | tf_op jit(solution)/shard_map/pallas_call | solution.py:58
  35.7 2.5 %collective-permute-start.10 = (bf16[3,3,32,128]{3,2,1,0:T(8,128)(2,1)S(1)}, bf16[3,3,32,128]{3,2,1,0:T(8,128)(2,1)S(1)}, u32[]{:S(2)}, u32[]{:S(2)}) collective-permute-start(bf16[3,3,32,128]{3,2,1,0:T(8,128)(2,1)S(1)} %get-tuple-element.54), channel_id=1, source_target_pairs={{0,3},{1,2},{2,1},{3,0},{4,7},{5,6},{6,5},{7,4},{8,11},{9,10},{10,... | collective-permute-start | bytes 221192 | tf_op jit(solution)/shard_map/ppermute | solution.py:42
  38.2 0.5 %collective-permute-start.11 = (bf16[3,3,32,128]{3,2,1,0:T(8,128)(2,1)S(1)}, bf16[3,3,32,128]{3,2,1,0:T(8,128)(2,1)S(1)}, u32[]{:S(2)}, u32[]{:S(2)}) collective-permute-start(bf16[3,3,32,128]{3,2,1,0:T(8,128)(2,1)S(1)} %get-tuple-element.55), channel_id=1, source_target_pairs={{0,2},{1,3},{2,0},{3,1},{4,6},{5,7},{6,4},{7,5},{8,10},{9,11},{10,... | collective-permute-start | bytes 221192 | tf_op jit(solution)/shard_map/ppermute | solution.py:42
  38.7 0.0 collective-permute-done.6.refs_1_
  38.7 0.5 %collective-permute-start.12 = (bf16[3,3,32,128]{3,2,1,0:T(8,128)(2,1)S(1)}, bf16[3,3,32,128]{3,2,1,0:T(8,128)(2,1)S(1)}, u32[]{:S(2)}, u32[]{:S(2)}) collective-permute-start(bf16[3,3,32,128]{3,2,1,0:T(8,128)(2,1)S(1)} %get-tuple-element.56), channel_id=1, source_target_pairs={{0,1},{1,0},{2,3},{3,2},{4,5},{5,4},{6,7},{7,6},{8,9},{9,8},{10,11... | collective-permute-start | bytes 221192 | tf_op jit(solution)/shard_map/ppermute | solution.py:42
  39.3 0.0 collective-permute-done.7.refs_2_
  39.3 1.8 %collective-permute-start.13 = (bf16[2,3,32,128]{3,2,1,0:T(8,128)(2,1)S(1)}, bf16[2,3,32,128]{3,2,1,0:T(8,128)(2,1)S(1)}, u32[]{:S(2)}, u32[]{:S(2)}) collective-permute-start(bf16[2,3,32,128]{3,2,1,0:T(8,128)(2,1)S(1)} %get-tuple-element.62), channel_id=1, source_target_pairs={{8,0},{12,4},{16,8},{20,12},{24,16},{28,20},{0,24},{4,28},{9,1},{1... | collective-permute-start | bytes 147464 | tf_op jit(solution)/shard_map/ppermute | solution.py:24
  41.1 2.3 %collective-permute-done.13.refs_5_ = bf16[2,3,32,128]{3,2,1,0:T(8,128)(2,1)S(1)} collective-permute-done((bf16[2,3,32,128]{3,2,1,0:T(8,128)(2,1)S(1)}, bf16[2,3,32,128]{3,2,1,0:T(8,128)(2,1)S(1)}, u32[]{:S(2)}, u32[]{:S(2)}) %collective-permute-start.13) | collective-permute-done | bytes 49184 | tf_op jit(solution)/shard_map/ppermute | solution.py:24
  43.5 0.7 %shard_map.44 = f32[3,5,32,128]{3,2,1,0:T(8,128)} custom-call(f32[3,3,32,128]{3,2,1,0:T(8,128)S(1)} %get-tuple-element.53.refs_0_, bf16[3,3,32,128]{3,2,1,0:T(8,128)(2,1)S(1)} %collective-permute-done.10.refs_1_, bf16[3,3,32,128]{3,2,1,0:T(8,128)(2,1)S(1)} %collective-permute-done.11.refs_2_, bf16[3,3,32,128]{3,2,1,0:T(8,128)(2,1)S(1)} %collective-permute-done.12.refs_3_, ...), custom_call_target="tpu_custom_call" | custom-call | tf_op jit(solution)/shard_map/pallas_call | solution.py:58
  (10 shorter events, 0.1 us)
Async XLA Ops:
  0.0 4.7 %copy-start.1 = (f32[4,8,128]{2,1,0:T(8,128)S(1)}, f32[4,8,128]{2,1,0:T(8,128)}, u32[]{:S(2)}) copy-start(f32[4,8,128]{2,1,0:T(8,128)} %refs_4_.1) | copy-start | bytes 49156
  0.0 4.7 %copy-start = (f32[3,4,8,128]{3,2,1,0:T(8,128)S(1)}, f32[3,4,8,128]{3,2,1,0:T(8,128)}, u32[]{:S(2)}) copy-start(f32[3,4,8,128]{3,2,1,0:T(8,128)} %refs_5_.1) | copy-start | bytes 147460
  0.0 28.4 %collective-permute-start.5 = (bf16[128,4,8,128]{3,2,1,0:T(8,128)(2,1)}, bf16[128,4,8,128]{3,2,1,0:T(8,128)(2,1)S(1)}, u32[]{:S(2)}, u32[]{:S(2)}) collective-permute-start(bf16[128,4,8,128]{3,2,1,0:T(8,128)(2,1)} %param.3), channel_id=1, source_target_pairs={{24,0},{28,4},{0,8},{4,12},{8,16},{12,20},{16,24},{20,28},{25,1},{... | collective-permute-start | bytes 3145736 | tf_op jit(solution)/shard_map/ppermute | solution.py:24
  4.9 9.2 %collective-permute-start = (bf16[128,1280]{1,0:T(8,128)(2,1)S(1)}, bf16[128,1280]{1,0:T(8,128)(2,1)S(1)}, u32[]{:S(2)}, u32[]{:S(2)}) collective-permute-start(bf16[128,1280]{1,0:T(8,128)(2,1)S(1)} %get-tuple-element.34), channel_id=1, source_target_pairs={{1,0},{0,1},{3,2},{2,3},{5,4},{4,5},{7,6},{6,7},{9,8},{8,9},{11,10... | collective-permute-start | bytes 983048 | tf_op jit(solution)/shard_map/ppermute | solution.py:24
  6.4 9.9 %collective-permute-start.1 = (bf16[128,1152]{1,0:T(8,128)(2,1)S(1)}, bf16[128,1152]{1,0:T(8,128)(2,1)S(1)}, u32[]{:S(2)}, u32[]{:S(2)}) collective-permute-start(bf16[128,1152]{1,0:T(8,128)(2,1)S(1)} %get-tuple-element.36), channel_id=1, source_target_pairs={{2,0},{0,2},{3,1},{1,3},{6,4},{4,6},{7,5},{5,7},{10,8},{8,10},{11,... | collective-permute-start | bytes 884744 | tf_op jit(solution)/shard_map/ppermute | solution.py:24
  8.0 13.0 %collective-permute-start.2 = (bf16[128,1152]{1,0:T(8,128)(2,1)S(1)}, bf16[128,1152]{1,0:T(8,128)(2,1)S(1)}, u32[]{:S(2)}, u32[]{:S(2)}) collective-permute-start(bf16[128,1152]{1,0:T(8,128)(2,1)S(1)} %get-tuple-element.37), channel_id=1, source_target_pairs={{2,0},{0,2},{3,1},{1,3},{6,4},{4,6},{7,5},{5,7},{10,8},{8,10},{11,... | collective-permute-start | bytes 884744 | tf_op jit(solution)/shard_map/ppermute | solution.py:24
  21.0 8.0 %collective-permute-start.3 = (bf16[384,2048]{1,0:T(8,128)(2,1)S(1)}, bf16[384,2048]{1,0:T(8,128)(2,1)S(1)}, u32[]{:S(2)}, u32[]{:S(2)}) collective-permute-start(bf16[384,2048]{1,0:T(8,128)(2,1)S(1)} %get-tuple-element.35.refs_0_), channel_id=1, source_target_pairs={{0,4},{4,0},{8,12},{12,8},{16,20},{20,16},{24,28},{28,24},{1,5},{5... | collective-permute-start | bytes 4718600 | tf_op jit(solution)/shard_map/ppermute | solution.py:320
  22.9 6.1 %collective-permute-start.4 = (bf16[384,2048]{1,0:T(8,128)(2,1)S(1)}, bf16[384,2048]{1,0:T(8,128)(2,1)S(1)}, u32[]{:S(2)}, u32[]{:S(2)}) collective-permute-start(bf16[384,2048]{1,0:T(8,128)(2,1)S(1)} %get-tuple-element.41.refs_1_), channel_id=1, source_target_pairs={{0,4},{4,0},{8,12},{12,8},{16,20},{20,16},{24,28},{28,24},{1,5},{5... | collective-permute-start | bytes 4718600 | tf_op jit(solution)/shard_map/ppermute | solution.py:320
  28.9 5.8 %collective-permute-start.9 = (bf16[128,4096]{1,0:T(8,128)(2,1)S(1)}, bf16[128,4096]{1,0:T(8,128)(2,1)S(1)}, u32[]{:S(2)}, u32[]{:S(2)}) collective-permute-start(bf16[128,4096]{1,0:T(8,128)(2,1)S(1)} %bitcast.15), channel_id=1, source_target_pairs={{0,4},{4,0},{8,12},{12,8},{16,20},{20,16},{24,28},{28,24},{1,5},{5... | collective-permute-start | bytes 3145736 | tf_op jit(solution)/shard_map/ppermute | solution.py:333
  31.1 7.6 %collective-permute-start.6 = (bf16[2,3,32,128]{3,2,1,0:T(8,128)(2,1)S(1)}, bf16[2,3,32,128]{3,2,1,0:T(8,128)(2,1)S(1)}, u32[]{:S(2)}, u32[]{:S(2)}) collective-permute-start(bf16[2,3,32,128]{3,2,1,0:T(8,128)(2,1)S(1)} %get-tuple-element.46), channel_id=1, source_target_pairs={{0,3},{1,2},{2,1},{3,0},{4,7},{5,6},{6,5},{7,4},{8,11},{9,10},{10,... | collective-permute-start | bytes 147464 | tf_op jit(solution)/shard_map/ppermute | solution.py:42
  33.6 5.7 %collective-permute-start.7 = (bf16[2,3,32,128]{3,2,1,0:T(8,128)(2,1)S(1)}, bf16[2,3,32,128]{3,2,1,0:T(8,128)(2,1)S(1)}, u32[]{:S(2)}, u32[]{:S(2)}) collective-permute-start(bf16[2,3,32,128]{3,2,1,0:T(8,128)(2,1)S(1)} %get-tuple-element.47), channel_id=1, source_target_pairs={{0,2},{1,3},{2,0},{3,1},{4,6},{5,7},{6,4},{7,5},{8,10},{9,11},{10,... | collective-permute-start | bytes 147464 | tf_op jit(solution)/shard_map/ppermute | solution.py:42
  34.1 5.1 %collective-permute-start.8 = (bf16[2,3,32,128]{3,2,1,0:T(8,128)(2,1)S(1)}, bf16[2,3,32,128]{3,2,1,0:T(8,128)(2,1)S(1)}, u32[]{:S(2)}, u32[]{:S(2)}) collective-permute-start(bf16[2,3,32,128]{3,2,1,0:T(8,128)(2,1)S(1)} %get-tuple-element.48), channel_id=1, source_target_pairs={{0,1},{1,0},{2,3},{3,2},{4,5},{5,4},{6,7},{7,6},{8,9},{9,8},{10,11... | collective-permute-start | bytes 147464 | tf_op jit(solution)/shard_map/ppermute | solution.py:42
  35.7 7.7 %collective-permute-start.10 = (bf16[3,3,32,128]{3,2,1,0:T(8,128)(2,1)S(1)}, bf16[3,3,32,128]{3,2,1,0:T(8,128)(2,1)S(1)}, u32[]{:S(2)}, u32[]{:S(2)}) collective-permute-start(bf16[3,3,32,128]{3,2,1,0:T(8,128)(2,1)S(1)} %get-tuple-element.54), channel_id=1, source_target_pairs={{0,3},{1,2},{2,1},{3,0},{4,7},{5,6},{6,5},{7,4},{8,11},{9,10},{10,... | collective-permute-start | bytes 221192 | tf_op jit(solution)/shard_map/ppermute | solution.py:42
  38.2 5.2 %collective-permute-start.11 = (bf16[3,3,32,128]{3,2,1,0:T(8,128)(2,1)S(1)}, bf16[3,3,32,128]{3,2,1,0:T(8,128)(2,1)S(1)}, u32[]{:S(2)}, u32[]{:S(2)}) collective-permute-start(bf16[3,3,32,128]{3,2,1,0:T(8,128)(2,1)S(1)} %get-tuple-element.55), channel_id=1, source_target_pairs={{0,2},{1,3},{2,0},{3,1},{4,6},{5,7},{6,4},{7,5},{8,10},{9,11},{10,... | collective-permute-start | bytes 221192 | tf_op jit(solution)/shard_map/ppermute | solution.py:42
  38.7 4.7 %collective-permute-start.12 = (bf16[3,3,32,128]{3,2,1,0:T(8,128)(2,1)S(1)}, bf16[3,3,32,128]{3,2,1,0:T(8,128)(2,1)S(1)}, u32[]{:S(2)}, u32[]{:S(2)}) collective-permute-start(bf16[3,3,32,128]{3,2,1,0:T(8,128)(2,1)S(1)} %get-tuple-element.56), channel_id=1, source_target_pairs={{0,1},{1,0},{2,3},{3,2},{4,5},{5,4},{6,7},{7,6},{8,9},{9,8},{10,11... | collective-permute-start | bytes 221192 | tf_op jit(solution)/shard_map/ppermute | solution.py:42
  39.3 4.1 %collective-permute-start.13 = (bf16[2,3,32,128]{3,2,1,0:T(8,128)(2,1)S(1)}, bf16[2,3,32,128]{3,2,1,0:T(8,128)(2,1)S(1)}, u32[]{:S(2)}, u32[]{:S(2)}) collective-permute-start(bf16[2,3,32,128]{3,2,1,0:T(8,128)(2,1)S(1)} %get-tuple-element.62), channel_id=1, source_target_pairs={{8,0},{12,4},{16,8},{20,12},{24,16},{28,20},{0,24},{4,28},{9,1},{1... | collective-permute-start | bytes 147464 | tf_op jit(solution)/shard_map/ppermute | solution.py:24

commit v19 on v18

--- a/solution.py
+++ b/solution.py
@@ -10,6 +10,7 @@
 
 F32, BF16 = jnp.float32, jnp.bfloat16
 VMEM = pl.BlockSpec(memory_space=pltpu.VMEM)
+ANY = pl.BlockSpec(memory_space=pl.ANY)
 LIMIT = 12 * 1024 * 1024
 NT = (((1,), (1,)), ((), ()))
 CHUNK = 16
@@ -43,13 +44,14 @@
     return got
 
 
-def call(body, outs, operands, scratch=(), specs=None, out_specs=None, us=0):
+def call(body, outs, operands, scratch=(), specs=None, out_specs=None, us=0, aliases=None):
     run = pl.pallas_call(
         body,
         out_shape=outs,
         in_specs=specs or [VMEM] * len(operands),
         out_specs=out_specs or [VMEM] * len(outs),
         scratch_shapes=list(scratch),
+        input_output_aliases=aliases or {},
         compiler_params=pltpu.CompilerParams(vmem_limit_bytes=LIMIT),
         cost_estimate=pl.CostEstimate(
             flops=0, bytes_accessed=int(us * 3e6), transcendentals=0
@@ -266,16 +268,34 @@
 
 
 def assemble(*refs):
-    group, (ours, back, out) = refs[:-3], refs[-3:]
+    group, (ours, out) = refs[:-2], refs[-2:]
     core = lax.rem(lax.axis_index("blk"), 2)
     for k in range(3):
         mate, third = total_of(group, 1, k), total_of(group, 2, k)
-        first, second = back[0, k].astype(F32), back[1, k].astype(F32)
         out[k, 0] = total_of(group, 0, k)
         out[k, 1] = jnp.where(core == 0, third, mate)
         out[k, 2] = jnp.where(core == 0, ours[k], third)
-        out[k, 3] = jnp.where(core == 0, mate, second)
-        out[k, 4] = jnp.where(core == 0, first + second, first)
+        out[k, 3] = mate
+        out[k, 4] = mate
+
+
+def place_back(back, _, out, tiles, sems):
+    core = lax.rem(lax.axis_index("blk"), 2)
+    copies = [
+        pltpu.make_async_copy(tiles.at[n], out.at[:, 4 - n], sems.at[n]) for n in range(2)
+    ]
+    for k in range(3):
+        first, second = back[0, k].astype(F32), back[1, k].astype(F32)
+        tiles[0, k] = jnp.where(core == 0, first + second, first)
+        tiles[1, k] = second
+    copies[0].start()
+
+    @pl.when(core == 1)
+    def _():
+        copies[1].start()
+        copies[1].wait()
+
+    copies[0].wait()
 
 
 def on_device(orbitals, coupling, pot_grad):
@@ -354,8 +374,16 @@
         add, [shape_of(small, F32), shape_of((2, *small), BF16)], [kept_there, *first]
     )
     back = shift(back, "blk", 2)
+    result = shape_of((3, 5, rows, states), F32)
+    (out,) = call(assemble, [result], [kept, *second, ours])
     (out,) = call(
-        assemble, [shape_of((3, 5, rows, states), F32)], [kept, *second, ours, back]
+        place_back,
+        [result],
+        [back, out],
+        scratch=[pltpu.VMEM((2, *small), F32), pltpu.SemaphoreType.DMA((2,))],
+        specs=[VMEM, ANY],
+        out_specs=[ANY],
+        aliases={1: 0},
     )
     return out
 

time: 44.4 us -> 44.6 us (level)
  Pallas kernels: 8.89 us -> 9.53 us
    ppermute x5, waiting for transfers between devices: 16.9 us -> 14.5 us  [shift(): lax.ppermute(block, axis, [((i + distance) % count, i) for i in range(cou...]
    ppermute x6, waiting for transfers between devices: 0.02 us -> 1.98 us  [exchange(): got.append(lax.ppermute(piece, ('dx', 'dy'), route))]
    pallas_call x8 -> x9, Pallas kernels: 8.89 us -> 9.53 us  [call(): return list(run(*operands))]
  transfers between devices with their start and end apart: 14 -> 14, of which waited for: 5 -> 6; matrix products, arithmetic and copies ran while one was open for 5% -> 5% of each run, Pallas kernels for 18% -> 20%
where the time goes in v19:
time: 44.6 us; the launch traced here: 44.5 us
  waiting for transfers between devices  16.5 us (37%)
  starting transfers between devices  16.2 us (36%)
  Pallas kernels  9.53 us (21%)
  local copies, waits for them, and re-layouts  2.16 us (5%)
    ppermute x5, waiting for transfers between devices, shift(): lax.ppermute(block, axis, [((i + distance) % count, i) for i in range(cou...  14.5 us
    pallas_call x9, Pallas kernels, call(): return list(run(*operands))  9.53 us
    ppermute x5, starting transfers between devices, shift(): lax.ppermute(block, axis, [((i + distance) % count, i) for i in range(cou...  8.4 us
    ppermute x6, starting transfers between devices, exchange(): got.append(lax.ppermute(piece, ('dx', 'dy'), route))  7.11 us
    unnamed x6, local copies, waits for them, and re-layouts  2.16 us
    ppermute x6, waiting for transfers between devices, exchange(): got.append(lax.ppermute(piece, ('dx', 'dy'), route))  1.98 us
  transfers between devices with their start and end apart: 14, of which 6 were waited for; matrix products, arithmetic and copies ran while one was open for 5% of the time, Pallas kernels for 20%

profile of v19, /device:TPU:0, one launch (start us, length us, event | category | flops | bytes accessed | tf_op | source)
XLA Modules:
  0.0 44.5 jit_solution(15718856628905926540)
XLA Ops:
  0.0 3.0 %collective-permute-start.5 = (bf16[128,4,8,128]{3,2,1,0:T(8,128)(2,1)}, bf16[128,4,8,128]{3,2,1,0:T(8,128)(2,1)S(1)}, u32[]{:S(2)}, u32[]{:S(2)}) collective-permute-start(bf16[128,4,8,128]{3,2,1,0:T(8,128)(2,1)} %param.3), channel_id=1, source_target_pairs={{24,0},{28,4},{0,8},{4,12},{8,16},{12,20},{16,24},{20,28},{25,1},{... | collective-permute-start | bytes 3145736 | tf_op jit(solution)/shard_map/ppermute | solution.py:25
  3.0 1.7 %copy.10 = bf16[16,8,32,128]{3,1,2,0:T(8,128)(2,1)S(1)} copy(bf16[16,8,32,128]{3,2,1,0:T(8,128)(2,1)} %bitcast.18) | data formatting | bytes 2097152
  4.8 0.1 shard_map.37
  4.9 1.6 %collective-permute-start = (bf16[128,1280]{1,0:T(8,128)(2,1)S(1)}, bf16[128,1280]{1,0:T(8,128)(2,1)S(1)}, u32[]{:S(2)}, u32[]{:S(2)}) collective-permute-start(bf16[128,1280]{1,0:T(8,128)(2,1)S(1)} %get-tuple-element.34), channel_id=1, source_target_pairs={{1,0},{0,1},{3,2},{2,3},{5,4},{4,5},{7,6},{6,7},{9,8},{8,9},{11,10... | collective-permute-start | bytes 983048 | tf_op jit(solution)/shard_map/ppermute | solution.py:25
  6.4 1.5 %collective-permute-start.1 = (bf16[128,1152]{1,0:T(8,128)(2,1)S(1)}, bf16[128,1152]{1,0:T(8,128)(2,1)S(1)}, u32[]{:S(2)}, u32[]{:S(2)}) collective-permute-start(bf16[128,1152]{1,0:T(8,128)(2,1)S(1)} %get-tuple-element.36), channel_id=1, source_target_pairs={{2,0},{0,2},{3,1},{1,3},{6,4},{4,6},{7,5},{5,7},{10,8},{8,10},{11,... | collective-permute-start | bytes 884744 | tf_op jit(solution)/shard_map/ppermute | solution.py:25
  8.0 0.5 %collective-permute-start.2 = (bf16[128,1152]{1,0:T(8,128)(2,1)S(1)}, bf16[128,1152]{1,0:T(8,128)(2,1)S(1)}, u32[]{:S(2)}, u32[]{:S(2)}) collective-permute-start(bf16[128,1152]{1,0:T(8,128)(2,1)S(1)} %get-tuple-element.37), channel_id=1, source_target_pairs={{2,0},{0,2},{3,1},{1,3},{6,4},{4,6},{7,5},{5,7},{10,8},{8,10},{11,... | collective-permute-start | bytes 884744 | tf_op jit(solution)/shard_map/ppermute | solution.py:25
  8.5 5.7 %collective-permute-done.refs_1_.refs_3_ = bf16[128,1280]{1,0:T(8,128)(2,1)S(1)} collective-permute-done((bf16[128,1280]{1,0:T(8,128)(2,1)S(1)}, bf16[128,1280]{1,0:T(8,128)(2,1)S(1)}, u32[]{:S(2)}, u32[]{:S(2)}) %collective-permute-start) | collective-permute-done | bytes 327712 | tf_op jit(solution)/shard_map/ppermute | solution.py:25
  14.1 1.9 %shard_map.38 = (bf16[384,2048]{1,0:T(8,128)(2,1)S(1)}, bf16[384,2048]{1,0:T(8,128)(2,1)S(1)}) custom-call(bf16[128,4096]{1,0:T(8,128)(2,1)S(1)} %bitcast.11, bf16[128,1280]{1,0:T(8,128)(2,1)S(1)} %collective-permute-done.refs_1_.refs_3_, f32[4,8,128]{2,1,0:T(8,128)S(1)} %copy-done.1, f32[3,4,8,128]{3,2,1,0:T(8,128)S(1)} %copy-done), custom_call_target="tpu_custom_call" | custom-call | tf_op jit(solution)/shard_map/pallas_call | solution.py:60
  16.0 0.4 collective-permute-done.1.refs_1_
  16.4 4.6 %collective-permute-done.2.refs_2_ = bf16[128,1152]{1,0:T(8,128)(2,1)S(1)} collective-permute-done((bf16[128,1152]{1,0:T(8,128)(2,1)S(1)}, bf16[128,1152]{1,0:T(8,128)(2,1)S(1)}, u32[]{:S(2)}, u32[]{:S(2)}) %collective-permute-start.2) | collective-permute-done | bytes 294944 | tf_op jit(solution)/shard_map/ppermute | solution.py:25
  21.0 0.0 collective-permute-start.3
  21.0 1.9 %shard_map.39 = (bf16[384,2048]{1,0:T(8,128)(2,1)S(1)}, bf16[384,2048]{1,0:T(8,128)(2,1)S(1)}) custom-call(bf16[128,4096]{1,0:T(8,128)(2,1)S(1)} %bitcast.12, bf16[128,1152]{1,0:T(8,128)(2,1)S(1)} %collective-permute-done.1.refs_1_, bf16[128,1152]{1,0:T(8,128)(2,1)S(1)} %collective-permute-done.2.refs_2_, ...), custom_call_target="tpu_custom_call" | custom-call | tf_op jit(solution)/shard_map/pallas_call | solution.py:60
  22.9 0.6 %collective-permute-start.4 = (bf16[384,2048]{1,0:T(8,128)(2,1)S(1)}, bf16[384,2048]{1,0:T(8,128)(2,1)S(1)}, u32[]{:S(2)}, u32[]{:S(2)}) collective-permute-start(bf16[384,2048]{1,0:T(8,128)(2,1)S(1)} %get-tuple-element.41.refs_1_), channel_id=1, source_target_pairs={{0,4},{4,0},{8,12},{12,8},{16,20},{20,16},{24,28},{28,24},{1,5},{5... | collective-permute-start | bytes 4718600 | tf_op jit(solution)/shard_map/ppermute | solution.py:340
  23.5 1.0 %shard_map.40.refs_6_.refs_4_ = f32[384,128]{1,0:T(8,128)S(1)} custom-call(bf16[384,2048]{1,0:T(8,128)(2,1)S(1)} %get-tuple-element.42.refs_0_, bf16[384,2048]{1,0:T(8,128)(2,1)S(1)} %get-tuple-element.43.refs_1_, bf16[128,4096]{1,0:T(8,128)(2,1)S(1)} %bitcast.13), custom_call_target="tpu_custom_call" | custom-call | tf_op jit(solution)/shard_map/pallas_call | solution.py:60
  24.4 4.0 %collective-permute-done.5 = bf16[128,4,8,128]{3,2,1,0:T(8,128)(2,1)S(1)} collective-permute-done((bf16[128,4,8,128]{3,2,1,0:T(8,128)(2,1)}, bf16[128,4,8,128]{3,2,1,0:T(8,128)(2,1)S(1)}, u32[]{:S(2)}, u32[]{:S(2)}) %collective-permute-start.5) | collective-permute-done | bytes 1048608 | tf_op jit(solution)/shard_map/ppermute | solution.py:25
  28.4 0.5 %copy.9 = bf16[16,8,32,128]{3,1,2,0:T(8,128)(2,1)S(1)} copy(bf16[16,8,32,128]{3,2,1,0:T(8,128)(2,1)S(1)} %bitcast.19) | data formatting | bytes 2097152
  28.9 0.1 collective-permute-start.9
  29.0 0.0 collective-permute-done.3.refs_2_
  29.0 2.1 %shard_map.41 = (f32[128,384]{1,0:T(8,128)S(1)}, f32[2,3,32,128]{3,2,1,0:T(8,128)S(1)}, bf16[2,3,32,128]{3,2,1,0:T(8,128)(2,1)S(1)}, bf16[2,3,32,128]{3,2,1,0:T(8,128)(2,1)S(1)}, bf16[2,3,32,128]{3,2,1,0:T(8,128)(2,1)S(1)}) custom-call(bf16[384,2048]{1,0:T(8,128)(2,1)S(1)} %get-tuple-element.35.refs_0_, bf16[384,2048]{1,0:T(8,128)(2,1)S(1)} %get-tuple-element.41.refs_1_, ...), custom_call_target="tpu_custom_call" | custom-call | bytes 3000000 | tf_op jit(solution)/shard_map/pallas_call | solution.py:60
  31.1 2.5 %collective-permute-start.6 = (bf16[2,3,32,128]{3,2,1,0:T(8,128)(2,1)S(1)}, bf16[2,3,32,128]{3,2,1,0:T(8,128)(2,1)S(1)}, u32[]{:S(2)}, u32[]{:S(2)}) collective-permute-start(bf16[2,3,32,128]{3,2,1,0:T(8,128)(2,1)S(1)} %get-tuple-element.47), channel_id=1, source_target_pairs={{0,3},{1,2},{2,1},{3,0},{4,7},{5,6},{6,5},{7,4},{8,11},{9,10},{10,... | collective-permute-start | bytes 147464 | tf_op jit(solution)/shard_map/ppermute | solution.py:43
  33.6 0.5 %collective-permute-start.7 = (bf16[2,3,32,128]{3,2,1,0:T(8,128)(2,1)S(1)}, bf16[2,3,32,128]{3,2,1,0:T(8,128)(2,1)S(1)}, u32[]{:S(2)}, u32[]{:S(2)}) collective-permute-start(bf16[2,3,32,128]{3,2,1,0:T(8,128)(2,1)S(1)} %get-tuple-element.48), channel_id=1, source_target_pairs={{0,2},{1,3},{2,0},{3,1},{4,6},{5,7},{6,4},{7,5},{8,10},{9,11},{10,... | collective-permute-start | bytes 147464 | tf_op jit(solution)/shard_map/ppermute | solution.py:43
  34.1 0.5 %collective-permute-start.8 = (bf16[2,3,32,128]{3,2,1,0:T(8,128)(2,1)S(1)}, bf16[2,3,32,128]{3,2,1,0:T(8,128)(2,1)S(1)}, u32[]{:S(2)}, u32[]{:S(2)}) collective-permute-start(bf16[2,3,32,128]{3,2,1,0:T(8,128)(2,1)S(1)} %get-tuple-element.49), channel_id=1, source_target_pairs={{0,1},{1,0},{2,3},{3,2},{4,5},{5,4},{6,7},{7,6},{8,9},{9,8},{10,11... | collective-permute-start | bytes 147464 | tf_op jit(solution)/shard_map/ppermute | solution.py:43
  34.7 1.0 %shard_map.42 = (f32[3,3,32,128]{3,2,1,0:T(8,128)S(1)}, bf16[3,3,32,128]{3,2,1,0:T(8,128)(2,1)S(1)}, bf16[3,3,32,128]{3,2,1,0:T(8,128)(2,1)S(1)}, bf16[3,3,32,128]{3,2,1,0:T(8,128)(2,1)S(1)}) custom-call(bf16[384,2048]{1,0:T(8,128)(2,1)S(1)} %get-tuple-element.42.refs_0_, bf16[384,2048]{1,0:T(8,128)(2,1)S(1)} %get-tuple-element.43.refs_1_, ...), custom_call_target="tpu_custom_call" | custom-call | bytes 3000000 | tf_op jit(solution)/shard_map/pallas_call | solution.py:60
  35.7 2.5 %collective-permute-start.11 = (bf16[3,3,32,128]{3,2,1,0:T(8,128)(2,1)S(1)}, bf16[3,3,32,128]{3,2,1,0:T(8,128)(2,1)S(1)}, u32[]{:S(2)}, u32[]{:S(2)}) collective-permute-start(bf16[3,3,32,128]{3,2,1,0:T(8,128)(2,1)S(1)} %get-tuple-element.59), channel_id=1, source_target_pairs={{0,3},{1,2},{2,1},{3,0},{4,7},{5,6},{6,5},{7,4},{8,11},{9,10},{10,... | collective-permute-start | bytes 221192 | tf_op jit(solution)/shard_map/ppermute | solution.py:43
  38.2 0.5 %collective-permute-start.12 = (bf16[3,3,32,128]{3,2,1,0:T(8,128)(2,1)S(1)}, bf16[3,3,32,128]{3,2,1,0:T(8,128)(2,1)S(1)}, u32[]{:S(2)}, u32[]{:S(2)}) collective-permute-start(bf16[3,3,32,128]{3,2,1,0:T(8,128)(2,1)S(1)} %get-tuple-element.60), channel_id=1, source_target_pairs={{0,2},{1,3},{2,0},{3,1},{4,6},{5,7},{6,4},{7,5},{8,10},{9,11},{10,... | collective-permute-start | bytes 221192 | tf_op jit(solution)/shard_map/ppermute | solution.py:43
  38.7 0.5 %collective-permute-start.13 = (bf16[3,3,32,128]{3,2,1,0:T(8,128)(2,1)S(1)}, bf16[3,3,32,128]{3,2,1,0:T(8,128)(2,1)S(1)}, u32[]{:S(2)}, u32[]{:S(2)}) collective-permute-start(bf16[3,3,32,128]{3,2,1,0:T(8,128)(2,1)S(1)} %get-tuple-element.61), channel_id=1, source_target_pairs={{0,1},{1,0},{2,3},{3,2},{4,5},{5,4},{6,7},{7,6},{8,9},{9,8},{10,11... | collective-permute-start | bytes 221192 | tf_op jit(solution)/shard_map/ppermute | solution.py:43
  39.3 1.8 %collective-permute-start.10 = (bf16[2,3,32,128]{3,2,1,0:T(8,128)(2,1)S(1)}, bf16[2,3,32,128]{3,2,1,0:T(8,128)(2,1)S(1)}, u32[]{:S(2)}, u32[]{:S(2)}) collective-permute-start(bf16[2,3,32,128]{3,2,1,0:T(8,128)(2,1)S(1)} %get-tuple-element.57), channel_id=1, source_target_pairs={{8,0},{12,4},{16,8},{20,12},{24,16},{28,20},{0,24},{4,28},{9,1},{1... | collective-permute-start | bytes 147464 | tf_op jit(solution)/shard_map/ppermute | solution.py:25
  41.1 0.0 collective-permute-done.11.refs_1_
  41.1 1.4 %collective-permute-done.12.refs_2_ = bf16[3,3,32,128]{3,2,1,0:T(8,128)(2,1)S(1)} collective-permute-done((bf16[3,3,32,128]{3,2,1,0:T(8,128)(2,1)S(1)}, bf16[3,3,32,128]{3,2,1,0:T(8,128)(2,1)S(1)}, u32[]{:S(2)}, u32[]{:S(2)}) %collective-permute-start.12) | collective-permute-done | bytes 73760 | tf_op jit(solution)/shard_map/ppermute | solution.py:43
  42.6 0.5 %collective-permute-done.13.refs_3_ = bf16[3,3,32,128]{3,2,1,0:T(8,128)(2,1)S(1)} collective-permute-done((bf16[3,3,32,128]{3,2,1,0:T(8,128)(2,1)S(1)}, bf16[3,3,32,128]{3,2,1,0:T(8,128)(2,1)S(1)}, u32[]{:S(2)}, u32[]{:S(2)}) %collective-permute-start.13) | collective-permute-done | bytes 73760 | tf_op jit(solution)/shard_map/ppermute | solution.py:43
  43.1 0.7 %shard_map.44._ = f32[3,5,32,128]{3,2,1,0:T(8,128)} custom-call(f32[3,3,32,128]{3,2,1,0:T(8,128)S(1)} %get-tuple-element.58.refs_0_, bf16[3,3,32,128]{3,2,1,0:T(8,128)(2,1)S(1)} %collective-permute-done.11.refs_1_, bf16[3,3,32,128]{3,2,1,0:T(8,128)(2,1)S(1)} %collective-permute-done.12.refs_2_, bf16[3,3,32,128]{3,2,1,0:T(8,128)(2,1)S(1)} %collective-permute-done.13.refs_3_, ...), custom_call_target="tpu_custom_call" | custom-call | tf_op jit(solution)/shard_map/pallas_call | solution.py:60
  43.8 0.7 %shard_map.45 = f32[3,5,32,128]{3,2,1,0:T(8,128)} custom-call(bf16[2,3,32,128]{3,2,1,0:T(8,128)(2,1)S(1)} %collective-permute-done.10.back, f32[3,5,32,128]{3,2,1,0:T(8,128)} %shard_map.44._), custom_call_target="tpu_custom_call", output_to_operand_aliasing={{}: (1, {})} | custom-call | tf_op jit(solution)/shard_map/pallas_call | solution.py:60
  (11 shorter events, 0.1 us)
Async XLA Ops:
  0.0 4.7 %copy-start.1 = (f32[4,8,128]{2,1,0:T(8,128)S(1)}, f32[4,8,128]{2,1,0:T(8,128)}, u32[]{:S(2)}) copy-start(f32[4,8,128]{2,1,0:T(8,128)} %refs_4_.1) | copy-start | bytes 49156
  0.0 4.7 %copy-start = (f32[3,4,8,128]{3,2,1,0:T(8,128)S(1)}, f32[3,4,8,128]{3,2,1,0:T(8,128)}, u32[]{:S(2)}) copy-start(f32[3,4,8,128]{3,2,1,0:T(8,128)} %refs_5_.1) | copy-start | bytes 147460
  0.0 28.4 %collective-permute-start.5 = (bf16[128,4,8,128]{3,2,1,0:T(8,128)(2,1)}, bf16[128,4,8,128]{3,2,1,0:T(8,128)(2,1)S(1)}, u32[]{:S(2)}, u32[]{:S(2)}) collective-permute-start(bf16[128,4,8,128]{3,2,1,0:T(8,128)(2,1)} %param.3), channel_id=1, source_target_pairs={{24,0},{28,4},{0,8},{4,12},{8,16},{12,20},{16,24},{20,28},{25,1},{... | collective-permute-start | bytes 3145736 | tf_op jit(solution)/shard_map/ppermute | solution.py:25
  4.9 9.2 %collective-permute-start = (bf16[128,1280]{1,0:T(8,128)(2,1)S(1)}, bf16[128,1280]{1,0:T(8,128)(2,1)S(1)}, u32[]{:S(2)}, u32[]{:S(2)}) collective-permute-start(bf16[128,1280]{1,0:T(8,128)(2,1)S(1)} %get-tuple-element.34), channel_id=1, source_target_pairs={{1,0},{0,1},{3,2},{2,3},{5,4},{4,5},{7,6},{6,7},{9,8},{8,9},{11,10... | collective-permute-start | bytes 983048 | tf_op jit(solution)/shard_map/ppermute | solution.py:25
  6.4 9.9 %collective-permute-start.1 = (bf16[128,1152]{1,0:T(8,128)(2,1)S(1)}, bf16[128,1152]{1,0:T(8,128)(2,1)S(1)}, u32[]{:S(2)}, u32[]{:S(2)}) collective-permute-start(bf16[128,1152]{1,0:T(8,128)(2,1)S(1)} %get-tuple-element.36), channel_id=1, source_target_pairs={{2,0},{0,2},{3,1},{1,3},{6,4},{4,6},{7,5},{5,7},{10,8},{8,10},{11,... | collective-permute-start | bytes 884744 | tf_op jit(solution)/shard_map/ppermute | solution.py:25
  8.0 13.0 %collective-permute-start.2 = (bf16[128,1152]{1,0:T(8,128)(2,1)S(1)}, bf16[128,1152]{1,0:T(8,128)(2,1)S(1)}, u32[]{:S(2)}, u32[]{:S(2)}) collective-permute-start(bf16[128,1152]{1,0:T(8,128)(2,1)S(1)} %get-tuple-element.37), channel_id=1, source_target_pairs={{2,0},{0,2},{3,1},{1,3},{6,4},{4,6},{7,5},{5,7},{10,8},{8,10},{11,... | collective-permute-start | bytes 884744 | tf_op jit(solution)/shard_map/ppermute | solution.py:25
  21.0 8.0 %collective-permute-start.3 = (bf16[384,2048]{1,0:T(8,128)(2,1)S(1)}, bf16[384,2048]{1,0:T(8,128)(2,1)S(1)}, u32[]{:S(2)}, u32[]{:S(2)}) collective-permute-start(bf16[384,2048]{1,0:T(8,128)(2,1)S(1)} %get-tuple-element.35.refs_0_), channel_id=1, source_target_pairs={{0,4},{4,0},{8,12},{12,8},{16,20},{20,16},{24,28},{28,24},{1,5},{5... | collective-permute-start | bytes 4718600 | tf_op jit(solution)/shard_map/ppermute | solution.py:340
  22.9 6.1 %collective-permute-start.4 = (bf16[384,2048]{1,0:T(8,128)(2,1)S(1)}, bf16[384,2048]{1,0:T(8,128)(2,1)S(1)}, u32[]{:S(2)}, u32[]{:S(2)}) collective-permute-start(bf16[384,2048]{1,0:T(8,128)(2,1)S(1)} %get-tuple-element.41.refs_1_), channel_id=1, source_target_pairs={{0,4},{4,0},{8,12},{12,8},{16,20},{20,16},{24,28},{28,24},{1,5},{5... | collective-permute-start | bytes 4718600 | tf_op jit(solution)/shard_map/ppermute | solution.py:340
  28.9 5.8 %collective-permute-start.9 = (bf16[128,4096]{1,0:T(8,128)(2,1)S(1)}, bf16[128,4096]{1,0:T(8,128)(2,1)S(1)}, u32[]{:S(2)}, u32[]{:S(2)}) collective-permute-start(bf16[128,4096]{1,0:T(8,128)(2,1)S(1)} %bitcast.15), channel_id=1, source_target_pairs={{0,4},{4,0},{8,12},{12,8},{16,20},{20,16},{24,28},{28,24},{1,5},{5... | collective-permute-start | bytes 3145736 | tf_op jit(solution)/shard_map/ppermute | solution.py:353
  31.1 7.6 %collective-permute-start.6 = (bf16[2,3,32,128]{3,2,1,0:T(8,128)(2,1)S(1)}, bf16[2,3,32,128]{3,2,1,0:T(8,128)(2,1)S(1)}, u32[]{:S(2)}, u32[]{:S(2)}) collective-permute-start(bf16[2,3,32,128]{3,2,1,0:T(8,128)(2,1)S(1)} %get-tuple-element.47), channel_id=1, source_target_pairs={{0,3},{1,2},{2,1},{3,0},{4,7},{5,6},{6,5},{7,4},{8,11},{9,10},{10,... | collective-permute-start | bytes 147464 | tf_op jit(solution)/shard_map/ppermute | solution.py:43
  33.6 5.7 %collective-permute-start.7 = (bf16[2,3,32,128]{3,2,1,0:T(8,128)(2,1)S(1)}, bf16[2,3,32,128]{3,2,1,0:T(8,128)(2,1)S(1)}, u32[]{:S(2)}, u32[]{:S(2)}) collective-permute-start(bf16[2,3,32,128]{3,2,1,0:T(8,128)(2,1)S(1)} %get-tuple-element.48), channel_id=1, source_target_pairs={{0,2},{1,3},{2,0},{3,1},{4,6},{5,7},{6,4},{7,5},{8,10},{9,11},{10,... | collective-permute-start | bytes 147464 | tf_op jit(solution)/shard_map/ppermute | solution.py:43
  34.1 5.1 %collective-permute-start.8 = (bf16[2,3,32,128]{3,2,1,0:T(8,128)(2,1)S(1)}, bf16[2,3,32,128]{3,2,1,0:T(8,128)(2,1)S(1)}, u32[]{:S(2)}, u32[]{:S(2)}) collective-permute-start(bf16[2,3,32,128]{3,2,1,0:T(8,128)(2,1)S(1)} %get-tuple-element.49), channel_id=1, source_target_pairs={{0,1},{1,0},{2,3},{3,2},{4,5},{5,4},{6,7},{7,6},{8,9},{9,8},{10,11... | collective-permute-start | bytes 147464 | tf_op jit(solution)/shard_map/ppermute | solution.py:43
  35.7 5.4 %collective-permute-start.11 = (bf16[3,3,32,128]{3,2,1,0:T(8,128)(2,1)S(1)}, bf16[3,3,32,128]{3,2,1,0:T(8,128)(2,1)S(1)}, u32[]{:S(2)}, u32[]{:S(2)}) collective-permute-start(bf16[3,3,32,128]{3,2,1,0:T(8,128)(2,1)S(1)} %get-tuple-element.59), channel_id=1, source_target_pairs={{0,3},{1,2},{2,1},{3,0},{4,7},{5,6},{6,5},{7,4},{8,11},{9,10},{10,... | collective-permute-start | bytes 221192 | tf_op jit(solution)/shard_map/ppermute | solution.py:43
  38.2 4.4 %collective-permute-start.12 = (bf16[3,3,32,128]{3,2,1,0:T(8,128)(2,1)S(1)}, bf16[3,3,32,128]{3,2,1,0:T(8,128)(2,1)S(1)}, u32[]{:S(2)}, u32[]{:S(2)}) collective-permute-start(bf16[3,3,32,128]{3,2,1,0:T(8,128)(2,1)S(1)} %get-tuple-element.60), channel_id=1, source_target_pairs={{0,2},{1,3},{2,0},{3,1},{4,6},{5,7},{6,4},{7,5},{8,10},{9,11},{10,... | collective-permute-start | bytes 221192 | tf_op jit(solution)/shard_map/ppermute | solution.py:43
  38.7 4.4 %collective-permute-start.13 = (bf16[3,3,32,128]{3,2,1,0:T(8,128)(2,1)S(1)}, bf16[3,3,32,128]{3,2,1,0:T(8,128)(2,1)S(1)}, u32[]{:S(2)}, u32[]{:S(2)}) collective-permute-start(bf16[3,3,32,128]{3,2,1,0:T(8,128)(2,1)S(1)} %get-tuple-element.61), channel_id=1, source_target_pairs={{0,1},{1,0},{2,3},{3,2},{4,5},{5,4},{6,7},{7,6},{8,9},{9,8},{10,11... | collective-permute-start | bytes 221192 | tf_op jit(solution)/shard_map/ppermute | solution.py:43
  39.3 4.5 %collective-permute-start.10 = (bf16[2,3,32,128]{3,2,1,0:T(8,128)(2,1)S(1)}, bf16[2,3,32,128]{3,2,1,0:T(8,128)(2,1)S(1)}, u32[]{:S(2)}, u32[]{:S(2)}) collective-permute-start(bf16[2,3,32,128]{3,2,1,0:T(8,128)(2,1)S(1)} %get-tuple-element.57), channel_id=1, source_target_pairs={{8,0},{12,4},{16,8},{20,12},{24,16},{28,20},{0,24},{4,28},{9,1},{1... | collective-permute-start | bytes 147464 | tf_op jit(solution)/shard_map/ppermute | solution.py:25

commit v20 on v18

--- a/solution.py
+++ b/solution.py
@@ -266,16 +266,34 @@
 
 
 def assemble(*refs):
-    group, (ours, back, out) = refs[:-3], refs[-3:]
+    group, (ours, back, out, tiles, sems) = refs[:-5], refs[-5:]
     core = lax.rem(lax.axis_index("blk"), 2)
-    for k in range(3):
-        mate, third = total_of(group, 1, k), total_of(group, 2, k)
-        first, second = back[0, k].astype(F32), back[1, k].astype(F32)
-        out[k, 0] = total_of(group, 0, k)
-        out[k, 1] = jnp.where(core == 0, third, mate)
-        out[k, 2] = jnp.where(core == 0, ours[k], third)
-        out[k, 3] = jnp.where(core == 0, mate, second)
-        out[k, 4] = jnp.where(core == 0, first + second, first)
+    copies = [
+        pltpu.make_async_copy(tiles.at[t], out.at[:, t], sems.at[t]) for t in range(5)
+    ]
+
+    def fill(t, value):
+        for k in range(3):
+            tiles[t, k] = value(k)
+        copies[t].start()
+
+    def returned(k):
+        first = back[0, k].astype(F32)
+        return jnp.where(core == 0, first + back[1, k].astype(F32), first)
+
+    def third(k):
+        return total_of(group, 2, k)
+
+    def mate(k):
+        return total_of(group, 1, k)
+
+    fill(0, lambda k: total_of(group, 0, k))
+    fill(1, lambda k: jnp.where(core == 0, third(k), mate(k)))
+    fill(2, lambda k: jnp.where(core == 0, ours[k], third(k)))
+    fill(3, lambda k: jnp.where(core == 0, mate(k), back[1, k].astype(F32)))
+    fill(4, returned)
+    for copy in copies:
+        copy.wait()
 
 
 def on_device(orbitals, coupling, pot_grad):
@@ -355,7 +373,11 @@
     )
     back = shift(back, "blk", 2)
     (out,) = call(
-        assemble, [shape_of((3, 5, rows, states), F32)], [kept, *second, ours, back]
+        assemble,
+        [shape_of((3, 5, rows, states), F32)],
+        [kept, *second, ours, back],
+        scratch=[pltpu.VMEM((5, *small), F32), pltpu.SemaphoreType.DMA((5,))],
+        out_specs=[pl.BlockSpec(memory_space=pl.ANY)],
     )
     return out
 

time: 44.4 us -> 44.4 us (level)
  no operation moved by 1% of the time
where the time goes in v20:
time: 44.4 us; the launch traced here: 44.2 us
  waiting for transfers between devices  16.9 us (38%)
  starting transfers between devices  16.2 us (36%)
  Pallas kernels  8.9 us (20%)
  local copies, waits for them, and re-layouts  2.16 us (5%)
    ppermute x5, waiting for transfers between devices, shift(): lax.ppermute(block, axis, [((i + distance) % count, i) for i in range(cou...  16.9 us
    pallas_call x8, Pallas kernels, call(): return list(run(*operands))  8.9 us
    ppermute x5, starting transfers between devices, shift(): lax.ppermute(block, axis, [((i + distance) % count, i) for i in range(cou...  8.4 us
    ppermute x6, starting transfers between devices, exchange(): got.append(lax.ppermute(piece, ('dx', 'dy'), route))  7.11 us
    unnamed x6, local copies, waits for them, and re-layouts  2.16 us
  transfers between devices with their start and end apart: 14, of which 5 were waited for; matrix products, arithmetic and copies ran while one was open for 5% of the time, Pallas kernels for 18%

profile of v20, /device:TPU:0, one launch (start us, length us, event | category | flops | bytes accessed | tf_op | source)
XLA Modules:
  0.0 44.2 jit_solution(7415618118887841730)
XLA Ops:
  0.0 3.0 %collective-permute-start.5 = (bf16[128,4,8,128]{3,2,1,0:T(8,128)(2,1)}, bf16[128,4,8,128]{3,2,1,0:T(8,128)(2,1)S(1)}, u32[]{:S(2)}, u32[]{:S(2)}) collective-permute-start(bf16[128,4,8,128]{3,2,1,0:T(8,128)(2,1)} %param.3), channel_id=1, source_target_pairs={{24,0},{28,4},{0,8},{4,12},{8,16},{12,20},{16,24},{20,28},{25,1},{... | collective-permute-start | bytes 3145736 | tf_op jit(solution)/shard_map/ppermute | solution.py:24
  3.0 1.7 %copy.9 = bf16[16,8,32,128]{3,1,2,0:T(8,128)(2,1)S(1)} copy(bf16[16,8,32,128]{3,2,1,0:T(8,128)(2,1)} %bitcast.18) | data formatting | bytes 2097152
  4.8 0.1 shard_map.37
  4.9 1.6 %collective-permute-start = (bf16[128,1280]{1,0:T(8,128)(2,1)S(1)}, bf16[128,1280]{1,0:T(8,128)(2,1)S(1)}, u32[]{:S(2)}, u32[]{:S(2)}) collective-permute-start(bf16[128,1280]{1,0:T(8,128)(2,1)S(1)} %get-tuple-element.34), channel_id=1, source_target_pairs={{1,0},{0,1},{3,2},{2,3},{5,4},{4,5},{7,6},{6,7},{9,8},{8,9},{11,10... | collective-permute-start | bytes 983048 | tf_op jit(solution)/shard_map/ppermute | solution.py:24
  6.4 1.5 %collective-permute-start.1 = (bf16[128,1152]{1,0:T(8,128)(2,1)S(1)}, bf16[128,1152]{1,0:T(8,128)(2,1)S(1)}, u32[]{:S(2)}, u32[]{:S(2)}) collective-permute-start(bf16[128,1152]{1,0:T(8,128)(2,1)S(1)} %get-tuple-element.36), channel_id=1, source_target_pairs={{2,0},{0,2},{3,1},{1,3},{6,4},{4,6},{7,5},{5,7},{10,8},{8,10},{11,... | collective-permute-start | bytes 884744 | tf_op jit(solution)/shard_map/ppermute | solution.py:24
  8.0 0.5 %collective-permute-start.2 = (bf16[128,1152]{1,0:T(8,128)(2,1)S(1)}, bf16[128,1152]{1,0:T(8,128)(2,1)S(1)}, u32[]{:S(2)}, u32[]{:S(2)}) collective-permute-start(bf16[128,1152]{1,0:T(8,128)(2,1)S(1)} %get-tuple-element.37), channel_id=1, source_target_pairs={{2,0},{0,2},{3,1},{1,3},{6,4},{4,6},{7,5},{5,7},{10,8},{8,10},{11,... | collective-permute-start | bytes 884744 | tf_op jit(solution)/shard_map/ppermute | solution.py:24
  8.5 5.7 %collective-permute-done.refs_1_.refs_3_ = bf16[128,1280]{1,0:T(8,128)(2,1)S(1)} collective-permute-done((bf16[128,1280]{1,0:T(8,128)(2,1)S(1)}, bf16[128,1280]{1,0:T(8,128)(2,1)S(1)}, u32[]{:S(2)}, u32[]{:S(2)}) %collective-permute-start) | collective-permute-done | bytes 327712 | tf_op jit(solution)/shard_map/ppermute | solution.py:24
  14.1 1.9 %shard_map.38 = (bf16[384,2048]{1,0:T(8,128)(2,1)S(1)}, bf16[384,2048]{1,0:T(8,128)(2,1)S(1)}) custom-call(bf16[128,4096]{1,0:T(8,128)(2,1)S(1)} %bitcast.11, bf16[128,1280]{1,0:T(8,128)(2,1)S(1)} %collective-permute-done.refs_1_.refs_3_, f32[4,8,128]{2,1,0:T(8,128)S(1)} %copy-done.1, f32[3,4,8,128]{3,2,1,0:T(8,128)S(1)} %copy-done), custom_call_target="tpu_custom_call" | custom-call | tf_op jit(solution)/shard_map/pallas_call | solution.py:58
  16.0 0.4 collective-permute-done.1.refs_1_
  16.4 4.6 %collective-permute-done.2.refs_2_ = bf16[128,1152]{1,0:T(8,128)(2,1)S(1)} collective-permute-done((bf16[128,1152]{1,0:T(8,128)(2,1)S(1)}, bf16[128,1152]{1,0:T(8,128)(2,1)S(1)}, u32[]{:S(2)}, u32[]{:S(2)}) %collective-permute-start.2) | collective-permute-done | bytes 294944 | tf_op jit(solution)/shard_map/ppermute | solution.py:24
  21.0 1.9 %shard_map.39 = (bf16[384,2048]{1,0:T(8,128)(2,1)S(1)}, bf16[384,2048]{1,0:T(8,128)(2,1)S(1)}) custom-call(bf16[128,4096]{1,0:T(8,128)(2,1)S(1)} %bitcast.12, bf16[128,1152]{1,0:T(8,128)(2,1)S(1)} %collective-permute-done.1.refs_1_, bf16[128,1152]{1,0:T(8,128)(2,1)S(1)} %collective-permute-done.2.refs_2_, ...), custom_call_target="tpu_custom_call" | custom-call | tf_op jit(solution)/shard_map/pallas_call | solution.py:58
  22.9 0.6 %collective-permute-start.4 = (bf16[384,2048]{1,0:T(8,128)(2,1)S(1)}, bf16[384,2048]{1,0:T(8,128)(2,1)S(1)}, u32[]{:S(2)}, u32[]{:S(2)}) collective-permute-start(bf16[384,2048]{1,0:T(8,128)(2,1)S(1)} %get-tuple-element.41.refs_1_), channel_id=1, source_target_pairs={{0,4},{4,0},{8,12},{12,8},{16,20},{20,16},{24,28},{28,24},{1,5},{5... | collective-permute-start | bytes 4718600 | tf_op jit(solution)/shard_map/ppermute | solution.py:338
  23.5 1.0 %shard_map.40.refs_6_.refs_4_ = f32[384,128]{1,0:T(8,128)S(1)} custom-call(bf16[384,2048]{1,0:T(8,128)(2,1)S(1)} %get-tuple-element.42.refs_0_, bf16[384,2048]{1,0:T(8,128)(2,1)S(1)} %get-tuple-element.43.refs_1_, bf16[128,4096]{1,0:T(8,128)(2,1)S(1)} %bitcast.13), custom_call_target="tpu_custom_call" | custom-call | tf_op jit(solution)/shard_map/pallas_call | solution.py:58
  24.4 4.0 %collective-permute-done.5 = bf16[128,4,8,128]{3,2,1,0:T(8,128)(2,1)S(1)} collective-permute-done((bf16[128,4,8,128]{3,2,1,0:T(8,128)(2,1)}, bf16[128,4,8,128]{3,2,1,0:T(8,128)(2,1)S(1)}, u32[]{:S(2)}, u32[]{:S(2)}) %collective-permute-start.5) | collective-permute-done | bytes 1048608 | tf_op jit(solution)/shard_map/ppermute | solution.py:24
  28.4 0.5 %copy.8 = bf16[16,8,32,128]{3,1,2,0:T(8,128)(2,1)S(1)} copy(bf16[16,8,32,128]{3,2,1,0:T(8,128)(2,1)S(1)} %bitcast.19) | data formatting | bytes 2097152
  28.9 0.1 collective-permute-start.9
  29.0 0.0 collective-permute-done.3.refs_2_
  29.0 0.0 collective-permute-done.4.refs_3_
  29.0 2.1 %shard_map.41 = (f32[128,384]{1,0:T(8,128)S(1)}, f32[2,3,32,128]{3,2,1,0:T(8,128)S(1)}, bf16[2,3,32,128]{3,2,1,0:T(8,128)(2,1)S(1)}, bf16[2,3,32,128]{3,2,1,0:T(8,128)(2,1)S(1)}, bf16[2,3,32,128]{3,2,1,0:T(8,128)(2,1)S(1)}) custom-call(bf16[384,2048]{1,0:T(8,128)(2,1)S(1)} %get-tuple-element.35.refs_0_, bf16[384,2048]{1,0:T(8,128)(2,1)S(1)} %get-tuple-element.41.refs_1_, ...), custom_call_target="tpu_custom_call" | custom-call | bytes 3000000 | tf_op jit(solution)/shard_map/pallas_call | solution.py:58
  31.1 2.5 %collective-permute-start.6 = (bf16[2,3,32,128]{3,2,1,0:T(8,128)(2,1)S(1)}, bf16[2,3,32,128]{3,2,1,0:T(8,128)(2,1)S(1)}, u32[]{:S(2)}, u32[]{:S(2)}) collective-permute-start(bf16[2,3,32,128]{3,2,1,0:T(8,128)(2,1)S(1)} %get-tuple-element.46), channel_id=1, source_target_pairs={{0,3},{1,2},{2,1},{3,0},{4,7},{5,6},{6,5},{7,4},{8,11},{9,10},{10,... | collective-permute-start | bytes 147464 | tf_op jit(solution)/shard_map/ppermute | solution.py:42
  33.6 0.5 %collective-permute-start.7 = (bf16[2,3,32,128]{3,2,1,0:T(8,128)(2,1)S(1)}, bf16[2,3,32,128]{3,2,1,0:T(8,128)(2,1)S(1)}, u32[]{:S(2)}, u32[]{:S(2)}) collective-permute-start(bf16[2,3,32,128]{3,2,1,0:T(8,128)(2,1)S(1)} %get-tuple-element.47), channel_id=1, source_target_pairs={{0,2},{1,3},{2,0},{3,1},{4,6},{5,7},{6,4},{7,5},{8,10},{9,11},{10,... | collective-permute-start | bytes 147464 | tf_op jit(solution)/shard_map/ppermute | solution.py:42
  34.1 0.5 %collective-permute-start.8 = (bf16[2,3,32,128]{3,2,1,0:T(8,128)(2,1)S(1)}, bf16[2,3,32,128]{3,2,1,0:T(8,128)(2,1)S(1)}, u32[]{:S(2)}, u32[]{:S(2)}) collective-permute-start(bf16[2,3,32,128]{3,2,1,0:T(8,128)(2,1)S(1)} %get-tuple-element.48), channel_id=1, source_target_pairs={{0,1},{1,0},{2,3},{3,2},{4,5},{5,4},{6,7},{7,6},{8,9},{9,8},{10,11... | collective-permute-start | bytes 147464 | tf_op jit(solution)/shard_map/ppermute | solution.py:42
  34.7 1.0 %shard_map.42 = (f32[3,3,32,128]{3,2,1,0:T(8,128)S(1)}, bf16[3,3,32,128]{3,2,1,0:T(8,128)(2,1)S(1)}, bf16[3,3,32,128]{3,2,1,0:T(8,128)(2,1)S(1)}, bf16[3,3,32,128]{3,2,1,0:T(8,128)(2,1)S(1)}) custom-call(bf16[384,2048]{1,0:T(8,128)(2,1)S(1)} %get-tuple-element.42.refs_0_, bf16[384,2048]{1,0:T(8,128)(2,1)S(1)} %get-tuple-element.43.refs_1_, ...), custom_call_target="tpu_custom_call" | custom-call | bytes 3000000 | tf_op jit(solution)/shard_map/pallas_call | solution.py:58
  35.7 2.5 %collective-permute-start.10 = (bf16[3,3,32,128]{3,2,1,0:T(8,128)(2,1)S(1)}, bf16[3,3,32,128]{3,2,1,0:T(8,128)(2,1)S(1)}, u32[]{:S(2)}, u32[]{:S(2)}) collective-permute-start(bf16[3,3,32,128]{3,2,1,0:T(8,128)(2,1)S(1)} %get-tuple-element.54), channel_id=1, source_target_pairs={{0,3},{1,2},{2,1},{3,0},{4,7},{5,6},{6,5},{7,4},{8,11},{9,10},{10,... | collective-permute-start | bytes 221192 | tf_op jit(solution)/shard_map/ppermute | solution.py:42
  38.2 0.5 %collective-permute-start.11 = (bf16[3,3,32,128]{3,2,1,0:T(8,128)(2,1)S(1)}, bf16[3,3,32,128]{3,2,1,0:T(8,128)(2,1)S(1)}, u32[]{:S(2)}, u32[]{:S(2)}) collective-permute-start(bf16[3,3,32,128]{3,2,1,0:T(8,128)(2,1)S(1)} %get-tuple-element.55), channel_id=1, source_target_pairs={{0,2},{1,3},{2,0},{3,1},{4,6},{5,7},{6,4},{7,5},{8,10},{9,11},{10,... | collective-permute-start | bytes 221192 | tf_op jit(solution)/shard_map/ppermute | solution.py:42
  38.7 0.5 %collective-permute-start.12 = (bf16[3,3,32,128]{3,2,1,0:T(8,128)(2,1)S(1)}, bf16[3,3,32,128]{3,2,1,0:T(8,128)(2,1)S(1)}, u32[]{:S(2)}, u32[]{:S(2)}) collective-permute-start(bf16[3,3,32,128]{3,2,1,0:T(8,128)(2,1)S(1)} %get-tuple-element.56), channel_id=1, source_target_pairs={{0,1},{1,0},{2,3},{3,2},{4,5},{5,4},{6,7},{7,6},{8,9},{9,8},{10,11... | collective-permute-start | bytes 221192 | tf_op jit(solution)/shard_map/ppermute | solution.py:42
  39.3 0.0 collective-permute-done.7.refs_2_
  39.3 0.0 collective-permute-done.8.refs_3_
  39.3 1.8 %collective-permute-start.13 = (bf16[2,3,32,128]{3,2,1,0:T(8,128)(2,1)S(1)}, bf16[2,3,32,128]{3,2,1,0:T(8,128)(2,1)S(1)}, u32[]{:S(2)}, u32[]{:S(2)}) collective-permute-start(bf16[2,3,32,128]{3,2,1,0:T(8,128)(2,1)S(1)} %get-tuple-element.62), channel_id=1, source_target_pairs={{8,0},{12,4},{16,8},{20,12},{24,16},{28,20},{0,24},{4,28},{9,1},{1... | collective-permute-start | bytes 147464 | tf_op jit(solution)/shard_map/ppermute | solution.py:24
  41.1 2.3 %collective-permute-done.13.refs_5_ = bf16[2,3,32,128]{3,2,1,0:T(8,128)(2,1)S(1)} collective-permute-done((bf16[2,3,32,128]{3,2,1,0:T(8,128)(2,1)S(1)}, bf16[2,3,32,128]{3,2,1,0:T(8,128)(2,1)S(1)}, u32[]{:S(2)}, u32[]{:S(2)}) %collective-permute-start.13) | collective-permute-done | bytes 49184 | tf_op jit(solution)/shard_map/ppermute | solution.py:24
  43.5 0.0 collective-permute-done.11.refs_2_
  43.5 0.8 %shard_map.44 = f32[3,5,32,128]{3,2,1,0:T(8,128)} custom-call(f32[3,3,32,128]{3,2,1,0:T(8,128)S(1)} %get-tuple-element.53.refs_0_, bf16[3,3,32,128]{3,2,1,0:T(8,128)(2,1)S(1)} %collective-permute-done.10.refs_1_, bf16[3,3,32,128]{3,2,1,0:T(8,128)(2,1)S(1)} %collective-permute-done.11.refs_2_, bf16[3,3,32,128]{3,2,1,0:T(8,128)(2,1)S(1)} %collective-permute-done.12.refs_3_, ...), custom_call_target="tpu_custom_call" | custom-call | tf_op jit(solution)/shard_map/pallas_call | solution.py:58
  (10 shorter events, 0.1 us)
Async XLA Ops:
  0.0 4.7 %copy-start.1 = (f32[4,8,128]{2,1,0:T(8,128)S(1)}, f32[4,8,128]{2,1,0:T(8,128)}, u32[]{:S(2)}) copy-start(f32[4,8,128]{2,1,0:T(8,128)} %refs_4_.1) | copy-start | bytes 49156
  0.0 4.7 %copy-start = (f32[3,4,8,128]{3,2,1,0:T(8,128)S(1)}, f32[3,4,8,128]{3,2,1,0:T(8,128)}, u32[]{:S(2)}) copy-start(f32[3,4,8,128]{3,2,1,0:T(8,128)} %refs_5_.1) | copy-start | bytes 147460
  0.0 28.4 %collective-permute-start.5 = (bf16[128,4,8,128]{3,2,1,0:T(8,128)(2,1)}, bf16[128,4,8,128]{3,2,1,0:T(8,128)(2,1)S(1)}, u32[]{:S(2)}, u32[]{:S(2)}) collective-permute-start(bf16[128,4,8,128]{3,2,1,0:T(8,128)(2,1)} %param.3), channel_id=1, source_target_pairs={{24,0},{28,4},{0,8},{4,12},{8,16},{12,20},{16,24},{20,28},{25,1},{... | collective-permute-start | bytes 3145736 | tf_op jit(solution)/shard_map/ppermute | solution.py:24
  4.9 9.2 %collective-permute-start = (bf16[128,1280]{1,0:T(8,128)(2,1)S(1)}, bf16[128,1280]{1,0:T(8,128)(2,1)S(1)}, u32[]{:S(2)}, u32[]{:S(2)}) collective-permute-start(bf16[128,1280]{1,0:T(8,128)(2,1)S(1)} %get-tuple-element.34), channel_id=1, source_target_pairs={{1,0},{0,1},{3,2},{2,3},{5,4},{4,5},{7,6},{6,7},{9,8},{8,9},{11,10... | collective-permute-start | bytes 983048 | tf_op jit(solution)/shard_map/ppermute | solution.py:24
  6.4 9.9 %collective-permute-start.1 = (bf16[128,1152]{1,0:T(8,128)(2,1)S(1)}, bf16[128,1152]{1,0:T(8,128)(2,1)S(1)}, u32[]{:S(2)}, u32[]{:S(2)}) collective-permute-start(bf16[128,1152]{1,0:T(8,128)(2,1)S(1)} %get-tuple-element.36), channel_id=1, source_target_pairs={{2,0},{0,2},{3,1},{1,3},{6,4},{4,6},{7,5},{5,7},{10,8},{8,10},{11,... | collective-permute-start | bytes 884744 | tf_op jit(solution)/shard_map/ppermute | solution.py:24
  8.0 13.0 %collective-permute-start.2 = (bf16[128,1152]{1,0:T(8,128)(2,1)S(1)}, bf16[128,1152]{1,0:T(8,128)(2,1)S(1)}, u32[]{:S(2)}, u32[]{:S(2)}) collective-permute-start(bf16[128,1152]{1,0:T(8,128)(2,1)S(1)} %get-tuple-element.37), channel_id=1, source_target_pairs={{2,0},{0,2},{3,1},{1,3},{6,4},{4,6},{7,5},{5,7},{10,8},{8,10},{11,... | collective-permute-start | bytes 884744 | tf_op jit(solution)/shard_map/ppermute | solution.py:24
  21.0 8.0 %collective-permute-start.3 = (bf16[384,2048]{1,0:T(8,128)(2,1)S(1)}, bf16[384,2048]{1,0:T(8,128)(2,1)S(1)}, u32[]{:S(2)}, u32[]{:S(2)}) collective-permute-start(bf16[384,2048]{1,0:T(8,128)(2,1)S(1)} %get-tuple-element.35.refs_0_), channel_id=1, source_target_pairs={{0,4},{4,0},{8,12},{12,8},{16,20},{20,16},{24,28},{28,24},{1,5},{5... | collective-permute-start | bytes 4718600 | tf_op jit(solution)/shard_map/ppermute | solution.py:338
  22.9 6.1 %collective-permute-start.4 = (bf16[384,2048]{1,0:T(8,128)(2,1)S(1)}, bf16[384,2048]{1,0:T(8,128)(2,1)S(1)}, u32[]{:S(2)}, u32[]{:S(2)}) collective-permute-start(bf16[384,2048]{1,0:T(8,128)(2,1)S(1)} %get-tuple-element.41.refs_1_), channel_id=1, source_target_pairs={{0,4},{4,0},{8,12},{12,8},{16,20},{20,16},{24,28},{28,24},{1,5},{5... | collective-permute-start | bytes 4718600 | tf_op jit(solution)/shard_map/ppermute | solution.py:338
  28.9 5.8 %collective-permute-start.9 = (bf16[128,4096]{1,0:T(8,128)(2,1)S(1)}, bf16[128,4096]{1,0:T(8,128)(2,1)S(1)}, u32[]{:S(2)}, u32[]{:S(2)}) collective-permute-start(bf16[128,4096]{1,0:T(8,128)(2,1)S(1)} %bitcast.15), channel_id=1, source_target_pairs={{0,4},{4,0},{8,12},{12,8},{16,20},{20,16},{24,28},{28,24},{1,5},{5... | collective-permute-start | bytes 3145736 | tf_op jit(solution)/shard_map/ppermute | solution.py:351
  31.1 7.6 %collective-permute-start.6 = (bf16[2,3,32,128]{3,2,1,0:T(8,128)(2,1)S(1)}, bf16[2,3,32,128]{3,2,1,0:T(8,128)(2,1)S(1)}, u32[]{:S(2)}, u32[]{:S(2)}) collective-permute-start(bf16[2,3,32,128]{3,2,1,0:T(8,128)(2,1)S(1)} %get-tuple-element.46), channel_id=1, source_target_pairs={{0,3},{1,2},{2,1},{3,0},{4,7},{5,6},{6,5},{7,4},{8,11},{9,10},{10,... | collective-permute-start | bytes 147464 | tf_op jit(solution)/shard_map/ppermute | solution.py:42
  33.6 5.7 %collective-permute-start.7 = (bf16[2,3,32,128]{3,2,1,0:T(8,128)(2,1)S(1)}, bf16[2,3,32,128]{3,2,1,0:T(8,128)(2,1)S(1)}, u32[]{:S(2)}, u32[]{:S(2)}) collective-permute-start(bf16[2,3,32,128]{3,2,1,0:T(8,128)(2,1)S(1)} %get-tuple-element.47), channel_id=1, source_target_pairs={{0,2},{1,3},{2,0},{3,1},{4,6},{5,7},{6,4},{7,5},{8,10},{9,11},{10,... | collective-permute-start | bytes 147464 | tf_op jit(solution)/shard_map/ppermute | solution.py:42
  34.1 5.1 %collective-permute-start.8 = (bf16[2,3,32,128]{3,2,1,0:T(8,128)(2,1)S(1)}, bf16[2,3,32,128]{3,2,1,0:T(8,128)(2,1)S(1)}, u32[]{:S(2)}, u32[]{:S(2)}) collective-permute-start(bf16[2,3,32,128]{3,2,1,0:T(8,128)(2,1)S(1)} %get-tuple-element.48), channel_id=1, source_target_pairs={{0,1},{1,0},{2,3},{3,2},{4,5},{5,4},{6,7},{7,6},{8,9},{9,8},{10,11... | collective-permute-start | bytes 147464 | tf_op jit(solution)/shard_map/ppermute | solution.py:42
  35.7 7.7 %collective-permute-start.10 = (bf16[3,3,32,128]{3,2,1,0:T(8,128)(2,1)S(1)}, bf16[3,3,32,128]{3,2,1,0:T(8,128)(2,1)S(1)}, u32[]{:S(2)}, u32[]{:S(2)}) collective-permute-start(bf16[3,3,32,128]{3,2,1,0:T(8,128)(2,1)S(1)} %get-tuple-element.54), channel_id=1, source_target_pairs={{0,3},{1,2},{2,1},{3,0},{4,7},{5,6},{6,5},{7,4},{8,11},{9,10},{10,... | collective-permute-start | bytes 221192 | tf_op jit(solution)/shard_map/ppermute | solution.py:42
  38.2 5.2 %collective-permute-start.11 = (bf16[3,3,32,128]{3,2,1,0:T(8,128)(2,1)S(1)}, bf16[3,3,32,128]{3,2,1,0:T(8,128)(2,1)S(1)}, u32[]{:S(2)}, u32[]{:S(2)}) collective-permute-start(bf16[3,3,32,128]{3,2,1,0:T(8,128)(2,1)S(1)} %get-tuple-element.55), channel_id=1, source_target_pairs={{0,2},{1,3},{2,0},{3,1},{4,6},{5,7},{6,4},{7,5},{8,10},{9,11},{10,... | collective-permute-start | bytes 221192 | tf_op jit(solution)/shard_map/ppermute | solution.py:42
  38.7 4.7 %collective-permute-start.12 = (bf16[3,3,32,128]{3,2,1,0:T(8,128)(2,1)S(1)}, bf16[3,3,32,128]{3,2,1,0:T(8,128)(2,1)S(1)}, u32[]{:S(2)}, u32[]{:S(2)}) collective-permute-start(bf16[3,3,32,128]{3,2,1,0:T(8,128)(2,1)S(1)} %get-tuple-element.56), channel_id=1, source_target_pairs={{0,1},{1,0},{2,3},{3,2},{4,5},{5,4},{6,7},{7,6},{8,9},{9,8},{10,11... | collective-permute-start | bytes 221192 | tf_op jit(solution)/shard_map/ppermute | solution.py:42
  39.3 4.1 %collective-permute-start.13 = (bf16[2,3,32,128]{3,2,1,0:T(8,128)(2,1)S(1)}, bf16[2,3,32,128]{3,2,1,0:T(8,128)(2,1)S(1)}, u32[]{:S(2)}, u32[]{:S(2)}) collective-permute-start(bf16[2,3,32,128]{3,2,1,0:T(8,128)(2,1)S(1)} %get-tuple-element.62), channel_id=1, source_target_pairs={{8,0},{12,4},{16,8},{20,12},{24,16},{28,20},{0,24},{4,28},{9,1},{1... | collective-permute-start | bytes 147464 | tf_op jit(solution)/shard_map/ppermute | solution.py:24

commit v21 on v18

--- a/solution.py
+++ b/solution.py
@@ -228,10 +228,26 @@
 def there_tiles(*refs, layer, plane, scale):
     w, w_mate, (two, psi, own), refs = refs[:2], refs[2:4], refs[4:7], refs[7:]
     mate, outs, (there, there_mate) = refs[0], refs[1:-2], refs[-2:]
-    states = two.shape[0]
-    there[...] = product(w, stacked(two), layer, True) * scale
-    both = product(w_mate, stacked(two, psi), layer, True) * scale
-    there_mate[...], mate[...] = both[:states], both[states:]
+    states, cells = two.shape
+    rows = stacked(two, psi)
+    sums = [0.0, 0.0, 0.0]
+    for part, at, start, stop in (
+        (0, 0, layer, cells - layer), (1, 0, 0, layer), (1, layer, cells - layer, cells)
+    ):
+        cols, both = slice(at, at + stop - start), rows(slice(start, stop))
+        ours, theirs = w[part], w_mate[part]
+        middle = jnp.concatenate([ours[2 * states :, cols], theirs[:states, cols]], axis=0)
+        pairs = (
+            (two[:, start:stop], ours[: 2 * states, cols]),
+            (both, middle),
+            (both, theirs[states:, cols]),
+        )
+        for n, (a, b) in enumerate(pairs):
+            sums[n] = sums[n] + lax.dot_general(a, b, NT, preferred_element_type=F32)
+    first, second, third = [total * scale for total in sums]
+    there[:, : 2 * states], there[:, 2 * states :] = first, second[:states, :states]
+    there_mate[:, :states], there_mate[:, states:] = second[:states, states:], third[:states]
+    mate[:, :states], mate[:, states:] = second[states:, states:], third[states:]
     slots = (wide_rows(there), either(tall_rows(own), wide_rows(there_mate)))
     cut(outs, slots, plane, states)
 

time: 44.4 us -> 44.2 us (level)
  no operation moved by 1% of the time
where the time goes in v21:
time: 44.2 us; the launch traced here: 44 us
  waiting for transfers between devices  16.9 us (38%)
  starting transfers between devices  16.2 us (37%)
  Pallas kernels  8.69 us (20%)
  local copies, waits for them, and re-layouts  2.16 us (5%)
    ppermute x5, waiting for transfers between devices, shift(): lax.ppermute(block, axis, [((i + distance) % count, i) for i in range(cou...  16.9 us
    pallas_call x8, Pallas kernels, call(): return list(run(*operands))  8.69 us
    ppermute x5, starting transfers between devices, shift(): lax.ppermute(block, axis, [((i + distance) % count, i) for i in range(cou...  8.4 us
    ppermute x6, starting transfers between devices, exchange(): got.append(lax.ppermute(piece, ('dx', 'dy'), route))  7.11 us
    unnamed x6, local copies, waits for them, and re-layouts  2.16 us
  transfers between devices with their start and end apart: 14, of which 5 were waited for; matrix products, arithmetic and copies ran while one was open for 5% of the time, Pallas kernels for 18%

profile of v21, /device:TPU:0, one launch (start us, length us, event | category | flops | bytes accessed | tf_op | source)
XLA Modules:
  0.0 44.0 jit_solution(6902805669533176396)
XLA Ops:
  0.0 3.0 %collective-permute-start.5 = (bf16[128,4,8,128]{3,2,1,0:T(8,128)(2,1)}, bf16[128,4,8,128]{3,2,1,0:T(8,128)(2,1)S(1)}, u32[]{:S(2)}, u32[]{:S(2)}) collective-permute-start(bf16[128,4,8,128]{3,2,1,0:T(8,128)(2,1)} %param.3), channel_id=1, source_target_pairs={{24,0},{28,4},{0,8},{4,12},{8,16},{12,20},{16,24},{20,28},{25,1},{... | collective-permute-start | bytes 3145736 | tf_op jit(solution)/shard_map/ppermute | solution.py:24
  3.0 1.7 %copy.9 = bf16[16,8,32,128]{3,1,2,0:T(8,128)(2,1)S(1)} copy(bf16[16,8,32,128]{3,2,1,0:T(8,128)(2,1)} %bitcast.18) | data formatting | bytes 2097152
  4.8 0.1 shard_map.37
  4.9 1.6 %collective-permute-start = (bf16[128,1280]{1,0:T(8,128)(2,1)S(1)}, bf16[128,1280]{1,0:T(8,128)(2,1)S(1)}, u32[]{:S(2)}, u32[]{:S(2)}) collective-permute-start(bf16[128,1280]{1,0:T(8,128)(2,1)S(1)} %get-tuple-element.34), channel_id=1, source_target_pairs={{1,0},{0,1},{3,2},{2,3},{5,4},{4,5},{7,6},{6,7},{9,8},{8,9},{11,10... | collective-permute-start | bytes 983048 | tf_op jit(solution)/shard_map/ppermute | solution.py:24
  6.4 1.5 %collective-permute-start.1 = (bf16[128,1152]{1,0:T(8,128)(2,1)S(1)}, bf16[128,1152]{1,0:T(8,128)(2,1)S(1)}, u32[]{:S(2)}, u32[]{:S(2)}) collective-permute-start(bf16[128,1152]{1,0:T(8,128)(2,1)S(1)} %get-tuple-element.36), channel_id=1, source_target_pairs={{2,0},{0,2},{3,1},{1,3},{6,4},{4,6},{7,5},{5,7},{10,8},{8,10},{11,... | collective-permute-start | bytes 884744 | tf_op jit(solution)/shard_map/ppermute | solution.py:24
  8.0 0.5 %collective-permute-start.2 = (bf16[128,1152]{1,0:T(8,128)(2,1)S(1)}, bf16[128,1152]{1,0:T(8,128)(2,1)S(1)}, u32[]{:S(2)}, u32[]{:S(2)}) collective-permute-start(bf16[128,1152]{1,0:T(8,128)(2,1)S(1)} %get-tuple-element.37), channel_id=1, source_target_pairs={{2,0},{0,2},{3,1},{1,3},{6,4},{4,6},{7,5},{5,7},{10,8},{8,10},{11,... | collective-permute-start | bytes 884744 | tf_op jit(solution)/shard_map/ppermute | solution.py:24
  8.5 5.7 %collective-permute-done.refs_1_.refs_3_ = bf16[128,1280]{1,0:T(8,128)(2,1)S(1)} collective-permute-done((bf16[128,1280]{1,0:T(8,128)(2,1)S(1)}, bf16[128,1280]{1,0:T(8,128)(2,1)S(1)}, u32[]{:S(2)}, u32[]{:S(2)}) %collective-permute-start) | collective-permute-done | bytes 327712 | tf_op jit(solution)/shard_map/ppermute | solution.py:24
  14.1 1.9 %shard_map.38 = (bf16[384,2048]{1,0:T(8,128)(2,1)S(1)}, bf16[384,2048]{1,0:T(8,128)(2,1)S(1)}) custom-call(bf16[128,4096]{1,0:T(8,128)(2,1)S(1)} %bitcast.11, bf16[128,1280]{1,0:T(8,128)(2,1)S(1)} %collective-permute-done.refs_1_.refs_3_, f32[4,8,128]{2,1,0:T(8,128)S(1)} %copy-done.1, f32[3,4,8,128]{3,2,1,0:T(8,128)S(1)} %copy-done), custom_call_target="tpu_custom_call" | custom-call | tf_op jit(solution)/shard_map/pallas_call | solution.py:58
  16.0 0.4 collective-permute-done.1.refs_1_
  16.4 4.6 %collective-permute-done.2.refs_2_ = bf16[128,1152]{1,0:T(8,128)(2,1)S(1)} collective-permute-done((bf16[128,1152]{1,0:T(8,128)(2,1)S(1)}, bf16[128,1152]{1,0:T(8,128)(2,1)S(1)}, u32[]{:S(2)}, u32[]{:S(2)}) %collective-permute-start.2) | collective-permute-done | bytes 294944 | tf_op jit(solution)/shard_map/ppermute | solution.py:24
  21.0 1.9 %shard_map.39 = (bf16[384,2048]{1,0:T(8,128)(2,1)S(1)}, bf16[384,2048]{1,0:T(8,128)(2,1)S(1)}) custom-call(bf16[128,4096]{1,0:T(8,128)(2,1)S(1)} %bitcast.12, bf16[128,1152]{1,0:T(8,128)(2,1)S(1)} %collective-permute-done.1.refs_1_, bf16[128,1152]{1,0:T(8,128)(2,1)S(1)} %collective-permute-done.2.refs_2_, ...), custom_call_target="tpu_custom_call" | custom-call | tf_op jit(solution)/shard_map/pallas_call | solution.py:58
  22.9 0.6 %collective-permute-start.4 = (bf16[384,2048]{1,0:T(8,128)(2,1)S(1)}, bf16[384,2048]{1,0:T(8,128)(2,1)S(1)}, u32[]{:S(2)}, u32[]{:S(2)}) collective-permute-start(bf16[384,2048]{1,0:T(8,128)(2,1)S(1)} %get-tuple-element.41.refs_1_), channel_id=1, source_target_pairs={{0,4},{4,0},{8,12},{12,8},{16,20},{20,16},{24,28},{28,24},{1,5},{5... | collective-permute-start | bytes 4718600 | tf_op jit(solution)/shard_map/ppermute | solution.py:336
  23.5 1.0 %shard_map.40.refs_6_.refs_4_ = f32[384,128]{1,0:T(8,128)S(1)} custom-call(bf16[384,2048]{1,0:T(8,128)(2,1)S(1)} %get-tuple-element.42.refs_0_, bf16[384,2048]{1,0:T(8,128)(2,1)S(1)} %get-tuple-element.43.refs_1_, bf16[128,4096]{1,0:T(8,128)(2,1)S(1)} %bitcast.13), custom_call_target="tpu_custom_call" | custom-call | tf_op jit(solution)/shard_map/pallas_call | solution.py:58
  24.4 4.0 %collective-permute-done.5 = bf16[128,4,8,128]{3,2,1,0:T(8,128)(2,1)S(1)} collective-permute-done((bf16[128,4,8,128]{3,2,1,0:T(8,128)(2,1)}, bf16[128,4,8,128]{3,2,1,0:T(8,128)(2,1)S(1)}, u32[]{:S(2)}, u32[]{:S(2)}) %collective-permute-start.5) | collective-permute-done | bytes 1048608 | tf_op jit(solution)/shard_map/ppermute | solution.py:24
  28.4 0.5 %copy.8 = bf16[16,8,32,128]{3,1,2,0:T(8,128)(2,1)S(1)} copy(bf16[16,8,32,128]{3,2,1,0:T(8,128)(2,1)S(1)} %bitcast.19) | data formatting | bytes 2097152
  28.9 0.1 collective-permute-start.9
  29.0 0.0 collective-permute-done.3.refs_2_
  29.0 0.0 collective-permute-done.4.refs_3_
  29.0 1.9 %shard_map.41 = (f32[128,384]{1,0:T(8,128)S(1)}, f32[2,3,32,128]{3,2,1,0:T(8,128)S(1)}, bf16[2,3,32,128]{3,2,1,0:T(8,128)(2,1)S(1)}, bf16[2,3,32,128]{3,2,1,0:T(8,128)(2,1)S(1)}, bf16[2,3,32,128]{3,2,1,0:T(8,128)(2,1)S(1)}) custom-call(bf16[384,2048]{1,0:T(8,128)(2,1)S(1)} %get-tuple-element.35.refs_0_, bf16[384,2048]{1,0:T(8,128)(2,1)S(1)} %get-tuple-element.41.refs_1_, ...), custom_call_target="tpu_custom_call" | custom-call | bytes 3000000 | tf_op jit(solution)/shard_map/pallas_call | solution.py:58
  30.9 2.5 %collective-permute-start.6 = (bf16[2,3,32,128]{3,2,1,0:T(8,128)(2,1)S(1)}, bf16[2,3,32,128]{3,2,1,0:T(8,128)(2,1)S(1)}, u32[]{:S(2)}, u32[]{:S(2)}) collective-permute-start(bf16[2,3,32,128]{3,2,1,0:T(8,128)(2,1)S(1)} %get-tuple-element.46), channel_id=1, source_target_pairs={{0,3},{1,2},{2,1},{3,0},{4,7},{5,6},{6,5},{7,4},{8,11},{9,10},{10,... | collective-permute-start | bytes 147464 | tf_op jit(solution)/shard_map/ppermute | solution.py:42
  33.4 0.5 %collective-permute-start.7 = (bf16[2,3,32,128]{3,2,1,0:T(8,128)(2,1)S(1)}, bf16[2,3,32,128]{3,2,1,0:T(8,128)(2,1)S(1)}, u32[]{:S(2)}, u32[]{:S(2)}) collective-permute-start(bf16[2,3,32,128]{3,2,1,0:T(8,128)(2,1)S(1)} %get-tuple-element.47), channel_id=1, source_target_pairs={{0,2},{1,3},{2,0},{3,1},{4,6},{5,7},{6,4},{7,5},{8,10},{9,11},{10,... | collective-permute-start | bytes 147464 | tf_op jit(solution)/shard_map/ppermute | solution.py:42
  33.9 0.5 %collective-permute-start.8 = (bf16[2,3,32,128]{3,2,1,0:T(8,128)(2,1)S(1)}, bf16[2,3,32,128]{3,2,1,0:T(8,128)(2,1)S(1)}, u32[]{:S(2)}, u32[]{:S(2)}) collective-permute-start(bf16[2,3,32,128]{3,2,1,0:T(8,128)(2,1)S(1)} %get-tuple-element.48), channel_id=1, source_target_pairs={{0,1},{1,0},{2,3},{3,2},{4,5},{5,4},{6,7},{7,6},{8,9},{9,8},{10,11... | collective-permute-start | bytes 147464 | tf_op jit(solution)/shard_map/ppermute | solution.py:42
  34.5 1.0 %shard_map.42 = (f32[3,3,32,128]{3,2,1,0:T(8,128)S(1)}, bf16[3,3,32,128]{3,2,1,0:T(8,128)(2,1)S(1)}, bf16[3,3,32,128]{3,2,1,0:T(8,128)(2,1)S(1)}, bf16[3,3,32,128]{3,2,1,0:T(8,128)(2,1)S(1)}) custom-call(bf16[384,2048]{1,0:T(8,128)(2,1)S(1)} %get-tuple-element.42.refs_0_, bf16[384,2048]{1,0:T(8,128)(2,1)S(1)} %get-tuple-element.43.refs_1_, ...), custom_call_target="tpu_custom_call" | custom-call | bytes 3000000 | tf_op jit(solution)/shard_map/pallas_call | solution.py:58
  35.5 2.5 %collective-permute-start.10 = (bf16[3,3,32,128]{3,2,1,0:T(8,128)(2,1)S(1)}, bf16[3,3,32,128]{3,2,1,0:T(8,128)(2,1)S(1)}, u32[]{:S(2)}, u32[]{:S(2)}) collective-permute-start(bf16[3,3,32,128]{3,2,1,0:T(8,128)(2,1)S(1)} %get-tuple-element.54), channel_id=1, source_target_pairs={{0,3},{1,2},{2,1},{3,0},{4,7},{5,6},{6,5},{7,4},{8,11},{9,10},{10,... | collective-permute-start | bytes 221192 | tf_op jit(solution)/shard_map/ppermute | solution.py:42
  38.0 0.5 %collective-permute-start.11 = (bf16[3,3,32,128]{3,2,1,0:T(8,128)(2,1)S(1)}, bf16[3,3,32,128]{3,2,1,0:T(8,128)(2,1)S(1)}, u32[]{:S(2)}, u32[]{:S(2)}) collective-permute-start(bf16[3,3,32,128]{3,2,1,0:T(8,128)(2,1)S(1)} %get-tuple-element.55), channel_id=1, source_target_pairs={{0,2},{1,3},{2,0},{3,1},{4,6},{5,7},{6,4},{7,5},{8,10},{9,11},{10,... | collective-permute-start | bytes 221192 | tf_op jit(solution)/shard_map/ppermute | solution.py:42
  38.5 0.5 %collective-permute-start.12 = (bf16[3,3,32,128]{3,2,1,0:T(8,128)(2,1)S(1)}, bf16[3,3,32,128]{3,2,1,0:T(8,128)(2,1)S(1)}, u32[]{:S(2)}, u32[]{:S(2)}) collective-permute-start(bf16[3,3,32,128]{3,2,1,0:T(8,128)(2,1)S(1)} %get-tuple-element.56), channel_id=1, source_target_pairs={{0,1},{1,0},{2,3},{3,2},{4,5},{5,4},{6,7},{7,6},{8,9},{9,8},{10,11... | collective-permute-start | bytes 221192 | tf_op jit(solution)/shard_map/ppermute | solution.py:42
  39.1 0.0 collective-permute-done.7.refs_2_
  39.1 0.0 collective-permute-done.8.refs_3_
  39.1 1.8 %collective-permute-start.13 = (bf16[2,3,32,128]{3,2,1,0:T(8,128)(2,1)S(1)}, bf16[2,3,32,128]{3,2,1,0:T(8,128)(2,1)S(1)}, u32[]{:S(2)}, u32[]{:S(2)}) collective-permute-start(bf16[2,3,32,128]{3,2,1,0:T(8,128)(2,1)S(1)} %get-tuple-element.62), channel_id=1, source_target_pairs={{8,0},{12,4},{16,8},{20,12},{24,16},{28,20},{0,24},{4,28},{9,1},{1... | collective-permute-start | bytes 147464 | tf_op jit(solution)/shard_map/ppermute | solution.py:24
  40.9 2.3 %collective-permute-done.13.refs_5_ = bf16[2,3,32,128]{3,2,1,0:T(8,128)(2,1)S(1)} collective-permute-done((bf16[2,3,32,128]{3,2,1,0:T(8,128)(2,1)S(1)}, bf16[2,3,32,128]{3,2,1,0:T(8,128)(2,1)S(1)}, u32[]{:S(2)}, u32[]{:S(2)}) %collective-permute-start.13) | collective-permute-done | bytes 49184 | tf_op jit(solution)/shard_map/ppermute | solution.py:24
  43.3 0.0 collective-permute-done.10.refs_1_
  43.3 0.7 %shard_map.44 = f32[3,5,32,128]{3,2,1,0:T(8,128)} custom-call(f32[3,3,32,128]{3,2,1,0:T(8,128)S(1)} %get-tuple-element.53.refs_0_, bf16[3,3,32,128]{3,2,1,0:T(8,128)(2,1)S(1)} %collective-permute-done.10.refs_1_, bf16[3,3,32,128]{3,2,1,0:T(8,128)(2,1)S(1)} %collective-permute-done.11.refs_2_, bf16[3,3,32,128]{3,2,1,0:T(8,128)(2,1)S(1)} %collective-permute-done.12.refs_3_, ...), custom_call_target="tpu_custom_call" | custom-call | tf_op jit(solution)/shard_map/pallas_call | solution.py:58
  (10 shorter events, 0.1 us)
Async XLA Ops:
  0.0 4.7 %copy-start.1 = (f32[4,8,128]{2,1,0:T(8,128)S(1)}, f32[4,8,128]{2,1,0:T(8,128)}, u32[]{:S(2)}) copy-start(f32[4,8,128]{2,1,0:T(8,128)} %refs_4_.1) | copy-start | bytes 49156
  0.0 4.7 %copy-start = (f32[3,4,8,128]{3,2,1,0:T(8,128)S(1)}, f32[3,4,8,128]{3,2,1,0:T(8,128)}, u32[]{:S(2)}) copy-start(f32[3,4,8,128]{3,2,1,0:T(8,128)} %refs_5_.1) | copy-start | bytes 147460
  0.0 28.4 %collective-permute-start.5 = (bf16[128,4,8,128]{3,2,1,0:T(8,128)(2,1)}, bf16[128,4,8,128]{3,2,1,0:T(8,128)(2,1)S(1)}, u32[]{:S(2)}, u32[]{:S(2)}) collective-permute-start(bf16[128,4,8,128]{3,2,1,0:T(8,128)(2,1)} %param.3), channel_id=1, source_target_pairs={{24,0},{28,4},{0,8},{4,12},{8,16},{12,20},{16,24},{20,28},{25,1},{... | collective-permute-start | bytes 3145736 | tf_op jit(solution)/shard_map/ppermute | solution.py:24
  4.9 9.2 %collective-permute-start = (bf16[128,1280]{1,0:T(8,128)(2,1)S(1)}, bf16[128,1280]{1,0:T(8,128)(2,1)S(1)}, u32[]{:S(2)}, u32[]{:S(2)}) collective-permute-start(bf16[128,1280]{1,0:T(8,128)(2,1)S(1)} %get-tuple-element.34), channel_id=1, source_target_pairs={{1,0},{0,1},{3,2},{2,3},{5,4},{4,5},{7,6},{6,7},{9,8},{8,9},{11,10... | collective-permute-start | bytes 983048 | tf_op jit(solution)/shard_map/ppermute | solution.py:24
  6.4 9.9 %collective-permute-start.1 = (bf16[128,1152]{1,0:T(8,128)(2,1)S(1)}, bf16[128,1152]{1,0:T(8,128)(2,1)S(1)}, u32[]{:S(2)}, u32[]{:S(2)}) collective-permute-start(bf16[128,1152]{1,0:T(8,128)(2,1)S(1)} %get-tuple-element.36), channel_id=1, source_target_pairs={{2,0},{0,2},{3,1},{1,3},{6,4},{4,6},{7,5},{5,7},{10,8},{8,10},{11,... | collective-permute-start | bytes 884744 | tf_op jit(solution)/shard_map/ppermute | solution.py:24
  8.0 13.0 %collective-permute-start.2 = (bf16[128,1152]{1,0:T(8,128)(2,1)S(1)}, bf16[128,1152]{1,0:T(8,128)(2,1)S(1)}, u32[]{:S(2)}, u32[]{:S(2)}) collective-permute-start(bf16[128,1152]{1,0:T(8,128)(2,1)S(1)} %get-tuple-element.37), channel_id=1, source_target_pairs={{2,0},{0,2},{3,1},{1,3},{6,4},{4,6},{7,5},{5,7},{10,8},{8,10},{11,... | collective-permute-start | bytes 884744 | tf_op jit(solution)/shard_map/ppermute | solution.py:24
  21.0 8.0 %collective-permute-start.3 = (bf16[384,2048]{1,0:T(8,128)(2,1)S(1)}, bf16[384,2048]{1,0:T(8,128)(2,1)S(1)}, u32[]{:S(2)}, u32[]{:S(2)}) collective-permute-start(bf16[384,2048]{1,0:T(8,128)(2,1)S(1)} %get-tuple-element.35.refs_0_), channel_id=1, source_target_pairs={{0,4},{4,0},{8,12},{12,8},{16,20},{20,16},{24,28},{28,24},{1,5},{5... | collective-permute-start | bytes 4718600 | tf_op jit(solution)/shard_map/ppermute | solution.py:336
  22.9 6.1 %collective-permute-start.4 = (bf16[384,2048]{1,0:T(8,128)(2,1)S(1)}, bf16[384,2048]{1,0:T(8,128)(2,1)S(1)}, u32[]{:S(2)}, u32[]{:S(2)}) collective-permute-start(bf16[384,2048]{1,0:T(8,128)(2,1)S(1)} %get-tuple-element.41.refs_1_), channel_id=1, source_target_pairs={{0,4},{4,0},{8,12},{12,8},{16,20},{20,16},{24,28},{28,24},{1,5},{5... | collective-permute-start | bytes 4718600 | tf_op jit(solution)/shard_map/ppermute | solution.py:336
  28.9 5.6 %collective-permute-start.9 = (bf16[128,4096]{1,0:T(8,128)(2,1)S(1)}, bf16[128,4096]{1,0:T(8,128)(2,1)S(1)}, u32[]{:S(2)}, u32[]{:S(2)}) collective-permute-start(bf16[128,4096]{1,0:T(8,128)(2,1)S(1)} %bitcast.15), channel_id=1, source_target_pairs={{0,4},{4,0},{8,12},{12,8},{16,20},{20,16},{24,28},{28,24},{1,5},{5... | collective-permute-start | bytes 3145736 | tf_op jit(solution)/shard_map/ppermute | solution.py:349
  30.9 7.6 %collective-permute-start.6 = (bf16[2,3,32,128]{3,2,1,0:T(8,128)(2,1)S(1)}, bf16[2,3,32,128]{3,2,1,0:T(8,128)(2,1)S(1)}, u32[]{:S(2)}, u32[]{:S(2)}) collective-permute-start(bf16[2,3,32,128]{3,2,1,0:T(8,128)(2,1)S(1)} %get-tuple-element.46), channel_id=1, source_target_pairs={{0,3},{1,2},{2,1},{3,0},{4,7},{5,6},{6,5},{7,4},{8,11},{9,10},{10,... | collective-permute-start | bytes 147464 | tf_op jit(solution)/shard_map/ppermute | solution.py:42
  33.4 5.6 %collective-permute-start.7 = (bf16[2,3,32,128]{3,2,1,0:T(8,128)(2,1)S(1)}, bf16[2,3,32,128]{3,2,1,0:T(8,128)(2,1)S(1)}, u32[]{:S(2)}, u32[]{:S(2)}) collective-permute-start(bf16[2,3,32,128]{3,2,1,0:T(8,128)(2,1)S(1)} %get-tuple-element.47), channel_id=1, source_target_pairs={{0,2},{1,3},{2,0},{3,1},{4,6},{5,7},{6,4},{7,5},{8,10},{9,11},{10,... | collective-permute-start | bytes 147464 | tf_op jit(solution)/shard_map/ppermute | solution.py:42
  33.9 5.1 %collective-permute-start.8 = (bf16[2,3,32,128]{3,2,1,0:T(8,128)(2,1)S(1)}, bf16[2,3,32,128]{3,2,1,0:T(8,128)(2,1)S(1)}, u32[]{:S(2)}, u32[]{:S(2)}) collective-permute-start(bf16[2,3,32,128]{3,2,1,0:T(8,128)(2,1)S(1)} %get-tuple-element.48), channel_id=1, source_target_pairs={{0,1},{1,0},{2,3},{3,2},{4,5},{5,4},{6,7},{7,6},{8,9},{9,8},{10,11... | collective-permute-start | bytes 147464 | tf_op jit(solution)/shard_map/ppermute | solution.py:42
  35.5 7.7 %collective-permute-start.10 = (bf16[3,3,32,128]{3,2,1,0:T(8,128)(2,1)S(1)}, bf16[3,3,32,128]{3,2,1,0:T(8,128)(2,1)S(1)}, u32[]{:S(2)}, u32[]{:S(2)}) collective-permute-start(bf16[3,3,32,128]{3,2,1,0:T(8,128)(2,1)S(1)} %get-tuple-element.54), channel_id=1, source_target_pairs={{0,3},{1,2},{2,1},{3,0},{4,7},{5,6},{6,5},{7,4},{8,11},{9,10},{10,... | collective-permute-start | bytes 221192 | tf_op jit(solution)/shard_map/ppermute | solution.py:42
  38.0 5.2 %collective-permute-start.11 = (bf16[3,3,32,128]{3,2,1,0:T(8,128)(2,1)S(1)}, bf16[3,3,32,128]{3,2,1,0:T(8,128)(2,1)S(1)}, u32[]{:S(2)}, u32[]{:S(2)}) collective-permute-start(bf16[3,3,32,128]{3,2,1,0:T(8,128)(2,1)S(1)} %get-tuple-element.55), channel_id=1, source_target_pairs={{0,2},{1,3},{2,0},{3,1},{4,6},{5,7},{6,4},{7,5},{8,10},{9,11},{10,... | collective-permute-start | bytes 221192 | tf_op jit(solution)/shard_map/ppermute | solution.py:42
  38.5 4.7 %collective-permute-start.12 = (bf16[3,3,32,128]{3,2,1,0:T(8,128)(2,1)S(1)}, bf16[3,3,32,128]{3,2,1,0:T(8,128)(2,1)S(1)}, u32[]{:S(2)}, u32[]{:S(2)}) collective-permute-start(bf16[3,3,32,128]{3,2,1,0:T(8,128)(2,1)S(1)} %get-tuple-element.56), channel_id=1, source_target_pairs={{0,1},{1,0},{2,3},{3,2},{4,5},{5,4},{6,7},{7,6},{8,9},{9,8},{10,11... | collective-permute-start | bytes 221192 | tf_op jit(solution)/shard_map/ppermute | solution.py:42
  39.1 4.1 %collective-permute-start.13 = (bf16[2,3,32,128]{3,2,1,0:T(8,128)(2,1)S(1)}, bf16[2,3,32,128]{3,2,1,0:T(8,128)(2,1)S(1)}, u32[]{:S(2)}, u32[]{:S(2)}) collective-permute-start(bf16[2,3,32,128]{3,2,1,0:T(8,128)(2,1)S(1)} %get-tuple-element.62), channel_id=1, source_target_pairs={{8,0},{12,4},{16,8},{20,12},{24,16},{28,20},{0,24},{4,28},{9,1},{1... | collective-permute-start | bytes 147464 | tf_op jit(solution)/shard_map/ppermute | solution.py:24

commit v22 on v18

--- a/solution.py
+++ b/solution.py
@@ -228,10 +228,36 @@
 def there_tiles(*refs, layer, plane, scale):
     w, w_mate, (two, psi, own), refs = refs[:2], refs[2:4], refs[4:7], refs[7:]
     mate, outs, (there, there_mate) = refs[0], refs[1:-2], refs[-2:]
-    states = two.shape[0]
-    there[...] = product(w, stacked(two), layer, True) * scale
-    both = product(w_mate, stacked(two, psi), layer, True) * scale
-    there_mate[...], mate[...] = both[:states], both[states:]
+    states, cells = two.shape
+    rows = stacked(two, psi)
+    places = ((0, 0, layer, cells - layer), (1, 0, 0, layer), (1, layer, cells - layer, cells))
+
+    def total(pair):
+        value = 0.0
+        for part, at, start, stop in places:
+            a, b = pair(w[part], w_mate[part], slice(at, at + stop - start), slice(start, stop))
+            value = value + lax.dot_general(a, b, NT, preferred_element_type=F32)
+        return value * scale
+
+    def middle(ours, theirs, cols, panel_cols):
+        parts = [ours[2 * states :, cols], theirs[:states, cols]]
+        return rows(panel_cols), jnp.concatenate(parts, axis=0)
+
+    there[:, : 2 * states] = total(lambda ours, _, cols, at: (two[:, at], ours[: 2 * states, cols]))
+    second = total(middle)
+    there[:, 2 * states :] = second[:states, :states]
+    there_mate[:, :states], mate[:, :states] = second[:states, states:], second[states:, states:]
+    core = lax.rem(lax.axis_index("blk"), 2)
+
+    @pl.when(core == 0)
+    def _():
+        mate[:, states:] = total(lambda _, theirs, cols, at: (psi[:, at], theirs[states:, cols]))
+
+    @pl.when(core == 1)
+    def _():
+        third = total(lambda _, theirs, cols, at: (rows(at), theirs[states:, cols]))
+        there_mate[:, states:], mate[:, states:] = third[:states], third[states:]
+
     slots = (wide_rows(there), either(tall_rows(own), wide_rows(there_mate)))
     cut(outs, slots, plane, states)
 

time: 44.4 us -> 44.4 us (level)
  no operation moved by 1% of the time
where the time goes in v22:
time: 44.4 us; the launch traced here: 44.2 us
  waiting for transfers between devices  16.9 us (38%)
  starting transfers between devices  16.2 us (36%)
  Pallas kernels  8.9 us (20%)
  local copies, waits for them, and re-layouts  2.16 us (5%)
    ppermute x5, waiting for transfers between devices, shift(): lax.ppermute(block, axis, [((i + distance) % count, i) for i in range(cou...  16.9 us
    pallas_call x8, Pallas kernels, call(): return list(run(*operands))  8.9 us
    ppermute x5, starting transfers between devices, shift(): lax.ppermute(block, axis, [((i + distance) % count, i) for i in range(cou...  8.4 us
    ppermute x6, starting transfers between devices, exchange(): got.append(lax.ppermute(piece, ('dx', 'dy'), route))  7.11 us
    unnamed x6, local copies, waits for them, and re-layouts  2.16 us
  transfers between devices with their start and end apart: 14, of which 5 were waited for; matrix products, arithmetic and copies ran while one was open for 5% of the time, Pallas kernels for 18%

profile of v22, /device:TPU:0, one launch (start us, length us, event | category | flops | bytes accessed | tf_op | source)
XLA Modules:
  0.0 44.2 jit_solution(8312962271528593138)
XLA Ops:
  0.0 3.0 %collective-permute-start.5 = (bf16[128,4,8,128]{3,2,1,0:T(8,128)(2,1)}, bf16[128,4,8,128]{3,2,1,0:T(8,128)(2,1)S(1)}, u32[]{:S(2)}, u32[]{:S(2)}) collective-permute-start(bf16[128,4,8,128]{3,2,1,0:T(8,128)(2,1)} %param.3), channel_id=1, source_target_pairs={{24,0},{28,4},{0,8},{4,12},{8,16},{12,20},{16,24},{20,28},{25,1},{... | collective-permute-start | bytes 3145736 | tf_op jit(solution)/shard_map/ppermute | solution.py:24
  3.0 1.7 %copy.9 = bf16[16,8,32,128]{3,1,2,0:T(8,128)(2,1)S(1)} copy(bf16[16,8,32,128]{3,2,1,0:T(8,128)(2,1)} %bitcast.18) | data formatting | bytes 2097152
  4.8 0.1 shard_map.37
  4.9 1.6 %collective-permute-start = (bf16[128,1280]{1,0:T(8,128)(2,1)S(1)}, bf16[128,1280]{1,0:T(8,128)(2,1)S(1)}, u32[]{:S(2)}, u32[]{:S(2)}) collective-permute-start(bf16[128,1280]{1,0:T(8,128)(2,1)S(1)} %get-tuple-element.34), channel_id=1, source_target_pairs={{1,0},{0,1},{3,2},{2,3},{5,4},{4,5},{7,6},{6,7},{9,8},{8,9},{11,10... | collective-permute-start | bytes 983048 | tf_op jit(solution)/shard_map/ppermute | solution.py:24
  6.4 1.5 %collective-permute-start.1 = (bf16[128,1152]{1,0:T(8,128)(2,1)S(1)}, bf16[128,1152]{1,0:T(8,128)(2,1)S(1)}, u32[]{:S(2)}, u32[]{:S(2)}) collective-permute-start(bf16[128,1152]{1,0:T(8,128)(2,1)S(1)} %get-tuple-element.36), channel_id=1, source_target_pairs={{2,0},{0,2},{3,1},{1,3},{6,4},{4,6},{7,5},{5,7},{10,8},{8,10},{11,... | collective-permute-start | bytes 884744 | tf_op jit(solution)/shard_map/ppermute | solution.py:24
  8.0 0.5 %collective-permute-start.2 = (bf16[128,1152]{1,0:T(8,128)(2,1)S(1)}, bf16[128,1152]{1,0:T(8,128)(2,1)S(1)}, u32[]{:S(2)}, u32[]{:S(2)}) collective-permute-start(bf16[128,1152]{1,0:T(8,128)(2,1)S(1)} %get-tuple-element.37), channel_id=1, source_target_pairs={{2,0},{0,2},{3,1},{1,3},{6,4},{4,6},{7,5},{5,7},{10,8},{8,10},{11,... | collective-permute-start | bytes 884744 | tf_op jit(solution)/shard_map/ppermute | solution.py:24
  8.5 5.7 %collective-permute-done.refs_1_.refs_3_ = bf16[128,1280]{1,0:T(8,128)(2,1)S(1)} collective-permute-done((bf16[128,1280]{1,0:T(8,128)(2,1)S(1)}, bf16[128,1280]{1,0:T(8,128)(2,1)S(1)}, u32[]{:S(2)}, u32[]{:S(2)}) %collective-permute-start) | collective-permute-done | bytes 327712 | tf_op jit(solution)/shard_map/ppermute | solution.py:24
  14.1 1.9 %shard_map.38 = (bf16[384,2048]{1,0:T(8,128)(2,1)S(1)}, bf16[384,2048]{1,0:T(8,128)(2,1)S(1)}) custom-call(bf16[128,4096]{1,0:T(8,128)(2,1)S(1)} %bitcast.11, bf16[128,1280]{1,0:T(8,128)(2,1)S(1)} %collective-permute-done.refs_1_.refs_3_, f32[4,8,128]{2,1,0:T(8,128)S(1)} %copy-done.1, f32[3,4,8,128]{3,2,1,0:T(8,128)S(1)} %copy-done), custom_call_target="tpu_custom_call" | custom-call | tf_op jit(solution)/shard_map/pallas_call | solution.py:58
  16.0 0.4 collective-permute-done.1.refs_1_
  16.4 4.6 %collective-permute-done.2.refs_2_ = bf16[128,1152]{1,0:T(8,128)(2,1)S(1)} collective-permute-done((bf16[128,1152]{1,0:T(8,128)(2,1)S(1)}, bf16[128,1152]{1,0:T(8,128)(2,1)S(1)}, u32[]{:S(2)}, u32[]{:S(2)}) %collective-permute-start.2) | collective-permute-done | bytes 294944 | tf_op jit(solution)/shard_map/ppermute | solution.py:24
  21.0 0.0 collective-permute-start.3
  21.0 1.9 %shard_map.39 = (bf16[384,2048]{1,0:T(8,128)(2,1)S(1)}, bf16[384,2048]{1,0:T(8,128)(2,1)S(1)}) custom-call(bf16[128,4096]{1,0:T(8,128)(2,1)S(1)} %bitcast.12, bf16[128,1152]{1,0:T(8,128)(2,1)S(1)} %collective-permute-done.1.refs_1_, bf16[128,1152]{1,0:T(8,128)(2,1)S(1)} %collective-permute-done.2.refs_2_, ...), custom_call_target="tpu_custom_call" | custom-call | tf_op jit(solution)/shard_map/pallas_call | solution.py:58
  22.9 0.6 %collective-permute-start.4 = (bf16[384,2048]{1,0:T(8,128)(2,1)S(1)}, bf16[384,2048]{1,0:T(8,128)(2,1)S(1)}, u32[]{:S(2)}, u32[]{:S(2)}) collective-permute-start(bf16[384,2048]{1,0:T(8,128)(2,1)S(1)} %get-tuple-element.41.refs_1_), channel_id=1, source_target_pairs={{0,4},{4,0},{8,12},{12,8},{16,20},{20,16},{24,28},{28,24},{1,5},{5... | collective-permute-start | bytes 4718600 | tf_op jit(solution)/shard_map/ppermute | solution.py:346
  23.5 1.0 %shard_map.40.refs_6_.refs_4_ = f32[384,128]{1,0:T(8,128)S(1)} custom-call(bf16[384,2048]{1,0:T(8,128)(2,1)S(1)} %get-tuple-element.42.refs_0_, bf16[384,2048]{1,0:T(8,128)(2,1)S(1)} %get-tuple-element.43.refs_1_, bf16[128,4096]{1,0:T(8,128)(2,1)S(1)} %bitcast.13), custom_call_target="tpu_custom_call" | custom-call | tf_op jit(solution)/shard_map/pallas_call | solution.py:58
  24.4 4.0 %collective-permute-done.5 = bf16[128,4,8,128]{3,2,1,0:T(8,128)(2,1)S(1)} collective-permute-done((bf16[128,4,8,128]{3,2,1,0:T(8,128)(2,1)}, bf16[128,4,8,128]{3,2,1,0:T(8,128)(2,1)S(1)}, u32[]{:S(2)}, u32[]{:S(2)}) %collective-permute-start.5) | collective-permute-done | bytes 1048608 | tf_op jit(solution)/shard_map/ppermute | solution.py:24
  28.4 0.5 %copy.8 = bf16[16,8,32,128]{3,1,2,0:T(8,128)(2,1)S(1)} copy(bf16[16,8,32,128]{3,2,1,0:T(8,128)(2,1)S(1)} %bitcast.19) | data formatting | bytes 2097152
  28.9 0.1 collective-permute-start.9
  29.0 0.0 collective-permute-done.3.refs_2_
  29.0 2.2 %shard_map.41 = (f32[128,384]{1,0:T(8,128)S(1)}, f32[2,3,32,128]{3,2,1,0:T(8,128)S(1)}, bf16[2,3,32,128]{3,2,1,0:T(8,128)(2,1)S(1)}, bf16[2,3,32,128]{3,2,1,0:T(8,128)(2,1)S(1)}, bf16[2,3,32,128]{3,2,1,0:T(8,128)(2,1)S(1)}) custom-call(bf16[384,2048]{1,0:T(8,128)(2,1)S(1)} %get-tuple-element.35.refs_0_, bf16[384,2048]{1,0:T(8,128)(2,1)S(1)} %get-tuple-element.41.refs_1_, ...), custom_call_target="tpu_custom_call" | custom-call | bytes 3000000 | tf_op jit(solution)/shard_map/pallas_call | solution.py:58
  31.1 2.5 %collective-permute-start.6 = (bf16[2,3,32,128]{3,2,1,0:T(8,128)(2,1)S(1)}, bf16[2,3,32,128]{3,2,1,0:T(8,128)(2,1)S(1)}, u32[]{:S(2)}, u32[]{:S(2)}) collective-permute-start(bf16[2,3,32,128]{3,2,1,0:T(8,128)(2,1)S(1)} %get-tuple-element.46), channel_id=1, source_target_pairs={{0,3},{1,2},{2,1},{3,0},{4,7},{5,6},{6,5},{7,4},{8,11},{9,10},{10,... | collective-permute-start | bytes 147464 | tf_op jit(solution)/shard_map/ppermute | solution.py:42
  33.6 0.5 %collective-permute-start.7 = (bf16[2,3,32,128]{3,2,1,0:T(8,128)(2,1)S(1)}, bf16[2,3,32,128]{3,2,1,0:T(8,128)(2,1)S(1)}, u32[]{:S(2)}, u32[]{:S(2)}) collective-permute-start(bf16[2,3,32,128]{3,2,1,0:T(8,128)(2,1)S(1)} %get-tuple-element.47), channel_id=1, source_target_pairs={{0,2},{1,3},{2,0},{3,1},{4,6},{5,7},{6,4},{7,5},{8,10},{9,11},{10,... | collective-permute-start | bytes 147464 | tf_op jit(solution)/shard_map/ppermute | solution.py:42
  34.2 0.5 %collective-permute-start.8 = (bf16[2,3,32,128]{3,2,1,0:T(8,128)(2,1)S(1)}, bf16[2,3,32,128]{3,2,1,0:T(8,128)(2,1)S(1)}, u32[]{:S(2)}, u32[]{:S(2)}) collective-permute-start(bf16[2,3,32,128]{3,2,1,0:T(8,128)(2,1)S(1)} %get-tuple-element.48), channel_id=1, source_target_pairs={{0,1},{1,0},{2,3},{3,2},{4,5},{5,4},{6,7},{7,6},{8,9},{9,8},{10,11... | collective-permute-start | bytes 147464 | tf_op jit(solution)/shard_map/ppermute | solution.py:42
  34.7 0.0 collective-permute-done.9.refs_3_
  34.7 1.0 %shard_map.42 = (f32[3,3,32,128]{3,2,1,0:T(8,128)S(1)}, bf16[3,3,32,128]{3,2,1,0:T(8,128)(2,1)S(1)}, bf16[3,3,32,128]{3,2,1,0:T(8,128)(2,1)S(1)}, bf16[3,3,32,128]{3,2,1,0:T(8,128)(2,1)S(1)}) custom-call(bf16[384,2048]{1,0:T(8,128)(2,1)S(1)} %get-tuple-element.42.refs_0_, bf16[384,2048]{1,0:T(8,128)(2,1)S(1)} %get-tuple-element.43.refs_1_, ...), custom_call_target="tpu_custom_call" | custom-call | bytes 3000000 | tf_op jit(solution)/shard_map/pallas_call | solution.py:58
  35.7 2.5 %collective-permute-start.10 = (bf16[3,3,32,128]{3,2,1,0:T(8,128)(2,1)S(1)}, bf16[3,3,32,128]{3,2,1,0:T(8,128)(2,1)S(1)}, u32[]{:S(2)}, u32[]{:S(2)}) collective-permute-start(bf16[3,3,32,128]{3,2,1,0:T(8,128)(2,1)S(1)} %get-tuple-element.54), channel_id=1, source_target_pairs={{0,3},{1,2},{2,1},{3,0},{4,7},{5,6},{6,5},{7,4},{8,11},{9,10},{10,... | collective-permute-start | bytes 221192 | tf_op jit(solution)/shard_map/ppermute | solution.py:42
  38.2 0.5 %collective-permute-start.11 = (bf16[3,3,32,128]{3,2,1,0:T(8,128)(2,1)S(1)}, bf16[3,3,32,128]{3,2,1,0:T(8,128)(2,1)S(1)}, u32[]{:S(2)}, u32[]{:S(2)}) collective-permute-start(bf16[3,3,32,128]{3,2,1,0:T(8,128)(2,1)S(1)} %get-tuple-element.55), channel_id=1, source_target_pairs={{0,2},{1,3},{2,0},{3,1},{4,6},{5,7},{6,4},{7,5},{8,10},{9,11},{10,... | collective-permute-start | bytes 221192 | tf_op jit(solution)/shard_map/ppermute | solution.py:42
  38.8 0.0 collective-permute-done.6.refs_1_
  38.8 0.5 %collective-permute-start.12 = (bf16[3,3,32,128]{3,2,1,0:T(8,128)(2,1)S(1)}, bf16[3,3,32,128]{3,2,1,0:T(8,128)(2,1)S(1)}, u32[]{:S(2)}, u32[]{:S(2)}) collective-permute-start(bf16[3,3,32,128]{3,2,1,0:T(8,128)(2,1)S(1)} %get-tuple-element.56), channel_id=1, source_target_pairs={{0,1},{1,0},{2,3},{3,2},{4,5},{5,4},{6,7},{7,6},{8,9},{9,8},{10,11... | collective-permute-start | bytes 221192 | tf_op jit(solution)/shard_map/ppermute | solution.py:42
  39.3 1.8 %collective-permute-start.13 = (bf16[2,3,32,128]{3,2,1,0:T(8,128)(2,1)S(1)}, bf16[2,3,32,128]{3,2,1,0:T(8,128)(2,1)S(1)}, u32[]{:S(2)}, u32[]{:S(2)}) collective-permute-start(bf16[2,3,32,128]{3,2,1,0:T(8,128)(2,1)S(1)} %get-tuple-element.62), channel_id=1, source_target_pairs={{8,0},{12,4},{16,8},{20,12},{24,16},{28,20},{0,24},{4,28},{9,1},{1... | collective-permute-start | bytes 147464 | tf_op jit(solution)/shard_map/ppermute | solution.py:24
  41.1 2.3 %collective-permute-done.13.refs_5_ = bf16[2,3,32,128]{3,2,1,0:T(8,128)(2,1)S(1)} collective-permute-done((bf16[2,3,32,128]{3,2,1,0:T(8,128)(2,1)S(1)}, bf16[2,3,32,128]{3,2,1,0:T(8,128)(2,1)S(1)}, u32[]{:S(2)}, u32[]{:S(2)}) %collective-permute-start.13) | collective-permute-done | bytes 49184 | tf_op jit(solution)/shard_map/ppermute | solution.py:24
  43.5 0.0 collective-permute-done.10.refs_1_
  43.5 0.7 %shard_map.44 = f32[3,5,32,128]{3,2,1,0:T(8,128)} custom-call(f32[3,3,32,128]{3,2,1,0:T(8,128)S(1)} %get-tuple-element.53.refs_0_, bf16[3,3,32,128]{3,2,1,0:T(8,128)(2,1)S(1)} %collective-permute-done.10.refs_1_, bf16[3,3,32,128]{3,2,1,0:T(8,128)(2,1)S(1)} %collective-permute-done.11.refs_2_, bf16[3,3,32,128]{3,2,1,0:T(8,128)(2,1)S(1)} %collective-permute-done.12.refs_3_, ...), custom_call_target="tpu_custom_call" | custom-call | tf_op jit(solution)/shard_map/pallas_call | solution.py:58
  (10 shorter events, 0.1 us)
Async XLA Ops:
  0.0 4.7 %copy-start.1 = (f32[4,8,128]{2,1,0:T(8,128)S(1)}, f32[4,8,128]{2,1,0:T(8,128)}, u32[]{:S(2)}) copy-start(f32[4,8,128]{2,1,0:T(8,128)} %refs_4_.1) | copy-start | bytes 49156
  0.0 4.7 %copy-start = (f32[3,4,8,128]{3,2,1,0:T(8,128)S(1)}, f32[3,4,8,128]{3,2,1,0:T(8,128)}, u32[]{:S(2)}) copy-start(f32[3,4,8,128]{3,2,1,0:T(8,128)} %refs_5_.1) | copy-start | bytes 147460
  0.0 28.4 %collective-permute-start.5 = (bf16[128,4,8,128]{3,2,1,0:T(8,128)(2,1)}, bf16[128,4,8,128]{3,2,1,0:T(8,128)(2,1)S(1)}, u32[]{:S(2)}, u32[]{:S(2)}) collective-permute-start(bf16[128,4,8,128]{3,2,1,0:T(8,128)(2,1)} %param.3), channel_id=1, source_target_pairs={{24,0},{28,4},{0,8},{4,12},{8,16},{12,20},{16,24},{20,28},{25,1},{... | collective-permute-start | bytes 3145736 | tf_op jit(solution)/shard_map/ppermute | solution.py:24
  4.9 9.2 %collective-permute-start = (bf16[128,1280]{1,0:T(8,128)(2,1)S(1)}, bf16[128,1280]{1,0:T(8,128)(2,1)S(1)}, u32[]{:S(2)}, u32[]{:S(2)}) collective-permute-start(bf16[128,1280]{1,0:T(8,128)(2,1)S(1)} %get-tuple-element.34), channel_id=1, source_target_pairs={{1,0},{0,1},{3,2},{2,3},{5,4},{4,5},{7,6},{6,7},{9,8},{8,9},{11,10... | collective-permute-start | bytes 983048 | tf_op jit(solution)/shard_map/ppermute | solution.py:24
  6.4 9.9 %collective-permute-start.1 = (bf16[128,1152]{1,0:T(8,128)(2,1)S(1)}, bf16[128,1152]{1,0:T(8,128)(2,1)S(1)}, u32[]{:S(2)}, u32[]{:S(2)}) collective-permute-start(bf16[128,1152]{1,0:T(8,128)(2,1)S(1)} %get-tuple-element.36), channel_id=1, source_target_pairs={{2,0},{0,2},{3,1},{1,3},{6,4},{4,6},{7,5},{5,7},{10,8},{8,10},{11,... | collective-permute-start | bytes 884744 | tf_op jit(solution)/shard_map/ppermute | solution.py:24
  8.0 13.0 %collective-permute-start.2 = (bf16[128,1152]{1,0:T(8,128)(2,1)S(1)}, bf16[128,1152]{1,0:T(8,128)(2,1)S(1)}, u32[]{:S(2)}, u32[]{:S(2)}) collective-permute-start(bf16[128,1152]{1,0:T(8,128)(2,1)S(1)} %get-tuple-element.37), channel_id=1, source_target_pairs={{2,0},{0,2},{3,1},{1,3},{6,4},{4,6},{7,5},{5,7},{10,8},{8,10},{11,... | collective-permute-start | bytes 884744 | tf_op jit(solution)/shard_map/ppermute | solution.py:24
  21.0 8.0 %collective-permute-start.3 = (bf16[384,2048]{1,0:T(8,128)(2,1)S(1)}, bf16[384,2048]{1,0:T(8,128)(2,1)S(1)}, u32[]{:S(2)}, u32[]{:S(2)}) collective-permute-start(bf16[384,2048]{1,0:T(8,128)(2,1)S(1)} %get-tuple-element.35.refs_0_), channel_id=1, source_target_pairs={{0,4},{4,0},{8,12},{12,8},{16,20},{20,16},{24,28},{28,24},{1,5},{5... | collective-permute-start | bytes 4718600 | tf_op jit(solution)/shard_map/ppermute | solution.py:346
  22.9 6.1 %collective-permute-start.4 = (bf16[384,2048]{1,0:T(8,128)(2,1)S(1)}, bf16[384,2048]{1,0:T(8,128)(2,1)S(1)}, u32[]{:S(2)}, u32[]{:S(2)}) collective-permute-start(bf16[384,2048]{1,0:T(8,128)(2,1)S(1)} %get-tuple-element.41.refs_1_), channel_id=1, source_target_pairs={{0,4},{4,0},{8,12},{12,8},{16,20},{20,16},{24,28},{28,24},{1,5},{5... | collective-permute-start | bytes 4718600 | tf_op jit(solution)/shard_map/ppermute | solution.py:346
  28.9 5.8 %collective-permute-start.9 = (bf16[128,4096]{1,0:T(8,128)(2,1)S(1)}, bf16[128,4096]{1,0:T(8,128)(2,1)S(1)}, u32[]{:S(2)}, u32[]{:S(2)}) collective-permute-start(bf16[128,4096]{1,0:T(8,128)(2,1)S(1)} %bitcast.15), channel_id=1, source_target_pairs={{0,4},{4,0},{8,12},{12,8},{16,20},{20,16},{24,28},{28,24},{1,5},{5... | collective-permute-start | bytes 3145736 | tf_op jit(solution)/shard_map/ppermute | solution.py:359
  31.1 7.6 %collective-permute-start.6 = (bf16[2,3,32,128]{3,2,1,0:T(8,128)(2,1)S(1)}, bf16[2,3,32,128]{3,2,1,0:T(8,128)(2,1)S(1)}, u32[]{:S(2)}, u32[]{:S(2)}) collective-permute-start(bf16[2,3,32,128]{3,2,1,0:T(8,128)(2,1)S(1)} %get-tuple-element.46), channel_id=1, source_target_pairs={{0,3},{1,2},{2,1},{3,0},{4,7},{5,6},{6,5},{7,4},{8,11},{9,10},{10,... | collective-permute-start | bytes 147464 | tf_op jit(solution)/shard_map/ppermute | solution.py:42
  33.6 5.6 %collective-permute-start.7 = (bf16[2,3,32,128]{3,2,1,0:T(8,128)(2,1)S(1)}, bf16[2,3,32,128]{3,2,1,0:T(8,128)(2,1)S(1)}, u32[]{:S(2)}, u32[]{:S(2)}) collective-permute-start(bf16[2,3,32,128]{3,2,1,0:T(8,128)(2,1)S(1)} %get-tuple-element.47), channel_id=1, source_target_pairs={{0,2},{1,3},{2,0},{3,1},{4,6},{5,7},{6,4},{7,5},{8,10},{9,11},{10,... | collective-permute-start | bytes 147464 | tf_op jit(solution)/shard_map/ppermute | solution.py:42
  34.2 5.1 %collective-permute-start.8 = (bf16[2,3,32,128]{3,2,1,0:T(8,128)(2,1)S(1)}, bf16[2,3,32,128]{3,2,1,0:T(8,128)(2,1)S(1)}, u32[]{:S(2)}, u32[]{:S(2)}) collective-permute-start(bf16[2,3,32,128]{3,2,1,0:T(8,128)(2,1)S(1)} %get-tuple-element.48), channel_id=1, source_target_pairs={{0,1},{1,0},{2,3},{3,2},{4,5},{5,4},{6,7},{7,6},{8,9},{9,8},{10,11... | collective-permute-start | bytes 147464 | tf_op jit(solution)/shard_map/ppermute | solution.py:42
  35.7 7.7 %collective-permute-start.10 = (bf16[3,3,32,128]{3,2,1,0:T(8,128)(2,1)S(1)}, bf16[3,3,32,128]{3,2,1,0:T(8,128)(2,1)S(1)}, u32[]{:S(2)}, u32[]{:S(2)}) collective-permute-start(bf16[3,3,32,128]{3,2,1,0:T(8,128)(2,1)S(1)} %get-tuple-element.54), channel_id=1, source_target_pairs={{0,3},{1,2},{2,1},{3,0},{4,7},{5,6},{6,5},{7,4},{8,11},{9,10},{10,... | collective-permute-start | bytes 221192 | tf_op jit(solution)/shard_map/ppermute | solution.py:42
  38.2 5.2 %collective-permute-start.11 = (bf16[3,3,32,128]{3,2,1,0:T(8,128)(2,1)S(1)}, bf16[3,3,32,128]{3,2,1,0:T(8,128)(2,1)S(1)}, u32[]{:S(2)}, u32[]{:S(2)}) collective-permute-start(bf16[3,3,32,128]{3,2,1,0:T(8,128)(2,1)S(1)} %get-tuple-element.55), channel_id=1, source_target_pairs={{0,2},{1,3},{2,0},{3,1},{4,6},{5,7},{6,4},{7,5},{8,10},{9,11},{10,... | collective-permute-start | bytes 221192 | tf_op jit(solution)/shard_map/ppermute | solution.py:42
  38.8 4.7 %collective-permute-start.12 = (bf16[3,3,32,128]{3,2,1,0:T(8,128)(2,1)S(1)}, bf16[3,3,32,128]{3,2,1,0:T(8,128)(2,1)S(1)}, u32[]{:S(2)}, u32[]{:S(2)}) collective-permute-start(bf16[3,3,32,128]{3,2,1,0:T(8,128)(2,1)S(1)} %get-tuple-element.56), channel_id=1, source_target_pairs={{0,1},{1,0},{2,3},{3,2},{4,5},{5,4},{6,7},{7,6},{8,9},{9,8},{10,11... | collective-permute-start | bytes 221192 | tf_op jit(solution)/shard_map/ppermute | solution.py:42
  39.3 4.1 %collective-permute-start.13 = (bf16[2,3,32,128]{3,2,1,0:T(8,128)(2,1)S(1)}, bf16[2,3,32,128]{3,2,1,0:T(8,128)(2,1)S(1)}, u32[]{:S(2)}, u32[]{:S(2)}) collective-permute-start(bf16[2,3,32,128]{3,2,1,0:T(8,128)(2,1)S(1)} %get-tuple-element.62), channel_id=1, source_target_pairs={{8,0},{12,4},{16,8},{20,12},{24,16},{28,20},{0,24},{4,28},{9,1},{1... | collective-permute-start | bytes 147464 | tf_op jit(solution)/shard_map/ppermute | solution.py:24

commit v23 on v21

--- a/solution.py
+++ b/solution.py
@@ -231,10 +231,10 @@
     states, cells = two.shape
     rows = stacked(two, psi)
     sums = [0.0, 0.0, 0.0]
-    for part, at, start, stop in (
-        (0, 0, layer, cells - layer), (1, 0, 0, layer), (1, layer, cells - layer, cells)
-    ):
-        cols, both = slice(at, at + stop - start), rows(slice(start, stop))
+    ends = [(1, 0, 0), (1, layer, cells - layer)]
+    for part, at, start in [(0, n, n + layer) for n in range(0, cells - 2 * layer, layer)] + ends:
+        stop = start + layer
+        cols, both = slice(at, at + layer), rows(slice(start, stop))
         ours, theirs = w[part], w_mate[part]
         middle = jnp.concatenate([ours[2 * states :, cols], theirs[:states, cols]], axis=0)
         pairs = (

time: 44.2 us -> 44.1 us (level)
  no operation moved by 1% of the time
where the time goes in v23:
time: 44.1 us; the launch traced here: 44 us
  waiting for transfers between devices  16.9 us (38%)
  starting transfers between devices  16.2 us (37%)
  Pallas kernels  8.64 us (20%)
  local copies, waits for them, and re-layouts  2.16 us (5%)
    ppermute x5, waiting for transfers between devices, shift(): lax.ppermute(block, axis, [((i + distance) % count, i) for i in range(cou...  16.9 us
    pallas_call x8, Pallas kernels, call(): return list(run(*operands))  8.64 us
    ppermute x5, starting transfers between devices, shift(): lax.ppermute(block, axis, [((i + distance) % count, i) for i in range(cou...  8.4 us
    ppermute x6, starting transfers between devices, exchange(): got.append(lax.ppermute(piece, ('dx', 'dy'), route))  7.11 us
    unnamed x6, local copies, waits for them, and re-layouts  2.16 us
  transfers between devices with their start and end apart: 14, of which 5 were waited for; matrix products, arithmetic and copies ran while one was open for 5% of the time, Pallas kernels for 18%

profile of v23, /device:TPU:0, one launch (start us, length us, event | category | flops | bytes accessed | tf_op | source)
XLA Modules:
  0.0 44.0 jit_solution(431557574688363280)
XLA Ops:
  0.0 3.0 %collective-permute-start.5 = (bf16[128,4,8,128]{3,2,1,0:T(8,128)(2,1)}, bf16[128,4,8,128]{3,2,1,0:T(8,128)(2,1)S(1)}, u32[]{:S(2)}, u32[]{:S(2)}) collective-permute-start(bf16[128,4,8,128]{3,2,1,0:T(8,128)(2,1)} %param.3), channel_id=1, source_target_pairs={{24,0},{28,4},{0,8},{4,12},{8,16},{12,20},{16,24},{20,28},{25,1},{... | collective-permute-start | bytes 3145736 | tf_op jit(solution)/shard_map/ppermute | solution.py:24
  3.0 1.7 %copy.9 = bf16[16,8,32,128]{3,1,2,0:T(8,128)(2,1)S(1)} copy(bf16[16,8,32,128]{3,2,1,0:T(8,128)(2,1)} %bitcast.18) | data formatting | bytes 2097152
  4.8 0.1 shard_map.37
  4.9 1.6 %collective-permute-start = (bf16[128,1280]{1,0:T(8,128)(2,1)S(1)}, bf16[128,1280]{1,0:T(8,128)(2,1)S(1)}, u32[]{:S(2)}, u32[]{:S(2)}) collective-permute-start(bf16[128,1280]{1,0:T(8,128)(2,1)S(1)} %get-tuple-element.34), channel_id=1, source_target_pairs={{1,0},{0,1},{3,2},{2,3},{5,4},{4,5},{7,6},{6,7},{9,8},{8,9},{11,10... | collective-permute-start | bytes 983048 | tf_op jit(solution)/shard_map/ppermute | solution.py:24
  6.4 1.5 %collective-permute-start.1 = (bf16[128,1152]{1,0:T(8,128)(2,1)S(1)}, bf16[128,1152]{1,0:T(8,128)(2,1)S(1)}, u32[]{:S(2)}, u32[]{:S(2)}) collective-permute-start(bf16[128,1152]{1,0:T(8,128)(2,1)S(1)} %get-tuple-element.36), channel_id=1, source_target_pairs={{2,0},{0,2},{3,1},{1,3},{6,4},{4,6},{7,5},{5,7},{10,8},{8,10},{11,... | collective-permute-start | bytes 884744 | tf_op jit(solution)/shard_map/ppermute | solution.py:24
  8.0 0.5 %collective-permute-start.2 = (bf16[128,1152]{1,0:T(8,128)(2,1)S(1)}, bf16[128,1152]{1,0:T(8,128)(2,1)S(1)}, u32[]{:S(2)}, u32[]{:S(2)}) collective-permute-start(bf16[128,1152]{1,0:T(8,128)(2,1)S(1)} %get-tuple-element.37), channel_id=1, source_target_pairs={{2,0},{0,2},{3,1},{1,3},{6,4},{4,6},{7,5},{5,7},{10,8},{8,10},{11,... | collective-permute-start | bytes 884744 | tf_op jit(solution)/shard_map/ppermute | solution.py:24
  8.5 5.7 %collective-permute-done.refs_1_.refs_3_ = bf16[128,1280]{1,0:T(8,128)(2,1)S(1)} collective-permute-done((bf16[128,1280]{1,0:T(8,128)(2,1)S(1)}, bf16[128,1280]{1,0:T(8,128)(2,1)S(1)}, u32[]{:S(2)}, u32[]{:S(2)}) %collective-permute-start) | collective-permute-done | bytes 327712 | tf_op jit(solution)/shard_map/ppermute | solution.py:24
  14.1 1.9 %shard_map.38 = (bf16[384,2048]{1,0:T(8,128)(2,1)S(1)}, bf16[384,2048]{1,0:T(8,128)(2,1)S(1)}) custom-call(bf16[128,4096]{1,0:T(8,128)(2,1)S(1)} %bitcast.11, bf16[128,1280]{1,0:T(8,128)(2,1)S(1)} %collective-permute-done.refs_1_.refs_3_, f32[4,8,128]{2,1,0:T(8,128)S(1)} %copy-done.1, f32[3,4,8,128]{3,2,1,0:T(8,128)S(1)} %copy-done), custom_call_target="tpu_custom_call" | custom-call | tf_op jit(solution)/shard_map/pallas_call | solution.py:58
  16.0 0.4 collective-permute-done.1.refs_1_
  16.4 4.6 %collective-permute-done.2.refs_2_ = bf16[128,1152]{1,0:T(8,128)(2,1)S(1)} collective-permute-done((bf16[128,1152]{1,0:T(8,128)(2,1)S(1)}, bf16[128,1152]{1,0:T(8,128)(2,1)S(1)}, u32[]{:S(2)}, u32[]{:S(2)}) %collective-permute-start.2) | collective-permute-done | bytes 294944 | tf_op jit(solution)/shard_map/ppermute | solution.py:24
  21.0 0.0 collective-permute-start.3
  21.0 1.9 %shard_map.39 = (bf16[384,2048]{1,0:T(8,128)(2,1)S(1)}, bf16[384,2048]{1,0:T(8,128)(2,1)S(1)}) custom-call(bf16[128,4096]{1,0:T(8,128)(2,1)S(1)} %bitcast.12, bf16[128,1152]{1,0:T(8,128)(2,1)S(1)} %collective-permute-done.1.refs_1_, bf16[128,1152]{1,0:T(8,128)(2,1)S(1)} %collective-permute-done.2.refs_2_, ...), custom_call_target="tpu_custom_call" | custom-call | tf_op jit(solution)/shard_map/pallas_call | solution.py:58
  22.9 0.6 %collective-permute-start.4 = (bf16[384,2048]{1,0:T(8,128)(2,1)S(1)}, bf16[384,2048]{1,0:T(8,128)(2,1)S(1)}, u32[]{:S(2)}, u32[]{:S(2)}) collective-permute-start(bf16[384,2048]{1,0:T(8,128)(2,1)S(1)} %get-tuple-element.41.refs_1_), channel_id=1, source_target_pairs={{0,4},{4,0},{8,12},{12,8},{16,20},{20,16},{24,28},{28,24},{1,5},{5... | collective-permute-start | bytes 4718600 | tf_op jit(solution)/shard_map/ppermute | solution.py:336
  23.5 1.0 %shard_map.40.refs_6_.refs_4_ = f32[384,128]{1,0:T(8,128)S(1)} custom-call(bf16[384,2048]{1,0:T(8,128)(2,1)S(1)} %get-tuple-element.42.refs_0_, bf16[384,2048]{1,0:T(8,128)(2,1)S(1)} %get-tuple-element.43.refs_1_, bf16[128,4096]{1,0:T(8,128)(2,1)S(1)} %bitcast.13), custom_call_target="tpu_custom_call" | custom-call | tf_op jit(solution)/shard_map/pallas_call | solution.py:58
  24.4 4.0 %collective-permute-done.5 = bf16[128,4,8,128]{3,2,1,0:T(8,128)(2,1)S(1)} collective-permute-done((bf16[128,4,8,128]{3,2,1,0:T(8,128)(2,1)}, bf16[128,4,8,128]{3,2,1,0:T(8,128)(2,1)S(1)}, u32[]{:S(2)}, u32[]{:S(2)}) %collective-permute-start.5) | collective-permute-done | bytes 1048608 | tf_op jit(solution)/shard_map/ppermute | solution.py:24
  28.4 0.5 %copy.8 = bf16[16,8,32,128]{3,1,2,0:T(8,128)(2,1)S(1)} copy(bf16[16,8,32,128]{3,2,1,0:T(8,128)(2,1)S(1)} %bitcast.19) | data formatting | bytes 2097152
  28.9 0.1 collective-permute-start.9
  29.0 0.0 collective-permute-done.3.refs_2_
  29.0 1.9 %shard_map.41 = (f32[128,384]{1,0:T(8,128)S(1)}, f32[2,3,32,128]{3,2,1,0:T(8,128)S(1)}, bf16[2,3,32,128]{3,2,1,0:T(8,128)(2,1)S(1)}, bf16[2,3,32,128]{3,2,1,0:T(8,128)(2,1)S(1)}, bf16[2,3,32,128]{3,2,1,0:T(8,128)(2,1)S(1)}) custom-call(bf16[384,2048]{1,0:T(8,128)(2,1)S(1)} %get-tuple-element.35.refs_0_, bf16[384,2048]{1,0:T(8,128)(2,1)S(1)} %get-tuple-element.41.refs_1_, ...), custom_call_target="tpu_custom_call" | custom-call | bytes 3000000 | tf_op jit(solution)/shard_map/pallas_call | solution.py:58
  30.9 2.5 %collective-permute-start.6 = (bf16[2,3,32,128]{3,2,1,0:T(8,128)(2,1)S(1)}, bf16[2,3,32,128]{3,2,1,0:T(8,128)(2,1)S(1)}, u32[]{:S(2)}, u32[]{:S(2)}) collective-permute-start(bf16[2,3,32,128]{3,2,1,0:T(8,128)(2,1)S(1)} %get-tuple-element.46), channel_id=1, source_target_pairs={{0,3},{1,2},{2,1},{3,0},{4,7},{5,6},{6,5},{7,4},{8,11},{9,10},{10,... | collective-permute-start | bytes 147464 | tf_op jit(solution)/shard_map/ppermute | solution.py:42
  33.4 0.5 %collective-permute-start.7 = (bf16[2,3,32,128]{3,2,1,0:T(8,128)(2,1)S(1)}, bf16[2,3,32,128]{3,2,1,0:T(8,128)(2,1)S(1)}, u32[]{:S(2)}, u32[]{:S(2)}) collective-permute-start(bf16[2,3,32,128]{3,2,1,0:T(8,128)(2,1)S(1)} %get-tuple-element.47), channel_id=1, source_target_pairs={{0,2},{1,3},{2,0},{3,1},{4,6},{5,7},{6,4},{7,5},{8,10},{9,11},{10,... | collective-permute-start | bytes 147464 | tf_op jit(solution)/shard_map/ppermute | solution.py:42
  33.9 0.5 %collective-permute-start.8 = (bf16[2,3,32,128]{3,2,1,0:T(8,128)(2,1)S(1)}, bf16[2,3,32,128]{3,2,1,0:T(8,128)(2,1)S(1)}, u32[]{:S(2)}, u32[]{:S(2)}) collective-permute-start(bf16[2,3,32,128]{3,2,1,0:T(8,128)(2,1)S(1)} %get-tuple-element.48), channel_id=1, source_target_pairs={{0,1},{1,0},{2,3},{3,2},{4,5},{5,4},{6,7},{7,6},{8,9},{9,8},{10,11... | collective-permute-start | bytes 147464 | tf_op jit(solution)/shard_map/ppermute | solution.py:42
  34.4 0.0 collective-permute-done.9.refs_3_
  34.4 1.0 %shard_map.42 = (f32[3,3,32,128]{3,2,1,0:T(8,128)S(1)}, bf16[3,3,32,128]{3,2,1,0:T(8,128)(2,1)S(1)}, bf16[3,3,32,128]{3,2,1,0:T(8,128)(2,1)S(1)}, bf16[3,3,32,128]{3,2,1,0:T(8,128)(2,1)S(1)}) custom-call(bf16[384,2048]{1,0:T(8,128)(2,1)S(1)} %get-tuple-element.42.refs_0_, bf16[384,2048]{1,0:T(8,128)(2,1)S(1)} %get-tuple-element.43.refs_1_, ...), custom_call_target="tpu_custom_call" | custom-call | bytes 3000000 | tf_op jit(solution)/shard_map/pallas_call | solution.py:58
  35.5 2.5 %collective-permute-start.10 = (bf16[3,3,32,128]{3,2,1,0:T(8,128)(2,1)S(1)}, bf16[3,3,32,128]{3,2,1,0:T(8,128)(2,1)S(1)}, u32[]{:S(2)}, u32[]{:S(2)}) collective-permute-start(bf16[3,3,32,128]{3,2,1,0:T(8,128)(2,1)S(1)} %get-tuple-element.54), channel_id=1, source_target_pairs={{0,3},{1,2},{2,1},{3,0},{4,7},{5,6},{6,5},{7,4},{8,11},{9,10},{10,... | collective-permute-start | bytes 221192 | tf_op jit(solution)/shard_map/ppermute | solution.py:42
  38.0 0.5 %collective-permute-start.11 = (bf16[3,3,32,128]{3,2,1,0:T(8,128)(2,1)S(1)}, bf16[3,3,32,128]{3,2,1,0:T(8,128)(2,1)S(1)}, u32[]{:S(2)}, u32[]{:S(2)}) collective-permute-start(bf16[3,3,32,128]{3,2,1,0:T(8,128)(2,1)S(1)} %get-tuple-element.55), channel_id=1, source_target_pairs={{0,2},{1,3},{2,0},{3,1},{4,6},{5,7},{6,4},{7,5},{8,10},{9,11},{10,... | collective-permute-start | bytes 221192 | tf_op jit(solution)/shard_map/ppermute | solution.py:42
  38.5 0.0 collective-permute-done.6.refs_1_
  38.5 0.5 %collective-permute-start.12 = (bf16[3,3,32,128]{3,2,1,0:T(8,128)(2,1)S(1)}, bf16[3,3,32,128]{3,2,1,0:T(8,128)(2,1)S(1)}, u32[]{:S(2)}, u32[]{:S(2)}) collective-permute-start(bf16[3,3,32,128]{3,2,1,0:T(8,128)(2,1)S(1)} %get-tuple-element.56), channel_id=1, source_target_pairs={{0,1},{1,0},{2,3},{3,2},{4,5},{5,4},{6,7},{7,6},{8,9},{9,8},{10,11... | collective-permute-start | bytes 221192 | tf_op jit(solution)/shard_map/ppermute | solution.py:42
  39.0 0.0 collective-permute-done.7.refs_2_
  39.1 1.8 %collective-permute-start.13 = (bf16[2,3,32,128]{3,2,1,0:T(8,128)(2,1)S(1)}, bf16[2,3,32,128]{3,2,1,0:T(8,128)(2,1)S(1)}, u32[]{:S(2)}, u32[]{:S(2)}) collective-permute-start(bf16[2,3,32,128]{3,2,1,0:T(8,128)(2,1)S(1)} %get-tuple-element.62), channel_id=1, source_target_pairs={{8,0},{12,4},{16,8},{20,12},{24,16},{28,20},{0,24},{4,28},{9,1},{1... | collective-permute-start | bytes 147464 | tf_op jit(solution)/shard_map/ppermute | solution.py:24
  40.9 2.3 %collective-permute-done.13.refs_5_ = bf16[2,3,32,128]{3,2,1,0:T(8,128)(2,1)S(1)} collective-permute-done((bf16[2,3,32,128]{3,2,1,0:T(8,128)(2,1)S(1)}, bf16[2,3,32,128]{3,2,1,0:T(8,128)(2,1)S(1)}, u32[]{:S(2)}, u32[]{:S(2)}) %collective-permute-start.13) | collective-permute-done | bytes 49184 | tf_op jit(solution)/shard_map/ppermute | solution.py:24
  43.2 0.7 %shard_map.44 = f32[3,5,32,128]{3,2,1,0:T(8,128)} custom-call(f32[3,3,32,128]{3,2,1,0:T(8,128)S(1)} %get-tuple-element.53.refs_0_, bf16[3,3,32,128]{3,2,1,0:T(8,128)(2,1)S(1)} %collective-permute-done.10.refs_1_, bf16[3,3,32,128]{3,2,1,0:T(8,128)(2,1)S(1)} %collective-permute-done.11.refs_2_, bf16[3,3,32,128]{3,2,1,0:T(8,128)(2,1)S(1)} %collective-permute-done.12.refs_3_, ...), custom_call_target="tpu_custom_call" | custom-call | tf_op jit(solution)/shard_map/pallas_call | solution.py:58
  (10 shorter events, 0.1 us)
Async XLA Ops:
  0.0 4.7 %copy-start.1 = (f32[4,8,128]{2,1,0:T(8,128)S(1)}, f32[4,8,128]{2,1,0:T(8,128)}, u32[]{:S(2)}) copy-start(f32[4,8,128]{2,1,0:T(8,128)} %refs_4_.1) | copy-start | bytes 49156
  0.0 4.7 %copy-start = (f32[3,4,8,128]{3,2,1,0:T(8,128)S(1)}, f32[3,4,8,128]{3,2,1,0:T(8,128)}, u32[]{:S(2)}) copy-start(f32[3,4,8,128]{3,2,1,0:T(8,128)} %refs_5_.1) | copy-start | bytes 147460
  0.0 28.4 %collective-permute-start.5 = (bf16[128,4,8,128]{3,2,1,0:T(8,128)(2,1)}, bf16[128,4,8,128]{3,2,1,0:T(8,128)(2,1)S(1)}, u32[]{:S(2)}, u32[]{:S(2)}) collective-permute-start(bf16[128,4,8,128]{3,2,1,0:T(8,128)(2,1)} %param.3), channel_id=1, source_target_pairs={{24,0},{28,4},{0,8},{4,12},{8,16},{12,20},{16,24},{20,28},{25,1},{... | collective-permute-start | bytes 3145736 | tf_op jit(solution)/shard_map/ppermute | solution.py:24
  4.9 9.2 %collective-permute-start = (bf16[128,1280]{1,0:T(8,128)(2,1)S(1)}, bf16[128,1280]{1,0:T(8,128)(2,1)S(1)}, u32[]{:S(2)}, u32[]{:S(2)}) collective-permute-start(bf16[128,1280]{1,0:T(8,128)(2,1)S(1)} %get-tuple-element.34), channel_id=1, source_target_pairs={{1,0},{0,1},{3,2},{2,3},{5,4},{4,5},{7,6},{6,7},{9,8},{8,9},{11,10... | collective-permute-start | bytes 983048 | tf_op jit(solution)/shard_map/ppermute | solution.py:24
  6.4 9.9 %collective-permute-start.1 = (bf16[128,1152]{1,0:T(8,128)(2,1)S(1)}, bf16[128,1152]{1,0:T(8,128)(2,1)S(1)}, u32[]{:S(2)}, u32[]{:S(2)}) collective-permute-start(bf16[128,1152]{1,0:T(8,128)(2,1)S(1)} %get-tuple-element.36), channel_id=1, source_target_pairs={{2,0},{0,2},{3,1},{1,3},{6,4},{4,6},{7,5},{5,7},{10,8},{8,10},{11,... | collective-permute-start | bytes 884744 | tf_op jit(solution)/shard_map/ppermute | solution.py:24
  8.0 13.0 %collective-permute-start.2 = (bf16[128,1152]{1,0:T(8,128)(2,1)S(1)}, bf16[128,1152]{1,0:T(8,128)(2,1)S(1)}, u32[]{:S(2)}, u32[]{:S(2)}) collective-permute-start(bf16[128,1152]{1,0:T(8,128)(2,1)S(1)} %get-tuple-element.37), channel_id=1, source_target_pairs={{2,0},{0,2},{3,1},{1,3},{6,4},{4,6},{7,5},{5,7},{10,8},{8,10},{11,... | collective-permute-start | bytes 884744 | tf_op jit(solution)/shard_map/ppermute | solution.py:24
  21.0 8.0 %collective-permute-start.3 = (bf16[384,2048]{1,0:T(8,128)(2,1)S(1)}, bf16[384,2048]{1,0:T(8,128)(2,1)S(1)}, u32[]{:S(2)}, u32[]{:S(2)}) collective-permute-start(bf16[384,2048]{1,0:T(8,128)(2,1)S(1)} %get-tuple-element.35.refs_0_), channel_id=1, source_target_pairs={{0,4},{4,0},{8,12},{12,8},{16,20},{20,16},{24,28},{28,24},{1,5},{5... | collective-permute-start | bytes 4718600 | tf_op jit(solution)/shard_map/ppermute | solution.py:336
  22.9 6.1 %collective-permute-start.4 = (bf16[384,2048]{1,0:T(8,128)(2,1)S(1)}, bf16[384,2048]{1,0:T(8,128)(2,1)S(1)}, u32[]{:S(2)}, u32[]{:S(2)}) collective-permute-start(bf16[384,2048]{1,0:T(8,128)(2,1)S(1)} %get-tuple-element.41.refs_1_), channel_id=1, source_target_pairs={{0,4},{4,0},{8,12},{12,8},{16,20},{20,16},{24,28},{28,24},{1,5},{5... | collective-permute-start | bytes 4718600 | tf_op jit(solution)/shard_map/ppermute | solution.py:336
  28.9 5.6 %collective-permute-start.9 = (bf16[128,4096]{1,0:T(8,128)(2,1)S(1)}, bf16[128,4096]{1,0:T(8,128)(2,1)S(1)}, u32[]{:S(2)}, u32[]{:S(2)}) collective-permute-start(bf16[128,4096]{1,0:T(8,128)(2,1)S(1)} %bitcast.15), channel_id=1, source_target_pairs={{0,4},{4,0},{8,12},{12,8},{16,20},{20,16},{24,28},{28,24},{1,5},{5... | collective-permute-start | bytes 3145736 | tf_op jit(solution)/shard_map/ppermute | solution.py:349
  30.9 7.6 %collective-permute-start.6 = (bf16[2,3,32,128]{3,2,1,0:T(8,128)(2,1)S(1)}, bf16[2,3,32,128]{3,2,1,0:T(8,128)(2,1)S(1)}, u32[]{:S(2)}, u32[]{:S(2)}) collective-permute-start(bf16[2,3,32,128]{3,2,1,0:T(8,128)(2,1)S(1)} %get-tuple-element.46), channel_id=1, source_target_pairs={{0,3},{1,2},{2,1},{3,0},{4,7},{5,6},{6,5},{7,4},{8,11},{9,10},{10,... | collective-permute-start | bytes 147464 | tf_op jit(solution)/shard_map/ppermute | solution.py:42
  33.4 5.6 %collective-permute-start.7 = (bf16[2,3,32,128]{3,2,1,0:T(8,128)(2,1)S(1)}, bf16[2,3,32,128]{3,2,1,0:T(8,128)(2,1)S(1)}, u32[]{:S(2)}, u32[]{:S(2)}) collective-permute-start(bf16[2,3,32,128]{3,2,1,0:T(8,128)(2,1)S(1)} %get-tuple-element.47), channel_id=1, source_target_pairs={{0,2},{1,3},{2,0},{3,1},{4,6},{5,7},{6,4},{7,5},{8,10},{9,11},{10,... | collective-permute-start | bytes 147464 | tf_op jit(solution)/shard_map/ppermute | solution.py:42
  33.9 5.1 %collective-permute-start.8 = (bf16[2,3,32,128]{3,2,1,0:T(8,128)(2,1)S(1)}, bf16[2,3,32,128]{3,2,1,0:T(8,128)(2,1)S(1)}, u32[]{:S(2)}, u32[]{:S(2)}) collective-permute-start(bf16[2,3,32,128]{3,2,1,0:T(8,128)(2,1)S(1)} %get-tuple-element.48), channel_id=1, source_target_pairs={{0,1},{1,0},{2,3},{3,2},{4,5},{5,4},{6,7},{7,6},{8,9},{9,8},{10,11... | collective-permute-start | bytes 147464 | tf_op jit(solution)/shard_map/ppermute | solution.py:42
  35.5 7.7 %collective-permute-start.10 = (bf16[3,3,32,128]{3,2,1,0:T(8,128)(2,1)S(1)}, bf16[3,3,32,128]{3,2,1,0:T(8,128)(2,1)S(1)}, u32[]{:S(2)}, u32[]{:S(2)}) collective-permute-start(bf16[3,3,32,128]{3,2,1,0:T(8,128)(2,1)S(1)} %get-tuple-element.54), channel_id=1, source_target_pairs={{0,3},{1,2},{2,1},{3,0},{4,7},{5,6},{6,5},{7,4},{8,11},{9,10},{10,... | collective-permute-start | bytes 221192 | tf_op jit(solution)/shard_map/ppermute | solution.py:42
  38.0 5.2 %collective-permute-start.11 = (bf16[3,3,32,128]{3,2,1,0:T(8,128)(2,1)S(1)}, bf16[3,3,32,128]{3,2,1,0:T(8,128)(2,1)S(1)}, u32[]{:S(2)}, u32[]{:S(2)}) collective-permute-start(bf16[3,3,32,128]{3,2,1,0:T(8,128)(2,1)S(1)} %get-tuple-element.55), channel_id=1, source_target_pairs={{0,2},{1,3},{2,0},{3,1},{4,6},{5,7},{6,4},{7,5},{8,10},{9,11},{10,... | collective-permute-start | bytes 221192 | tf_op jit(solution)/shard_map/ppermute | solution.py:42
  38.5 4.7 %collective-permute-start.12 = (bf16[3,3,32,128]{3,2,1,0:T(8,128)(2,1)S(1)}, bf16[3,3,32,128]{3,2,1,0:T(8,128)(2,1)S(1)}, u32[]{:S(2)}, u32[]{:S(2)}) collective-permute-start(bf16[3,3,32,128]{3,2,1,0:T(8,128)(2,1)S(1)} %get-tuple-element.56), channel_id=1, source_target_pairs={{0,1},{1,0},{2,3},{3,2},{4,5},{5,4},{6,7},{7,6},{8,9},{9,8},{10,11... | collective-permute-start | bytes 221192 | tf_op jit(solution)/shard_map/ppermute | solution.py:42
  39.1 4.1 %collective-permute-start.13 = (bf16[2,3,32,128]{3,2,1,0:T(8,128)(2,1)S(1)}, bf16[2,3,32,128]{3,2,1,0:T(8,128)(2,1)S(1)}, u32[]{:S(2)}, u32[]{:S(2)}) collective-permute-start(bf16[2,3,32,128]{3,2,1,0:T(8,128)(2,1)S(1)} %get-tuple-element.62), channel_id=1, source_target_pairs={{8,0},{12,4},{16,8},{20,12},{24,16},{28,20},{0,24},{4,28},{9,1},{1... | collective-permute-start | bytes 147464 | tf_op jit(solution)/shard_map/ppermute | solution.py:24

commit v24 on v23

--- a/solution.py
+++ b/solution.py
@@ -34,7 +34,8 @@
 def exchange(sends):
     nx, ny = lax.axis_size("dx"), lax.axis_size("dy")
     got = []
-    for o, piece in reversed(list(enumerate(sends, 1))):
+    pieces = list(enumerate(sends, 1))
+    for o, piece in pieces[-1:] + pieces[:-1]:
         ox, oy = o // ny, o % ny
         route = [
             (i * ny + j, ((i + ox) % nx) * ny + (j + oy) % ny) for i in range(nx) for j in range(ny)

time: 44.1 us -> 44.1 us (level)
  no operation moved by 1% of the time
where the time goes in v24:
time: 44.1 us; the launch traced here: 44 us
  waiting for transfers between devices  16.9 us (38%)
  starting transfers between devices  16.2 us (37%)
  Pallas kernels  8.64 us (20%)
  local copies, waits for them, and re-layouts  2.16 us (5%)
    ppermute x5, waiting for transfers between devices, shift(): lax.ppermute(block, axis, [((i + distance) % count, i) for i in range(cou...  16.9 us
    pallas_call x8, Pallas kernels, call(): return list(run(*operands))  8.64 us
    ppermute x5, starting transfers between devices, shift(): lax.ppermute(block, axis, [((i + distance) % count, i) for i in range(cou...  8.4 us
    ppermute x6, starting transfers between devices, exchange(): got.append(lax.ppermute(piece, ('dx', 'dy'), route))  7.11 us
    unnamed x6, local copies, waits for them, and re-layouts  2.16 us
  transfers between devices with their start and end apart: 14, of which 5 were waited for; matrix products, arithmetic and copies ran while one was open for 5% of the time, Pallas kernels for 18%

profile of v24, /device:TPU:0, one launch (start us, length us, event | category | flops | bytes accessed | tf_op | source)
XLA Modules:
  0.0 44.0 jit_solution(17769246790752590021)
XLA Ops:
  0.0 3.0 %collective-permute-start.5 = (bf16[128,4,8,128]{3,2,1,0:T(8,128)(2,1)}, bf16[128,4,8,128]{3,2,1,0:T(8,128)(2,1)S(1)}, u32[]{:S(2)}, u32[]{:S(2)}) collective-permute-start(bf16[128,4,8,128]{3,2,1,0:T(8,128)(2,1)} %param.3), channel_id=1, source_target_pairs={{24,0},{28,4},{0,8},{4,12},{8,16},{12,20},{16,24},{20,28},{25,1},{... | collective-permute-start | bytes 3145736 | tf_op jit(solution)/shard_map/ppermute | solution.py:24
  3.0 1.7 %copy.9 = bf16[16,8,32,128]{3,1,2,0:T(8,128)(2,1)S(1)} copy(bf16[16,8,32,128]{3,2,1,0:T(8,128)(2,1)} %bitcast.18) | data formatting | bytes 2097152
  4.8 0.1 shard_map.37
  4.9 1.6 %collective-permute-start = (bf16[128,1280]{1,0:T(8,128)(2,1)S(1)}, bf16[128,1280]{1,0:T(8,128)(2,1)S(1)}, u32[]{:S(2)}, u32[]{:S(2)}) collective-permute-start(bf16[128,1280]{1,0:T(8,128)(2,1)S(1)} %get-tuple-element.34), channel_id=1, source_target_pairs={{1,0},{0,1},{3,2},{2,3},{5,4},{4,5},{7,6},{6,7},{9,8},{8,9},{11,10... | collective-permute-start | bytes 983048 | tf_op jit(solution)/shard_map/ppermute | solution.py:24
  6.4 1.5 %collective-permute-start.1 = (bf16[128,1152]{1,0:T(8,128)(2,1)S(1)}, bf16[128,1152]{1,0:T(8,128)(2,1)S(1)}, u32[]{:S(2)}, u32[]{:S(2)}) collective-permute-start(bf16[128,1152]{1,0:T(8,128)(2,1)S(1)} %get-tuple-element.36), channel_id=1, source_target_pairs={{2,0},{0,2},{3,1},{1,3},{6,4},{4,6},{7,5},{5,7},{10,8},{8,10},{11,... | collective-permute-start | bytes 884744 | tf_op jit(solution)/shard_map/ppermute | solution.py:24
  8.0 0.5 %collective-permute-start.2 = (bf16[128,1152]{1,0:T(8,128)(2,1)S(1)}, bf16[128,1152]{1,0:T(8,128)(2,1)S(1)}, u32[]{:S(2)}, u32[]{:S(2)}) collective-permute-start(bf16[128,1152]{1,0:T(8,128)(2,1)S(1)} %get-tuple-element.37), channel_id=1, source_target_pairs={{2,0},{0,2},{3,1},{1,3},{6,4},{4,6},{7,5},{5,7},{10,8},{8,10},{11,... | collective-permute-start | bytes 884744 | tf_op jit(solution)/shard_map/ppermute | solution.py:24
  8.5 5.7 %collective-permute-done.refs_1_.refs_3_ = bf16[128,1280]{1,0:T(8,128)(2,1)S(1)} collective-permute-done((bf16[128,1280]{1,0:T(8,128)(2,1)S(1)}, bf16[128,1280]{1,0:T(8,128)(2,1)S(1)}, u32[]{:S(2)}, u32[]{:S(2)}) %collective-permute-start) | collective-permute-done | bytes 327712 | tf_op jit(solution)/shard_map/ppermute | solution.py:24
  14.1 1.9 %shard_map.38 = (bf16[384,2048]{1,0:T(8,128)(2,1)S(1)}, bf16[384,2048]{1,0:T(8,128)(2,1)S(1)}) custom-call(bf16[128,4096]{1,0:T(8,128)(2,1)S(1)} %bitcast.11, bf16[128,1280]{1,0:T(8,128)(2,1)S(1)} %collective-permute-done.refs_1_.refs_3_, f32[4,8,128]{2,1,0:T(8,128)S(1)} %copy-done.1, f32[3,4,8,128]{3,2,1,0:T(8,128)S(1)} %copy-done), custom_call_target="tpu_custom_call" | custom-call | tf_op jit(solution)/shard_map/pallas_call | solution.py:59
  16.0 0.4 collective-permute-done.1.refs_1_
  16.4 4.6 %collective-permute-done.2.refs_2_ = bf16[128,1152]{1,0:T(8,128)(2,1)S(1)} collective-permute-done((bf16[128,1152]{1,0:T(8,128)(2,1)S(1)}, bf16[128,1152]{1,0:T(8,128)(2,1)S(1)}, u32[]{:S(2)}, u32[]{:S(2)}) %collective-permute-start.2) | collective-permute-done | bytes 294944 | tf_op jit(solution)/shard_map/ppermute | solution.py:24
  21.0 0.0 collective-permute-start.3
  21.0 1.9 %shard_map.39 = (bf16[384,2048]{1,0:T(8,128)(2,1)S(1)}, bf16[384,2048]{1,0:T(8,128)(2,1)S(1)}) custom-call(bf16[128,4096]{1,0:T(8,128)(2,1)S(1)} %bitcast.12, bf16[128,1152]{1,0:T(8,128)(2,1)S(1)} %collective-permute-done.1.refs_1_, bf16[128,1152]{1,0:T(8,128)(2,1)S(1)} %collective-permute-done.2.refs_2_, ...), custom_call_target="tpu_custom_call" | custom-call | tf_op jit(solution)/shard_map/pallas_call | solution.py:59
  22.9 0.6 %collective-permute-start.4 = (bf16[384,2048]{1,0:T(8,128)(2,1)S(1)}, bf16[384,2048]{1,0:T(8,128)(2,1)S(1)}, u32[]{:S(2)}, u32[]{:S(2)}) collective-permute-start(bf16[384,2048]{1,0:T(8,128)(2,1)S(1)} %get-tuple-element.41.refs_1_), channel_id=1, source_target_pairs={{0,4},{4,0},{8,12},{12,8},{16,20},{20,16},{24,28},{28,24},{1,5},{5... | collective-permute-start | bytes 4718600 | tf_op jit(solution)/shard_map/ppermute | solution.py:337
  23.5 1.0 %shard_map.40.refs_6_.refs_4_ = f32[384,128]{1,0:T(8,128)S(1)} custom-call(bf16[384,2048]{1,0:T(8,128)(2,1)S(1)} %get-tuple-element.42.refs_0_, bf16[384,2048]{1,0:T(8,128)(2,1)S(1)} %get-tuple-element.43.refs_1_, bf16[128,4096]{1,0:T(8,128)(2,1)S(1)} %bitcast.13), custom_call_target="tpu_custom_call" | custom-call | tf_op jit(solution)/shard_map/pallas_call | solution.py:59
  24.4 4.0 %collective-permute-done.5 = bf16[128,4,8,128]{3,2,1,0:T(8,128)(2,1)S(1)} collective-permute-done((bf16[128,4,8,128]{3,2,1,0:T(8,128)(2,1)}, bf16[128,4,8,128]{3,2,1,0:T(8,128)(2,1)S(1)}, u32[]{:S(2)}, u32[]{:S(2)}) %collective-permute-start.5) | collective-permute-done | bytes 1048608 | tf_op jit(solution)/shard_map/ppermute | solution.py:24
  28.4 0.5 %copy.8 = bf16[16,8,32,128]{3,1,2,0:T(8,128)(2,1)S(1)} copy(bf16[16,8,32,128]{3,2,1,0:T(8,128)(2,1)S(1)} %bitcast.19) | data formatting | bytes 2097152
  28.9 0.1 collective-permute-start.9
  29.0 0.0 collective-permute-done.3.refs_2_
  29.0 1.9 %shard_map.41 = (f32[128,384]{1,0:T(8,128)S(1)}, f32[2,3,32,128]{3,2,1,0:T(8,128)S(1)}, bf16[2,3,32,128]{3,2,1,0:T(8,128)(2,1)S(1)}, bf16[2,3,32,128]{3,2,1,0:T(8,128)(2,1)S(1)}, bf16[2,3,32,128]{3,2,1,0:T(8,128)(2,1)S(1)}) custom-call(bf16[384,2048]{1,0:T(8,128)(2,1)S(1)} %get-tuple-element.35.refs_0_, bf16[384,2048]{1,0:T(8,128)(2,1)S(1)} %get-tuple-element.41.refs_1_, ...), custom_call_target="tpu_custom_call" | custom-call | bytes 3000000 | tf_op jit(solution)/shard_map/pallas_call | solution.py:59
  30.9 2.5 %collective-permute-start.6 = (bf16[2,3,32,128]{3,2,1,0:T(8,128)(2,1)S(1)}, bf16[2,3,32,128]{3,2,1,0:T(8,128)(2,1)S(1)}, u32[]{:S(2)}, u32[]{:S(2)}) collective-permute-start(bf16[2,3,32,128]{3,2,1,0:T(8,128)(2,1)S(1)} %get-tuple-element.46), channel_id=1, source_target_pairs={{0,3},{1,2},{2,1},{3,0},{4,7},{5,6},{6,5},{7,4},{8,11},{9,10},{10,... | collective-permute-start | bytes 147464 | tf_op jit(solution)/shard_map/ppermute | solution.py:43
  33.4 0.5 %collective-permute-start.7 = (bf16[2,3,32,128]{3,2,1,0:T(8,128)(2,1)S(1)}, bf16[2,3,32,128]{3,2,1,0:T(8,128)(2,1)S(1)}, u32[]{:S(2)}, u32[]{:S(2)}) collective-permute-start(bf16[2,3,32,128]{3,2,1,0:T(8,128)(2,1)S(1)} %get-tuple-element.47), channel_id=1, source_target_pairs={{0,1},{1,0},{2,3},{3,2},{4,5},{5,4},{6,7},{7,6},{8,9},{9,8},{10,11... | collective-permute-start | bytes 147464 | tf_op jit(solution)/shard_map/ppermute | solution.py:43
  33.9 0.5 %collective-permute-start.8 = (bf16[2,3,32,128]{3,2,1,0:T(8,128)(2,1)S(1)}, bf16[2,3,32,128]{3,2,1,0:T(8,128)(2,1)S(1)}, u32[]{:S(2)}, u32[]{:S(2)}) collective-permute-start(bf16[2,3,32,128]{3,2,1,0:T(8,128)(2,1)S(1)} %get-tuple-element.48), channel_id=1, source_target_pairs={{0,2},{1,3},{2,0},{3,1},{4,6},{5,7},{6,4},{7,5},{8,10},{9,11},{10,... | collective-permute-start | bytes 147464 | tf_op jit(solution)/shard_map/ppermute | solution.py:43
  34.4 0.0 collective-permute-done.9.refs_3_
  34.4 1.0 %shard_map.42 = (f32[3,3,32,128]{3,2,1,0:T(8,128)S(1)}, bf16[3,3,32,128]{3,2,1,0:T(8,128)(2,1)S(1)}, bf16[3,3,32,128]{3,2,1,0:T(8,128)(2,1)S(1)}, bf16[3,3,32,128]{3,2,1,0:T(8,128)(2,1)S(1)}) custom-call(bf16[384,2048]{1,0:T(8,128)(2,1)S(1)} %get-tuple-element.42.refs_0_, bf16[384,2048]{1,0:T(8,128)(2,1)S(1)} %get-tuple-element.43.refs_1_, ...), custom_call_target="tpu_custom_call" | custom-call | bytes 3000000 | tf_op jit(solution)/shard_map/pallas_call | solution.py:59
  35.5 2.5 %collective-permute-start.10 = (bf16[3,3,32,128]{3,2,1,0:T(8,128)(2,1)S(1)}, bf16[3,3,32,128]{3,2,1,0:T(8,128)(2,1)S(1)}, u32[]{:S(2)}, u32[]{:S(2)}) collective-permute-start(bf16[3,3,32,128]{3,2,1,0:T(8,128)(2,1)S(1)} %get-tuple-element.54), channel_id=1, source_target_pairs={{0,3},{1,2},{2,1},{3,0},{4,7},{5,6},{6,5},{7,4},{8,11},{9,10},{10,... | collective-permute-start | bytes 221192 | tf_op jit(solution)/shard_map/ppermute | solution.py:43
  38.0 0.5 %collective-permute-start.11 = (bf16[3,3,32,128]{3,2,1,0:T(8,128)(2,1)S(1)}, bf16[3,3,32,128]{3,2,1,0:T(8,128)(2,1)S(1)}, u32[]{:S(2)}, u32[]{:S(2)}) collective-permute-start(bf16[3,3,32,128]{3,2,1,0:T(8,128)(2,1)S(1)} %get-tuple-element.55), channel_id=1, source_target_pairs={{0,1},{1,0},{2,3},{3,2},{4,5},{5,4},{6,7},{7,6},{8,9},{9,8},{10,11... | collective-permute-start | bytes 221192 | tf_op jit(solution)/shard_map/ppermute | solution.py:43
  38.5 0.5 %collective-permute-start.12 = (bf16[3,3,32,128]{3,2,1,0:T(8,128)(2,1)S(1)}, bf16[3,3,32,128]{3,2,1,0:T(8,128)(2,1)S(1)}, u32[]{:S(2)}, u32[]{:S(2)}) collective-permute-start(bf16[3,3,32,128]{3,2,1,0:T(8,128)(2,1)S(1)} %get-tuple-element.56), channel_id=1, source_target_pairs={{0,2},{1,3},{2,0},{3,1},{4,6},{5,7},{6,4},{7,5},{8,10},{9,11},{10,... | collective-permute-start | bytes 221192 | tf_op jit(solution)/shard_map/ppermute | solution.py:43
  39.0 0.0 collective-permute-done.7.refs_2_
  39.0 0.0 collective-permute-done.8.refs_3_
  39.1 1.8 %collective-permute-start.13 = (bf16[2,3,32,128]{3,2,1,0:T(8,128)(2,1)S(1)}, bf16[2,3,32,128]{3,2,1,0:T(8,128)(2,1)S(1)}, u32[]{:S(2)}, u32[]{:S(2)}) collective-permute-start(bf16[2,3,32,128]{3,2,1,0:T(8,128)(2,1)S(1)} %get-tuple-element.62), channel_id=1, source_target_pairs={{8,0},{12,4},{16,8},{20,12},{24,16},{28,20},{0,24},{4,28},{9,1},{1... | collective-permute-start | bytes 147464 | tf_op jit(solution)/shard_map/ppermute | solution.py:24
  40.9 2.3 %collective-permute-done.13.refs_5_ = bf16[2,3,32,128]{3,2,1,0:T(8,128)(2,1)S(1)} collective-permute-done((bf16[2,3,32,128]{3,2,1,0:T(8,128)(2,1)S(1)}, bf16[2,3,32,128]{3,2,1,0:T(8,128)(2,1)S(1)}, u32[]{:S(2)}, u32[]{:S(2)}) %collective-permute-start.13) | collective-permute-done | bytes 49184 | tf_op jit(solution)/shard_map/ppermute | solution.py:24
  43.2 0.7 %shard_map.44 = f32[3,5,32,128]{3,2,1,0:T(8,128)} custom-call(f32[3,3,32,128]{3,2,1,0:T(8,128)S(1)} %get-tuple-element.53.refs_0_, bf16[3,3,32,128]{3,2,1,0:T(8,128)(2,1)S(1)} %collective-permute-done.10.refs_1_, bf16[3,3,32,128]{3,2,1,0:T(8,128)(2,1)S(1)} %collective-permute-done.11.refs_2_, bf16[3,3,32,128]{3,2,1,0:T(8,128)(2,1)S(1)} %collective-permute-done.12.refs_3_, ...), custom_call_target="tpu_custom_call" | custom-call | tf_op jit(solution)/shard_map/pallas_call | solution.py:59
  (10 shorter events, 0.1 us)
Async XLA Ops:
  0.0 4.7 %copy-start.1 = (f32[4,8,128]{2,1,0:T(8,128)S(1)}, f32[4,8,128]{2,1,0:T(8,128)}, u32[]{:S(2)}) copy-start(f32[4,8,128]{2,1,0:T(8,128)} %refs_4_.1) | copy-start | bytes 49156
  0.0 4.7 %copy-start = (f32[3,4,8,128]{3,2,1,0:T(8,128)S(1)}, f32[3,4,8,128]{3,2,1,0:T(8,128)}, u32[]{:S(2)}) copy-start(f32[3,4,8,128]{3,2,1,0:T(8,128)} %refs_5_.1) | copy-start | bytes 147460
  0.0 28.4 %collective-permute-start.5 = (bf16[128,4,8,128]{3,2,1,0:T(8,128)(2,1)}, bf16[128,4,8,128]{3,2,1,0:T(8,128)(2,1)S(1)}, u32[]{:S(2)}, u32[]{:S(2)}) collective-permute-start(bf16[128,4,8,128]{3,2,1,0:T(8,128)(2,1)} %param.3), channel_id=1, source_target_pairs={{24,0},{28,4},{0,8},{4,12},{8,16},{12,20},{16,24},{20,28},{25,1},{... | collective-permute-start | bytes 3145736 | tf_op jit(solution)/shard_map/ppermute | solution.py:24
  4.9 9.2 %collective-permute-start = (bf16[128,1280]{1,0:T(8,128)(2,1)S(1)}, bf16[128,1280]{1,0:T(8,128)(2,1)S(1)}, u32[]{:S(2)}, u32[]{:S(2)}) collective-permute-start(bf16[128,1280]{1,0:T(8,128)(2,1)S(1)} %get-tuple-element.34), channel_id=1, source_target_pairs={{1,0},{0,1},{3,2},{2,3},{5,4},{4,5},{7,6},{6,7},{9,8},{8,9},{11,10... | collective-permute-start | bytes 983048 | tf_op jit(solution)/shard_map/ppermute | solution.py:24
  6.4 9.9 %collective-permute-start.1 = (bf16[128,1152]{1,0:T(8,128)(2,1)S(1)}, bf16[128,1152]{1,0:T(8,128)(2,1)S(1)}, u32[]{:S(2)}, u32[]{:S(2)}) collective-permute-start(bf16[128,1152]{1,0:T(8,128)(2,1)S(1)} %get-tuple-element.36), channel_id=1, source_target_pairs={{2,0},{0,2},{3,1},{1,3},{6,4},{4,6},{7,5},{5,7},{10,8},{8,10},{11,... | collective-permute-start | bytes 884744 | tf_op jit(solution)/shard_map/ppermute | solution.py:24
  8.0 13.0 %collective-permute-start.2 = (bf16[128,1152]{1,0:T(8,128)(2,1)S(1)}, bf16[128,1152]{1,0:T(8,128)(2,1)S(1)}, u32[]{:S(2)}, u32[]{:S(2)}) collective-permute-start(bf16[128,1152]{1,0:T(8,128)(2,1)S(1)} %get-tuple-element.37), channel_id=1, source_target_pairs={{2,0},{0,2},{3,1},{1,3},{6,4},{4,6},{7,5},{5,7},{10,8},{8,10},{11,... | collective-permute-start | bytes 884744 | tf_op jit(solution)/shard_map/ppermute | solution.py:24
  21.0 8.0 %collective-permute-start.3 = (bf16[384,2048]{1,0:T(8,128)(2,1)S(1)}, bf16[384,2048]{1,0:T(8,128)(2,1)S(1)}, u32[]{:S(2)}, u32[]{:S(2)}) collective-permute-start(bf16[384,2048]{1,0:T(8,128)(2,1)S(1)} %get-tuple-element.35.refs_0_), channel_id=1, source_target_pairs={{0,4},{4,0},{8,12},{12,8},{16,20},{20,16},{24,28},{28,24},{1,5},{5... | collective-permute-start | bytes 4718600 | tf_op jit(solution)/shard_map/ppermute | solution.py:337
  22.9 6.1 %collective-permute-start.4 = (bf16[384,2048]{1,0:T(8,128)(2,1)S(1)}, bf16[384,2048]{1,0:T(8,128)(2,1)S(1)}, u32[]{:S(2)}, u32[]{:S(2)}) collective-permute-start(bf16[384,2048]{1,0:T(8,128)(2,1)S(1)} %get-tuple-element.41.refs_1_), channel_id=1, source_target_pairs={{0,4},{4,0},{8,12},{12,8},{16,20},{20,16},{24,28},{28,24},{1,5},{5... | collective-permute-start | bytes 4718600 | tf_op jit(solution)/shard_map/ppermute | solution.py:337
  28.9 5.6 %collective-permute-start.9 = (bf16[128,4096]{1,0:T(8,128)(2,1)S(1)}, bf16[128,4096]{1,0:T(8,128)(2,1)S(1)}, u32[]{:S(2)}, u32[]{:S(2)}) collective-permute-start(bf16[128,4096]{1,0:T(8,128)(2,1)S(1)} %bitcast.15), channel_id=1, source_target_pairs={{0,4},{4,0},{8,12},{12,8},{16,20},{20,16},{24,28},{28,24},{1,5},{5... | collective-permute-start | bytes 3145736 | tf_op jit(solution)/shard_map/ppermute | solution.py:350
  30.9 7.6 %collective-permute-start.6 = (bf16[2,3,32,128]{3,2,1,0:T(8,128)(2,1)S(1)}, bf16[2,3,32,128]{3,2,1,0:T(8,128)(2,1)S(1)}, u32[]{:S(2)}, u32[]{:S(2)}) collective-permute-start(bf16[2,3,32,128]{3,2,1,0:T(8,128)(2,1)S(1)} %get-tuple-element.46), channel_id=1, source_target_pairs={{0,3},{1,2},{2,1},{3,0},{4,7},{5,6},{6,5},{7,4},{8,11},{9,10},{10,... | collective-permute-start | bytes 147464 | tf_op jit(solution)/shard_map/ppermute | solution.py:43
  33.4 5.6 %collective-permute-start.7 = (bf16[2,3,32,128]{3,2,1,0:T(8,128)(2,1)S(1)}, bf16[2,3,32,128]{3,2,1,0:T(8,128)(2,1)S(1)}, u32[]{:S(2)}, u32[]{:S(2)}) collective-permute-start(bf16[2,3,32,128]{3,2,1,0:T(8,128)(2,1)S(1)} %get-tuple-element.47), channel_id=1, source_target_pairs={{0,1},{1,0},{2,3},{3,2},{4,5},{5,4},{6,7},{7,6},{8,9},{9,8},{10,11... | collective-permute-start | bytes 147464 | tf_op jit(solution)/shard_map/ppermute | solution.py:43
  33.9 5.1 %collective-permute-start.8 = (bf16[2,3,32,128]{3,2,1,0:T(8,128)(2,1)S(1)}, bf16[2,3,32,128]{3,2,1,0:T(8,128)(2,1)S(1)}, u32[]{:S(2)}, u32[]{:S(2)}) collective-permute-start(bf16[2,3,32,128]{3,2,1,0:T(8,128)(2,1)S(1)} %get-tuple-element.48), channel_id=1, source_target_pairs={{0,2},{1,3},{2,0},{3,1},{4,6},{5,7},{6,4},{7,5},{8,10},{9,11},{10,... | collective-permute-start | bytes 147464 | tf_op jit(solution)/shard_map/ppermute | solution.py:43
  35.5 7.7 %collective-permute-start.10 = (bf16[3,3,32,128]{3,2,1,0:T(8,128)(2,1)S(1)}, bf16[3,3,32,128]{3,2,1,0:T(8,128)(2,1)S(1)}, u32[]{:S(2)}, u32[]{:S(2)}) collective-permute-start(bf16[3,3,32,128]{3,2,1,0:T(8,128)(2,1)S(1)} %get-tuple-element.54), channel_id=1, source_target_pairs={{0,3},{1,2},{2,1},{3,0},{4,7},{5,6},{6,5},{7,4},{8,11},{9,10},{10,... | collective-permute-start | bytes 221192 | tf_op jit(solution)/shard_map/ppermute | solution.py:43
  38.0 5.2 %collective-permute-start.11 = (bf16[3,3,32,128]{3,2,1,0:T(8,128)(2,1)S(1)}, bf16[3,3,32,128]{3,2,1,0:T(8,128)(2,1)S(1)}, u32[]{:S(2)}, u32[]{:S(2)}) collective-permute-start(bf16[3,3,32,128]{3,2,1,0:T(8,128)(2,1)S(1)} %get-tuple-element.55), channel_id=1, source_target_pairs={{0,1},{1,0},{2,3},{3,2},{4,5},{5,4},{6,7},{7,6},{8,9},{9,8},{10,11... | collective-permute-start | bytes 221192 | tf_op jit(solution)/shard_map/ppermute | solution.py:43
  38.5 4.7 %collective-permute-start.12 = (bf16[3,3,32,128]{3,2,1,0:T(8,128)(2,1)S(1)}, bf16[3,3,32,128]{3,2,1,0:T(8,128)(2,1)S(1)}, u32[]{:S(2)}, u32[]{:S(2)}) collective-permute-start(bf16[3,3,32,128]{3,2,1,0:T(8,128)(2,1)S(1)} %get-tuple-element.56), channel_id=1, source_target_pairs={{0,2},{1,3},{2,0},{3,1},{4,6},{5,7},{6,4},{7,5},{8,10},{9,11},{10,... | collective-permute-start | bytes 221192 | tf_op jit(solution)/shard_map/ppermute | solution.py:43
  39.1 4.1 %collective-permute-start.13 = (bf16[2,3,32,128]{3,2,1,0:T(8,128)(2,1)S(1)}, bf16[2,3,32,128]{3,2,1,0:T(8,128)(2,1)S(1)}, u32[]{:S(2)}, u32[]{:S(2)}) collective-permute-start(bf16[2,3,32,128]{3,2,1,0:T(8,128)(2,1)S(1)} %get-tuple-element.62), channel_id=1, source_target_pairs={{8,0},{12,4},{16,8},{20,12},{24,16},{28,20},{0,24},{4,28},{9,1},{1... | collective-permute-start | bytes 147464 | tf_op jit(solution)/shard_map/ppermute | solution.py:24

commit v25 on v23

--- a/solution.py
+++ b/solution.py
@@ -169,18 +169,14 @@
     lax.fori_loop(0, states // CHUNK, group, 0)
 
 
-def product(fields, panel, layer, flip=False):
+def product(fields, panel, layer):
     inner, outer = fields
     cells = inner.shape[1] + outer.shape[1]
     total = 0.0
-    for a, start, stop in (
-        (inner[...], layer, cells - layer),
-        (outer[:, :layer], 0, layer),
-        (outer[:, layer:], cells - layer, cells),
-    ):
-        b = panel(slice(start, stop))
-        a, b = (b, a) if flip else (a, b)
-        total = total + lax.dot_general(a, b, NT, preferred_element_type=F32)
+    ends = [(outer, 0, 0), (outer, layer, cells - layer)]
+    for a, at, start in [(inner, n, n + layer) for n in range(0, inner.shape[1], layer)] + ends:
+        b = panel(slice(start, start + layer))
+        total = total + lax.dot_general(a[:, at : at + layer], b, NT, preferred_element_type=F32)
     return total
 
 

time: 44.1 us -> 44.1 us (level)
  no operation moved by 1% of the time
where the time goes in v25:
time: 44.1 us; the launch traced here: 44 us
  waiting for transfers between devices  16.9 us (38%)
  starting transfers between devices  16.2 us (37%)
  Pallas kernels  8.64 us (20%)
  local copies, waits for them, and re-layouts  2.16 us (5%)
    ppermute x5, waiting for transfers between devices, shift(): lax.ppermute(block, axis, [((i + distance) % count, i) for i in range(cou...  16.9 us
    pallas_call x8, Pallas kernels, call(): return list(run(*operands))  8.64 us
    ppermute x5, starting transfers between devices, shift(): lax.ppermute(block, axis, [((i + distance) % count, i) for i in range(cou...  8.4 us
    ppermute x6, starting transfers between devices, exchange(): got.append(lax.ppermute(piece, ('dx', 'dy'), route))  7.11 us
    unnamed x6, local copies, waits for them, and re-layouts  2.16 us
  transfers between devices with their start and end apart: 14, of which 5 were waited for; matrix products, arithmetic and copies ran while one was open for 5% of the time, Pallas kernels for 18%

profile of v25, /device:TPU:0, one launch (start us, length us, event | category | flops | bytes accessed | tf_op | source)
XLA Modules:
  0.0 44.0 jit_solution(16155012447066702553)
XLA Ops:
  0.0 3.0 %collective-permute-start.5 = (bf16[128,4,8,128]{3,2,1,0:T(8,128)(2,1)}, bf16[128,4,8,128]{3,2,1,0:T(8,128)(2,1)S(1)}, u32[]{:S(2)}, u32[]{:S(2)}) collective-permute-start(bf16[128,4,8,128]{3,2,1,0:T(8,128)(2,1)} %param.3), channel_id=1, source_target_pairs={{24,0},{28,4},{0,8},{4,12},{8,16},{12,20},{16,24},{20,28},{25,1},{... | collective-permute-start | bytes 3145736 | tf_op jit(solution)/shard_map/ppermute | solution.py:24
  3.0 1.7 %copy.9 = bf16[16,8,32,128]{3,1,2,0:T(8,128)(2,1)S(1)} copy(bf16[16,8,32,128]{3,2,1,0:T(8,128)(2,1)} %bitcast.18) | data formatting | bytes 2097152
  4.8 0.1 shard_map.37
  4.9 1.6 %collective-permute-start = (bf16[128,1280]{1,0:T(8,128)(2,1)S(1)}, bf16[128,1280]{1,0:T(8,128)(2,1)S(1)}, u32[]{:S(2)}, u32[]{:S(2)}) collective-permute-start(bf16[128,1280]{1,0:T(8,128)(2,1)S(1)} %get-tuple-element.34), channel_id=1, source_target_pairs={{1,0},{0,1},{3,2},{2,3},{5,4},{4,5},{7,6},{6,7},{9,8},{8,9},{11,10... | collective-permute-start | bytes 983048 | tf_op jit(solution)/shard_map/ppermute | solution.py:24
  6.4 1.5 %collective-permute-start.1 = (bf16[128,1152]{1,0:T(8,128)(2,1)S(1)}, bf16[128,1152]{1,0:T(8,128)(2,1)S(1)}, u32[]{:S(2)}, u32[]{:S(2)}) collective-permute-start(bf16[128,1152]{1,0:T(8,128)(2,1)S(1)} %get-tuple-element.36), channel_id=1, source_target_pairs={{2,0},{0,2},{3,1},{1,3},{6,4},{4,6},{7,5},{5,7},{10,8},{8,10},{11,... | collective-permute-start | bytes 884744 | tf_op jit(solution)/shard_map/ppermute | solution.py:24
  8.0 0.5 %collective-permute-start.2 = (bf16[128,1152]{1,0:T(8,128)(2,1)S(1)}, bf16[128,1152]{1,0:T(8,128)(2,1)S(1)}, u32[]{:S(2)}, u32[]{:S(2)}) collective-permute-start(bf16[128,1152]{1,0:T(8,128)(2,1)S(1)} %get-tuple-element.37), channel_id=1, source_target_pairs={{2,0},{0,2},{3,1},{1,3},{6,4},{4,6},{7,5},{5,7},{10,8},{8,10},{11,... | collective-permute-start | bytes 884744 | tf_op jit(solution)/shard_map/ppermute | solution.py:24
  8.5 5.7 %collective-permute-done.refs_1_.refs_3_ = bf16[128,1280]{1,0:T(8,128)(2,1)S(1)} collective-permute-done((bf16[128,1280]{1,0:T(8,128)(2,1)S(1)}, bf16[128,1280]{1,0:T(8,128)(2,1)S(1)}, u32[]{:S(2)}, u32[]{:S(2)}) %collective-permute-start) | collective-permute-done | bytes 327712 | tf_op jit(solution)/shard_map/ppermute | solution.py:24
  14.1 1.9 %shard_map.38 = (bf16[384,2048]{1,0:T(8,128)(2,1)S(1)}, bf16[384,2048]{1,0:T(8,128)(2,1)S(1)}) custom-call(bf16[128,4096]{1,0:T(8,128)(2,1)S(1)} %bitcast.11, bf16[128,1280]{1,0:T(8,128)(2,1)S(1)} %collective-permute-done.refs_1_.refs_3_, f32[4,8,128]{2,1,0:T(8,128)S(1)} %copy-done.1, f32[3,4,8,128]{3,2,1,0:T(8,128)S(1)} %copy-done), custom_call_target="tpu_custom_call" | custom-call | tf_op jit(solution)/shard_map/pallas_call | solution.py:58
  16.0 0.4 collective-permute-done.1.refs_1_
  16.4 4.6 %collective-permute-done.2.refs_2_ = bf16[128,1152]{1,0:T(8,128)(2,1)S(1)} collective-permute-done((bf16[128,1152]{1,0:T(8,128)(2,1)S(1)}, bf16[128,1152]{1,0:T(8,128)(2,1)S(1)}, u32[]{:S(2)}, u32[]{:S(2)}) %collective-permute-start.2) | collective-permute-done | bytes 294944 | tf_op jit(solution)/shard_map/ppermute | solution.py:24
  21.0 0.0 collective-permute-start.3
  21.0 1.9 %shard_map.39 = (bf16[384,2048]{1,0:T(8,128)(2,1)S(1)}, bf16[384,2048]{1,0:T(8,128)(2,1)S(1)}) custom-call(bf16[128,4096]{1,0:T(8,128)(2,1)S(1)} %bitcast.12, bf16[128,1152]{1,0:T(8,128)(2,1)S(1)} %collective-permute-done.1.refs_1_, bf16[128,1152]{1,0:T(8,128)(2,1)S(1)} %collective-permute-done.2.refs_2_, ...), custom_call_target="tpu_custom_call" | custom-call | tf_op jit(solution)/shard_map/pallas_call | solution.py:58
  22.9 0.6 %collective-permute-start.4 = (bf16[384,2048]{1,0:T(8,128)(2,1)S(1)}, bf16[384,2048]{1,0:T(8,128)(2,1)S(1)}, u32[]{:S(2)}, u32[]{:S(2)}) collective-permute-start(bf16[384,2048]{1,0:T(8,128)(2,1)S(1)} %get-tuple-element.41.refs_1_), channel_id=1, source_target_pairs={{0,4},{4,0},{8,12},{12,8},{16,20},{20,16},{24,28},{28,24},{1,5},{5... | collective-permute-start | bytes 4718600 | tf_op jit(solution)/shard_map/ppermute | solution.py:332
  23.5 1.0 %shard_map.40.refs_6_.refs_4_ = f32[384,128]{1,0:T(8,128)S(1)} custom-call(bf16[384,2048]{1,0:T(8,128)(2,1)S(1)} %get-tuple-element.42.refs_0_, bf16[384,2048]{1,0:T(8,128)(2,1)S(1)} %get-tuple-element.43.refs_1_, bf16[128,4096]{1,0:T(8,128)(2,1)S(1)} %bitcast.13), custom_call_target="tpu_custom_call" | custom-call | tf_op jit(solution)/shard_map/pallas_call | solution.py:58
  24.4 4.0 %collective-permute-done.5 = bf16[128,4,8,128]{3,2,1,0:T(8,128)(2,1)S(1)} collective-permute-done((bf16[128,4,8,128]{3,2,1,0:T(8,128)(2,1)}, bf16[128,4,8,128]{3,2,1,0:T(8,128)(2,1)S(1)}, u32[]{:S(2)}, u32[]{:S(2)}) %collective-permute-start.5) | collective-permute-done | bytes 1048608 | tf_op jit(solution)/shard_map/ppermute | solution.py:24
  28.4 0.5 %copy.8 = bf16[16,8,32,128]{3,1,2,0:T(8,128)(2,1)S(1)} copy(bf16[16,8,32,128]{3,2,1,0:T(8,128)(2,1)S(1)} %bitcast.19) | data formatting | bytes 2097152
  28.9 0.1 collective-permute-start.9
  29.0 0.0 collective-permute-done.3.refs_2_
  29.0 1.9 %shard_map.41 = (f32[128,384]{1,0:T(8,128)S(1)}, f32[2,3,32,128]{3,2,1,0:T(8,128)S(1)}, bf16[2,3,32,128]{3,2,1,0:T(8,128)(2,1)S(1)}, bf16[2,3,32,128]{3,2,1,0:T(8,128)(2,1)S(1)}, bf16[2,3,32,128]{3,2,1,0:T(8,128)(2,1)S(1)}) custom-call(bf16[384,2048]{1,0:T(8,128)(2,1)S(1)} %get-tuple-element.35.refs_0_, bf16[384,2048]{1,0:T(8,128)(2,1)S(1)} %get-tuple-element.41.refs_1_, ...), custom_call_target="tpu_custom_call" | custom-call | bytes 3000000 | tf_op jit(solution)/shard_map/pallas_call | solution.py:58
  30.9 2.5 %collective-permute-start.6 = (bf16[2,3,32,128]{3,2,1,0:T(8,128)(2,1)S(1)}, bf16[2,3,32,128]{3,2,1,0:T(8,128)(2,1)S(1)}, u32[]{:S(2)}, u32[]{:S(2)}) collective-permute-start(bf16[2,3,32,128]{3,2,1,0:T(8,128)(2,1)S(1)} %get-tuple-element.46), channel_id=1, source_target_pairs={{0,3},{1,2},{2,1},{3,0},{4,7},{5,6},{6,5},{7,4},{8,11},{9,10},{10,... | collective-permute-start | bytes 147464 | tf_op jit(solution)/shard_map/ppermute | solution.py:42
  33.4 0.5 %collective-permute-start.7 = (bf16[2,3,32,128]{3,2,1,0:T(8,128)(2,1)S(1)}, bf16[2,3,32,128]{3,2,1,0:T(8,128)(2,1)S(1)}, u32[]{:S(2)}, u32[]{:S(2)}) collective-permute-start(bf16[2,3,32,128]{3,2,1,0:T(8,128)(2,1)S(1)} %get-tuple-element.47), channel_id=1, source_target_pairs={{0,2},{1,3},{2,0},{3,1},{4,6},{5,7},{6,4},{7,5},{8,10},{9,11},{10,... | collective-permute-start | bytes 147464 | tf_op jit(solution)/shard_map/ppermute | solution.py:42
  33.9 0.5 %collective-permute-start.8 = (bf16[2,3,32,128]{3,2,1,0:T(8,128)(2,1)S(1)}, bf16[2,3,32,128]{3,2,1,0:T(8,128)(2,1)S(1)}, u32[]{:S(2)}, u32[]{:S(2)}) collective-permute-start(bf16[2,3,32,128]{3,2,1,0:T(8,128)(2,1)S(1)} %get-tuple-element.48), channel_id=1, source_target_pairs={{0,1},{1,0},{2,3},{3,2},{4,5},{5,4},{6,7},{7,6},{8,9},{9,8},{10,11... | collective-permute-start | bytes 147464 | tf_op jit(solution)/shard_map/ppermute | solution.py:42
  34.4 0.0 collective-permute-done.9.refs_3_
  34.4 1.0 %shard_map.42 = (f32[3,3,32,128]{3,2,1,0:T(8,128)S(1)}, bf16[3,3,32,128]{3,2,1,0:T(8,128)(2,1)S(1)}, bf16[3,3,32,128]{3,2,1,0:T(8,128)(2,1)S(1)}, bf16[3,3,32,128]{3,2,1,0:T(8,128)(2,1)S(1)}) custom-call(bf16[384,2048]{1,0:T(8,128)(2,1)S(1)} %get-tuple-element.42.refs_0_, bf16[384,2048]{1,0:T(8,128)(2,1)S(1)} %get-tuple-element.43.refs_1_, ...), custom_call_target="tpu_custom_call" | custom-call | bytes 3000000 | tf_op jit(solution)/shard_map/pallas_call | solution.py:58
  35.5 2.5 %collective-permute-start.10 = (bf16[3,3,32,128]{3,2,1,0:T(8,128)(2,1)S(1)}, bf16[3,3,32,128]{3,2,1,0:T(8,128)(2,1)S(1)}, u32[]{:S(2)}, u32[]{:S(2)}) collective-permute-start(bf16[3,3,32,128]{3,2,1,0:T(8,128)(2,1)S(1)} %get-tuple-element.54), channel_id=1, source_target_pairs={{0,3},{1,2},{2,1},{3,0},{4,7},{5,6},{6,5},{7,4},{8,11},{9,10},{10,... | collective-permute-start | bytes 221192 | tf_op jit(solution)/shard_map/ppermute | solution.py:42
  38.0 0.5 %collective-permute-start.11 = (bf16[3,3,32,128]{3,2,1,0:T(8,128)(2,1)S(1)}, bf16[3,3,32,128]{3,2,1,0:T(8,128)(2,1)S(1)}, u32[]{:S(2)}, u32[]{:S(2)}) collective-permute-start(bf16[3,3,32,128]{3,2,1,0:T(8,128)(2,1)S(1)} %get-tuple-element.55), channel_id=1, source_target_pairs={{0,2},{1,3},{2,0},{3,1},{4,6},{5,7},{6,4},{7,5},{8,10},{9,11},{10,... | collective-permute-start | bytes 221192 | tf_op jit(solution)/shard_map/ppermute | solution.py:42
  38.5 0.0 collective-permute-done.6.refs_1_
  38.5 0.5 %collective-permute-start.12 = (bf16[3,3,32,128]{3,2,1,0:T(8,128)(2,1)S(1)}, bf16[3,3,32,128]{3,2,1,0:T(8,128)(2,1)S(1)}, u32[]{:S(2)}, u32[]{:S(2)}) collective-permute-start(bf16[3,3,32,128]{3,2,1,0:T(8,128)(2,1)S(1)} %get-tuple-element.56), channel_id=1, source_target_pairs={{0,1},{1,0},{2,3},{3,2},{4,5},{5,4},{6,7},{7,6},{8,9},{9,8},{10,11... | collective-permute-start | bytes 221192 | tf_op jit(solution)/shard_map/ppermute | solution.py:42
  39.0 0.0 collective-permute-done.7.refs_2_
  39.1 1.8 %collective-permute-start.13 = (bf16[2,3,32,128]{3,2,1,0:T(8,128)(2,1)S(1)}, bf16[2,3,32,128]{3,2,1,0:T(8,128)(2,1)S(1)}, u32[]{:S(2)}, u32[]{:S(2)}) collective-permute-start(bf16[2,3,32,128]{3,2,1,0:T(8,128)(2,1)S(1)} %get-tuple-element.62), channel_id=1, source_target_pairs={{8,0},{12,4},{16,8},{20,12},{24,16},{28,20},{0,24},{4,28},{9,1},{1... | collective-permute-start | bytes 147464 | tf_op jit(solution)/shard_map/ppermute | solution.py:24
  40.9 2.3 %collective-permute-done.13.refs_5_ = bf16[2,3,32,128]{3,2,1,0:T(8,128)(2,1)S(1)} collective-permute-done((bf16[2,3,32,128]{3,2,1,0:T(8,128)(2,1)S(1)}, bf16[2,3,32,128]{3,2,1,0:T(8,128)(2,1)S(1)}, u32[]{:S(2)}, u32[]{:S(2)}) %collective-permute-start.13) | collective-permute-done | bytes 49184 | tf_op jit(solution)/shard_map/ppermute | solution.py:24
  43.2 0.7 %shard_map.44 = f32[3,5,32,128]{3,2,1,0:T(8,128)} custom-call(f32[3,3,32,128]{3,2,1,0:T(8,128)S(1)} %get-tuple-element.53.refs_0_, bf16[3,3,32,128]{3,2,1,0:T(8,128)(2,1)S(1)} %collective-permute-done.10.refs_1_, bf16[3,3,32,128]{3,2,1,0:T(8,128)(2,1)S(1)} %collective-permute-done.11.refs_2_, bf16[3,3,32,128]{3,2,1,0:T(8,128)(2,1)S(1)} %collective-permute-done.12.refs_3_, ...), custom_call_target="tpu_custom_call" | custom-call | tf_op jit(solution)/shard_map/pallas_call | solution.py:58
  (10 shorter events, 0.1 us)
Async XLA Ops:
  0.0 4.7 %copy-start.1 = (f32[4,8,128]{2,1,0:T(8,128)S(1)}, f32[4,8,128]{2,1,0:T(8,128)}, u32[]{:S(2)}) copy-start(f32[4,8,128]{2,1,0:T(8,128)} %refs_4_.1) | copy-start | bytes 49156
  0.0 4.7 %copy-start = (f32[3,4,8,128]{3,2,1,0:T(8,128)S(1)}, f32[3,4,8,128]{3,2,1,0:T(8,128)}, u32[]{:S(2)}) copy-start(f32[3,4,8,128]{3,2,1,0:T(8,128)} %refs_5_.1) | copy-start | bytes 147460
  0.0 28.4 %collective-permute-start.5 = (bf16[128,4,8,128]{3,2,1,0:T(8,128)(2,1)}, bf16[128,4,8,128]{3,2,1,0:T(8,128)(2,1)S(1)}, u32[]{:S(2)}, u32[]{:S(2)}) collective-permute-start(bf16[128,4,8,128]{3,2,1,0:T(8,128)(2,1)} %param.3), channel_id=1, source_target_pairs={{24,0},{28,4},{0,8},{4,12},{8,16},{12,20},{16,24},{20,28},{25,1},{... | collective-permute-start | bytes 3145736 | tf_op jit(solution)/shard_map/ppermute | solution.py:24
  4.9 9.2 %collective-permute-start = (bf16[128,1280]{1,0:T(8,128)(2,1)S(1)}, bf16[128,1280]{1,0:T(8,128)(2,1)S(1)}, u32[]{:S(2)}, u32[]{:S(2)}) collective-permute-start(bf16[128,1280]{1,0:T(8,128)(2,1)S(1)} %get-tuple-element.34), channel_id=1, source_target_pairs={{1,0},{0,1},{3,2},{2,3},{5,4},{4,5},{7,6},{6,7},{9,8},{8,9},{11,10... | collective-permute-start | bytes 983048 | tf_op jit(solution)/shard_map/ppermute | solution.py:24
  6.4 9.9 %collective-permute-start.1 = (bf16[128,1152]{1,0:T(8,128)(2,1)S(1)}, bf16[128,1152]{1,0:T(8,128)(2,1)S(1)}, u32[]{:S(2)}, u32[]{:S(2)}) collective-permute-start(bf16[128,1152]{1,0:T(8,128)(2,1)S(1)} %get-tuple-element.36), channel_id=1, source_target_pairs={{2,0},{0,2},{3,1},{1,3},{6,4},{4,6},{7,5},{5,7},{10,8},{8,10},{11,... | collective-permute-start | bytes 884744 | tf_op jit(solution)/shard_map/ppermute | solution.py:24
  8.0 13.0 %collective-permute-start.2 = (bf16[128,1152]{1,0:T(8,128)(2,1)S(1)}, bf16[128,1152]{1,0:T(8,128)(2,1)S(1)}, u32[]{:S(2)}, u32[]{:S(2)}) collective-permute-start(bf16[128,1152]{1,0:T(8,128)(2,1)S(1)} %get-tuple-element.37), channel_id=1, source_target_pairs={{2,0},{0,2},{3,1},{1,3},{6,4},{4,6},{7,5},{5,7},{10,8},{8,10},{11,... | collective-permute-start | bytes 884744 | tf_op jit(solution)/shard_map/ppermute | solution.py:24
  21.0 8.0 %collective-permute-start.3 = (bf16[384,2048]{1,0:T(8,128)(2,1)S(1)}, bf16[384,2048]{1,0:T(8,128)(2,1)S(1)}, u32[]{:S(2)}, u32[]{:S(2)}) collective-permute-start(bf16[384,2048]{1,0:T(8,128)(2,1)S(1)} %get-tuple-element.35.refs_0_), channel_id=1, source_target_pairs={{0,4},{4,0},{8,12},{12,8},{16,20},{20,16},{24,28},{28,24},{1,5},{5... | collective-permute-start | bytes 4718600 | tf_op jit(solution)/shard_map/ppermute | solution.py:332
  22.9 6.1 %collective-permute-start.4 = (bf16[384,2048]{1,0:T(8,128)(2,1)S(1)}, bf16[384,2048]{1,0:T(8,128)(2,1)S(1)}, u32[]{:S(2)}, u32[]{:S(2)}) collective-permute-start(bf16[384,2048]{1,0:T(8,128)(2,1)S(1)} %get-tuple-element.41.refs_1_), channel_id=1, source_target_pairs={{0,4},{4,0},{8,12},{12,8},{16,20},{20,16},{24,28},{28,24},{1,5},{5... | collective-permute-start | bytes 4718600 | tf_op jit(solution)/shard_map/ppermute | solution.py:332
  28.9 5.6 %collective-permute-start.9 = (bf16[128,4096]{1,0:T(8,128)(2,1)S(1)}, bf16[128,4096]{1,0:T(8,128)(2,1)S(1)}, u32[]{:S(2)}, u32[]{:S(2)}) collective-permute-start(bf16[128,4096]{1,0:T(8,128)(2,1)S(1)} %bitcast.15), channel_id=1, source_target_pairs={{0,4},{4,0},{8,12},{12,8},{16,20},{20,16},{24,28},{28,24},{1,5},{5... | collective-permute-start | bytes 3145736 | tf_op jit(solution)/shard_map/ppermute | solution.py:345
  30.9 7.6 %collective-permute-start.6 = (bf16[2,3,32,128]{3,2,1,0:T(8,128)(2,1)S(1)}, bf16[2,3,32,128]{3,2,1,0:T(8,128)(2,1)S(1)}, u32[]{:S(2)}, u32[]{:S(2)}) collective-permute-start(bf16[2,3,32,128]{3,2,1,0:T(8,128)(2,1)S(1)} %get-tuple-element.46), channel_id=1, source_target_pairs={{0,3},{1,2},{2,1},{3,0},{4,7},{5,6},{6,5},{7,4},{8,11},{9,10},{10,... | collective-permute-start | bytes 147464 | tf_op jit(solution)/shard_map/ppermute | solution.py:42
  33.4 5.6 %collective-permute-start.7 = (bf16[2,3,32,128]{3,2,1,0:T(8,128)(2,1)S(1)}, bf16[2,3,32,128]{3,2,1,0:T(8,128)(2,1)S(1)}, u32[]{:S(2)}, u32[]{:S(2)}) collective-permute-start(bf16[2,3,32,128]{3,2,1,0:T(8,128)(2,1)S(1)} %get-tuple-element.47), channel_id=1, source_target_pairs={{0,2},{1,3},{2,0},{3,1},{4,6},{5,7},{6,4},{7,5},{8,10},{9,11},{10,... | collective-permute-start | bytes 147464 | tf_op jit(solution)/shard_map/ppermute | solution.py:42
  33.9 5.1 %collective-permute-start.8 = (bf16[2,3,32,128]{3,2,1,0:T(8,128)(2,1)S(1)}, bf16[2,3,32,128]{3,2,1,0:T(8,128)(2,1)S(1)}, u32[]{:S(2)}, u32[]{:S(2)}) collective-permute-start(bf16[2,3,32,128]{3,2,1,0:T(8,128)(2,1)S(1)} %get-tuple-element.48), channel_id=1, source_target_pairs={{0,1},{1,0},{2,3},{3,2},{4,5},{5,4},{6,7},{7,6},{8,9},{9,8},{10,11... | collective-permute-start | bytes 147464 | tf_op jit(solution)/shard_map/ppermute | solution.py:42
  35.5 7.7 %collective-permute-start.10 = (bf16[3,3,32,128]{3,2,1,0:T(8,128)(2,1)S(1)}, bf16[3,3,32,128]{3,2,1,0:T(8,128)(2,1)S(1)}, u32[]{:S(2)}, u32[]{:S(2)}) collective-permute-start(bf16[3,3,32,128]{3,2,1,0:T(8,128)(2,1)S(1)} %get-tuple-element.54), channel_id=1, source_target_pairs={{0,3},{1,2},{2,1},{3,0},{4,7},{5,6},{6,5},{7,4},{8,11},{9,10},{10,... | collective-permute-start | bytes 221192 | tf_op jit(solution)/shard_map/ppermute | solution.py:42
  38.0 5.2 %collective-permute-start.11 = (bf16[3,3,32,128]{3,2,1,0:T(8,128)(2,1)S(1)}, bf16[3,3,32,128]{3,2,1,0:T(8,128)(2,1)S(1)}, u32[]{:S(2)}, u32[]{:S(2)}) collective-permute-start(bf16[3,3,32,128]{3,2,1,0:T(8,128)(2,1)S(1)} %get-tuple-element.55), channel_id=1, source_target_pairs={{0,2},{1,3},{2,0},{3,1},{4,6},{5,7},{6,4},{7,5},{8,10},{9,11},{10,... | collective-permute-start | bytes 221192 | tf_op jit(solution)/shard_map/ppermute | solution.py:42
  38.5 4.7 %collective-permute-start.12 = (bf16[3,3,32,128]{3,2,1,0:T(8,128)(2,1)S(1)}, bf16[3,3,32,128]{3,2,1,0:T(8,128)(2,1)S(1)}, u32[]{:S(2)}, u32[]{:S(2)}) collective-permute-start(bf16[3,3,32,128]{3,2,1,0:T(8,128)(2,1)S(1)} %get-tuple-element.56), channel_id=1, source_target_pairs={{0,1},{1,0},{2,3},{3,2},{4,5},{5,4},{6,7},{7,6},{8,9},{9,8},{10,11... | collective-permute-start | bytes 221192 | tf_op jit(solution)/shard_map/ppermute | solution.py:42
  39.1 4.1 %collective-permute-start.13 = (bf16[2,3,32,128]{3,2,1,0:T(8,128)(2,1)S(1)}, bf16[2,3,32,128]{3,2,1,0:T(8,128)(2,1)S(1)}, u32[]{:S(2)}, u32[]{:S(2)}) collective-permute-start(bf16[2,3,32,128]{3,2,1,0:T(8,128)(2,1)S(1)} %get-tuple-element.62), channel_id=1, source_target_pairs={{8,0},{12,4},{16,8},{20,12},{24,16},{28,20},{0,24},{4,28},{9,1},{1... | collective-permute-start | bytes 147464 | tf_op jit(solution)/shard_map/ppermute | solution.py:24
